TPU v7x, 32 devices: a whole 2x2x4 slice. The times are simulated.
32 devices in a mesh: ctx: 8 (over y, x, core), head: 4 (over z).
Axes of the slice: x: 2, y: 2, z: 4, core: 2. Of those that a mesh axis runs over, the one named last changes fastest.
Arguments:
- queries: bfloat16 [8192, 2048], P('ctx', 'head'), may hold values from -4.5 to 4.5
- keys: bfloat16 [8192, 2048], P('ctx', 'head'), may hold values from -4.5 to 4.5
- values: bfloat16 [8192, 2048], P('ctx', 'head'), may hold values from -6 to 6
- out_weight: bfloat16 [2048, 2048], P('head'), may hold values from -0.5 to 0.5
Outputs:
- mixed: bfloat16 [8192, 2048], P(('ctx', 'head'))
All inputs are finite; a program needn't handle non-finite values.
Results may differ from a plain program's by a relative error of at most 0.019.
Values may be sent and summed in bfloat16 or wider, within the bound.
No kernel may reach another device: no remote copies, remote signals or barrier semaphores. Data moves between devices by JAX's collectives and lax.ppermute only.
A program may use at most 64 MiB of HBM per device.

v0:
```python
import functools
import math

import jax
import jax.numpy as jnp
from jax import lax
from jax.experimental import pallas as pl
from jax.experimental.pallas import tpu as pltpu
from jax.sharding import PartitionSpec as P

HEAD_SIZE = 128
WINDOW = 512
STRIDE = 16
BLOCK = 128
SUMCOLS = 8

BIG_NEG = -1e30
TILE = 256
LOG_SCALE = HEAD_SIZE ** (-0.5) * math.log2(math.e)
F32 = jnp.float32
BF16 = jnp.bfloat16


def params(mib):
    return pltpu.CompilerParams(vmem_limit_bytes=mib * 1024 * 1024)


def cost(flops, bytes_accessed, exps=0):
    return pl.CostEstimate(
        flops=int(flops), bytes_accessed=int(bytes_accessed), transcendentals=int(exps)
    )


def iota2(shape, dim):
    return lax.broadcasted_iota(jnp.int32, shape, dim)


def scores(query, key_rows):
    return lax.dot_general(query, key_rows, (((1,), (1,)), ((), ())), preferred_element_type=F32)


def dot(left, right):
    return jnp.dot(left, right, preferred_element_type=F32)


def regroup_matrix():
    rows = iota2((TILE, TILE), 0)
    cols = iota2((TILE, TILE), 1)
    return (cols == (rows & 15) * 16 + (rows >> 4)).astype(BF16)


def with_ones(value_rows):
    return jnp.concatenate([value_rows, jnp.ones_like(value_rows)], axis=1)


def weighted(score_blocks, value_blocks, extra=None):
    top = functools.reduce(jnp.maximum, score_blocks)
    top = jnp.max(top, axis=-1, keepdims=True)
    if extra is not None:
        top = jnp.maximum(top, extra[0])
    total = None
    for block, value_block in zip(score_blocks, value_blocks):
        weights = jnp.exp2((block - top) * LOG_SCALE).astype(BF16)
        part = dot(weights, value_block)
        total = part if total is None else total + part
    if extra is not None:
        own = jnp.exp2((extra[0] - top) * LOG_SCALE).astype(BF16).astype(F32)
        total = total + own * extra[1].astype(F32)
    return total[:, :HEAD_SIZE] / total[:, HEAD_SIZE:]


def prep_kernel(q_ref, k_ref, v_ref, *refs, rim_start, chunks):
    send_refs, rim_ref, sum_ref = refs[:chunks], refs[chunks], refs[chunks + 1]
    step = pl.program_id(0)
    matrix = regroup_matrix()
    ctx, _, per, rows, width = send_refs[0].shape
    for number, ref in enumerate((q_ref, k_ref, v_ref)):
        grouped = dot(matrix, ref[...]).astype(BF16)
        for chunk in range(chunks):
            send_refs[chunk][:, number] = grouped[:, chunk * width : (chunk + 1) * width].reshape(
                ctx, per, rows, width
            )
    picks = TILE // BLOCK * SUMCOLS
    row = iota2((picks, TILE), 0)
    col = iota2((picks, TILE), 1)
    pick = (col == (row // SUMCOLS) * BLOCK + BLOCK - SUMCOLS + row % SUMCOLS).astype(BF16)
    sum_ref[0] = dot(pick, k_ref[...]).astype(BF16)
    sum_ref[1] = dot(pick, v_ref[...]).astype(BF16)

    @pl.when(step >= rim_start)
    def _():
        rim_ref[0] = k_ref[...]
        rim_ref[1] = v_ref[...]


def prepare(queries, keys, values, ctx, chunks):
    tokens_dev, width = queries.shape
    tiles = tokens_dev // TILE
    per = STRIDE // ctx
    rows = tokens_dev // STRIDE
    part = width // chunks
    rim_start = tiles - WINDOW // TILE
    picks = TILE // BLOCK * SUMCOLS
    source = pl.BlockSpec((TILE, width), lambda b: (b, 0))
    return pl.pallas_call(
        functools.partial(prep_kernel, rim_start=rim_start, chunks=chunks),
        grid=(tiles,),
        in_specs=[source] * 3,
        out_specs=[
            pl.BlockSpec((ctx, 3, per, TILE // STRIDE, part), lambda b: (0, 0, 0, b, 0))
        ]
        * chunks
        + [
            pl.BlockSpec((2, TILE, width), lambda b: (0, jnp.maximum(b - rim_start, 0), 0)),
            pl.BlockSpec((2, picks, width), lambda b: (0, b, 0)),
        ],
        out_shape=[jax.ShapeDtypeStruct((ctx, 3, per, rows, part), BF16)] * chunks
        + [
            jax.ShapeDtypeStruct((2, WINDOW, width), BF16),
            jax.ShapeDtypeStruct((2, tiles * picks, width), BF16),
        ],
        compiler_params=params(24),
        cost_estimate=cost(6 * tokens_dev * TILE * width, 16 * tokens_dev * width),
        name="prepare",
    )(queries, keys, values)


def home_kernel(place_ref, q_ref, k_ref, v_ref, rim_ref, sum_ref, o_ref):
    place = place_ref[0]
    tokens_dev = q_ref.shape[0]
    back = WINDOW // TILE
    key_blocks = [rim_ref[0, e * TILE : (e + 1) * TILE] for e in range(back)]
    value_blocks = [with_ones(rim_ref[1, e * TILE : (e + 1) * TILE]) for e in range(back)]
    for e in range(tokens_dev // TILE):
        key_blocks.append(k_ref[e * TILE : (e + 1) * TILE])
        value_blocks.append(with_ones(v_ref[e * TILE : (e + 1) * TILE]))
    order = gathered_order(sum_ref.shape[1])
    sum_keys = jnp.concatenate([sum_ref[0, i] for i in order])
    sum_values = with_ones(jnp.concatenate([sum_ref[1, i] for i in order]))
    row = iota2((TILE, TILE), 0)
    col = iota2((TILE, TILE), 1)
    sum_col = iota2((TILE, sum_keys.shape[0]), 1)
    for b in range(tokens_dev // TILE):
        query = q_ref[b * TILE : (b + 1) * TILE]
        blocks = []
        for e in range(back + 1):
            block = scores(query, key_blocks[b + e])
            allowed = None
            if e == 0:
                allowed = col > row
            if e == back:
                allowed = col <= row
            if b + e < back:
                held = place > 0
                allowed = held if allowed is None else allowed & held
            if allowed is not None:
                block = jnp.where(allowed, block, BIG_NEG)
            blocks.append(block)
        local = weighted(blocks, value_blocks[b : b + back + 1])
        pos = place * tokens_dev + b * TILE + iota2((TILE, 1), 0)
        within = pos % BLOCK
        held = pos // BLOCK * SUMCOLS + jnp.maximum(within - (BLOCK - SUMCOLS - 1), 0)
        block = jnp.where(sum_col < held, scores(query, sum_keys), BIG_NEG)
        own_key = key_blocks[b + back].astype(F32)
        own = jnp.sum(query.astype(F32) * own_key, axis=-1, keepdims=True)
        own = jnp.where(within < BLOCK - SUMCOLS, own, BIG_NEG)
        summary = weighted([block], [sum_values], (own, value_blocks[b + back]))
        o_ref[b * TILE : (b + 1) * TILE] = local + summary


def home_sections(place, queries, keys, values, rim, summary):
    tokens_dev, width = queries.shape
    heads = width // HEAD_SIZE
    pieces, picks = summary.shape[1:3]
    total = pieces * picks
    own = pl.BlockSpec((tokens_dev, HEAD_SIZE), lambda h: (0, h))
    pairs = tokens_dev * (WINDOW + TILE + total) * heads
    return pl.pallas_call(
        home_kernel,
        grid=(heads,),
        in_specs=[
            pl.BlockSpec(memory_space=pltpu.SMEM),
            own,
            own,
            own,
            pl.BlockSpec((2, WINDOW, HEAD_SIZE), lambda h: (0, 0, h)),
            pl.BlockSpec((2, pieces, picks, HEAD_SIZE), lambda h: (0, 0, 0, h)),
        ],
        out_specs=own,
        out_shape=jax.ShapeDtypeStruct((tokens_dev, width), F32),
        compiler_params=params(32),
        cost_estimate=cost(8 * pairs * HEAD_SIZE, 14 * tokens_dev * width, pairs),
        name="home",
    )(place, queries, keys, values, rim, summary)


def stride_kernel(x_ref, o_ref):
    ctx, _, _, rows, _ = x_ref.shape
    count = ctx * rows
    query = x_ref[:, 0, 0].reshape(count, HEAD_SIZE)
    key_rows = x_ref[:, 1, 0].reshape(count, HEAD_SIZE)
    value_rows = with_ones(x_ref[:, 2, 0].reshape(count, HEAD_SIZE))
    row = iota2((TILE, TILE), 0)
    col = iota2((TILE, TILE), 1)
    for b in range(count // TILE):
        part = query[b * TILE : (b + 1) * TILE]
        blocks = [scores(part, key_rows[e * TILE : (e + 1) * TILE]) for e in range(b + 1)]
        blocks[b] = jnp.where(col <= row, blocks[b], BIG_NEG)
        result = weighted(
            blocks, [value_rows[e * TILE : (e + 1) * TILE] for e in range(b + 1)]
        ).astype(BF16)
        sources = TILE // rows
        o_ref[b * sources : (b + 1) * sources, 0] = result.reshape(sources, rows, HEAD_SIZE)


def stride_attend(moved):
    ctx, _, per, rows, width = moved.shape
    count = ctx * rows
    heads = width // HEAD_SIZE
    pairs = per * heads * count * (count + TILE) // 2
    return pl.pallas_call(
        stride_kernel,
        grid=(heads, per),
        in_specs=[pl.BlockSpec((ctx, 3, 1, rows, HEAD_SIZE), lambda h, r: (0, 0, r, 0, h))],
        out_specs=pl.BlockSpec((ctx, 1, rows, HEAD_SIZE), lambda h, r: (0, r, 0, h)),
        out_shape=jax.ShapeDtypeStruct((ctx, per, rows, width), BF16),
        compiler_params=params(32),
        cost_estimate=cost(8 * pairs * HEAD_SIZE, 8 * per * count * width, pairs),
        name="stride",
    )(moved)


def combine_kernel(home_ref, back_ref, o_ref):
    width = home_ref.shape[1]
    back = dot(regroup_matrix(), back_ref[...].reshape(TILE, width))
    o_ref[...] = (home_ref[...] + back).astype(BF16)


def combine(home, back, chunk):
    tokens_dev = home.shape[0]
    ctx, per, _, width = back.shape
    return pl.pallas_call(
        combine_kernel,
        grid=(tokens_dev // TILE,),
        in_specs=[
            pl.BlockSpec((TILE, width), lambda b: (b, chunk)),
            pl.BlockSpec((ctx, per, TILE // STRIDE, width), lambda b: (0, 0, b, 0)),
        ],
        out_specs=pl.BlockSpec((TILE, width), lambda b: (b, 0)),
        out_shape=jax.ShapeDtypeStruct((tokens_dev, width), BF16),
        compiler_params=params(24),
        cost_estimate=cost(2 * tokens_dev * TILE * width, 8 * tokens_dev * width),
        name="combine",
    )(home, back)


def project_kernel(side_ref, *refs, chunks):
    moved_refs = refs[:chunks]
    mine_ref, other_ref, o_ref = refs[chunks:]

    def add_up(weight_ref):
        total = None
        for group in range(weight_ref.shape[0]):
            partial_value = None
            for chunk, ref in enumerate(moved_refs):
                width = ref.shape[2]
                part = dot(ref[group], weight_ref[group, chunk * width : (chunk + 1) * width])
                partial_value = part if partial_value is None else partial_value + part
            rounded = partial_value.astype(BF16).astype(F32)
            total = rounded if total is None else total + rounded
        o_ref[...] = total.astype(BF16)

    @pl.when(pl.program_id(0) == 0)
    def _():
        add_up(mine_ref)

    @pl.when(pl.program_id(0) == 1)
    def _():
        add_up(other_ref)


def project(side, moved, mine, other):
    groups, tokens, part = moved[0].shape
    width, half = mine.shape[1:]
    tile = min(half, 512)
    tiles = half // tile
    return pl.pallas_call(
        functools.partial(project_kernel, chunks=len(moved)),
        grid_spec=pltpu.PrefetchScalarGridSpec(
            num_scalar_prefetch=1,
            grid=(2, tiles),
            in_specs=[pl.BlockSpec((groups, tokens, part), lambda s, j, side: (0, 0, 0))]
            * len(moved)
            + [
                pl.BlockSpec(
                    (groups, width, tile),
                    lambda s, j, side: (0, 0, jnp.where(s == 0, j, tiles - 1)),
                ),
                pl.BlockSpec(
                    (groups, width, tile), lambda s, j, side: (0, 0, jnp.where(s == 0, 0, j))
                ),
            ],
            out_specs=pl.BlockSpec(
                (tokens, tile), lambda s, j, side: (0, (s ^ side[0]) * tiles + j)
            ),
        ),
        out_shape=jax.ShapeDtypeStruct((tokens, 2 * half), BF16),
        compiler_params=params(40),
        cost_estimate=cost(
            4 * groups * tokens * width * half,
            4 * groups * width * half + 2 * groups * tokens * width + 4 * tokens * half,
        ),
        name="project",
    )(side, *moved, mine, other)


def gathered_order(count):
    if count & (count - 1):
        return list(range(count))
    bits = count.bit_length() - 1
    return [sum(((i >> b) & 1) << (bits - 1 - b) for b in range(bits)) for i in range(count)]


def gather_ctx(rows):
    count = lax.axis_size("ctx")
    if count & (count - 1):
        return lax.all_gather(rows, "ctx", axis=1)
    place = lax.axis_index("ctx")
    held = rows[:, None]
    distance = count // 2
    while distance:
        received = lax.ppermute(held, "ctx", [(i, i ^ distance) for i in range(count)])
        low = (place & distance) == 0
        held = jnp.concatenate(
            [jnp.where(low, held, received), jnp.where(low, received, held)], axis=1
        )
        distance //= 2
    return held


def stride_general(queries, keys, values):
    tokens_dev, width = queries.shape
    heads = width // HEAD_SIZE
    ctx = lax.axis_size("ctx")
    copies = max(ctx // STRIDE, 1)
    rows = tokens_dev // STRIDE
    held_rows = ctx * rows // copies
    own_copy = lax.axis_index("ctx") // STRIDE
    query_pos = (jnp.arange(held_rows) // (rows // copies)) * rows
    query_pos = query_pos + (jnp.arange(held_rows) % (rows // copies)) * copies + own_copy
    shaped = queries.reshape(1, rows // copies, ctx, width)
    query = lax.all_to_all(shaped, "ctx", split_axis=2, concat_axis=1, tiled=True)
    query = query.reshape(held_rows, heads, HEAD_SIZE)
    both = jnp.stack([keys, values]).reshape(2, rows, 1, STRIDE, width)
    both = jnp.broadcast_to(both, (2, rows, copies, STRIDE, width)).reshape(2, rows, ctx, width)
    both = lax.all_to_all(both, "ctx", split_axis=2, concat_axis=1, tiled=True)
    both = both.reshape(2, ctx * rows, heads, HEAD_SIZE)
    allowed = jnp.arange(ctx * rows)[None, :] <= query_pos[:, None]

    def one_head(operands):
        head_query, head_keys, head_values = operands
        masked = jnp.where(allowed, scores(head_query, head_keys), BIG_NEG)
        return weighted([masked], [with_ones(head_values)])

    result = lax.map(
        one_head,
        (query.transpose(1, 0, 2), both[0].transpose(1, 0, 2), both[1].transpose(1, 0, 2)),
    )
    result = result.transpose(1, 0, 2).reshape(ctx, rows // copies, 1, width).astype(BF16)
    back = lax.all_to_all(result, "ctx", split_axis=0, concat_axis=2, tiled=True)
    return back.reshape(tokens_dev, width)


def body(queries, keys, values, out_weight, chunks):
    tokens_dev, width = queries.shape
    ctx = lax.axis_size("ctx")
    groups = lax.axis_size("head")
    place = lax.axis_index("ctx")
    place_word = place.astype(jnp.int32).reshape(1)
    side = place % 2
    sibling = [(i, i ^ 1) for i in range(ctx)]

    half = out_weight.shape[1] // 2
    weight_half = lax.dynamic_slice_in_dim(out_weight, side * half, half, axis=1)
    mine = lax.all_gather(weight_half, "head", axis=0)
    other = lax.ppermute(mine, "ctx", sibling)

    if ctx > STRIDE:
        stride_out = stride_general(queries, keys, values)
        rim = jnp.stack([keys[tokens_dev - WINDOW :], values[tokens_dev - WINDOW :]])
        picked = jnp.stack([keys, values]).reshape(2, tokens_dev // BLOCK, BLOCK, width)
        picked = picked[:, :, BLOCK - SUMCOLS :].reshape(2, -1, width)
        send = None
    else:
        *send, rim, picked = prepare(queries, keys, values, ctx, chunks)
        send = [
            lax.all_to_all(part, "ctx", split_axis=0, concat_axis=0, tiled=True) for part in send
        ]
    before = lax.ppermute(rim, "ctx", [(i, i + 1) for i in range(ctx - 1)])
    summary = gather_ctx(picked)
    home = home_sections(place_word, queries, keys, values, before, summary)

    moved = []
    for chunk in range(chunks):
        if send is None:
            attended = (home + stride_out.astype(F32)).astype(BF16)
        else:
            result = stride_attend(send[chunk])
            back = lax.all_to_all(result, "ctx", split_axis=0, concat_axis=0, tiled=True)
            attended = combine(home, back, chunk)
        attended = attended.reshape(groups, tokens_dev // groups, width // chunks)
        moved.append(lax.all_to_all(attended, "head", split_axis=0, concat_axis=0, tiled=True))
    return project(side.astype(jnp.int32).reshape(1), moved, mine, other)


def solution(mesh):
    chunks = 1
    placed = (P("ctx", "head"), P("ctx", "head"), P("ctx", "head"), P("head", None))
    return jax.shard_map(
        functools.partial(body, chunks=chunks),
        mesh=mesh,
        in_specs=placed,
        out_specs=P(("ctx", "head"), None),
        check_vma=False,
    )
```

profile of v0, /device:TPU:10, one launch (start us, length us, event | category | flops | bytes accessed | tf_op | source)
XLA Modules:
  0.0 180.7 jit_solution(12719153445507456434)
XLA Ops:
  6.5 0.0 copy-start
  6.5 0.0 copy-start.5
  6.5 0.0 all-gather.3.cloned.1.call-start
  6.5 1.6 copy-done
  8.1 1.1 constant_dynamic-slice_fusion
  9.2 0.0 all-gather.3.cloned.1.call-update
  9.3 0.0 copy-done.5
  9.3 0.0 copy-start.7
  9.3 1.2 copy-done.7
  10.5 0.0 copy-start.9
  10.5 1.2 copy-done.9
  11.7 2.7 %prepare.1 = (bf16[8,3,2,64,512]{4,3,2,1,0:T(8,128)(2,1)S(1)}, bf16[2,512,512]{2,1,0:T(8,128)(2,1)}, bf16[2,64,512]{2,1,0:T(8,128)(2,1)S(1)}) custom-call(bf16[1024,512]{1,0:T(8,128)(2,1)S(1)} %copy-done.5, bf16[1024,512]{1,0:T(8,128)(2,1)S(1)} %copy-done.7, bf16[1024,512]{1,0:T(8,128)(2,1)S(1)} %copy-done.9), custom_call_target="tpu_custom_call" | custom-call | flops 805306368 | bytes 8388608 | tf_op jit(solution)/shard_map/prepare/pallas_call | solution.py:105
  14.5 0.0 copy-start.2
  14.5 1.7 copy-done.2
  16.2 5.0 %all-to-all-start = ((bf16[8,3,2,64,512]{4,3,2,1,0:T(8,128)(2,1)}), bf16[8,3,2,64,512]{4,3,2,1,0:T(8,128)(2,1)}, u32[]{:S(2)}, u32[]{:S(2)}) async-start(bf16[8,3,2,64,512]{4,3,2,1,0:T(8,128)(2,1)} %copy-done.2), calls=%async_computation | async-start | bytes 6291456 | tf_op jit(solution)/shard_map/all_to_all | solution.py:397
  21.1 67.7 %all-gather.3.cloned.1.call-done = bf16[2048,1024]{1,0:T(8,128)(2,1)} async-done(((bf16[512,1024]{1,0:T(8,128)(2,1)}), bf16[2048,1024]{1,0:T(8,128)(2,1)}) %all-gather.3.cloned.1.call-update) | async-done | bytes 4194320 | tf_op jit(solution)/shard_map/all_gather | solution.py:385
  88.9 0.0 collective-permute-start.4
  88.9 1.5 collective-permute-start.1
  90.3 4.4 %collective-permute-done.1 = bf16[2,1,64,512]{3,2,1,0:T(8,128)(2,1)S(1)} collective-permute-done((bf16[2,1,64,512]{3,2,1,0:T(8,128)(2,1)S(1)}, bf16[2,1,64,512]{3,2,1,0:T(8,128)(2,1)S(1)}, u32[]{:S(2)}, u32[]{:S(2)}) %collective-permute-start.1) | collective-permute-done | bytes 131104 | tf_op jit(solution)/shard_map/ppermute | solution.py:332
  94.8 0.4 collective-permute-start.2
  95.3 1.9 %collective-permute-start = (bf16[2,512,512]{2,1,0:T(8,128)(2,1)}, bf16[2,512,512]{2,1,0:T(8,128)(2,1)}, u32[]{:S(2)}, u32[]{:S(2)}) collective-permute-start(bf16[2,512,512]{2,1,0:T(8,128)(2,1)} %get-tuple-element.8), channel_id=1, source_target_pairs={{0,4},{4,8},{8,12},{12,16},{16,20},{20,24},{24,28},{1,5},{5,9},{9,... | collective-permute-start | bytes 3145736 | tf_op jit(solution)/shard_map/ppermute | solution.py:399
  97.2 6.9 %collective-permute-done.2 = bf16[2,2,64,512]{3,2,1,0:T(8,128)(2,1)S(1)} collective-permute-done((bf16[2,2,64,512]{3,2,1,0:T(8,128)(2,1)S(1)}, bf16[2,2,64,512]{3,2,1,0:T(8,128)(2,1)S(1)}, u32[]{:S(2)}, u32[]{:S(2)}) %collective-permute-start.2) | collective-permute-done | bytes 262176 | tf_op jit(solution)/shard_map/ppermute | solution.py:332
  104.2 0.0 copy-start.12
  104.2 0.7 copy-done.12
  104.9 0.8 pad_maximum_fusion.1
  105.7 0.0 collective-permute-start.3
  105.7 0.0 all-to-all-done.x_ref
  105.7 8.2 %stride.1 = bf16[8,2,64,512]{3,2,1,0:T(8,128)(2,1)S(1)} custom-call(bf16[8,3,2,64,512]{4,3,2,1,0:T(8,128)(2,1)} %all-to-all-done.x_ref), custom_call_target="tpu_custom_call" | custom-call | flops 1610612736 | bytes 4194304 | tf_op jit(solution)/shard_map/stride/pallas_call | solution.py:221
  114.0 0.0 copy-start.11
  114.0 1.0 copy-done.11
  114.9 4.3 %all-to-all-start.1 = ((bf16[8,2,64,512]{3,2,1,0:T(8,128)(2,1)}), bf16[8,2,64,512]{3,2,1,0:T(8,128)(2,1)S(1)}, u32[]{:S(2)}, u32[]{:S(2)}) async-start(bf16[8,2,64,512]{3,2,1,0:T(8,128)(2,1)} %copy-done.11), calls=%async_computation.1 | async-start | bytes 2097152 | tf_op jit(solution)/shard_map/all_to_all | solution.py:409
  119.3 0.0 collective-permute-done.3
  119.3 1.3 broadcast_select_fusion.1
  120.6 0.1 pad_maximum_fusion.sum_ref
  120.7 0.0 collective-permute-done.rim_ref
  120.7 0.0 copy-done.6
  120.7 0.3 copy-done.8
  121.0 0.3 copy-done.10
  121.4 12.0 %home.1.home_ref = f32[1024,512]{1,0:T(8,128)S(1)} custom-call(s32[1]{0:T(128)} %bitcast.1.place_ref, bf16[1024,512]{1,0:T(8,128)(2,1)S(1)} %copy-done.6, bf16[1024,512]{1,0:T(8,128)(2,1)S(1)} %copy-done.8, bf16[1024,512]{1,0:T(8,128)(2,1)S(1)} %copy-done.10, bf16[2,512,512]{2,1,0:T(8,128)(2,1)} %collective-permute-done.rim_ref, ...), custom_call_target="tpu_custom_call" | custom-call | flops 5368709120 | bytes 7340032 | tf_op jit(solution)/shard_map/home/pallas_call | solution.py:178
  133.3 0.0 copy-start.3
  133.3 1.4 copy-done.3
  134.7 0.0 all-to-all-done.1.back_ref
  134.7 1.6 copy-done.4
  136.3 1.0 combine.1
  137.4 30.1 %all_to_all.15.refs_0_ = bf16[4,256,512]{2,1,0:T(8,128)(2,1)S(1)} all-to-all(bf16[4,256,512]{2,1,0:T(8,128)(2,1)S(1)} %bitcast.9), channel_id=1, replica_groups=mesh['ctx'=8,'head'=4] {'head'}, dimensions={0} | all-to-all | bytes 2097152 | tf_op jit(solution)/shard_map/all_to_all | solution.py:412
  167.5 0.0 collective-permute-done.4.refs_2_
  167.5 0.0 copy-done.1
  167.5 6.4 %project.1 = bf16[256,2048]{1,0:T(8,128)(2,1)} custom-call(s32[1]{0:T(128)} %bitcast.side_ref, bf16[4,256,512]{2,1,0:T(8,128)(2,1)S(1)} %all_to_all.15.refs_0_, bf16[4,512,1024]{2,1,0:T(8,128)(2,1)S(1)} %bitcast.8, bf16[4,512,1024]{2,1,0:T(8,128)(2,1)} %collective-permute-done.4.refs_2_), custom_call_target="tpu_custom_call" | custom-call | flops 2147483648 | bytes 10485760 | tf_op jit(solution)/shard_map/project/pallas_call | solution.py:287
  (8 shorter events, 0.1 us)
Async XLA Ops:
  6.5 1.6 copy-start
  6.5 2.7 %copy-start.5 = (bf16[1024,512]{1,0:T(8,128)(2,1)S(1)}, bf16[1024,512]{1,0:T(8,128)(2,1)}, u32[]{:S(2)}) copy-start(bf16[1024,512]{1,0:T(8,128)(2,1)} %q_ref.3) | copy-start | bytes 3145732
  6.5 82.3 %all-gather.3.cloned.1.call-start = ((), (), s32[]{:S(2)}) async-start(), calls=%async_computation.3 | async-start | bytes 5242880 | tf_op jit(solution)/shard_map/all_gather | solution.py:385
  9.3 1.2 copy-start.7
  10.5 1.2 copy-start.9
  14.5 1.7 copy-start.2
  16.2 89.5 %all-to-all-start = ((bf16[8,3,2,64,512]{4,3,2,1,0:T(8,128)(2,1)}), bf16[8,3,2,64,512]{4,3,2,1,0:T(8,128)(2,1)}, u32[]{:S(2)}, u32[]{:S(2)}) async-start(bf16[8,3,2,64,512]{4,3,2,1,0:T(8,128)(2,1)} %copy-done.2), calls=%async_computation | async-start | bytes 6291456 | tf_op jit(solution)/shard_map/all_to_all | solution.py:397
  88.9 78.6 %collective-permute-start.4 = (bf16[4,512,1024]{2,1,0:T(8,128)(2,1)}, bf16[4,512,1024]{2,1,0:T(8,128)(2,1)}, u32[]{:S(2)}, u32[]{:S(2)}) collective-permute-start(bf16[4,512,1024]{2,1,0:T(8,128)(2,1)} %bitcast.7), channel_id=1, source_target_pairs={{0,4},{4,0},{8,12},{12,8},{16,20},{20,16},{24,28},{28,24},{1,5},{5... | collective-permute-start | bytes 12582920 | tf_op jit(solution)/shard_map/ppermute | solution.py:386
  88.9 5.9 %collective-permute-start.1 = (bf16[2,1,64,512]{3,2,1,0:T(8,128)(2,1)S(1)}, bf16[2,1,64,512]{3,2,1,0:T(8,128)(2,1)S(1)}, u32[]{:S(2)}, u32[]{:S(2)}) collective-permute-start(bf16[2,1,64,512]{3,2,1,0:T(8,128)(2,1)S(1)} %bitcast.10), channel_id=1, source_target_pairs={{0,16},{4,20},{8,24},{12,28},{16,0},{20,4},{24,8},{28,12},{1,17},{... | collective-permute-start | bytes 393224 | tf_op jit(solution)/shard_map/ppermute | solution.py:332
  94.8 9.3 %collective-permute-start.2 = (bf16[2,2,64,512]{3,2,1,0:T(8,128)(2,1)S(1)}, bf16[2,2,64,512]{3,2,1,0:T(8,128)(2,1)S(1)}, u32[]{:S(2)}, u32[]{:S(2)}) collective-permute-start(bf16[2,2,64,512]{3,2,1,0:T(8,128)(2,1)S(1)} %pad_maximum_fusion.2), channel_id=1, source_target_pairs={{0,8},{4,12},{8,0},{12,4},{16,24},{20,28},{24,16},{28,20},{1,9},{5... | collective-permute-start | bytes 786440 | tf_op jit(solution)/shard_map/ppermute | solution.py:332
  95.3 25.5 %collective-permute-start = (bf16[2,512,512]{2,1,0:T(8,128)(2,1)}, bf16[2,512,512]{2,1,0:T(8,128)(2,1)}, u32[]{:S(2)}, u32[]{:S(2)}) collective-permute-start(bf16[2,512,512]{2,1,0:T(8,128)(2,1)} %get-tuple-element.8), channel_id=1, source_target_pairs={{0,4},{4,8},{8,12},{12,16},{16,20},{20,24},{24,28},{1,5},{5,9},{9,... | collective-permute-start | bytes 3145736 | tf_op jit(solution)/shard_map/ppermute | solution.py:399
  104.2 0.7 copy-start.12
  105.7 13.6 %collective-permute-start.3 = (bf16[2,4,64,512]{3,2,1,0:T(8,128)(2,1)}, bf16[2,4,64,512]{3,2,1,0:T(8,128)(2,1)}, u32[]{:S(2)}, u32[]{:S(2)}) collective-permute-start(bf16[2,4,64,512]{3,2,1,0:T(8,128)(2,1)} %pad_maximum_fusion.1), channel_id=1, source_target_pairs={{0,4},{4,0},{8,12},{12,8},{16,20},{20,16},{24,28},{28,24},{1,5},{5... | collective-permute-start | bytes 1572872 | tf_op jit(solution)/shard_map/ppermute | solution.py:332
  114.0 1.0 copy-start.11
  114.9 19.8 %all-to-all-start.1 = ((bf16[8,2,64,512]{3,2,1,0:T(8,128)(2,1)}), bf16[8,2,64,512]{3,2,1,0:T(8,128)(2,1)S(1)}, u32[]{:S(2)}, u32[]{:S(2)}) async-start(bf16[8,2,64,512]{3,2,1,0:T(8,128)(2,1)} %copy-done.11), calls=%async_computation.1 | async-start | bytes 2097152 | tf_op jit(solution)/shard_map/all_to_all | solution.py:409
  119.3 1.5 copy-start.6
  119.3 1.8 copy-start.8
  119.3 2.1 %copy-start.10 = (bf16[1024,512]{1,0:T(8,128)(2,1)S(1)}, bf16[1024,512]{1,0:T(8,128)(2,1)}, u32[]{:S(2)}) copy-start(bf16[1024,512]{1,0:T(8,128)(2,1)} %v_ref.3) | copy-start | bytes 3145732
  133.3 1.4 copy-start.3
  134.7 1.6 copy-start.4
  136.3 31.1 %copy-start.1 = (bf16[2048,1024]{1,0:T(8,128)(2,1)S(1)}, bf16[2048,1024]{1,0:T(8,128)(2,1)}, u32[]{:S(2)}) copy-start(bf16[2048,1024]{1,0:T(8,128)(2,1)} %all-gather.3.cloned.1.call-done) | copy-start | bytes 12582916
Sparse Core Ops, SparseCore 0:
  9.4 79.4 all-gather.2
where the time goes:
time: 184 us; the launch traced here: 181 us
  waiting for transfers between devices  79.1 us (43%)
  Pallas kernels  30.4 us (17%)
  blocking collectives  30.1 us (16%)
  between operations  13.5 us (7%)
  starting transfers between devices  13.1 us (7%)
  local copies, waits for them, and re-layouts  12.1 us (7%)
  other arithmetic  2.36 us (1%)
    all_gather x1, waiting for transfers between devices, body(): mine = lax.all_gather(weight_half, 'head', axis=0)  67.7 us
    all_to_all x1, blocking collectives, body(): lax.all_to_all(attended, 'head', split_axis=0, concat_axis=0, tiled=True)  30.1 us
    pallas_call x1, Pallas kernels, home_sections(): pl.pallas_call(home_kernel, grid=(heads,), in_specs=[pl.BlockSpec(memory_...  12 us
    ppermute x3, waiting for transfers between devices, gather_ctx(): lax.ppermute(held, 'ctx', [(i, i ^ distance) for i in range(count)])  11.4 us
    unnamed x26, local copies, waits for them, and re-layouts  11 us
    pallas_call x1, Pallas kernels, stride_attend(): pl.pallas_call(stride_kernel, grid=(heads, per), in_specs=[pl.BlockSpec((...  8.24 us
    pallas_call x1, Pallas kernels, project(): pl.pallas_call(functools.partial(project_kernel, chunks=len(moved)), grid...  6.37 us
    all_to_all x1, starting transfers between devices, body(): lax.all_to_all(part, 'ctx', split_axis=0, concat_axis=0, tiled=True)  4.97 us
  transfers between devices with their start and end apart: 8, of which 3 were waited for; matrix products, arithmetic and copies ran while one was open for 1% of the time, Pallas kernels for 13%

commit v1 on v0

--- a/solution.py
+++ b/solution.py
@@ -8,6 +8,7 @@
 from jax.experimental.pallas import tpu as pltpu
 from jax.sharding import PartitionSpec as P
 
+HEADS = 16
 HEAD_SIZE = 128
 WINDOW = 512
 STRIDE = 16
@@ -25,10 +26,40 @@
     return pltpu.CompilerParams(vmem_limit_bytes=mib * 1024 * 1024)
 
 
+MARK = jax.ShapeDtypeStruct((8, 128), F32)
+
+
+def mark_spec():
+    return pl.BlockSpec(MARK.shape, lambda *place: (0, 0))
+
+
+def moments(arrays):
+    return [pl.BlockSpec(memory_space=pl.ANY)] * len(arrays)
+
+
+def after(array, others):
+    anywhere = pl.BlockSpec(memory_space=pl.ANY)
+    return pl.pallas_call(
+        lambda *refs: None,
+        in_specs=[anywhere] * (1 + len(others)),
+        out_specs=anywhere,
+        out_shape=jax.ShapeDtypeStruct(array.shape, array.dtype),
+        input_output_aliases={0: 0},
+        compiler_params=params(2),
+        cost_estimate=cost(0, 0),
+        name="after",
+    )(array, *others)
+
+
 def cost(flops, bytes_accessed, exps=0):
     return pl.CostEstimate(
         flops=int(flops), bytes_accessed=int(bytes_accessed), transcendentals=int(exps)
     )
+
+
+def partner(place, slot, count):
+    assert count & (count - 1) == 0
+    return place ^ slot
 
 
 def iota2(shape, dim):
@@ -119,13 +150,15 @@
             jax.ShapeDtypeStruct((2, WINDOW, width), BF16),
             jax.ShapeDtypeStruct((2, tiles * picks, width), BF16),
         ],
-        compiler_params=params(24),
+        compiler_params=params(60),
         cost_estimate=cost(6 * tokens_dev * TILE * width, 16 * tokens_dev * width),
         name="prepare",
     )(queries, keys, values)
 
 
-def home_kernel(place_ref, q_ref, k_ref, v_ref, rim_ref, sum_ref, o_ref):
+def home_kernel(place_ref, q_ref, k_ref, v_ref, rim_ref, sum_ref, *refs, order):
+    o_ref, mark_ref = refs[-2:]
+    mark_ref[...] = jnp.zeros_like(mark_ref)
     place = place_ref[0]
     tokens_dev = q_ref.shape[0]
     back = WINDOW // TILE
@@ -134,12 +167,14 @@
     for e in range(tokens_dev // TILE):
         key_blocks.append(k_ref[e * TILE : (e + 1) * TILE])
         value_blocks.append(with_ones(v_ref[e * TILE : (e + 1) * TILE]))
-    order = gathered_order(sum_ref.shape[1])
-    sum_keys = jnp.concatenate([sum_ref[0, i] for i in order])
-    sum_values = with_ones(jnp.concatenate([sum_ref[1, i] for i in order]))
+    pieces, picks = sum_ref.shape[1:3]
+    sum_keys = sum_ref[0].reshape(pieces * picks, HEAD_SIZE)
+    sum_values = with_ones(sum_ref[1].reshape(pieces * picks, HEAD_SIZE))
+    sum_col = jnp.concatenate(
+        [iota2((TILE, picks), 1) + (place ^ i) * picks for i in order], axis=1
+    )
     row = iota2((TILE, TILE), 0)
     col = iota2((TILE, TILE), 1)
-    sum_col = iota2((TILE, sum_keys.shape[0]), 1)
     for b in range(tokens_dev // TILE):
         query = q_ref[b * TILE : (b + 1) * TILE]
         blocks = []
@@ -168,138 +203,161 @@
         o_ref[b * TILE : (b + 1) * TILE] = local + summary
 
 
-def home_sections(place, queries, keys, values, rim, summary):
+def home_sections(place, queries, keys, values, rim, summary, order, chunk, chunks, waits):
     tokens_dev, width = queries.shape
-    heads = width // HEAD_SIZE
+    heads = width // chunks // HEAD_SIZE
+    first = chunk * heads
     pieces, picks = summary.shape[1:3]
     total = pieces * picks
-    own = pl.BlockSpec((tokens_dev, HEAD_SIZE), lambda h: (0, h))
+    own = pl.BlockSpec((tokens_dev, HEAD_SIZE), lambda h: (0, first + h))
     pairs = tokens_dev * (WINDOW + TILE + total) * heads
     return pl.pallas_call(
-        home_kernel,
+        functools.partial(home_kernel, order=order),
         grid=(heads,),
         in_specs=[
             pl.BlockSpec(memory_space=pltpu.SMEM),
             own,
             own,
             own,
-            pl.BlockSpec((2, WINDOW, HEAD_SIZE), lambda h: (0, 0, h)),
-            pl.BlockSpec((2, pieces, picks, HEAD_SIZE), lambda h: (0, 0, 0, h)),
-        ],
-        out_specs=own,
-        out_shape=jax.ShapeDtypeStruct((tokens_dev, width), F32),
-        compiler_params=params(32),
+            pl.BlockSpec((2, WINDOW, HEAD_SIZE), lambda h: (0, 0, first + h)),
+            pl.BlockSpec((2, pieces, picks, HEAD_SIZE), lambda h: (0, 0, 0, first + h)),
+        ]
+        + moments(waits),
+        out_specs=[pl.BlockSpec((tokens_dev, HEAD_SIZE), lambda h: (0, h)), mark_spec()],
+        out_shape=[jax.ShapeDtypeStruct((tokens_dev, heads * HEAD_SIZE), F32), MARK],
+        compiler_params=params(60),
         cost_estimate=cost(8 * pairs * HEAD_SIZE, 14 * tokens_dev * width, pairs),
         name="home",
-    )(place, queries, keys, values, rim, summary)
-
-
-def stride_kernel(x_ref, o_ref):
-    ctx, _, _, rows, _ = x_ref.shape
+    )(place, queries, keys, values, rim, summary, *waits)
+
+
+def stride_kernel(place_ref, x_ref, *refs):
+    ctx, _, _, rows, width = x_ref.shape
+    o_refs, mark_ref, held_ref = refs[-ctx - 2 : -2], refs[-2], refs[-1]
+    mark_ref[...] = jnp.zeros_like(mark_ref)
     count = ctx * rows
-    query = x_ref[:, 0, 0].reshape(count, HEAD_SIZE)
-    key_rows = x_ref[:, 1, 0].reshape(count, HEAD_SIZE)
-    value_rows = with_ones(x_ref[:, 2, 0].reshape(count, HEAD_SIZE))
     row = iota2((TILE, TILE), 0)
     col = iota2((TILE, TILE), 1)
-    for b in range(count // TILE):
-        part = query[b * TILE : (b + 1) * TILE]
-        blocks = [scores(part, key_rows[e * TILE : (e + 1) * TILE]) for e in range(b + 1)]
-        blocks[b] = jnp.where(col <= row, blocks[b], BIG_NEG)
+    sources = TILE // rows
+    units = []
+    for head in range(width // HEAD_SIZE):
+        lanes = slice(head * HEAD_SIZE, (head + 1) * HEAD_SIZE)
+        query = x_ref[:, 0, 0, :, lanes].reshape(count, HEAD_SIZE)
+        key_rows = x_ref[:, 1, 0, :, lanes].reshape(count, HEAD_SIZE)
+        value_rows = with_ones(x_ref[:, 2, 0, :, lanes].reshape(count, HEAD_SIZE))
+        for b in range(count // TILE):
+            part = query[b * TILE : (b + 1) * TILE]
+            blocks = [scores(part, key_rows[e * TILE : (e + 1) * TILE]) for e in range(b + 1)]
+            blocks[b] = jnp.where(col <= row, blocks[b], BIG_NEG)
+            units.append((lanes, b, blocks, value_rows))
+    for lanes, b, blocks, value_rows in units:
         result = weighted(
             blocks, [value_rows[e * TILE : (e + 1) * TILE] for e in range(b + 1)]
         ).astype(BF16)
-        sources = TILE // rows
-        o_ref[b * sources : (b + 1) * sources, 0] = result.reshape(sources, rows, HEAD_SIZE)
-
-
-def stride_attend(moved):
+        held_ref[b * sources : (b + 1) * sources, :, lanes] = result.reshape(
+            sources, rows, HEAD_SIZE
+        )
+    for slot in range(ctx):
+        o_refs[slot][0] = held_ref[partner(place_ref[0], slot, ctx)]
+
+
+def stride_attend(place, moved, waits):
     ctx, _, per, rows, width = moved.shape
     count = ctx * rows
-    heads = width // HEAD_SIZE
-    pairs = per * heads * count * (count + TILE) // 2
+    pairs = per * (width // HEAD_SIZE) * count * (count + TILE) // 2
     return pl.pallas_call(
         stride_kernel,
-        grid=(heads, per),
-        in_specs=[pl.BlockSpec((ctx, 3, 1, rows, HEAD_SIZE), lambda h, r: (0, 0, r, 0, h))],
-        out_specs=pl.BlockSpec((ctx, 1, rows, HEAD_SIZE), lambda h, r: (0, r, 0, h)),
-        out_shape=jax.ShapeDtypeStruct((ctx, per, rows, width), BF16),
-        compiler_params=params(32),
+        grid=(per,),
+        in_specs=[
+            pl.BlockSpec(memory_space=pltpu.SMEM),
+            pl.BlockSpec((ctx, 3, 1, rows, width), lambda r: (0, 0, r, 0, 0)),
+        ]
+        + moments(waits),
+        out_specs=[pl.BlockSpec((1, rows, width), lambda r: (r, 0, 0))] * ctx + [mark_spec()],
+        out_shape=[jax.ShapeDtypeStruct((per, rows, width), BF16)] * ctx + [MARK],
+        scratch_shapes=[pltpu.VMEM((ctx, rows, width), BF16)],
+        compiler_params=params(24),
         cost_estimate=cost(8 * pairs * HEAD_SIZE, 8 * per * count * width, pairs),
         name="stride",
-    )(moved)
-
-
-def combine_kernel(home_ref, back_ref, o_ref):
-    width = home_ref.shape[1]
-    back = dot(regroup_matrix(), back_ref[...].reshape(TILE, width))
-    o_ref[...] = (home_ref[...] + back).astype(BF16)
-
-
-def combine(home, back, chunk):
-    tokens_dev = home.shape[0]
-    ctx, per, _, width = back.shape
+    )(place, moved, *waits)
+
+
+def combine_kernel(seat_ref, home_ref, *refs, slots, ctx):
+    back_refs, o_refs, mark_ref = refs[:ctx], refs[-slots - 1 : -1], refs[-1]
+    mark_ref[...] = jnp.zeros_like(mark_ref)
+    tokens_dev, width = home_ref.shape
+    size = tokens_dev // slots
+    per = STRIDE // ctx
+    token = iota2((TILE, TILE), 0)
+    col = iota2((TILE, TILE), 1)
+    group = col >> 4
+    residue = partner(seat_ref[1], group // per, ctx) * per + group % per
+    matrix = (token == (col & 15) * 16 + residue).astype(BF16)
+    for slot in range(slots):
+        owner = partner(seat_ref[0], slot, slots)
+        for b in range(size // TILE):
+            first = owner * (size // TILE) + b
+            here = pl.ds(pl.multiple_of(first * STRIDE, STRIDE), STRIDE)
+            rows = [ref[r, here] for ref in back_refs for r in range(per)]
+            back = dot(matrix, jnp.concatenate(rows))
+            home = home_ref[pl.ds(pl.multiple_of(first * TILE, TILE), TILE)]
+            o_refs[slot][b * TILE : (b + 1) * TILE] = (home + back).astype(BF16)
+
+
+def combine(seat, home, backs, slots, waits):
+    tokens_dev, width = home.shape
+    size = tokens_dev // slots
     return pl.pallas_call(
-        combine_kernel,
-        grid=(tokens_dev // TILE,),
-        in_specs=[
-            pl.BlockSpec((TILE, width), lambda b: (b, chunk)),
-            pl.BlockSpec((ctx, per, TILE // STRIDE, width), lambda b: (0, 0, b, 0)),
-        ],
-        out_specs=pl.BlockSpec((TILE, width), lambda b: (b, 0)),
-        out_shape=jax.ShapeDtypeStruct((tokens_dev, width), BF16),
+        functools.partial(combine_kernel, slots=slots, ctx=len(backs)),
+        in_specs=[pl.BlockSpec(memory_space=pltpu.SMEM)]
+        + [pl.BlockSpec(memory_space=pltpu.VMEM)] * (1 + len(backs))
+        + moments(waits),
+        out_specs=[pl.BlockSpec(memory_space=pltpu.VMEM)] * (slots + 1),
+        out_shape=[jax.ShapeDtypeStruct((size, width), BF16)] * slots + [MARK],
         compiler_params=params(24),
         cost_estimate=cost(2 * tokens_dev * TILE * width, 8 * tokens_dev * width),
         name="combine",
-    )(home, back)
-
-
-def project_kernel(side_ref, *refs, chunks):
-    moved_refs = refs[:chunks]
-    mine_ref, other_ref, o_ref = refs[chunks:]
-
-    def add_up(weight_ref):
+    )(seat, home, *backs, *waits)
+
+
+def project_kernel(side_ref, *refs, slots, chunks):
+    moved_refs, refs = refs[: slots * chunks], refs[slots * chunks :]
+    mine_refs, other_refs, o_ref = refs[:chunks], refs[chunks : 2 * chunks], refs[-1]
+
+    def add_up(weight_refs):
         total = None
-        for group in range(weight_ref.shape[0]):
-            partial_value = None
-            for chunk, ref in enumerate(moved_refs):
-                width = ref.shape[2]
-                part = dot(ref[group], weight_ref[group, chunk * width : (chunk + 1) * width])
-                partial_value = part if partial_value is None else partial_value + part
-            rounded = partial_value.astype(BF16).astype(F32)
-            total = rounded if total is None else total + rounded
-        o_ref[...] = total.astype(BF16)
+        for slot in range(slots):
+            group = partner(side_ref[1], slot, slots)
+            for chunk in range(chunks):
+                part = dot(moved_refs[chunk * slots + slot][...], weight_refs[chunk][group])
+                total = part if total is None else total + part
+        o_ref[...] = total.astype(o_ref.dtype)
 
     @pl.when(pl.program_id(0) == 0)
     def _():
-        add_up(mine_ref)
+        add_up(mine_refs)
 
     @pl.when(pl.program_id(0) == 1)
     def _():
-        add_up(other_ref)
+        add_up(other_refs)
 
 
 def project(side, moved, mine, other):
-    groups, tokens, part = moved[0].shape
-    width, half = mine.shape[1:]
+    chunks, slots = len(moved), len(moved[0])
+    tokens, part = moved[0][0].shape
+    half = mine[0].shape[2]
     tile = min(half, 512)
     tiles = half // tile
+    block = (slots, part, tile)
     return pl.pallas_call(
-        functools.partial(project_kernel, chunks=len(moved)),
+        functools.partial(project_kernel, slots=slots, chunks=chunks),
         grid_spec=pltpu.PrefetchScalarGridSpec(
             num_scalar_prefetch=1,
             grid=(2, tiles),
-            in_specs=[pl.BlockSpec((groups, tokens, part), lambda s, j, side: (0, 0, 0))]
-            * len(moved)
-            + [
-                pl.BlockSpec(
-                    (groups, width, tile),
-                    lambda s, j, side: (0, 0, jnp.where(s == 0, j, tiles - 1)),
-                ),
-                pl.BlockSpec(
-                    (groups, width, tile), lambda s, j, side: (0, 0, jnp.where(s == 0, 0, j))
-                ),
-            ],
+            in_specs=[pl.BlockSpec((tokens, part), lambda s, j, side: (0, 0))] * (slots * chunks)
+            + [pl.BlockSpec(block, lambda s, j, side: (0, 0, jnp.where(s == 0, j, tiles - 1)))]
+            * chunks
+            + [pl.BlockSpec(block, lambda s, j, side: (0, 0, jnp.where(s == 0, 0, j)))] * chunks,
             out_specs=pl.BlockSpec(
                 (tokens, tile), lambda s, j, side: (0, (s ^ side[0]) * tiles + j)
             ),
@@ -307,35 +365,27 @@
         out_shape=jax.ShapeDtypeStruct((tokens, 2 * half), BF16),
         compiler_params=params(40),
         cost_estimate=cost(
-            4 * groups * tokens * width * half,
-            4 * groups * width * half + 2 * groups * tokens * width + 4 * tokens * half,
+            4 * chunks * slots * tokens * part * half,
+            chunks * slots * part * (4 * half + 2 * tokens) + 4 * tokens * half,
         ),
         name="project",
-    )(side, *moved, mine, other)
-
-
-def gathered_order(count):
-    if count & (count - 1):
-        return list(range(count))
-    bits = count.bit_length() - 1
-    return [sum(((i >> b) & 1) << (bits - 1 - b) for b in range(bits)) for i in range(count)]
+    )(side, *[slab for slabs in moved for slab in slabs], *mine, *other)
 
 
 def gather_ctx(rows):
     count = lax.axis_size("ctx")
-    if count & (count - 1):
-        return lax.all_gather(rows, "ctx", axis=1)
-    place = lax.axis_index("ctx")
     held = rows[:, None]
+    steps = []
     distance = count // 2
     while distance:
+        steps.append(distance)
+        distance //= 2
+    order = [0]
+    for distance in steps:
         received = lax.ppermute(held, "ctx", [(i, i ^ distance) for i in range(count)])
-        low = (place & distance) == 0
-        held = jnp.concatenate(
-            [jnp.where(low, held, received), jnp.where(low, received, held)], axis=1
-        )
-        distance //= 2
-    return held
+        held = jnp.concatenate([held, received], axis=1)
+        order = order + [i ^ distance for i in order]
+    return held, order
 
 
 def stride_general(queries, keys, values):
@@ -381,40 +431,70 @@
     sibling = [(i, i ^ 1) for i in range(ctx)]
 
     half = out_weight.shape[1] // 2
-    weight_half = lax.dynamic_slice_in_dim(out_weight, side * half, half, axis=1)
-    mine = lax.all_gather(weight_half, "head", axis=0)
-    other = lax.ppermute(mine, "ctx", sibling)
+    part = width // chunks
+    mine = []
+    for chunk in range(chunks):
+        piece = lax.dynamic_slice(out_weight, (chunk * part, side * half), (part, half))
+        mine.append(lax.all_gather(piece, "head", axis=0))
 
     if ctx > STRIDE:
         stride_out = stride_general(queries, keys, values)
         rim = jnp.stack([keys[tokens_dev - WINDOW :], values[tokens_dev - WINDOW :]])
         picked = jnp.stack([keys, values]).reshape(2, tokens_dev // BLOCK, BLOCK, width)
         picked = picked[:, :, BLOCK - SUMCOLS :].reshape(2, -1, width)
-        send = None
     else:
         *send, rim, picked = prepare(queries, keys, values, ctx, chunks)
-        send = [
+        received = [
             lax.all_to_all(part, "ctx", split_axis=0, concat_axis=0, tiled=True) for part in send
         ]
+    summary, order = gather_ctx(picked)
     before = lax.ppermute(rim, "ctx", [(i, i + 1) for i in range(ctx - 1)])
-    summary = gather_ctx(picked)
-    home = home_sections(place_word, queries, keys, values, before, summary)
-
-    moved = []
-    for chunk in range(chunks):
-        if send is None:
-            attended = (home + stride_out.astype(F32)).astype(BF16)
-        else:
-            result = stride_attend(send[chunk])
-            back = lax.all_to_all(result, "ctx", split_axis=0, concat_axis=0, tiled=True)
-            attended = combine(home, back, chunk)
-        attended = attended.reshape(groups, tokens_dev // groups, width // chunks)
-        moved.append(lax.all_to_all(attended, "head", split_axis=0, concat_axis=0, tiled=True))
-    return project(side.astype(jnp.int32).reshape(1), moved, mine, other)
+
+    def home(chunk, waits):
+        return home_sections(
+            place_word, queries, keys, values, before, summary, order, chunk, chunks, waits
+        )
+
+    seat = lax.axis_index("head").astype(jnp.int32)
+
+    def exchange(slabs, axis):
+        count = len(slabs)
+        moved = [slabs[0]]
+        for slot in range(1, count):
+            pairs = [(i, partner(i, slot, count)) for i in range(count)]
+            moved.append(lax.ppermute(slabs[slot], axis, pairs))
+        return moved
+
+    moved, waits = [], ()
+    if ctx > STRIDE:
+        for chunk in range(chunks):
+            lanes = slice(chunk * part, (chunk + 1) * part)
+            homes, mark = home(chunk, waits)
+            attended = (homes + stride_out[:, lanes].astype(F32)).astype(BF16)
+            attended = attended.reshape(groups, tokens_dev // groups, part)
+            owners = [partner(seat, slot, groups) for slot in range(groups)]
+            moved.append(exchange([attended[owner] for owner in owners], "head"))
+            waits = (mark,)
+    else:
+        seats = jnp.stack([seat, place.astype(jnp.int32)])
+        sections, mark = home(0, ())
+        for chunk in range(chunks):
+            *slabs, mark = stride_attend(place_word, received[chunk], (mark,))
+            backs = exchange(slabs, "ctx")
+            here = sections
+            if chunk < chunks - 1:
+                sections, mark = home(chunk + 1, (mark,))
+            arrived = moved[-1][1:] if moved else []
+            *slabs, mark = combine(seats, here, backs, groups, (mark, *arrived))
+            moved.append(exchange(slabs, "head"))
+    sides = jnp.stack([side.astype(jnp.int32), seat])
+    held = [after(piece, slabs[1:]) for piece, slabs in zip(mine, moved)]
+    other = [lax.ppermute(piece, "ctx", sibling) for piece in held]
+    return project(sides, moved, held, other)
 
 
 def solution(mesh):
-    chunks = 1
+    chunks = 2 if HEADS // mesh.shape["head"] > 1 else 1
     placed = (P("ctx", "head"), P("ctx", "head"), P("ctx", "head"), P("head", None))
     return jax.shard_map(
         functools.partial(body, chunks=chunks),

time: 184 us -> 155 us (0.84); the launches traced: 181 us -> 154 us
  blocking collectives: 30.1 us -> 0 us
  starting transfers between devices: 13.1 us -> 32.9 us
  waiting for transfers between devices: 79.1 us -> 65.5 us
  local copies, waits for them, and re-layouts: 12.1 us -> 6.13 us
  other arithmetic: 2.36 us -> 4.85 us
    all_gather x1 -> x2, waiting for transfers between devices: 67.7 us -> 0.01 us  [body(): mine.append(lax.all_gather(piece, 'head', axis=0))]
    all_to_all x1 -> x0, blocking collectives: 30.1 us -> none  [body(): lax.all_to_all(attended, 'head', split_axis=0, concat_axis=0, tiled=True)]
    ppermute x1 -> x22, waiting for transfers between devices: 0.01 us -> 28.7 us  [the longest x20 21.9 us: exchange(): moved.append(lax.ppermute(slabs[slot], axis, pairs))]
    ppermute x1 -> x22, starting transfers between devices: 0.01 us -> 18.7 us  [the longest x20 18.3 us: exchange(): moved.append(lax.ppermute(slabs[slot], axis, pairs))]
    ppermute x1, waiting for transfers between devices: 0.01 us -> 12.5 us  [body(): before = lax.ppermute(rim, 'ctx', [(i, i + 1) for i in range(ctx - 1)])]
    ppermute x3, waiting for transfers between devices: 11.4 us -> 23.5 us  [gather_ctx(): lax.ppermute(held, 'ctx', [(i, i ^ distance) for i in range(count)])]
    unnamed x26 -> x20, local copies, waits for them, and re-layouts: 11 us -> 3.89 us
    all_to_all x1 -> x2, starting transfers between devices: 4.97 us -> 10.1 us  [body(): lax.all_to_all(part, 'ctx', split_axis=0, concat_axis=0, tiled=True)]
  transfers between devices with their start and end apart: 8 -> 30, of which waited for: 3 -> 15; matrix products, arithmetic and copies ran while one was open for 1% -> 3% of each run, Pallas kernels for 13% -> 16%
where the time goes in v1:
time: 155 us; the launch traced here: 154 us
  waiting for transfers between devices  65.5 us (42%)
  starting transfers between devices  32.9 us (21%)
  Pallas kernels  31.1 us (20%)
  between operations  13.6 us (9%)
  local copies, waits for them, and re-layouts  6.13 us (4%)
  other arithmetic  4.85 us (3%)
    ppermute x3, waiting for transfers between devices, gather_ctx(): lax.ppermute(held, 'ctx', [(i, i ^ distance) for i in range(count)])  23.5 us
    ppermute x20, waiting for transfers between devices, exchange(): moved.append(lax.ppermute(slabs[slot], axis, pairs))  21.9 us
    ppermute x20, starting transfers between devices, exchange(): moved.append(lax.ppermute(slabs[slot], axis, pairs))  18.3 us
    pallas_call x2, Pallas kernels, home_sections(): pl.pallas_call(functools.partial(home_kernel, order=order), grid=(heads,)...  14.2 us
    ppermute x1, waiting for transfers between devices, body(): before = lax.ppermute(rim, 'ctx', [(i, i + 1) for i in range(ctx - 1)])  12.5 us
    all_to_all x2, starting transfers between devices, body(): lax.all_to_all(part, 'ctx', split_axis=0, concat_axis=0, tiled=True)  10.1 us
    ppermute x2, waiting for transfers between devices, body(): other = [lax.ppermute(piece, 'ctx', sibling) for piece in held]  6.78 us
    pallas_call x1, Pallas kernels, project(): pl.pallas_call(functools.partial(project_kernel, slots=slots, chunks=chun...  5.97 us
  transfers between devices with their start and end apart: 30, of which 15 were waited for; matrix products, arithmetic and copies ran while one was open for 3% of the time, Pallas kernels for 16%

profile of v1, /device:TPU:10, one launch (start us, length us, event | category | flops | bytes accessed | tf_op | source)
XLA Modules:
  0.0 154.0 jit_solution(5936396399000756758)
XLA Ops:
  6.5 2.2 %constant_dynamic-slice_fusion = (bf16[256,1024]{1,0:T(8,128)(2,1)}, bf16[256,1024]{1,0:T(8,128)(2,1)}) fusion(bf16[512,2048]{1,0:T(8,128)(2,1)} %param.7, s32[]{:T(128)S(6)} %select_n.12), kind=kLoop, calls=%fused_computation.5 | loop fusion | bytes 2097156 | tf_op jit(solution)/shard_map/dynamic_slice | solution.py:437
  8.8 5.1 %prepare.1 = (bf16[8,3,2,64,256]{4,3,2,1,0:T(8,128)(2,1)}, bf16[8,3,2,64,256]{4,3,2,1,0:T(8,128)(2,1)}, bf16[2,512,512]{2,1,0:T(8,128)(2,1)}, bf16[2,64,512]{2,1,0:T(8,128)(2,1)}) custom-call(bf16[1024,512]{1,0:T(8,128)(2,1)} %q_ref.5, bf16[1024,512]{1,0:T(8,128)(2,1)} %k_ref.5, bf16[1024,512]{1,0:T(8,128)(2,1)} %v_ref.5), custom_call_target="tpu_custom_call" | custom-call | flops 805306368 | bytes 8388608 | tf_op jit(solution)/shard_map/prepare/pallas_call | solution.py:136
  13.9 4.4 %all-to-all-start = ((bf16[8,3,2,64,256]{4,3,2,1,0:T(8,128)(2,1)}), bf16[8,3,2,64,256]{4,3,2,1,0:T(8,128)(2,1)S(1)}, u32[]{:S(2)}, u32[]{:S(2)}) async-start(bf16[8,3,2,64,256]{4,3,2,1,0:T(8,128)(2,1)} %get-tuple-element.43), calls=%async_computation | async-start | bytes 3145728 | tf_op jit(solution)/shard_map/all_to_all | solution.py:448
  18.3 0.7 all-gather.5.cloned.1.call-update
  19.1 1.5 collective-permute-start.1
  20.6 20.1 %collective-permute-done.1 = bf16[2,1,64,512]{3,2,1,0:T(8,128)(2,1)S(1)} collective-permute-done((bf16[2,1,64,512]{3,2,1,0:T(8,128)(2,1)S(1)}, bf16[2,1,64,512]{3,2,1,0:T(8,128)(2,1)S(1)}, u32[]{:S(2)}, u32[]{:S(2)}) %collective-permute-start.1) | collective-permute-done | bytes 131104 | tf_op jit(solution)/shard_map/ppermute | solution.py:385
  40.7 0.7 pad_maximum_fusion.2
  42.0 1.9 %collective-permute-start = (bf16[2,512,512]{2,1,0:T(8,128)(2,1)}, bf16[2,512,512]{2,1,0:T(8,128)(2,1)}, u32[]{:S(2)}, u32[]{:S(2)}) collective-permute-start(bf16[2,512,512]{2,1,0:T(8,128)(2,1)} %get-tuple-element.40), channel_id=1, source_target_pairs={{0,4},{4,8},{8,12},{12,16},{16,20},{20,24},{24,28},{1,5},{5,9},{9,... | collective-permute-start | bytes 3145736 | tf_op jit(solution)/shard_map/ppermute | solution.py:451
  43.9 5.7 %all-to-all-start.1 = ((bf16[8,3,2,64,256]{4,3,2,1,0:T(8,128)(2,1)}), bf16[8,3,2,64,256]{4,3,2,1,0:T(8,128)(2,1)S(1)}, u32[]{:S(2)}, u32[]{:S(2)}) async-start(bf16[8,3,2,64,256]{4,3,2,1,0:T(8,128)(2,1)} %get-tuple-element.60), calls=%async_computation.1 | async-start | bytes 3145728 | tf_op jit(solution)/shard_map/all_to_all | solution.py:448
  49.6 1.2 collective-permute-done.2
  50.9 1.8 %pad_maximum_fusion.1 = bf16[2,4,64,512]{3,2,1,0:T(8,128)(2,1)} fusion(bf16[2,2,64,512]{3,2,1,0:T(8,128)(2,1)} %collective-permute-done.2, bf16[2,1,64,512]{3,2,1,0:T(8,128)(2,1)S(1)} %collective-permute-done.1, bf16[2,1,64,512]{3,2,1,0:T(8,128)(2,1)S(1)} %bitcast.8), kind=kLoop, calls=%fused_computation.1 | loop fusion | flops 524288 | bytes 1048576 | tf_op jit(solution)/shard_map/concatenate | solution.py:386
  52.7 2.2 %collective-permute-done.3 = bf16[2,4,64,512]{3,2,1,0:T(8,128)(2,1)} collective-permute-done((bf16[2,4,64,512]{3,2,1,0:T(8,128)(2,1)}, bf16[2,4,64,512]{3,2,1,0:T(8,128)(2,1)}, u32[]{:S(2)}, u32[]{:S(2)}) %collective-permute-start.3) | collective-permute-done | bytes 524320 | tf_op jit(solution)/shard_map/ppermute | solution.py:385
  54.9 2.2 %pad_maximum_fusion.sum_ref = bf16[2,8,64,512]{3,2,1,0:T(8,128)(2,1)} fusion(bf16[2,4,64,512]{3,2,1,0:T(8,128)(2,1)} %collective-permute-done.3, bf16[2,2,64,512]{3,2,1,0:T(8,128)(2,1)} %collective-permute-done.2, bf16[2,1,64,512]{3,2,1,0:T(8,128)(2,1)S(1)} %collective-permute-done.1, bf16[2,1,64,512]{3,2,1,0:T(8,128)(2,1)S(1)} %bitcast.9), kind=kLoop, calls=%fused_computation | loop fusion | flops 1572864 | bytes 2097152 | tf_op jit(solution)/shard_map/concatenate | solution.py:386
  57.1 12.5 %collective-permute-done.rim_ref = bf16[2,512,512]{2,1,0:T(8,128)(2,1)} collective-permute-done((bf16[2,512,512]{2,1,0:T(8,128)(2,1)}, bf16[2,512,512]{2,1,0:T(8,128)(2,1)}, u32[]{:S(2)}, u32[]{:S(2)}) %collective-permute-start) | collective-permute-done | bytes 1048608 | tf_op jit(solution)/shard_map/ppermute | solution.py:451
  69.6 7.1 %home.2 = (f32[1024,256]{1,0:T(8,128)}, f32[8,128]{1,0:T(8,128)}) custom-call(s32[1]{0:T(128)} %bitcast.2.place_ref, bf16[1024,512]{1,0:T(8,128)(2,1)} %q_ref.5, bf16[1024,512]{1,0:T(8,128)(2,1)} %k_ref.5, bf16[1024,512]{1,0:T(8,128)(2,1)} %v_ref.5, bf16[2,512,512]{2,1,0:T(8,128)(2,1)} %collective-permute-done.rim_ref, ...), custom_call_target="tpu_custom_call" | custom-call | flops 2684354560 | bytes 7340032 | tf_op jit(solution)/shard_map/home/pallas_call | solution.py:214
  76.7 0.7 copy-done.8
  77.4 1.8 %stride.2 = (bf16[2,64,256]{2,1,0:T(8,128)(2,1)S(1)}, bf16[2,64,256]{2,1,0:T(8,128)(2,1)S(1)}, bf16[2,64,256]{2,1,0:T(8,128)(2,1)S(1)}, bf16[2,64,256]{2,1,0:T(8...) custom-call(s32[1]{0:T(128)} %bitcast.2.place_ref, ...), custom_call_target="tpu_custom_call" | custom-call | flops 805306368 | bytes 2097152 | tf_op jit(solution)/shard_map/stride/pallas_call | solution.py:268
  79.3 0.9 collective-permute-start.4
  80.2 0.8 collective-permute-start.5
  81.6 1.4 collective-permute-start.7
  82.9 0.9 collective-permute-done.10.refs_7_
  83.9 2.0 %collective-permute-start.9 = (bf16[2,64,256]{2,1,0:T(8,128)(2,1)S(1)}, bf16[2,64,256]{2,1,0:T(8,128)(2,1)S(1)}, u32[]{:S(2)}, u32[]{:S(2)}) collective-permute-start(bf16[2,64,256]{2,1,0:T(8,128)(2,1)S(1)} %get-tuple-element.51), channel_id=1, source_target_pairs={{0,24},{4,28},{8,16},{12,20},{16,8},{20,12},{24,0},{28,4},{1,25},{... | collective-permute-start | bytes 196616 | tf_op jit(solution)/shard_map/ppermute | solution.py:465
  85.9 7.1 %home.3 = (f32[1024,256]{1,0:T(8,128)}, f32[8,128]{1,0:T(8,128)}) custom-call(s32[1]{0:T(128)} %bitcast.2.place_ref, bf16[1024,512]{1,0:T(8,128)(2,1)} %q_ref.5, bf16[1024,512]{1,0:T(8,128)(2,1)} %k_ref.5, bf16[1024,512]{1,0:T(8,128)(2,1)} %v_ref.5, bf16[2,512,512]{2,1,0:T(8,128)(2,1)} %collective-permute-done.rim_ref, ...), custom_call_target="tpu_custom_call" | custom-call | flops 2684354560 | bytes 7340032 | tf_op jit(solution)/shard_map/home/pallas_call | solution.py:214
  93.0 1.2 copy-done.1
  94.2 0.7 copy-done.6
  94.9 0.8 combine.2
  95.8 0.6 copy-done.2
  96.4 1.8 %stride.3 = (bf16[2,64,256]{2,1,0:T(8,128)(2,1)S(1)}, bf16[2,64,256]{2,1,0:T(8,128)(2,1)S(1)}, bf16[2,64,256]{2,1,0:T(8,128)(2,1)S(1)}, bf16[2,64,256]{2,1,0:T(8...) custom-call(s32[1]{0:T(128)} %bitcast.2.place_ref, ...), custom_call_target="tpu_custom_call" | custom-call | flops 805306368 | bytes 2097152 | tf_op jit(solution)/shard_map/stride/pallas_call | solution.py:268
  98.3 1.3 collective-permute-start.15
  100.2 0.9 collective-permute-start.17
  101.1 0.8 collective-permute-start.18
  102.4 0.6 collective-permute-done.15.refs_2_
  103.1 2.7 %collective-permute-start.12 = (bf16[256,256]{1,0:T(8,128)(2,1)S(1)}, bf16[256,256]{1,0:T(8,128)(2,1)S(1)}, u32[]{:S(2)}, u32[]{:S(2)}) collective-permute-start(bf16[256,256]{1,0:T(8,128)(2,1)S(1)} %get-tuple-element.57), channel_id=1, source_target_pairs={{0,2},{1,3},{2,0},{3,1},{4,6},{5,7},{6,4},{7,5},{8,10},{9,11},{10,... | collective-permute-start | bytes 393224 | tf_op jit(solution)/shard_map/ppermute | solution.py:465
  105.8 0.9 collective-permute-start.19
  106.7 1.2 collective-permute-start.20
  108.0 3.5 %collective-permute-done.19.refs_6_ = bf16[2,64,256]{2,1,0:T(8,128)(2,1)S(1)} collective-permute-done((bf16[2,64,256]{2,1,0:T(8,128)(2,1)S(1)}, bf16[2,64,256]{2,1,0:T(8,128)(2,1)S(1)}, u32[]{:S(2)}, u32[]{:S(2)}) %collective-permute-start.19) | collective-permute-done | bytes 65568 | tf_op jit(solution)/shard_map/ppermute | solution.py:465
  111.4 0.6 collective-permute-done.20.refs_7_
  112.0 3.1 %collective-permute-done.12.refs_10_.refs_2_ = bf16[256,256]{1,0:T(8,128)(2,1)S(1)} collective-permute-done((bf16[256,256]{1,0:T(8,128)(2,1)S(1)}, bf16[256,256]{1,0:T(8,128)(2,1)S(1)}, u32[]{:S(2)}, u32[]{:S(2)}) %collective-permute-start.12) | collective-permute-done | bytes 131104 | tf_op jit(solution)/shard_map/ppermute | solution.py:465
  115.1 2.3 %collective-permute-done.13.refs_11_.refs_3_ = bf16[256,256]{1,0:T(8,128)(2,1)S(1)} collective-permute-done((bf16[256,256]{1,0:T(8,128)(2,1)S(1)}, bf16[256,256]{1,0:T(8,128)(2,1)S(1)}, u32[]{:S(2)}, u32[]{:S(2)}) %collective-permute-start.13) | collective-permute-done | bytes 131104 | tf_op jit(solution)/shard_map/ppermute | solution.py:465
  117.4 1.4 combine.3
  118.8 0.6 copy-done.4
  119.4 3.1 %collective-permute-start.22 = (bf16[256,256]{1,0:T(8,128)(2,1)S(1)}, bf16[256,256]{1,0:T(8,128)(2,1)S(1)}, u32[]{:S(2)}, u32[]{:S(2)}) collective-permute-start(bf16[256,256]{1,0:T(8,128)(2,1)S(1)} %get-tuple-element.73), channel_id=1, source_target_pairs={{0,2},{1,3},{2,0},{3,1},{4,6},{5,7},{6,4},{7,5},{8,10},{9,11},{10,... | collective-permute-start | bytes 393224 | tf_op jit(solution)/shard_map/ppermute | solution.py:465
  122.9 2.9 %collective-permute-done.21.refs_1_.refs_5_ = bf16[256,256]{1,0:T(8,128)(2,1)S(1)} collective-permute-done((bf16[256,256]{1,0:T(8,128)(2,1)S(1)}, bf16[256,256]{1,0:T(8,128)(2,1)S(1)}, u32[]{:S(2)}, u32[]{:S(2)}) %collective-permute-start.21) | collective-permute-done | bytes 131104 | tf_op jit(solution)/shard_map/ppermute | solution.py:465
  125.9 5.0 %collective-permute-done.22.refs_2_.refs_6_ = bf16[256,256]{1,0:T(8,128)(2,1)S(1)} collective-permute-done((bf16[256,256]{1,0:T(8,128)(2,1)S(1)}, bf16[256,256]{1,0:T(8,128)(2,1)S(1)}, u32[]{:S(2)}, u32[]{:S(2)}) %collective-permute-start.22) | collective-permute-done | bytes 131104 | tf_op jit(solution)/shard_map/ppermute | solution.py:465
  130.9 2.9 %collective-permute-done.23.refs_3_.refs_7_ = bf16[256,256]{1,0:T(8,128)(2,1)S(1)} collective-permute-done((bf16[256,256]{1,0:T(8,128)(2,1)S(1)}, bf16[256,256]{1,0:T(8,128)(2,1)S(1)}, u32[]{:S(2)}, u32[]{:S(2)}) %collective-permute-start.23) | collective-permute-done | bytes 131104 | tf_op jit(solution)/shard_map/ppermute | solution.py:465
  134.4 3.8 %collective-permute-done.25.refs_11_ = bf16[4,256,1024]{2,1,0:T(8,128)(2,1)S(1)} collective-permute-done((bf16[4,256,1024]{2,1,0:T(8,128)(2,1)}, bf16[4,256,1024]{2,1,0:T(8,128)(2,1)S(1)}, u32[]{:S(2)}, u32[]{:S(2)}) %collective-permute-start.25) | collective-permute-done | bytes 2097184 | tf_op jit(solution)/shard_map/ppermute | solution.py:492
  138.2 3.0 %collective-permute-done.24.refs_10_ = bf16[4,256,1024]{2,1,0:T(8,128)(2,1)S(1)} collective-permute-done((bf16[4,256,1024]{2,1,0:T(8,128)(2,1)}, bf16[4,256,1024]{2,1,0:T(8,128)(2,1)S(1)}, u32[]{:S(2)}, u32[]{:S(2)}) %collective-permute-start.24) | collective-permute-done | bytes 2097184 | tf_op jit(solution)/shard_map/ppermute | solution.py:492
  141.2 6.0 %project.1 = bf16[256,2048]{1,0:T(8,128)(2,1)} custom-call(s32[2]{0:T(128)S(1)} %pad_add_fusion.side_ref, bf16[256,256]{1,0:T(8,128)(2,1)S(1)} %copy-done.3, bf16[256,256]{1,0:T(8,128)(2,1)S(1)} %collective-permute-done.11.refs_9_.refs_1_, bf16[256,256]{1,0:T(8,128)(2,1)S(1)} %collective-permute-done.12.refs_10_.refs_2_, ...), custom_call_target="tpu_custom_call" | custom-call | flops 2147483648 | bytes 10485760 | tf_op jit(solution)/shard_map/project/pallas_call | solution.py:352
  (50 shorter events, 3.5 us)
Async XLA Ops:
  6.5 127.3 %all-gather.7.cloned.1.call-start = ((), (), s32[]{:S(2)}) async-start(), calls=%async_computation.3 | async-start | bytes 2621440 | tf_op jit(solution)/shard_map/all_gather | solution.py:438
  13.9 5.1 %copy-start.9 = (bf16[2,64,512]{2,1,0:T(8,128)(2,1)S(1)}, bf16[2,64,512]{2,1,0:T(8,128)(2,1)}, u32[]{:S(2)}) copy-start(bf16[2,64,512]{2,1,0:T(8,128)(2,1)} %get-tuple-element.41) | copy-start | bytes 393220
  13.9 29.9 %all-to-all-start = ((bf16[8,3,2,64,256]{4,3,2,1,0:T(8,128)(2,1)}), bf16[8,3,2,64,256]{4,3,2,1,0:T(8,128)(2,1)S(1)}, u32[]{:S(2)}, u32[]{:S(2)}) async-start(bf16[8,3,2,64,256]{4,3,2,1,0:T(8,128)(2,1)} %get-tuple-element.43), calls=%async_computation | async-start | bytes 3145728 | tf_op jit(solution)/shard_map/all_to_all | solution.py:448
  18.3 115.5 %all-gather.5.cloned.1.call-start = ((), (), s32[]{:S(2)}) async-start(), calls=%async_computation.2 | async-start | bytes 2621440 | tf_op jit(solution)/shard_map/all_gather | solution.py:438
  19.1 21.6 %collective-permute-start.1 = (bf16[2,1,64,512]{3,2,1,0:T(8,128)(2,1)S(1)}, bf16[2,1,64,512]{3,2,1,0:T(8,128)(2,1)S(1)}, u32[]{:S(2)}, u32[]{:S(2)}) collective-permute-start(bf16[2,1,64,512]{3,2,1,0:T(8,128)(2,1)S(1)} %bitcast.6), channel_id=1, source_target_pairs={{0,16},{4,20},{8,24},{12,28},{16,0},{20,4},{24,8},{28,12},{1,17},{... | collective-permute-start | bytes 393224 | tf_op jit(solution)/shard_map/ppermute | solution.py:385
  41.4 9.5 %collective-permute-start.2 = (bf16[2,2,64,512]{3,2,1,0:T(8,128)(2,1)}, bf16[2,2,64,512]{3,2,1,0:T(8,128)(2,1)}, u32[]{:S(2)}, u32[]{:S(2)}) collective-permute-start(bf16[2,2,64,512]{3,2,1,0:T(8,128)(2,1)} %pad_maximum_fusion.2), channel_id=1, source_target_pairs={{0,8},{4,12},{8,0},{12,4},{16,24},{20,28},{24,16},{28,20},{1,9},{5... | collective-permute-start | bytes 786440 | tf_op jit(solution)/shard_map/ppermute | solution.py:385
  42.0 27.7 %collective-permute-start = (bf16[2,512,512]{2,1,0:T(8,128)(2,1)}, bf16[2,512,512]{2,1,0:T(8,128)(2,1)}, u32[]{:S(2)}, u32[]{:S(2)}) collective-permute-start(bf16[2,512,512]{2,1,0:T(8,128)(2,1)} %get-tuple-element.40), channel_id=1, source_target_pairs={{0,4},{4,8},{8,12},{12,16},{16,20},{20,24},{24,28},{1,5},{5,9},{9,... | collective-permute-start | bytes 3145736 | tf_op jit(solution)/shard_map/ppermute | solution.py:451
  43.9 52.6 %all-to-all-start.1 = ((bf16[8,3,2,64,256]{4,3,2,1,0:T(8,128)(2,1)}), bf16[8,3,2,64,256]{4,3,2,1,0:T(8,128)(2,1)S(1)}, u32[]{:S(2)}, u32[]{:S(2)}) async-start(bf16[8,3,2,64,256]{4,3,2,1,0:T(8,128)(2,1)} %get-tuple-element.60), calls=%async_computation.1 | async-start | bytes 3145728 | tf_op jit(solution)/shard_map/all_to_all | solution.py:448
  52.7 2.3 %collective-permute-start.3 = (bf16[2,4,64,512]{3,2,1,0:T(8,128)(2,1)}, bf16[2,4,64,512]{3,2,1,0:T(8,128)(2,1)}, u32[]{:S(2)}, u32[]{:S(2)}) collective-permute-start(bf16[2,4,64,512]{3,2,1,0:T(8,128)(2,1)} %pad_maximum_fusion.1), channel_id=1, source_target_pairs={{0,4},{4,0},{8,12},{12,8},{16,20},{20,16},{24,28},{28,24},{1,5},{5... | collective-permute-start | bytes 1572872 | tf_op jit(solution)/shard_map/ppermute | solution.py:385
  76.7 0.7 copy-start.8
  79.2 6.7 %copy-start.7 = (f32[8,128]{1,0:T(8,128)}, f32[8,128]{1,0:T(8,128)S(1)}, u32[]{:S(2)}) copy-start(f32[8,128]{1,0:T(8,128)S(1)} %get-tuple-element.53.refs_0_) | copy-start | bytes 12292
  79.2 4.7 %collective-permute-start.10 = (bf16[2,64,256]{2,1,0:T(8,128)(2,1)S(1)}, bf16[2,64,256]{2,1,0:T(8,128)(2,1)S(1)}, u32[]{:S(2)}, u32[]{:S(2)}) collective-permute-start(bf16[2,64,256]{2,1,0:T(8,128)(2,1)S(1)} %get-tuple-element.52), channel_id=1, source_target_pairs={{0,28},{4,24},{8,20},{12,16},{16,12},{20,8},{24,4},{28,0},{1,29},{... | collective-permute-start | bytes 196616 | tf_op jit(solution)/shard_map/ppermute | solution.py:465
  79.3 4.6 %collective-permute-start.4 = (bf16[2,64,256]{2,1,0:T(8,128)(2,1)S(1)}, bf16[2,64,256]{2,1,0:T(8,128)(2,1)S(1)}, u32[]{:S(2)}, u32[]{:S(2)}) collective-permute-start(bf16[2,64,256]{2,1,0:T(8,128)(2,1)S(1)} %get-tuple-element.46), channel_id=1, source_target_pairs={{0,4},{4,0},{8,12},{12,8},{16,20},{20,16},{24,28},{28,24},{1,5},{5... | collective-permute-start | bytes 196616 | tf_op jit(solution)/shard_map/ppermute | solution.py:465
  80.2 12.8 %collective-permute-start.5 = (bf16[2,64,256]{2,1,0:T(8,128)(2,1)S(1)}, bf16[2,64,256]{2,1,0:T(8,128)(2,1)S(1)}, u32[]{:S(2)}, u32[]{:S(2)}) collective-permute-start(bf16[2,64,256]{2,1,0:T(8,128)(2,1)S(1)} %get-tuple-element.47), channel_id=1, source_target_pairs={{0,8},{4,12},{8,0},{12,4},{16,24},{20,28},{24,16},{28,20},{1,9},{5... | collective-permute-start | bytes 196616 | tf_op jit(solution)/shard_map/ppermute | solution.py:465
  81.0 12.0 %collective-permute-start.6 = (bf16[2,64,256]{2,1,0:T(8,128)(2,1)S(1)}, bf16[2,64,256]{2,1,0:T(8,128)(2,1)S(1)}, u32[]{:S(2)}, u32[]{:S(2)}) collective-permute-start(bf16[2,64,256]{2,1,0:T(8,128)(2,1)S(1)} %get-tuple-element.48), channel_id=1, source_target_pairs={{0,12},{4,8},{8,4},{12,0},{16,28},{20,24},{24,20},{28,16},{1,13},{... | collective-permute-start | bytes 196616 | tf_op jit(solution)/shard_map/ppermute | solution.py:465
  81.6 11.4 %collective-permute-start.7 = (bf16[2,64,256]{2,1,0:T(8,128)(2,1)S(1)}, bf16[2,64,256]{2,1,0:T(8,128)(2,1)S(1)}, u32[]{:S(2)}, u32[]{:S(2)}) collective-permute-start(bf16[2,64,256]{2,1,0:T(8,128)(2,1)S(1)} %get-tuple-element.49), channel_id=1, source_target_pairs={{0,16},{4,20},{8,24},{12,28},{16,0},{20,4},{24,8},{28,12},{1,17},{... | collective-permute-start | bytes 196616 | tf_op jit(solution)/shard_map/ppermute | solution.py:465
  83.8 9.1 %collective-permute-start.8 = (bf16[2,64,256]{2,1,0:T(8,128)(2,1)S(1)}, bf16[2,64,256]{2,1,0:T(8,128)(2,1)S(1)}, u32[]{:S(2)}, u32[]{:S(2)}) collective-permute-start(bf16[2,64,256]{2,1,0:T(8,128)(2,1)S(1)} %get-tuple-element.50), channel_id=1, source_target_pairs={{0,20},{4,16},{8,28},{12,24},{16,4},{20,0},{24,12},{28,8},{1,21},{... | collective-permute-start | bytes 196616 | tf_op jit(solution)/shard_map/ppermute | solution.py:465
  83.9 9.1 %collective-permute-start.9 = (bf16[2,64,256]{2,1,0:T(8,128)(2,1)S(1)}, bf16[2,64,256]{2,1,0:T(8,128)(2,1)S(1)}, u32[]{:S(2)}, u32[]{:S(2)}) collective-permute-start(bf16[2,64,256]{2,1,0:T(8,128)(2,1)S(1)} %get-tuple-element.51), channel_id=1, source_target_pairs={{0,24},{4,28},{8,16},{12,20},{16,8},{20,12},{24,0},{28,4},{1,25},{... | collective-permute-start | bytes 196616 | tf_op jit(solution)/shard_map/ppermute | solution.py:465
  93.0 1.2 copy-start.1
  94.2 0.7 copy-start.6
  94.9 22.5 %copy-start = (f32[1024,256]{1,0:T(8,128)S(1)}, f32[1024,256]{1,0:T(8,128)}, u32[]{:S(2)}) copy-start(f32[1024,256]{1,0:T(8,128)} %get-tuple-element.59.home_ref) | copy-start | bytes 3145732
  95.8 0.7 copy-start.2
  98.2 3.6 %collective-permute-start.14 = (bf16[2,64,256]{2,1,0:T(8,128)(2,1)S(1)}, bf16[2,64,256]{2,1,0:T(8,128)(2,1)S(1)}, u32[]{:S(2)}, u32[]{:S(2)}) collective-permute-start(bf16[2,64,256]{2,1,0:T(8,128)(2,1)S(1)} %get-tuple-element.63), channel_id=1, source_target_pairs={{0,4},{4,0},{8,12},{12,8},{16,20},{20,16},{24,28},{28,24},{1,5},{5... | collective-permute-start | bytes 196616 | tf_op jit(solution)/shard_map/ppermute | solution.py:465
  98.3 4.8 %collective-permute-start.15 = (bf16[2,64,256]{2,1,0:T(8,128)(2,1)S(1)}, bf16[2,64,256]{2,1,0:T(8,128)(2,1)S(1)}, u32[]{:S(2)}, u32[]{:S(2)}) collective-permute-start(bf16[2,64,256]{2,1,0:T(8,128)(2,1)S(1)} %get-tuple-element.64), channel_id=1, source_target_pairs={{0,8},{4,12},{8,0},{12,4},{16,24},{20,28},{24,16},{28,20},{1,9},{5... | collective-permute-start | bytes 196616 | tf_op jit(solution)/shard_map/ppermute | solution.py:465
  99.6 6.2 %collective-permute-start.16 = (bf16[2,64,256]{2,1,0:T(8,128)(2,1)S(1)}, bf16[2,64,256]{2,1,0:T(8,128)(2,1)S(1)}, u32[]{:S(2)}, u32[]{:S(2)}) collective-permute-start(bf16[2,64,256]{2,1,0:T(8,128)(2,1)S(1)} %get-tuple-element.65), channel_id=1, source_target_pairs={{0,12},{4,8},{8,4},{12,0},{16,28},{20,24},{24,20},{28,16},{1,13},{... | collective-permute-start | bytes 196616 | tf_op jit(solution)/shard_map/ppermute | solution.py:465
  100.2 5.6 %collective-permute-start.17 = (bf16[2,64,256]{2,1,0:T(8,128)(2,1)S(1)}, bf16[2,64,256]{2,1,0:T(8,128)(2,1)S(1)}, u32[]{:S(2)}, u32[]{:S(2)}) collective-permute-start(bf16[2,64,256]{2,1,0:T(8,128)(2,1)S(1)} %get-tuple-element.66), channel_id=1, source_target_pairs={{0,16},{4,20},{8,24},{12,28},{16,0},{20,4},{24,8},{28,12},{1,17},{... | collective-permute-start | bytes 196616 | tf_op jit(solution)/shard_map/ppermute | solution.py:465
  101.1 5.7 %collective-permute-start.18 = (bf16[2,64,256]{2,1,0:T(8,128)(2,1)S(1)}, bf16[2,64,256]{2,1,0:T(8,128)(2,1)S(1)}, u32[]{:S(2)}, u32[]{:S(2)}) collective-permute-start(bf16[2,64,256]{2,1,0:T(8,128)(2,1)S(1)} %get-tuple-element.67), channel_id=1, source_target_pairs={{0,20},{4,16},{8,28},{12,24},{16,4},{20,0},{24,12},{28,8},{1,21},{... | collective-permute-start | bytes 196616 | tf_op jit(solution)/shard_map/ppermute | solution.py:465
  101.9 10.2 %collective-permute-start.11 = (bf16[256,256]{1,0:T(8,128)(2,1)S(1)}, bf16[256,256]{1,0:T(8,128)(2,1)S(1)}, u32[]{:S(2)}, u32[]{:S(2)}) collective-permute-start(bf16[256,256]{1,0:T(8,128)(2,1)S(1)} %get-tuple-element.56), channel_id=1, source_target_pairs={{0,1},{1,0},{2,3},{3,2},{4,5},{5,4},{6,7},{7,6},{8,9},{9,8},{10,11... | collective-permute-start | bytes 393224 | tf_op jit(solution)/shard_map/ppermute | solution.py:465
  103.1 12.0 %collective-permute-start.12 = (bf16[256,256]{1,0:T(8,128)(2,1)S(1)}, bf16[256,256]{1,0:T(8,128)(2,1)S(1)}, u32[]{:S(2)}, u32[]{:S(2)}) collective-permute-start(bf16[256,256]{1,0:T(8,128)(2,1)S(1)} %get-tuple-element.57), channel_id=1, source_target_pairs={{0,2},{1,3},{2,0},{3,1},{4,6},{5,7},{6,4},{7,5},{8,10},{9,11},{10,... | collective-permute-start | bytes 393224 | tf_op jit(solution)/shard_map/ppermute | solution.py:465
  105.8 11.6 %collective-permute-start.13 = (bf16[256,256]{1,0:T(8,128)(2,1)S(1)}, bf16[256,256]{1,0:T(8,128)(2,1)S(1)}, u32[]{:S(2)}, u32[]{:S(2)}) collective-permute-start(bf16[256,256]{1,0:T(8,128)(2,1)S(1)} %get-tuple-element.58), channel_id=1, source_target_pairs={{0,3},{1,2},{2,1},{3,0},{4,7},{5,6},{6,5},{7,4},{8,11},{9,10},{10,... | collective-permute-start | bytes 393224 | tf_op jit(solution)/shard_map/ppermute | solution.py:465
  105.8 5.6 %collective-permute-start.19 = (bf16[2,64,256]{2,1,0:T(8,128)(2,1)S(1)}, bf16[2,64,256]{2,1,0:T(8,128)(2,1)S(1)}, u32[]{:S(2)}, u32[]{:S(2)}) collective-permute-start(bf16[2,64,256]{2,1,0:T(8,128)(2,1)S(1)} %get-tuple-element.68), channel_id=1, source_target_pairs={{0,24},{4,28},{8,16},{12,20},{16,8},{20,12},{24,0},{28,4},{1,25},{... | collective-permute-start | bytes 196616 | tf_op jit(solution)/shard_map/ppermute | solution.py:465
  106.7 5.3 %collective-permute-start.20 = (bf16[2,64,256]{2,1,0:T(8,128)(2,1)S(1)}, bf16[2,64,256]{2,1,0:T(8,128)(2,1)S(1)}, u32[]{:S(2)}, u32[]{:S(2)}) collective-permute-start(bf16[2,64,256]{2,1,0:T(8,128)(2,1)S(1)} %get-tuple-element.69), channel_id=1, source_target_pairs={{0,28},{4,24},{8,20},{12,16},{16,12},{20,8},{24,4},{28,0},{1,29},{... | collective-permute-start | bytes 196616 | tf_op jit(solution)/shard_map/ppermute | solution.py:465
  118.8 0.6 copy-start.4
  119.4 6.4 %collective-permute-start.21 = (bf16[256,256]{1,0:T(8,128)(2,1)S(1)}, bf16[256,256]{1,0:T(8,128)(2,1)S(1)}, u32[]{:S(2)}, u32[]{:S(2)}) collective-permute-start(bf16[256,256]{1,0:T(8,128)(2,1)S(1)} %get-tuple-element.72), channel_id=1, source_target_pairs={{0,1},{1,0},{2,3},{3,2},{4,5},{5,4},{6,7},{7,6},{8,9},{9,8},{10,11... | collective-permute-start | bytes 393224 | tf_op jit(solution)/shard_map/ppermute | solution.py:465
  119.4 11.5 %collective-permute-start.22 = (bf16[256,256]{1,0:T(8,128)(2,1)S(1)}, bf16[256,256]{1,0:T(8,128)(2,1)S(1)}, u32[]{:S(2)}, u32[]{:S(2)}) collective-permute-start(bf16[256,256]{1,0:T(8,128)(2,1)S(1)} %get-tuple-element.73), channel_id=1, source_target_pairs={{0,2},{1,3},{2,0},{3,1},{4,6},{5,7},{6,4},{7,5},{8,10},{9,11},{10,... | collective-permute-start | bytes 393224 | tf_op jit(solution)/shard_map/ppermute | solution.py:465
  122.5 11.3 %collective-permute-start.23 = (bf16[256,256]{1,0:T(8,128)(2,1)S(1)}, bf16[256,256]{1,0:T(8,128)(2,1)S(1)}, u32[]{:S(2)}, u32[]{:S(2)}) collective-permute-start(bf16[256,256]{1,0:T(8,128)(2,1)S(1)} %get-tuple-element.74), channel_id=1, source_target_pairs={{0,3},{1,2},{2,1},{3,0},{4,7},{5,6},{6,5},{7,4},{8,11},{9,10},{10,... | collective-permute-start | bytes 393224 | tf_op jit(solution)/shard_map/ppermute | solution.py:465
  133.8 4.4 %collective-permute-start.25 = (bf16[4,256,1024]{2,1,0:T(8,128)(2,1)}, bf16[4,256,1024]{2,1,0:T(8,128)(2,1)S(1)}, u32[]{:S(2)}, u32[]{:S(2)}) collective-permute-start(bf16[4,256,1024]{2,1,0:T(8,128)(2,1)} %after.3.refs_9_), channel_id=1, source_target_pairs={{0,4},{4,0},{8,12},{12,8},{16,20},{20,16},{24,28},{28,24},{1,5},{5... | collective-permute-start | bytes 6291464 | tf_op jit(solution)/shard_map/ppermute | solution.py:492
  133.9 7.3 %copy-start.3 = (bf16[256,256]{1,0:T(8,128)(2,1)S(1)}, bf16[256,256]{1,0:T(8,128)(2,1)}, u32[]{:S(2)}) copy-start(bf16[256,256]{1,0:T(8,128)(2,1)} %copy-done.2) | copy-start | bytes 393220
  133.9 7.3 %copy-start.5 = (bf16[256,256]{1,0:T(8,128)(2,1)S(1)}, bf16[256,256]{1,0:T(8,128)(2,1)}, u32[]{:S(2)}) copy-start(bf16[256,256]{1,0:T(8,128)(2,1)} %copy-done.4) | copy-start | bytes 393220
  133.9 7.3 %collective-permute-start.24 = (bf16[4,256,1024]{2,1,0:T(8,128)(2,1)}, bf16[4,256,1024]{2,1,0:T(8,128)(2,1)S(1)}, u32[]{:S(2)}, u32[]{:S(2)}) collective-permute-start(bf16[4,256,1024]{2,1,0:T(8,128)(2,1)} %after.2.refs_8_), channel_id=1, source_target_pairs={{0,4},{4,0},{8,12},{12,8},{16,20},{20,16},{24,28},{28,24},{1,5},{5... | collective-permute-start | bytes 6291464 | tf_op jit(solution)/shard_map/ppermute | solution.py:492
Sparse Core Ops, SparseCore 0:
  8.9 45.4 all-gather.6
  56.0 44.6 all-gather.4

commit v2 on v1

--- a/solution.py
+++ b/solution.py
@@ -45,7 +45,7 @@
         out_specs=anywhere,
         out_shape=jax.ShapeDtypeStruct(array.shape, array.dtype),
         input_output_aliases={0: 0},
-        compiler_params=params(2),
+        compiler_params=params(24),
         cost_estimate=cost(0, 0),
         name="after",
     )(array, *others)
@@ -100,64 +100,65 @@
     return total[:, :HEAD_SIZE] / total[:, HEAD_SIZE:]
 
 
-def prep_kernel(q_ref, k_ref, v_ref, *refs, rim_start, chunks):
-    send_refs, rim_ref, sum_ref = refs[:chunks], refs[chunks], refs[chunks + 1]
-    step = pl.program_id(0)
+def prep_kernel(q_ref, k_ref, v_ref, *refs, rim_start, whole):
+    send_ref = refs[2] if whole else refs[-1]
     matrix = regroup_matrix()
-    ctx, _, per, rows, width = send_refs[0].shape
+    ctx, _, per, rows, width = send_ref.shape
     for number, ref in enumerate((q_ref, k_ref, v_ref)):
         grouped = dot(matrix, ref[...]).astype(BF16)
-        for chunk in range(chunks):
-            send_refs[chunk][:, number] = grouped[:, chunk * width : (chunk + 1) * width].reshape(
-                ctx, per, rows, width
-            )
+        send_ref[:, number] = grouped.reshape(ctx, per, rows, width)
+    if not whole:
+        return
+    all_keys, all_values, _, rim_ref, sum_ref = refs
     picks = TILE // BLOCK * SUMCOLS
     row = iota2((picks, TILE), 0)
     col = iota2((picks, TILE), 1)
     pick = (col == (row // SUMCOLS) * BLOCK + BLOCK - SUMCOLS + row % SUMCOLS).astype(BF16)
-    sum_ref[0] = dot(pick, k_ref[...]).astype(BF16)
-    sum_ref[1] = dot(pick, v_ref[...]).astype(BF16)
-
-    @pl.when(step >= rim_start)
+    sum_ref[0] = dot(pick, all_keys[...]).astype(BF16)
+    sum_ref[1] = dot(pick, all_values[...]).astype(BF16)
+
+    @pl.when(pl.program_id(0) >= rim_start)
     def _():
-        rim_ref[0] = k_ref[...]
-        rim_ref[1] = v_ref[...]
-
-
-def prepare(queries, keys, values, ctx, chunks):
+        rim_ref[0] = all_keys[...]
+        rim_ref[1] = all_values[...]
+
+
+def prepare(queries, keys, values, ctx, chunk, chunks, waits):
     tokens_dev, width = queries.shape
+    whole = chunk == chunks - 1
     tiles = tokens_dev // TILE
     per = STRIDE // ctx
     rows = tokens_dev // STRIDE
     part = width // chunks
     rim_start = tiles - WINDOW // TILE
     picks = TILE // BLOCK * SUMCOLS
-    source = pl.BlockSpec((TILE, width), lambda b: (b, 0))
-    return pl.pallas_call(
-        functools.partial(prep_kernel, rim_start=rim_start, chunks=chunks),
-        grid=(tiles,),
-        in_specs=[source] * 3,
-        out_specs=[
-            pl.BlockSpec((ctx, 3, per, TILE // STRIDE, part), lambda b: (0, 0, 0, b, 0))
-        ]
-        * chunks
-        + [
+    source = pl.BlockSpec((TILE, part), lambda b: (b, chunk))
+    full = pl.BlockSpec((TILE, width), lambda b: (b, 0))
+    out_specs = [pl.BlockSpec((ctx, 3, per, TILE // STRIDE, part), lambda b: (0, 0, 0, b, 0))]
+    out_shape = [jax.ShapeDtypeStruct((ctx, 3, per, rows, part), BF16)]
+    if whole:
+        out_specs += [
             pl.BlockSpec((2, TILE, width), lambda b: (0, jnp.maximum(b - rim_start, 0), 0)),
             pl.BlockSpec((2, picks, width), lambda b: (0, b, 0)),
-        ],
-        out_shape=[jax.ShapeDtypeStruct((ctx, 3, per, rows, part), BF16)] * chunks
-        + [
+        ]
+        out_shape += [
             jax.ShapeDtypeStruct((2, WINDOW, width), BF16),
             jax.ShapeDtypeStruct((2, tiles * picks, width), BF16),
-        ],
+        ]
+    return pl.pallas_call(
+        functools.partial(prep_kernel, rim_start=rim_start, whole=whole),
+        grid=(tiles,),
+        in_specs=[source] * 3 + [full] * 2 * whole,
+        out_specs=out_specs,
+        out_shape=out_shape,
         compiler_params=params(60),
-        cost_estimate=cost(6 * tokens_dev * TILE * width, 16 * tokens_dev * width),
+        cost_estimate=cost(6 * tokens_dev * TILE * part, 16 * tokens_dev * part),
         name="prepare",
-    )(queries, keys, values)
-
-
-def home_kernel(place_ref, q_ref, k_ref, v_ref, rim_ref, sum_ref, *refs, order):
-    o_ref, mark_ref = refs[-2:]
+    )(queries, keys, values, *([keys, values] * whole))
+
+
+def home_kernel(place_ref, q_ref, k_ref, v_ref, rim_ref, *refs, order):
+    sum_refs, (o_ref, mark_ref) = refs[: len(order)], refs[-2:]
     mark_ref[...] = jnp.zeros_like(mark_ref)
     place = place_ref[0]
     tokens_dev = q_ref.shape[0]
@@ -167,9 +168,9 @@
     for e in range(tokens_dev // TILE):
         key_blocks.append(k_ref[e * TILE : (e + 1) * TILE])
         value_blocks.append(with_ones(v_ref[e * TILE : (e + 1) * TILE]))
-    pieces, picks = sum_ref.shape[1:3]
-    sum_keys = sum_ref[0].reshape(pieces * picks, HEAD_SIZE)
-    sum_values = with_ones(sum_ref[1].reshape(pieces * picks, HEAD_SIZE))
+    picks = sum_refs[0].shape[1]
+    sum_keys = jnp.concatenate([ref[0] for ref in sum_refs])
+    sum_values = with_ones(jnp.concatenate([ref[1] for ref in sum_refs]))
     sum_col = jnp.concatenate(
         [iota2((TILE, picks), 1) + (place ^ i) * picks for i in order], axis=1
     )
@@ -207,8 +208,8 @@
     tokens_dev, width = queries.shape
     heads = width // chunks // HEAD_SIZE
     first = chunk * heads
-    pieces, picks = summary.shape[1:3]
-    total = pieces * picks
+    picks = summary[0].shape[1]
+    total = len(summary) * picks
     own = pl.BlockSpec((tokens_dev, HEAD_SIZE), lambda h: (0, first + h))
     pairs = tokens_dev * (WINDOW + TILE + total) * heads
     return pl.pallas_call(
@@ -220,15 +221,15 @@
             own,
             own,
             pl.BlockSpec((2, WINDOW, HEAD_SIZE), lambda h: (0, 0, first + h)),
-            pl.BlockSpec((2, pieces, picks, HEAD_SIZE), lambda h: (0, 0, 0, first + h)),
         ]
+        + [pl.BlockSpec((2, picks, HEAD_SIZE), lambda h: (0, 0, first + h))] * len(summary)
         + moments(waits),
         out_specs=[pl.BlockSpec((tokens_dev, HEAD_SIZE), lambda h: (0, h)), mark_spec()],
         out_shape=[jax.ShapeDtypeStruct((tokens_dev, heads * HEAD_SIZE), F32), MARK],
-        compiler_params=params(60),
+        compiler_params=params(24),
         cost_estimate=cost(8 * pairs * HEAD_SIZE, 14 * tokens_dev * width, pairs),
         name="home",
-    )(place, queries, keys, values, rim, summary, *waits)
+    )(place, queries, keys, values, rim, *summary, *waits)
 
 
 def stride_kernel(place_ref, x_ref, *refs):
@@ -321,71 +322,55 @@
 
 
 def project_kernel(side_ref, *refs, slots, chunks):
-    moved_refs, refs = refs[: slots * chunks], refs[slots * chunks :]
-    mine_refs, other_refs, o_ref = refs[:chunks], refs[chunks : 2 * chunks], refs[-1]
-
-    def add_up(weight_refs):
-        total = None
-        for slot in range(slots):
-            group = partner(side_ref[1], slot, slots)
-            for chunk in range(chunks):
-                part = dot(moved_refs[chunk * slots + slot][...], weight_refs[chunk][group])
-                total = part if total is None else total + part
-        o_ref[...] = total.astype(o_ref.dtype)
-
-    @pl.when(pl.program_id(0) == 0)
-    def _():
-        add_up(mine_refs)
-
-    @pl.when(pl.program_id(0) == 1)
-    def _():
-        add_up(other_refs)
-
-
-def project(side, moved, mine, other):
+    moved_refs, weight_refs = refs[: slots * chunks], refs[slots * chunks : (slots + 1) * chunks]
+    total = None
+    for slot in range(slots):
+        group = partner(side_ref[1], slot, slots)
+        for chunk in range(chunks):
+            part = dot(moved_refs[chunk * slots + slot][...], weight_refs[chunk][group])
+            total = part if total is None else total + part
+    refs[-1][...] = total.astype(BF16)
+
+
+def project(side, moved, weights, result):
     chunks, slots = len(moved), len(moved[0])
     tokens, part = moved[0][0].shape
-    half = mine[0].shape[2]
-    tile = min(half, 512)
+    half = weights[0].shape[2]
+    tile = min(half, 256)
     tiles = half // tile
-    block = (slots, part, tile)
+    later = 0 if result is None else 1
     return pl.pallas_call(
         functools.partial(project_kernel, slots=slots, chunks=chunks),
         grid_spec=pltpu.PrefetchScalarGridSpec(
             num_scalar_prefetch=1,
-            grid=(2, tiles),
-            in_specs=[pl.BlockSpec((tokens, part), lambda s, j, side: (0, 0))] * (slots * chunks)
-            + [pl.BlockSpec(block, lambda s, j, side: (0, 0, jnp.where(s == 0, j, tiles - 1)))]
-            * chunks
-            + [pl.BlockSpec(block, lambda s, j, side: (0, 0, jnp.where(s == 0, 0, j)))] * chunks,
+            grid=(tiles,),
+            in_specs=[pl.BlockSpec((tokens, part), lambda j, side: (0, 0))] * (slots * chunks)
+            + [pl.BlockSpec((slots, part, tile), lambda j, side: (0, 0, j))] * chunks
+            + [pl.BlockSpec(memory_space=pl.ANY)] * later,
             out_specs=pl.BlockSpec(
-                (tokens, tile), lambda s, j, side: (0, (s ^ side[0]) * tiles + j)
+                (tokens, tile), lambda j, side: (0, (side[0] ^ later) * tiles + j)
             ),
         ),
         out_shape=jax.ShapeDtypeStruct((tokens, 2 * half), BF16),
-        compiler_params=params(40),
+        input_output_aliases={1 + (slots + 1) * chunks: 0} if later else {},
+        compiler_params=params(24),
         cost_estimate=cost(
-            4 * chunks * slots * tokens * part * half,
-            chunks * slots * part * (4 * half + 2 * tokens) + 4 * tokens * half,
+            2 * chunks * slots * tokens * part * half,
+            chunks * slots * part * 2 * (half + tokens) + 2 * tokens * half,
         ),
         name="project",
-    )(side, *[slab for slabs in moved for slab in slabs], *mine, *other)
+    )(side, *[slab for slabs in moved for slab in slabs], *weights, *([result] * later))
 
 
 def gather_ctx(rows):
     count = lax.axis_size("ctx")
-    held = rows[:, None]
-    steps = []
-    distance = count // 2
-    while distance:
-        steps.append(distance)
-        distance //= 2
-    order = [0]
-    for distance in steps:
-        received = lax.ppermute(held, "ctx", [(i, i ^ distance) for i in range(count)])
-        held = jnp.concatenate([held, received], axis=1)
-        order = order + [i ^ distance for i in order]
-    return held, order
+
+    def swapped(piece, distance):
+        return lax.ppermute(piece, "ctx", [(i, i ^ distance) for i in range(count)])
+
+    order = list(range(0, count, 2))
+    pieces = [rows] + [swapped(rows, distance) for distance in order[1:]]
+    return pieces + [swapped(piece, 1) for piece in pieces], order + [i ^ 1 for i in order]
 
 
 def stride_general(queries, keys, values):
@@ -443,7 +428,11 @@
         picked = jnp.stack([keys, values]).reshape(2, tokens_dev // BLOCK, BLOCK, width)
         picked = picked[:, :, BLOCK - SUMCOLS :].reshape(2, -1, width)
     else:
-        *send, rim, picked = prepare(queries, keys, values, ctx, chunks)
+        send = []
+        for chunk in range(chunks):
+            part_send, *rest = prepare(queries, keys, values, ctx, chunk, chunks, ())
+            send.append(part_send)
+        rim, picked = rest
         received = [
             lax.all_to_all(part, "ctx", split_axis=0, concat_axis=0, tiled=True) for part in send
         ]
@@ -465,7 +454,13 @@
             moved.append(lax.ppermute(slabs[slot], axis, pairs))
         return moved
 
-    moved, waits = [], ()
+    held, other = [], []
+
+    def swap(chunk, others):
+        held.append(after(mine[chunk], others))
+        other.append(lax.ppermute(held[-1], "ctx", sibling))
+
+    moved, waits, arrived = [], (), ()
     if ctx > STRIDE:
         for chunk in range(chunks):
             lanes = slice(chunk * part, (chunk + 1) * part)
@@ -475,22 +470,31 @@
             owners = [partner(seat, slot, groups) for slot in range(groups)]
             moved.append(exchange([attended[owner] for owner in owners], "head"))
             waits = (mark,)
+            if chunk < chunks - 1:
+                swap(chunk, waits)
     else:
         seats = jnp.stack([seat, place.astype(jnp.int32)])
-        sections, mark = home(0, ())
+        homes, backs = [], []
         for chunk in range(chunks):
-            *slabs, mark = stride_attend(place_word, received[chunk], (mark,))
-            backs = exchange(slabs, "ctx")
-            here = sections
+            *slabs, mark = stride_attend(place_word, received[chunk], waits)
+            backs.append(exchange(slabs, "ctx"))
+            waits = (mark,)
+            for ready in range(chunk, chunks if chunk == chunks - 2 else chunk + 1):
+                if ready >= len(homes):
+                    sections, mark = home(ready, waits)
+                    homes.append(sections)
+                    waits = (mark,)
+        for chunk in range(chunks):
+            *slabs, mark = combine(seats, homes[chunk], backs[chunk], groups, (*waits, *arrived))
+            moved.append(exchange(slabs, "head"))
+            waits = (mark,)
             if chunk < chunks - 1:
-                sections, mark = home(chunk + 1, (mark,))
-            arrived = moved[-1][1:] if moved else []
-            *slabs, mark = combine(seats, here, backs, groups, (mark, *arrived))
-            moved.append(exchange(slabs, "head"))
+                swap(chunk, waits)
+                arrived = (*moved[-1][1:], other[-1])
+    swap(chunks - 1, moved[-1][1:])
     sides = jnp.stack([side.astype(jnp.int32), seat])
-    held = [after(piece, slabs[1:]) for piece, slabs in zip(mine, moved)]
-    other = [lax.ppermute(piece, "ctx", sibling) for piece in held]
-    return project(sides, moved, held, other)
+    result = project(sides, moved, held, None)
+    return project(sides, moved, other, result)
 
 
 def solution(mesh):

time: 155 us -> 162 us (1.045)
  waiting for transfers between devices: 65.5 us -> 54.8 us
  Pallas kernels: 31.1 us -> 38.8 us
  local copies, waits for them, and re-layouts: 6.13 us -> 13.8 us
  starting transfers between devices: 32.9 us -> 39 us
  other arithmetic: 4.85 us -> 0.15 us
    ppermute x1, waiting for transfers between devices: 12.5 us -> 0.01 us  [body(): before = lax.ppermute(rim, 'ctx', [(i, i + 1) for i in range(ctx - 1)])]
    all_to_all x2, waiting for transfers between devices: 0.01 us -> 12.4 us  [body(): lax.all_to_all(part, 'ctx', split_axis=0, concat_axis=0, tiled=True)]
    ppermute x5 -> x9, waiting for transfers between devices: 30.3 us -> 19.1 us  [the longest x7 19.1 us: swapped(): return lax.ppermute(piece, 'ctx', [(i, i ^ distance) for i in range(count)])]
    unnamed x20 -> x40, local copies, waits for them, and re-layouts: 3.89 us -> 11.6 us
    ppermute x5 -> x9, starting transfers between devices: 2.56 us -> 7.72 us  [the longest x7 7.65 us: swapped(): return lax.ppermute(piece, 'ctx', [(i, i ^ distance) for i in range(count)])]
    concatenate x3 -> x0, other arithmetic: 4.7 us -> none  [gather_ctx(): held = jnp.concatenate([held, received], axis=1)]
    pallas_call x1 -> x2, Pallas kernels: 5.14 us -> 9.13 us  [prepare(): pl.pallas_call(functools.partial(prep_kernel, rim_start=rim_start, whole=...]
    pallas_call x1 -> x2, Pallas kernels: 5.97 us -> 8.67 us  [project(): pl.pallas_call(functools.partial(project_kernel, slots=slots, chunks=chun...]
  transfers between devices with their start and end apart: 30 -> 34, of which waited for: 15 -> 12; matrix products, arithmetic and copies ran while one was open for 3% -> 0% of each run, Pallas kernels for 16% -> 22%
where the time goes in v2:
time: 162 us; the launch traced here: 160 us
  waiting for transfers between devices  54.8 us (34%)
  starting transfers between devices  39 us (24%)
  Pallas kernels  38.8 us (24%)
  local copies, waits for them, and re-layouts  13.8 us (9%)
  between operations  13.6 us (8%)
    ppermute x20, waiting for transfers between devices, exchange(): moved.append(lax.ppermute(slabs[slot], axis, pairs))  23.2 us
    ppermute x7, waiting for transfers between devices, swapped(): return lax.ppermute(piece, 'ctx', [(i, i ^ distance) for i in range(count)])  19.1 us
    ppermute x20, starting transfers between devices, exchange(): moved.append(lax.ppermute(slabs[slot], axis, pairs))  19.1 us
    all_to_all x2, waiting for transfers between devices, body(): lax.all_to_all(part, 'ctx', split_axis=0, concat_axis=0, tiled=True)  12.4 us
    pallas_call x2, Pallas kernels, home_sections(): pl.pallas_call(functools.partial(home_kernel, order=order), grid=(heads,)...  12.3 us
    unnamed x40, local copies, waits for them, and re-layouts  11.6 us
    all_to_all x2, starting transfers between devices, body(): lax.all_to_all(part, 'ctx', split_axis=0, concat_axis=0, tiled=True)  9.96 us
    pallas_call x2, Pallas kernels, prepare(): pl.pallas_call(functools.partial(prep_kernel, rim_start=rim_start, whole=...  9.13 us
  transfers between devices with their start and end apart: 34, of which 12 were waited for; matrix products, arithmetic and copies ran while one was open for 0% of the time, Pallas kernels for 22%

profile of v2, /device:TPU:10, one launch (start us, length us, event | category | flops | bytes accessed | tf_op | source)
XLA Modules:
  0.0 160.1 jit_solution(8420392976536006014)
XLA Ops:
  6.5 2.2 %constant_dynamic-slice_fusion = (bf16[256,1024]{1,0:T(8,128)(2,1)}, bf16[256,1024]{1,0:T(8,128)(2,1)}) fusion(bf16[512,2048]{1,0:T(8,128)(2,1)} %param.7, s32[]{:T(128)S(6)} %select_n.12), kind=kLoop, calls=%fused_computation.2 | loop fusion | bytes 2097156 | tf_op jit(solution)/shard_map/dynamic_slice | solution.py:422
  8.8 4.2 %prepare.3 = bf16[8,3,2,64,256]{4,3,2,1,0:T(8,128)(2,1)} custom-call(bf16[1024,512]{1,0:T(8,128)(2,1)} %q_ref.7, bf16[1024,512]{1,0:T(8,128)(2,1)} %k_ref.7, bf16[1024,512]{1,0:T(8,128)(2,1)} %v_ref.7), custom_call_target="tpu_custom_call" | custom-call | flops 402653184 | bytes 4194304 | tf_op jit(solution)/shard_map/prepare/pallas_call | solution.py:148
  13.0 4.3 %all-to-all-start = ((bf16[8,3,2,64,256]{4,3,2,1,0:T(8,128)(2,1)}), bf16[8,3,2,64,256]{4,3,2,1,0:T(8,128)(2,1)S(1)}, u32[]{:S(2)}, u32[]{:S(2)}) async-start(bf16[8,3,2,64,256]{4,3,2,1,0:T(8,128)(2,1)} %prepare.3), calls=%async_computation | async-start | bytes 3145728 | tf_op jit(solution)/shard_map/all_to_all | solution.py:437
  17.3 4.9 %prepare.2 = (bf16[8,3,2,64,256]{4,3,2,1,0:T(8,128)(2,1)}, bf16[2,512,512]{2,1,0:T(8,128)(2,1)}, bf16[2,64,512]{2,1,0:T(8,128)(2,1)}) custom-call(bf16[1024,512]{1,0:T(8,128)(2,1)} %q_ref.7, bf16[1024,512]{1,0:T(8,128)(2,1)} %k_ref.7, bf16[1024,512]{1,0:T(8,128)(2,1)} %v_ref.7, bf16[1024,512]{1,0:T(8,128)(2,1)} %k_ref.7, bf16[1024,512]{1,0:T(8,128)(2,1)} %v_ref.7), custom_call_target="tpu_custom_call" | custom-call | flops 402653184 | bytes 4194304 | tf_op jit(solution)/shard_map/prepare/pallas_call | solution.py:148
  22.2 2.2 %collective-permute-start = (bf16[2,512,512]{2,1,0:T(8,128)(2,1)}, bf16[2,512,512]{2,1,0:T(8,128)(2,1)}, u32[]{:S(2)}, u32[]{:S(2)}) collective-permute-start(bf16[2,512,512]{2,1,0:T(8,128)(2,1)} %get-tuple-element.39), channel_id=1, source_target_pairs={{0,4},{4,8},{8,12},{12,16},{16,20},{20,24},{24,28},{1,5},{5,9},{9,... | collective-permute-start | bytes 3145736 | tf_op jit(solution)/shard_map/ppermute | solution.py:440
  24.4 12.4 %all-to-all-done.x_ref = bf16[8,3,2,64,256]{4,3,2,1,0:T(8,128)(2,1)S(1)} async-done(((bf16[8,3,2,64,256]{4,3,2,1,0:T(8,128)(2,1)}), bf16[8,3,2,64,256]{4,3,2,1,0:T(8,128)(2,1)S(1)}, u32[]{:S(2)}, u32[]{:S(2)}) %all-to-all-start) | async-done | bytes 1572896 | tf_op jit(solution)/shard_map/all_to_all | solution.py:437
  36.8 1.2 copy-done.6
  38.0 5.7 %all-to-all-start.1 = ((bf16[8,3,2,64,256]{4,3,2,1,0:T(8,128)(2,1)}), bf16[8,3,2,64,256]{4,3,2,1,0:T(8,128)(2,1)}, u32[]{:S(2)}, u32[]{:S(2)}) async-start(bf16[8,3,2,64,256]{4,3,2,1,0:T(8,128)(2,1)} %get-tuple-element.51), calls=%async_computation.1 | async-start | bytes 3145728 | tf_op jit(solution)/shard_map/all_to_all | solution.py:437
  44.0 1.9 %collective-permute-start.2 = (bf16[2,64,512]{2,1,0:T(8,128)(2,1)S(1)}, bf16[2,64,512]{2,1,0:T(8,128)(2,1)}, u32[]{:S(2)}, u32[]{:S(2)}) collective-permute-start(bf16[2,64,512]{2,1,0:T(8,128)(2,1)S(1)} %copy-done.12), channel_id=1, source_target_pairs={{0,16},{4,20},{8,24},{12,28},{16,0},{20,4},{24,8},{28,12},{1,17},{... | collective-permute-start | bytes 393224 | tf_op jit(solution)/shard_map/ppermute | solution.py:369
  45.9 1.4 collective-permute-start.3
  47.5 17.9 %collective-permute-done.1.refs_1_ = bf16[2,64,512]{2,1,0:T(8,128)(2,1)S(1)} collective-permute-done((bf16[2,64,512]{2,1,0:T(8,128)(2,1)S(1)}, bf16[2,64,512]{2,1,0:T(8,128)(2,1)S(1)}, u32[]{:S(2)}, u32[]{:S(2)}) %collective-permute-start.1) | collective-permute-done | bytes 131104 | tf_op jit(solution)/shard_map/ppermute | solution.py:369
  65.4 3.0 %collective-permute-start.5 = (bf16[2,64,512]{2,1,0:T(8,128)(2,1)S(1)}, bf16[2,64,512]{2,1,0:T(8,128)(2,1)S(1)}, u32[]{:S(2)}, u32[]{:S(2)}) collective-permute-start(bf16[2,64,512]{2,1,0:T(8,128)(2,1)S(1)} %collective-permute-done.1.refs_1_), channel_id=1, source_target_pairs={{0,4},{4,0},{8,12},{12,8},{16,20},{20,16},{24,28},{28,24},{1,5},{5... | collective-permute-start | bytes 393224 | tf_op jit(solution)/shard_map/ppermute | solution.py:369
  68.5 1.2 collective-permute-done.3.refs_3_
  69.7 0.9 collective-permute-start.7
  70.7 1.4 copy-done.7
  72.1 2.4 %stride.2 = (bf16[2,64,256]{2,1,0:T(8,128)(2,1)S(1)}, bf16[2,64,256]{2,1,0:T(8,128)(2,1)}, bf16[2,64,256]{2,1,0:T(8,128)(2,1)}, bf16[2,64,256]{2,1,0:T(8,128)(2,...) custom-call(s32[1]{0:T(128)} %bitcast.2.place_ref, ...), custom_call_target="tpu_custom_call" | custom-call | flops 805306368 | bytes 2097152 | tf_op jit(solution)/shard_map/stride/pallas_call | solution.py:269
  74.7 1.5 collective-permute-start.11
  76.4 1.6 %collective-permute-start.13 = (bf16[2,64,256]{2,1,0:T(8,128)(2,1)}, bf16[2,64,256]{2,1,0:T(8,128)(2,1)S(1)}, u32[]{:S(2)}, u32[]{:S(2)}) collective-permute-start(bf16[2,64,256]{2,1,0:T(8,128)(2,1)} %get-tuple-element.49), channel_id=1, source_target_pairs={{0,24},{4,28},{8,16},{12,20},{16,8},{20,12},{24,0},{28,4},{1,25},{... | collective-permute-start | bytes 196616 | tf_op jit(solution)/shard_map/ppermute | solution.py:454
  78.1 1.1 collective-permute-start.14
  79.1 0.9 copy-done.13
  80.0 0.9 copy-done.15
  80.9 6.1 %home.2 = (f32[1024,256]{1,0:T(8,128)S(1)}, f32[8,128]{1,0:T(8,128)S(1)}) custom-call(s32[1]{0:T(128)} %bitcast.2.place_ref, bf16[1024,512]{1,0:T(8,128)(2,1)S(1)} %copy-done.5, bf16[1024,512]{1,0:T(8,128)(2,1)S(1)} %copy-done, bf16[1024,512]{1,0:T(8,128)(2,1)S(1)} %copy-done.1, bf16[2,512,512]{2,1,0:T(8,128)(2,1)} %collective-permute-done.rim_ref, ...), custom_call_target="tpu_custom_call" | custom-call | flops 2684354560 | bytes 7340032 | tf_op jit(solution)/shard_map/home/pallas_call | solution.py:215
  87.1 1.0 copy-done.10
  88.0 6.1 %home.3 = (f32[1024,256]{1,0:T(8,128)S(1)}, f32[8,128]{1,0:T(8,128)S(1)}) custom-call(s32[1]{0:T(128)} %bitcast.2.place_ref, bf16[1024,512]{1,0:T(8,128)(2,1)S(1)} %copy-done.5, bf16[1024,512]{1,0:T(8,128)(2,1)S(1)} %copy-done, bf16[1024,512]{1,0:T(8,128)(2,1)S(1)} %copy-done.1, bf16[2,512,512]{2,1,0:T(8,128)(2,1)} %collective-permute-done.rim_ref, ...), custom_call_target="tpu_custom_call" | custom-call | flops 2684354560 | bytes 7340032 | tf_op jit(solution)/shard_map/home/pallas_call | solution.py:215
  94.2 1.0 copy-done.8
  95.6 1.7 %collective-permute-start.9 = (bf16[2,64,256]{2,1,0:T(8,128)(2,1)}, bf16[2,64,256]{2,1,0:T(8,128)(2,1)S(1)}, u32[]{:S(2)}, u32[]{:S(2)}) collective-permute-start(bf16[2,64,256]{2,1,0:T(8,128)(2,1)} %get-tuple-element.45), channel_id=1, source_target_pairs={{0,8},{4,12},{8,0},{12,4},{16,24},{20,28},{24,16},{28,20},{1,9},{5... | collective-permute-start | bytes 196616 | tf_op jit(solution)/shard_map/ppermute | solution.py:454
  97.3 3.4 %stride.3 = (bf16[2,64,256]{2,1,0:T(8,128)(2,1)S(1)}, bf16[2,64,256]{2,1,0:T(8,128)(2,1)S(1)}, bf16[2,64,256]{2,1,0:T(8,128)(2,1)S(1)}, bf16[2,64,256]{2,1,0:T(8...) custom-call(s32[1]{0:T(128)} %bitcast.2.place_ref, ...), custom_call_target="tpu_custom_call" | custom-call | flops 805306368 | bytes 2097152 | tf_op jit(solution)/shard_map/stride/pallas_call | solution.py:269
  101.3 1.5 combine.2
  102.9 1.6 %copy-done.2 = bf16[1024,1024]{1,0:T(8,128)(2,1)S(1)} copy-done((bf16[1024,1024]{1,0:T(8,128)(2,1)S(1)}, bf16[1024,1024]{1,0:T(8,128)(2,1)}, u32[]{:S(2)}) %copy-start.2) | copy-done | bytes 2097176
  104.6 1.3 copy-done.3
  106.8 0.9 collective-permute-start.20
  107.8 0.6 collective-permute-start.21
  108.8 1.1 collective-permute-start.22
  109.9 1.3 collective-permute-done.19.refs_2_
  111.2 1.5 collective-permute-start.23
  112.8 0.6 collective-permute-start.15
  113.4 2.5 %collective-permute-start.16 = (bf16[256,256]{1,0:T(8,128)(2,1)}, bf16[256,256]{1,0:T(8,128)(2,1)S(1)}, u32[]{:S(2)}, u32[]{:S(2)}) collective-permute-start(bf16[256,256]{1,0:T(8,128)(2,1)} %get-tuple-element.57), channel_id=1, source_target_pairs={{0,2},{1,3},{2,0},{3,1},{4,6},{5,7},{6,4},{7,5},{8,10},{9,11},{10,... | collective-permute-start | bytes 393224 | tf_op jit(solution)/shard_map/ppermute | solution.py:454
  117.0 4.4 %collective-permute-done.24.refs_7_ = bf16[2,64,256]{2,1,0:T(8,128)(2,1)S(1)} collective-permute-done((bf16[2,64,256]{2,1,0:T(8,128)(2,1)S(1)}, bf16[2,64,256]{2,1,0:T(8,128)(2,1)S(1)}, u32[]{:S(2)}, u32[]{:S(2)}) %collective-permute-start.24) | collective-permute-done | bytes 65568 | tf_op jit(solution)/shard_map/ppermute | solution.py:454
  121.4 4.0 %collective-permute-done.16.refs_10_.refs_2_ = bf16[256,256]{1,0:T(8,128)(2,1)S(1)} collective-permute-done((bf16[256,256]{1,0:T(8,128)(2,1)}, bf16[256,256]{1,0:T(8,128)(2,1)S(1)}, u32[]{:S(2)}, u32[]{:S(2)}) %collective-permute-start.16) | collective-permute-done | bytes 131104 | tf_op jit(solution)/shard_map/ppermute | solution.py:454
  125.4 2.2 %collective-permute-done.17.refs_11_.refs_3_ = bf16[256,256]{1,0:T(8,128)(2,1)S(1)} collective-permute-done((bf16[256,256]{1,0:T(8,128)(2,1)}, bf16[256,256]{1,0:T(8,128)(2,1)S(1)}, u32[]{:S(2)}, u32[]{:S(2)}) %collective-permute-start.17) | collective-permute-done | bytes 131104 | tf_op jit(solution)/shard_map/ppermute | solution.py:454
  127.6 1.4 combine.3
  128.9 3.3 %collective-permute-start.27 = (bf16[256,256]{1,0:T(8,128)(2,1)S(1)}, bf16[256,256]{1,0:T(8,128)(2,1)S(1)}, u32[]{:S(2)}, u32[]{:S(2)}) collective-permute-start(bf16[256,256]{1,0:T(8,128)(2,1)S(1)} %get-tuple-element.71), channel_id=1, source_target_pairs={{0,2},{1,3},{2,0},{3,1},{4,6},{5,7},{6,4},{7,5},{8,10},{9,11},{10,... | collective-permute-start | bytes 393224 | tf_op jit(solution)/shard_map/ppermute | solution.py:454
  132.4 2.8 %collective-permute-done.26.refs_1_.refs_5_ = bf16[256,256]{1,0:T(8,128)(2,1)S(1)} collective-permute-done((bf16[256,256]{1,0:T(8,128)(2,1)S(1)}, bf16[256,256]{1,0:T(8,128)(2,1)S(1)}, u32[]{:S(2)}, u32[]{:S(2)}) %collective-permute-start.26) | collective-permute-done | bytes 131104 | tf_op jit(solution)/shard_map/ppermute | solution.py:454
  135.3 4.9 %collective-permute-done.27.refs_2_.refs_6_ = bf16[256,256]{1,0:T(8,128)(2,1)S(1)} collective-permute-done((bf16[256,256]{1,0:T(8,128)(2,1)S(1)}, bf16[256,256]{1,0:T(8,128)(2,1)S(1)}, u32[]{:S(2)}, u32[]{:S(2)}) %collective-permute-start.27) | collective-permute-done | bytes 131104 | tf_op jit(solution)/shard_map/ppermute | solution.py:454
  140.2 2.8 %collective-permute-done.28.refs_3_.refs_7_ = bf16[256,256]{1,0:T(8,128)(2,1)S(1)} collective-permute-done((bf16[256,256]{1,0:T(8,128)(2,1)S(1)}, bf16[256,256]{1,0:T(8,128)(2,1)S(1)}, u32[]{:S(2)}, u32[]{:S(2)}) %collective-permute-start.28) | collective-permute-done | bytes 131104 | tf_op jit(solution)/shard_map/ppermute | solution.py:454
  143.1 1.5 copy-done.4
  144.6 5.0 %project.2.refs_10_ = bf16[256,2048]{1,0:T(8,128)(2,1)} custom-call(s32[2]{0:T(128)S(1)} %pad_add_fusion.side_ref, bf16[256,256]{1,0:T(8,128)(2,1)S(1)} %get-tuple-element.55.refs_0_, bf16[256,256]{1,0:T(8,128)(2,1)S(1)} %collective-permute-done.15.refs_9_.refs_1_, bf16[256,256]{1,0:T(8,128)(2,1)S(1)} %collective-permute-done.16.refs_10_.refs_2_, ...), custom_call_target="tpu_custom_call" | custom-call | flops 1073741824 | bytes 5767168 | tf_op jit(solution)/shard_map/project/pallas_call | solution.py:342
  149.6 3.7 %project.3 = bf16[256,2048]{1,0:T(8,128)(2,1)} custom-call(s32[2]{0:T(128)S(1)} %pad_add_fusion.side_ref, bf16[256,256]{1,0:T(8,128)(2,1)S(1)} %get-tuple-element.55.refs_0_, bf16[256,256]{1,0:T(8,128)(2,1)S(1)} %collective-permute-done.15.refs_9_.refs_1_, ...), custom_call_target="tpu_custom_call", output_to_operand_aliasing={{}: (11, {})} | custom-call | flops 1073741824 | bytes 5767168 | tf_op jit(solution)/shard_map/project/pallas_call | solution.py:342
  (77 shorter events, 4.7 us)
Async XLA Ops:
  6.5 96.3 %all-gather.5.cloned.1.call-start = ((), (), s32[]{:S(2)}) async-start(), calls=%async_computation.2 | async-start | bytes 2621440 | tf_op jit(solution)/shard_map/all_gather | solution.py:423
  13.0 23.8 %all-to-all-start = ((bf16[8,3,2,64,256]{4,3,2,1,0:T(8,128)(2,1)}), bf16[8,3,2,64,256]{4,3,2,1,0:T(8,128)(2,1)S(1)}, u32[]{:S(2)}, u32[]{:S(2)}) async-start(bf16[8,3,2,64,256]{4,3,2,1,0:T(8,128)(2,1)} %prepare.3), calls=%async_computation | async-start | bytes 3145728 | tf_op jit(solution)/shard_map/all_to_all | solution.py:437
  22.2 21.6 %copy-start.12 = (bf16[2,64,512]{2,1,0:T(8,128)(2,1)S(1)}, bf16[2,64,512]{2,1,0:T(8,128)(2,1)}, u32[]{:S(2)}) copy-start(bf16[2,64,512]{2,1,0:T(8,128)(2,1)} %get-tuple-element.40.refs_0_) | copy-start | bytes 393220
  22.2 55.9 %collective-permute-start = (bf16[2,512,512]{2,1,0:T(8,128)(2,1)}, bf16[2,512,512]{2,1,0:T(8,128)(2,1)}, u32[]{:S(2)}, u32[]{:S(2)}) collective-permute-start(bf16[2,512,512]{2,1,0:T(8,128)(2,1)} %get-tuple-element.39), channel_id=1, source_target_pairs={{0,4},{4,8},{8,12},{12,16},{16,20},{20,24},{24,28},{1,5},{5,9},{9,... | collective-permute-start | bytes 3145736 | tf_op jit(solution)/shard_map/ppermute | solution.py:440
  38.0 59.2 %all-to-all-start.1 = ((bf16[8,3,2,64,256]{4,3,2,1,0:T(8,128)(2,1)}), bf16[8,3,2,64,256]{4,3,2,1,0:T(8,128)(2,1)}, u32[]{:S(2)}, u32[]{:S(2)}) async-start(bf16[8,3,2,64,256]{4,3,2,1,0:T(8,128)(2,1)} %get-tuple-element.51), calls=%async_computation.1 | async-start | bytes 3145728 | tf_op jit(solution)/shard_map/all_to_all | solution.py:437
  43.8 35.4 %copy-start = (bf16[1024,512]{1,0:T(8,128)(2,1)S(1)}, bf16[1024,512]{1,0:T(8,128)(2,1)}, u32[]{:S(2)}) copy-start(bf16[1024,512]{1,0:T(8,128)(2,1)} %k_ref.7) | copy-start | bytes 3145732
  43.8 35.4 %copy-start.1 = (bf16[1024,512]{1,0:T(8,128)(2,1)S(1)}, bf16[1024,512]{1,0:T(8,128)(2,1)}, u32[]{:S(2)}) copy-start(bf16[1024,512]{1,0:T(8,128)(2,1)} %v_ref.7) | copy-start | bytes 3145732
  43.8 35.4 %copy-start.5 = (bf16[1024,512]{1,0:T(8,128)(2,1)S(1)}, bf16[1024,512]{1,0:T(8,128)(2,1)}, u32[]{:S(2)}) copy-start(bf16[1024,512]{1,0:T(8,128)(2,1)} %q_ref.7) | copy-start | bytes 3145732
  43.8 88.7 %all-gather.7.cloned.1.call-start = ((), (), s32[]{:S(2)}) async-start(), calls=%async_computation.3 | async-start | bytes 2621440 | tf_op jit(solution)/shard_map/all_gather | solution.py:423
  43.8 21.5 %collective-permute-start.1 = (bf16[2,64,512]{2,1,0:T(8,128)(2,1)S(1)}, bf16[2,64,512]{2,1,0:T(8,128)(2,1)S(1)}, u32[]{:S(2)}, u32[]{:S(2)}) collective-permute-start(bf16[2,64,512]{2,1,0:T(8,128)(2,1)S(1)} %copy-done.12), channel_id=1, source_target_pairs={{0,8},{4,12},{8,0},{12,4},{16,24},{20,28},{24,16},{28,20},{1,9},{5... | collective-permute-start | bytes 393224 | tf_op jit(solution)/shard_map/ppermute | solution.py:369
  44.0 24.4 %collective-permute-start.2 = (bf16[2,64,512]{2,1,0:T(8,128)(2,1)S(1)}, bf16[2,64,512]{2,1,0:T(8,128)(2,1)}, u32[]{:S(2)}, u32[]{:S(2)}) collective-permute-start(bf16[2,64,512]{2,1,0:T(8,128)(2,1)S(1)} %copy-done.12), channel_id=1, source_target_pairs={{0,16},{4,20},{8,24},{12,28},{16,0},{20,4},{24,8},{28,12},{1,17},{... | collective-permute-start | bytes 393224 | tf_op jit(solution)/shard_map/ppermute | solution.py:369
  45.9 23.8 %collective-permute-start.3 = (bf16[2,64,512]{2,1,0:T(8,128)(2,1)S(1)}, bf16[2,64,512]{2,1,0:T(8,128)(2,1)}, u32[]{:S(2)}, u32[]{:S(2)}) collective-permute-start(bf16[2,64,512]{2,1,0:T(8,128)(2,1)S(1)} %copy-done.12), channel_id=1, source_target_pairs={{0,24},{4,28},{8,16},{12,20},{16,8},{20,12},{24,0},{28,4},{1,25},{... | collective-permute-start | bytes 393224 | tf_op jit(solution)/shard_map/ppermute | solution.py:369
  47.4 27.1 %collective-permute-start.4 = (bf16[2,64,512]{2,1,0:T(8,128)(2,1)S(1)}, bf16[2,64,512]{2,1,0:T(8,128)(2,1)}, u32[]{:S(2)}, u32[]{:S(2)}) collective-permute-start(bf16[2,64,512]{2,1,0:T(8,128)(2,1)S(1)} %copy-done.12), channel_id=1, source_target_pairs={{0,4},{4,0},{8,12},{12,8},{16,20},{20,16},{24,28},{28,24},{1,5},{5... | collective-permute-start | bytes 393224 | tf_op jit(solution)/shard_map/ppermute | solution.py:369
  65.4 10.9 %copy-start.14 = (bf16[2,64,512]{2,1,0:T(8,128)(2,1)}, bf16[2,64,512]{2,1,0:T(8,128)(2,1)S(1)}, u32[]{:S(2)}) copy-start(bf16[2,64,512]{2,1,0:T(8,128)(2,1)S(1)} %collective-permute-done.1.refs_1_) | copy-start | bytes 393220
  65.4 9.3 %collective-permute-start.5 = (bf16[2,64,512]{2,1,0:T(8,128)(2,1)S(1)}, bf16[2,64,512]{2,1,0:T(8,128)(2,1)S(1)}, u32[]{:S(2)}, u32[]{:S(2)}) collective-permute-start(bf16[2,64,512]{2,1,0:T(8,128)(2,1)S(1)} %collective-permute-done.1.refs_1_), channel_id=1, source_target_pairs={{0,4},{4,0},{8,12},{12,8},{16,20},{20,16},{24,28},{28,24},{1,5},{5... | collective-permute-start | bytes 393224 | tf_op jit(solution)/shard_map/ppermute | solution.py:369
  68.4 7.8 %collective-permute-start.6 = (bf16[2,64,512]{2,1,0:T(8,128)(2,1)}, bf16[2,64,512]{2,1,0:T(8,128)(2,1)S(1)}, u32[]{:S(2)}, u32[]{:S(2)}) collective-permute-start(bf16[2,64,512]{2,1,0:T(8,128)(2,1)} %collective-permute-done.2.refs_2_), channel_id=1, source_target_pairs={{0,4},{4,0},{8,12},{12,8},{16,20},{20,16},{24,28},{28,24},{1,5},{5... | collective-permute-start | bytes 393224 | tf_op jit(solution)/shard_map/ppermute | solution.py:369
  69.7 6.7 %collective-permute-start.7 = (bf16[2,64,512]{2,1,0:T(8,128)(2,1)}, bf16[2,64,512]{2,1,0:T(8,128)(2,1)S(1)}, u32[]{:S(2)}, u32[]{:S(2)}) collective-permute-start(bf16[2,64,512]{2,1,0:T(8,128)(2,1)} %collective-permute-done.3.refs_3_), channel_id=1, source_target_pairs={{0,4},{4,0},{8,12},{12,8},{16,20},{20,16},{24,28},{28,24},{1,5},{5... | collective-permute-start | bytes 393224 | tf_op jit(solution)/shard_map/ppermute | solution.py:369
  70.7 1.4 copy-start.7
  74.5 20.7 %collective-permute-start.10 = (bf16[2,64,256]{2,1,0:T(8,128)(2,1)S(1)}, bf16[2,64,256]{2,1,0:T(8,128)(2,1)S(1)}, u32[]{:S(2)}, u32[]{:S(2)}) collective-permute-start(bf16[2,64,256]{2,1,0:T(8,128)(2,1)S(1)} %get-tuple-element.46), channel_id=1, source_target_pairs={{0,12},{4,8},{8,4},{12,0},{16,28},{20,24},{24,20},{28,16},{1,13},{... | collective-permute-start | bytes 196616 | tf_op jit(solution)/shard_map/ppermute | solution.py:454
  74.7 20.9 %collective-permute-start.11 = (bf16[2,64,256]{2,1,0:T(8,128)(2,1)S(1)}, bf16[2,64,256]{2,1,0:T(8,128)(2,1)S(1)}, u32[]{:S(2)}, u32[]{:S(2)}) collective-permute-start(bf16[2,64,256]{2,1,0:T(8,128)(2,1)S(1)} %get-tuple-element.47), channel_id=1, source_target_pairs={{0,16},{4,20},{8,24},{12,28},{16,0},{20,4},{24,8},{28,12},{1,17},{... | collective-permute-start | bytes 196616 | tf_op jit(solution)/shard_map/ppermute | solution.py:454
  76.2 25.1 %collective-permute-start.12 = (bf16[2,64,256]{2,1,0:T(8,128)(2,1)}, bf16[2,64,256]{2,1,0:T(8,128)(2,1)S(1)}, u32[]{:S(2)}, u32[]{:S(2)}) collective-permute-start(bf16[2,64,256]{2,1,0:T(8,128)(2,1)} %get-tuple-element.48), channel_id=1, source_target_pairs={{0,20},{4,16},{8,28},{12,24},{16,4},{20,0},{24,12},{28,8},{1,21},{... | collective-permute-start | bytes 196616 | tf_op jit(solution)/shard_map/ppermute | solution.py:454
  76.4 24.9 %collective-permute-start.13 = (bf16[2,64,256]{2,1,0:T(8,128)(2,1)}, bf16[2,64,256]{2,1,0:T(8,128)(2,1)S(1)}, u32[]{:S(2)}, u32[]{:S(2)}) collective-permute-start(bf16[2,64,256]{2,1,0:T(8,128)(2,1)} %get-tuple-element.49), channel_id=1, source_target_pairs={{0,24},{4,28},{8,16},{12,20},{16,8},{20,12},{24,0},{28,4},{1,25},{... | collective-permute-start | bytes 196616 | tf_op jit(solution)/shard_map/ppermute | solution.py:454
  78.1 23.3 %collective-permute-start.14 = (bf16[2,64,256]{2,1,0:T(8,128)(2,1)}, bf16[2,64,256]{2,1,0:T(8,128)(2,1)S(1)}, u32[]{:S(2)}, u32[]{:S(2)}) collective-permute-start(bf16[2,64,256]{2,1,0:T(8,128)(2,1)} %get-tuple-element.50), channel_id=1, source_target_pairs={{0,28},{4,24},{8,20},{12,16},{16,12},{20,8},{24,4},{28,0},{1,29},{... | collective-permute-start | bytes 196616 | tf_op jit(solution)/shard_map/ppermute | solution.py:454
  80.9 7.1 %copy-start.16 = (bf16[2,64,512]{2,1,0:T(8,128)(2,1)S(1)}, bf16[2,64,512]{2,1,0:T(8,128)(2,1)}, u32[]{:S(2)}) copy-start(bf16[2,64,512]{2,1,0:T(8,128)(2,1)} %copy-done.14) | copy-start | bytes 393220
  95.2 6.1 %copy-start.11 = (f32[1024,256]{1,0:T(8,128)S(1)}, f32[1024,256]{1,0:T(8,128)}, u32[]{:S(2)}) copy-start(f32[1024,256]{1,0:T(8,128)} %copy-done.10) | copy-start | bytes 3145732
  95.2 6.1 %collective-permute-start.8 = (bf16[2,64,256]{2,1,0:T(8,128)(2,1)}, bf16[2,64,256]{2,1,0:T(8,128)(2,1)S(1)}, u32[]{:S(2)}, u32[]{:S(2)}) collective-permute-start(bf16[2,64,256]{2,1,0:T(8,128)(2,1)} %get-tuple-element.44), channel_id=1, source_target_pairs={{0,4},{4,0},{8,12},{12,8},{16,20},{20,16},{24,28},{28,24},{1,5},{5... | collective-permute-start | bytes 196616 | tf_op jit(solution)/shard_map/ppermute | solution.py:454
  95.6 5.7 %collective-permute-start.9 = (bf16[2,64,256]{2,1,0:T(8,128)(2,1)}, bf16[2,64,256]{2,1,0:T(8,128)(2,1)S(1)}, u32[]{:S(2)}, u32[]{:S(2)}) collective-permute-start(bf16[2,64,256]{2,1,0:T(8,128)(2,1)} %get-tuple-element.45), channel_id=1, source_target_pairs={{0,8},{4,12},{8,0},{12,4},{16,24},{20,28},{24,16},{28,20},{1,9},{5... | collective-permute-start | bytes 196616 | tf_op jit(solution)/shard_map/ppermute | solution.py:454
  102.9 1.7 %copy-start.17 = (bf16[256,256]{1,0:T(8,128)(2,1)}, bf16[256,256]{1,0:T(8,128)(2,1)S(1)}, u32[]{:S(2)}) copy-start(bf16[256,256]{1,0:T(8,128)(2,1)S(1)} %get-tuple-element.58) | copy-start | bytes 393220
  102.9 1.6 %copy-start.2 = (bf16[1024,1024]{1,0:T(8,128)(2,1)S(1)}, bf16[1024,1024]{1,0:T(8,128)(2,1)}, u32[]{:S(2)}) copy-start(bf16[1024,1024]{1,0:T(8,128)(2,1)} %all-gather.5.cloned.1.call-done) | copy-start | bytes 6291460
  104.5 12.1 %copy-start.19 = (bf16[2,64,256]{2,1,0:T(8,128)(2,1)S(1)}, bf16[2,64,256]{2,1,0:T(8,128)(2,1)}, u32[]{:S(2)}) copy-start(bf16[2,64,256]{2,1,0:T(8,128)(2,1)} %copy-done.18) | copy-start | bytes 196612
  104.5 23.1 %copy-start.9 = (f32[1024,256]{1,0:T(8,128)S(1)}, f32[1024,256]{1,0:T(8,128)}, u32[]{:S(2)}) copy-start(f32[1024,256]{1,0:T(8,128)} %copy-done.8) | copy-start | bytes 3145732
  104.5 23.0 %collective-permute-start.25 = (bf16[4,256,1024]{2,1,0:T(8,128)(2,1)S(1)}, bf16[4,256,1024]{2,1,0:T(8,128)(2,1)S(1)}, u32[]{:S(2)}, u32[]{:S(2)}) collective-permute-start(bf16[4,256,1024]{2,1,0:T(8,128)(2,1)S(1)} %after.2.refs_8_), channel_id=1, source_target_pairs={{0,4},{4,0},{8,12},{12,8},{16,20},{20,16},{24,28},{28,24},{1,5},{5... | collective-permute-start | bytes 6291464 | tf_op jit(solution)/shard_map/ppermute | solution.py:461
  104.6 1.3 copy-start.3
  105.9 2.9 %collective-permute-start.18 = (bf16[2,64,256]{2,1,0:T(8,128)(2,1)S(1)}, bf16[2,64,256]{2,1,0:T(8,128)(2,1)S(1)}, u32[]{:S(2)}, u32[]{:S(2)}) collective-permute-start(bf16[2,64,256]{2,1,0:T(8,128)(2,1)S(1)} %get-tuple-element.61), channel_id=1, source_target_pairs={{0,4},{4,0},{8,12},{12,8},{16,20},{20,16},{24,28},{28,24},{1,5},{5... | collective-permute-start | bytes 196616 | tf_op jit(solution)/shard_map/ppermute | solution.py:454
  106.4 4.8 %collective-permute-start.19 = (bf16[2,64,256]{2,1,0:T(8,128)(2,1)S(1)}, bf16[2,64,256]{2,1,0:T(8,128)(2,1)S(1)}, u32[]{:S(2)}, u32[]{:S(2)}) collective-permute-start(bf16[2,64,256]{2,1,0:T(8,128)(2,1)S(1)} %get-tuple-element.62), channel_id=1, source_target_pairs={{0,8},{4,12},{8,0},{12,4},{16,24},{20,28},{24,16},{28,20},{1,9},{5... | collective-permute-start | bytes 196616 | tf_op jit(solution)/shard_map/ppermute | solution.py:454
  106.8 5.9 %collective-permute-start.20 = (bf16[2,64,256]{2,1,0:T(8,128)(2,1)S(1)}, bf16[2,64,256]{2,1,0:T(8,128)(2,1)S(1)}, u32[]{:S(2)}, u32[]{:S(2)}) collective-permute-start(bf16[2,64,256]{2,1,0:T(8,128)(2,1)S(1)} %get-tuple-element.63), channel_id=1, source_target_pairs={{0,12},{4,8},{8,4},{12,0},{16,28},{20,24},{24,20},{28,16},{1,13},{... | collective-permute-start | bytes 196616 | tf_op jit(solution)/shard_map/ppermute | solution.py:454
  107.8 5.6 %collective-permute-start.21 = (bf16[2,64,256]{2,1,0:T(8,128)(2,1)S(1)}, bf16[2,64,256]{2,1,0:T(8,128)(2,1)S(1)}, u32[]{:S(2)}, u32[]{:S(2)}) collective-permute-start(bf16[2,64,256]{2,1,0:T(8,128)(2,1)S(1)} %get-tuple-element.64), channel_id=1, source_target_pairs={{0,16},{4,20},{8,24},{12,28},{16,0},{20,4},{24,8},{28,12},{1,17},{... | collective-permute-start | bytes 196616 | tf_op jit(solution)/shard_map/ppermute | solution.py:454
  108.8 7.0 %collective-permute-start.22 = (bf16[2,64,256]{2,1,0:T(8,128)(2,1)S(1)}, bf16[2,64,256]{2,1,0:T(8,128)(2,1)S(1)}, u32[]{:S(2)}, u32[]{:S(2)}) collective-permute-start(bf16[2,64,256]{2,1,0:T(8,128)(2,1)S(1)} %get-tuple-element.65), channel_id=1, source_target_pairs={{0,20},{4,16},{8,28},{12,24},{16,4},{20,0},{24,12},{28,8},{1,21},{... | collective-permute-start | bytes 196616 | tf_op jit(solution)/shard_map/ppermute | solution.py:454
  111.2 5.4 %collective-permute-start.23 = (bf16[2,64,256]{2,1,0:T(8,128)(2,1)}, bf16[2,64,256]{2,1,0:T(8,128)(2,1)S(1)}, u32[]{:S(2)}, u32[]{:S(2)}) collective-permute-start(bf16[2,64,256]{2,1,0:T(8,128)(2,1)} %get-tuple-element.66), channel_id=1, source_target_pairs={{0,24},{4,28},{8,16},{12,20},{16,8},{20,12},{24,0},{28,4},{1,25},{... | collective-permute-start | bytes 196616 | tf_op jit(solution)/shard_map/ppermute | solution.py:454
  112.8 8.6 %collective-permute-start.15 = (bf16[256,256]{1,0:T(8,128)(2,1)}, bf16[256,256]{1,0:T(8,128)(2,1)S(1)}, u32[]{:S(2)}, u32[]{:S(2)}) collective-permute-start(bf16[256,256]{1,0:T(8,128)(2,1)} %get-tuple-element.56), channel_id=1, source_target_pairs={{0,1},{1,0},{2,3},{3,2},{4,5},{5,4},{6,7},{7,6},{8,9},{9,8},{10,11... | collective-permute-start | bytes 393224 | tf_op jit(solution)/shard_map/ppermute | solution.py:454
  113.4 12.0 %collective-permute-start.16 = (bf16[256,256]{1,0:T(8,128)(2,1)}, bf16[256,256]{1,0:T(8,128)(2,1)S(1)}, u32[]{:S(2)}, u32[]{:S(2)}) collective-permute-start(bf16[256,256]{1,0:T(8,128)(2,1)} %get-tuple-element.57), channel_id=1, source_target_pairs={{0,2},{1,3},{2,0},{3,1},{4,6},{5,7},{6,4},{7,5},{8,10},{9,11},{10,... | collective-permute-start | bytes 393224 | tf_op jit(solution)/shard_map/ppermute | solution.py:454
  115.9 11.7 %collective-permute-start.17 = (bf16[256,256]{1,0:T(8,128)(2,1)}, bf16[256,256]{1,0:T(8,128)(2,1)S(1)}, u32[]{:S(2)}, u32[]{:S(2)}) collective-permute-start(bf16[256,256]{1,0:T(8,128)(2,1)} %copy-done.17), channel_id=1, source_target_pairs={{0,3},{1,2},{2,1},{3,0},{4,7},{5,6},{6,5},{7,4},{8,11},{9,10},{10,... | collective-permute-start | bytes 393224 | tf_op jit(solution)/shard_map/ppermute | solution.py:454
  116.6 4.8 %collective-permute-start.24 = (bf16[2,64,256]{2,1,0:T(8,128)(2,1)S(1)}, bf16[2,64,256]{2,1,0:T(8,128)(2,1)S(1)}, u32[]{:S(2)}, u32[]{:S(2)}) collective-permute-start(bf16[2,64,256]{2,1,0:T(8,128)(2,1)S(1)} %copy-done.19), channel_id=1, source_target_pairs={{0,28},{4,24},{8,20},{12,16},{16,12},{20,8},{24,4},{28,0},{1,29},{... | collective-permute-start | bytes 196616 | tf_op jit(solution)/shard_map/ppermute | solution.py:454
  128.9 6.3 %collective-permute-start.26 = (bf16[256,256]{1,0:T(8,128)(2,1)S(1)}, bf16[256,256]{1,0:T(8,128)(2,1)S(1)}, u32[]{:S(2)}, u32[]{:S(2)}) collective-permute-start(bf16[256,256]{1,0:T(8,128)(2,1)S(1)} %get-tuple-element.70), channel_id=1, source_target_pairs={{0,1},{1,0},{2,3},{3,2},{4,5},{5,4},{6,7},{7,6},{8,9},{9,8},{10,11... | collective-permute-start | bytes 393224 | tf_op jit(solution)/shard_map/ppermute | solution.py:454
  128.9 11.2 %collective-permute-start.27 = (bf16[256,256]{1,0:T(8,128)(2,1)S(1)}, bf16[256,256]{1,0:T(8,128)(2,1)S(1)}, u32[]{:S(2)}, u32[]{:S(2)}) collective-permute-start(bf16[256,256]{1,0:T(8,128)(2,1)S(1)} %get-tuple-element.71), channel_id=1, source_target_pairs={{0,2},{1,3},{2,0},{3,1},{4,6},{5,7},{6,4},{7,5},{8,10},{9,11},{10,... | collective-permute-start | bytes 393224 | tf_op jit(solution)/shard_map/ppermute | solution.py:454
  132.2 10.7 %collective-permute-start.28 = (bf16[256,256]{1,0:T(8,128)(2,1)S(1)}, bf16[256,256]{1,0:T(8,128)(2,1)S(1)}, u32[]{:S(2)}, u32[]{:S(2)}) collective-permute-start(bf16[256,256]{1,0:T(8,128)(2,1)S(1)} %get-tuple-element.72), channel_id=1, source_target_pairs={{0,3},{1,2},{2,1},{3,0},{4,7},{5,6},{6,5},{7,4},{8,11},{9,10},{10,... | collective-permute-start | bytes 393224 | tf_op jit(solution)/shard_map/ppermute | solution.py:454
  143.0 1.6 copy-start.4
  143.0 6.6 %collective-permute-start.29 = (bf16[4,256,1024]{2,1,0:T(8,128)(2,1)}, bf16[4,256,1024]{2,1,0:T(8,128)(2,1)S(1)}, u32[]{:S(2)}, u32[]{:S(2)}) collective-permute-start(bf16[4,256,1024]{2,1,0:T(8,128)(2,1)} %after.3.refs_9_), channel_id=1, source_target_pairs={{0,4},{4,0},{8,12},{12,8},{16,20},{20,16},{24,28},{28,24},{1,5},{5... | collective-permute-start | bytes 6291464 | tf_op jit(solution)/shard_map/ppermute | solution.py:461
  (6 other events, 5.7 us)
Sparse Core Ops, SparseCore 0:
  8.9 45.4 all-gather.4
  56.0 44.6 all-gather.6

commit v3 on v1

--- a/solution.py
+++ b/solution.py
@@ -45,7 +45,7 @@
         out_specs=anywhere,
         out_shape=jax.ShapeDtypeStruct(array.shape, array.dtype),
         input_output_aliases={0: 0},
-        compiler_params=params(2),
+        compiler_params=params(60),
         cost_estimate=cost(0, 0),
         name="after",
     )(array, *others)
@@ -100,17 +100,7 @@
     return total[:, :HEAD_SIZE] / total[:, HEAD_SIZE:]
 
 
-def prep_kernel(q_ref, k_ref, v_ref, *refs, rim_start, chunks):
-    send_refs, rim_ref, sum_ref = refs[:chunks], refs[chunks], refs[chunks + 1]
-    step = pl.program_id(0)
-    matrix = regroup_matrix()
-    ctx, _, per, rows, width = send_refs[0].shape
-    for number, ref in enumerate((q_ref, k_ref, v_ref)):
-        grouped = dot(matrix, ref[...]).astype(BF16)
-        for chunk in range(chunks):
-            send_refs[chunk][:, number] = grouped[:, chunk * width : (chunk + 1) * width].reshape(
-                ctx, per, rows, width
-            )
+def edge_kernel(k_ref, v_ref, rim_ref, sum_ref, *, rim_start):
     picks = TILE // BLOCK * SUMCOLS
     row = iota2((picks, TILE), 0)
     col = iota2((picks, TILE), 1)
@@ -118,46 +108,63 @@
     sum_ref[0] = dot(pick, k_ref[...]).astype(BF16)
     sum_ref[1] = dot(pick, v_ref[...]).astype(BF16)
 
-    @pl.when(step >= rim_start)
+    @pl.when(pl.program_id(0) >= rim_start)
     def _():
         rim_ref[0] = k_ref[...]
         rim_ref[1] = v_ref[...]
 
 
-def prepare(queries, keys, values, ctx, chunks):
-    tokens_dev, width = queries.shape
+def edges(keys, values):
+    tokens_dev, width = keys.shape
     tiles = tokens_dev // TILE
-    per = STRIDE // ctx
-    rows = tokens_dev // STRIDE
-    part = width // chunks
     rim_start = tiles - WINDOW // TILE
     picks = TILE // BLOCK * SUMCOLS
     source = pl.BlockSpec((TILE, width), lambda b: (b, 0))
     return pl.pallas_call(
-        functools.partial(prep_kernel, rim_start=rim_start, chunks=chunks),
+        functools.partial(edge_kernel, rim_start=rim_start),
         grid=(tiles,),
-        in_specs=[source] * 3,
+        in_specs=[source] * 2,
         out_specs=[
-            pl.BlockSpec((ctx, 3, per, TILE // STRIDE, part), lambda b: (0, 0, 0, b, 0))
-        ]
-        * chunks
-        + [
             pl.BlockSpec((2, TILE, width), lambda b: (0, jnp.maximum(b - rim_start, 0), 0)),
             pl.BlockSpec((2, picks, width), lambda b: (0, b, 0)),
         ],
-        out_shape=[jax.ShapeDtypeStruct((ctx, 3, per, rows, part), BF16)] * chunks
-        + [
+        out_shape=[
             jax.ShapeDtypeStruct((2, WINDOW, width), BF16),
             jax.ShapeDtypeStruct((2, tiles * picks, width), BF16),
         ],
         compiler_params=params(60),
-        cost_estimate=cost(6 * tokens_dev * TILE * width, 16 * tokens_dev * width),
+        cost_estimate=cost(4 * tokens_dev * picks * width, 7 * tokens_dev * width),
+        name="edges",
+    )(keys, values)
+
+
+def prep_kernel(q_ref, k_ref, v_ref, *refs):
+    send_ref = refs[-1]
+    matrix = regroup_matrix()
+    ctx, _, per, rows, width = send_ref.shape
+    for number, ref in enumerate((q_ref, k_ref, v_ref)):
+        grouped = dot(matrix, ref[...]).astype(BF16)
+        send_ref[:, number] = grouped.reshape(ctx, per, rows, width)
+
+
+def prepare(queries, keys, values, ctx, chunk, chunks, waits):
+    tokens_dev, width = queries.shape
+    per = STRIDE // ctx
+    part = width // chunks
+    return pl.pallas_call(
+        prep_kernel,
+        grid=(tokens_dev // TILE,),
+        in_specs=[pl.BlockSpec((TILE, part), lambda b: (b, chunk))] * 3 + moments(waits),
+        out_specs=pl.BlockSpec((ctx, 3, per, TILE // STRIDE, part), lambda b: (0, 0, 0, b, 0)),
+        out_shape=jax.ShapeDtypeStruct((ctx, 3, per, tokens_dev // STRIDE, part), BF16),
+        compiler_params=params(60),
+        cost_estimate=cost(6 * tokens_dev * TILE * part, 12 * tokens_dev * part),
         name="prepare",
-    )(queries, keys, values)
-
-
-def home_kernel(place_ref, q_ref, k_ref, v_ref, rim_ref, sum_ref, *refs, order):
-    o_ref, mark_ref = refs[-2:]
+    )(queries, keys, values, *waits)
+
+
+def home_kernel(place_ref, q_ref, k_ref, v_ref, rim_ref, *refs, order):
+    sum_refs, (o_ref, mark_ref) = refs[: len(order)], refs[-2:]
     mark_ref[...] = jnp.zeros_like(mark_ref)
     place = place_ref[0]
     tokens_dev = q_ref.shape[0]
@@ -167,9 +174,9 @@
     for e in range(tokens_dev // TILE):
         key_blocks.append(k_ref[e * TILE : (e + 1) * TILE])
         value_blocks.append(with_ones(v_ref[e * TILE : (e + 1) * TILE]))
-    pieces, picks = sum_ref.shape[1:3]
-    sum_keys = sum_ref[0].reshape(pieces * picks, HEAD_SIZE)
-    sum_values = with_ones(sum_ref[1].reshape(pieces * picks, HEAD_SIZE))
+    picks = sum_refs[0].shape[1]
+    sum_keys = jnp.concatenate([ref[0] for ref in sum_refs])
+    sum_values = with_ones(jnp.concatenate([ref[1] for ref in sum_refs]))
     sum_col = jnp.concatenate(
         [iota2((TILE, picks), 1) + (place ^ i) * picks for i in order], axis=1
     )
@@ -207,8 +214,8 @@
     tokens_dev, width = queries.shape
     heads = width // chunks // HEAD_SIZE
     first = chunk * heads
-    pieces, picks = summary.shape[1:3]
-    total = pieces * picks
+    picks = summary[0].shape[1]
+    total = len(summary) * picks
     own = pl.BlockSpec((tokens_dev, HEAD_SIZE), lambda h: (0, first + h))
     pairs = tokens_dev * (WINDOW + TILE + total) * heads
     return pl.pallas_call(
@@ -220,15 +227,15 @@
             own,
             own,
             pl.BlockSpec((2, WINDOW, HEAD_SIZE), lambda h: (0, 0, first + h)),
-            pl.BlockSpec((2, pieces, picks, HEAD_SIZE), lambda h: (0, 0, 0, first + h)),
         ]
+        + [pl.BlockSpec((2, picks, HEAD_SIZE), lambda h: (0, 0, first + h))] * len(summary)
         + moments(waits),
         out_specs=[pl.BlockSpec((tokens_dev, HEAD_SIZE), lambda h: (0, h)), mark_spec()],
         out_shape=[jax.ShapeDtypeStruct((tokens_dev, heads * HEAD_SIZE), F32), MARK],
-        compiler_params=params(60),
+        compiler_params=params(24),
         cost_estimate=cost(8 * pairs * HEAD_SIZE, 14 * tokens_dev * width, pairs),
         name="home",
-    )(place, queries, keys, values, rim, summary, *waits)
+    )(place, queries, keys, values, rim, *summary, *waits)
 
 
 def stride_kernel(place_ref, x_ref, *refs):
@@ -321,71 +328,68 @@
 
 
 def project_kernel(side_ref, *refs, slots, chunks):
-    moved_refs, refs = refs[: slots * chunks], refs[slots * chunks :]
-    mine_refs, other_refs, o_ref = refs[:chunks], refs[chunks : 2 * chunks], refs[-1]
-
-    def add_up(weight_refs):
+    moved_refs, (mine_ref, other_ref, o_ref) = refs[: slots * chunks], refs[slots * chunks :]
+    width = moved_refs[0].shape[1]
+
+    def add_up(weight_ref):
         total = None
         for slot in range(slots):
             group = partner(side_ref[1], slot, slots)
             for chunk in range(chunks):
-                part = dot(moved_refs[chunk * slots + slot][...], weight_refs[chunk][group])
+                rows = weight_ref[group, chunk * width : (chunk + 1) * width]
+                part = dot(moved_refs[chunk * slots + slot][...], rows)
                 total = part if total is None else total + part
-        o_ref[...] = total.astype(o_ref.dtype)
+        o_ref[...] = total.astype(BF16)
 
     @pl.when(pl.program_id(0) == 0)
     def _():
-        add_up(mine_refs)
+        add_up(mine_ref)
 
     @pl.when(pl.program_id(0) == 1)
     def _():
-        add_up(other_refs)
+        add_up(other_ref)
 
 
 def project(side, moved, mine, other):
     chunks, slots = len(moved), len(moved[0])
     tokens, part = moved[0][0].shape
-    half = mine[0].shape[2]
-    tile = min(half, 512)
+    width, half = mine.shape[1:]
+    tile = min(half, 256)
     tiles = half // tile
-    block = (slots, part, tile)
+    block = (slots, width, tile)
     return pl.pallas_call(
         functools.partial(project_kernel, slots=slots, chunks=chunks),
         grid_spec=pltpu.PrefetchScalarGridSpec(
             num_scalar_prefetch=1,
             grid=(2, tiles),
             in_specs=[pl.BlockSpec((tokens, part), lambda s, j, side: (0, 0))] * (slots * chunks)
-            + [pl.BlockSpec(block, lambda s, j, side: (0, 0, jnp.where(s == 0, j, tiles - 1)))]
-            * chunks
-            + [pl.BlockSpec(block, lambda s, j, side: (0, 0, jnp.where(s == 0, 0, j)))] * chunks,
+            + [
+                pl.BlockSpec(block, lambda s, j, side: (0, 0, jnp.where(s == 0, j, tiles - 1))),
+                pl.BlockSpec(block, lambda s, j, side: (0, 0, jnp.where(s == 0, 0, j))),
+            ],
             out_specs=pl.BlockSpec(
                 (tokens, tile), lambda s, j, side: (0, (s ^ side[0]) * tiles + j)
             ),
         ),
         out_shape=jax.ShapeDtypeStruct((tokens, 2 * half), BF16),
-        compiler_params=params(40),
+        compiler_params=params(24),
         cost_estimate=cost(
-            4 * chunks * slots * tokens * part * half,
-            chunks * slots * part * (4 * half + 2 * tokens) + 4 * tokens * half,
+            4 * slots * tokens * width * half, 2 * slots * width * (2 * half + tokens)
         ),
         name="project",
-    )(side, *[slab for slabs in moved for slab in slabs], *mine, *other)
+    )(side, *[slab for slabs in moved for slab in slabs], mine, other)
 
 
 def gather_ctx(rows):
     count = lax.axis_size("ctx")
-    held = rows[:, None]
-    steps = []
-    distance = count // 2
-    while distance:
-        steps.append(distance)
-        distance //= 2
-    order = [0]
-    for distance in steps:
-        received = lax.ppermute(held, "ctx", [(i, i ^ distance) for i in range(count)])
-        held = jnp.concatenate([held, received], axis=1)
-        order = order + [i ^ distance for i in order]
-    return held, order
+
+    def swapped(piece, distance):
+        return lax.ppermute(piece, "ctx", [(i, i ^ distance) for i in range(count)])
+
+    order = list(range(0, count, 2))
+    pieces = [rows] + [swapped(rows, distance) for distance in order[1:]]
+    within = [swapped(piece, 1) for piece in pieces]
+    return pieces, within, order + [i ^ 1 for i in order]
 
 
 def stride_general(queries, keys, values):
@@ -432,23 +436,24 @@
 
     half = out_weight.shape[1] // 2
     part = width // chunks
-    mine = []
-    for chunk in range(chunks):
-        piece = lax.dynamic_slice(out_weight, (chunk * part, side * half), (part, half))
-        mine.append(lax.all_gather(piece, "head", axis=0))
-
+    weight_half = lax.dynamic_slice_in_dim(out_weight, side * half, half, axis=1)
+    mine = lax.all_gather(weight_half, "head", axis=0)
+
+    rim, picked = edges(keys, values)
+    between, within, order = gather_ctx(picked)
+    summary = between + within
+    before = lax.ppermute(rim, "ctx", [(i, i + 1) for i in range(ctx - 1)])
     if ctx > STRIDE:
         stride_out = stride_general(queries, keys, values)
-        rim = jnp.stack([keys[tokens_dev - WINDOW :], values[tokens_dev - WINDOW :]])
-        picked = jnp.stack([keys, values]).reshape(2, tokens_dev // BLOCK, BLOCK, width)
-        picked = picked[:, :, BLOCK - SUMCOLS :].reshape(2, -1, width)
     else:
-        *send, rim, picked = prepare(queries, keys, values, ctx, chunks)
-        received = [
-            lax.all_to_all(part, "ctx", split_axis=0, concat_axis=0, tiled=True) for part in send
-        ]
-    summary, order = gather_ctx(picked)
-    before = lax.ppermute(rim, "ctx", [(i, i + 1) for i in range(ctx - 1)])
+        received = []
+        for chunk in range(chunks):
+            send = prepare(queries, keys, values, ctx, chunk, chunks, (picked,))
+            if chunk > 0:
+                send = after(send, between[1:])
+            received.append(
+                lax.all_to_all(send, "ctx", split_axis=0, concat_axis=0, tiled=True)
+            )
 
     def home(chunk, waits):
         return home_sections(
@@ -477,19 +482,22 @@
             waits = (mark,)
     else:
         seats = jnp.stack([seat, place.astype(jnp.int32)])
-        sections, mark = home(0, ())
+        homes, backs = [], []
         for chunk in range(chunks):
-            *slabs, mark = stride_attend(place_word, received[chunk], (mark,))
-            backs = exchange(slabs, "ctx")
-            here = sections
-            if chunk < chunks - 1:
-                sections, mark = home(chunk + 1, (mark,))
-            arrived = moved[-1][1:] if moved else []
-            *slabs, mark = combine(seats, here, backs, groups, (mark, *arrived))
+            *slabs, mark = stride_attend(place_word, received[chunk], waits)
+            backs.append(exchange(slabs, "ctx"))
+            waits = (mark,)
+            for ready in range(chunks) if chunk == 0 else ():
+                sections, mark = home(ready, waits)
+                homes.append(sections)
+                waits = (mark,)
+        for chunk in range(chunks):
+            *slabs, mark = combine(seats, homes[chunk], backs[chunk], groups, waits)
             moved.append(exchange(slabs, "head"))
+            waits = (mark, *moved[-1][1:])
+    held = after(mine, moved[-1][2:])
+    other = lax.ppermute(held, "ctx", sibling)
     sides = jnp.stack([side.astype(jnp.int32), seat])
-    held = [after(piece, slabs[1:]) for piece, slabs in zip(mine, moved)]
-    other = [lax.ppermute(piece, "ctx", sibling) for piece in held]
     return project(sides, moved, held, other)
 
 

time: 155 us -> 159 us (1.026); the launches traced: 154 us -> 156 us
  waiting for transfers between devices: 65.5 us -> 45.1 us
  starting transfers between devices: 32.9 us -> 44.2 us
  Pallas kernels: 31.1 us -> 40.2 us
  local copies, waits for them, and re-layouts: 6.13 us -> 13 us
  other arithmetic: 4.85 us -> 0.15 us
    ppermute x5 -> x8, waiting for transfers between devices: 30.3 us -> 17.4 us  [the longest x7 15.9 us: swapped(): return lax.ppermute(piece, 'ctx', [(i, i ^ distance) for i in range(count)])]
    ppermute x1, waiting for transfers between devices: 12.5 us -> 0.01 us  [body(): before = lax.ppermute(rim, 'ctx', [(i, i + 1) for i in range(ctx - 1)])]
    all_to_all x2, starting transfers between devices: 10.1 us -> 18.9 us  [body(): lax.all_to_all(send, 'ctx', split_axis=0, concat_axis=0, tiled=True)]
    unnamed x20 -> x54, local copies, waits for them, and re-layouts: 3.89 us -> 11.9 us
    pallas_call x1 -> x3, Pallas kernels: 5.14 us -> 12.3 us  [the longest x2 8.44 us: prepare(): pl.pallas_call(prep_kernel, grid=(tokens_dev // TILE,), in_specs=[pl.Bloc...]
    ppermute x20, waiting for transfers between devices: 21.9 us -> 27.7 us  [exchange(): moved.append(lax.ppermute(slabs[slot], axis, pairs))]
    concatenate x3 -> x0, other arithmetic: 4.7 us -> none  [gather_ctx(): held = jnp.concatenate([held, received], axis=1)]
    ppermute x5 -> x8, starting transfers between devices: 2.56 us -> 5.58 us  [the longest x7 5.58 us: swapped(): return lax.ppermute(piece, 'ctx', [(i, i ^ distance) for i in range(count)])]
  transfers between devices with their start and end apart: 30 -> 32, of which waited for: 15 -> 12; matrix products, arithmetic and copies ran while one was open for 3% -> 0% of each run, Pallas kernels for 16% -> 22%
where the time goes in v3:
time: 159 us; the launch traced here: 156 us
  waiting for transfers between devices  45.1 us (28%)
  starting transfers between devices  44.2 us (28%)
  Pallas kernels  40.2 us (25%)
  between operations  13.6 us (9%)
  local copies, waits for them, and re-layouts  13 us (8%)
    ppermute x20, waiting for transfers between devices, exchange(): moved.append(lax.ppermute(slabs[slot], axis, pairs))  27.7 us
    all_to_all x2, starting transfers between devices, body(): lax.all_to_all(send, 'ctx', split_axis=0, concat_axis=0, tiled=True)  18.9 us
    ppermute x20, starting transfers between devices, exchange(): moved.append(lax.ppermute(slabs[slot], axis, pairs))  17.7 us
    ppermute x7, waiting for transfers between devices, swapped(): return lax.ppermute(piece, 'ctx', [(i, i ^ distance) for i in range(count)])  15.9 us
    pallas_call x2, Pallas kernels, home_sections(): pl.pallas_call(functools.partial(home_kernel, order=order), grid=(heads,)...  12.2 us
    unnamed x54, local copies, waits for them, and re-layouts  11.9 us
    pallas_call x2, Pallas kernels, prepare(): pl.pallas_call(prep_kernel, grid=(tokens_dev // TILE,), in_specs=[pl.Bloc...  8.44 us
    pallas_call x2, Pallas kernels, stride_attend(): pl.pallas_call(stride_kernel, grid=(per,), in_specs=[pl.BlockSpec(memory_...  6.5 us
  transfers between devices with their start and end apart: 32, of which 12 were waited for; matrix products, arithmetic and copies ran while one was open for 0% of the time, Pallas kernels for 22%

profile of v3, /device:TPU:10, one launch (start us, length us, event | category | flops | bytes accessed | tf_op | source)
XLA Modules:
  0.0 156.2 jit_solution(5228187431468407341)
XLA Ops:
  6.5 1.6 %copy-done = bf16[512,2048]{1,0:T(8,128)(2,1)S(1)} copy-done((bf16[512,2048]{1,0:T(8,128)(2,1)S(1)}, bf16[512,2048]{1,0:T(8,128)(2,1)}, u32[]{:S(2)}) %copy-start) | copy-done | bytes 2097176
  8.1 1.1 constant_dynamic-slice_fusion
  9.2 3.9 %edges.1 = (bf16[2,512,512]{2,1,0:T(8,128)(2,1)}, bf16[2,64,512]{2,1,0:T(8,128)(2,1)}) custom-call(bf16[1024,512]{1,0:T(8,128)(2,1)} %k_ref.9, bf16[1024,512]{1,0:T(8,128)(2,1)} %v_ref.9), custom_call_target="tpu_custom_call" | custom-call | flops 33554432 | bytes 3670016 | tf_op jit(solution)/shard_map/edges/pallas_call | solution.py:123
  13.1 4.2 %prepare.2 = bf16[8,3,2,64,256]{4,3,2,1,0:T(8,128)(2,1)} custom-call(bf16[1024,512]{1,0:T(8,128)(2,1)} %q_ref.7, bf16[1024,512]{1,0:T(8,128)(2,1)} %k_ref.9, bf16[1024,512]{1,0:T(8,128)(2,1)} %v_ref.9, bf16[2,64,512]{2,1,0:T(8,128)(2,1)} %get-tuple-element.39.refs_0_), custom_call_target="tpu_custom_call" | custom-call | flops 402653184 | bytes 3145728 | tf_op jit(solution)/shard_map/prepare/pallas_call | solution.py:154
  17.4 4.9 %all-to-all-start = ((bf16[8,3,2,64,256]{4,3,2,1,0:T(8,128)(2,1)}), bf16[8,3,2,64,256]{4,3,2,1,0:T(8,128)(2,1)}, u32[]{:S(2)}, u32[]{:S(2)}) async-start(bf16[8,3,2,64,256]{4,3,2,1,0:T(8,128)(2,1)} %prepare.2), calls=%async_computation | async-start | bytes 3145728 | tf_op jit(solution)/shard_map/all_to_all | solution.py:455
  22.2 2.0 %collective-permute-start = (bf16[2,512,512]{2,1,0:T(8,128)(2,1)}, bf16[2,512,512]{2,1,0:T(8,128)(2,1)}, u32[]{:S(2)}, u32[]{:S(2)}) collective-permute-start(bf16[2,512,512]{2,1,0:T(8,128)(2,1)} %get-tuple-element.38), channel_id=1, source_target_pairs={{0,4},{4,8},{8,12},{12,16},{16,20},{20,24},{24,28},{1,5},{5,9},{9,... | collective-permute-start | bytes 3145736 | tf_op jit(solution)/shard_map/ppermute | solution.py:445
  24.3 1.3 collective-permute-start.1
  25.6 0.8 collective-permute-start.2
  26.4 1.4 collective-permute-start.3
  27.9 4.2 %prepare.3.refs_0_ = bf16[8,3,2,64,256]{4,3,2,1,0:T(8,128)(2,1)} custom-call(bf16[1024,512]{1,0:T(8,128)(2,1)} %q_ref.7, bf16[1024,512]{1,0:T(8,128)(2,1)} %k_ref.9, bf16[1024,512]{1,0:T(8,128)(2,1)} %v_ref.9, bf16[2,64,512]{2,1,0:T(8,128)(2,1)} %get-tuple-element.39.refs_0_), custom_call_target="tpu_custom_call" | custom-call | flops 402653184 | bytes 3145728 | tf_op jit(solution)/shard_map/prepare/pallas_call | solution.py:154
  32.1 11.7 %collective-permute-done.1.refs_1_ = bf16[2,64,512]{2,1,0:T(8,128)(2,1)S(1)} collective-permute-done((bf16[2,64,512]{2,1,0:T(8,128)(2,1)S(1)}, bf16[2,64,512]{2,1,0:T(8,128)(2,1)S(1)}, u32[]{:S(2)}, u32[]{:S(2)}) %collective-permute-start.1) | collective-permute-done | bytes 131104 | tf_op jit(solution)/shard_map/ppermute | solution.py:387
  43.8 0.8 collective-permute-done.2.refs_2_
  44.6 3.4 %collective-permute-done.3.refs_3_ = bf16[2,64,512]{2,1,0:T(8,128)(2,1)S(1)} collective-permute-done((bf16[2,64,512]{2,1,0:T(8,128)(2,1)S(1)}, bf16[2,64,512]{2,1,0:T(8,128)(2,1)S(1)}, u32[]{:S(2)}, u32[]{:S(2)}) %collective-permute-start.3) | collective-permute-done | bytes 131104 | tf_op jit(solution)/shard_map/ppermute | solution.py:387
  48.6 14.0 %all-to-all-start.1 = ((bf16[8,3,2,64,256]{4,3,2,1,0:T(8,128)(2,1)}), bf16[8,3,2,64,256]{4,3,2,1,0:T(8,128)(2,1)}, u32[]{:S(2)}, u32[]{:S(2)}) async-start(bf16[8,3,2,64,256]{4,3,2,1,0:T(8,128)(2,1)} %after.2), calls=%async_computation.1 | async-start | bytes 3145728 | tf_op jit(solution)/shard_map/all_to_all | solution.py:455
  62.7 1.4 collective-permute-start.4
  64.7 3.5 %stride.2 = (bf16[2,64,256]{2,1,0:T(8,128)(2,1)S(1)}, bf16[2,64,256]{2,1,0:T(8,128)(2,1)S(1)}, bf16[2,64,256]{2,1,0:T(8,128)(2,1)S(1)}, bf16[2,64,256]{2,1,0:T(8...) custom-call(s32[1]{0:T(128)} %bitcast.2.place_ref, ...), custom_call_target="tpu_custom_call" | custom-call | flops 805306368 | bytes 2097152 | tf_op jit(solution)/shard_map/stride/pallas_call | solution.py:275
  70.1 2.1 %collective-permute-start.11 = (bf16[2,64,256]{2,1,0:T(8,128)(2,1)}, bf16[2,64,256]{2,1,0:T(8,128)(2,1)}, u32[]{:S(2)}, u32[]{:S(2)}) collective-permute-start(bf16[2,64,256]{2,1,0:T(8,128)(2,1)} %get-tuple-element.46), channel_id=1, source_target_pairs={{0,16},{4,20},{8,24},{12,28},{16,0},{20,4},{24,8},{28,12},{1,17},{... | collective-permute-start | bytes 196616 | tf_op jit(solution)/shard_map/ppermute | solution.py:470
  72.2 1.5 collective-permute-start.13
  73.7 0.9 collective-permute-start.14
  74.7 1.2 copy-done.4
  75.9 6.1 %home.2 = (f32[1024,256]{1,0:T(8,128)S(1)}, f32[8,128]{1,0:T(8,128)S(1)}) custom-call(s32[1]{0:T(128)} %bitcast.2.place_ref, bf16[1024,512]{1,0:T(8,128)(2,1)S(1)} %copy-done.4, bf16[1024,512]{1,0:T(8,128)(2,1)S(1)} %copy-done.2, bf16[1024,512]{1,0:T(8,128)(2,1)S(1)} %copy-done.3, bf16[2,512,512]{2,1,0:T(8,128)(2,1)} %collective-permute-done.rim_ref, ...), custom_call_target="tpu_custom_call" | custom-call | flops 2684354560 | bytes 7340032 | tf_op jit(solution)/shard_map/home/pallas_call | solution.py:221
  82.0 1.0 copy-done.7
  83.0 6.1 %home.3 = (f32[1024,256]{1,0:T(8,128)S(1)}, f32[8,128]{1,0:T(8,128)S(1)}) custom-call(s32[1]{0:T(128)} %bitcast.2.place_ref, bf16[1024,512]{1,0:T(8,128)(2,1)S(1)} %copy-done.4, bf16[1024,512]{1,0:T(8,128)(2,1)S(1)} %copy-done.2, bf16[1024,512]{1,0:T(8,128)(2,1)S(1)} %copy-done.3, bf16[2,512,512]{2,1,0:T(8,128)(2,1)} %collective-permute-done.rim_ref, ...), custom_call_target="tpu_custom_call" | custom-call | flops 2684354560 | bytes 7340032 | tf_op jit(solution)/shard_map/home/pallas_call | solution.py:221
  89.1 0.9 copy-done.5
  90.1 3.0 %stride.3 = (bf16[2,64,256]{2,1,0:T(8,128)(2,1)S(1)}, bf16[2,64,256]{2,1,0:T(8,128)(2,1)S(1)}, bf16[2,64,256]{2,1,0:T(8,128)(2,1)S(1)}, bf16[2,64,256]{2,1,0:T(8...) custom-call(s32[1]{0:T(128)} %bitcast.2.place_ref, ...), custom_call_target="tpu_custom_call" | custom-call | flops 805306368 | bytes 2097152 | tf_op jit(solution)/shard_map/stride/pallas_call | solution.py:275
  93.1 0.7 collective-permute-start.8
  93.8 1.4 collective-permute-start.9
  95.9 1.1 collective-permute-start.20
  97.2 0.9 collective-permute-done.9.refs_2_
  98.1 1.3 combine.2
  99.5 2.1 %collective-permute-start.21 = (bf16[2,64,256]{2,1,0:T(8,128)(2,1)S(1)}, bf16[2,64,256]{2,1,0:T(8,128)(2,1)S(1)}, u32[]{:S(2)}, u32[]{:S(2)}) collective-permute-start(bf16[2,64,256]{2,1,0:T(8,128)(2,1)S(1)} %get-tuple-element.62), channel_id=1, source_target_pairs={{0,16},{4,20},{8,24},{12,28},{16,0},{20,4},{24,8},{28,12},{1,17},{... | collective-permute-start | bytes 196616 | tf_op jit(solution)/shard_map/ppermute | solution.py:470
  101.6 2.7 %collective-permute-start.16 = (bf16[256,256]{1,0:T(8,128)(2,1)S(1)}, bf16[256,256]{1,0:T(8,128)(2,1)S(1)}, u32[]{:S(2)}, u32[]{:S(2)}) collective-permute-start(bf16[256,256]{1,0:T(8,128)(2,1)S(1)} %get-tuple-element.55), channel_id=1, source_target_pairs={{0,2},{1,3},{2,0},{3,1},{4,6},{5,7},{6,4},{7,5},{8,10},{9,11},{10,... | collective-permute-start | bytes 393224 | tf_op jit(solution)/shard_map/ppermute | solution.py:470
  104.2 0.8 collective-permute-start.17
  105.0 1.4 collective-permute-start.23
  106.8 3.4 %collective-permute-done.23.refs_6_ = bf16[2,64,256]{2,1,0:T(8,128)(2,1)S(1)} collective-permute-done((bf16[2,64,256]{2,1,0:T(8,128)(2,1)S(1)}, bf16[2,64,256]{2,1,0:T(8,128)(2,1)S(1)}, u32[]{:S(2)}, u32[]{:S(2)}) %collective-permute-start.23) | collective-permute-done | bytes 65568 | tf_op jit(solution)/shard_map/ppermute | solution.py:470
  110.2 1.4 collective-permute-done.24.refs_7_
  111.6 2.1 %collective-permute-done.16.refs_10_.refs_2_ = bf16[256,256]{1,0:T(8,128)(2,1)S(1)} collective-permute-done((bf16[256,256]{1,0:T(8,128)(2,1)S(1)}, bf16[256,256]{1,0:T(8,128)(2,1)S(1)}, u32[]{:S(2)}, u32[]{:S(2)}) %collective-permute-start.16) | collective-permute-done | bytes 131104 | tf_op jit(solution)/shard_map/ppermute | solution.py:470
  113.7 2.8 %collective-permute-done.17.refs_11_.refs_3_ = bf16[256,256]{1,0:T(8,128)(2,1)S(1)} collective-permute-done((bf16[256,256]{1,0:T(8,128)(2,1)S(1)}, bf16[256,256]{1,0:T(8,128)(2,1)S(1)}, u32[]{:S(2)}, u32[]{:S(2)}) %collective-permute-start.17) | collective-permute-done | bytes 131104 | tf_op jit(solution)/shard_map/ppermute | solution.py:470
  116.5 1.4 combine.3
  118.5 1.1 collective-permute-start.27
  119.6 8.4 %collective-permute-done.26.refs_1_.refs_6_ = bf16[256,256]{1,0:T(8,128)(2,1)S(1)} collective-permute-done((bf16[256,256]{1,0:T(8,128)(2,1)S(1)}, bf16[256,256]{1,0:T(8,128)(2,1)S(1)}, u32[]{:S(2)}, u32[]{:S(2)}) %collective-permute-start.26) | collective-permute-done | bytes 131104 | tf_op jit(solution)/shard_map/ppermute | solution.py:470
  128.0 2.9 %collective-permute-done.27.refs_2_.refs_7_ = bf16[256,256]{1,0:T(8,128)(2,1)S(1)} collective-permute-done((bf16[256,256]{1,0:T(8,128)(2,1)S(1)}, bf16[256,256]{1,0:T(8,128)(2,1)S(1)}, u32[]{:S(2)}, u32[]{:S(2)}) %collective-permute-start.27) | collective-permute-done | bytes 131104 | tf_op jit(solution)/shard_map/ppermute | solution.py:470
  131.8 5.7 %collective-permute-done.25.refs_5_ = bf16[256,256]{1,0:T(8,128)(2,1)S(1)} collective-permute-done((bf16[256,256]{1,0:T(8,128)(2,1)S(1)}, bf16[256,256]{1,0:T(8,128)(2,1)S(1)}, u32[]{:S(2)}, u32[]{:S(2)}) %collective-permute-start.25) | collective-permute-done | bytes 131104 | tf_op jit(solution)/shard_map/ppermute | solution.py:470
  137.5 1.5 collective-permute-done.28.refs_9_
  139.0 2.2 %copy-done.1 = bf16[4,512,1024]{2,1,0:T(8,128)(2,1)S(1)} copy-done((bf16[4,512,1024]{2,1,0:T(8,128)(2,1)S(1)}, bf16[4,512,1024]{2,1,0:T(8,128)(2,1)}, u32[]{:S(2)}) %copy-start.1) | copy-done | bytes 4194328
  141.2 0.9 copy-done.10
  142.1 0.9 copy-done.12
  143.0 6.4 %project.1 = bf16[256,2048]{1,0:T(8,128)(2,1)} custom-call(s32[2]{0:T(128)S(1)} %pad_add_fusion.side_ref, bf16[256,256]{1,0:T(8,128)(2,1)S(1)} %get-tuple-element.53.refs_0_, bf16[256,256]{1,0:T(8,128)(2,1)S(1)} %collective-permute-done.15.refs_9_.refs_1_, bf16[256,256]{1,0:T(8,128)(2,1)S(1)} %collective-permute-done.16.refs_10_.refs_2_, ...), custom_call_target="tpu_custom_call" | custom-call | flops 2147483648 | bytes 9437184 | tf_op jit(solution)/shard_map/project/pallas_call | solution.py:360
  (86 shorter events, 5.9 us)
Async XLA Ops:
  6.5 124.4 %all-gather.3.cloned.1.call-start = ((), (), s32[]{:S(2)}) async-start(), calls=%async_computation.2 | async-start | bytes 5242880 | tf_op jit(solution)/shard_map/all_gather | solution.py:440
  17.4 6.9 %copy-start.13 = (bf16[2,64,512]{2,1,0:T(8,128)(2,1)S(1)}, bf16[2,64,512]{2,1,0:T(8,128)(2,1)}, u32[]{:S(2)}) copy-start(bf16[2,64,512]{2,1,0:T(8,128)(2,1)} %get-tuple-element.39.refs_0_) | copy-start | bytes 393220
  17.4 31.3 %all-to-all-start = ((bf16[8,3,2,64,256]{4,3,2,1,0:T(8,128)(2,1)}), bf16[8,3,2,64,256]{4,3,2,1,0:T(8,128)(2,1)}, u32[]{:S(2)}, u32[]{:S(2)}) async-start(bf16[8,3,2,64,256]{4,3,2,1,0:T(8,128)(2,1)} %prepare.2), calls=%async_computation | async-start | bytes 3145728 | tf_op jit(solution)/shard_map/all_to_all | solution.py:455
  22.2 51.5 %collective-permute-start = (bf16[2,512,512]{2,1,0:T(8,128)(2,1)}, bf16[2,512,512]{2,1,0:T(8,128)(2,1)}, u32[]{:S(2)}, u32[]{:S(2)}) collective-permute-start(bf16[2,512,512]{2,1,0:T(8,128)(2,1)} %get-tuple-element.38), channel_id=1, source_target_pairs={{0,4},{4,8},{8,12},{12,16},{16,20},{20,24},{24,28},{1,5},{5,9},{9,... | collective-permute-start | bytes 3145736 | tf_op jit(solution)/shard_map/ppermute | solution.py:445
  24.3 19.5 %collective-permute-start.1 = (bf16[2,64,512]{2,1,0:T(8,128)(2,1)S(1)}, bf16[2,64,512]{2,1,0:T(8,128)(2,1)S(1)}, u32[]{:S(2)}, u32[]{:S(2)}) collective-permute-start(bf16[2,64,512]{2,1,0:T(8,128)(2,1)S(1)} %copy-done.13), channel_id=1, source_target_pairs={{0,8},{4,12},{8,0},{12,4},{16,24},{20,28},{24,16},{28,20},{1,9},{5... | collective-permute-start | bytes 393224 | tf_op jit(solution)/shard_map/ppermute | solution.py:387
  25.6 19.0 %collective-permute-start.2 = (bf16[2,64,512]{2,1,0:T(8,128)(2,1)S(1)}, bf16[2,64,512]{2,1,0:T(8,128)(2,1)S(1)}, u32[]{:S(2)}, u32[]{:S(2)}) collective-permute-start(bf16[2,64,512]{2,1,0:T(8,128)(2,1)S(1)} %copy-done.13), channel_id=1, source_target_pairs={{0,16},{4,20},{8,24},{12,28},{16,0},{20,4},{24,8},{28,12},{1,17},{... | collective-permute-start | bytes 393224 | tf_op jit(solution)/shard_map/ppermute | solution.py:387
  26.4 21.5 %collective-permute-start.3 = (bf16[2,64,512]{2,1,0:T(8,128)(2,1)S(1)}, bf16[2,64,512]{2,1,0:T(8,128)(2,1)S(1)}, u32[]{:S(2)}, u32[]{:S(2)}) collective-permute-start(bf16[2,64,512]{2,1,0:T(8,128)(2,1)S(1)} %copy-done.13), channel_id=1, source_target_pairs={{0,24},{4,28},{8,16},{12,20},{16,8},{20,12},{24,0},{28,4},{1,25},{... | collective-permute-start | bytes 393224 | tf_op jit(solution)/shard_map/ppermute | solution.py:387
  43.8 4.2 %copy-start.15 = (bf16[2,64,512]{2,1,0:T(8,128)(2,1)}, bf16[2,64,512]{2,1,0:T(8,128)(2,1)S(1)}, u32[]{:S(2)}) copy-start(bf16[2,64,512]{2,1,0:T(8,128)(2,1)S(1)} %collective-permute-done.1.refs_1_) | copy-start | bytes 393220
  44.6 3.4 %copy-start.17 = (bf16[2,64,512]{2,1,0:T(8,128)(2,1)}, bf16[2,64,512]{2,1,0:T(8,128)(2,1)S(1)}, u32[]{:S(2)}) copy-start(bf16[2,64,512]{2,1,0:T(8,128)(2,1)S(1)} %collective-permute-done.2.refs_2_) | copy-start | bytes 393220
  48.6 14.0 %copy-start.14 = (bf16[2,64,512]{2,1,0:T(8,128)(2,1)S(1)}, bf16[2,64,512]{2,1,0:T(8,128)(2,1)}, u32[]{:S(2)}) copy-start(bf16[2,64,512]{2,1,0:T(8,128)(2,1)} %get-tuple-element.39.refs_0_) | copy-start | bytes 393220
  48.6 15.5 %copy-start.16 = (bf16[2,64,512]{2,1,0:T(8,128)(2,1)S(1)}, bf16[2,64,512]{2,1,0:T(8,128)(2,1)}, u32[]{:S(2)}) copy-start(bf16[2,64,512]{2,1,0:T(8,128)(2,1)} %copy-done.15) | copy-start | bytes 393220
  48.6 15.6 %copy-start.18 = (bf16[2,64,512]{2,1,0:T(8,128)(2,1)S(1)}, bf16[2,64,512]{2,1,0:T(8,128)(2,1)}, u32[]{:S(2)}) copy-start(bf16[2,64,512]{2,1,0:T(8,128)(2,1)} %copy-done.17) | copy-start | bytes 393220
  48.6 41.5 %all-to-all-start.1 = ((bf16[8,3,2,64,256]{4,3,2,1,0:T(8,128)(2,1)}), bf16[8,3,2,64,256]{4,3,2,1,0:T(8,128)(2,1)}, u32[]{:S(2)}, u32[]{:S(2)}) async-start(bf16[8,3,2,64,256]{4,3,2,1,0:T(8,128)(2,1)} %after.2), calls=%async_computation.1 | async-start | bytes 3145728 | tf_op jit(solution)/shard_map/all_to_all | solution.py:455
  62.7 12.0 %copy-start.2 = (bf16[1024,512]{1,0:T(8,128)(2,1)S(1)}, bf16[1024,512]{1,0:T(8,128)(2,1)}, u32[]{:S(2)}) copy-start(bf16[1024,512]{1,0:T(8,128)(2,1)} %k_ref.9) | copy-start | bytes 3145732
  62.7 7.5 %collective-permute-start.4 = (bf16[2,64,512]{2,1,0:T(8,128)(2,1)S(1)}, bf16[2,64,512]{2,1,0:T(8,128)(2,1)}, u32[]{:S(2)}, u32[]{:S(2)}) collective-permute-start(bf16[2,64,512]{2,1,0:T(8,128)(2,1)S(1)} %copy-done.14), channel_id=1, source_target_pairs={{0,4},{4,0},{8,12},{12,8},{16,20},{20,16},{24,28},{28,24},{1,5},{5... | collective-permute-start | bytes 393224 | tf_op jit(solution)/shard_map/ppermute | solution.py:387
  64.1 6.0 %collective-permute-start.5 = (bf16[2,64,512]{2,1,0:T(8,128)(2,1)S(1)}, bf16[2,64,512]{2,1,0:T(8,128)(2,1)}, u32[]{:S(2)}, u32[]{:S(2)}) collective-permute-start(bf16[2,64,512]{2,1,0:T(8,128)(2,1)S(1)} %copy-done.16), channel_id=1, source_target_pairs={{0,4},{4,0},{8,12},{12,8},{16,20},{20,16},{24,28},{28,24},{1,5},{5... | collective-permute-start | bytes 393224 | tf_op jit(solution)/shard_map/ppermute | solution.py:387
  64.2 8.0 %collective-permute-start.6 = (bf16[2,64,512]{2,1,0:T(8,128)(2,1)S(1)}, bf16[2,64,512]{2,1,0:T(8,128)(2,1)}, u32[]{:S(2)}, u32[]{:S(2)}) collective-permute-start(bf16[2,64,512]{2,1,0:T(8,128)(2,1)S(1)} %copy-done.18), channel_id=1, source_target_pairs={{0,4},{4,0},{8,12},{12,8},{16,20},{20,16},{24,28},{28,24},{1,5},{5... | collective-permute-start | bytes 393224 | tf_op jit(solution)/shard_map/ppermute | solution.py:387
  64.6 7.6 %collective-permute-start.7 = (bf16[2,64,512]{2,1,0:T(8,128)(2,1)}, bf16[2,64,512]{2,1,0:T(8,128)(2,1)}, u32[]{:S(2)}, u32[]{:S(2)}) collective-permute-start(bf16[2,64,512]{2,1,0:T(8,128)(2,1)} %copy-done.19), channel_id=1, source_target_pairs={{0,4},{4,0},{8,12},{12,8},{16,20},{20,16},{24,28},{28,24},{1,5},{5... | collective-permute-start | bytes 393224 | tf_op jit(solution)/shard_map/ppermute | solution.py:387
  64.7 9.9 %copy-start.3 = (bf16[1024,512]{1,0:T(8,128)(2,1)S(1)}, bf16[1024,512]{1,0:T(8,128)(2,1)}, u32[]{:S(2)}) copy-start(bf16[1024,512]{1,0:T(8,128)(2,1)} %v_ref.9) | copy-start | bytes 3145732
  64.7 9.9 %copy-start.20 = (bf16[2,64,512]{2,1,0:T(8,128)(2,1)S(1)}, bf16[2,64,512]{2,1,0:T(8,128)(2,1)}, u32[]{:S(2)}) copy-start(bf16[2,64,512]{2,1,0:T(8,128)(2,1)} %copy-done.19) | copy-start | bytes 393220
  70.1 23.0 %collective-permute-start.10 = (bf16[2,64,256]{2,1,0:T(8,128)(2,1)}, bf16[2,64,256]{2,1,0:T(8,128)(2,1)}, u32[]{:S(2)}, u32[]{:S(2)}) collective-permute-start(bf16[2,64,256]{2,1,0:T(8,128)(2,1)} %get-tuple-element.45), channel_id=1, source_target_pairs={{0,12},{4,8},{8,4},{12,0},{16,28},{20,24},{24,20},{28,16},{1,13},{... | collective-permute-start | bytes 196616 | tf_op jit(solution)/shard_map/ppermute | solution.py:470
  70.1 23.7 %collective-permute-start.11 = (bf16[2,64,256]{2,1,0:T(8,128)(2,1)}, bf16[2,64,256]{2,1,0:T(8,128)(2,1)}, u32[]{:S(2)}, u32[]{:S(2)}) collective-permute-start(bf16[2,64,256]{2,1,0:T(8,128)(2,1)} %get-tuple-element.46), channel_id=1, source_target_pairs={{0,16},{4,20},{8,24},{12,28},{16,0},{20,4},{24,8},{28,12},{1,17},{... | collective-permute-start | bytes 196616 | tf_op jit(solution)/shard_map/ppermute | solution.py:470
  72.2 23.0 %collective-permute-start.12 = (bf16[2,64,256]{2,1,0:T(8,128)(2,1)}, bf16[2,64,256]{2,1,0:T(8,128)(2,1)}, u32[]{:S(2)}, u32[]{:S(2)}) collective-permute-start(bf16[2,64,256]{2,1,0:T(8,128)(2,1)} %get-tuple-element.47), channel_id=1, source_target_pairs={{0,20},{4,16},{8,28},{12,24},{16,4},{20,0},{24,12},{28,8},{1,21},{... | collective-permute-start | bytes 196616 | tf_op jit(solution)/shard_map/ppermute | solution.py:470
  72.2 23.2 %collective-permute-start.13 = (bf16[2,64,256]{2,1,0:T(8,128)(2,1)}, bf16[2,64,256]{2,1,0:T(8,128)(2,1)}, u32[]{:S(2)}, u32[]{:S(2)}) collective-permute-start(bf16[2,64,256]{2,1,0:T(8,128)(2,1)} %get-tuple-element.48), channel_id=1, source_target_pairs={{0,24},{4,28},{8,16},{12,20},{16,8},{20,12},{24,0},{28,4},{1,25},{... | collective-permute-start | bytes 196616 | tf_op jit(solution)/shard_map/ppermute | solution.py:470
  73.7 22.2 %collective-permute-start.14 = (bf16[2,64,256]{2,1,0:T(8,128)(2,1)}, bf16[2,64,256]{2,1,0:T(8,128)(2,1)}, u32[]{:S(2)}, u32[]{:S(2)}) collective-permute-start(bf16[2,64,256]{2,1,0:T(8,128)(2,1)} %get-tuple-element.49), channel_id=1, source_target_pairs={{0,28},{4,24},{8,20},{12,16},{16,12},{20,8},{24,4},{28,0},{1,29},{... | collective-permute-start | bytes 196616 | tf_op jit(solution)/shard_map/ppermute | solution.py:470
  90.1 3.0 %copy-start.26 = (bf16[2,64,256]{2,1,0:T(8,128)(2,1)S(1)}, bf16[2,64,256]{2,1,0:T(8,128)(2,1)}, u32[]{:S(2)}) copy-start(bf16[2,64,256]{2,1,0:T(8,128)(2,1)} %copy-done.25) | copy-start | bytes 196612
  90.1 3.8 %copy-start.24 = (bf16[2,64,256]{2,1,0:T(8,128)(2,1)S(1)}, bf16[2,64,256]{2,1,0:T(8,128)(2,1)}, u32[]{:S(2)}) copy-start(bf16[2,64,256]{2,1,0:T(8,128)(2,1)} %copy-done.23) | copy-start | bytes 196612
  90.1 8.0 %copy-start.8 = (f32[1024,256]{1,0:T(8,128)S(1)}, f32[1024,256]{1,0:T(8,128)}, u32[]{:S(2)}) copy-start(f32[1024,256]{1,0:T(8,128)} %copy-done.7) | copy-start | bytes 3145732
  90.1 8.0 %copy-start.22 = (bf16[2,64,256]{2,1,0:T(8,128)(2,1)S(1)}, bf16[2,64,256]{2,1,0:T(8,128)(2,1)}, u32[]{:S(2)}) copy-start(bf16[2,64,256]{2,1,0:T(8,128)(2,1)} %copy-done.21) | copy-start | bytes 196612
  90.1 26.4 %copy-start.6 = (f32[1024,256]{1,0:T(8,128)S(1)}, f32[1024,256]{1,0:T(8,128)}, u32[]{:S(2)}) copy-start(f32[1024,256]{1,0:T(8,128)} %copy-done.5) | copy-start | bytes 3145732
  93.1 4.1 %collective-permute-start.8 = (bf16[2,64,256]{2,1,0:T(8,128)(2,1)S(1)}, bf16[2,64,256]{2,1,0:T(8,128)(2,1)S(1)}, u32[]{:S(2)}, u32[]{:S(2)}) collective-permute-start(bf16[2,64,256]{2,1,0:T(8,128)(2,1)S(1)} %copy-done.26), channel_id=1, source_target_pairs={{0,4},{4,0},{8,12},{12,8},{16,20},{20,16},{24,28},{28,24},{1,5},{5... | collective-permute-start | bytes 196616 | tf_op jit(solution)/shard_map/ppermute | solution.py:470
  93.8 4.3 %collective-permute-start.9 = (bf16[2,64,256]{2,1,0:T(8,128)(2,1)S(1)}, bf16[2,64,256]{2,1,0:T(8,128)(2,1)S(1)}, u32[]{:S(2)}, u32[]{:S(2)}) collective-permute-start(bf16[2,64,256]{2,1,0:T(8,128)(2,1)S(1)} %copy-done.24), channel_id=1, source_target_pairs={{0,8},{4,12},{8,0},{12,4},{16,24},{20,28},{24,16},{28,20},{1,9},{5... | collective-permute-start | bytes 196616 | tf_op jit(solution)/shard_map/ppermute | solution.py:470
  95.2 6.3 %collective-permute-start.18 = (bf16[2,64,256]{2,1,0:T(8,128)(2,1)S(1)}, bf16[2,64,256]{2,1,0:T(8,128)(2,1)S(1)}, u32[]{:S(2)}, u32[]{:S(2)}) collective-permute-start(bf16[2,64,256]{2,1,0:T(8,128)(2,1)S(1)} %get-tuple-element.59), channel_id=1, source_target_pairs={{0,4},{4,0},{8,12},{12,8},{16,20},{20,16},{24,28},{28,24},{1,5},{5... | collective-permute-start | bytes 196616 | tf_op jit(solution)/shard_map/ppermute | solution.py:470
  95.4 6.2 %collective-permute-start.19 = (bf16[2,64,256]{2,1,0:T(8,128)(2,1)S(1)}, bf16[2,64,256]{2,1,0:T(8,128)(2,1)S(1)}, u32[]{:S(2)}, u32[]{:S(2)}) collective-permute-start(bf16[2,64,256]{2,1,0:T(8,128)(2,1)S(1)} %get-tuple-element.60), channel_id=1, source_target_pairs={{0,8},{4,12},{8,0},{12,4},{16,24},{20,28},{24,16},{28,20},{1,9},{5... | collective-permute-start | bytes 196616 | tf_op jit(solution)/shard_map/ppermute | solution.py:470
  95.9 8.3 %collective-permute-start.20 = (bf16[2,64,256]{2,1,0:T(8,128)(2,1)S(1)}, bf16[2,64,256]{2,1,0:T(8,128)(2,1)S(1)}, u32[]{:S(2)}, u32[]{:S(2)}) collective-permute-start(bf16[2,64,256]{2,1,0:T(8,128)(2,1)S(1)} %get-tuple-element.61), channel_id=1, source_target_pairs={{0,12},{4,8},{8,4},{12,0},{16,28},{20,24},{24,20},{28,16},{1,13},{... | collective-permute-start | bytes 196616 | tf_op jit(solution)/shard_map/ppermute | solution.py:470
  99.4 12.2 %collective-permute-start.15 = (bf16[256,256]{1,0:T(8,128)(2,1)S(1)}, bf16[256,256]{1,0:T(8,128)(2,1)S(1)}, u32[]{:S(2)}, u32[]{:S(2)}) collective-permute-start(bf16[256,256]{1,0:T(8,128)(2,1)S(1)} %get-tuple-element.54), channel_id=1, source_target_pairs={{0,1},{1,0},{2,3},{3,2},{4,5},{5,4},{6,7},{7,6},{8,9},{9,8},{10,11... | collective-permute-start | bytes 393224 | tf_op jit(solution)/shard_map/ppermute | solution.py:470
  99.5 5.6 %collective-permute-start.21 = (bf16[2,64,256]{2,1,0:T(8,128)(2,1)S(1)}, bf16[2,64,256]{2,1,0:T(8,128)(2,1)S(1)}, u32[]{:S(2)}, u32[]{:S(2)}) collective-permute-start(bf16[2,64,256]{2,1,0:T(8,128)(2,1)S(1)} %get-tuple-element.62), channel_id=1, source_target_pairs={{0,16},{4,20},{8,24},{12,28},{16,0},{20,4},{24,8},{28,12},{1,17},{... | collective-permute-start | bytes 196616 | tf_op jit(solution)/shard_map/ppermute | solution.py:470
  101.6 4.9 %collective-permute-start.22 = (bf16[2,64,256]{2,1,0:T(8,128)(2,1)S(1)}, bf16[2,64,256]{2,1,0:T(8,128)(2,1)S(1)}, u32[]{:S(2)}, u32[]{:S(2)}) collective-permute-start(bf16[2,64,256]{2,1,0:T(8,128)(2,1)S(1)} %get-tuple-element.63), channel_id=1, source_target_pairs={{0,20},{4,16},{8,28},{12,24},{16,4},{20,0},{24,12},{28,8},{1,21},{... | collective-permute-start | bytes 196616 | tf_op jit(solution)/shard_map/ppermute | solution.py:470
  101.6 12.1 %collective-permute-start.16 = (bf16[256,256]{1,0:T(8,128)(2,1)S(1)}, bf16[256,256]{1,0:T(8,128)(2,1)S(1)}, u32[]{:S(2)}, u32[]{:S(2)}) collective-permute-start(bf16[256,256]{1,0:T(8,128)(2,1)S(1)} %get-tuple-element.55), channel_id=1, source_target_pairs={{0,2},{1,3},{2,0},{3,1},{4,6},{5,7},{6,4},{7,5},{8,10},{9,11},{10,... | collective-permute-start | bytes 393224 | tf_op jit(solution)/shard_map/ppermute | solution.py:470
  104.2 12.3 %collective-permute-start.17 = (bf16[256,256]{1,0:T(8,128)(2,1)S(1)}, bf16[256,256]{1,0:T(8,128)(2,1)S(1)}, u32[]{:S(2)}, u32[]{:S(2)}) collective-permute-start(bf16[256,256]{1,0:T(8,128)(2,1)S(1)} %get-tuple-element.56), channel_id=1, source_target_pairs={{0,3},{1,2},{2,1},{3,0},{4,7},{5,6},{6,5},{7,4},{8,11},{9,10},{10,... | collective-permute-start | bytes 393224 | tf_op jit(solution)/shard_map/ppermute | solution.py:470
  105.0 5.2 %collective-permute-start.23 = (bf16[2,64,256]{2,1,0:T(8,128)(2,1)S(1)}, bf16[2,64,256]{2,1,0:T(8,128)(2,1)S(1)}, u32[]{:S(2)}, u32[]{:S(2)}) collective-permute-start(bf16[2,64,256]{2,1,0:T(8,128)(2,1)S(1)} %get-tuple-element.64), channel_id=1, source_target_pairs={{0,24},{4,28},{8,16},{12,20},{16,8},{20,12},{24,0},{28,4},{1,25},{... | collective-permute-start | bytes 196616 | tf_op jit(solution)/shard_map/ppermute | solution.py:470
  106.5 5.1 %collective-permute-start.24 = (bf16[2,64,256]{2,1,0:T(8,128)(2,1)S(1)}, bf16[2,64,256]{2,1,0:T(8,128)(2,1)S(1)}, u32[]{:S(2)}, u32[]{:S(2)}) collective-permute-start(bf16[2,64,256]{2,1,0:T(8,128)(2,1)S(1)} %get-tuple-element.65), channel_id=1, source_target_pairs={{0,28},{4,24},{8,20},{12,16},{16,12},{20,8},{24,4},{28,0},{1,29},{... | collective-permute-start | bytes 196616 | tf_op jit(solution)/shard_map/ppermute | solution.py:470
  117.9 10.1 %collective-permute-start.26 = (bf16[256,256]{1,0:T(8,128)(2,1)S(1)}, bf16[256,256]{1,0:T(8,128)(2,1)S(1)}, u32[]{:S(2)}, u32[]{:S(2)}) collective-permute-start(bf16[256,256]{1,0:T(8,128)(2,1)S(1)} %get-tuple-element.69), channel_id=1, source_target_pairs={{0,2},{1,3},{2,0},{3,1},{4,6},{5,7},{6,4},{7,5},{8,10},{9,11},{10,... | collective-permute-start | bytes 393224 | tf_op jit(solution)/shard_map/ppermute | solution.py:470
  118.5 12.5 %collective-permute-start.27 = (bf16[256,256]{1,0:T(8,128)(2,1)S(1)}, bf16[256,256]{1,0:T(8,128)(2,1)S(1)}, u32[]{:S(2)}, u32[]{:S(2)}) collective-permute-start(bf16[256,256]{1,0:T(8,128)(2,1)S(1)} %get-tuple-element.70), channel_id=1, source_target_pairs={{0,3},{1,2},{2,1},{3,0},{4,7},{5,6},{6,5},{7,4},{8,11},{9,10},{10,... | collective-permute-start | bytes 393224 | tf_op jit(solution)/shard_map/ppermute | solution.py:470
  128.0 2.9 %copy-start.9 = (bf16[256,256]{1,0:T(8,128)(2,1)}, bf16[256,256]{1,0:T(8,128)(2,1)S(1)}, u32[]{:S(2)}) copy-start(bf16[256,256]{1,0:T(8,128)(2,1)S(1)} %collective-permute-done.26.refs_1_.refs_6_) | copy-start | bytes 393220
  131.6 7.4 %collective-permute-start.28 = (bf16[4,512,1024]{2,1,0:T(8,128)(2,1)}, bf16[4,512,1024]{2,1,0:T(8,128)(2,1)S(1)}, u32[]{:S(2)}, u32[]{:S(2)}) collective-permute-start(bf16[4,512,1024]{2,1,0:T(8,128)(2,1)} %after.3.refs_8_), channel_id=1, source_target_pairs={{0,4},{4,0},{8,12},{12,8},{16,20},{20,16},{24,28},{28,24},{1,5},{5... | collective-permute-start | bytes 12582920 | tf_op jit(solution)/shard_map/ppermute | solution.py:499
  131.6 5.9 %collective-permute-start.25 = (bf16[256,256]{1,0:T(8,128)(2,1)S(1)}, bf16[256,256]{1,0:T(8,128)(2,1)S(1)}, u32[]{:S(2)}, u32[]{:S(2)}) collective-permute-start(bf16[256,256]{1,0:T(8,128)(2,1)S(1)} %get-tuple-element.68), channel_id=1, source_target_pairs={{0,1},{1,0},{2,3},{3,2},{4,5},{5,4},{6,7},{7,6},{8,9},{9,8},{10,11... | collective-permute-start | bytes 393224 | tf_op jit(solution)/shard_map/ppermute | solution.py:470
  139.0 2.2 %copy-start.1 = (bf16[4,512,1024]{2,1,0:T(8,128)(2,1)S(1)}, bf16[4,512,1024]{2,1,0:T(8,128)(2,1)}, u32[]{:S(2)}) copy-start(bf16[4,512,1024]{2,1,0:T(8,128)(2,1)} %after.3.refs_8_) | copy-start | bytes 12582916
  (11 other events, 9.7 us)
Sparse Core Ops, SparseCore 0:
  9.4 79.4 all-gather.2

commit v4 on v3

--- a/solution.py
+++ b/solution.py
@@ -100,42 +100,45 @@
     return total[:, :HEAD_SIZE] / total[:, HEAD_SIZE:]
 
 
-def edge_kernel(k_ref, v_ref, rim_ref, sum_ref, *, rim_start):
-    picks = TILE // BLOCK * SUMCOLS
-    row = iota2((picks, TILE), 0)
-    col = iota2((picks, TILE), 1)
-    pick = (col == (row // SUMCOLS) * BLOCK + BLOCK - SUMCOLS + row % SUMCOLS).astype(BF16)
-    sum_ref[0] = dot(pick, k_ref[...]).astype(BF16)
-    sum_ref[1] = dot(pick, v_ref[...]).astype(BF16)
-
-    @pl.when(pl.program_id(0) >= rim_start)
+def edge_kernel(k_ref, v_ref, k_ends_ref, v_ends_ref, rim_ref, sum_ref):
+    rim_ref[0] = k_ref[...]
+    rim_ref[1] = v_ref[...]
+
+    @pl.when(pl.program_id(0) == 0)
     def _():
-        rim_ref[0] = k_ref[...]
-        rim_ref[1] = v_ref[...]
+        for number, ref in enumerate((k_ends_ref, v_ends_ref)):
+            rows = ref[...].astype(F32)[:, 16 - SUMCOLS :]
+            sum_ref[number] = rows.reshape(sum_ref.shape[1:]).astype(BF16)
 
 
 def edges(keys, values):
     tokens_dev, width = keys.shape
-    tiles = tokens_dev // TILE
-    rim_start = tiles - WINDOW // TILE
-    picks = TILE // BLOCK * SUMCOLS
-    source = pl.BlockSpec((TILE, width), lambda b: (b, 0))
-    return pl.pallas_call(
-        functools.partial(edge_kernel, rim_start=rim_start),
-        grid=(tiles,),
-        in_specs=[source] * 2,
+    blocks = tokens_dev // BLOCK
+    first = (tokens_dev - WINDOW) // TILE
+    source = pl.BlockSpec((TILE, width), lambda i: (first + i, 0))
+    ends = pl.BlockSpec((blocks, 16, width), lambda i: (0, BLOCK // 16 - 1, 0))
+    shape = (2, blocks * SUMCOLS, width)
+    return pl.pallas_call(
+        edge_kernel,
+        grid=(WINDOW // TILE,),
+        in_specs=[source] * 2 + [ends] * 2,
         out_specs=[
-            pl.BlockSpec((2, TILE, width), lambda b: (0, jnp.maximum(b - rim_start, 0), 0)),
-            pl.BlockSpec((2, picks, width), lambda b: (0, b, 0)),
+            pl.BlockSpec((2, TILE, width), lambda i: (0, i, 0)),
+            pl.BlockSpec(shape, lambda i: (0, 0, 0)),
         ],
         out_shape=[
             jax.ShapeDtypeStruct((2, WINDOW, width), BF16),
-            jax.ShapeDtypeStruct((2, tiles * picks, width), BF16),
+            jax.ShapeDtypeStruct(shape, BF16),
         ],
         compiler_params=params(60),
-        cost_estimate=cost(4 * tokens_dev * picks * width, 7 * tokens_dev * width),
+        cost_estimate=cost(0, 8 * WINDOW * width),
         name="edges",
-    )(keys, values)
+    )(
+        keys,
+        values,
+        keys.reshape(blocks, BLOCK, width),
+        values.reshape(blocks, BLOCK, width),
+    )
 
 
 def prep_kernel(q_ref, k_ref, v_ref, *refs):
@@ -232,7 +235,7 @@
         + moments(waits),
         out_specs=[pl.BlockSpec((tokens_dev, HEAD_SIZE), lambda h: (0, h)), mark_spec()],
         out_shape=[jax.ShapeDtypeStruct((tokens_dev, heads * HEAD_SIZE), F32), MARK],
-        compiler_params=params(24),
+        compiler_params=params(60),
         cost_estimate=cost(8 * pairs * HEAD_SIZE, 14 * tokens_dev * width, pairs),
         name="home",
     )(place, queries, keys, values, rim, *summary, *waits)
@@ -446,14 +449,11 @@
     if ctx > STRIDE:
         stride_out = stride_general(queries, keys, values)
     else:
-        received = []
-        for chunk in range(chunks):
-            send = prepare(queries, keys, values, ctx, chunk, chunks, (picked,))
-            if chunk > 0:
-                send = after(send, between[1:])
-            received.append(
-                lax.all_to_all(send, "ctx", split_axis=0, concat_axis=0, tiled=True)
-            )
+        sends = [
+            prepare(queries, keys, values, ctx, chunk, chunks, within[-1:] if chunk else (picked,))
+            for chunk in range(chunks)
+        ]
+        sends[0] = after(sends[0], (between[-1], before))
 
     def home(chunk, waits):
         return home_sections(
@@ -484,18 +484,21 @@
         seats = jnp.stack([seat, place.astype(jnp.int32)])
         homes, backs = [], []
         for chunk in range(chunks):
-            *slabs, mark = stride_attend(place_word, received[chunk], waits)
+            sections, mark = home(chunk, waits)
+            homes.append(sections)
+            waits = (mark,)
+        if chunks > 1:
+            sends[1] = after(sends[1], waits)
+        for chunk in range(chunks):
+            received = lax.all_to_all(sends[chunk], "ctx", split_axis=0, concat_axis=0, tiled=True)
+            *slabs, mark = stride_attend(place_word, received, waits)
             backs.append(exchange(slabs, "ctx"))
             waits = (mark,)
-            for ready in range(chunks) if chunk == 0 else ():
-                sections, mark = home(ready, waits)
-                homes.append(sections)
-                waits = (mark,)
         for chunk in range(chunks):
             *slabs, mark = combine(seats, homes[chunk], backs[chunk], groups, waits)
             moved.append(exchange(slabs, "head"))
             waits = (mark, *moved[-1][1:])
-    held = after(mine, moved[-1][2:])
+    held = after(mine, (mark,))
     other = lax.ppermute(held, "ctx", sibling)
     sides = jnp.stack([side.astype(jnp.int32), seat])
     return project(sides, moved, held, other)

time: 159 us -> 166 us (1.044); the launches traced: 156 us -> 165 us
  waiting for transfers between devices: 45.1 us -> 62.7 us
  starting transfers between devices: 44.2 us -> 37.1 us
    all_to_all x2, waiting for transfers between devices: 0.01 us -> 10.4 us  [body(): lax.all_to_all(sends[chunk], 'ctx', split_axis=0, concat_axis=0, tiled=True)]
    ppermute x1, waiting for transfers between devices: 0.01 us -> 8.31 us  [body(): before = lax.ppermute(rim, 'ctx', [(i, i + 1) for i in range(ctx - 1)])]
    all_to_all x2, starting transfers between devices: 18.9 us -> 11.6 us  [body(): lax.all_to_all(sends[chunk], 'ctx', split_axis=0, concat_axis=0, tiled=True)]
    ppermute x7, waiting for transfers between devices: 15.9 us -> 21.5 us  [swapped(): return lax.ppermute(piece, 'ctx', [(i, i ^ distance) for i in range(count)])]
    ppermute x20, waiting for transfers between devices: 27.7 us -> 22.4 us  [exchange(): moved.append(lax.ppermute(slabs[slot], axis, pairs))]
    pallas_call x2, Pallas kernels: 12.2 us -> 14.3 us  [home_sections(): pl.pallas_call(functools.partial(home_kernel, order=order), grid=(heads,)...]
    pallas_call x1, Pallas kernels: 3.89 us -> 2.18 us  [edges(): pl.pallas_call(edge_kernel, grid=(WINDOW // TILE,), in_specs=[source] * 2...]
    unnamed x54 -> x48, local copies, waits for them, and re-layouts: 11.9 us -> 10.9 us
  transfers between devices with their start and end apart: 32 -> 32, of which waited for: 12 -> 12; matrix products, arithmetic and copies ran while one was open for 0% -> 0% of each run, Pallas kernels for 22% -> 20%
where the time goes in v4:
time: 166 us; the launch traced here: 165 us
  waiting for transfers between devices  62.7 us (38%)
  Pallas kernels  39.9 us (24%)
  starting transfers between devices  37.1 us (22%)
  between operations  13.6 us (8%)
  local copies, waits for them, and re-layouts  12 us (7%)
    ppermute x20, waiting for transfers between devices, exchange(): moved.append(lax.ppermute(slabs[slot], axis, pairs))  22.4 us
    ppermute x7, waiting for transfers between devices, swapped(): return lax.ppermute(piece, 'ctx', [(i, i ^ distance) for i in range(count)])  21.5 us
    ppermute x20, starting transfers between devices, exchange(): moved.append(lax.ppermute(slabs[slot], axis, pairs))  19.2 us
    pallas_call x2, Pallas kernels, home_sections(): pl.pallas_call(functools.partial(home_kernel, order=order), grid=(heads,)...  14.3 us
    all_to_all x2, starting transfers between devices, body(): lax.all_to_all(sends[chunk], 'ctx', split_axis=0, concat_axis=0, tiled=True)  11.6 us
    unnamed x48, local copies, waits for them, and re-layouts  10.9 us
    all_to_all x2, waiting for transfers between devices, body(): lax.all_to_all(sends[chunk], 'ctx', split_axis=0, concat_axis=0, tiled=True)  10.4 us
    pallas_call x2, Pallas kernels, prepare(): pl.pallas_call(prep_kernel, grid=(tokens_dev // TILE,), in_specs=[pl.Bloc...  8.43 us
  transfers between devices with their start and end apart: 32, of which 12 were waited for; matrix products, arithmetic and copies ran while one was open for 0% of the time, Pallas kernels for 20%

profile of v4, /device:TPU:10, one launch (start us, length us, event | category | flops | bytes accessed | tf_op | source)
XLA Modules:
  0.0 165.5 jit_solution(6434337918987861071)
XLA Ops:
  6.5 1.6 copy-done
  8.1 1.1 constant_dynamic-slice_fusion
  9.3 2.2 %edges.1 = (bf16[2,512,512]{2,1,0:T(8,128)(2,1)}, bf16[2,64,512]{2,1,0:T(8,128)(2,1)}) custom-call(bf16[1024,512]{1,0:T(8,128)(2,1)} %k_ref.9, bf16[1024,512]{1,0:T(8,128)(2,1)} %v_ref.9, bf16[8,128,512]{2,1,0:T(8,128)(2,1)} %bitcast.7, bf16[8,128,512]{2,1,0:T(8,128)(2,1)} %bitcast.8), custom_call_target="tpu_custom_call" | custom-call | bytes 2097152 | tf_op jit(solution)/shard_map/edges/pallas_call | solution.py:121
  11.4 1.9 %collective-permute-start = (bf16[2,512,512]{2,1,0:T(8,128)(2,1)}, bf16[2,512,512]{2,1,0:T(8,128)(2,1)S(1)}, u32[]{:S(2)}, u32[]{:S(2)}) collective-permute-start(bf16[2,512,512]{2,1,0:T(8,128)(2,1)} %get-tuple-element.39), channel_id=1, source_target_pairs={{0,4},{4,8},{8,12},{12,16},{16,20},{20,24},{24,28},{1,5},{5,9},{9,... | collective-permute-start | bytes 3145736 | tf_op jit(solution)/shard_map/ppermute | solution.py:448
  13.3 1.6 collective-permute-start.3
  14.9 4.2 %prepare.2.refs_0_ = bf16[8,3,2,64,256]{4,3,2,1,0:T(8,128)(2,1)} custom-call(bf16[1024,512]{1,0:T(8,128)(2,1)} %q_ref.7, bf16[1024,512]{1,0:T(8,128)(2,1)} %k_ref.9, bf16[1024,512]{1,0:T(8,128)(2,1)} %v_ref.9, bf16[2,64,512]{2,1,0:T(8,128)(2,1)} %get-tuple-element.40.refs_0_), custom_call_target="tpu_custom_call" | custom-call | flops 402653184 | bytes 3145728 | tf_op jit(solution)/shard_map/prepare/pallas_call | solution.py:157
  19.1 1.7 %collective-permute-done.3.refs_3_.refs_1_ = bf16[2,64,512]{2,1,0:T(8,128)(2,1)S(1)} collective-permute-done((bf16[2,64,512]{2,1,0:T(8,128)(2,1)}, bf16[2,64,512]{2,1,0:T(8,128)(2,1)S(1)}, u32[]{:S(2)}, u32[]{:S(2)}) %collective-permute-start.3) | collective-permute-done | bytes 131104 | tf_op jit(solution)/shard_map/ppermute | solution.py:390
  20.8 8.3 %collective-permute-done.rim_ref.refs_2_ = bf16[2,512,512]{2,1,0:T(8,128)(2,1)S(1)} collective-permute-done((bf16[2,512,512]{2,1,0:T(8,128)(2,1)}, bf16[2,512,512]{2,1,0:T(8,128)(2,1)S(1)}, u32[]{:S(2)}, u32[]{:S(2)}) %collective-permute-start) | collective-permute-done | bytes 1048608 | tf_op jit(solution)/shard_map/ppermute | solution.py:448
  29.2 1.0 copy-done.14
  30.1 6.2 %all-to-all-start = ((bf16[8,3,2,64,256]{4,3,2,1,0:T(8,128)(2,1)}), bf16[8,3,2,64,256]{4,3,2,1,0:T(8,128)(2,1)}, u32[]{:S(2)}, u32[]{:S(2)}) async-start(bf16[8,3,2,64,256]{4,3,2,1,0:T(8,128)(2,1)} %after.3), calls=%async_computation | async-start | bytes 3145728 | tf_op jit(solution)/shard_map/all_to_all | solution.py:493
  36.4 2.0 %collective-permute-start.2 = (bf16[2,64,512]{2,1,0:T(8,128)(2,1)S(1)}, bf16[2,64,512]{2,1,0:T(8,128)(2,1)S(1)}, u32[]{:S(2)}, u32[]{:S(2)}) collective-permute-start(bf16[2,64,512]{2,1,0:T(8,128)(2,1)S(1)} %copy-done.15), channel_id=1, source_target_pairs={{0,16},{4,20},{8,24},{12,28},{16,0},{20,4},{24,8},{28,12},{1,17},{... | collective-permute-start | bytes 393224 | tf_op jit(solution)/shard_map/ppermute | solution.py:390
  38.4 0.7 collective-permute-start.7
  39.1 18.6 %collective-permute-done.1.refs_1_ = bf16[2,64,512]{2,1,0:T(8,128)(2,1)S(1)} collective-permute-done((bf16[2,64,512]{2,1,0:T(8,128)(2,1)S(1)}, bf16[2,64,512]{2,1,0:T(8,128)(2,1)S(1)}, u32[]{:S(2)}, u32[]{:S(2)}) %collective-permute-start.1) | collective-permute-done | bytes 131104 | tf_op jit(solution)/shard_map/ppermute | solution.py:390
  57.7 1.2 collective-permute-done.2.refs_2_
  58.9 0.7 copy-done.18
  59.6 4.2 %prepare.3.refs_0_ = bf16[8,3,2,64,256]{4,3,2,1,0:T(8,128)(2,1)} custom-call(bf16[1024,512]{1,0:T(8,128)(2,1)} %q_ref.7, bf16[1024,512]{1,0:T(8,128)(2,1)} %k_ref.9, bf16[1024,512]{1,0:T(8,128)(2,1)} %v_ref.9, bf16[2,64,512]{2,1,0:T(8,128)(2,1)} %copy-done.18), custom_call_target="tpu_custom_call" | custom-call | flops 402653184 | bytes 3145728 | tf_op jit(solution)/shard_map/prepare/pallas_call | solution.py:157
  63.9 0.6 copy-done.21
  64.6 7.1 %home.2 = (f32[1024,256]{1,0:T(8,128)}, f32[8,128]{1,0:T(8,128)}) custom-call(s32[1]{0:T(128)} %bitcast.2.place_ref, bf16[1024,512]{1,0:T(8,128)(2,1)} %q_ref.7, bf16[1024,512]{1,0:T(8,128)(2,1)} %k_ref.9, bf16[1024,512]{1,0:T(8,128)(2,1)} %v_ref.9, bf16[2,512,512]{2,1,0:T(8,128)(2,1)} %copy-done.14, bf16[2,64,512]{2,1,0:T(8,128)(2,1)} %get-tuple-element.40.refs_0_, ...), custom_call_target="tpu_custom_call" | custom-call | flops 2684354560 | bytes 7340032 | tf_op jit(solution)/shard_map/home/pallas_call | solution.py:224
  71.7 7.2 %home.3 = (f32[1024,256]{1,0:T(8,128)}, f32[8,128]{1,0:T(8,128)}) custom-call(s32[1]{0:T(128)} %bitcast.2.place_ref, bf16[1024,512]{1,0:T(8,128)(2,1)} %q_ref.7, bf16[1024,512]{1,0:T(8,128)(2,1)} %k_ref.9, bf16[1024,512]{1,0:T(8,128)(2,1)} %v_ref.9, bf16[2,512,512]{2,1,0:T(8,128)(2,1)} %copy-done.14, bf16[2,64,512]{2,1,0:T(8,128)(2,1)} %get-tuple-element.40.refs_0_, ...), custom_call_target="tpu_custom_call" | custom-call | flops 2684354560 | bytes 7340032 | tf_op jit(solution)/shard_map/home/pallas_call | solution.py:224
  78.9 5.4 %all-to-all-start.1 = ((bf16[8,3,2,64,256]{4,3,2,1,0:T(8,128)(2,1)}), bf16[8,3,2,64,256]{4,3,2,1,0:T(8,128)(2,1)}, u32[]{:S(2)}, u32[]{:S(2)}) async-start(bf16[8,3,2,64,256]{4,3,2,1,0:T(8,128)(2,1)} %after.4), calls=%async_computation.1 | async-start | bytes 3145728 | tf_op jit(solution)/shard_map/all_to_all | solution.py:493
  84.3 3.4 %stride.2 = (bf16[2,64,256]{2,1,0:T(8,128)(2,1)S(1)}, bf16[2,64,256]{2,1,0:T(8,128)(2,1)S(1)}, bf16[2,64,256]{2,1,0:T(8,128)(2,1)S(1)}, bf16[2,64,256]{2,1,0:T(8...) custom-call(s32[1]{0:T(128)} %bitcast.2.place_ref, ...), custom_call_target="tpu_custom_call" | custom-call | flops 805306368 | bytes 2097152 | tf_op jit(solution)/shard_map/stride/pallas_call | solution.py:278
  87.7 0.6 copy-done.10
  88.4 0.6 copy-done.12
  89.2 1.6 collective-permute-start.11
  90.8 2.6 %collective-permute-start.13 = (bf16[2,64,256]{2,1,0:T(8,128)(2,1)}, bf16[2,64,256]{2,1,0:T(8,128)(2,1)S(1)}, u32[]{:S(2)}, u32[]{:S(2)}) collective-permute-start(bf16[2,64,256]{2,1,0:T(8,128)(2,1)} %get-tuple-element.50), channel_id=1, source_target_pairs={{0,24},{4,28},{8,16},{12,20},{16,8},{20,12},{24,0},{28,4},{1,25},{... | collective-permute-start | bytes 196616 | tf_op jit(solution)/shard_map/ppermute | solution.py:470
  93.6 10.4 %all-to-all-done.1.x_ref = bf16[8,3,2,64,256]{4,3,2,1,0:T(8,128)(2,1)} async-done(((bf16[8,3,2,64,256]{4,3,2,1,0:T(8,128)(2,1)}), bf16[8,3,2,64,256]{4,3,2,1,0:T(8,128)(2,1)}, u32[]{:S(2)}, u32[]{:S(2)}) %all-to-all-start.1) | async-done | bytes 1572896 | tf_op jit(solution)/shard_map/all_to_all | solution.py:493
  104.0 2.9 %stride.3 = (bf16[2,64,256]{2,1,0:T(8,128)(2,1)S(1)}, bf16[2,64,256]{2,1,0:T(8,128)(2,1)S(1)}, bf16[2,64,256]{2,1,0:T(8,128)(2,1)S(1)}, bf16[2,64,256]{2,1,0:T(8...) custom-call(s32[1]{0:T(128)} %bitcast.2.place_ref, ...), custom_call_target="tpu_custom_call" | custom-call | flops 805306368 | bytes 2097152 | tf_op jit(solution)/shard_map/stride/pallas_call | solution.py:278
  107.0 2.1 %collective-permute-start.9 = (bf16[2,64,256]{2,1,0:T(8,128)(2,1)S(1)}, bf16[2,64,256]{2,1,0:T(8,128)(2,1)S(1)}, u32[]{:S(2)}, u32[]{:S(2)}) collective-permute-start(bf16[2,64,256]{2,1,0:T(8,128)(2,1)S(1)} %copy-done.11), channel_id=1, source_target_pairs={{0,8},{4,12},{8,0},{12,4},{16,24},{20,28},{24,16},{28,20},{1,9},{5... | collective-permute-start | bytes 196616 | tf_op jit(solution)/shard_map/ppermute | solution.py:470
  109.5 0.6 copy-done.4
  110.5 0.6 copy-done.6
  111.1 1.4 collective-permute-start.20
  112.9 1.5 collective-permute-start.22
  114.4 0.8 copy-done.5
  115.2 0.8 copy-done.7
  116.1 0.8 combine.2
  117.5 2.2 %collective-permute-start.16 = (bf16[256,256]{1,0:T(8,128)(2,1)S(1)}, bf16[256,256]{1,0:T(8,128)(2,1)S(1)}, u32[]{:S(2)}, u32[]{:S(2)}) collective-permute-start(bf16[256,256]{1,0:T(8,128)(2,1)S(1)} %get-tuple-element.56), channel_id=1, source_target_pairs={{0,2},{1,3},{2,0},{3,1},{4,6},{5,7},{6,4},{7,5},{8,10},{9,11},{10,... | collective-permute-start | bytes 393224 | tf_op jit(solution)/shard_map/ppermute | solution.py:470
  119.7 0.8 collective-permute-start.17
  120.7 1.6 collective-permute-start.24
  122.3 3.7 %collective-permute-done.23.refs_6_ = bf16[2,64,256]{2,1,0:T(8,128)(2,1)S(1)} collective-permute-done((bf16[2,64,256]{2,1,0:T(8,128)(2,1)S(1)}, bf16[2,64,256]{2,1,0:T(8,128)(2,1)S(1)}, u32[]{:S(2)}, u32[]{:S(2)}) %collective-permute-start.23) | collective-permute-done | bytes 65568 | tf_op jit(solution)/shard_map/ppermute | solution.py:470
  126.0 3.2 %collective-permute-done.16.refs_10_.refs_2_ = bf16[256,256]{1,0:T(8,128)(2,1)S(1)} collective-permute-done((bf16[256,256]{1,0:T(8,128)(2,1)S(1)}, bf16[256,256]{1,0:T(8,128)(2,1)S(1)}, u32[]{:S(2)}, u32[]{:S(2)}) %collective-permute-start.16) | collective-permute-done | bytes 131104 | tf_op jit(solution)/shard_map/ppermute | solution.py:470
  129.2 3.2 %collective-permute-done.17.refs_11_.refs_3_ = bf16[256,256]{1,0:T(8,128)(2,1)S(1)} collective-permute-done((bf16[256,256]{1,0:T(8,128)(2,1)S(1)}, bf16[256,256]{1,0:T(8,128)(2,1)S(1)}, u32[]{:S(2)}, u32[]{:S(2)}) %collective-permute-start.17) | collective-permute-done | bytes 131104 | tf_op jit(solution)/shard_map/ppermute | solution.py:470
  132.4 1.4 combine.3
  134.5 3.0 %collective-permute-start.26 = (bf16[256,256]{1,0:T(8,128)(2,1)S(1)}, bf16[256,256]{1,0:T(8,128)(2,1)S(1)}, u32[]{:S(2)}, u32[]{:S(2)}) collective-permute-start(bf16[256,256]{1,0:T(8,128)(2,1)S(1)} %get-tuple-element.70), channel_id=1, source_target_pairs={{0,2},{1,3},{2,0},{3,1},{4,6},{5,7},{6,4},{7,5},{8,10},{9,11},{10,... | collective-permute-start | bytes 393224 | tf_op jit(solution)/shard_map/ppermute | solution.py:470
  138.0 2.9 %collective-permute-done.25.refs_5_ = bf16[256,256]{1,0:T(8,128)(2,1)S(1)} collective-permute-done((bf16[256,256]{1,0:T(8,128)(2,1)}, bf16[256,256]{1,0:T(8,128)(2,1)S(1)}, u32[]{:S(2)}, u32[]{:S(2)}) %collective-permute-start.25) | collective-permute-done | bytes 131104 | tf_op jit(solution)/shard_map/ppermute | solution.py:470
  141.0 6.0 %collective-permute-done.26.refs_6_ = bf16[256,256]{1,0:T(8,128)(2,1)S(1)} collective-permute-done((bf16[256,256]{1,0:T(8,128)(2,1)S(1)}, bf16[256,256]{1,0:T(8,128)(2,1)S(1)}, u32[]{:S(2)}, u32[]{:S(2)}) %collective-permute-start.26) | collective-permute-done | bytes 131104 | tf_op jit(solution)/shard_map/ppermute | solution.py:470
  147.0 3.0 %collective-permute-done.27.refs_7_ = bf16[256,256]{1,0:T(8,128)(2,1)S(1)} collective-permute-done((bf16[256,256]{1,0:T(8,128)(2,1)S(1)}, bf16[256,256]{1,0:T(8,128)(2,1)S(1)}, u32[]{:S(2)}, u32[]{:S(2)}) %collective-permute-start.27) | collective-permute-done | bytes 131104 | tf_op jit(solution)/shard_map/ppermute | solution.py:470
  150.0 2.2 %copy-done.1 = bf16[4,512,1024]{2,1,0:T(8,128)(2,1)S(1)} copy-done((bf16[4,512,1024]{2,1,0:T(8,128)(2,1)S(1)}, bf16[4,512,1024]{2,1,0:T(8,128)(2,1)}, u32[]{:S(2)}) %copy-start.1) | copy-done | bytes 4194328
  152.2 6.4 %project.1 = bf16[256,2048]{1,0:T(8,128)(2,1)} custom-call(s32[2]{0:T(128)S(1)} %pad_add_fusion.side_ref, bf16[256,256]{1,0:T(8,128)(2,1)S(1)} %get-tuple-element.54.refs_0_, bf16[256,256]{1,0:T(8,128)(2,1)S(1)} %collective-permute-done.15.refs_9_.refs_1_, bf16[256,256]{1,0:T(8,128)(2,1)S(1)} %collective-permute-done.16.refs_10_.refs_2_, ...), custom_call_target="tpu_custom_call" | custom-call | flops 2147483648 | bytes 9437184 | tf_op jit(solution)/shard_map/project/pallas_call | solution.py:363
  (81 shorter events, 3.9 us)
Async XLA Ops:
  6.5 1.6 copy-start
  6.5 127.9 %all-gather.3.cloned.1.call-start = ((), (), s32[]{:S(2)}) async-start(), calls=%async_computation.2 | async-start | bytes 5242880 | tf_op jit(solution)/shard_map/all_gather | solution.py:443
  11.4 17.7 %collective-permute-start = (bf16[2,512,512]{2,1,0:T(8,128)(2,1)}, bf16[2,512,512]{2,1,0:T(8,128)(2,1)S(1)}, u32[]{:S(2)}, u32[]{:S(2)}) collective-permute-start(bf16[2,512,512]{2,1,0:T(8,128)(2,1)} %get-tuple-element.39), channel_id=1, source_target_pairs={{0,4},{4,8},{8,12},{12,16},{16,20},{20,24},{24,28},{1,5},{5,9},{9,... | collective-permute-start | bytes 3145736 | tf_op jit(solution)/shard_map/ppermute | solution.py:448
  13.3 7.5 %collective-permute-start.3 = (bf16[2,64,512]{2,1,0:T(8,128)(2,1)}, bf16[2,64,512]{2,1,0:T(8,128)(2,1)S(1)}, u32[]{:S(2)}, u32[]{:S(2)}) collective-permute-start(bf16[2,64,512]{2,1,0:T(8,128)(2,1)} %get-tuple-element.40.refs_0_), channel_id=1, source_target_pairs={{0,24},{4,28},{8,16},{12,20},{16,8},{20,12},{24,0},{28,4},{1,25},{... | collective-permute-start | bytes 393224 | tf_op jit(solution)/shard_map/ppermute | solution.py:390
  20.8 8.3 %copy-start.16 = (bf16[2,64,512]{2,1,0:T(8,128)(2,1)}, bf16[2,64,512]{2,1,0:T(8,128)(2,1)S(1)}, u32[]{:S(2)}) copy-start(bf16[2,64,512]{2,1,0:T(8,128)(2,1)S(1)} %collective-permute-done.3.refs_3_.refs_1_) | copy-start | bytes 393220
  29.2 1.0 copy-start.14
  30.1 6.2 %copy-start.15 = (bf16[2,64,512]{2,1,0:T(8,128)(2,1)S(1)}, bf16[2,64,512]{2,1,0:T(8,128)(2,1)}, u32[]{:S(2)}) copy-start(bf16[2,64,512]{2,1,0:T(8,128)(2,1)} %get-tuple-element.40.refs_0_) | copy-start | bytes 393220
  30.1 8.2 %copy-start.17 = (bf16[2,64,512]{2,1,0:T(8,128)(2,1)S(1)}, bf16[2,64,512]{2,1,0:T(8,128)(2,1)}, u32[]{:S(2)}) copy-start(bf16[2,64,512]{2,1,0:T(8,128)(2,1)} %copy-done.16) | copy-start | bytes 393220
  30.1 48.7 %all-to-all-start = ((bf16[8,3,2,64,256]{4,3,2,1,0:T(8,128)(2,1)}), bf16[8,3,2,64,256]{4,3,2,1,0:T(8,128)(2,1)}, u32[]{:S(2)}, u32[]{:S(2)}) async-start(bf16[8,3,2,64,256]{4,3,2,1,0:T(8,128)(2,1)} %after.3), calls=%async_computation | async-start | bytes 3145728 | tf_op jit(solution)/shard_map/all_to_all | solution.py:493
  36.3 21.3 %collective-permute-start.1 = (bf16[2,64,512]{2,1,0:T(8,128)(2,1)S(1)}, bf16[2,64,512]{2,1,0:T(8,128)(2,1)S(1)}, u32[]{:S(2)}, u32[]{:S(2)}) collective-permute-start(bf16[2,64,512]{2,1,0:T(8,128)(2,1)S(1)} %copy-done.15), channel_id=1, source_target_pairs={{0,8},{4,12},{8,0},{12,4},{16,24},{20,28},{24,16},{28,20},{1,9},{5... | collective-permute-start | bytes 393224 | tf_op jit(solution)/shard_map/ppermute | solution.py:390
  36.4 22.5 %collective-permute-start.2 = (bf16[2,64,512]{2,1,0:T(8,128)(2,1)S(1)}, bf16[2,64,512]{2,1,0:T(8,128)(2,1)S(1)}, u32[]{:S(2)}, u32[]{:S(2)}) collective-permute-start(bf16[2,64,512]{2,1,0:T(8,128)(2,1)S(1)} %copy-done.15), channel_id=1, source_target_pairs={{0,16},{4,20},{8,24},{12,28},{16,0},{20,4},{24,8},{28,12},{1,17},{... | collective-permute-start | bytes 393224 | tf_op jit(solution)/shard_map/ppermute | solution.py:390
  38.4 20.6 %collective-permute-start.7 = (bf16[2,64,512]{2,1,0:T(8,128)(2,1)S(1)}, bf16[2,64,512]{2,1,0:T(8,128)(2,1)S(1)}, u32[]{:S(2)}, u32[]{:S(2)}) collective-permute-start(bf16[2,64,512]{2,1,0:T(8,128)(2,1)S(1)} %copy-done.17), channel_id=1, source_target_pairs={{0,4},{4,0},{8,12},{12,8},{16,20},{20,16},{24,28},{28,24},{1,5},{5... | collective-permute-start | bytes 393224 | tf_op jit(solution)/shard_map/ppermute | solution.py:390
  39.1 24.8 %collective-permute-start.4 = (bf16[2,64,512]{2,1,0:T(8,128)(2,1)S(1)}, bf16[2,64,512]{2,1,0:T(8,128)(2,1)S(1)}, u32[]{:S(2)}, u32[]{:S(2)}) collective-permute-start(bf16[2,64,512]{2,1,0:T(8,128)(2,1)S(1)} %copy-done.15), channel_id=1, source_target_pairs={{0,4},{4,0},{8,12},{12,8},{16,20},{20,16},{24,28},{28,24},{1,5},{5... | collective-permute-start | bytes 393224 | tf_op jit(solution)/shard_map/ppermute | solution.py:390
  57.7 6.2 %copy-start.19 = (bf16[2,64,512]{2,1,0:T(8,128)(2,1)}, bf16[2,64,512]{2,1,0:T(8,128)(2,1)S(1)}, u32[]{:S(2)}) copy-start(bf16[2,64,512]{2,1,0:T(8,128)(2,1)S(1)} %collective-permute-done.1.refs_1_) | copy-start | bytes 393220
  57.7 6.2 %collective-permute-start.5 = (bf16[2,64,512]{2,1,0:T(8,128)(2,1)S(1)}, bf16[2,64,512]{2,1,0:T(8,128)(2,1)S(1)}, u32[]{:S(2)}, u32[]{:S(2)}) collective-permute-start(bf16[2,64,512]{2,1,0:T(8,128)(2,1)S(1)} %collective-permute-done.1.refs_1_), channel_id=1, source_target_pairs={{0,4},{4,0},{8,12},{12,8},{16,20},{20,16},{24,28},{28,24},{1,5},{5... | collective-permute-start | bytes 393224 | tf_op jit(solution)/shard_map/ppermute | solution.py:390
  58.9 5.0 %copy-start.20 = (bf16[2,64,512]{2,1,0:T(8,128)(2,1)}, bf16[2,64,512]{2,1,0:T(8,128)(2,1)S(1)}, u32[]{:S(2)}) copy-start(bf16[2,64,512]{2,1,0:T(8,128)(2,1)S(1)} %collective-permute-done.2.refs_2_) | copy-start | bytes 393220
  58.9 4.9 %collective-permute-start.6 = (bf16[2,64,512]{2,1,0:T(8,128)(2,1)S(1)}, bf16[2,64,512]{2,1,0:T(8,128)(2,1)S(1)}, u32[]{:S(2)}, u32[]{:S(2)}) collective-permute-start(bf16[2,64,512]{2,1,0:T(8,128)(2,1)S(1)} %collective-permute-done.2.refs_2_), channel_id=1, source_target_pairs={{0,4},{4,0},{8,12},{12,8},{16,20},{20,16},{24,28},{28,24},{1,5},{5... | collective-permute-start | bytes 393224 | tf_op jit(solution)/shard_map/ppermute | solution.py:390
  63.8 0.7 copy-start.23
  78.9 5.4 %copy-start.8 = (f32[8,128]{1,0:T(8,128)S(1)}, f32[8,128]{1,0:T(8,128)}, u32[]{:S(2)}) copy-start(f32[8,128]{1,0:T(8,128)} %get-tuple-element.43.refs_0_.refs_1_) | copy-start | bytes 12292
  78.9 25.1 %all-to-all-start.1 = ((bf16[8,3,2,64,256]{4,3,2,1,0:T(8,128)(2,1)}), bf16[8,3,2,64,256]{4,3,2,1,0:T(8,128)(2,1)}, u32[]{:S(2)}, u32[]{:S(2)}) async-start(bf16[8,3,2,64,256]{4,3,2,1,0:T(8,128)(2,1)} %after.4), calls=%async_computation.1 | async-start | bytes 3145728 | tf_op jit(solution)/shard_map/all_to_all | solution.py:493
  89.0 25.4 %copy-start.3 = (f32[1024,256]{1,0:T(8,128)S(1)}, f32[1024,256]{1,0:T(8,128)}, u32[]{:S(2)}) copy-start(f32[1024,256]{1,0:T(8,128)} %get-tuple-element.41.home_ref) | copy-start | bytes 3145732
  89.0 17.9 %collective-permute-start.10 = (bf16[2,64,256]{2,1,0:T(8,128)(2,1)}, bf16[2,64,256]{2,1,0:T(8,128)(2,1)S(1)}, u32[]{:S(2)}, u32[]{:S(2)}) collective-permute-start(bf16[2,64,256]{2,1,0:T(8,128)(2,1)} %get-tuple-element.47), channel_id=1, source_target_pairs={{0,12},{4,8},{8,4},{12,0},{16,28},{20,24},{24,20},{28,16},{1,13},{... | collective-permute-start | bytes 196616 | tf_op jit(solution)/shard_map/ppermute | solution.py:470
  89.2 17.8 %collective-permute-start.11 = (bf16[2,64,256]{2,1,0:T(8,128)(2,1)}, bf16[2,64,256]{2,1,0:T(8,128)(2,1)S(1)}, u32[]{:S(2)}, u32[]{:S(2)}) collective-permute-start(bf16[2,64,256]{2,1,0:T(8,128)(2,1)} %get-tuple-element.48), channel_id=1, source_target_pairs={{0,16},{4,20},{8,24},{12,28},{16,0},{20,4},{24,8},{28,12},{1,17},{... | collective-permute-start | bytes 196616 | tf_op jit(solution)/shard_map/ppermute | solution.py:470
  90.8 18.6 %collective-permute-start.12 = (bf16[2,64,256]{2,1,0:T(8,128)(2,1)}, bf16[2,64,256]{2,1,0:T(8,128)(2,1)S(1)}, u32[]{:S(2)}, u32[]{:S(2)}) collective-permute-start(bf16[2,64,256]{2,1,0:T(8,128)(2,1)} %get-tuple-element.49), channel_id=1, source_target_pairs={{0,20},{4,16},{8,28},{12,24},{16,4},{20,0},{24,12},{28,8},{1,21},{... | collective-permute-start | bytes 196616 | tf_op jit(solution)/shard_map/ppermute | solution.py:470
  90.8 18.7 %collective-permute-start.13 = (bf16[2,64,256]{2,1,0:T(8,128)(2,1)}, bf16[2,64,256]{2,1,0:T(8,128)(2,1)S(1)}, u32[]{:S(2)}, u32[]{:S(2)}) collective-permute-start(bf16[2,64,256]{2,1,0:T(8,128)(2,1)} %get-tuple-element.50), channel_id=1, source_target_pairs={{0,24},{4,28},{8,16},{12,20},{16,8},{20,12},{24,0},{28,4},{1,25},{... | collective-permute-start | bytes 196616 | tf_op jit(solution)/shard_map/ppermute | solution.py:470
  93.4 17.1 %collective-permute-start.14 = (bf16[2,64,256]{2,1,0:T(8,128)(2,1)}, bf16[2,64,256]{2,1,0:T(8,128)(2,1)S(1)}, u32[]{:S(2)}, u32[]{:S(2)}) collective-permute-start(bf16[2,64,256]{2,1,0:T(8,128)(2,1)} %get-tuple-element.51), channel_id=1, source_target_pairs={{0,28},{4,24},{8,20},{12,16},{16,12},{20,8},{24,4},{28,0},{1,29},{... | collective-permute-start | bytes 196616 | tf_op jit(solution)/shard_map/ppermute | solution.py:470
  104.0 2.9 %copy-start.13 = (bf16[2,64,256]{2,1,0:T(8,128)(2,1)S(1)}, bf16[2,64,256]{2,1,0:T(8,128)(2,1)}, u32[]{:S(2)}) copy-start(bf16[2,64,256]{2,1,0:T(8,128)(2,1)} %copy-done.12) | copy-start | bytes 196612
  104.0 3.0 %copy-start.11 = (bf16[2,64,256]{2,1,0:T(8,128)(2,1)S(1)}, bf16[2,64,256]{2,1,0:T(8,128)(2,1)}, u32[]{:S(2)}) copy-start(bf16[2,64,256]{2,1,0:T(8,128)(2,1)} %copy-done.10) | copy-start | bytes 196612
  104.0 28.4 %copy-start.2 = (f32[1024,256]{1,0:T(8,128)S(1)}, f32[1024,256]{1,0:T(8,128)}, u32[]{:S(2)}) copy-start(f32[1024,256]{1,0:T(8,128)} %get-tuple-element.58.home_ref) | copy-start | bytes 3145732
  106.9 5.7 %collective-permute-start.8 = (bf16[2,64,256]{2,1,0:T(8,128)(2,1)S(1)}, bf16[2,64,256]{2,1,0:T(8,128)(2,1)S(1)}, u32[]{:S(2)}, u32[]{:S(2)}) collective-permute-start(bf16[2,64,256]{2,1,0:T(8,128)(2,1)S(1)} %copy-done.13), channel_id=1, source_target_pairs={{0,4},{4,0},{8,12},{12,8},{16,20},{20,16},{24,28},{28,24},{1,5},{5... | collective-permute-start | bytes 196616 | tf_op jit(solution)/shard_map/ppermute | solution.py:470
  107.0 5.9 %collective-permute-start.9 = (bf16[2,64,256]{2,1,0:T(8,128)(2,1)S(1)}, bf16[2,64,256]{2,1,0:T(8,128)(2,1)S(1)}, u32[]{:S(2)}, u32[]{:S(2)}) collective-permute-start(bf16[2,64,256]{2,1,0:T(8,128)(2,1)S(1)} %copy-done.11), channel_id=1, source_target_pairs={{0,8},{4,12},{8,0},{12,4},{16,24},{20,28},{24,16},{28,20},{1,9},{5... | collective-permute-start | bytes 196616 | tf_op jit(solution)/shard_map/ppermute | solution.py:470
  109.4 7.5 %collective-permute-start.18 = (bf16[2,64,256]{2,1,0:T(8,128)(2,1)S(1)}, bf16[2,64,256]{2,1,0:T(8,128)(2,1)S(1)}, u32[]{:S(2)}, u32[]{:S(2)}) collective-permute-start(bf16[2,64,256]{2,1,0:T(8,128)(2,1)S(1)} %get-tuple-element.60), channel_id=1, source_target_pairs={{0,4},{4,0},{8,12},{12,8},{16,20},{20,16},{24,28},{28,24},{1,5},{5... | collective-permute-start | bytes 196616 | tf_op jit(solution)/shard_map/ppermute | solution.py:470
  110.1 7.4 %collective-permute-start.19 = (bf16[2,64,256]{2,1,0:T(8,128)(2,1)S(1)}, bf16[2,64,256]{2,1,0:T(8,128)(2,1)S(1)}, u32[]{:S(2)}, u32[]{:S(2)}) collective-permute-start(bf16[2,64,256]{2,1,0:T(8,128)(2,1)S(1)} %get-tuple-element.61), channel_id=1, source_target_pairs={{0,8},{4,12},{8,0},{12,4},{16,24},{20,28},{24,16},{28,20},{1,9},{5... | collective-permute-start | bytes 196616 | tf_op jit(solution)/shard_map/ppermute | solution.py:470
  111.1 8.7 %collective-permute-start.20 = (bf16[2,64,256]{2,1,0:T(8,128)(2,1)S(1)}, bf16[2,64,256]{2,1,0:T(8,128)(2,1)S(1)}, u32[]{:S(2)}, u32[]{:S(2)}) collective-permute-start(bf16[2,64,256]{2,1,0:T(8,128)(2,1)S(1)} %get-tuple-element.62), channel_id=1, source_target_pairs={{0,12},{4,8},{8,4},{12,0},{16,28},{20,24},{24,20},{28,16},{1,13},{... | collective-permute-start | bytes 196616 | tf_op jit(solution)/shard_map/ppermute | solution.py:470
  112.6 7.9 %collective-permute-start.21 = (bf16[2,64,256]{2,1,0:T(8,128)(2,1)S(1)}, bf16[2,64,256]{2,1,0:T(8,128)(2,1)S(1)}, u32[]{:S(2)}, u32[]{:S(2)}) collective-permute-start(bf16[2,64,256]{2,1,0:T(8,128)(2,1)S(1)} %get-tuple-element.63), channel_id=1, source_target_pairs={{0,16},{4,20},{8,24},{12,28},{16,0},{20,4},{24,8},{28,12},{1,17},{... | collective-permute-start | bytes 196616 | tf_op jit(solution)/shard_map/ppermute | solution.py:470
  112.9 7.8 %collective-permute-start.22 = (bf16[2,64,256]{2,1,0:T(8,128)(2,1)S(1)}, bf16[2,64,256]{2,1,0:T(8,128)(2,1)S(1)}, u32[]{:S(2)}, u32[]{:S(2)}) collective-permute-start(bf16[2,64,256]{2,1,0:T(8,128)(2,1)S(1)} %get-tuple-element.64), channel_id=1, source_target_pairs={{0,20},{4,16},{8,28},{12,24},{16,4},{20,0},{24,12},{28,8},{1,21},{... | collective-permute-start | bytes 196616 | tf_op jit(solution)/shard_map/ppermute | solution.py:470
  114.4 0.8 copy-start.5
  115.2 0.8 copy-start.7
  116.9 9.1 %collective-permute-start.15 = (bf16[256,256]{1,0:T(8,128)(2,1)S(1)}, bf16[256,256]{1,0:T(8,128)(2,1)S(1)}, u32[]{:S(2)}, u32[]{:S(2)}) collective-permute-start(bf16[256,256]{1,0:T(8,128)(2,1)S(1)} %get-tuple-element.55), channel_id=1, source_target_pairs={{0,1},{1,0},{2,3},{3,2},{4,5},{5,4},{6,7},{7,6},{8,9},{9,8},{10,11... | collective-permute-start | bytes 393224 | tf_op jit(solution)/shard_map/ppermute | solution.py:470
  117.5 11.7 %collective-permute-start.16 = (bf16[256,256]{1,0:T(8,128)(2,1)S(1)}, bf16[256,256]{1,0:T(8,128)(2,1)S(1)}, u32[]{:S(2)}, u32[]{:S(2)}) collective-permute-start(bf16[256,256]{1,0:T(8,128)(2,1)S(1)} %get-tuple-element.56), channel_id=1, source_target_pairs={{0,2},{1,3},{2,0},{3,1},{4,6},{5,7},{6,4},{7,5},{8,10},{9,11},{10,... | collective-permute-start | bytes 393224 | tf_op jit(solution)/shard_map/ppermute | solution.py:470
  119.7 12.7 %collective-permute-start.17 = (bf16[256,256]{1,0:T(8,128)(2,1)S(1)}, bf16[256,256]{1,0:T(8,128)(2,1)S(1)}, u32[]{:S(2)}, u32[]{:S(2)}) collective-permute-start(bf16[256,256]{1,0:T(8,128)(2,1)S(1)} %get-tuple-element.57), channel_id=1, source_target_pairs={{0,3},{1,2},{2,1},{3,0},{4,7},{5,6},{6,5},{7,4},{8,11},{9,10},{10,... | collective-permute-start | bytes 393224 | tf_op jit(solution)/shard_map/ppermute | solution.py:470
  120.5 5.5 %collective-permute-start.23 = (bf16[2,64,256]{2,1,0:T(8,128)(2,1)S(1)}, bf16[2,64,256]{2,1,0:T(8,128)(2,1)S(1)}, u32[]{:S(2)}, u32[]{:S(2)}) collective-permute-start(bf16[2,64,256]{2,1,0:T(8,128)(2,1)S(1)} %get-tuple-element.65), channel_id=1, source_target_pairs={{0,24},{4,28},{8,16},{12,20},{16,8},{20,12},{24,0},{28,4},{1,25},{... | collective-permute-start | bytes 196616 | tf_op jit(solution)/shard_map/ppermute | solution.py:470
  120.7 5.3 %collective-permute-start.24 = (bf16[2,64,256]{2,1,0:T(8,128)(2,1)S(1)}, bf16[2,64,256]{2,1,0:T(8,128)(2,1)S(1)}, u32[]{:S(2)}, u32[]{:S(2)}) collective-permute-start(bf16[2,64,256]{2,1,0:T(8,128)(2,1)S(1)} %get-tuple-element.66), channel_id=1, source_target_pairs={{0,28},{4,24},{8,20},{12,16},{16,12},{20,8},{24,4},{28,0},{1,29},{... | collective-permute-start | bytes 196616 | tf_op jit(solution)/shard_map/ppermute | solution.py:470
  134.4 15.6 %collective-permute-start.28 = (bf16[4,512,1024]{2,1,0:T(8,128)(2,1)}, bf16[4,512,1024]{2,1,0:T(8,128)(2,1)S(1)}, u32[]{:S(2)}, u32[]{:S(2)}) collective-permute-start(bf16[4,512,1024]{2,1,0:T(8,128)(2,1)} %after.5.refs_8_), channel_id=1, source_target_pairs={{0,4},{4,0},{8,12},{12,8},{16,20},{20,16},{24,28},{28,24},{1,5},{5... | collective-permute-start | bytes 12582920 | tf_op jit(solution)/shard_map/ppermute | solution.py:502
  134.4 6.5 %collective-permute-start.25 = (bf16[256,256]{1,0:T(8,128)(2,1)}, bf16[256,256]{1,0:T(8,128)(2,1)S(1)}, u32[]{:S(2)}, u32[]{:S(2)}) collective-permute-start(bf16[256,256]{1,0:T(8,128)(2,1)} %get-tuple-element.69), channel_id=1, source_target_pairs={{0,1},{1,0},{2,3},{3,2},{4,5},{5,4},{6,7},{7,6},{8,9},{9,8},{10,11... | collective-permute-start | bytes 393224 | tf_op jit(solution)/shard_map/ppermute | solution.py:470
  134.5 12.5 %collective-permute-start.26 = (bf16[256,256]{1,0:T(8,128)(2,1)S(1)}, bf16[256,256]{1,0:T(8,128)(2,1)S(1)}, u32[]{:S(2)}, u32[]{:S(2)}) collective-permute-start(bf16[256,256]{1,0:T(8,128)(2,1)S(1)} %get-tuple-element.70), channel_id=1, source_target_pairs={{0,2},{1,3},{2,0},{3,1},{4,6},{5,7},{6,4},{7,5},{8,10},{9,11},{10,... | collective-permute-start | bytes 393224 | tf_op jit(solution)/shard_map/ppermute | solution.py:470
  137.5 12.6 %collective-permute-start.27 = (bf16[256,256]{1,0:T(8,128)(2,1)S(1)}, bf16[256,256]{1,0:T(8,128)(2,1)S(1)}, u32[]{:S(2)}, u32[]{:S(2)}) collective-permute-start(bf16[256,256]{1,0:T(8,128)(2,1)S(1)} %get-tuple-element.71), channel_id=1, source_target_pairs={{0,3},{1,2},{2,1},{3,0},{4,7},{5,6},{6,5},{7,4},{8,11},{9,10},{10,... | collective-permute-start | bytes 393224 | tf_op jit(solution)/shard_map/ppermute | solution.py:470
  150.0 2.2 %copy-start.1 = (bf16[4,512,1024]{2,1,0:T(8,128)(2,1)S(1)}, bf16[4,512,1024]{2,1,0:T(8,128)(2,1)}, u32[]{:S(2)}) copy-start(bf16[4,512,1024]{2,1,0:T(8,128)(2,1)} %after.5.refs_8_) | copy-start | bytes 12582916
  (8 other events, 5.1 us)
Sparse Core Ops, SparseCore 0:
  9.4 79.4 all-gather.2

commit v5 on v4

--- a/solution.py
+++ b/solution.py
@@ -100,7 +100,8 @@
     return total[:, :HEAD_SIZE] / total[:, HEAD_SIZE:]
 
 
-def edge_kernel(k_ref, v_ref, k_ends_ref, v_ends_ref, rim_ref, sum_ref):
+def edge_kernel(k_ref, v_ref, k_ends_ref, v_ends_ref, *refs):
+    rim_ref, sum_ref = refs[-2:]
     rim_ref[0] = k_ref[...]
     rim_ref[1] = v_ref[...]
 
@@ -111,7 +112,7 @@
             sum_ref[number] = rows.reshape(sum_ref.shape[1:]).astype(BF16)
 
 
-def edges(keys, values):
+def edges(keys, values, waits):
     tokens_dev, width = keys.shape
     blocks = tokens_dev // BLOCK
     first = (tokens_dev - WINDOW) // TILE
@@ -121,7 +122,7 @@
     return pl.pallas_call(
         edge_kernel,
         grid=(WINDOW // TILE,),
-        in_specs=[source] * 2 + [ends] * 2,
+        in_specs=[source] * 2 + [ends] * 2 + moments(waits),
         out_specs=[
             pl.BlockSpec((2, TILE, width), lambda i: (0, i, 0)),
             pl.BlockSpec(shape, lambda i: (0, 0, 0)),
@@ -138,6 +139,7 @@
         values,
         keys.reshape(blocks, BLOCK, width),
         values.reshape(blocks, BLOCK, width),
+        *waits,
     )
 
 
@@ -442,18 +444,19 @@
     weight_half = lax.dynamic_slice_in_dim(out_weight, side * half, half, axis=1)
     mine = lax.all_gather(weight_half, "head", axis=0)
 
-    rim, picked = edges(keys, values)
+    sends = []
+    if ctx <= STRIDE:
+        sends.append(prepare(queries, keys, values, ctx, 0, chunks, ()))
+    rim, picked = edges(keys, values, sends)
     between, within, order = gather_ctx(picked)
     summary = between + within
-    before = lax.ppermute(rim, "ctx", [(i, i + 1) for i in range(ctx - 1)])
     if ctx > STRIDE:
         stride_out = stride_general(queries, keys, values)
-    else:
-        sends = [
-            prepare(queries, keys, values, ctx, chunk, chunks, within[-1:] if chunk else (picked,))
-            for chunk in range(chunks)
-        ]
-        sends[0] = after(sends[0], (between[-1], before))
+    for chunk in range(len(sends), chunks * len(sends)):
+        sends.append(prepare(queries, keys, values, ctx, chunk, chunks, (picked,)))
+    rim = after(rim, (*between[1:], *sends[1:]))
+    before = lax.ppermute(rim, "ctx", [(i, i + 1) for i in range(ctx - 1)])
+    sends[1:] = [after(send, between[1:]) for send in sends[1:]]
 
     def home(chunk, waits):
         return home_sections(
@@ -484,20 +487,18 @@
         seats = jnp.stack([seat, place.astype(jnp.int32)])
         homes, backs = [], []
         for chunk in range(chunks):
-            sections, mark = home(chunk, waits)
-            homes.append(sections)
-            waits = (mark,)
-        if chunks > 1:
-            sends[1] = after(sends[1], waits)
-        for chunk in range(chunks):
             received = lax.all_to_all(sends[chunk], "ctx", split_axis=0, concat_axis=0, tiled=True)
             *slabs, mark = stride_attend(place_word, received, waits)
             backs.append(exchange(slabs, "ctx"))
             waits = (mark,)
+            for ready in range(chunks) if chunk == 0 else ():
+                sections, mark = home(ready, waits)
+                homes.append(sections)
+                waits = (mark,)
         for chunk in range(chunks):
             *slabs, mark = combine(seats, homes[chunk], backs[chunk], groups, waits)
             moved.append(exchange(slabs, "head"))
-            waits = (mark, *moved[-1][1:])
+            waits = (mark, *moved[-1][1:3])
     held = after(mine, (mark,))
     other = lax.ppermute(held, "ctx", sibling)
     sides = jnp.stack([side.astype(jnp.int32), seat])

time: 166 us -> 144 us (0.87)
  waiting for transfers between devices: 62.7 us -> 38.2 us
    all_to_all x2, waiting for transfers between devices: 10.4 us -> 0.01 us  [body(): lax.all_to_all(sends[chunk], 'ctx', split_axis=0, concat_axis=0, tiled=True)]
    ppermute x7, waiting for transfers between devices: 21.5 us -> 15.2 us  [swapped(): return lax.ppermute(piece, 'ctx', [(i, i ^ distance) for i in range(count)])]
    ppermute x1, waiting for transfers between devices: 8.31 us -> 3.98 us  [body(): before = lax.ppermute(rim, 'ctx', [(i, i + 1) for i in range(ctx - 1)])]
    ppermute x20, waiting for transfers between devices: 22.4 us -> 19 us  [exchange(): moved.append(lax.ppermute(slabs[slot], axis, pairs))]
    unnamed x48 -> x56, local copies, waits for them, and re-layouts: 10.9 us -> 11.5 us
  transfers between devices with their start and end apart: 32 -> 32, of which waited for: 12 -> 11; matrix products, arithmetic and copies ran while one was open for 0% -> 0% of each run, Pallas kernels for 20% -> 23%
where the time goes in v5:
time: 144 us; the launch traced here: 142 us
  Pallas kernels  39.5 us (27%)
  waiting for transfers between devices  38.2 us (27%)
  starting transfers between devices  38.1 us (26%)
  between operations  13.6 us (9%)
  local copies, waits for them, and re-layouts  12.6 us (9%)
    ppermute x20, starting transfers between devices, exchange(): moved.append(lax.ppermute(slabs[slot], axis, pairs))  20.5 us
    ppermute x20, waiting for transfers between devices, exchange(): moved.append(lax.ppermute(slabs[slot], axis, pairs))  19 us
    ppermute x7, waiting for transfers between devices, swapped(): return lax.ppermute(piece, 'ctx', [(i, i ^ distance) for i in range(count)])  15.2 us
    pallas_call x2, Pallas kernels, home_sections(): pl.pallas_call(functools.partial(home_kernel, order=order), grid=(heads,)...  14.3 us
    unnamed x56, local copies, waits for them, and re-layouts  11.5 us
    all_to_all x2, starting transfers between devices, body(): lax.all_to_all(sends[chunk], 'ctx', split_axis=0, concat_axis=0, tiled=True)  11.1 us
    pallas_call x2, Pallas kernels, prepare(): pl.pallas_call(prep_kernel, grid=(tokens_dev // TILE,), in_specs=[pl.Bloc...  8.42 us
    pallas_call x1, Pallas kernels, project(): pl.pallas_call(functools.partial(project_kernel, slots=slots, chunks=chun...  6.4 us
  transfers between devices with their start and end apart: 32, of which 11 were waited for; matrix products, arithmetic and copies ran while one was open for 0% of the time, Pallas kernels for 23%

profile of v5, /device:TPU:10, one launch (start us, length us, event | category | flops | bytes accessed | tf_op | source)
XLA Modules:
  0.0 142.1 jit_solution(3609917722162127359)
XLA Ops:
  6.5 1.6 %copy-done = bf16[512,2048]{1,0:T(8,128)(2,1)S(1)} copy-done((bf16[512,2048]{1,0:T(8,128)(2,1)S(1)}, bf16[512,2048]{1,0:T(8,128)(2,1)}, u32[]{:S(2)}) %copy-start) | copy-done | bytes 2097176
  8.1 1.1 constant_dynamic-slice_fusion
  9.2 4.2 %prepare.2.refs_0_ = bf16[8,3,2,64,256]{4,3,2,1,0:T(8,128)(2,1)} custom-call(bf16[1024,512]{1,0:T(8,128)(2,1)} %q_ref.7, bf16[1024,512]{1,0:T(8,128)(2,1)} %k_ref.9, bf16[1024,512]{1,0:T(8,128)(2,1)} %v_ref.9), custom_call_target="tpu_custom_call" | custom-call | flops 402653184 | bytes 3145728 | tf_op jit(solution)/shard_map/prepare/pallas_call | solution.py:159
  13.5 4.7 %all-to-all-start = ((bf16[8,3,2,64,256]{4,3,2,1,0:T(8,128)(2,1)}), bf16[8,3,2,64,256]{4,3,2,1,0:T(8,128)(2,1)}, u32[]{:S(2)}, u32[]{:S(2)}) async-start(bf16[8,3,2,64,256]{4,3,2,1,0:T(8,128)(2,1)} %prepare.2.refs_0_), calls=%async_computation | async-start | bytes 3145728 | tf_op jit(solution)/shard_map/all_to_all | solution.py:490
  18.2 2.3 %edges.1 = (bf16[2,512,512]{2,1,0:T(8,128)(2,1)}, bf16[2,64,512]{2,1,0:T(8,128)(2,1)}) custom-call(bf16[1024,512]{1,0:T(8,128)(2,1)} %k_ref.9, bf16[1024,512]{1,0:T(8,128)(2,1)} %v_ref.9, bf16[8,128,512]{2,1,0:T(8,128)(2,1)} %bitcast.7, bf16[8,128,512]{2,1,0:T(8,128)(2,1)} %bitcast.8, bf16[8,3,2,64,256]{4,3,2,1,0:T(8,128)(2,1)} %prepare.2.refs_0_), custom_call_target="tpu_custom_call" | custom-call | bytes 2097152 | tf_op jit(solution)/shard_map/edges/pallas_call | solution.py:122
  20.6 1.9 %collective-permute-start.1 = (bf16[2,64,512]{2,1,0:T(8,128)(2,1)}, bf16[2,64,512]{2,1,0:T(8,128)(2,1)S(1)}, u32[]{:S(2)}, u32[]{:S(2)}) collective-permute-start(bf16[2,64,512]{2,1,0:T(8,128)(2,1)} %get-tuple-element.40.refs_0_), channel_id=1, source_target_pairs={{0,16},{4,20},{8,24},{12,28},{16,0},{20,4},{24,8},{28,12},{1,17},{... | collective-permute-start | bytes 393224 | tf_op jit(solution)/shard_map/ppermute | solution.py:392
  22.5 1.4 %collective-permute-start.2 = (bf16[2,64,512]{2,1,0:T(8,128)(2,1)}, bf16[2,64,512]{2,1,0:T(8,128)(2,1)S(1)}, u32[]{:S(2)}, u32[]{:S(2)}) collective-permute-start(bf16[2,64,512]{2,1,0:T(8,128)(2,1)} %get-tuple-element.40.refs_0_), channel_id=1, source_target_pairs={{0,24},{4,28},{8,16},{12,20},{16,8},{20,12},{24,0},{28,4},{1,25},{... | collective-permute-start | bytes 393224 | tf_op jit(solution)/shard_map/ppermute | solution.py:392
  24.0 4.2 %prepare.3.refs_4_.refs_0_ = bf16[8,3,2,64,256]{4,3,2,1,0:T(8,128)(2,1)} custom-call(bf16[1024,512]{1,0:T(8,128)(2,1)} %q_ref.7, bf16[1024,512]{1,0:T(8,128)(2,1)} %k_ref.9, bf16[1024,512]{1,0:T(8,128)(2,1)} %v_ref.9, bf16[2,64,512]{2,1,0:T(8,128)(2,1)} %get-tuple-element.40.refs_0_), custom_call_target="tpu_custom_call" | custom-call | flops 402653184 | bytes 3145728 | tf_op jit(solution)/shard_map/prepare/pallas_call | solution.py:159
  28.2 11.5 %collective-permute-done.refs_1_ = bf16[2,64,512]{2,1,0:T(8,128)(2,1)S(1)} collective-permute-done((bf16[2,64,512]{2,1,0:T(8,128)(2,1)}, bf16[2,64,512]{2,1,0:T(8,128)(2,1)S(1)}, u32[]{:S(2)}, u32[]{:S(2)}) %collective-permute-start) | collective-permute-done | bytes 131104 | tf_op jit(solution)/shard_map/ppermute | solution.py:392
  39.7 1.2 collective-permute-done.1.refs_2_
  40.9 2.5 %collective-permute-done.2.refs_3_ = bf16[2,64,512]{2,1,0:T(8,128)(2,1)S(1)} collective-permute-done((bf16[2,64,512]{2,1,0:T(8,128)(2,1)}, bf16[2,64,512]{2,1,0:T(8,128)(2,1)S(1)}, u32[]{:S(2)}, u32[]{:S(2)}) %collective-permute-start.2) | collective-permute-done | bytes 131104 | tf_op jit(solution)/shard_map/ppermute | solution.py:392
  43.4 0.6 copy-done.21
  44.0 1.9 %collective-permute-start.3 = (bf16[2,512,512]{2,1,0:T(8,128)(2,1)}, bf16[2,512,512]{2,1,0:T(8,128)(2,1)}, u32[]{:S(2)}, u32[]{:S(2)}) collective-permute-start(bf16[2,512,512]{2,1,0:T(8,128)(2,1)} %after.3), channel_id=1, source_target_pairs={{0,4},{4,8},{8,12},{12,16},{16,20},{20,24},{24,28},{1,5},{5,9},{9,... | collective-permute-start | bytes 3145736 | tf_op jit(solution)/shard_map/ppermute | solution.py:458
  46.0 6.4 %all-to-all-start.1 = ((bf16[8,3,2,64,256]{4,3,2,1,0:T(8,128)(2,1)}), bf16[8,3,2,64,256]{4,3,2,1,0:T(8,128)(2,1)}, u32[]{:S(2)}, u32[]{:S(2)}) async-start(bf16[8,3,2,64,256]{4,3,2,1,0:T(8,128)(2,1)} %after.4), calls=%async_computation.1 | async-start | bytes 3145728 | tf_op jit(solution)/shard_map/all_to_all | solution.py:490
  53.4 3.5 %stride.2 = (bf16[2,64,256]{2,1,0:T(8,128)(2,1)S(1)}, bf16[2,64,256]{2,1,0:T(8,128)(2,1)S(1)}, bf16[2,64,256]{2,1,0:T(8,128)(2,1)S(1)}, bf16[2,64,256]{2,1,0:T(8...) custom-call(s32[1]{0:T(128)} %bitcast.2.place_ref, ...), custom_call_target="tpu_custom_call" | custom-call | flops 805306368 | bytes 2097152 | tf_op jit(solution)/shard_map/stride/pallas_call | solution.py:280
  56.9 0.6 copy-done.11
  57.5 0.6 copy-done.13
  58.3 1.7 %collective-permute-start.11 = (bf16[2,64,256]{2,1,0:T(8,128)(2,1)}, bf16[2,64,256]{2,1,0:T(8,128)(2,1)S(1)}, u32[]{:S(2)}, u32[]{:S(2)}) collective-permute-start(bf16[2,64,256]{2,1,0:T(8,128)(2,1)} %get-tuple-element.47), channel_id=1, source_target_pairs={{0,16},{4,20},{8,24},{12,28},{16,0},{20,4},{24,8},{28,12},{1,17},{... | collective-permute-start | bytes 196616 | tf_op jit(solution)/shard_map/ppermute | solution.py:473
  60.0 2.6 %collective-permute-start.13 = (bf16[2,64,256]{2,1,0:T(8,128)(2,1)}, bf16[2,64,256]{2,1,0:T(8,128)(2,1)S(1)}, u32[]{:S(2)}, u32[]{:S(2)}) collective-permute-start(bf16[2,64,256]{2,1,0:T(8,128)(2,1)} %get-tuple-element.49), channel_id=1, source_target_pairs={{0,24},{4,28},{8,16},{12,20},{16,8},{20,12},{24,0},{28,4},{1,25},{... | collective-permute-start | bytes 196616 | tf_op jit(solution)/shard_map/ppermute | solution.py:473
  62.6 4.0 %collective-permute-done.3.rim_ref = bf16[2,512,512]{2,1,0:T(8,128)(2,1)} collective-permute-done((bf16[2,512,512]{2,1,0:T(8,128)(2,1)}, bf16[2,512,512]{2,1,0:T(8,128)(2,1)}, u32[]{:S(2)}, u32[]{:S(2)}) %collective-permute-start.3) | collective-permute-done | bytes 1048608 | tf_op jit(solution)/shard_map/ppermute | solution.py:458
  66.6 7.1 %home.2 = (f32[1024,256]{1,0:T(8,128)}, f32[8,128]{1,0:T(8,128)}) custom-call(s32[1]{0:T(128)} %bitcast.2.place_ref, bf16[1024,512]{1,0:T(8,128)(2,1)} %q_ref.7, bf16[1024,512]{1,0:T(8,128)(2,1)} %k_ref.9, bf16[1024,512]{1,0:T(8,128)(2,1)} %v_ref.9, bf16[2,512,512]{2,1,0:T(8,128)(2,1)} %collective-permute-done.3.rim_ref, ...), custom_call_target="tpu_custom_call" | custom-call | flops 2684354560 | bytes 7340032 | tf_op jit(solution)/shard_map/home/pallas_call | solution.py:226
  73.7 7.2 %home.3 = (f32[1024,256]{1,0:T(8,128)}, f32[8,128]{1,0:T(8,128)}) custom-call(s32[1]{0:T(128)} %bitcast.2.place_ref, bf16[1024,512]{1,0:T(8,128)(2,1)} %q_ref.7, bf16[1024,512]{1,0:T(8,128)(2,1)} %k_ref.9, bf16[1024,512]{1,0:T(8,128)(2,1)} %v_ref.9, bf16[2,512,512]{2,1,0:T(8,128)(2,1)} %collective-permute-done.3.rim_ref, ...), custom_call_target="tpu_custom_call" | custom-call | flops 2684354560 | bytes 7340032 | tf_op jit(solution)/shard_map/home/pallas_call | solution.py:226
  80.9 0.8 copy-done.15
  81.7 2.9 %stride.3 = (bf16[2,64,256]{2,1,0:T(8,128)(2,1)S(1)}, bf16[2,64,256]{2,1,0:T(8,128)(2,1)S(1)}, bf16[2,64,256]{2,1,0:T(8,128)(2,1)S(1)}, bf16[2,64,256]{2,1,0:T(8...) custom-call(s32[1]{0:T(128)} %bitcast.2.place_ref, ...), custom_call_target="tpu_custom_call" | custom-call | flops 805306368 | bytes 2097152 | tf_op jit(solution)/shard_map/stride/pallas_call | solution.py:280
  84.6 2.0 %collective-permute-start.8 = (bf16[2,64,256]{2,1,0:T(8,128)(2,1)S(1)}, bf16[2,64,256]{2,1,0:T(8,128)(2,1)S(1)}, u32[]{:S(2)}, u32[]{:S(2)}) collective-permute-start(bf16[2,64,256]{2,1,0:T(8,128)(2,1)S(1)} %copy-done.14), channel_id=1, source_target_pairs={{0,4},{4,0},{8,12},{12,8},{16,20},{20,16},{24,28},{28,24},{1,5},{5... | collective-permute-start | bytes 196616 | tf_op jit(solution)/shard_map/ppermute | solution.py:473
  87.5 1.9 %collective-permute-start.19 = (bf16[2,64,256]{2,1,0:T(8,128)(2,1)S(1)}, bf16[2,64,256]{2,1,0:T(8,128)(2,1)S(1)}, u32[]{:S(2)}, u32[]{:S(2)}) collective-permute-start(bf16[2,64,256]{2,1,0:T(8,128)(2,1)S(1)} %get-tuple-element.61), channel_id=1, source_target_pairs={{0,8},{4,12},{8,0},{12,4},{16,24},{20,28},{24,16},{28,20},{1,9},{5... | collective-permute-start | bytes 196616 | tf_op jit(solution)/shard_map/ppermute | solution.py:473
  90.1 1.3 collective-permute-start.21
  91.5 0.8 copy-done.5
  92.3 0.8 copy-done.7
  93.1 0.8 combine.2
  94.0 0.6 copy-done.9
  94.7 2.9 %collective-permute-start.16 = (bf16[256,256]{1,0:T(8,128)(2,1)S(1)}, bf16[256,256]{1,0:T(8,128)(2,1)S(1)}, u32[]{:S(2)}, u32[]{:S(2)}) collective-permute-start(bf16[256,256]{1,0:T(8,128)(2,1)S(1)} %get-tuple-element.56), channel_id=1, source_target_pairs={{0,2},{1,3},{2,0},{3,1},{4,6},{5,7},{6,4},{7,5},{8,10},{9,11},{10,... | collective-permute-start | bytes 393224 | tf_op jit(solution)/shard_map/ppermute | solution.py:473
  97.6 1.9 %collective-permute-start.23 = (bf16[2,64,256]{2,1,0:T(8,128)(2,1)S(1)}, bf16[2,64,256]{2,1,0:T(8,128)(2,1)S(1)}, u32[]{:S(2)}, u32[]{:S(2)}) collective-permute-start(bf16[2,64,256]{2,1,0:T(8,128)(2,1)S(1)} %get-tuple-element.65), channel_id=1, source_target_pairs={{0,24},{4,28},{8,16},{12,20},{16,8},{20,12},{24,0},{28,4},{1,25},{... | collective-permute-start | bytes 196616 | tf_op jit(solution)/shard_map/ppermute | solution.py:473
  99.5 1.1 collective-permute-start.24
  100.7 1.0 collective-permute-done.22.refs_5_
  101.6 1.7 %collective-permute-done.23.refs_6_ = bf16[2,64,256]{2,1,0:T(8,128)(2,1)S(1)} collective-permute-done((bf16[2,64,256]{2,1,0:T(8,128)(2,1)S(1)}, bf16[2,64,256]{2,1,0:T(8,128)(2,1)S(1)}, u32[]{:S(2)}, u32[]{:S(2)}) %collective-permute-start.23) | collective-permute-done | bytes 65568 | tf_op jit(solution)/shard_map/ppermute | solution.py:473
  103.3 1.5 %collective-permute-done.24.refs_7_ = bf16[2,64,256]{2,1,0:T(8,128)(2,1)S(1)} collective-permute-done((bf16[2,64,256]{2,1,0:T(8,128)(2,1)S(1)}, bf16[2,64,256]{2,1,0:T(8,128)(2,1)S(1)}, u32[]{:S(2)}, u32[]{:S(2)}) %collective-permute-start.24) | collective-permute-done | bytes 65568 | tf_op jit(solution)/shard_map/ppermute | solution.py:473
  104.8 0.9 combine.3
  106.3 0.8 copy-done.10
  107.7 2.6 %collective-permute-start.25 = (bf16[256,256]{1,0:T(8,128)(2,1)S(1)}, bf16[256,256]{1,0:T(8,128)(2,1)S(1)}, u32[]{:S(2)}, u32[]{:S(2)}) collective-permute-start(bf16[256,256]{1,0:T(8,128)(2,1)S(1)} %get-tuple-element.69), channel_id=1, source_target_pairs={{0,1},{1,0},{2,3},{3,2},{4,5},{5,4},{6,7},{7,6},{8,9},{9,8},{10,11... | collective-permute-start | bytes 393224 | tf_op jit(solution)/shard_map/ppermute | solution.py:473
  110.3 0.8 collective-permute-start.26
  111.1 0.7 collective-permute-start.27
  111.8 4.4 %collective-permute-done.17.refs_3_ = bf16[256,256]{1,0:T(8,128)(2,1)S(1)} collective-permute-done((bf16[256,256]{1,0:T(8,128)(2,1)S(1)}, bf16[256,256]{1,0:T(8,128)(2,1)S(1)}, u32[]{:S(2)}, u32[]{:S(2)}) %collective-permute-start.17) | collective-permute-done | bytes 131104 | tf_op jit(solution)/shard_map/ppermute | solution.py:473
  116.2 1.3 collective-permute-done.25.refs_5_
  117.5 5.3 %collective-permute-done.26.refs_6_ = bf16[256,256]{1,0:T(8,128)(2,1)S(1)} collective-permute-done((bf16[256,256]{1,0:T(8,128)(2,1)S(1)}, bf16[256,256]{1,0:T(8,128)(2,1)S(1)}, u32[]{:S(2)}, u32[]{:S(2)}) %collective-permute-start.26) | collective-permute-done | bytes 131104 | tf_op jit(solution)/shard_map/ppermute | solution.py:473
  122.8 3.9 %collective-permute-done.27.refs_7_ = bf16[256,256]{1,0:T(8,128)(2,1)S(1)} collective-permute-done((bf16[256,256]{1,0:T(8,128)(2,1)S(1)}, bf16[256,256]{1,0:T(8,128)(2,1)S(1)}, u32[]{:S(2)}, u32[]{:S(2)}) %collective-permute-start.27) | collective-permute-done | bytes 131104 | tf_op jit(solution)/shard_map/ppermute | solution.py:473
  126.7 2.2 %copy-done.1 = bf16[4,512,1024]{2,1,0:T(8,128)(2,1)S(1)} copy-done((bf16[4,512,1024]{2,1,0:T(8,128)(2,1)S(1)}, bf16[4,512,1024]{2,1,0:T(8,128)(2,1)}, u32[]{:S(2)}) %copy-start.1) | copy-done | bytes 4194328
  128.9 6.4 %project.1 = bf16[256,2048]{1,0:T(8,128)(2,1)} custom-call(s32[2]{0:T(128)S(1)} %pad_add_fusion.side_ref, bf16[256,256]{1,0:T(8,128)(2,1)S(1)} %get-tuple-element.54.refs_0_, bf16[256,256]{1,0:T(8,128)(2,1)S(1)} %collective-permute-done.15.refs_9_.refs_1_, bf16[256,256]{1,0:T(8,128)(2,1)S(1)} %collective-permute-done.16.refs_10_.refs_2_, ...), custom_call_target="tpu_custom_call" | custom-call | flops 2147483648 | bytes 9437184 | tf_op jit(solution)/shard_map/project/pallas_call | solution.py:365
  (89 shorter events, 4.3 us)
Async XLA Ops:
  6.5 99.7 %all-gather.3.cloned.1.call-start = ((), (), s32[]{:S(2)}) async-start(), calls=%async_computation.2 | async-start | bytes 5242880 | tf_op jit(solution)/shard_map/all_gather | solution.py:445
  13.5 32.6 %all-to-all-start = ((bf16[8,3,2,64,256]{4,3,2,1,0:T(8,128)(2,1)}), bf16[8,3,2,64,256]{4,3,2,1,0:T(8,128)(2,1)}, u32[]{:S(2)}, u32[]{:S(2)}) async-start(bf16[8,3,2,64,256]{4,3,2,1,0:T(8,128)(2,1)} %prepare.2.refs_0_), calls=%async_computation | async-start | bytes 3145728 | tf_op jit(solution)/shard_map/all_to_all | solution.py:490
  20.5 19.2 %collective-permute-start = (bf16[2,64,512]{2,1,0:T(8,128)(2,1)}, bf16[2,64,512]{2,1,0:T(8,128)(2,1)S(1)}, u32[]{:S(2)}, u32[]{:S(2)}) collective-permute-start(bf16[2,64,512]{2,1,0:T(8,128)(2,1)} %get-tuple-element.40.refs_0_), channel_id=1, source_target_pairs={{0,8},{4,12},{8,0},{12,4},{16,24},{20,28},{24,16},{28,20},{1,9},{5... | collective-permute-start | bytes 393224 | tf_op jit(solution)/shard_map/ppermute | solution.py:392
  20.6 20.3 %collective-permute-start.1 = (bf16[2,64,512]{2,1,0:T(8,128)(2,1)}, bf16[2,64,512]{2,1,0:T(8,128)(2,1)S(1)}, u32[]{:S(2)}, u32[]{:S(2)}) collective-permute-start(bf16[2,64,512]{2,1,0:T(8,128)(2,1)} %get-tuple-element.40.refs_0_), channel_id=1, source_target_pairs={{0,16},{4,20},{8,24},{12,28},{16,0},{20,4},{24,8},{28,12},{1,17},{... | collective-permute-start | bytes 393224 | tf_op jit(solution)/shard_map/ppermute | solution.py:392
  22.5 20.9 %collective-permute-start.2 = (bf16[2,64,512]{2,1,0:T(8,128)(2,1)}, bf16[2,64,512]{2,1,0:T(8,128)(2,1)S(1)}, u32[]{:S(2)}, u32[]{:S(2)}) collective-permute-start(bf16[2,64,512]{2,1,0:T(8,128)(2,1)} %get-tuple-element.40.refs_0_), channel_id=1, source_target_pairs={{0,24},{4,28},{8,16},{12,20},{16,8},{20,12},{24,0},{28,4},{1,25},{... | collective-permute-start | bytes 393224 | tf_op jit(solution)/shard_map/ppermute | solution.py:392
  39.7 3.7 %copy-start.17 = (bf16[2,64,512]{2,1,0:T(8,128)(2,1)}, bf16[2,64,512]{2,1,0:T(8,128)(2,1)S(1)}, u32[]{:S(2)}) copy-start(bf16[2,64,512]{2,1,0:T(8,128)(2,1)S(1)} %collective-permute-done.refs_1_) | copy-start | bytes 393220
  40.9 2.5 %copy-start.19 = (bf16[2,64,512]{2,1,0:T(8,128)(2,1)}, bf16[2,64,512]{2,1,0:T(8,128)(2,1)S(1)}, u32[]{:S(2)}) copy-start(bf16[2,64,512]{2,1,0:T(8,128)(2,1)S(1)} %collective-permute-done.1.refs_2_) | copy-start | bytes 393220
  44.0 22.5 %collective-permute-start.3 = (bf16[2,512,512]{2,1,0:T(8,128)(2,1)}, bf16[2,512,512]{2,1,0:T(8,128)(2,1)}, u32[]{:S(2)}, u32[]{:S(2)}) collective-permute-start(bf16[2,512,512]{2,1,0:T(8,128)(2,1)} %after.3), channel_id=1, source_target_pairs={{0,4},{4,8},{8,12},{12,16},{16,20},{20,24},{24,28},{1,5},{5,9},{9,... | collective-permute-start | bytes 3145736 | tf_op jit(solution)/shard_map/ppermute | solution.py:458
  46.0 6.4 %copy-start.23 = (bf16[2,64,512]{2,1,0:T(8,128)(2,1)S(1)}, bf16[2,64,512]{2,1,0:T(8,128)(2,1)}, u32[]{:S(2)}) copy-start(bf16[2,64,512]{2,1,0:T(8,128)(2,1)} %get-tuple-element.40.refs_0_) | copy-start | bytes 393220
  46.0 6.6 %copy-start.18 = (bf16[2,64,512]{2,1,0:T(8,128)(2,1)S(1)}, bf16[2,64,512]{2,1,0:T(8,128)(2,1)}, u32[]{:S(2)}) copy-start(bf16[2,64,512]{2,1,0:T(8,128)(2,1)} %copy-done.17) | copy-start | bytes 393220
  46.0 6.9 %copy-start.20 = (bf16[2,64,512]{2,1,0:T(8,128)(2,1)S(1)}, bf16[2,64,512]{2,1,0:T(8,128)(2,1)}, u32[]{:S(2)}) copy-start(bf16[2,64,512]{2,1,0:T(8,128)(2,1)} %copy-done.19) | copy-start | bytes 393220
  46.0 7.1 %copy-start.22 = (bf16[2,64,512]{2,1,0:T(8,128)(2,1)S(1)}, bf16[2,64,512]{2,1,0:T(8,128)(2,1)}, u32[]{:S(2)}) copy-start(bf16[2,64,512]{2,1,0:T(8,128)(2,1)} %copy-done.21) | copy-start | bytes 393220
  46.0 34.9 %all-to-all-start.1 = ((bf16[8,3,2,64,256]{4,3,2,1,0:T(8,128)(2,1)}), bf16[8,3,2,64,256]{4,3,2,1,0:T(8,128)(2,1)}, u32[]{:S(2)}, u32[]{:S(2)}) async-start(bf16[8,3,2,64,256]{4,3,2,1,0:T(8,128)(2,1)} %after.4), calls=%async_computation.1 | async-start | bytes 3145728 | tf_op jit(solution)/shard_map/all_to_all | solution.py:490
  52.4 5.8 %collective-permute-start.4 = (bf16[2,64,512]{2,1,0:T(8,128)(2,1)S(1)}, bf16[2,64,512]{2,1,0:T(8,128)(2,1)S(1)}, u32[]{:S(2)}, u32[]{:S(2)}) collective-permute-start(bf16[2,64,512]{2,1,0:T(8,128)(2,1)S(1)} %copy-done.23), channel_id=1, source_target_pairs={{0,4},{4,0},{8,12},{12,8},{16,20},{20,16},{24,28},{28,24},{1,5},{5... | collective-permute-start | bytes 393224 | tf_op jit(solution)/shard_map/ppermute | solution.py:392
  52.5 5.7 %collective-permute-start.5 = (bf16[2,64,512]{2,1,0:T(8,128)(2,1)S(1)}, bf16[2,64,512]{2,1,0:T(8,128)(2,1)S(1)}, u32[]{:S(2)}, u32[]{:S(2)}) collective-permute-start(bf16[2,64,512]{2,1,0:T(8,128)(2,1)S(1)} %copy-done.18), channel_id=1, source_target_pairs={{0,4},{4,0},{8,12},{12,8},{16,20},{20,16},{24,28},{28,24},{1,5},{5... | collective-permute-start | bytes 393224 | tf_op jit(solution)/shard_map/ppermute | solution.py:392
  52.9 7.1 %collective-permute-start.6 = (bf16[2,64,512]{2,1,0:T(8,128)(2,1)S(1)}, bf16[2,64,512]{2,1,0:T(8,128)(2,1)S(1)}, u32[]{:S(2)}, u32[]{:S(2)}) collective-permute-start(bf16[2,64,512]{2,1,0:T(8,128)(2,1)S(1)} %copy-done.20), channel_id=1, source_target_pairs={{0,4},{4,0},{8,12},{12,8},{16,20},{20,16},{24,28},{28,24},{1,5},{5... | collective-permute-start | bytes 393224 | tf_op jit(solution)/shard_map/ppermute | solution.py:392
  53.1 7.0 %collective-permute-start.7 = (bf16[2,64,512]{2,1,0:T(8,128)(2,1)S(1)}, bf16[2,64,512]{2,1,0:T(8,128)(2,1)S(1)}, u32[]{:S(2)}, u32[]{:S(2)}) collective-permute-start(bf16[2,64,512]{2,1,0:T(8,128)(2,1)S(1)} %copy-done.22), channel_id=1, source_target_pairs={{0,4},{4,0},{8,12},{12,8},{16,20},{20,16},{24,28},{28,24},{1,5},{5... | collective-permute-start | bytes 393224 | tf_op jit(solution)/shard_map/ppermute | solution.py:392
  58.2 8.4 %copy-start.16 = (f32[8,128]{1,0:T(8,128)}, f32[8,128]{1,0:T(8,128)S(1)}, u32[]{:S(2)}) copy-start(f32[8,128]{1,0:T(8,128)S(1)} %get-tuple-element.41.refs_8_) | copy-start | bytes 12292
  58.2 8.4 %copy-start.24 = (bf16[2,64,512]{2,1,0:T(8,128)(2,1)}, bf16[2,64,512]{2,1,0:T(8,128)(2,1)S(1)}, u32[]{:S(2)}) copy-start(bf16[2,64,512]{2,1,0:T(8,128)(2,1)S(1)} %collective-permute-done.4.refs_4_) | copy-start | bytes 393220
  58.2 26.4 %collective-permute-start.10 = (bf16[2,64,256]{2,1,0:T(8,128)(2,1)}, bf16[2,64,256]{2,1,0:T(8,128)(2,1)S(1)}, u32[]{:S(2)}, u32[]{:S(2)}) collective-permute-start(bf16[2,64,256]{2,1,0:T(8,128)(2,1)} %get-tuple-element.46), channel_id=1, source_target_pairs={{0,12},{4,8},{8,4},{12,0},{16,28},{20,24},{24,20},{28,16},{1,13},{... | collective-permute-start | bytes 196616 | tf_op jit(solution)/shard_map/ppermute | solution.py:473
  58.3 8.3 %copy-start.25 = (bf16[2,64,512]{2,1,0:T(8,128)(2,1)}, bf16[2,64,512]{2,1,0:T(8,128)(2,1)S(1)}, u32[]{:S(2)}) copy-start(bf16[2,64,512]{2,1,0:T(8,128)(2,1)S(1)} %collective-permute-done.5.refs_5_) | copy-start | bytes 393220
  58.3 28.3 %collective-permute-start.11 = (bf16[2,64,256]{2,1,0:T(8,128)(2,1)}, bf16[2,64,256]{2,1,0:T(8,128)(2,1)S(1)}, u32[]{:S(2)}, u32[]{:S(2)}) collective-permute-start(bf16[2,64,256]{2,1,0:T(8,128)(2,1)} %get-tuple-element.47), channel_id=1, source_target_pairs={{0,16},{4,20},{8,24},{12,28},{16,0},{20,4},{24,8},{28,12},{1,17},{... | collective-permute-start | bytes 196616 | tf_op jit(solution)/shard_map/ppermute | solution.py:473
  60.0 6.6 %copy-start.26 = (bf16[2,64,512]{2,1,0:T(8,128)(2,1)}, bf16[2,64,512]{2,1,0:T(8,128)(2,1)S(1)}, u32[]{:S(2)}) copy-start(bf16[2,64,512]{2,1,0:T(8,128)(2,1)S(1)} %collective-permute-done.6.refs_6_) | copy-start | bytes 393220
  60.0 26.6 %collective-permute-start.12 = (bf16[2,64,256]{2,1,0:T(8,128)(2,1)}, bf16[2,64,256]{2,1,0:T(8,128)(2,1)S(1)}, u32[]{:S(2)}, u32[]{:S(2)}) collective-permute-start(bf16[2,64,256]{2,1,0:T(8,128)(2,1)} %get-tuple-element.48), channel_id=1, source_target_pairs={{0,20},{4,16},{8,28},{12,24},{16,4},{20,0},{24,12},{28,8},{1,21},{... | collective-permute-start | bytes 196616 | tf_op jit(solution)/shard_map/ppermute | solution.py:473
  60.0 6.6 %copy-start.27 = (bf16[2,64,512]{2,1,0:T(8,128)(2,1)}, bf16[2,64,512]{2,1,0:T(8,128)(2,1)S(1)}, u32[]{:S(2)}) copy-start(bf16[2,64,512]{2,1,0:T(8,128)(2,1)S(1)} %collective-permute-done.7.refs_7_) | copy-start | bytes 393220
  60.0 26.8 %collective-permute-start.13 = (bf16[2,64,256]{2,1,0:T(8,128)(2,1)}, bf16[2,64,256]{2,1,0:T(8,128)(2,1)S(1)}, u32[]{:S(2)}, u32[]{:S(2)}) collective-permute-start(bf16[2,64,256]{2,1,0:T(8,128)(2,1)} %get-tuple-element.49), channel_id=1, source_target_pairs={{0,24},{4,28},{8,16},{12,20},{16,8},{20,12},{24,0},{28,4},{1,25},{... | collective-permute-start | bytes 196616 | tf_op jit(solution)/shard_map/ppermute | solution.py:473
  66.6 22.8 %collective-permute-start.14 = (bf16[2,64,256]{2,1,0:T(8,128)(2,1)}, bf16[2,64,256]{2,1,0:T(8,128)(2,1)S(1)}, u32[]{:S(2)}, u32[]{:S(2)}) collective-permute-start(bf16[2,64,256]{2,1,0:T(8,128)(2,1)} %get-tuple-element.50), channel_id=1, source_target_pairs={{0,28},{4,24},{8,20},{12,16},{16,12},{20,8},{24,4},{28,0},{1,29},{... | collective-permute-start | bytes 196616 | tf_op jit(solution)/shard_map/ppermute | solution.py:473
  80.9 10.6 %copy-start.3 = (f32[1024,256]{1,0:T(8,128)S(1)}, f32[1024,256]{1,0:T(8,128)}, u32[]{:S(2)}) copy-start(f32[1024,256]{1,0:T(8,128)} %get-tuple-element.42.home_ref) | copy-start | bytes 3145732
  80.9 3.7 %copy-start.14 = (bf16[2,64,256]{2,1,0:T(8,128)(2,1)S(1)}, bf16[2,64,256]{2,1,0:T(8,128)(2,1)}, u32[]{:S(2)}) copy-start(bf16[2,64,256]{2,1,0:T(8,128)(2,1)} %copy-done.13) | copy-start | bytes 196612
  80.9 5.7 %copy-start.12 = (bf16[2,64,256]{2,1,0:T(8,128)(2,1)S(1)}, bf16[2,64,256]{2,1,0:T(8,128)(2,1)}, u32[]{:S(2)}) copy-start(bf16[2,64,256]{2,1,0:T(8,128)(2,1)} %copy-done.11) | copy-start | bytes 196612
  81.7 23.1 %copy-start.2 = (f32[1024,256]{1,0:T(8,128)S(1)}, f32[1024,256]{1,0:T(8,128)}, u32[]{:S(2)}) copy-start(f32[1024,256]{1,0:T(8,128)} %get-tuple-element.58.home_ref) | copy-start | bytes 3145732
  84.6 5.5 %collective-permute-start.8 = (bf16[2,64,256]{2,1,0:T(8,128)(2,1)S(1)}, bf16[2,64,256]{2,1,0:T(8,128)(2,1)S(1)}, u32[]{:S(2)}, u32[]{:S(2)}) collective-permute-start(bf16[2,64,256]{2,1,0:T(8,128)(2,1)S(1)} %copy-done.14), channel_id=1, source_target_pairs={{0,4},{4,0},{8,12},{12,8},{16,20},{20,16},{24,28},{28,24},{1,5},{5... | collective-permute-start | bytes 196616 | tf_op jit(solution)/shard_map/ppermute | solution.py:473
  86.6 4.8 %collective-permute-start.9 = (bf16[2,64,256]{2,1,0:T(8,128)(2,1)S(1)}, bf16[2,64,256]{2,1,0:T(8,128)(2,1)S(1)}, u32[]{:S(2)}, u32[]{:S(2)}) collective-permute-start(bf16[2,64,256]{2,1,0:T(8,128)(2,1)S(1)} %copy-done.12), channel_id=1, source_target_pairs={{0,8},{4,12},{8,0},{12,4},{16,24},{20,28},{24,16},{28,20},{1,9},{5... | collective-permute-start | bytes 196616 | tf_op jit(solution)/shard_map/ppermute | solution.py:473
  86.6 8.0 %collective-permute-start.18 = (bf16[2,64,256]{2,1,0:T(8,128)(2,1)S(1)}, bf16[2,64,256]{2,1,0:T(8,128)(2,1)S(1)}, u32[]{:S(2)}, u32[]{:S(2)}) collective-permute-start(bf16[2,64,256]{2,1,0:T(8,128)(2,1)S(1)} %get-tuple-element.60), channel_id=1, source_target_pairs={{0,4},{4,0},{8,12},{12,8},{16,20},{20,16},{24,28},{28,24},{1,5},{5... | collective-permute-start | bytes 196616 | tf_op jit(solution)/shard_map/ppermute | solution.py:473
  87.5 10.1 %collective-permute-start.19 = (bf16[2,64,256]{2,1,0:T(8,128)(2,1)S(1)}, bf16[2,64,256]{2,1,0:T(8,128)(2,1)S(1)}, u32[]{:S(2)}, u32[]{:S(2)}) collective-permute-start(bf16[2,64,256]{2,1,0:T(8,128)(2,1)S(1)} %get-tuple-element.61), channel_id=1, source_target_pairs={{0,8},{4,12},{8,0},{12,4},{16,24},{20,28},{24,16},{28,20},{1,9},{5... | collective-permute-start | bytes 196616 | tf_op jit(solution)/shard_map/ppermute | solution.py:473
  90.0 7.6 %collective-permute-start.20 = (bf16[2,64,256]{2,1,0:T(8,128)(2,1)S(1)}, bf16[2,64,256]{2,1,0:T(8,128)(2,1)S(1)}, u32[]{:S(2)}, u32[]{:S(2)}) collective-permute-start(bf16[2,64,256]{2,1,0:T(8,128)(2,1)S(1)} %get-tuple-element.62), channel_id=1, source_target_pairs={{0,12},{4,8},{8,4},{12,0},{16,28},{20,24},{24,20},{28,16},{1,13},{... | collective-permute-start | bytes 196616 | tf_op jit(solution)/shard_map/ppermute | solution.py:473
  90.1 9.4 %collective-permute-start.21 = (bf16[2,64,256]{2,1,0:T(8,128)(2,1)S(1)}, bf16[2,64,256]{2,1,0:T(8,128)(2,1)S(1)}, u32[]{:S(2)}, u32[]{:S(2)}) collective-permute-start(bf16[2,64,256]{2,1,0:T(8,128)(2,1)S(1)} %get-tuple-element.63), channel_id=1, source_target_pairs={{0,16},{4,20},{8,24},{12,28},{16,0},{20,4},{24,8},{28,12},{1,17},{... | collective-permute-start | bytes 196616 | tf_op jit(solution)/shard_map/ppermute | solution.py:473
  94.7 10.1 %collective-permute-start.15 = (bf16[256,256]{1,0:T(8,128)(2,1)S(1)}, bf16[256,256]{1,0:T(8,128)(2,1)S(1)}, u32[]{:S(2)}, u32[]{:S(2)}) collective-permute-start(bf16[256,256]{1,0:T(8,128)(2,1)S(1)} %get-tuple-element.55), channel_id=1, source_target_pairs={{0,1},{1,0},{2,3},{3,2},{4,5},{5,4},{6,7},{7,6},{8,9},{9,8},{10,11... | collective-permute-start | bytes 393224 | tf_op jit(solution)/shard_map/ppermute | solution.py:473
  94.7 10.1 %collective-permute-start.16 = (bf16[256,256]{1,0:T(8,128)(2,1)S(1)}, bf16[256,256]{1,0:T(8,128)(2,1)S(1)}, u32[]{:S(2)}, u32[]{:S(2)}) collective-permute-start(bf16[256,256]{1,0:T(8,128)(2,1)S(1)} %get-tuple-element.56), channel_id=1, source_target_pairs={{0,2},{1,3},{2,0},{3,1},{4,6},{5,7},{6,4},{7,5},{8,10},{9,11},{10,... | collective-permute-start | bytes 393224 | tf_op jit(solution)/shard_map/ppermute | solution.py:473
  97.6 4.0 %collective-permute-start.22 = (bf16[2,64,256]{2,1,0:T(8,128)(2,1)S(1)}, bf16[2,64,256]{2,1,0:T(8,128)(2,1)S(1)}, u32[]{:S(2)}, u32[]{:S(2)}) collective-permute-start(bf16[2,64,256]{2,1,0:T(8,128)(2,1)S(1)} %get-tuple-element.64), channel_id=1, source_target_pairs={{0,20},{4,16},{8,28},{12,24},{16,4},{20,0},{24,12},{28,8},{1,21},{... | collective-permute-start | bytes 196616 | tf_op jit(solution)/shard_map/ppermute | solution.py:473
  97.6 5.7 %collective-permute-start.23 = (bf16[2,64,256]{2,1,0:T(8,128)(2,1)S(1)}, bf16[2,64,256]{2,1,0:T(8,128)(2,1)S(1)}, u32[]{:S(2)}, u32[]{:S(2)}) collective-permute-start(bf16[2,64,256]{2,1,0:T(8,128)(2,1)S(1)} %get-tuple-element.65), channel_id=1, source_target_pairs={{0,24},{4,28},{8,16},{12,20},{16,8},{20,12},{24,0},{28,4},{1,25},{... | collective-permute-start | bytes 196616 | tf_op jit(solution)/shard_map/ppermute | solution.py:473
  99.5 5.3 %collective-permute-start.24 = (bf16[2,64,256]{2,1,0:T(8,128)(2,1)S(1)}, bf16[2,64,256]{2,1,0:T(8,128)(2,1)S(1)}, u32[]{:S(2)}, u32[]{:S(2)}) collective-permute-start(bf16[2,64,256]{2,1,0:T(8,128)(2,1)S(1)} %get-tuple-element.66), channel_id=1, source_target_pairs={{0,28},{4,24},{8,20},{12,16},{16,12},{20,8},{24,4},{28,0},{1,29},{... | collective-permute-start | bytes 196616 | tf_op jit(solution)/shard_map/ppermute | solution.py:473
  106.3 20.4 %collective-permute-start.28 = (bf16[4,512,1024]{2,1,0:T(8,128)(2,1)}, bf16[4,512,1024]{2,1,0:T(8,128)(2,1)S(1)}, u32[]{:S(2)}, u32[]{:S(2)}) collective-permute-start(bf16[4,512,1024]{2,1,0:T(8,128)(2,1)} %after.5.refs_8_), channel_id=1, source_target_pairs={{0,4},{4,0},{8,12},{12,8},{16,20},{20,16},{24,28},{28,24},{1,5},{5... | collective-permute-start | bytes 12582920 | tf_op jit(solution)/shard_map/ppermute | solution.py:503
  107.2 9.0 %collective-permute-start.17 = (bf16[256,256]{1,0:T(8,128)(2,1)S(1)}, bf16[256,256]{1,0:T(8,128)(2,1)S(1)}, u32[]{:S(2)}, u32[]{:S(2)}) collective-permute-start(bf16[256,256]{1,0:T(8,128)(2,1)S(1)} %copy-done.10), channel_id=1, source_target_pairs={{0,3},{1,2},{2,1},{3,0},{4,7},{5,6},{6,5},{7,4},{8,11},{9,10},{10,... | collective-permute-start | bytes 393224 | tf_op jit(solution)/shard_map/ppermute | solution.py:473
  107.7 9.8 %collective-permute-start.25 = (bf16[256,256]{1,0:T(8,128)(2,1)S(1)}, bf16[256,256]{1,0:T(8,128)(2,1)S(1)}, u32[]{:S(2)}, u32[]{:S(2)}) collective-permute-start(bf16[256,256]{1,0:T(8,128)(2,1)S(1)} %get-tuple-element.69), channel_id=1, source_target_pairs={{0,1},{1,0},{2,3},{3,2},{4,5},{5,4},{6,7},{7,6},{8,9},{9,8},{10,11... | collective-permute-start | bytes 393224 | tf_op jit(solution)/shard_map/ppermute | solution.py:473
  110.3 12.5 %collective-permute-start.26 = (bf16[256,256]{1,0:T(8,128)(2,1)S(1)}, bf16[256,256]{1,0:T(8,128)(2,1)S(1)}, u32[]{:S(2)}, u32[]{:S(2)}) collective-permute-start(bf16[256,256]{1,0:T(8,128)(2,1)S(1)} %get-tuple-element.70), channel_id=1, source_target_pairs={{0,2},{1,3},{2,0},{3,1},{4,6},{5,7},{6,4},{7,5},{8,10},{9,11},{10,... | collective-permute-start | bytes 393224 | tf_op jit(solution)/shard_map/ppermute | solution.py:473
  111.1 15.6 %collective-permute-start.27 = (bf16[256,256]{1,0:T(8,128)(2,1)S(1)}, bf16[256,256]{1,0:T(8,128)(2,1)S(1)}, u32[]{:S(2)}, u32[]{:S(2)}) collective-permute-start(bf16[256,256]{1,0:T(8,128)(2,1)S(1)} %get-tuple-element.71), channel_id=1, source_target_pairs={{0,3},{1,2},{2,1},{3,0},{4,7},{5,6},{6,5},{7,4},{8,11},{9,10},{10,... | collective-permute-start | bytes 393224 | tf_op jit(solution)/shard_map/ppermute | solution.py:473
  126.7 2.2 %copy-start.1 = (bf16[4,512,1024]{2,1,0:T(8,128)(2,1)S(1)}, bf16[4,512,1024]{2,1,0:T(8,128)(2,1)}, u32[]{:S(2)}) copy-start(bf16[4,512,1024]{2,1,0:T(8,128)(2,1)} %after.5.refs_8_) | copy-start | bytes 12582916
  (12 other events, 9.4 us)
Sparse Core Ops, SparseCore 0:
  9.4 79.4 all-gather.2

commit v6 on v5

--- a/solution.py
+++ b/solution.py
@@ -141,6 +141,28 @@
         values.reshape(blocks, BLOCK, width),
         *waits,
     )
+
+
+def half_kernel(side_ref, weight_ref, *refs):
+    refs[-1][...] = weight_ref[...]
+
+
+def half_of(side, weight, waits):
+    rows, width = weight.shape
+    return pl.pallas_call(
+        half_kernel,
+        grid_spec=pltpu.PrefetchScalarGridSpec(
+            num_scalar_prefetch=1,
+            grid=(2,),
+            in_specs=[pl.BlockSpec((rows // 2, width // 2), lambda i, side: (i, side[0]))]
+            + moments(waits),
+            out_specs=pl.BlockSpec((rows // 2, width // 2), lambda i, side: (i, 0)),
+        ),
+        out_shape=jax.ShapeDtypeStruct((rows, width // 2), BF16),
+        compiler_params=params(60),
+        cost_estimate=cost(0, 2 * rows * width),
+        name="half",
+    )(side, weight, *waits)
 
 
 def prep_kernel(q_ref, k_ref, v_ref, *refs):
@@ -238,7 +260,7 @@
         out_specs=[pl.BlockSpec((tokens_dev, HEAD_SIZE), lambda h: (0, h)), mark_spec()],
         out_shape=[jax.ShapeDtypeStruct((tokens_dev, heads * HEAD_SIZE), F32), MARK],
         compiler_params=params(60),
-        cost_estimate=cost(8 * pairs * HEAD_SIZE, 14 * tokens_dev * width, pairs),
+        cost_estimate=cost(64 * pairs * HEAD_SIZE, 14 * tokens_dev * width, 8 * pairs),
         name="home",
     )(place, queries, keys, values, rim, *summary, *waits)
 
@@ -377,7 +399,7 @@
             ),
         ),
         out_shape=jax.ShapeDtypeStruct((tokens, 2 * half), BF16),
-        compiler_params=params(24),
+        compiler_params=params(60),
         cost_estimate=cost(
             4 * slots * tokens * width * half, 2 * slots * width * (2 * half + tokens)
         ),
@@ -439,14 +461,14 @@
     side = place % 2
     sibling = [(i, i ^ 1) for i in range(ctx)]
 
-    half = out_weight.shape[1] // 2
     part = width // chunks
-    weight_half = lax.dynamic_slice_in_dim(out_weight, side * half, half, axis=1)
-    mine = lax.all_gather(weight_half, "head", axis=0)
+    seat = lax.axis_index("head").astype(jnp.int32)
+    sides = jnp.stack([side.astype(jnp.int32), seat])
 
     sends = []
     if ctx <= STRIDE:
         sends.append(prepare(queries, keys, values, ctx, 0, chunks, ()))
+    mine = lax.all_gather(half_of(sides, out_weight, sends), "head", axis=0)
     rim, picked = edges(keys, values, sends)
     between, within, order = gather_ctx(picked)
     summary = between + within
@@ -456,14 +478,12 @@
         sends.append(prepare(queries, keys, values, ctx, chunk, chunks, (picked,)))
     rim = after(rim, (*between[1:], *sends[1:]))
     before = lax.ppermute(rim, "ctx", [(i, i + 1) for i in range(ctx - 1)])
-    sends[1:] = [after(send, between[1:]) for send in sends[1:]]
+    sends[1:] = [after(send, (rim,)) for send in sends[1:]]
 
     def home(chunk, waits):
         return home_sections(
             place_word, queries, keys, values, before, summary, order, chunk, chunks, waits
         )
-
-    seat = lax.axis_index("head").astype(jnp.int32)
 
     def exchange(slabs, axis):
         count = len(slabs)
@@ -485,23 +505,26 @@
             waits = (mark,)
     else:
         seats = jnp.stack([seat, place.astype(jnp.int32)])
-        homes, backs = [], []
-        for chunk in range(chunks):
-            received = lax.all_to_all(sends[chunk], "ctx", split_axis=0, concat_axis=0, tiled=True)
-            *slabs, mark = stride_attend(place_word, received, waits)
-            backs.append(exchange(slabs, "ctx"))
-            waits = (mark,)
-            for ready in range(chunks) if chunk == 0 else ():
-                sections, mark = home(ready, waits)
-                homes.append(sections)
+        arrived = ()
+        for chunk in range(chunks + 1):
+            if chunk < chunks:
+                send = sends[chunk]
+                received = lax.all_to_all(send, "ctx", split_axis=0, concat_axis=0, tiled=True)
+                *slabs, mark = stride_attend(place_word, received, waits)
+                backs = exchange(slabs, "ctx")
                 waits = (mark,)
-        for chunk in range(chunks):
-            *slabs, mark = combine(seats, homes[chunk], backs[chunk], groups, waits)
-            moved.append(exchange(slabs, "head"))
-            waits = (mark, *moved[-1][1:3])
+            if chunk > 0:
+                seats = jnp.stack([seat, place.astype(jnp.int32)])
+                *slabs, mark = combine(seats, sections, ready, groups, (*waits, *arrived))
+                moved.append(exchange(slabs, "head"))
+                waits = (mark,)
+                arrived = moved[-1][1:]
+            if chunk < chunks:
+                sections, mark = home(chunk, waits)
+                ready = backs
+                waits = (mark,)
     held = after(mine, (mark,))
     other = lax.ppermute(held, "ctx", sibling)
-    sides = jnp.stack([side.astype(jnp.int32), seat])
     return project(sides, moved, held, other)
 
 

time: 144 us -> 146 us (1.014)
  local copies, waits for them, and re-layouts: 12.6 us -> 5.91 us
  Pallas kernels: 39.5 us -> 43 us
  waiting for transfers between devices: 38.2 us -> 41.1 us
  starting transfers between devices: 38.1 us -> 39.9 us
    unnamed x56 -> x36, local copies, waits for them, and re-layouts: 11.5 us -> 5.91 us
    ppermute x1, waiting for transfers between devices: 3.98 us -> 8.67 us  [body(): before = lax.ppermute(rim, 'ctx', [(i, i + 1) for i in range(ctx - 1)])]
    ppermute x20, starting transfers between devices: 20.5 us -> 23.9 us  [exchange(): moved.append(lax.ppermute(slabs[slot], axis, pairs))]
    pallas_call x1, Pallas kernels: 6.4 us -> 9.57 us  [project(): pl.pallas_call(functools.partial(project_kernel, slots=slots, chunks=chun...]
    all_to_all x2, starting transfers between devices: 11.1 us -> 8.29 us  [body(): lax.all_to_all(send, 'ctx', split_axis=0, concat_axis=0, tiled=True)]
    pallas_call x0 -> x1, Pallas kernels: none -> 2.76 us  [half_of(): pl.pallas_call(half_kernel, grid_spec=pltpu.PrefetchScalarGridSpec(num_sc...]
    pallas_call x2, Pallas kernels: 6.36 us -> 4.17 us  [stride_attend(): pl.pallas_call(stride_kernel, grid=(per,), in_specs=[pl.BlockSpec(memory_...]
    ppermute x20, waiting for transfers between devices: 19 us -> 17.1 us  [exchange(): moved.append(lax.ppermute(slabs[slot], axis, pairs))]
  transfers between devices with their start and end apart: 32 -> 32, of which waited for: 11 -> 8; matrix products, arithmetic and copies ran while one was open for 0% -> 0% of each run, Pallas kernels for 23% -> 18%
where the time goes in v6:
time: 146 us; the launch traced here: 144 us
  Pallas kernels  43 us (29%)
  waiting for transfers between devices  41.1 us (28%)
  starting transfers between devices  39.9 us (27%)
  between operations  13.6 us (9%)
  local copies, waits for them, and re-layouts  5.91 us (4%)
    ppermute x20, starting transfers between devices, exchange(): moved.append(lax.ppermute(slabs[slot], axis, pairs))  23.9 us
    ppermute x20, waiting for transfers between devices, exchange(): moved.append(lax.ppermute(slabs[slot], axis, pairs))  17.1 us
    ppermute x7, waiting for transfers between devices, swapped(): return lax.ppermute(piece, 'ctx', [(i, i ^ distance) for i in range(count)])  15.2 us
    pallas_call x2, Pallas kernels, home_sections(): pl.pallas_call(functools.partial(home_kernel, order=order), grid=(heads,)...  14.1 us
    pallas_call x1, Pallas kernels, project(): pl.pallas_call(functools.partial(project_kernel, slots=slots, chunks=chun...  9.57 us
    ppermute x1, waiting for transfers between devices, body(): before = lax.ppermute(rim, 'ctx', [(i, i + 1) for i in range(ctx - 1)])  8.67 us
    pallas_call x2, Pallas kernels, prepare(): pl.pallas_call(prep_kernel, grid=(tokens_dev // TILE,), in_specs=[pl.Bloc...  8.45 us
    all_to_all x2, starting transfers between devices, body(): lax.all_to_all(send, 'ctx', split_axis=0, concat_axis=0, tiled=True)  8.29 us
  transfers between devices with their start and end apart: 32, of which 8 were waited for; matrix products, arithmetic and copies ran while one was open for 0% of the time, Pallas kernels for 18%

profile of v6, /device:TPU:10, one launch (start us, length us, event | category | flops | bytes accessed | tf_op | source)
XLA Modules:
  0.0 144.2 jit_solution(3028748298778445224)
XLA Ops:
  6.5 0.7 pad_add_fusion.side_ref
  7.2 4.2 %prepare.2.refs_0_ = bf16[8,3,2,64,256]{4,3,2,1,0:T(8,128)(2,1)} custom-call(bf16[1024,512]{1,0:T(8,128)(2,1)} %q_ref.7, bf16[1024,512]{1,0:T(8,128)(2,1)} %k_ref.9, bf16[1024,512]{1,0:T(8,128)(2,1)} %v_ref.9), custom_call_target="tpu_custom_call" | custom-call | flops 402653184 | bytes 3145728 | tf_op jit(solution)/shard_map/prepare/pallas_call | solution.py:181
  11.4 2.8 %half.1 = bf16[512,1024]{1,0:T(8,128)(2,1)} custom-call(s32[2]{0:T(128)} %pad_add_fusion.side_ref, bf16[512,2048]{1,0:T(8,128)(2,1)} %weight_ref.1, bf16[8,3,2,64,256]{4,3,2,1,0:T(8,128)(2,1)} %prepare.2.refs_0_), custom_call_target="tpu_custom_call" | custom-call | bytes 2097152 | tf_op jit(solution)/shard_map/half/pallas_call | solution.py:152
  14.2 4.3 %all-to-all-start = ((bf16[8,3,2,64,256]{4,3,2,1,0:T(8,128)(2,1)}), bf16[8,3,2,64,256]{4,3,2,1,0:T(8,128)(2,1)S(1)}, u32[]{:S(2)}, u32[]{:S(2)}) async-start(bf16[8,3,2,64,256]{4,3,2,1,0:T(8,128)(2,1)} %prepare.2.refs_0_), calls=%async_computation | async-start | bytes 3145728 | tf_op jit(solution)/shard_map/all_to_all | solution.py:512
  18.5 2.2 %edges.1 = (bf16[2,512,512]{2,1,0:T(8,128)(2,1)}, bf16[2,64,512]{2,1,0:T(8,128)(2,1)}) custom-call(bf16[1024,512]{1,0:T(8,128)(2,1)} %k_ref.9, bf16[1024,512]{1,0:T(8,128)(2,1)} %v_ref.9, bf16[8,128,512]{2,1,0:T(8,128)(2,1)} %bitcast.7, bf16[8,128,512]{2,1,0:T(8,128)(2,1)} %bitcast.8, bf16[8,3,2,64,256]{4,3,2,1,0:T(8,128)(2,1)} %prepare.2.refs_0_), custom_call_target="tpu_custom_call" | custom-call | bytes 2097152 | tf_op jit(solution)/shard_map/edges/pallas_call | solution.py:122
  20.6 1.5 %collective-permute-start.2 = (bf16[2,64,512]{2,1,0:T(8,128)(2,1)}, bf16[2,64,512]{2,1,0:T(8,128)(2,1)S(1)}, u32[]{:S(2)}, u32[]{:S(2)}) collective-permute-start(bf16[2,64,512]{2,1,0:T(8,128)(2,1)} %get-tuple-element.40.refs_0_), channel_id=1, source_target_pairs={{0,24},{4,28},{8,16},{12,20},{16,8},{20,12},{24,0},{28,4},{1,25},{... | collective-permute-start | bytes 393224 | tf_op jit(solution)/shard_map/ppermute | solution.py:414
  22.2 1.9 %collective-permute-start = (bf16[2,64,512]{2,1,0:T(8,128)(2,1)}, bf16[2,64,512]{2,1,0:T(8,128)(2,1)S(1)}, u32[]{:S(2)}, u32[]{:S(2)}) collective-permute-start(bf16[2,64,512]{2,1,0:T(8,128)(2,1)} %get-tuple-element.40.refs_0_), channel_id=1, source_target_pairs={{0,8},{4,12},{8,0},{12,4},{16,24},{20,28},{24,16},{28,20},{1,9},{5... | collective-permute-start | bytes 393224 | tf_op jit(solution)/shard_map/ppermute | solution.py:414
  24.1 4.2 %prepare.3.refs_4_.refs_0_ = bf16[8,3,2,64,256]{4,3,2,1,0:T(8,128)(2,1)} custom-call(bf16[1024,512]{1,0:T(8,128)(2,1)} %q_ref.7, bf16[1024,512]{1,0:T(8,128)(2,1)} %k_ref.9, bf16[1024,512]{1,0:T(8,128)(2,1)} %v_ref.9, bf16[2,64,512]{2,1,0:T(8,128)(2,1)} %get-tuple-element.40.refs_0_), custom_call_target="tpu_custom_call" | custom-call | flops 402653184 | bytes 3145728 | tf_op jit(solution)/shard_map/prepare/pallas_call | solution.py:181
  28.4 13.0 %collective-permute-done.2.refs_3_ = bf16[2,64,512]{2,1,0:T(8,128)(2,1)S(1)} collective-permute-done((bf16[2,64,512]{2,1,0:T(8,128)(2,1)}, bf16[2,64,512]{2,1,0:T(8,128)(2,1)S(1)}, u32[]{:S(2)}, u32[]{:S(2)}) %collective-permute-start.2) | collective-permute-done | bytes 131104 | tf_op jit(solution)/shard_map/ppermute | solution.py:414
  41.4 2.2 %collective-permute-done.1.refs_2_ = bf16[2,64,512]{2,1,0:T(8,128)(2,1)S(1)} collective-permute-done((bf16[2,64,512]{2,1,0:T(8,128)(2,1)}, bf16[2,64,512]{2,1,0:T(8,128)(2,1)S(1)}, u32[]{:S(2)}, u32[]{:S(2)}) %collective-permute-start.1) | collective-permute-done | bytes 131104 | tf_op jit(solution)/shard_map/ppermute | solution.py:414
  43.6 0.6 copy-done.16
  44.3 2.0 %collective-permute-start.3 = (bf16[2,512,512]{2,1,0:T(8,128)(2,1)}, bf16[2,512,512]{2,1,0:T(8,128)(2,1)}, u32[]{:S(2)}, u32[]{:S(2)}) collective-permute-start(bf16[2,512,512]{2,1,0:T(8,128)(2,1)} %after.3.refs_1_), channel_id=1, source_target_pairs={{0,4},{4,8},{8,12},{12,16},{16,20},{20,24},{24,28},{1,5},{5,9},{9,... | collective-permute-start | bytes 3145736 | tf_op jit(solution)/shard_map/ppermute | solution.py:480
  46.3 1.6 %collective-permute-start.4 = (bf16[2,64,512]{2,1,0:T(8,128)(2,1)}, bf16[2,64,512]{2,1,0:T(8,128)(2,1)}, u32[]{:S(2)}, u32[]{:S(2)}) collective-permute-start(bf16[2,64,512]{2,1,0:T(8,128)(2,1)} %get-tuple-element.40.refs_0_), channel_id=1, source_target_pairs={{0,4},{4,0},{8,12},{12,8},{16,20},{20,16},{24,28},{28,24},{1,5},{5... | collective-permute-start | bytes 393224 | tf_op jit(solution)/shard_map/ppermute | solution.py:414
  48.5 4.0 %all-to-all-start.1 = ((bf16[8,3,2,64,256]{4,3,2,1,0:T(8,128)(2,1)}), bf16[8,3,2,64,256]{4,3,2,1,0:T(8,128)(2,1)S(1)}, u32[]{:S(2)}, u32[]{:S(2)}) async-start(bf16[8,3,2,64,256]{4,3,2,1,0:T(8,128)(2,1)} %after.4), calls=%async_computation.1 | async-start | bytes 3145728 | tf_op jit(solution)/shard_map/all_to_all | solution.py:512
  52.5 2.4 %stride.2 = (bf16[2,64,256]{2,1,0:T(8,128)(2,1)S(1)}, bf16[2,64,256]{2,1,0:T(8,128)(2,1)S(1)}, bf16[2,64,256]{2,1,0:T(8,128)(2,1)S(1)}, bf16[2,64,256]{2,1,0:T(8...) custom-call(s32[1]{0:T(128)} %bitcast.2.place_ref, ...), custom_call_target="tpu_custom_call" | custom-call | flops 805306368 | bytes 2097152 | tf_op jit(solution)/shard_map/stride/pallas_call | solution.py:302
  55.5 1.4 collective-permute-start.10
  56.8 1.5 %collective-permute-start.11 = (bf16[2,64,256]{2,1,0:T(8,128)(2,1)}, bf16[2,64,256]{2,1,0:T(8,128)(2,1)S(1)}, u32[]{:S(2)}, u32[]{:S(2)}) collective-permute-start(bf16[2,64,256]{2,1,0:T(8,128)(2,1)} %get-tuple-element.47), channel_id=1, source_target_pairs={{0,16},{4,20},{8,24},{12,28},{16,0},{20,4},{24,8},{28,12},{1,17},{... | collective-permute-start | bytes 196616 | tf_op jit(solution)/shard_map/ppermute | solution.py:493
  58.3 8.7 %collective-permute-done.3.rim_ref = bf16[2,512,512]{2,1,0:T(8,128)(2,1)} collective-permute-done((bf16[2,512,512]{2,1,0:T(8,128)(2,1)}, bf16[2,512,512]{2,1,0:T(8,128)(2,1)}, u32[]{:S(2)}, u32[]{:S(2)}) %collective-permute-start.3) | collective-permute-done | bytes 1048608 | tf_op jit(solution)/shard_map/ppermute | solution.py:480
  67.0 7.1 %home.2 = (f32[1024,256]{1,0:T(8,128)}, f32[8,128]{1,0:T(8,128)}) custom-call(s32[1]{0:T(128)} %bitcast.2.place_ref, bf16[1024,512]{1,0:T(8,128)(2,1)} %q_ref.7, bf16[1024,512]{1,0:T(8,128)(2,1)} %k_ref.9, bf16[1024,512]{1,0:T(8,128)(2,1)} %v_ref.9, bf16[2,512,512]{2,1,0:T(8,128)(2,1)} %collective-permute-done.3.rim_ref, ...), custom_call_target="tpu_custom_call" | custom-call | flops 21474836480 | bytes 7340032 | tf_op jit(solution)/shard_map/home/pallas_call | solution.py:248
  74.1 2.0 %collective-permute-start.13 = (bf16[2,64,256]{2,1,0:T(8,128)(2,1)S(1)}, bf16[2,64,256]{2,1,0:T(8,128)(2,1)S(1)}, u32[]{:S(2)}, u32[]{:S(2)}) collective-permute-start(bf16[2,64,256]{2,1,0:T(8,128)(2,1)S(1)} %get-tuple-element.49), channel_id=1, source_target_pairs={{0,24},{4,28},{8,16},{12,20},{16,8},{20,12},{24,0},{28,4},{1,25},{... | collective-permute-start | bytes 196616 | tf_op jit(solution)/shard_map/ppermute | solution.py:493
  76.1 3.6 %collective-permute-start.14 = (bf16[2,64,256]{2,1,0:T(8,128)(2,1)S(1)}, bf16[2,64,256]{2,1,0:T(8,128)(2,1)S(1)}, u32[]{:S(2)}, u32[]{:S(2)}) collective-permute-start(bf16[2,64,256]{2,1,0:T(8,128)(2,1)S(1)} %get-tuple-element.50), channel_id=1, source_target_pairs={{0,28},{4,24},{8,20},{12,16},{16,12},{20,8},{24,4},{28,0},{1,29},{... | collective-permute-start | bytes 196616 | tf_op jit(solution)/shard_map/ppermute | solution.py:493
  79.7 0.7 copy-done.10
  80.4 1.8 %stride.3 = (bf16[2,64,256]{2,1,0:T(8,128)(2,1)S(1)}, bf16[2,64,256]{2,1,0:T(8,128)(2,1)S(1)}, bf16[2,64,256]{2,1,0:T(8,128)(2,1)S(1)}, bf16[2,64,256]{2,1,0:T(8...) custom-call(s32[1]{0:T(128)} %bitcast.2.place_ref, ...), custom_call_target="tpu_custom_call" | custom-call | flops 805306368 | bytes 2097152 | tf_op jit(solution)/shard_map/stride/pallas_call | solution.py:302
  82.2 0.9 collective-permute-start.18
  83.1 1.8 %collective-permute-start.19 = (bf16[2,64,256]{2,1,0:T(8,128)(2,1)S(1)}, bf16[2,64,256]{2,1,0:T(8,128)(2,1)S(1)}, u32[]{:S(2)}, u32[]{:S(2)}) collective-permute-start(bf16[2,64,256]{2,1,0:T(8,128)(2,1)S(1)} %get-tuple-element.61), channel_id=1, source_target_pairs={{0,8},{4,12},{8,0},{12,4},{16,24},{20,28},{24,16},{28,20},{1,9},{5... | collective-permute-start | bytes 196616 | tf_op jit(solution)/shard_map/ppermute | solution.py:493
  85.0 2.6 %collective-permute-start.21 = (bf16[2,64,256]{2,1,0:T(8,128)(2,1)S(1)}, bf16[2,64,256]{2,1,0:T(8,128)(2,1)S(1)}, u32[]{:S(2)}, u32[]{:S(2)}) collective-permute-start(bf16[2,64,256]{2,1,0:T(8,128)(2,1)S(1)} %get-tuple-element.63), channel_id=1, source_target_pairs={{0,16},{4,20},{8,24},{12,28},{16,0},{20,4},{24,8},{28,12},{1,17},{... | collective-permute-start | bytes 196616 | tf_op jit(solution)/shard_map/ppermute | solution.py:493
  87.7 0.8 combine.2
  88.6 0.7 copy-done.5
  89.3 1.5 %collective-permute-start.23 = (bf16[2,64,256]{2,1,0:T(8,128)(2,1)S(1)}, bf16[2,64,256]{2,1,0:T(8,128)(2,1)S(1)}, u32[]{:S(2)}, u32[]{:S(2)}) collective-permute-start(bf16[2,64,256]{2,1,0:T(8,128)(2,1)S(1)} %get-tuple-element.65), channel_id=1, source_target_pairs={{0,24},{4,28},{8,16},{12,20},{16,8},{20,12},{24,0},{28,4},{1,25},{... | collective-permute-start | bytes 196616 | tf_op jit(solution)/shard_map/ppermute | solution.py:493
  90.8 0.9 collective-permute-start.24
  91.7 0.5 collective-permute-start.15
  92.1 2.6 %collective-permute-start.16 = (bf16[256,256]{1,0:T(8,128)(2,1)S(1)}, bf16[256,256]{1,0:T(8,128)(2,1)S(1)}, u32[]{:S(2)}, u32[]{:S(2)}) collective-permute-start(bf16[256,256]{1,0:T(8,128)(2,1)S(1)} %get-tuple-element.55), channel_id=1, source_target_pairs={{0,2},{1,3},{2,0},{3,1},{4,6},{5,7},{6,4},{7,5},{8,10},{9,11},{10,... | collective-permute-start | bytes 393224 | tf_op jit(solution)/shard_map/ppermute | solution.py:493
  94.7 0.4 collective-permute-start.17
  95.2 7.1 %home.3 = (f32[1024,256]{1,0:T(8,128)}, f32[8,128]{1,0:T(8,128)}) custom-call(s32[1]{0:T(128)} %bitcast.2.place_ref, bf16[1024,512]{1,0:T(8,128)(2,1)} %q_ref.7, bf16[1024,512]{1,0:T(8,128)(2,1)} %k_ref.9, bf16[1024,512]{1,0:T(8,128)(2,1)} %v_ref.9, bf16[2,512,512]{2,1,0:T(8,128)(2,1)} %collective-permute-done.3.rim_ref, ...), custom_call_target="tpu_custom_call" | custom-call | flops 21474836480 | bytes 7340032 | tf_op jit(solution)/shard_map/home/pallas_call | solution.py:248
  102.3 1.9 %collective-permute-done.16.refs_10_.refs_2_ = bf16[256,256]{1,0:T(8,128)(2,1)S(1)} collective-permute-done((bf16[256,256]{1,0:T(8,128)(2,1)S(1)}, bf16[256,256]{1,0:T(8,128)(2,1)S(1)}, u32[]{:S(2)}, u32[]{:S(2)}) %collective-permute-start.16) | collective-permute-done | bytes 131104 | tf_op jit(solution)/shard_map/ppermute | solution.py:493
  104.2 3.2 %collective-permute-done.17.refs_11_.refs_3_ = bf16[256,256]{1,0:T(8,128)(2,1)S(1)} collective-permute-done((bf16[256,256]{1,0:T(8,128)(2,1)S(1)}, bf16[256,256]{1,0:T(8,128)(2,1)S(1)}, u32[]{:S(2)}, u32[]{:S(2)}) %collective-permute-start.17) | collective-permute-done | bytes 131104 | tf_op jit(solution)/shard_map/ppermute | solution.py:493
  107.4 1.3 copy-done.1
  108.6 0.7 copy-done.7
  109.3 0.8 combine.3
  110.2 0.6 copy-done.6
  110.8 0.6 copy-done.8
  111.6 3.0 %collective-permute-start.26 = (bf16[256,256]{1,0:T(8,128)(2,1)S(1)}, bf16[256,256]{1,0:T(8,128)(2,1)S(1)}, u32[]{:S(2)}, u32[]{:S(2)}) collective-permute-start(bf16[256,256]{1,0:T(8,128)(2,1)S(1)} %get-tuple-element.70), channel_id=1, source_target_pairs={{0,2},{1,3},{2,0},{3,1},{4,6},{5,7},{6,4},{7,5},{8,10},{9,11},{10,... | collective-permute-start | bytes 393224 | tf_op jit(solution)/shard_map/ppermute | solution.py:493
  114.6 0.5 collective-permute-start.27
  115.1 2.8 %collective-permute-done.25.refs_5_ = bf16[256,256]{1,0:T(8,128)(2,1)S(1)} collective-permute-done((bf16[256,256]{1,0:T(8,128)(2,1)S(1)}, bf16[256,256]{1,0:T(8,128)(2,1)S(1)}, u32[]{:S(2)}, u32[]{:S(2)}) %collective-permute-start.25) | collective-permute-done | bytes 131104 | tf_op jit(solution)/shard_map/ppermute | solution.py:493
  117.9 6.3 %collective-permute-done.26.refs_6_ = bf16[256,256]{1,0:T(8,128)(2,1)S(1)} collective-permute-done((bf16[256,256]{1,0:T(8,128)(2,1)S(1)}, bf16[256,256]{1,0:T(8,128)(2,1)S(1)}, u32[]{:S(2)}, u32[]{:S(2)}) %collective-permute-start.26) | collective-permute-done | bytes 131104 | tf_op jit(solution)/shard_map/ppermute | solution.py:493
  124.1 2.9 %collective-permute-done.27.refs_7_ = bf16[256,256]{1,0:T(8,128)(2,1)S(1)} collective-permute-done((bf16[256,256]{1,0:T(8,128)(2,1)S(1)}, bf16[256,256]{1,0:T(8,128)(2,1)S(1)}, u32[]{:S(2)}, u32[]{:S(2)}) %collective-permute-start.27) | collective-permute-done | bytes 131104 | tf_op jit(solution)/shard_map/ppermute | solution.py:493
  127.1 0.6 copy-done.14
  127.8 9.6 %project.1 = bf16[256,2048]{1,0:T(8,128)(2,1)} custom-call(s32[2]{0:T(128)} %pad_add_fusion.side_ref, bf16[256,256]{1,0:T(8,128)(2,1)} %copy-done.5, bf16[256,256]{1,0:T(8,128)(2,1)} %copy-done.2, bf16[256,256]{1,0:T(8,128)(2,1)} %copy-done.3, bf16[256,256]{1,0:T(8,128)(2,1)} %copy-done.4, bf16[256,256]{1,0:T(8,128)(2,1)} %copy-done.6, ...), custom_call_target="tpu_custom_call" | custom-call | flops 2147483648 | bytes 9437184 | tf_op jit(solution)/shard_map/project/pallas_call | solution.py:387
  (69 shorter events, 1.8 us)
Async XLA Ops:
  6.5 104.9 %all-gather.3.cloned.1.call-start = ((), (), s32[]{:S(2)}) async-start(), calls=%async_computation.2 | async-start | bytes 5242880 | tf_op jit(solution)/shard_map/all_gather | solution.py:471
  14.2 34.3 %all-to-all-start = ((bf16[8,3,2,64,256]{4,3,2,1,0:T(8,128)(2,1)}), bf16[8,3,2,64,256]{4,3,2,1,0:T(8,128)(2,1)S(1)}, u32[]{:S(2)}, u32[]{:S(2)}) async-start(bf16[8,3,2,64,256]{4,3,2,1,0:T(8,128)(2,1)} %prepare.2.refs_0_), calls=%async_computation | async-start | bytes 3145728 | tf_op jit(solution)/shard_map/all_to_all | solution.py:512
  20.6 20.8 %collective-permute-start.2 = (bf16[2,64,512]{2,1,0:T(8,128)(2,1)}, bf16[2,64,512]{2,1,0:T(8,128)(2,1)S(1)}, u32[]{:S(2)}, u32[]{:S(2)}) collective-permute-start(bf16[2,64,512]{2,1,0:T(8,128)(2,1)} %get-tuple-element.40.refs_0_), channel_id=1, source_target_pairs={{0,24},{4,28},{8,16},{12,20},{16,8},{20,12},{24,0},{28,4},{1,25},{... | collective-permute-start | bytes 393224 | tf_op jit(solution)/shard_map/ppermute | solution.py:414
  22.1 21.5 %collective-permute-start.1 = (bf16[2,64,512]{2,1,0:T(8,128)(2,1)}, bf16[2,64,512]{2,1,0:T(8,128)(2,1)S(1)}, u32[]{:S(2)}, u32[]{:S(2)}) collective-permute-start(bf16[2,64,512]{2,1,0:T(8,128)(2,1)} %get-tuple-element.40.refs_0_), channel_id=1, source_target_pairs={{0,16},{4,20},{8,24},{12,28},{16,0},{20,4},{24,8},{28,12},{1,17},{... | collective-permute-start | bytes 393224 | tf_op jit(solution)/shard_map/ppermute | solution.py:414
  22.2 21.4 %collective-permute-start = (bf16[2,64,512]{2,1,0:T(8,128)(2,1)}, bf16[2,64,512]{2,1,0:T(8,128)(2,1)S(1)}, u32[]{:S(2)}, u32[]{:S(2)}) collective-permute-start(bf16[2,64,512]{2,1,0:T(8,128)(2,1)} %get-tuple-element.40.refs_0_), channel_id=1, source_target_pairs={{0,8},{4,12},{8,0},{12,4},{16,24},{20,28},{24,16},{28,20},{1,9},{5... | collective-permute-start | bytes 393224 | tf_op jit(solution)/shard_map/ppermute | solution.py:414
  41.4 2.2 %copy-start.15 = (bf16[2,64,512]{2,1,0:T(8,128)(2,1)}, bf16[2,64,512]{2,1,0:T(8,128)(2,1)S(1)}, u32[]{:S(2)}) copy-start(bf16[2,64,512]{2,1,0:T(8,128)(2,1)S(1)} %collective-permute-done.2.refs_3_) | copy-start | bytes 393220
  43.6 0.7 copy-start.17
  44.3 22.7 %collective-permute-start.3 = (bf16[2,512,512]{2,1,0:T(8,128)(2,1)}, bf16[2,512,512]{2,1,0:T(8,128)(2,1)}, u32[]{:S(2)}, u32[]{:S(2)}) collective-permute-start(bf16[2,512,512]{2,1,0:T(8,128)(2,1)} %after.3.refs_1_), channel_id=1, source_target_pairs={{0,4},{4,8},{8,12},{12,16},{16,20},{20,24},{24,28},{1,5},{5,9},{9,... | collective-permute-start | bytes 3145736 | tf_op jit(solution)/shard_map/ppermute | solution.py:480
  46.3 8.6 %collective-permute-start.4 = (bf16[2,64,512]{2,1,0:T(8,128)(2,1)}, bf16[2,64,512]{2,1,0:T(8,128)(2,1)}, u32[]{:S(2)}, u32[]{:S(2)}) collective-permute-start(bf16[2,64,512]{2,1,0:T(8,128)(2,1)} %get-tuple-element.40.refs_0_), channel_id=1, source_target_pairs={{0,4},{4,0},{8,12},{12,8},{16,20},{20,16},{24,28},{28,24},{1,5},{5... | collective-permute-start | bytes 393224 | tf_op jit(solution)/shard_map/ppermute | solution.py:414
  47.9 7.2 %collective-permute-start.7 = (bf16[2,64,512]{2,1,0:T(8,128)(2,1)}, bf16[2,64,512]{2,1,0:T(8,128)(2,1)}, u32[]{:S(2)}, u32[]{:S(2)}) collective-permute-start(bf16[2,64,512]{2,1,0:T(8,128)(2,1)} %copy-done.15), channel_id=1, source_target_pairs={{0,4},{4,0},{8,12},{12,8},{16,20},{20,16},{24,28},{28,24},{1,5},{5... | collective-permute-start | bytes 393224 | tf_op jit(solution)/shard_map/ppermute | solution.py:414
  48.0 7.5 %collective-permute-start.6 = (bf16[2,64,512]{2,1,0:T(8,128)(2,1)}, bf16[2,64,512]{2,1,0:T(8,128)(2,1)}, u32[]{:S(2)}, u32[]{:S(2)}) collective-permute-start(bf16[2,64,512]{2,1,0:T(8,128)(2,1)} %copy-done.16), channel_id=1, source_target_pairs={{0,4},{4,0},{8,12},{12,8},{16,20},{20,16},{24,28},{28,24},{1,5},{5... | collective-permute-start | bytes 393224 | tf_op jit(solution)/shard_map/ppermute | solution.py:414
  48.4 8.4 %collective-permute-start.5 = (bf16[2,64,512]{2,1,0:T(8,128)(2,1)}, bf16[2,64,512]{2,1,0:T(8,128)(2,1)}, u32[]{:S(2)}, u32[]{:S(2)}) collective-permute-start(bf16[2,64,512]{2,1,0:T(8,128)(2,1)} %copy-done.17), channel_id=1, source_target_pairs={{0,4},{4,0},{8,12},{12,8},{16,20},{20,16},{24,28},{28,24},{1,5},{5... | collective-permute-start | bytes 393224 | tf_op jit(solution)/shard_map/ppermute | solution.py:414
  48.5 31.2 %all-to-all-start.1 = ((bf16[8,3,2,64,256]{4,3,2,1,0:T(8,128)(2,1)}), bf16[8,3,2,64,256]{4,3,2,1,0:T(8,128)(2,1)S(1)}, u32[]{:S(2)}, u32[]{:S(2)}) async-start(bf16[8,3,2,64,256]{4,3,2,1,0:T(8,128)(2,1)} %after.4), calls=%async_computation.1 | async-start | bytes 3145728 | tf_op jit(solution)/shard_map/all_to_all | solution.py:512
  54.9 12.1 %copy-start.11 = (f32[8,128]{1,0:T(8,128)}, f32[8,128]{1,0:T(8,128)S(1)}, u32[]{:S(2)}) copy-start(f32[8,128]{1,0:T(8,128)S(1)} %get-tuple-element.41.refs_8_) | copy-start | bytes 12292
  54.9 19.2 %collective-permute-start.8 = (bf16[2,64,256]{2,1,0:T(8,128)(2,1)S(1)}, bf16[2,64,256]{2,1,0:T(8,128)(2,1)S(1)}, u32[]{:S(2)}, u32[]{:S(2)}) collective-permute-start(bf16[2,64,256]{2,1,0:T(8,128)(2,1)S(1)} %get-tuple-element.44), channel_id=1, source_target_pairs={{0,4},{4,0},{8,12},{12,8},{16,20},{20,16},{24,28},{28,24},{1,5},{5... | collective-permute-start | bytes 196616 | tf_op jit(solution)/shard_map/ppermute | solution.py:493
  55.1 21.0 %collective-permute-start.9 = (bf16[2,64,256]{2,1,0:T(8,128)(2,1)S(1)}, bf16[2,64,256]{2,1,0:T(8,128)(2,1)S(1)}, u32[]{:S(2)}, u32[]{:S(2)}) collective-permute-start(bf16[2,64,256]{2,1,0:T(8,128)(2,1)S(1)} %get-tuple-element.45), channel_id=1, source_target_pairs={{0,8},{4,12},{8,0},{12,4},{16,24},{20,28},{24,16},{28,20},{1,9},{5... | collective-permute-start | bytes 196616 | tf_op jit(solution)/shard_map/ppermute | solution.py:493
  55.5 26.7 %collective-permute-start.10 = (bf16[2,64,256]{2,1,0:T(8,128)(2,1)}, bf16[2,64,256]{2,1,0:T(8,128)(2,1)S(1)}, u32[]{:S(2)}, u32[]{:S(2)}) collective-permute-start(bf16[2,64,256]{2,1,0:T(8,128)(2,1)} %get-tuple-element.46), channel_id=1, source_target_pairs={{0,12},{4,8},{8,4},{12,0},{16,28},{20,24},{24,20},{28,16},{1,13},{... | collective-permute-start | bytes 196616 | tf_op jit(solution)/shard_map/ppermute | solution.py:493
  56.8 26.2 %collective-permute-start.11 = (bf16[2,64,256]{2,1,0:T(8,128)(2,1)}, bf16[2,64,256]{2,1,0:T(8,128)(2,1)S(1)}, u32[]{:S(2)}, u32[]{:S(2)}) collective-permute-start(bf16[2,64,256]{2,1,0:T(8,128)(2,1)} %get-tuple-element.47), channel_id=1, source_target_pairs={{0,16},{4,20},{8,24},{12,28},{16,0},{20,4},{24,8},{28,12},{1,17},{... | collective-permute-start | bytes 196616 | tf_op jit(solution)/shard_map/ppermute | solution.py:493
  67.0 17.9 %collective-permute-start.12 = (bf16[2,64,256]{2,1,0:T(8,128)(2,1)S(1)}, bf16[2,64,256]{2,1,0:T(8,128)(2,1)S(1)}, u32[]{:S(2)}, u32[]{:S(2)}) collective-permute-start(bf16[2,64,256]{2,1,0:T(8,128)(2,1)S(1)} %get-tuple-element.48), channel_id=1, source_target_pairs={{0,20},{4,16},{8,28},{12,24},{16,4},{20,0},{24,12},{28,8},{1,21},{... | collective-permute-start | bytes 196616 | tf_op jit(solution)/shard_map/ppermute | solution.py:493
  74.1 13.7 %copy-start = (f32[1024,256]{1,0:T(8,128)S(1)}, f32[1024,256]{1,0:T(8,128)}, u32[]{:S(2)}) copy-start(f32[1024,256]{1,0:T(8,128)} %get-tuple-element.42.home_ref) | copy-start | bytes 3145732
  74.1 10.9 %collective-permute-start.13 = (bf16[2,64,256]{2,1,0:T(8,128)(2,1)S(1)}, bf16[2,64,256]{2,1,0:T(8,128)(2,1)S(1)}, u32[]{:S(2)}, u32[]{:S(2)}) collective-permute-start(bf16[2,64,256]{2,1,0:T(8,128)(2,1)S(1)} %get-tuple-element.49), channel_id=1, source_target_pairs={{0,24},{4,28},{8,16},{12,20},{16,8},{20,12},{24,0},{28,4},{1,25},{... | collective-permute-start | bytes 196616 | tf_op jit(solution)/shard_map/ppermute | solution.py:493
  76.1 11.5 %collective-permute-start.14 = (bf16[2,64,256]{2,1,0:T(8,128)(2,1)S(1)}, bf16[2,64,256]{2,1,0:T(8,128)(2,1)S(1)}, u32[]{:S(2)}, u32[]{:S(2)}) collective-permute-start(bf16[2,64,256]{2,1,0:T(8,128)(2,1)S(1)} %get-tuple-element.50), channel_id=1, source_target_pairs={{0,28},{4,24},{8,20},{12,16},{16,12},{20,8},{24,4},{28,0},{1,29},{... | collective-permute-start | bytes 196616 | tf_op jit(solution)/shard_map/ppermute | solution.py:493
  79.7 0.7 copy-start.10
  82.2 7.1 %collective-permute-start.18 = (bf16[2,64,256]{2,1,0:T(8,128)(2,1)S(1)}, bf16[2,64,256]{2,1,0:T(8,128)(2,1)S(1)}, u32[]{:S(2)}, u32[]{:S(2)}) collective-permute-start(bf16[2,64,256]{2,1,0:T(8,128)(2,1)S(1)} %get-tuple-element.60), channel_id=1, source_target_pairs={{0,4},{4,0},{8,12},{12,8},{16,20},{20,16},{24,28},{28,24},{1,5},{5... | collective-permute-start | bytes 196616 | tf_op jit(solution)/shard_map/ppermute | solution.py:493
  83.1 7.7 %collective-permute-start.19 = (bf16[2,64,256]{2,1,0:T(8,128)(2,1)S(1)}, bf16[2,64,256]{2,1,0:T(8,128)(2,1)S(1)}, u32[]{:S(2)}, u32[]{:S(2)}) collective-permute-start(bf16[2,64,256]{2,1,0:T(8,128)(2,1)S(1)} %get-tuple-element.61), channel_id=1, source_target_pairs={{0,8},{4,12},{8,0},{12,4},{16,24},{20,28},{24,16},{28,20},{1,9},{5... | collective-permute-start | bytes 196616 | tf_op jit(solution)/shard_map/ppermute | solution.py:493
  84.9 6.8 %collective-permute-start.20 = (bf16[2,64,256]{2,1,0:T(8,128)(2,1)S(1)}, bf16[2,64,256]{2,1,0:T(8,128)(2,1)S(1)}, u32[]{:S(2)}, u32[]{:S(2)}) collective-permute-start(bf16[2,64,256]{2,1,0:T(8,128)(2,1)S(1)} %get-tuple-element.62), channel_id=1, source_target_pairs={{0,12},{4,8},{8,4},{12,0},{16,28},{20,24},{24,20},{28,16},{1,13},{... | collective-permute-start | bytes 196616 | tf_op jit(solution)/shard_map/ppermute | solution.py:493
  85.0 7.1 %collective-permute-start.21 = (bf16[2,64,256]{2,1,0:T(8,128)(2,1)S(1)}, bf16[2,64,256]{2,1,0:T(8,128)(2,1)S(1)}, u32[]{:S(2)}, u32[]{:S(2)}) collective-permute-start(bf16[2,64,256]{2,1,0:T(8,128)(2,1)S(1)} %get-tuple-element.63), channel_id=1, source_target_pairs={{0,16},{4,20},{8,24},{12,28},{16,0},{20,4},{24,8},{28,12},{1,17},{... | collective-permute-start | bytes 196616 | tf_op jit(solution)/shard_map/ppermute | solution.py:493
  87.6 7.1 %collective-permute-start.22 = (bf16[2,64,256]{2,1,0:T(8,128)(2,1)S(1)}, bf16[2,64,256]{2,1,0:T(8,128)(2,1)S(1)}, u32[]{:S(2)}, u32[]{:S(2)}) collective-permute-start(bf16[2,64,256]{2,1,0:T(8,128)(2,1)S(1)} %get-tuple-element.64), channel_id=1, source_target_pairs={{0,20},{4,16},{8,28},{12,24},{16,4},{20,0},{24,12},{28,8},{1,21},{... | collective-permute-start | bytes 196616 | tf_op jit(solution)/shard_map/ppermute | solution.py:493
  88.6 0.7 copy-start.5
  89.3 5.9 %copy-start.9 = (f32[8,128]{1,0:T(8,128)}, f32[8,128]{1,0:T(8,128)S(1)}, u32[]{:S(2)}) copy-start(f32[8,128]{1,0:T(8,128)S(1)} %get-tuple-element.57.refs_8_) | copy-start | bytes 12292
  89.3 13.0 %collective-permute-start.23 = (bf16[2,64,256]{2,1,0:T(8,128)(2,1)S(1)}, bf16[2,64,256]{2,1,0:T(8,128)(2,1)S(1)}, u32[]{:S(2)}, u32[]{:S(2)}) collective-permute-start(bf16[2,64,256]{2,1,0:T(8,128)(2,1)S(1)} %get-tuple-element.65), channel_id=1, source_target_pairs={{0,24},{4,28},{8,16},{12,20},{16,8},{20,12},{24,0},{28,4},{1,25},{... | collective-permute-start | bytes 196616 | tf_op jit(solution)/shard_map/ppermute | solution.py:493
  90.8 11.5 %collective-permute-start.24 = (bf16[2,64,256]{2,1,0:T(8,128)(2,1)S(1)}, bf16[2,64,256]{2,1,0:T(8,128)(2,1)S(1)}, u32[]{:S(2)}, u32[]{:S(2)}) collective-permute-start(bf16[2,64,256]{2,1,0:T(8,128)(2,1)S(1)} %get-tuple-element.66), channel_id=1, source_target_pairs={{0,28},{4,24},{8,20},{12,16},{16,12},{20,8},{24,4},{28,0},{1,29},{... | collective-permute-start | bytes 196616 | tf_op jit(solution)/shard_map/ppermute | solution.py:493
  91.7 10.6 %collective-permute-start.15 = (bf16[256,256]{1,0:T(8,128)(2,1)S(1)}, bf16[256,256]{1,0:T(8,128)(2,1)S(1)}, u32[]{:S(2)}, u32[]{:S(2)}) collective-permute-start(bf16[256,256]{1,0:T(8,128)(2,1)S(1)} %get-tuple-element.54), channel_id=1, source_target_pairs={{0,1},{1,0},{2,3},{3,2},{4,5},{5,4},{6,7},{7,6},{8,9},{9,8},{10,11... | collective-permute-start | bytes 393224 | tf_op jit(solution)/shard_map/ppermute | solution.py:493
  92.1 12.1 %collective-permute-start.16 = (bf16[256,256]{1,0:T(8,128)(2,1)S(1)}, bf16[256,256]{1,0:T(8,128)(2,1)S(1)}, u32[]{:S(2)}, u32[]{:S(2)}) collective-permute-start(bf16[256,256]{1,0:T(8,128)(2,1)S(1)} %get-tuple-element.55), channel_id=1, source_target_pairs={{0,2},{1,3},{2,0},{3,1},{4,6},{5,7},{6,4},{7,5},{8,10},{9,11},{10,... | collective-permute-start | bytes 393224 | tf_op jit(solution)/shard_map/ppermute | solution.py:493
  94.7 12.6 %collective-permute-start.17 = (bf16[256,256]{1,0:T(8,128)(2,1)S(1)}, bf16[256,256]{1,0:T(8,128)(2,1)S(1)}, u32[]{:S(2)}, u32[]{:S(2)}) collective-permute-start(bf16[256,256]{1,0:T(8,128)(2,1)S(1)} %get-tuple-element.56), channel_id=1, source_target_pairs={{0,3},{1,2},{2,1},{3,0},{4,7},{5,6},{6,5},{7,4},{8,11},{9,10},{10,... | collective-permute-start | bytes 393224 | tf_op jit(solution)/shard_map/ppermute | solution.py:493
  102.3 9.2 %copy-start.2 = (bf16[256,256]{1,0:T(8,128)(2,1)}, bf16[256,256]{1,0:T(8,128)(2,1)S(1)}, u32[]{:S(2)}) copy-start(bf16[256,256]{1,0:T(8,128)(2,1)S(1)} %collective-permute-done.15.refs_9_.refs_1_) | copy-start | bytes 393220
  104.2 7.2 %copy-start.3 = (bf16[256,256]{1,0:T(8,128)(2,1)}, bf16[256,256]{1,0:T(8,128)(2,1)S(1)}, u32[]{:S(2)}) copy-start(bf16[256,256]{1,0:T(8,128)(2,1)S(1)} %collective-permute-done.16.refs_10_.refs_2_) | copy-start | bytes 393220
  107.4 4.1 %copy-start.4 = (bf16[256,256]{1,0:T(8,128)(2,1)}, bf16[256,256]{1,0:T(8,128)(2,1)S(1)}, u32[]{:S(2)}) copy-start(bf16[256,256]{1,0:T(8,128)(2,1)S(1)} %collective-permute-done.17.refs_11_.refs_3_) | copy-start | bytes 393220
  107.4 1.3 copy-start.1
  108.6 0.7 copy-start.7
  110.2 0.7 copy-start.6
  111.4 15.7 %collective-permute-start.28 = (bf16[4,512,1024]{2,1,0:T(8,128)(2,1)}, bf16[4,512,1024]{2,1,0:T(8,128)(2,1)}, u32[]{:S(2)}, u32[]{:S(2)}) collective-permute-start(bf16[4,512,1024]{2,1,0:T(8,128)(2,1)} %after.5.refs_8_), channel_id=1, source_target_pairs={{0,4},{4,0},{8,12},{12,8},{16,20},{20,16},{24,28},{28,24},{1,5},{5... | collective-permute-start | bytes 12582920 | tf_op jit(solution)/shard_map/ppermute | solution.py:527
  111.5 6.4 %collective-permute-start.25 = (bf16[256,256]{1,0:T(8,128)(2,1)S(1)}, bf16[256,256]{1,0:T(8,128)(2,1)S(1)}, u32[]{:S(2)}, u32[]{:S(2)}) collective-permute-start(bf16[256,256]{1,0:T(8,128)(2,1)S(1)} %get-tuple-element.69), channel_id=1, source_target_pairs={{0,1},{1,0},{2,3},{3,2},{4,5},{5,4},{6,7},{7,6},{8,9},{9,8},{10,11... | collective-permute-start | bytes 393224 | tf_op jit(solution)/shard_map/ppermute | solution.py:493
  111.6 12.5 %collective-permute-start.26 = (bf16[256,256]{1,0:T(8,128)(2,1)S(1)}, bf16[256,256]{1,0:T(8,128)(2,1)S(1)}, u32[]{:S(2)}, u32[]{:S(2)}) collective-permute-start(bf16[256,256]{1,0:T(8,128)(2,1)S(1)} %get-tuple-element.70), channel_id=1, source_target_pairs={{0,2},{1,3},{2,0},{3,1},{4,6},{5,7},{6,4},{7,5},{8,10},{9,11},{10,... | collective-permute-start | bytes 393224 | tf_op jit(solution)/shard_map/ppermute | solution.py:493
  114.6 12.5 %collective-permute-start.27 = (bf16[256,256]{1,0:T(8,128)(2,1)S(1)}, bf16[256,256]{1,0:T(8,128)(2,1)S(1)}, u32[]{:S(2)}, u32[]{:S(2)}) collective-permute-start(bf16[256,256]{1,0:T(8,128)(2,1)S(1)} %get-tuple-element.71), channel_id=1, source_target_pairs={{0,3},{1,2},{2,1},{3,0},{4,7},{5,6},{6,5},{7,4},{8,11},{9,10},{10,... | collective-permute-start | bytes 393224 | tf_op jit(solution)/shard_map/ppermute | solution.py:493
  117.9 9.2 %copy-start.12 = (bf16[256,256]{1,0:T(8,128)(2,1)}, bf16[256,256]{1,0:T(8,128)(2,1)S(1)}, u32[]{:S(2)}) copy-start(bf16[256,256]{1,0:T(8,128)(2,1)S(1)} %collective-permute-done.25.refs_5_) | copy-start | bytes 393220
  124.1 3.0 %copy-start.13 = (bf16[256,256]{1,0:T(8,128)(2,1)}, bf16[256,256]{1,0:T(8,128)(2,1)S(1)}, u32[]{:S(2)}) copy-start(bf16[256,256]{1,0:T(8,128)(2,1)S(1)} %collective-permute-done.26.refs_6_) | copy-start | bytes 393220
  127.1 0.7 copy-start.14
  (2 other events, 1.2 us)
Sparse Core Ops, SparseCore 0:
  14.3 79.4 all-gather.2

commit v7 on v6

--- a/solution.py
+++ b/solution.py
@@ -355,33 +355,38 @@
 
 
 def project_kernel(side_ref, *refs, slots, chunks):
-    moved_refs, (mine_ref, other_ref, o_ref) = refs[: slots * chunks], refs[slots * chunks :]
-    width = moved_refs[0].shape[1]
-
-    def add_up(weight_ref):
-        total = None
+    moved_refs = refs[: slots * chunks]
+    mine_ref, other_ref, o_ref, rows_ref = refs[slots * chunks :]
+    part = moved_refs[0].shape[1]
+    first = (pl.program_id(0) == 0) & (pl.program_id(1) == 0)
+
+    @pl.when(first)
+    def _():
         for slot in range(slots):
             group = partner(side_ref[1], slot, slots)
             for chunk in range(chunks):
-                rows = weight_ref[group, chunk * width : (chunk + 1) * width]
-                part = dot(moved_refs[chunk * slots + slot][...], rows)
-                total = part if total is None else total + part
-        o_ref[...] = total.astype(BF16)
+                here = pl.ds(pl.multiple_of((group * chunks + chunk) * part, part), part)
+                rows_ref[:, here] = moved_refs[chunk * slots + slot][...]
+
+    def multiply(weight_ref):
+        groups, width, tile = weight_ref.shape
+        weight = weight_ref[...].reshape(groups * width, tile)
+        o_ref[...] = dot(rows_ref[...], weight).astype(BF16)
 
     @pl.when(pl.program_id(0) == 0)
     def _():
-        add_up(mine_ref)
+        multiply(mine_ref)
 
     @pl.when(pl.program_id(0) == 1)
     def _():
-        add_up(other_ref)
+        multiply(other_ref)
 
 
 def project(side, moved, mine, other):
     chunks, slots = len(moved), len(moved[0])
     tokens, part = moved[0][0].shape
     width, half = mine.shape[1:]
-    tile = min(half, 256)
+    tile = min(half, 512)
     tiles = half // tile
     block = (slots, width, tile)
     return pl.pallas_call(
@@ -397,9 +402,10 @@
             out_specs=pl.BlockSpec(
                 (tokens, tile), lambda s, j, side: (0, (s ^ side[0]) * tiles + j)
             ),
+            scratch_shapes=[pltpu.VMEM((tokens, slots * width), BF16)],
         ),
         out_shape=jax.ShapeDtypeStruct((tokens, 2 * half), BF16),
-        compiler_params=params(60),
+        compiler_params=params(24),
         cost_estimate=cost(
             4 * slots * tokens * width * half, 2 * slots * width * (2 * half + tokens)
         ),
@@ -465,20 +471,21 @@
     seat = lax.axis_index("head").astype(jnp.int32)
     sides = jnp.stack([side.astype(jnp.int32), seat])
 
-    sends = []
-    if ctx <= STRIDE:
-        sends.append(prepare(queries, keys, values, ctx, 0, chunks, ()))
-    mine = lax.all_gather(half_of(sides, out_weight, sends), "head", axis=0)
-    rim, picked = edges(keys, values, sends)
+    rim, picked = edges(keys, values, ())
     between, within, order = gather_ctx(picked)
     summary = between + within
+    weight_half = half_of(sides, out_weight, (picked,))
+    mine = lax.all_gather(weight_half, "head", axis=0)
     if ctx > STRIDE:
         stride_out = stride_general(queries, keys, values)
+        sends = []
+    else:
+        sends = [prepare(queries, keys, values, ctx, 0, chunks, (weight_half,))]
+    rim = after(rim, (*between[1:], *sends))
+    sends = [after(send, (rim,)) for send in sends]
+    before = lax.ppermute(rim, "ctx", [(i, i + 1) for i in range(ctx - 1)])
     for chunk in range(len(sends), chunks * len(sends)):
-        sends.append(prepare(queries, keys, values, ctx, chunk, chunks, (picked,)))
-    rim = after(rim, (*between[1:], *sends[1:]))
-    before = lax.ppermute(rim, "ctx", [(i, i + 1) for i in range(ctx - 1)])
-    sends[1:] = [after(send, (rim,)) for send in sends[1:]]
+        sends.append(prepare(queries, keys, values, ctx, chunk, chunks, within[-1:]))
 
     def home(chunk, waits):
         return home_sections(
@@ -505,24 +512,23 @@
             waits = (mark,)
     else:
         seats = jnp.stack([seat, place.astype(jnp.int32)])
-        arrived = ()
-        for chunk in range(chunks + 1):
-            if chunk < chunks:
-                send = sends[chunk]
-                received = lax.all_to_all(send, "ctx", split_axis=0, concat_axis=0, tiled=True)
-                *slabs, mark = stride_attend(place_word, received, waits)
-                backs = exchange(slabs, "ctx")
+        seats = jnp.stack([seat, place.astype(jnp.int32)])
+        sections, mark = home(0, ())
+        homes, backs, waits = [sections], [], ()
+        sends[1:] = [after(send, (mark,)) for send in sends[1:]]
+        for chunk, send in enumerate(sends):
+            received = lax.all_to_all(send, "ctx", split_axis=0, concat_axis=0, tiled=True)
+            *slabs, mark = stride_attend(place_word, received, waits)
+            backs.append(exchange(slabs, "ctx"))
+            waits = (mark,)
+            for later in range(1, chunks) if chunk == 0 else ():
+                sections, mark = home(later, waits)
+                homes.append(sections)
                 waits = (mark,)
-            if chunk > 0:
-                seats = jnp.stack([seat, place.astype(jnp.int32)])
-                *slabs, mark = combine(seats, sections, ready, groups, (*waits, *arrived))
-                moved.append(exchange(slabs, "head"))
-                waits = (mark,)
-                arrived = moved[-1][1:]
-            if chunk < chunks:
-                sections, mark = home(chunk, waits)
-                ready = backs
-                waits = (mark,)
+        for chunk in range(chunks):
+            *slabs, mark = combine(seats, homes[chunk], backs[chunk], groups, waits)
+            moved.append(exchange(slabs, "head"))
+            waits = (mark, *moved[-1][1:])
     held = after(mine, (mark,))
     other = lax.ppermute(held, "ctx", sibling)
     return project(sides, moved, held, other)

time: 146 us -> 139 us (0.952)
  Pallas kernels: 43 us -> 38.6 us
  starting transfers between devices: 39.9 us -> 37 us
    ppermute x7, waiting for transfers between devices: 15.2 us -> 1.37 us  [swapped(): return lax.ppermute(piece, 'ctx', [(i, i ^ distance) for i in range(count)])]
    all_to_all x2, waiting for transfers between devices: 0.01 us -> 8.86 us  [body(): lax.all_to_all(send, 'ctx', split_axis=0, concat_axis=0, tiled=True)]
    pallas_call x1, Pallas kernels: 9.57 us -> 4.99 us  [project(): pl.pallas_call(functools.partial(project_kernel, slots=slots, chunks=chun...]
    ppermute x20, waiting for transfers between devices: 17.1 us -> 21.4 us  [exchange(): moved.append(lax.ppermute(slabs[slot], axis, pairs))]
    ppermute x20, starting transfers between devices: 23.9 us -> 20.9 us  [exchange(): moved.append(lax.ppermute(slabs[slot], axis, pairs))]
    unnamed x36 -> x32, local copies, waits for them, and re-layouts: 5.91 us -> 5.76 us
  transfers between devices with their start and end apart: 32 -> 32, of which waited for: 8 -> 13; matrix products, arithmetic and copies ran while one was open for 0% -> 0% of each run, Pallas kernels for 18% -> 21%
where the time goes in v7:
time: 139 us; the launch traced here: 137 us
  waiting for transfers between devices  41.1 us (30%)
  Pallas kernels  38.6 us (28%)
  starting transfers between devices  37 us (27%)
  between operations  13.6 us (10%)
  local copies, waits for them, and re-layouts  5.76 us (4%)
    ppermute x20, waiting for transfers between devices, exchange(): moved.append(lax.ppermute(slabs[slot], axis, pairs))  21.4 us
    ppermute x20, starting transfers between devices, exchange(): moved.append(lax.ppermute(slabs[slot], axis, pairs))  20.9 us
    pallas_call x2, Pallas kernels, home_sections(): pl.pallas_call(functools.partial(home_kernel, order=order), grid=(heads,)...  14.2 us
    ppermute x1, waiting for transfers between devices, body(): before = lax.ppermute(rim, 'ctx', [(i, i + 1) for i in range(ctx - 1)])  9.44 us
    all_to_all x2, waiting for transfers between devices, body(): lax.all_to_all(send, 'ctx', split_axis=0, concat_axis=0, tiled=True)  8.86 us
    pallas_call x2, Pallas kernels, prepare(): pl.pallas_call(prep_kernel, grid=(tokens_dev // TILE,), in_specs=[pl.Bloc...  8.44 us
    all_to_all x2, starting transfers between devices, body(): lax.all_to_all(send, 'ctx', split_axis=0, concat_axis=0, tiled=True)  8.31 us
    unnamed x32, local copies, waits for them, and re-layouts  5.76 us
  transfers between devices with their start and end apart: 32, of which 13 were waited for; matrix products, arithmetic and copies ran while one was open for 0% of the time, Pallas kernels for 21%

profile of v7, /device:TPU:10, one launch (start us, length us, event | category | flops | bytes accessed | tf_op | source)
XLA Modules:
  0.0 136.7 jit_solution(11584425271244553730)
XLA Ops:
  6.5 0.7 pad_add_fusion.side_ref
  7.2 2.1 %edges.1 = (bf16[2,512,512]{2,1,0:T(8,128)(2,1)}, bf16[2,64,512]{2,1,0:T(8,128)(2,1)}) custom-call(bf16[1024,512]{1,0:T(8,128)(2,1)} %k_ref.9, bf16[1024,512]{1,0:T(8,128)(2,1)} %v_ref.9, bf16[8,128,512]{2,1,0:T(8,128)(2,1)} %bitcast.7, bf16[8,128,512]{2,1,0:T(8,128)(2,1)} %bitcast.8), custom_call_target="tpu_custom_call" | custom-call | bytes 2097152 | tf_op jit(solution)/shard_map/edges/pallas_call | solution.py:122
  9.3 2.9 %half.1.refs_0_ = bf16[512,1024]{1,0:T(8,128)(2,1)} custom-call(s32[2]{0:T(128)} %pad_add_fusion.side_ref, bf16[512,2048]{1,0:T(8,128)(2,1)} %weight_ref.1, bf16[2,64,512]{2,1,0:T(8,128)(2,1)} %get-tuple-element.40.refs_0_), custom_call_target="tpu_custom_call" | custom-call | bytes 2097152 | tf_op jit(solution)/shard_map/half/pallas_call | solution.py:152
  12.3 1.6 %collective-permute-start.2 = (bf16[2,64,512]{2,1,0:T(8,128)(2,1)S(1)}, bf16[2,64,512]{2,1,0:T(8,128)(2,1)S(1)}, u32[]{:S(2)}, u32[]{:S(2)}) collective-permute-start(bf16[2,64,512]{2,1,0:T(8,128)(2,1)S(1)} %copy-done.7), channel_id=1, source_target_pairs={{0,24},{4,28},{8,16},{12,20},{16,8},{20,12},{24,0},{28,4},{1,25},{... | collective-permute-start | bytes 393224 | tf_op jit(solution)/shard_map/ppermute | solution.py:420
  13.9 0.5 collective-permute-start.1
  14.4 1.5 %collective-permute-start = (bf16[2,64,512]{2,1,0:T(8,128)(2,1)S(1)}, bf16[2,64,512]{2,1,0:T(8,128)(2,1)S(1)}, u32[]{:S(2)}, u32[]{:S(2)}) collective-permute-start(bf16[2,64,512]{2,1,0:T(8,128)(2,1)S(1)} %copy-done.7), channel_id=1, source_target_pairs={{0,8},{4,12},{8,0},{12,4},{16,24},{20,28},{24,16},{28,20},{1,9},{5... | collective-permute-start | bytes 393224 | tf_op jit(solution)/shard_map/ppermute | solution.py:420
  15.8 4.2 %prepare.2.refs_4_.refs_0_ = bf16[8,3,2,64,256]{4,3,2,1,0:T(8,128)(2,1)} custom-call(bf16[1024,512]{1,0:T(8,128)(2,1)} %q_ref.7, bf16[1024,512]{1,0:T(8,128)(2,1)} %k_ref.9, bf16[1024,512]{1,0:T(8,128)(2,1)} %v_ref.9, bf16[512,1024]{1,0:T(8,128)(2,1)} %half.1.refs_0_), custom_call_target="tpu_custom_call" | custom-call | flops 402653184 | bytes 3145728 | tf_op jit(solution)/shard_map/prepare/pallas_call | solution.py:181
  20.0 1.3 collective-permute-done.1.refs_2_
  21.4 0.6 copy-done.9
  22.1 1.9 %collective-permute-start.3 = (bf16[2,512,512]{2,1,0:T(8,128)(2,1)}, bf16[2,512,512]{2,1,0:T(8,128)(2,1)S(1)}, u32[]{:S(2)}, u32[]{:S(2)}) collective-permute-start(bf16[2,512,512]{2,1,0:T(8,128)(2,1)} %after.4.refs_1_), channel_id=1, source_target_pairs={{0,4},{4,8},{8,12},{12,16},{16,20},{20,24},{24,28},{1,5},{5,9},{9,... | collective-permute-start | bytes 3145736 | tf_op jit(solution)/shard_map/ppermute | solution.py:486
  24.0 1.6 %collective-permute-start.7 = (bf16[2,64,512]{2,1,0:T(8,128)(2,1)}, bf16[2,64,512]{2,1,0:T(8,128)(2,1)S(1)}, u32[]{:S(2)}, u32[]{:S(2)}) collective-permute-start(bf16[2,64,512]{2,1,0:T(8,128)(2,1)} %copy-done.8), channel_id=1, source_target_pairs={{0,4},{4,0},{8,12},{12,8},{16,20},{20,16},{24,28},{28,24},{1,5},{5... | collective-permute-start | bytes 393224 | tf_op jit(solution)/shard_map/ppermute | solution.py:420
  25.7 0.4 collective-permute-start.6
  26.2 4.1 %all-to-all-start = ((bf16[8,3,2,64,256]{4,3,2,1,0:T(8,128)(2,1)}), bf16[8,3,2,64,256]{4,3,2,1,0:T(8,128)(2,1)S(1)}, u32[]{:S(2)}, u32[]{:S(2)}) async-start(bf16[8,3,2,64,256]{4,3,2,1,0:T(8,128)(2,1)} %after.5), calls=%async_computation | async-start | bytes 3145728 | tf_op jit(solution)/shard_map/all_to_all | solution.py:520
  30.3 0.7 copy-done.11
  30.9 4.2 %prepare.3.refs_0_ = bf16[8,3,2,64,256]{4,3,2,1,0:T(8,128)(2,1)} custom-call(bf16[1024,512]{1,0:T(8,128)(2,1)} %q_ref.7, bf16[1024,512]{1,0:T(8,128)(2,1)} %k_ref.9, bf16[1024,512]{1,0:T(8,128)(2,1)} %v_ref.9, bf16[2,64,512]{2,1,0:T(8,128)(2,1)} %copy-done.11), custom_call_target="tpu_custom_call" | custom-call | flops 402653184 | bytes 3145728 | tf_op jit(solution)/shard_map/prepare/pallas_call | solution.py:181
  35.2 9.4 %collective-permute-done.3.rim_ref = bf16[2,512,512]{2,1,0:T(8,128)(2,1)S(1)} collective-permute-done((bf16[2,512,512]{2,1,0:T(8,128)(2,1)}, bf16[2,512,512]{2,1,0:T(8,128)(2,1)S(1)}, u32[]{:S(2)}, u32[]{:S(2)}) %collective-permute-start.3) | collective-permute-done | bytes 1048608 | tf_op jit(solution)/shard_map/ppermute | solution.py:486
  44.7 1.0 copy-done.12
  45.6 7.1 %home.2 = (f32[1024,256]{1,0:T(8,128)}, f32[8,128]{1,0:T(8,128)}) custom-call(s32[1]{0:T(128)} %bitcast.2.place_ref, bf16[1024,512]{1,0:T(8,128)(2,1)} %q_ref.7, bf16[1024,512]{1,0:T(8,128)(2,1)} %k_ref.9, bf16[1024,512]{1,0:T(8,128)(2,1)} %v_ref.9, bf16[2,512,512]{2,1,0:T(8,128)(2,1)} %copy-done.12, bf16[2,64,512]{2,1,0:T(8,128)(2,1)} %get-tuple-element.40.refs_0_, ...), custom_call_target="tpu_custom_call" | custom-call | flops 21474836480 | bytes 7340032 | tf_op jit(solution)/shard_map/home/pallas_call | solution.py:248
  52.8 2.5 %all-to-all-done.x_ref = bf16[8,3,2,64,256]{4,3,2,1,0:T(8,128)(2,1)S(1)} async-done(((bf16[8,3,2,64,256]{4,3,2,1,0:T(8,128)(2,1)}), bf16[8,3,2,64,256]{4,3,2,1,0:T(8,128)(2,1)S(1)}, u32[]{:S(2)}, u32[]{:S(2)}) %all-to-all-start) | async-done | bytes 1572896 | tf_op jit(solution)/shard_map/all_to_all | solution.py:520
  55.2 4.2 %all-to-all-start.1 = ((bf16[8,3,2,64,256]{4,3,2,1,0:T(8,128)(2,1)}), bf16[8,3,2,64,256]{4,3,2,1,0:T(8,128)(2,1)S(1)}, u32[]{:S(2)}, u32[]{:S(2)}) async-start(bf16[8,3,2,64,256]{4,3,2,1,0:T(8,128)(2,1)} %after.6), calls=%async_computation.1 | async-start | bytes 3145728 | tf_op jit(solution)/shard_map/all_to_all | solution.py:520
  59.5 2.4 %stride.2 = (bf16[2,64,256]{2,1,0:T(8,128)(2,1)S(1)}, bf16[2,64,256]{2,1,0:T(8,128)(2,1)}, bf16[2,64,256]{2,1,0:T(8,128)(2,1)}, bf16[2,64,256]{2,1,0:T(8,128)(2,...) custom-call(s32[1]{0:T(128)} %bitcast.2.place_ref, ...), custom_call_target="tpu_custom_call" | custom-call | flops 805306368 | bytes 2097152 | tf_op jit(solution)/shard_map/stride/pallas_call | solution.py:302
  62.4 1.4 collective-permute-start.10
  63.8 1.5 %collective-permute-start.11 = (bf16[2,64,256]{2,1,0:T(8,128)(2,1)S(1)}, bf16[2,64,256]{2,1,0:T(8,128)(2,1)S(1)}, u32[]{:S(2)}, u32[]{:S(2)}) collective-permute-start(bf16[2,64,256]{2,1,0:T(8,128)(2,1)S(1)} %get-tuple-element.46), channel_id=1, source_target_pairs={{0,16},{4,20},{8,24},{12,28},{16,0},{20,4},{24,8},{28,12},{1,17},{... | collective-permute-start | bytes 196616 | tf_op jit(solution)/shard_map/ppermute | solution.py:500
  65.6 7.1 %home.3 = (f32[1024,256]{1,0:T(8,128)}, f32[8,128]{1,0:T(8,128)}) custom-call(s32[1]{0:T(128)} %bitcast.2.place_ref, bf16[1024,512]{1,0:T(8,128)(2,1)} %q_ref.7, bf16[1024,512]{1,0:T(8,128)(2,1)} %k_ref.9, bf16[1024,512]{1,0:T(8,128)(2,1)} %v_ref.9, bf16[2,512,512]{2,1,0:T(8,128)(2,1)} %copy-done.12, bf16[2,64,512]{2,1,0:T(8,128)(2,1)} %get-tuple-element.40.refs_0_, ...), custom_call_target="tpu_custom_call" | custom-call | flops 21474836480 | bytes 7340032 | tf_op jit(solution)/shard_map/home/pallas_call | solution.py:248
  72.7 6.4 %all-to-all-done.1.x_ref = bf16[8,3,2,64,256]{4,3,2,1,0:T(8,128)(2,1)S(1)} async-done(((bf16[8,3,2,64,256]{4,3,2,1,0:T(8,128)(2,1)}), bf16[8,3,2,64,256]{4,3,2,1,0:T(8,128)(2,1)S(1)}, u32[]{:S(2)}, u32[]{:S(2)}) %all-to-all-start.1) | async-done | bytes 1572896 | tf_op jit(solution)/shard_map/all_to_all | solution.py:520
  79.1 0.7 copy-done.5
  79.7 1.8 %stride.3 = (bf16[2,64,256]{2,1,0:T(8,128)(2,1)S(1)}, bf16[2,64,256]{2,1,0:T(8,128)(2,1)S(1)}, bf16[2,64,256]{2,1,0:T(8,128)(2,1)S(1)}, bf16[2,64,256]{2,1,0:T(8...) custom-call(s32[1]{0:T(128)} %bitcast.2.place_ref, ...), custom_call_target="tpu_custom_call" | custom-call | flops 805306368 | bytes 2097152 | tf_op jit(solution)/shard_map/stride/pallas_call | solution.py:302
  81.5 2.0 %collective-permute-start.13 = (bf16[2,64,256]{2,1,0:T(8,128)(2,1)S(1)}, bf16[2,64,256]{2,1,0:T(8,128)(2,1)S(1)}, u32[]{:S(2)}, u32[]{:S(2)}) collective-permute-start(bf16[2,64,256]{2,1,0:T(8,128)(2,1)S(1)} %get-tuple-element.48), channel_id=1, source_target_pairs={{0,24},{4,28},{8,16},{12,20},{16,8},{20,12},{24,0},{28,4},{1,25},{... | collective-permute-start | bytes 196616 | tf_op jit(solution)/shard_map/ppermute | solution.py:500
  83.6 0.4 collective-permute-start.14
  84.0 0.7 collective-permute-start.18
  84.6 2.0 %collective-permute-start.19 = (bf16[2,64,256]{2,1,0:T(8,128)(2,1)S(1)}, bf16[2,64,256]{2,1,0:T(8,128)(2,1)S(1)}, u32[]{:S(2)}, u32[]{:S(2)}) collective-permute-start(bf16[2,64,256]{2,1,0:T(8,128)(2,1)S(1)} %get-tuple-element.61), channel_id=1, source_target_pairs={{0,8},{4,12},{8,0},{12,4},{16,24},{20,28},{24,16},{28,20},{1,9},{5... | collective-permute-start | bytes 196616 | tf_op jit(solution)/shard_map/ppermute | solution.py:500
  86.8 1.5 %collective-permute-start.21 = (bf16[2,64,256]{2,1,0:T(8,128)(2,1)S(1)}, bf16[2,64,256]{2,1,0:T(8,128)(2,1)S(1)}, u32[]{:S(2)}, u32[]{:S(2)}) collective-permute-start(bf16[2,64,256]{2,1,0:T(8,128)(2,1)S(1)} %get-tuple-element.63), channel_id=1, source_target_pairs={{0,16},{4,20},{8,24},{12,28},{16,0},{20,4},{24,8},{28,12},{1,17},{... | collective-permute-start | bytes 196616 | tf_op jit(solution)/shard_map/ppermute | solution.py:500
  88.4 0.9 combine.2
  89.2 0.9 collective-permute-start.15
  90.2 2.6 %collective-permute-start.16 = (bf16[256,256]{1,0:T(8,128)(2,1)S(1)}, bf16[256,256]{1,0:T(8,128)(2,1)S(1)}, u32[]{:S(2)}, u32[]{:S(2)}) collective-permute-start(bf16[256,256]{1,0:T(8,128)(2,1)S(1)} %get-tuple-element.56), channel_id=1, source_target_pairs={{0,2},{1,3},{2,0},{3,1},{4,6},{5,7},{6,4},{7,5},{8,10},{9,11},{10,... | collective-permute-start | bytes 393224 | tf_op jit(solution)/shard_map/ppermute | solution.py:500
  92.9 3.3 %collective-permute-start.23 = (bf16[2,64,256]{2,1,0:T(8,128)(2,1)S(1)}, bf16[2,64,256]{2,1,0:T(8,128)(2,1)S(1)}, u32[]{:S(2)}, u32[]{:S(2)}) collective-permute-start(bf16[2,64,256]{2,1,0:T(8,128)(2,1)S(1)} %get-tuple-element.65), channel_id=1, source_target_pairs={{0,24},{4,28},{8,16},{12,20},{16,8},{20,12},{24,0},{28,4},{1,25},{... | collective-permute-start | bytes 196616 | tf_op jit(solution)/shard_map/ppermute | solution.py:500
  96.2 2.2 %collective-permute-done.23.refs_6_ = bf16[2,64,256]{2,1,0:T(8,128)(2,1)S(1)} collective-permute-done((bf16[2,64,256]{2,1,0:T(8,128)(2,1)S(1)}, bf16[2,64,256]{2,1,0:T(8,128)(2,1)S(1)}, u32[]{:S(2)}, u32[]{:S(2)}) %collective-permute-start.23) | collective-permute-done | bytes 65568 | tf_op jit(solution)/shard_map/ppermute | solution.py:500
  98.5 2.4 %collective-permute-done.24.refs_7_ = bf16[2,64,256]{2,1,0:T(8,128)(2,1)S(1)} collective-permute-done((bf16[2,64,256]{2,1,0:T(8,128)(2,1)S(1)}, bf16[2,64,256]{2,1,0:T(8,128)(2,1)S(1)}, u32[]{:S(2)}, u32[]{:S(2)}) %collective-permute-start.24) | collective-permute-done | bytes 65568 | tf_op jit(solution)/shard_map/ppermute | solution.py:500
  100.8 1.5 %collective-permute-done.16.refs_10_.refs_2_ = bf16[256,256]{1,0:T(8,128)(2,1)S(1)} collective-permute-done((bf16[256,256]{1,0:T(8,128)(2,1)S(1)}, bf16[256,256]{1,0:T(8,128)(2,1)S(1)}, u32[]{:S(2)}, u32[]{:S(2)}) %collective-permute-start.16) | collective-permute-done | bytes 131104 | tf_op jit(solution)/shard_map/ppermute | solution.py:500
  102.3 3.3 %collective-permute-done.17.refs_11_.refs_3_ = bf16[256,256]{1,0:T(8,128)(2,1)S(1)} collective-permute-done((bf16[256,256]{1,0:T(8,128)(2,1)S(1)}, bf16[256,256]{1,0:T(8,128)(2,1)S(1)}, u32[]{:S(2)}, u32[]{:S(2)}) %collective-permute-start.17) | collective-permute-done | bytes 131104 | tf_op jit(solution)/shard_map/ppermute | solution.py:500
  105.6 0.8 combine.3
  106.5 0.6 copy-done.3
  107.2 3.1 %collective-permute-start.26 = (bf16[256,256]{1,0:T(8,128)(2,1)S(1)}, bf16[256,256]{1,0:T(8,128)(2,1)S(1)}, u32[]{:S(2)}, u32[]{:S(2)}) collective-permute-start(bf16[256,256]{1,0:T(8,128)(2,1)S(1)} %get-tuple-element.70), channel_id=1, source_target_pairs={{0,2},{1,3},{2,0},{3,1},{4,6},{5,7},{6,4},{7,5},{8,10},{9,11},{10,... | collective-permute-start | bytes 393224 | tf_op jit(solution)/shard_map/ppermute | solution.py:500
  110.7 2.8 %collective-permute-done.25.refs_5_ = bf16[256,256]{1,0:T(8,128)(2,1)S(1)} collective-permute-done((bf16[256,256]{1,0:T(8,128)(2,1)S(1)}, bf16[256,256]{1,0:T(8,128)(2,1)S(1)}, u32[]{:S(2)}, u32[]{:S(2)}) %collective-permute-start.25) | collective-permute-done | bytes 131104 | tf_op jit(solution)/shard_map/ppermute | solution.py:500
  113.5 6.3 %collective-permute-done.26.refs_6_ = bf16[256,256]{1,0:T(8,128)(2,1)S(1)} collective-permute-done((bf16[256,256]{1,0:T(8,128)(2,1)S(1)}, bf16[256,256]{1,0:T(8,128)(2,1)S(1)}, u32[]{:S(2)}, u32[]{:S(2)}) %collective-permute-start.26) | collective-permute-done | bytes 131104 | tf_op jit(solution)/shard_map/ppermute | solution.py:500
  119.8 2.8 %collective-permute-done.27.refs_7_ = bf16[256,256]{1,0:T(8,128)(2,1)S(1)} collective-permute-done((bf16[256,256]{1,0:T(8,128)(2,1)S(1)}, bf16[256,256]{1,0:T(8,128)(2,1)S(1)}, u32[]{:S(2)}, u32[]{:S(2)}) %collective-permute-start.27) | collective-permute-done | bytes 131104 | tf_op jit(solution)/shard_map/ppermute | solution.py:500
  122.7 2.2 %copy-done = bf16[4,512,1024]{2,1,0:T(8,128)(2,1)S(1)} copy-done((bf16[4,512,1024]{2,1,0:T(8,128)(2,1)S(1)}, bf16[4,512,1024]{2,1,0:T(8,128)(2,1)}, u32[]{:S(2)}) %copy-start) | copy-done | bytes 4194328
  124.8 5.0 %project.1 = bf16[256,2048]{1,0:T(8,128)(2,1)} custom-call(s32[2]{0:T(128)S(1)} %copy-done.4, bf16[256,256]{1,0:T(8,128)(2,1)S(1)} %get-tuple-element.54.refs_0_, bf16[256,256]{1,0:T(8,128)(2,1)S(1)} %collective-permute-done.15.refs_9_.refs_1_, bf16[256,256]{1,0:T(8,128)(2,1)S(1)} %collective-permute-done.16.refs_10_.refs_2_, ...), custom_call_target="tpu_custom_call" | custom-call | flops 2147483648 | bytes 9437184 | tf_op jit(solution)/shard_map/project/pallas_call | solution.py:392
  (66 shorter events, 2.3 us)
Async XLA Ops:
  6.5 100.5 %all-gather.3.cloned.1.call-start = ((), (), s32[]{:S(2)}) async-start(), calls=%async_computation.2 | async-start | bytes 5242880 | tf_op jit(solution)/shard_map/all_gather | solution.py:478
  9.3 3.0 %copy-start.7 = (bf16[2,64,512]{2,1,0:T(8,128)(2,1)S(1)}, bf16[2,64,512]{2,1,0:T(8,128)(2,1)}, u32[]{:S(2)}) copy-start(bf16[2,64,512]{2,1,0:T(8,128)(2,1)} %get-tuple-element.40.refs_0_) | copy-start | bytes 393220
  12.3 7.8 %collective-permute-start.2 = (bf16[2,64,512]{2,1,0:T(8,128)(2,1)S(1)}, bf16[2,64,512]{2,1,0:T(8,128)(2,1)S(1)}, u32[]{:S(2)}, u32[]{:S(2)}) collective-permute-start(bf16[2,64,512]{2,1,0:T(8,128)(2,1)S(1)} %copy-done.7), channel_id=1, source_target_pairs={{0,24},{4,28},{8,16},{12,20},{16,8},{20,12},{24,0},{28,4},{1,25},{... | collective-permute-start | bytes 393224 | tf_op jit(solution)/shard_map/ppermute | solution.py:420
  13.9 7.5 %collective-permute-start.1 = (bf16[2,64,512]{2,1,0:T(8,128)(2,1)S(1)}, bf16[2,64,512]{2,1,0:T(8,128)(2,1)S(1)}, u32[]{:S(2)}, u32[]{:S(2)}) collective-permute-start(bf16[2,64,512]{2,1,0:T(8,128)(2,1)S(1)} %copy-done.7), channel_id=1, source_target_pairs={{0,16},{4,20},{8,24},{12,28},{16,0},{20,4},{24,8},{28,12},{1,17},{... | collective-permute-start | bytes 393224 | tf_op jit(solution)/shard_map/ppermute | solution.py:420
  14.4 7.0 %collective-permute-start = (bf16[2,64,512]{2,1,0:T(8,128)(2,1)S(1)}, bf16[2,64,512]{2,1,0:T(8,128)(2,1)S(1)}, u32[]{:S(2)}, u32[]{:S(2)}) collective-permute-start(bf16[2,64,512]{2,1,0:T(8,128)(2,1)S(1)} %copy-done.7), channel_id=1, source_target_pairs={{0,8},{4,12},{8,0},{12,4},{16,24},{20,28},{24,16},{28,20},{1,9},{5... | collective-permute-start | bytes 393224 | tf_op jit(solution)/shard_map/ppermute | solution.py:420
  20.0 1.4 copy-start.8
  21.3 0.7 copy-start.9
  21.4 0.7 copy-start.10
  22.1 22.6 %collective-permute-start.3 = (bf16[2,512,512]{2,1,0:T(8,128)(2,1)}, bf16[2,512,512]{2,1,0:T(8,128)(2,1)S(1)}, u32[]{:S(2)}, u32[]{:S(2)}) collective-permute-start(bf16[2,512,512]{2,1,0:T(8,128)(2,1)} %after.4.refs_1_), channel_id=1, source_target_pairs={{0,4},{4,8},{8,12},{12,16},{16,20},{20,24},{24,28},{1,5},{5,9},{9,... | collective-permute-start | bytes 3145736 | tf_op jit(solution)/shard_map/ppermute | solution.py:486
  24.0 6.3 %collective-permute-start.7 = (bf16[2,64,512]{2,1,0:T(8,128)(2,1)}, bf16[2,64,512]{2,1,0:T(8,128)(2,1)S(1)}, u32[]{:S(2)}, u32[]{:S(2)}) collective-permute-start(bf16[2,64,512]{2,1,0:T(8,128)(2,1)} %copy-done.8), channel_id=1, source_target_pairs={{0,4},{4,0},{8,12},{12,8},{16,20},{20,16},{24,28},{28,24},{1,5},{5... | collective-permute-start | bytes 393224 | tf_op jit(solution)/shard_map/ppermute | solution.py:420
  25.6 9.6 %collective-permute-start.4 = (bf16[2,64,512]{2,1,0:T(8,128)(2,1)S(1)}, bf16[2,64,512]{2,1,0:T(8,128)(2,1)S(1)}, u32[]{:S(2)}, u32[]{:S(2)}) collective-permute-start(bf16[2,64,512]{2,1,0:T(8,128)(2,1)S(1)} %copy-done.7), channel_id=1, source_target_pairs={{0,4},{4,0},{8,12},{12,8},{16,20},{20,16},{24,28},{28,24},{1,5},{5... | collective-permute-start | bytes 393224 | tf_op jit(solution)/shard_map/ppermute | solution.py:420
  25.7 9.5 %collective-permute-start.6 = (bf16[2,64,512]{2,1,0:T(8,128)(2,1)}, bf16[2,64,512]{2,1,0:T(8,128)(2,1)S(1)}, u32[]{:S(2)}, u32[]{:S(2)}) collective-permute-start(bf16[2,64,512]{2,1,0:T(8,128)(2,1)} %copy-done.9), channel_id=1, source_target_pairs={{0,4},{4,0},{8,12},{12,8},{16,20},{20,16},{24,28},{28,24},{1,5},{5... | collective-permute-start | bytes 393224 | tf_op jit(solution)/shard_map/ppermute | solution.py:420
  26.1 9.1 %collective-permute-start.5 = (bf16[2,64,512]{2,1,0:T(8,128)(2,1)}, bf16[2,64,512]{2,1,0:T(8,128)(2,1)S(1)}, u32[]{:S(2)}, u32[]{:S(2)}) collective-permute-start(bf16[2,64,512]{2,1,0:T(8,128)(2,1)} %copy-done.10), channel_id=1, source_target_pairs={{0,4},{4,0},{8,12},{12,8},{16,20},{20,16},{24,28},{28,24},{1,5},{5... | collective-permute-start | bytes 393224 | tf_op jit(solution)/shard_map/ppermute | solution.py:420
  26.2 29.0 %all-to-all-start = ((bf16[8,3,2,64,256]{4,3,2,1,0:T(8,128)(2,1)}), bf16[8,3,2,64,256]{4,3,2,1,0:T(8,128)(2,1)S(1)}, u32[]{:S(2)}, u32[]{:S(2)}) async-start(bf16[8,3,2,64,256]{4,3,2,1,0:T(8,128)(2,1)} %after.5), calls=%async_computation | async-start | bytes 3145728 | tf_op jit(solution)/shard_map/all_to_all | solution.py:520
  30.3 0.7 copy-start.11
  35.2 9.5 %copy-start.13 = (bf16[2,64,512]{2,1,0:T(8,128)(2,1)}, bf16[2,64,512]{2,1,0:T(8,128)(2,1)S(1)}, u32[]{:S(2)}) copy-start(bf16[2,64,512]{2,1,0:T(8,128)(2,1)S(1)} %collective-permute-done.4.refs_4_) | copy-start | bytes 393220
  35.2 9.5 %copy-start.14 = (bf16[2,64,512]{2,1,0:T(8,128)(2,1)}, bf16[2,64,512]{2,1,0:T(8,128)(2,1)S(1)}, u32[]{:S(2)}) copy-start(bf16[2,64,512]{2,1,0:T(8,128)(2,1)S(1)} %collective-permute-done.6.refs_6_) | copy-start | bytes 393220
  35.2 9.5 %copy-start.15 = (bf16[2,64,512]{2,1,0:T(8,128)(2,1)}, bf16[2,64,512]{2,1,0:T(8,128)(2,1)S(1)}, u32[]{:S(2)}) copy-start(bf16[2,64,512]{2,1,0:T(8,128)(2,1)S(1)} %collective-permute-done.5.refs_5_) | copy-start | bytes 393220
  44.7 1.0 copy-start.12
  55.2 23.8 %all-to-all-start.1 = ((bf16[8,3,2,64,256]{4,3,2,1,0:T(8,128)(2,1)}), bf16[8,3,2,64,256]{4,3,2,1,0:T(8,128)(2,1)S(1)}, u32[]{:S(2)}, u32[]{:S(2)}) async-start(bf16[8,3,2,64,256]{4,3,2,1,0:T(8,128)(2,1)} %after.6), calls=%async_computation.1 | async-start | bytes 3145728 | tf_op jit(solution)/shard_map/all_to_all | solution.py:520
  61.9 3.7 %copy-start.6 = (f32[8,128]{1,0:T(8,128)}, f32[8,128]{1,0:T(8,128)S(1)}, u32[]{:S(2)}) copy-start(f32[8,128]{1,0:T(8,128)S(1)} %get-tuple-element.51.refs_8_) | copy-start | bytes 12292
  61.9 19.6 %collective-permute-start.8 = (bf16[2,64,256]{2,1,0:T(8,128)(2,1)}, bf16[2,64,256]{2,1,0:T(8,128)(2,1)S(1)}, u32[]{:S(2)}, u32[]{:S(2)}) collective-permute-start(bf16[2,64,256]{2,1,0:T(8,128)(2,1)} %get-tuple-element.43), channel_id=1, source_target_pairs={{0,4},{4,0},{8,12},{12,8},{16,20},{20,16},{24,28},{28,24},{1,5},{5... | collective-permute-start | bytes 196616 | tf_op jit(solution)/shard_map/ppermute | solution.py:500
  62.1 21.5 %collective-permute-start.9 = (bf16[2,64,256]{2,1,0:T(8,128)(2,1)}, bf16[2,64,256]{2,1,0:T(8,128)(2,1)S(1)}, u32[]{:S(2)}, u32[]{:S(2)}) collective-permute-start(bf16[2,64,256]{2,1,0:T(8,128)(2,1)} %get-tuple-element.44), channel_id=1, source_target_pairs={{0,8},{4,12},{8,0},{12,4},{16,24},{20,28},{24,16},{28,20},{1,9},{5... | collective-permute-start | bytes 196616 | tf_op jit(solution)/shard_map/ppermute | solution.py:500
  62.4 21.6 %collective-permute-start.10 = (bf16[2,64,256]{2,1,0:T(8,128)(2,1)S(1)}, bf16[2,64,256]{2,1,0:T(8,128)(2,1)S(1)}, u32[]{:S(2)}, u32[]{:S(2)}) collective-permute-start(bf16[2,64,256]{2,1,0:T(8,128)(2,1)S(1)} %get-tuple-element.45), channel_id=1, source_target_pairs={{0,12},{4,8},{8,4},{12,0},{16,28},{20,24},{24,20},{28,16},{1,13},{... | collective-permute-start | bytes 196616 | tf_op jit(solution)/shard_map/ppermute | solution.py:500
  63.8 20.9 %collective-permute-start.11 = (bf16[2,64,256]{2,1,0:T(8,128)(2,1)S(1)}, bf16[2,64,256]{2,1,0:T(8,128)(2,1)S(1)}, u32[]{:S(2)}, u32[]{:S(2)}) collective-permute-start(bf16[2,64,256]{2,1,0:T(8,128)(2,1)S(1)} %get-tuple-element.46), channel_id=1, source_target_pairs={{0,16},{4,20},{8,24},{12,28},{16,0},{20,4},{24,8},{28,12},{1,17},{... | collective-permute-start | bytes 196616 | tf_op jit(solution)/shard_map/ppermute | solution.py:500
  65.2 21.4 %collective-permute-start.12 = (bf16[2,64,256]{2,1,0:T(8,128)(2,1)S(1)}, bf16[2,64,256]{2,1,0:T(8,128)(2,1)S(1)}, u32[]{:S(2)}, u32[]{:S(2)}) collective-permute-start(bf16[2,64,256]{2,1,0:T(8,128)(2,1)S(1)} %get-tuple-element.47), channel_id=1, source_target_pairs={{0,20},{4,16},{8,28},{12,24},{16,4},{20,0},{24,12},{28,8},{1,21},{... | collective-permute-start | bytes 196616 | tf_op jit(solution)/shard_map/ppermute | solution.py:500
  72.7 15.7 %copy-start.2 = (f32[1024,256]{1,0:T(8,128)S(1)}, f32[1024,256]{1,0:T(8,128)}, u32[]{:S(2)}) copy-start(f32[1024,256]{1,0:T(8,128)} %get-tuple-element.41.home_ref) | copy-start | bytes 3145732
  79.1 0.7 copy-start.5
  79.7 25.9 %copy-start.1 = (f32[1024,256]{1,0:T(8,128)S(1)}, f32[1024,256]{1,0:T(8,128)}, u32[]{:S(2)}) copy-start(f32[1024,256]{1,0:T(8,128)} %get-tuple-element.58.home_ref) | copy-start | bytes 3145732
  81.5 5.2 %collective-permute-start.13 = (bf16[2,64,256]{2,1,0:T(8,128)(2,1)S(1)}, bf16[2,64,256]{2,1,0:T(8,128)(2,1)S(1)}, u32[]{:S(2)}, u32[]{:S(2)}) collective-permute-start(bf16[2,64,256]{2,1,0:T(8,128)(2,1)S(1)} %get-tuple-element.48), channel_id=1, source_target_pairs={{0,24},{4,28},{8,16},{12,20},{16,8},{20,12},{24,0},{28,4},{1,25},{... | collective-permute-start | bytes 196616 | tf_op jit(solution)/shard_map/ppermute | solution.py:500
  83.6 4.7 %collective-permute-start.14 = (bf16[2,64,256]{2,1,0:T(8,128)(2,1)S(1)}, bf16[2,64,256]{2,1,0:T(8,128)(2,1)S(1)}, u32[]{:S(2)}, u32[]{:S(2)}) collective-permute-start(bf16[2,64,256]{2,1,0:T(8,128)(2,1)S(1)} %get-tuple-element.49), channel_id=1, source_target_pairs={{0,28},{4,24},{8,20},{12,16},{16,12},{20,8},{24,4},{28,0},{1,29},{... | collective-permute-start | bytes 196616 | tf_op jit(solution)/shard_map/ppermute | solution.py:500
  84.0 5.3 %collective-permute-start.18 = (bf16[2,64,256]{2,1,0:T(8,128)(2,1)S(1)}, bf16[2,64,256]{2,1,0:T(8,128)(2,1)S(1)}, u32[]{:S(2)}, u32[]{:S(2)}) collective-permute-start(bf16[2,64,256]{2,1,0:T(8,128)(2,1)S(1)} %get-tuple-element.60), channel_id=1, source_target_pairs={{0,4},{4,0},{8,12},{12,8},{16,20},{20,16},{24,28},{28,24},{1,5},{5... | collective-permute-start | bytes 196616 | tf_op jit(solution)/shard_map/ppermute | solution.py:500
  84.6 5.5 %collective-permute-start.19 = (bf16[2,64,256]{2,1,0:T(8,128)(2,1)S(1)}, bf16[2,64,256]{2,1,0:T(8,128)(2,1)S(1)}, u32[]{:S(2)}, u32[]{:S(2)}) collective-permute-start(bf16[2,64,256]{2,1,0:T(8,128)(2,1)S(1)} %get-tuple-element.61), channel_id=1, source_target_pairs={{0,8},{4,12},{8,0},{12,4},{16,24},{20,28},{24,16},{28,20},{1,9},{5... | collective-permute-start | bytes 196616 | tf_op jit(solution)/shard_map/ppermute | solution.py:500
  86.6 6.1 %collective-permute-start.20 = (bf16[2,64,256]{2,1,0:T(8,128)(2,1)S(1)}, bf16[2,64,256]{2,1,0:T(8,128)(2,1)S(1)}, u32[]{:S(2)}, u32[]{:S(2)}) collective-permute-start(bf16[2,64,256]{2,1,0:T(8,128)(2,1)S(1)} %get-tuple-element.62), channel_id=1, source_target_pairs={{0,12},{4,8},{8,4},{12,0},{16,28},{20,24},{24,20},{28,16},{1,13},{... | collective-permute-start | bytes 196616 | tf_op jit(solution)/shard_map/ppermute | solution.py:500
  86.8 6.2 %collective-permute-start.21 = (bf16[2,64,256]{2,1,0:T(8,128)(2,1)S(1)}, bf16[2,64,256]{2,1,0:T(8,128)(2,1)S(1)}, u32[]{:S(2)}, u32[]{:S(2)}) collective-permute-start(bf16[2,64,256]{2,1,0:T(8,128)(2,1)S(1)} %get-tuple-element.63), channel_id=1, source_target_pairs={{0,16},{4,20},{8,24},{12,28},{16,0},{20,4},{24,8},{28,12},{1,17},{... | collective-permute-start | bytes 196616 | tf_op jit(solution)/shard_map/ppermute | solution.py:500
  88.3 8.0 %collective-permute-start.22 = (bf16[2,64,256]{2,1,0:T(8,128)(2,1)S(1)}, bf16[2,64,256]{2,1,0:T(8,128)(2,1)S(1)}, u32[]{:S(2)}, u32[]{:S(2)}) collective-permute-start(bf16[2,64,256]{2,1,0:T(8,128)(2,1)S(1)} %get-tuple-element.64), channel_id=1, source_target_pairs={{0,20},{4,16},{8,28},{12,24},{16,4},{20,0},{24,12},{28,8},{1,21},{... | collective-permute-start | bytes 196616 | tf_op jit(solution)/shard_map/ppermute | solution.py:500
  89.2 11.6 %collective-permute-start.15 = (bf16[256,256]{1,0:T(8,128)(2,1)S(1)}, bf16[256,256]{1,0:T(8,128)(2,1)S(1)}, u32[]{:S(2)}, u32[]{:S(2)}) collective-permute-start(bf16[256,256]{1,0:T(8,128)(2,1)S(1)} %get-tuple-element.55), channel_id=1, source_target_pairs={{0,1},{1,0},{2,3},{3,2},{4,5},{5,4},{6,7},{7,6},{8,9},{9,8},{10,11... | collective-permute-start | bytes 393224 | tf_op jit(solution)/shard_map/ppermute | solution.py:500
  90.2 12.1 %collective-permute-start.16 = (bf16[256,256]{1,0:T(8,128)(2,1)S(1)}, bf16[256,256]{1,0:T(8,128)(2,1)S(1)}, u32[]{:S(2)}, u32[]{:S(2)}) collective-permute-start(bf16[256,256]{1,0:T(8,128)(2,1)S(1)} %get-tuple-element.56), channel_id=1, source_target_pairs={{0,2},{1,3},{2,0},{3,1},{4,6},{5,7},{6,4},{7,5},{8,10},{9,11},{10,... | collective-permute-start | bytes 393224 | tf_op jit(solution)/shard_map/ppermute | solution.py:500
  92.8 12.9 %collective-permute-start.17 = (bf16[256,256]{1,0:T(8,128)(2,1)S(1)}, bf16[256,256]{1,0:T(8,128)(2,1)S(1)}, u32[]{:S(2)}, u32[]{:S(2)}) collective-permute-start(bf16[256,256]{1,0:T(8,128)(2,1)S(1)} %get-tuple-element.57), channel_id=1, source_target_pairs={{0,3},{1,2},{2,1},{3,0},{4,7},{5,6},{6,5},{7,4},{8,11},{9,10},{10,... | collective-permute-start | bytes 393224 | tf_op jit(solution)/shard_map/ppermute | solution.py:500
  92.9 5.5 %collective-permute-start.23 = (bf16[2,64,256]{2,1,0:T(8,128)(2,1)S(1)}, bf16[2,64,256]{2,1,0:T(8,128)(2,1)S(1)}, u32[]{:S(2)}, u32[]{:S(2)}) collective-permute-start(bf16[2,64,256]{2,1,0:T(8,128)(2,1)S(1)} %get-tuple-element.65), channel_id=1, source_target_pairs={{0,24},{4,28},{8,16},{12,20},{16,8},{20,12},{24,0},{28,4},{1,25},{... | collective-permute-start | bytes 196616 | tf_op jit(solution)/shard_map/ppermute | solution.py:500
  96.2 4.6 %collective-permute-start.24 = (bf16[2,64,256]{2,1,0:T(8,128)(2,1)S(1)}, bf16[2,64,256]{2,1,0:T(8,128)(2,1)S(1)}, u32[]{:S(2)}, u32[]{:S(2)}) collective-permute-start(bf16[2,64,256]{2,1,0:T(8,128)(2,1)S(1)} %get-tuple-element.66), channel_id=1, source_target_pairs={{0,28},{4,24},{8,20},{12,16},{16,12},{20,8},{24,4},{28,0},{1,29},{... | collective-permute-start | bytes 196616 | tf_op jit(solution)/shard_map/ppermute | solution.py:500
  106.5 0.6 copy-start.3
  107.1 15.6 %copy-start.4 = (s32[2]{0:T(128)S(1)}, s32[2]{0:T(128)}, u32[]{:S(2)}) copy-start(s32[2]{0:T(128)} %pad_add_fusion.side_ref) | copy-start | bytes 28
  107.1 15.6 %collective-permute-start.28 = (bf16[4,512,1024]{2,1,0:T(8,128)(2,1)}, bf16[4,512,1024]{2,1,0:T(8,128)(2,1)S(1)}, u32[]{:S(2)}, u32[]{:S(2)}) collective-permute-start(bf16[4,512,1024]{2,1,0:T(8,128)(2,1)} %after.7.refs_8_), channel_id=1, source_target_pairs={{0,4},{4,0},{8,12},{12,8},{16,20},{20,16},{24,28},{28,24},{1,5},{5... | collective-permute-start | bytes 12582920 | tf_op jit(solution)/shard_map/ppermute | solution.py:533
  107.2 6.3 %collective-permute-start.25 = (bf16[256,256]{1,0:T(8,128)(2,1)S(1)}, bf16[256,256]{1,0:T(8,128)(2,1)S(1)}, u32[]{:S(2)}, u32[]{:S(2)}) collective-permute-start(bf16[256,256]{1,0:T(8,128)(2,1)S(1)} %get-tuple-element.69), channel_id=1, source_target_pairs={{0,1},{1,0},{2,3},{3,2},{4,5},{5,4},{6,7},{7,6},{8,9},{9,8},{10,11... | collective-permute-start | bytes 393224 | tf_op jit(solution)/shard_map/ppermute | solution.py:500
  107.2 12.6 %collective-permute-start.26 = (bf16[256,256]{1,0:T(8,128)(2,1)S(1)}, bf16[256,256]{1,0:T(8,128)(2,1)S(1)}, u32[]{:S(2)}, u32[]{:S(2)}) collective-permute-start(bf16[256,256]{1,0:T(8,128)(2,1)S(1)} %get-tuple-element.70), channel_id=1, source_target_pairs={{0,2},{1,3},{2,0},{3,1},{4,6},{5,7},{6,4},{7,5},{8,10},{9,11},{10,... | collective-permute-start | bytes 393224 | tf_op jit(solution)/shard_map/ppermute | solution.py:500
  110.3 12.3 %collective-permute-start.27 = (bf16[256,256]{1,0:T(8,128)(2,1)S(1)}, bf16[256,256]{1,0:T(8,128)(2,1)S(1)}, u32[]{:S(2)}, u32[]{:S(2)}) collective-permute-start(bf16[256,256]{1,0:T(8,128)(2,1)S(1)} %get-tuple-element.71), channel_id=1, source_target_pairs={{0,3},{1,2},{2,1},{3,0},{4,7},{5,6},{6,5},{7,4},{8,11},{9,10},{10,... | collective-permute-start | bytes 393224 | tf_op jit(solution)/shard_map/ppermute | solution.py:500
  122.6 2.2 %copy-start = (bf16[4,512,1024]{2,1,0:T(8,128)(2,1)S(1)}, bf16[4,512,1024]{2,1,0:T(8,128)(2,1)}, u32[]{:S(2)}) copy-start(bf16[4,512,1024]{2,1,0:T(8,128)(2,1)} %after.7.refs_8_) | copy-start | bytes 12582916
Sparse Core Ops, SparseCore 0:
  12.4 79.4 all-gather.2

commit v8 on v7

--- a/solution.py
+++ b/solution.py
@@ -37,18 +37,18 @@
     return [pl.BlockSpec(memory_space=pl.ANY)] * len(arrays)
 
 
-def after(array, others):
+def after(arrays, others):
     anywhere = pl.BlockSpec(memory_space=pl.ANY)
     return pl.pallas_call(
         lambda *refs: None,
-        in_specs=[anywhere] * (1 + len(others)),
-        out_specs=anywhere,
-        out_shape=jax.ShapeDtypeStruct(array.shape, array.dtype),
-        input_output_aliases={0: 0},
+        in_specs=[anywhere] * (len(arrays) + len(others)),
+        out_specs=[anywhere] * len(arrays),
+        out_shape=[jax.ShapeDtypeStruct(array.shape, array.dtype) for array in arrays],
+        input_output_aliases={i: i for i in range(len(arrays))},
         compiler_params=params(60),
         cost_estimate=cost(0, 0),
         name="after",
-    )(array, *others)
+    )(*arrays, *others)
 
 
 def cost(flops, bytes_accessed, exps=0):
@@ -153,10 +153,10 @@
         half_kernel,
         grid_spec=pltpu.PrefetchScalarGridSpec(
             num_scalar_prefetch=1,
-            grid=(2,),
-            in_specs=[pl.BlockSpec((rows // 2, width // 2), lambda i, side: (i, side[0]))]
+            grid=(1,),
+            in_specs=[pl.BlockSpec((rows, width // 2), lambda i, side: (i, side[0]))]
             + moments(waits),
-            out_specs=pl.BlockSpec((rows // 2, width // 2), lambda i, side: (i, 0)),
+            out_specs=pl.BlockSpec((rows, width // 2), lambda i, side: (i, 0)),
         ),
         out_shape=jax.ShapeDtypeStruct((rows, width // 2), BF16),
         compiler_params=params(60),
@@ -174,18 +174,17 @@
         send_ref[:, number] = grouped.reshape(ctx, per, rows, width)
 
 
-def prepare(queries, keys, values, ctx, chunk, chunks, waits):
+def prepare(queries, keys, values, ctx, waits):
     tokens_dev, width = queries.shape
     per = STRIDE // ctx
-    part = width // chunks
     return pl.pallas_call(
         prep_kernel,
         grid=(tokens_dev // TILE,),
-        in_specs=[pl.BlockSpec((TILE, part), lambda b: (b, chunk))] * 3 + moments(waits),
-        out_specs=pl.BlockSpec((ctx, 3, per, TILE // STRIDE, part), lambda b: (0, 0, 0, b, 0)),
-        out_shape=jax.ShapeDtypeStruct((ctx, 3, per, tokens_dev // STRIDE, part), BF16),
+        in_specs=[pl.BlockSpec((TILE, width), lambda b: (b, 0))] * 3 + moments(waits),
+        out_specs=pl.BlockSpec((ctx, 3, per, TILE // STRIDE, width), lambda b: (0, 0, 0, b, 0)),
+        out_shape=jax.ShapeDtypeStruct((ctx, 3, per, tokens_dev // STRIDE, width), BF16),
         compiler_params=params(60),
-        cost_estimate=cost(6 * tokens_dev * TILE * part, 12 * tokens_dev * part),
+        cost_estimate=cost(6 * tokens_dev * TILE * width, 12 * tokens_dev * width),
         name="prepare",
     )(queries, keys, values, *waits)
 
@@ -265,9 +264,9 @@
     )(place, queries, keys, values, rim, *summary, *waits)
 
 
-def stride_kernel(place_ref, x_ref, *refs):
+def stride_kernel(x_ref, *refs):
     ctx, _, _, rows, width = x_ref.shape
-    o_refs, mark_ref, held_ref = refs[-ctx - 2 : -2], refs[-2], refs[-1]
+    o_ref, mark_ref = refs[-2:]
     mark_ref[...] = jnp.zeros_like(mark_ref)
     count = ctx * rows
     row = iota2((TILE, TILE), 0)
@@ -288,121 +287,114 @@
         result = weighted(
             blocks, [value_rows[e * TILE : (e + 1) * TILE] for e in range(b + 1)]
         ).astype(BF16)
-        held_ref[b * sources : (b + 1) * sources, :, lanes] = result.reshape(
+        o_ref[b * sources : (b + 1) * sources, 0, :, lanes] = result.reshape(
             sources, rows, HEAD_SIZE
         )
-    for slot in range(ctx):
-        o_refs[slot][0] = held_ref[partner(place_ref[0], slot, ctx)]
-
-
-def stride_attend(place, moved, waits):
+
+
+def stride_attend(moved, chunk, chunks, waits):
     ctx, _, per, rows, width = moved.shape
+    part = width // chunks
     count = ctx * rows
-    pairs = per * (width // HEAD_SIZE) * count * (count + TILE) // 2
+    pairs = per * (part // HEAD_SIZE) * count * (count + TILE) // 2
     return pl.pallas_call(
         stride_kernel,
         grid=(per,),
-        in_specs=[
-            pl.BlockSpec(memory_space=pltpu.SMEM),
-            pl.BlockSpec((ctx, 3, 1, rows, width), lambda r: (0, 0, r, 0, 0)),
-        ]
+        in_specs=[pl.BlockSpec((ctx, 3, 1, rows, part), lambda r: (0, 0, r, 0, chunk))]
         + moments(waits),
-        out_specs=[pl.BlockSpec((1, rows, width), lambda r: (r, 0, 0))] * ctx + [mark_spec()],
-        out_shape=[jax.ShapeDtypeStruct((per, rows, width), BF16)] * ctx + [MARK],
-        scratch_shapes=[pltpu.VMEM((ctx, rows, width), BF16)],
+        out_specs=[pl.BlockSpec((ctx, 1, rows, part), lambda r: (0, r, 0, 0)), mark_spec()],
+        out_shape=[jax.ShapeDtypeStruct((ctx, per, rows, part), BF16), MARK],
         compiler_params=params(24),
-        cost_estimate=cost(8 * pairs * HEAD_SIZE, 8 * per * count * width, pairs),
+        cost_estimate=cost(8 * pairs * HEAD_SIZE, 8 * per * count * part, pairs),
         name="stride",
-    )(place, moved, *waits)
-
-
-def combine_kernel(seat_ref, home_ref, *refs, slots, ctx):
-    back_refs, o_refs, mark_ref = refs[:ctx], refs[-slots - 1 : -1], refs[-1]
+    )(moved, *waits)
+
+
+def combine_kernel(seat_ref, home_ref, back_ref, *refs, slots):
+    o_refs, mark_ref = refs[-slots - 1 : -1], refs[-1]
     mark_ref[...] = jnp.zeros_like(mark_ref)
     tokens_dev, width = home_ref.shape
     size = tokens_dev // slots
-    per = STRIDE // ctx
-    token = iota2((TILE, TILE), 0)
-    col = iota2((TILE, TILE), 1)
-    group = col >> 4
-    residue = partner(seat_ref[1], group // per, ctx) * per + group % per
-    matrix = (token == (col & 15) * 16 + residue).astype(BF16)
+    matrix = regroup_matrix()
     for slot in range(slots):
-        owner = partner(seat_ref[0], slot, slots)
+        owner = partner(seat_ref[1], slot, slots)
         for b in range(size // TILE):
             first = owner * (size // TILE) + b
             here = pl.ds(pl.multiple_of(first * STRIDE, STRIDE), STRIDE)
-            rows = [ref[r, here] for ref in back_refs for r in range(per)]
-            back = dot(matrix, jnp.concatenate(rows))
+            back = dot(matrix, back_ref[:, :, here].reshape(TILE, width))
             home = home_ref[pl.ds(pl.multiple_of(first * TILE, TILE), TILE)]
             o_refs[slot][b * TILE : (b + 1) * TILE] = (home + back).astype(BF16)
 
 
-def combine(seat, home, backs, slots, waits):
+def combine(seat, home, back, slots, waits):
     tokens_dev, width = home.shape
     size = tokens_dev // slots
     return pl.pallas_call(
-        functools.partial(combine_kernel, slots=slots, ctx=len(backs)),
+        functools.partial(combine_kernel, slots=slots),
         in_specs=[pl.BlockSpec(memory_space=pltpu.SMEM)]
-        + [pl.BlockSpec(memory_space=pltpu.VMEM)] * (1 + len(backs))
+        + [pl.BlockSpec(memory_space=pltpu.VMEM)] * 2
         + moments(waits),
         out_specs=[pl.BlockSpec(memory_space=pltpu.VMEM)] * (slots + 1),
         out_shape=[jax.ShapeDtypeStruct((size, width), BF16)] * slots + [MARK],
         compiler_params=params(24),
         cost_estimate=cost(2 * tokens_dev * TILE * width, 8 * tokens_dev * width),
         name="combine",
-    )(seat, home, *backs, *waits)
+    )(seat, home, back, *waits)
 
 
 def project_kernel(side_ref, *refs, slots, chunks):
     moved_refs = refs[: slots * chunks]
-    mine_ref, other_ref, o_ref, rows_ref = refs[slots * chunks :]
+    mine_ref, other_ref, o_ref, total_ref = refs[slots * chunks :]
     part = moved_refs[0].shape[1]
-    first = (pl.program_id(0) == 0) & (pl.program_id(1) == 0)
-
-    @pl.when(first)
+    half = mine_ref.shape[2]
+    phase, slot = pl.program_id(0), pl.program_id(1)
+
+    def add_up(weight_ref):
+        for one in range(slots):
+
+            @pl.when(slot == one)
+            def _():
+                total = None if one == 0 else total_ref[...]
+                for chunk in range(chunks):
+                    rows = weight_ref[0, chunk * part : (chunk + 1) * part]
+                    product = dot(moved_refs[chunk * slots + one][...], rows)
+                    total = product if total is None else total + product
+                if one < slots - 1:
+                    total_ref[...] = total
+                else:
+                    first = pl.multiple_of((side_ref[0] ^ phase) * half, half)
+                    o_ref[:, pl.ds(first, half)] = total.astype(BF16)
+
+    @pl.when(phase == 0)
     def _():
-        for slot in range(slots):
-            group = partner(side_ref[1], slot, slots)
-            for chunk in range(chunks):
-                here = pl.ds(pl.multiple_of((group * chunks + chunk) * part, part), part)
-                rows_ref[:, here] = moved_refs[chunk * slots + slot][...]
-
-    def multiply(weight_ref):
-        groups, width, tile = weight_ref.shape
-        weight = weight_ref[...].reshape(groups * width, tile)
-        o_ref[...] = dot(rows_ref[...], weight).astype(BF16)
-
-    @pl.when(pl.program_id(0) == 0)
+        add_up(mine_ref)
+
+    @pl.when(phase == 1)
     def _():
-        multiply(mine_ref)
-
-    @pl.when(pl.program_id(0) == 1)
-    def _():
-        multiply(other_ref)
+        add_up(other_ref)
 
 
 def project(side, moved, mine, other):
     chunks, slots = len(moved), len(moved[0])
     tokens, part = moved[0][0].shape
     width, half = mine.shape[1:]
-    tile = min(half, 512)
-    tiles = half // tile
-    block = (slots, width, tile)
+
+    def mine_group(p, s, side):
+        return (side[1] ^ jnp.where(p == 0, s, slots - 1), 0, 0)
+
+    def other_group(p, s, side):
+        return (side[1] ^ jnp.where(p == 0, 0, s), 0, 0)
+
     return pl.pallas_call(
         functools.partial(project_kernel, slots=slots, chunks=chunks),
         grid_spec=pltpu.PrefetchScalarGridSpec(
             num_scalar_prefetch=1,
-            grid=(2, tiles),
-            in_specs=[pl.BlockSpec((tokens, part), lambda s, j, side: (0, 0))] * (slots * chunks)
-            + [
-                pl.BlockSpec(block, lambda s, j, side: (0, 0, jnp.where(s == 0, j, tiles - 1))),
-                pl.BlockSpec(block, lambda s, j, side: (0, 0, jnp.where(s == 0, 0, j))),
-            ],
-            out_specs=pl.BlockSpec(
-                (tokens, tile), lambda s, j, side: (0, (s ^ side[0]) * tiles + j)
-            ),
-            scratch_shapes=[pltpu.VMEM((tokens, slots * width), BF16)],
+            grid=(2, slots),
+            in_specs=[pl.BlockSpec((tokens, part), lambda p, s, side: (0, 0))] * (slots * chunks)
+            + [pl.BlockSpec((1, width, half), mine_group)]
+            + [pl.BlockSpec((1, width, half), other_group)],
+            out_specs=pl.BlockSpec((tokens, 2 * half), lambda p, s, side: (0, 0)),
+            scratch_shapes=[pltpu.VMEM((tokens, half), F32)],
         ),
         out_shape=jax.ShapeDtypeStruct((tokens, 2 * half), BF16),
         compiler_params=params(24),
@@ -462,35 +454,13 @@
     tokens_dev, width = queries.shape
     ctx = lax.axis_size("ctx")
     groups = lax.axis_size("head")
-    place = lax.axis_index("ctx")
-    place_word = place.astype(jnp.int32).reshape(1)
+    place = lax.axis_index("ctx").astype(jnp.int32)
+    place_word = place.reshape(1)
+    seat = lax.axis_index("head").astype(jnp.int32)
     side = place % 2
     sibling = [(i, i ^ 1) for i in range(ctx)]
-
     part = width // chunks
-    seat = lax.axis_index("head").astype(jnp.int32)
-    sides = jnp.stack([side.astype(jnp.int32), seat])
-
-    rim, picked = edges(keys, values, ())
-    between, within, order = gather_ctx(picked)
-    summary = between + within
-    weight_half = half_of(sides, out_weight, (picked,))
-    mine = lax.all_gather(weight_half, "head", axis=0)
-    if ctx > STRIDE:
-        stride_out = stride_general(queries, keys, values)
-        sends = []
-    else:
-        sends = [prepare(queries, keys, values, ctx, 0, chunks, (weight_half,))]
-    rim = after(rim, (*between[1:], *sends))
-    sends = [after(send, (rim,)) for send in sends]
-    before = lax.ppermute(rim, "ctx", [(i, i + 1) for i in range(ctx - 1)])
-    for chunk in range(len(sends), chunks * len(sends)):
-        sends.append(prepare(queries, keys, values, ctx, chunk, chunks, within[-1:]))
-
-    def home(chunk, waits):
-        return home_sections(
-            place_word, queries, keys, values, before, summary, order, chunk, chunks, waits
-        )
+    sides = jnp.stack([side, seat])
 
     def exchange(slabs, axis):
         count = len(slabs)
@@ -500,8 +470,23 @@
             moved.append(lax.ppermute(slabs[slot], axis, pairs))
         return moved
 
+    rim, picked = edges(keys, values, ())
+    between, within, order = gather_ctx(picked)
+    summary = list(between) + within
+    weight_half = half_of(sides, out_weight, (picked,))
+    mine = lax.all_gather(weight_half, "head", axis=0)
+    send = () if ctx > STRIDE else (prepare(queries, keys, values, ctx, (weight_half,)),)
+    (rim,) = after([rim], (*between[1:], *send))
+    before = lax.ppermute(rim, "ctx", [(i, i + 1) for i in range(ctx - 1)])
+
+    def home(chunk, waits):
+        return home_sections(
+            place_word, queries, keys, values, before, summary, order, chunk, chunks, waits
+        )
+
     moved, waits = [], ()
     if ctx > STRIDE:
+        stride_out = stride_general(queries, keys, values)
         for chunk in range(chunks):
             lanes = slice(chunk * part, (chunk + 1) * part)
             homes, mark = home(chunk, waits)
@@ -511,25 +496,22 @@
             moved.append(exchange([attended[owner] for owner in owners], "head"))
             waits = (mark,)
     else:
-        seats = jnp.stack([seat, place.astype(jnp.int32)])
-        seats = jnp.stack([seat, place.astype(jnp.int32)])
-        sections, mark = home(0, ())
-        homes, backs, waits = [sections], [], ()
-        sends[1:] = [after(send, (mark,)) for send in sends[1:]]
-        for chunk, send in enumerate(sends):
-            received = lax.all_to_all(send, "ctx", split_axis=0, concat_axis=0, tiled=True)
-            *slabs, mark = stride_attend(place_word, received, waits)
-            backs.append(exchange(slabs, "ctx"))
+        (send,) = after(send, (rim,))
+        received = lax.all_to_all(send, "ctx", split_axis=0, concat_axis=0, tiled=True)
+        homes, backs = [], []
+        for chunk in range(chunks):
+            sections, mark = home(chunk, waits)
+            homes.append(sections)
             waits = (mark,)
-            for later in range(1, chunks) if chunk == 0 else ():
-                sections, mark = home(later, waits)
-                homes.append(sections)
-                waits = (mark,)
         for chunk in range(chunks):
-            *slabs, mark = combine(seats, homes[chunk], backs[chunk], groups, waits)
+            result, mark = stride_attend(received, chunk, chunks, waits)
+            backs.append(lax.all_to_all(result, "ctx", split_axis=0, concat_axis=0, tiled=True))
+            waits = (mark,)
+        for chunk in range(chunks):
+            *slabs, mark = combine(sides, homes[chunk], backs[chunk], groups, waits)
             moved.append(exchange(slabs, "head"))
             waits = (mark, *moved[-1][1:])
-    held = after(mine, (mark,))
+    (held,) = after([mine], (mark,))
     other = lax.ppermute(held, "ctx", sibling)
     return project(sides, moved, held, other)
 

time: 139 us -> 142 us (1.022); the launches traced: 137 us -> 141 us
  waiting for transfers between devices: 41.1 us -> 55.3 us
  starting transfers between devices: 37 us -> 29.4 us
  Pallas kernels: 38.6 us -> 35.5 us
    ppermute x20 -> x6, starting transfers between devices: 20.9 us -> 8.07 us  [exchange(): moved.append(lax.ppermute(slabs[slot], axis, pairs))]
    all_to_all x0 -> x2, starting transfers between devices: none -> 9.54 us  [body(): lax.all_to_all(result, 'ctx', split_axis=0, concat_axis=0, tiled=True)]
    all_to_all x0 -> x2, waiting for transfers between devices: none -> 7.36 us  [body(): lax.all_to_all(result, 'ctx', split_axis=0, concat_axis=0, tiled=True)]
    ppermute x1, waiting for transfers between devices: 9.44 us -> 14.3 us  [body(): before = lax.ppermute(rim, 'ctx', [(i, i + 1) for i in range(ctx - 1)])]
    all_to_all x2 -> x1, starting transfers between devices: 8.31 us -> 3.79 us  [body(): lax.all_to_all(send, 'ctx', split_axis=0, concat_axis=0, tiled=True)]
    all_to_all x2 -> x1, waiting for transfers between devices: 8.86 us -> 13.2 us  [body(): lax.all_to_all(send, 'ctx', split_axis=0, concat_axis=0, tiled=True)]
    pallas_call x2 -> x1, Pallas kernels: 8.44 us -> 4.95 us  [prepare(): pl.pallas_call(prep_kernel, grid=(tokens_dev // TILE,), in_specs=[pl.Bloc...]
    ppermute x20 -> x6, waiting for transfers between devices: 21.4 us -> 19.8 us  [exchange(): moved.append(lax.ppermute(slabs[slot], axis, pairs))]
  transfers between devices with their start and end apart: 32 -> 19, of which waited for: 13 -> 11; matrix products, arithmetic and copies ran while one was open for 0% -> 0% of each run, Pallas kernels for 21% -> 18%
where the time goes in v8:
time: 142 us; the launch traced here: 141 us
  waiting for transfers between devices  55.3 us (39%)
  Pallas kernels  35.5 us (25%)
  starting transfers between devices  29.4 us (21%)
  between operations  13.5 us (10%)
  local copies, waits for them, and re-layouts  6.97 us (5%)
    ppermute x6, waiting for transfers between devices, exchange(): moved.append(lax.ppermute(slabs[slot], axis, pairs))  19.8 us
    ppermute x1, waiting for transfers between devices, body(): before = lax.ppermute(rim, 'ctx', [(i, i + 1) for i in range(ctx - 1)])  14.3 us
    pallas_call x2, Pallas kernels, home_sections(): pl.pallas_call(functools.partial(home_kernel, order=order), grid=(heads,)...  14.2 us
    all_to_all x1, waiting for transfers between devices, body(): lax.all_to_all(send, 'ctx', split_axis=0, concat_axis=0, tiled=True)  13.2 us
    all_to_all x2, starting transfers between devices, body(): lax.all_to_all(result, 'ctx', split_axis=0, concat_axis=0, tiled=True)  9.54 us
    ppermute x6, starting transfers between devices, exchange(): moved.append(lax.ppermute(slabs[slot], axis, pairs))  8.07 us
    all_to_all x2, waiting for transfers between devices, body(): lax.all_to_all(result, 'ctx', split_axis=0, concat_axis=0, tiled=True)  7.36 us
    unnamed x28, local copies, waits for them, and re-layouts  6.97 us
  transfers between devices with their start and end apart: 19, of which 11 were waited for; matrix products, arithmetic and copies ran while one was open for 0% of the time, Pallas kernels for 18%

profile of v8, /device:TPU:10, one launch (start us, length us, event | category | flops | bytes accessed | tf_op | source)
XLA Modules:
  0.0 141.3 jit_solution(13622032101164516636)
XLA Ops:
  6.5 0.6 pad_add_fusion.side_ref.seat_ref
  7.2 2.1 %edges.1 = (bf16[2,512,512]{2,1,0:T(8,128)(2,1)}, bf16[2,64,512]{2,1,0:T(8,128)(2,1)}) custom-call(bf16[1024,512]{1,0:T(8,128)(2,1)} %k_ref.7, bf16[1024,512]{1,0:T(8,128)(2,1)} %v_ref.7, bf16[8,128,512]{2,1,0:T(8,128)(2,1)} %bitcast.7, bf16[8,128,512]{2,1,0:T(8,128)(2,1)} %bitcast.8), custom_call_target="tpu_custom_call" | custom-call | bytes 2097152 | tf_op jit(solution)/shard_map/edges/pallas_call | solution.py:122
  9.3 3.1 %half.1.refs_0_ = bf16[512,1024]{1,0:T(8,128)(2,1)} custom-call(s32[2]{0:T(128)} %pad_add_fusion.side_ref.seat_ref, bf16[512,2048]{1,0:T(8,128)(2,1)} %weight_ref.1, bf16[2,64,512]{2,1,0:T(8,128)(2,1)} %get-tuple-element.26.refs_0_), custom_call_target="tpu_custom_call" | custom-call | bytes 2097152 | tf_op jit(solution)/shard_map/half/pallas_call | solution.py:152
  12.4 0.0 all-gather.3.cloned.1.call-update
  12.5 0.6 collective-permute-start
  13.1 1.5 %collective-permute-start.1 = (bf16[2,64,512]{2,1,0:T(8,128)(2,1)S(1)}, bf16[2,64,512]{2,1,0:T(8,128)(2,1)S(1)}, u32[]{:S(2)}, u32[]{:S(2)}) collective-permute-start(bf16[2,64,512]{2,1,0:T(8,128)(2,1)S(1)} %copy-done.8), channel_id=1, source_target_pairs={{0,16},{4,20},{8,24},{12,28},{16,0},{20,4},{24,8},{28,12},{1,17},{... | collective-permute-start | bytes 393224 | tf_op jit(solution)/shard_map/ppermute | solution.py:412
  14.6 1.4 %collective-permute-start.2 = (bf16[2,64,512]{2,1,0:T(8,128)(2,1)S(1)}, bf16[2,64,512]{2,1,0:T(8,128)(2,1)S(1)}, u32[]{:S(2)}, u32[]{:S(2)}) collective-permute-start(bf16[2,64,512]{2,1,0:T(8,128)(2,1)S(1)} %copy-done.8), channel_id=1, source_target_pairs={{0,24},{4,28},{8,16},{12,20},{16,8},{20,12},{24,0},{28,4},{1,25},{... | collective-permute-start | bytes 393224 | tf_op jit(solution)/shard_map/ppermute | solution.py:412
  16.0 4.9 %prepare.1.refs_4_.refs_0_ = bf16[8,3,2,64,512]{4,3,2,1,0:T(8,128)(2,1)} custom-call(bf16[1024,512]{1,0:T(8,128)(2,1)} %q_ref.5, bf16[1024,512]{1,0:T(8,128)(2,1)} %k_ref.7, bf16[1024,512]{1,0:T(8,128)(2,1)} %v_ref.7, bf16[512,1024]{1,0:T(8,128)(2,1)} %half.1.refs_0_), custom_call_target="tpu_custom_call" | custom-call | flops 805306368 | bytes 6291456 | tf_op jit(solution)/shard_map/prepare/pallas_call | solution.py:180
  21.0 0.5 collective-permute-done.2.refs_3_
  21.6 0.1 copy-done.9
  21.6 0.1 copy-done.10
  21.7 0.5 copy-done.11
  22.2 1.9 %collective-permute-start.3 = (bf16[2,512,512]{2,1,0:T(8,128)(2,1)}, bf16[2,512,512]{2,1,0:T(8,128)(2,1)}, u32[]{:S(2)}, u32[]{:S(2)}) collective-permute-start(bf16[2,512,512]{2,1,0:T(8,128)(2,1)} %after.3.refs_1_), channel_id=1, source_target_pairs={{0,4},{4,8},{8,12},{12,16},{16,20},{20,24},{24,28},{1,5},{5,9},{9,... | collective-permute-start | bytes 3145736 | tf_op jit(solution)/shard_map/ppermute | solution.py:480
  24.1 2.0 %collective-permute-start.4 = (bf16[2,64,512]{2,1,0:T(8,128)(2,1)S(1)}, bf16[2,64,512]{2,1,0:T(8,128)(2,1)S(1)}, u32[]{:S(2)}, u32[]{:S(2)}) collective-permute-start(bf16[2,64,512]{2,1,0:T(8,128)(2,1)S(1)} %copy-done.8), channel_id=1, source_target_pairs={{0,4},{4,0},{8,12},{12,8},{16,20},{20,16},{24,28},{28,24},{1,5},{5... | collective-permute-start | bytes 393224 | tf_op jit(solution)/shard_map/ppermute | solution.py:412
  26.1 0.1 collective-permute-start.5
  26.2 0.4 collective-permute-start.6
  26.6 0.1 collective-permute-start.7
  26.7 3.8 %all-to-all-start = ((bf16[8,3,2,64,512]{4,3,2,1,0:T(8,128)(2,1)}), bf16[8,3,2,64,512]{4,3,2,1,0:T(8,128)(2,1)S(1)}, u32[]{:S(2)}, u32[]{:S(2)}) async-start(bf16[8,3,2,64,512]{4,3,2,1,0:T(8,128)(2,1)} %after.4), calls=%async_computation | async-start | bytes 6291456 | tf_op jit(solution)/shard_map/all_to_all | solution.py:500
  30.5 14.3 %collective-permute-done.3.rim_ref = bf16[2,512,512]{2,1,0:T(8,128)(2,1)} collective-permute-done((bf16[2,512,512]{2,1,0:T(8,128)(2,1)}, bf16[2,512,512]{2,1,0:T(8,128)(2,1)}, u32[]{:S(2)}, u32[]{:S(2)}) %collective-permute-start.3) | collective-permute-done | bytes 1048608 | tf_op jit(solution)/shard_map/ppermute | solution.py:480
  44.8 7.1 %home.2 = (f32[1024,256]{1,0:T(8,128)}, f32[8,128]{1,0:T(8,128)}) custom-call(s32[1]{0:T(128)} %bitcast.2.place_ref, bf16[1024,512]{1,0:T(8,128)(2,1)} %q_ref.5, bf16[1024,512]{1,0:T(8,128)(2,1)} %k_ref.7, bf16[1024,512]{1,0:T(8,128)(2,1)} %v_ref.7, bf16[2,512,512]{2,1,0:T(8,128)(2,1)} %collective-permute-done.3.rim_ref, ...), custom_call_target="tpu_custom_call" | custom-call | flops 21474836480 | bytes 7340032 | tf_op jit(solution)/shard_map/home/pallas_call | solution.py:247
  51.9 7.1 %home.3 = (f32[1024,256]{1,0:T(8,128)}, f32[8,128]{1,0:T(8,128)}) custom-call(s32[1]{0:T(128)} %bitcast.2.place_ref, bf16[1024,512]{1,0:T(8,128)(2,1)} %q_ref.5, bf16[1024,512]{1,0:T(8,128)(2,1)} %k_ref.7, bf16[1024,512]{1,0:T(8,128)(2,1)} %v_ref.7, bf16[2,512,512]{2,1,0:T(8,128)(2,1)} %collective-permute-done.3.rim_ref, ...), custom_call_target="tpu_custom_call" | custom-call | flops 21474836480 | bytes 7340032 | tf_op jit(solution)/shard_map/home/pallas_call | solution.py:247
  59.0 13.2 %all-to-all-done.x_ref = bf16[8,3,2,64,512]{4,3,2,1,0:T(8,128)(2,1)S(1)} async-done(((bf16[8,3,2,64,512]{4,3,2,1,0:T(8,128)(2,1)}), bf16[8,3,2,64,512]{4,3,2,1,0:T(8,128)(2,1)S(1)}, u32[]{:S(2)}, u32[]{:S(2)}) %all-to-all-start) | async-done | bytes 3145760 | tf_op jit(solution)/shard_map/all_to_all | solution.py:500
  72.3 0.7 copy-done.6
  72.9 1.8 %stride.2 = (bf16[8,2,64,256]{3,2,1,0:T(8,128)(2,1)S(1)}, f32[8,128]{1,0:T(8,128)S(1)}) custom-call(bf16[8,3,2,64,512]{4,3,2,1,0:T(8,128)(2,1)S(1)} %all-to-all-done.x_ref, f32[8,128]{1,0:T(8,128)S(1)} %copy-done.6), custom_call_target="tpu_custom_call" | custom-call | flops 805306368 | bytes 2097152 | tf_op jit(solution)/shard_map/stride/pallas_call | solution.py:300
  74.7 0.8 copy-done.4
  75.5 4.7 %all-to-all-start.1 = ((bf16[8,2,64,256]{3,2,1,0:T(8,128)(2,1)}), bf16[8,2,64,256]{3,2,1,0:T(8,128)(2,1)}, u32[]{:S(2)}, u32[]{:S(2)}) async-start(bf16[8,2,64,256]{3,2,1,0:T(8,128)(2,1)} %copy-done.4), calls=%async_computation.1 | async-start | bytes 1048576 | tf_op jit(solution)/shard_map/all_to_all | solution.py:508
  80.2 1.8 %stride.3 = (bf16[8,2,64,256]{3,2,1,0:T(8,128)(2,1)S(1)}, f32[8,128]{1,0:T(8,128)S(1)}) custom-call(bf16[8,3,2,64,512]{4,3,2,1,0:T(8,128)(2,1)S(1)} %all-to-all-done.x_ref, f32[8,128]{1,0:T(8,128)S(1)} %get-tuple-element.31.refs_0_), custom_call_target="tpu_custom_call" | custom-call | flops 805306368 | bytes 2097152 | tf_op jit(solution)/shard_map/stride/pallas_call | solution.py:300
  82.0 0.8 copy-done.3
  82.8 5.8 %all-to-all-done.1.back_ref = bf16[8,2,64,256]{3,2,1,0:T(8,128)(2,1)} async-done(((bf16[8,2,64,256]{3,2,1,0:T(8,128)(2,1)}), bf16[8,2,64,256]{3,2,1,0:T(8,128)(2,1)}, u32[]{:S(2)}, u32[]{:S(2)}) %all-to-all-start.1) | async-done | bytes 524320 | tf_op jit(solution)/shard_map/all_to_all | solution.py:508
  88.6 4.9 %all-to-all-start.2 = ((bf16[8,2,64,256]{3,2,1,0:T(8,128)(2,1)}), bf16[8,2,64,256]{3,2,1,0:T(8,128)(2,1)S(1)}, u32[]{:S(2)}, u32[]{:S(2)}) async-start(bf16[8,2,64,256]{3,2,1,0:T(8,128)(2,1)} %copy-done.3), calls=%async_computation.2 | async-start | bytes 1048576 | tf_op jit(solution)/shard_map/all_to_all | solution.py:508
  93.5 1.2 copy-done.2
  94.7 1.4 combine.2
  96.0 1.6 %collective-permute-start.10 = (bf16[256,256]{1,0:T(8,128)(2,1)S(1)}, bf16[256,256]{1,0:T(8,128)(2,1)S(1)}, u32[]{:S(2)}, u32[]{:S(2)}) collective-permute-start(bf16[256,256]{1,0:T(8,128)(2,1)S(1)} %get-tuple-element.36), channel_id=1, source_target_pairs={{0,3},{1,2},{2,1},{3,0},{4,7},{5,6},{6,5},{7,4},{8,11},{9,10},{10,... | collective-permute-start | bytes 393224 | tf_op jit(solution)/shard_map/ppermute | solution.py:470
  97.7 2.5 %collective-permute-start.8 = (bf16[256,256]{1,0:T(8,128)(2,1)S(1)}, bf16[256,256]{1,0:T(8,128)(2,1)S(1)}, u32[]{:S(2)}, u32[]{:S(2)}) collective-permute-start(bf16[256,256]{1,0:T(8,128)(2,1)S(1)} %get-tuple-element.34), channel_id=1, source_target_pairs={{0,1},{1,0},{2,3},{3,2},{4,5},{5,4},{6,7},{7,6},{8,9},{9,8},{10,11... | collective-permute-start | bytes 393224 | tf_op jit(solution)/shard_map/ppermute | solution.py:470
  100.2 1.6 %all-to-all-done.2.back_ref = bf16[8,2,64,256]{3,2,1,0:T(8,128)(2,1)S(1)} async-done(((bf16[8,2,64,256]{3,2,1,0:T(8,128)(2,1)}), bf16[8,2,64,256]{3,2,1,0:T(8,128)(2,1)S(1)}, u32[]{:S(2)}, u32[]{:S(2)}) %all-to-all-start.2) | async-done | bytes 524320 | tf_op jit(solution)/shard_map/all_to_all | solution.py:508
  101.7 4.1 %collective-permute-done.10.refs_3_ = bf16[256,256]{1,0:T(8,128)(2,1)S(1)} collective-permute-done((bf16[256,256]{1,0:T(8,128)(2,1)S(1)}, bf16[256,256]{1,0:T(8,128)(2,1)S(1)}, u32[]{:S(2)}, u32[]{:S(2)}) %collective-permute-start.10) | collective-permute-done | bytes 131104 | tf_op jit(solution)/shard_map/ppermute | solution.py:470
  105.9 1.5 %collective-permute-done.8.refs_1_ = bf16[256,256]{1,0:T(8,128)(2,1)S(1)} collective-permute-done((bf16[256,256]{1,0:T(8,128)(2,1)S(1)}, bf16[256,256]{1,0:T(8,128)(2,1)S(1)}, u32[]{:S(2)}, u32[]{:S(2)}) %collective-permute-start.8) | collective-permute-done | bytes 131104 | tf_op jit(solution)/shard_map/ppermute | solution.py:470
  107.3 1.9 %collective-permute-done.9.refs_2_ = bf16[256,256]{1,0:T(8,128)(2,1)S(1)} collective-permute-done((bf16[256,256]{1,0:T(8,128)(2,1)S(1)}, bf16[256,256]{1,0:T(8,128)(2,1)S(1)}, u32[]{:S(2)}, u32[]{:S(2)}) %collective-permute-start.9) | collective-permute-done | bytes 131104 | tf_op jit(solution)/shard_map/ppermute | solution.py:470
  109.2 0.8 combine.3
  110.0 0.6 copy-done.7
  110.6 2.4 %collective-permute-start.11 = (bf16[256,256]{1,0:T(8,128)(2,1)S(1)}, bf16[256,256]{1,0:T(8,128)(2,1)S(1)}, u32[]{:S(2)}, u32[]{:S(2)}) collective-permute-start(bf16[256,256]{1,0:T(8,128)(2,1)S(1)} %get-tuple-element.41), channel_id=1, source_target_pairs={{0,1},{1,0},{2,3},{3,2},{4,5},{5,4},{6,7},{7,6},{8,9},{9,8},{10,11... | collective-permute-start | bytes 393224 | tf_op jit(solution)/shard_map/ppermute | solution.py:470
  113.0 1.1 collective-permute-start.12
  114.1 0.5 collective-permute-start.13
  114.6 4.3 %collective-permute-done.11.refs_5_ = bf16[256,256]{1,0:T(8,128)(2,1)S(1)} collective-permute-done((bf16[256,256]{1,0:T(8,128)(2,1)S(1)}, bf16[256,256]{1,0:T(8,128)(2,1)S(1)}, u32[]{:S(2)}, u32[]{:S(2)}) %collective-permute-start.11) | collective-permute-done | bytes 131104 | tf_op jit(solution)/shard_map/ppermute | solution.py:470
  118.9 4.6 %collective-permute-done.12.refs_6_ = bf16[256,256]{1,0:T(8,128)(2,1)S(1)} collective-permute-done((bf16[256,256]{1,0:T(8,128)(2,1)S(1)}, bf16[256,256]{1,0:T(8,128)(2,1)S(1)}, u32[]{:S(2)}, u32[]{:S(2)}) %collective-permute-start.12) | collective-permute-done | bytes 131104 | tf_op jit(solution)/shard_map/ppermute | solution.py:470
  123.6 3.4 %collective-permute-done.13.refs_7_ = bf16[256,256]{1,0:T(8,128)(2,1)S(1)} collective-permute-done((bf16[256,256]{1,0:T(8,128)(2,1)S(1)}, bf16[256,256]{1,0:T(8,128)(2,1)S(1)}, u32[]{:S(2)}, u32[]{:S(2)}) %collective-permute-start.13) | collective-permute-done | bytes 131104 | tf_op jit(solution)/shard_map/ppermute | solution.py:470
  127.0 2.2 %copy-done = bf16[4,512,1024]{2,1,0:T(8,128)(2,1)S(1)} copy-done((bf16[4,512,1024]{2,1,0:T(8,128)(2,1)S(1)}, bf16[4,512,1024]{2,1,0:T(8,128)(2,1)}, u32[]{:S(2)}) %copy-start) | copy-done | bytes 4194328
  129.1 5.3 %project.1 = bf16[256,2048]{1,0:T(8,128)(2,1)} custom-call(s32[2]{0:T(128)S(1)} %copy-done.5, bf16[256,256]{1,0:T(8,128)(2,1)S(1)} %get-tuple-element.33.refs_0_, bf16[256,256]{1,0:T(8,128)(2,1)S(1)} %collective-permute-done.8.refs_1_, bf16[256,256]{1,0:T(8,128)(2,1)S(1)} %collective-permute-done.9.refs_2_, ...), custom_call_target="tpu_custom_call" | custom-call | flops 2147483648 | bytes 9437184 | tf_op jit(solution)/shard_map/project/pallas_call | solution.py:388
  (33 shorter events, 0.1 us)
Async XLA Ops:
  6.5 104.1 %all-gather.3.cloned.1.call-start = ((), (), s32[]{:S(2)}) async-start(), calls=%async_computation.3 | async-start | bytes 5242880 | tf_op jit(solution)/shard_map/all_gather | solution.py:477
  9.3 3.2 %copy-start.8 = (bf16[2,64,512]{2,1,0:T(8,128)(2,1)S(1)}, bf16[2,64,512]{2,1,0:T(8,128)(2,1)}, u32[]{:S(2)}) copy-start(bf16[2,64,512]{2,1,0:T(8,128)(2,1)} %get-tuple-element.26.refs_0_) | copy-start | bytes 393220
  12.5 8.5 %collective-permute-start = (bf16[2,64,512]{2,1,0:T(8,128)(2,1)S(1)}, bf16[2,64,512]{2,1,0:T(8,128)(2,1)S(1)}, u32[]{:S(2)}, u32[]{:S(2)}) collective-permute-start(bf16[2,64,512]{2,1,0:T(8,128)(2,1)S(1)} %copy-done.8), channel_id=1, source_target_pairs={{0,8},{4,12},{8,0},{12,4},{16,24},{20,28},{24,16},{28,20},{1,9},{5... | collective-permute-start | bytes 393224 | tf_op jit(solution)/shard_map/ppermute | solution.py:412
  13.1 7.9 %collective-permute-start.1 = (bf16[2,64,512]{2,1,0:T(8,128)(2,1)S(1)}, bf16[2,64,512]{2,1,0:T(8,128)(2,1)S(1)}, u32[]{:S(2)}, u32[]{:S(2)}) collective-permute-start(bf16[2,64,512]{2,1,0:T(8,128)(2,1)S(1)} %copy-done.8), channel_id=1, source_target_pairs={{0,16},{4,20},{8,24},{12,28},{16,0},{20,4},{24,8},{28,12},{1,17},{... | collective-permute-start | bytes 393224 | tf_op jit(solution)/shard_map/ppermute | solution.py:412
  14.6 6.9 %collective-permute-start.2 = (bf16[2,64,512]{2,1,0:T(8,128)(2,1)S(1)}, bf16[2,64,512]{2,1,0:T(8,128)(2,1)S(1)}, u32[]{:S(2)}, u32[]{:S(2)}) collective-permute-start(bf16[2,64,512]{2,1,0:T(8,128)(2,1)S(1)} %copy-done.8), channel_id=1, source_target_pairs={{0,24},{4,28},{8,16},{12,20},{16,8},{20,12},{24,0},{28,4},{1,25},{... | collective-permute-start | bytes 393224 | tf_op jit(solution)/shard_map/ppermute | solution.py:412
  21.0 0.7 copy-start.9
  21.0 0.7 copy-start.10
  21.6 0.7 copy-start.11
  22.2 22.6 %collective-permute-start.3 = (bf16[2,512,512]{2,1,0:T(8,128)(2,1)}, bf16[2,512,512]{2,1,0:T(8,128)(2,1)}, u32[]{:S(2)}, u32[]{:S(2)}) collective-permute-start(bf16[2,512,512]{2,1,0:T(8,128)(2,1)} %after.3.refs_1_), channel_id=1, source_target_pairs={{0,4},{4,8},{8,12},{12,16},{16,20},{20,24},{24,28},{1,5},{5,9},{9,... | collective-permute-start | bytes 3145736 | tf_op jit(solution)/shard_map/ppermute | solution.py:480
  24.1 6.3 %collective-permute-start.4 = (bf16[2,64,512]{2,1,0:T(8,128)(2,1)S(1)}, bf16[2,64,512]{2,1,0:T(8,128)(2,1)S(1)}, u32[]{:S(2)}, u32[]{:S(2)}) collective-permute-start(bf16[2,64,512]{2,1,0:T(8,128)(2,1)S(1)} %copy-done.8), channel_id=1, source_target_pairs={{0,4},{4,0},{8,12},{12,8},{16,20},{20,16},{24,28},{28,24},{1,5},{5... | collective-permute-start | bytes 393224 | tf_op jit(solution)/shard_map/ppermute | solution.py:412
  26.1 4.4 %collective-permute-start.5 = (bf16[2,64,512]{2,1,0:T(8,128)(2,1)}, bf16[2,64,512]{2,1,0:T(8,128)(2,1)S(1)}, u32[]{:S(2)}, u32[]{:S(2)}) collective-permute-start(bf16[2,64,512]{2,1,0:T(8,128)(2,1)} %copy-done.9), channel_id=1, source_target_pairs={{0,4},{4,0},{8,12},{12,8},{16,20},{20,16},{24,28},{28,24},{1,5},{5... | collective-permute-start | bytes 393224 | tf_op jit(solution)/shard_map/ppermute | solution.py:412
  26.2 4.3 %collective-permute-start.6 = (bf16[2,64,512]{2,1,0:T(8,128)(2,1)}, bf16[2,64,512]{2,1,0:T(8,128)(2,1)}, u32[]{:S(2)}, u32[]{:S(2)}) collective-permute-start(bf16[2,64,512]{2,1,0:T(8,128)(2,1)} %copy-done.10), channel_id=1, source_target_pairs={{0,4},{4,0},{8,12},{12,8},{16,20},{20,16},{24,28},{28,24},{1,5},{5... | collective-permute-start | bytes 393224 | tf_op jit(solution)/shard_map/ppermute | solution.py:412
  26.6 3.9 %collective-permute-start.7 = (bf16[2,64,512]{2,1,0:T(8,128)(2,1)}, bf16[2,64,512]{2,1,0:T(8,128)(2,1)}, u32[]{:S(2)}, u32[]{:S(2)}) collective-permute-start(bf16[2,64,512]{2,1,0:T(8,128)(2,1)} %copy-done.11), channel_id=1, source_target_pairs={{0,4},{4,0},{8,12},{12,8},{16,20},{20,16},{24,28},{28,24},{1,5},{5... | collective-permute-start | bytes 393224 | tf_op jit(solution)/shard_map/ppermute | solution.py:412
  26.7 45.6 %all-to-all-start = ((bf16[8,3,2,64,512]{4,3,2,1,0:T(8,128)(2,1)}), bf16[8,3,2,64,512]{4,3,2,1,0:T(8,128)(2,1)S(1)}, u32[]{:S(2)}, u32[]{:S(2)}) async-start(bf16[8,3,2,64,512]{4,3,2,1,0:T(8,128)(2,1)} %after.4), calls=%async_computation | async-start | bytes 6291456 | tf_op jit(solution)/shard_map/all_to_all | solution.py:500
  30.5 14.4 %copy-start.12 = (bf16[2,64,512]{2,1,0:T(8,128)(2,1)}, bf16[2,64,512]{2,1,0:T(8,128)(2,1)S(1)}, u32[]{:S(2)}) copy-start(bf16[2,64,512]{2,1,0:T(8,128)(2,1)S(1)} %collective-permute-done.4.refs_4_) | copy-start | bytes 393220
  30.5 14.3 %copy-start.13 = (bf16[2,64,512]{2,1,0:T(8,128)(2,1)}, bf16[2,64,512]{2,1,0:T(8,128)(2,1)S(1)}, u32[]{:S(2)}) copy-start(bf16[2,64,512]{2,1,0:T(8,128)(2,1)S(1)} %collective-permute-done.5.refs_5_) | copy-start | bytes 393220
  72.3 0.7 copy-start.6
  74.7 0.8 copy-start.4
  75.5 17.9 %copy-start.5 = (s32[2]{0:T(128)S(1)}, s32[2]{0:T(128)}, u32[]{:S(2)}) copy-start(s32[2]{0:T(128)} %pad_add_fusion.side_ref.seat_ref) | copy-start | bytes 28
  75.5 13.1 %all-to-all-start.1 = ((bf16[8,2,64,256]{3,2,1,0:T(8,128)(2,1)}), bf16[8,2,64,256]{3,2,1,0:T(8,128)(2,1)}, u32[]{:S(2)}, u32[]{:S(2)}) async-start(bf16[8,2,64,256]{3,2,1,0:T(8,128)(2,1)} %copy-done.4), calls=%async_computation.1 | async-start | bytes 1048576 | tf_op jit(solution)/shard_map/all_to_all | solution.py:508
  82.0 0.8 copy-start.3
  82.8 26.4 %copy-start.1 = (f32[1024,256]{1,0:T(8,128)S(1)}, f32[1024,256]{1,0:T(8,128)}, u32[]{:S(2)}) copy-start(f32[1024,256]{1,0:T(8,128)} %get-tuple-element.37.home_ref) | copy-start | bytes 3145732
  88.6 13.2 %all-to-all-start.2 = ((bf16[8,2,64,256]{3,2,1,0:T(8,128)(2,1)}), bf16[8,2,64,256]{3,2,1,0:T(8,128)(2,1)S(1)}, u32[]{:S(2)}, u32[]{:S(2)}) async-start(bf16[8,2,64,256]{3,2,1,0:T(8,128)(2,1)} %copy-done.3), calls=%async_computation.2 | async-start | bytes 1048576 | tf_op jit(solution)/shard_map/all_to_all | solution.py:508
  93.4 1.2 copy-start.2
  96.0 9.8 %collective-permute-start.10 = (bf16[256,256]{1,0:T(8,128)(2,1)S(1)}, bf16[256,256]{1,0:T(8,128)(2,1)S(1)}, u32[]{:S(2)}, u32[]{:S(2)}) collective-permute-start(bf16[256,256]{1,0:T(8,128)(2,1)S(1)} %get-tuple-element.36), channel_id=1, source_target_pairs={{0,3},{1,2},{2,1},{3,0},{4,7},{5,6},{6,5},{7,4},{8,11},{9,10},{10,... | collective-permute-start | bytes 393224 | tf_op jit(solution)/shard_map/ppermute | solution.py:470
  97.7 9.6 %collective-permute-start.8 = (bf16[256,256]{1,0:T(8,128)(2,1)S(1)}, bf16[256,256]{1,0:T(8,128)(2,1)S(1)}, u32[]{:S(2)}, u32[]{:S(2)}) collective-permute-start(bf16[256,256]{1,0:T(8,128)(2,1)S(1)} %get-tuple-element.34), channel_id=1, source_target_pairs={{0,1},{1,0},{2,3},{3,2},{4,5},{5,4},{6,7},{7,6},{8,9},{9,8},{10,11... | collective-permute-start | bytes 393224 | tf_op jit(solution)/shard_map/ppermute | solution.py:470
  100.2 9.0 %collective-permute-start.9 = (bf16[256,256]{1,0:T(8,128)(2,1)S(1)}, bf16[256,256]{1,0:T(8,128)(2,1)S(1)}, u32[]{:S(2)}, u32[]{:S(2)}) collective-permute-start(bf16[256,256]{1,0:T(8,128)(2,1)S(1)} %get-tuple-element.35), channel_id=1, source_target_pairs={{0,2},{1,3},{2,0},{3,1},{4,6},{5,7},{6,4},{7,5},{8,10},{9,11},{10,... | collective-permute-start | bytes 393224 | tf_op jit(solution)/shard_map/ppermute | solution.py:470
  110.0 0.6 copy-start.7
  110.6 16.3 %collective-permute-start.14 = (bf16[4,512,1024]{2,1,0:T(8,128)(2,1)}, bf16[4,512,1024]{2,1,0:T(8,128)(2,1)S(1)}, u32[]{:S(2)}, u32[]{:S(2)}) collective-permute-start(bf16[4,512,1024]{2,1,0:T(8,128)(2,1)} %after.5.refs_8_), channel_id=1, source_target_pairs={{0,4},{4,0},{8,12},{12,8},{16,20},{20,16},{24,28},{28,24},{1,5},{5... | collective-permute-start | bytes 12582920 | tf_op jit(solution)/shard_map/ppermute | solution.py:515
  110.6 8.3 %collective-permute-start.11 = (bf16[256,256]{1,0:T(8,128)(2,1)S(1)}, bf16[256,256]{1,0:T(8,128)(2,1)S(1)}, u32[]{:S(2)}, u32[]{:S(2)}) collective-permute-start(bf16[256,256]{1,0:T(8,128)(2,1)S(1)} %get-tuple-element.41), channel_id=1, source_target_pairs={{0,1},{1,0},{2,3},{3,2},{4,5},{5,4},{6,7},{7,6},{8,9},{9,8},{10,11... | collective-permute-start | bytes 393224 | tf_op jit(solution)/shard_map/ppermute | solution.py:470
  113.0 10.6 %collective-permute-start.12 = (bf16[256,256]{1,0:T(8,128)(2,1)S(1)}, bf16[256,256]{1,0:T(8,128)(2,1)S(1)}, u32[]{:S(2)}, u32[]{:S(2)}) collective-permute-start(bf16[256,256]{1,0:T(8,128)(2,1)S(1)} %get-tuple-element.42), channel_id=1, source_target_pairs={{0,2},{1,3},{2,0},{3,1},{4,6},{5,7},{6,4},{7,5},{8,10},{9,11},{10,... | collective-permute-start | bytes 393224 | tf_op jit(solution)/shard_map/ppermute | solution.py:470
  114.1 12.8 %collective-permute-start.13 = (bf16[256,256]{1,0:T(8,128)(2,1)S(1)}, bf16[256,256]{1,0:T(8,128)(2,1)S(1)}, u32[]{:S(2)}, u32[]{:S(2)}) collective-permute-start(bf16[256,256]{1,0:T(8,128)(2,1)S(1)} %get-tuple-element.43), channel_id=1, source_target_pairs={{0,3},{1,2},{2,1},{3,0},{4,7},{5,6},{6,5},{7,4},{8,11},{9,10},{10,... | collective-permute-start | bytes 393224 | tf_op jit(solution)/shard_map/ppermute | solution.py:470
  126.9 2.2 %copy-start = (bf16[4,512,1024]{2,1,0:T(8,128)(2,1)S(1)}, bf16[4,512,1024]{2,1,0:T(8,128)(2,1)}, u32[]{:S(2)}) copy-start(bf16[4,512,1024]{2,1,0:T(8,128)(2,1)} %after.5.refs_8_) | copy-start | bytes 12582916
Sparse Core Ops, SparseCore 0:
  12.6 79.4 all-gather.2

commit v9 on v7

--- a/solution.py
+++ b/solution.py
@@ -37,18 +37,18 @@
     return [pl.BlockSpec(memory_space=pl.ANY)] * len(arrays)
 
 
-def after(array, others):
+def after(arrays, others):
     anywhere = pl.BlockSpec(memory_space=pl.ANY)
     return pl.pallas_call(
         lambda *refs: None,
-        in_specs=[anywhere] * (1 + len(others)),
-        out_specs=anywhere,
-        out_shape=jax.ShapeDtypeStruct(array.shape, array.dtype),
-        input_output_aliases={0: 0},
+        in_specs=[anywhere] * (len(arrays) + len(others)),
+        out_specs=[anywhere] * len(arrays),
+        out_shape=[jax.ShapeDtypeStruct(array.shape, array.dtype) for array in arrays],
+        input_output_aliases={i: i for i in range(len(arrays))},
         compiler_params=params(60),
         cost_estimate=cost(0, 0),
         name="after",
-    )(array, *others)
+    )(*arrays, *others)
 
 
 def cost(flops, bytes_accessed, exps=0):
@@ -143,25 +143,25 @@
     )
 
 
-def half_kernel(side_ref, weight_ref, *refs):
+def cut_kernel(side_ref, weight_ref, *refs):
     refs[-1][...] = weight_ref[...]
 
 
-def half_of(side, weight, waits):
-    rows, width = weight.shape
-    return pl.pallas_call(
-        half_kernel,
+def cut(side, weight, size, first, waits):
+    rows = weight.shape[0]
+    return pl.pallas_call(
+        cut_kernel,
         grid_spec=pltpu.PrefetchScalarGridSpec(
             num_scalar_prefetch=1,
-            grid=(2,),
-            in_specs=[pl.BlockSpec((rows // 2, width // 2), lambda i, side: (i, side[0]))]
+            grid=(1,),
+            in_specs=[pl.BlockSpec((rows, size), lambda i, side: (0, first + side[0]))]
             + moments(waits),
-            out_specs=pl.BlockSpec((rows // 2, width // 2), lambda i, side: (i, 0)),
+            out_specs=pl.BlockSpec((rows, size), lambda i, side: (0, 0)),
         ),
-        out_shape=jax.ShapeDtypeStruct((rows, width // 2), BF16),
+        out_shape=jax.ShapeDtypeStruct((rows, size), BF16),
         compiler_params=params(60),
-        cost_estimate=cost(0, 2 * rows * width),
-        name="half",
+        cost_estimate=cost(0, 4 * rows * size),
+        name="cut",
     )(side, weight, *waits)
 
 
@@ -245,6 +245,7 @@
     total = len(summary) * picks
     own = pl.BlockSpec((tokens_dev, HEAD_SIZE), lambda h: (0, first + h))
     pairs = tokens_dev * (WINDOW + TILE + total) * heads
+    weight = 8 if chunk == 0 else 64
     return pl.pallas_call(
         functools.partial(home_kernel, order=order),
         grid=(heads,),
@@ -260,14 +261,14 @@
         out_specs=[pl.BlockSpec((tokens_dev, HEAD_SIZE), lambda h: (0, h)), mark_spec()],
         out_shape=[jax.ShapeDtypeStruct((tokens_dev, heads * HEAD_SIZE), F32), MARK],
         compiler_params=params(60),
-        cost_estimate=cost(64 * pairs * HEAD_SIZE, 14 * tokens_dev * width, 8 * pairs),
+        cost_estimate=cost(weight * pairs * HEAD_SIZE, 14 * tokens_dev * width, weight * pairs // 8),
         name="home",
     )(place, queries, keys, values, rim, *summary, *waits)
 
 
-def stride_kernel(place_ref, x_ref, *refs):
+def stride_kernel(place_ref, x_ref, *refs, slabs):
     ctx, _, _, rows, width = x_ref.shape
-    o_refs, mark_ref, held_ref = refs[-ctx - 2 : -2], refs[-2], refs[-1]
+    o_refs, mark_ref, held_ref = refs[-2 - (ctx if slabs else 1) : -2], refs[-2], refs[-1]
     mark_ref[...] = jnp.zeros_like(mark_ref)
     count = ctx * rows
     row = iota2((TILE, TILE), 0)
@@ -291,24 +292,33 @@
         held_ref[b * sources : (b + 1) * sources, :, lanes] = result.reshape(
             sources, rows, HEAD_SIZE
         )
+    if not slabs:
+        o_refs[0][:, 0] = held_ref[...]
+        return
     for slot in range(ctx):
         o_refs[slot][0] = held_ref[partner(place_ref[0], slot, ctx)]
 
 
-def stride_attend(place, moved, waits):
+def stride_attend(place, moved, slabs, waits):
     ctx, _, per, rows, width = moved.shape
     count = ctx * rows
     pairs = per * (width // HEAD_SIZE) * count * (count + TILE) // 2
-    return pl.pallas_call(
-        stride_kernel,
+    if slabs:
+        out_specs = [pl.BlockSpec((1, rows, width), lambda r: (r, 0, 0))] * ctx
+        out_shape = [jax.ShapeDtypeStruct((per, rows, width), BF16)] * ctx
+    else:
+        out_specs = [pl.BlockSpec((ctx, 1, rows, width), lambda r: (0, r, 0, 0))]
+        out_shape = [jax.ShapeDtypeStruct((ctx, per, rows, width), BF16)]
+    return pl.pallas_call(
+        functools.partial(stride_kernel, slabs=slabs),
         grid=(per,),
         in_specs=[
             pl.BlockSpec(memory_space=pltpu.SMEM),
             pl.BlockSpec((ctx, 3, 1, rows, width), lambda r: (0, 0, r, 0, 0)),
         ]
         + moments(waits),
-        out_specs=[pl.BlockSpec((1, rows, width), lambda r: (r, 0, 0))] * ctx + [mark_spec()],
-        out_shape=[jax.ShapeDtypeStruct((per, rows, width), BF16)] * ctx + [MARK],
+        out_specs=out_specs + [mark_spec()],
+        out_shape=out_shape + [MARK],
         scratch_shapes=[pltpu.VMEM((ctx, rows, width), BF16)],
         compiler_params=params(24),
         cost_estimate=cost(8 * pairs * HEAD_SIZE, 8 * per * count * width, pairs),
@@ -316,8 +326,8 @@
     )(place, moved, *waits)
 
 
-def combine_kernel(seat_ref, home_ref, *refs, slots, ctx):
-    back_refs, o_refs, mark_ref = refs[:ctx], refs[-slots - 1 : -1], refs[-1]
+def combine_kernel(seat_ref, home_ref, *refs, slots, arrays, ctx):
+    back_refs, o_refs, mark_ref = refs[:arrays], refs[-slots - 1 : -1], refs[-1]
     mark_ref[...] = jnp.zeros_like(mark_ref)
     tokens_dev, width = home_ref.shape
     size = tokens_dev // slots
@@ -325,24 +335,27 @@
     token = iota2((TILE, TILE), 0)
     col = iota2((TILE, TILE), 1)
     group = col >> 4
-    residue = partner(seat_ref[1], group // per, ctx) * per + group % per
-    matrix = (token == (col & 15) * 16 + residue).astype(BF16)
+    owner = group // per if arrays == 1 else partner(seat_ref[1], group // per, ctx)
+    matrix = (token == (col & 15) * 16 + owner * per + group % per).astype(BF16)
     for slot in range(slots):
         owner = partner(seat_ref[0], slot, slots)
         for b in range(size // TILE):
             first = owner * (size // TILE) + b
             here = pl.ds(pl.multiple_of(first * STRIDE, STRIDE), STRIDE)
-            rows = [ref[r, here] for ref in back_refs for r in range(per)]
-            back = dot(matrix, jnp.concatenate(rows))
+            if arrays == 1:
+                rows = back_refs[0][:, :, here].reshape(TILE, width)
+            else:
+                rows = jnp.concatenate([ref[r, here] for ref in back_refs for r in range(per)])
+            back = dot(matrix, rows)
             home = home_ref[pl.ds(pl.multiple_of(first * TILE, TILE), TILE)]
             o_refs[slot][b * TILE : (b + 1) * TILE] = (home + back).astype(BF16)
 
 
-def combine(seat, home, backs, slots, waits):
+def combine(seat, home, backs, slots, ctx, waits):
     tokens_dev, width = home.shape
     size = tokens_dev // slots
     return pl.pallas_call(
-        functools.partial(combine_kernel, slots=slots, ctx=len(backs)),
+        functools.partial(combine_kernel, slots=slots, arrays=len(backs), ctx=ctx),
         in_specs=[pl.BlockSpec(memory_space=pltpu.SMEM)]
         + [pl.BlockSpec(memory_space=pltpu.VMEM)] * (1 + len(backs))
         + moments(waits),
@@ -356,61 +369,77 @@
 
 def project_kernel(side_ref, *refs, slots, chunks):
     moved_refs = refs[: slots * chunks]
-    mine_ref, other_ref, o_ref, rows_ref = refs[slots * chunks :]
+    mine_ref, other_ref, mine_last_ref, other_last_ref, o_ref, total_ref = refs[slots * chunks :]
     part = moved_refs[0].shape[1]
-    first = (pl.program_id(0) == 0) & (pl.program_id(1) == 0)
-
-    @pl.when(first)
+    half, last = mine_ref.shape[2], mine_last_ref.shape[2]
+    phase, slot = pl.program_id(0), pl.program_id(1)
+
+    def add_up(weight_ref, begin, first):
+        size = weight_ref.shape[2]
+        here = slice(begin, begin + size)
+        for one in range(slots):
+
+            @pl.when(slot == one)
+            def _():
+                total = None if one == 0 else total_ref[:, here]
+                for chunk in range(chunks):
+                    rows = weight_ref[0, chunk * part : (chunk + 1) * part]
+                    product = dot(moved_refs[chunk * slots + one][...], rows)
+                    total = product if total is None else total + product
+                if one < slots - 1:
+                    total_ref[:, here] = total
+                else:
+                    o_ref[:, pl.ds(pl.multiple_of(first, size), size)] = total.astype(BF16)
+
+    @pl.when(phase == 0)
     def _():
-        for slot in range(slots):
-            group = partner(side_ref[1], slot, slots)
-            for chunk in range(chunks):
-                here = pl.ds(pl.multiple_of((group * chunks + chunk) * part, part), part)
-                rows_ref[:, here] = moved_refs[chunk * slots + slot][...]
-
-    def multiply(weight_ref):
-        groups, width, tile = weight_ref.shape
-        weight = weight_ref[...].reshape(groups * width, tile)
-        o_ref[...] = dot(rows_ref[...], weight).astype(BF16)
-
-    @pl.when(pl.program_id(0) == 0)
+        add_up(mine_ref, 0, side_ref[0] * half)
+
+    @pl.when(phase == 1)
     def _():
-        multiply(mine_ref)
-
-    @pl.when(pl.program_id(0) == 1)
+        add_up(other_ref, 0, (1 - side_ref[0]) * half)
+
+    @pl.when(phase == 2)
     def _():
-        multiply(other_ref)
-
-
-def project(side, moved, mine, other):
+        add_up(mine_last_ref, 0, 2 * half + side_ref[0] * last)
+        add_up(other_last_ref, last, 2 * half + (1 - side_ref[0]) * last)
+
+
+def project(side, moved, mine, other, mine_last, other_last):
     chunks, slots = len(moved), len(moved[0])
     tokens, part = moved[0][0].shape
     width, half = mine.shape[1:]
-    tile = min(half, 512)
-    tiles = half // tile
-    block = (slots, width, tile)
+    last = mine_last.shape[2]
+
+    def mine_group(p, s, side):
+        return (side[1] ^ jnp.where(p == 0, s, slots - 1), 0, 0)
+
+    def other_group(p, s, side):
+        return (side[1] ^ jnp.where(p == 0, 0, jnp.where(p == 1, s, slots - 1)), 0, 0)
+
+    def last_slot(p, s, side):
+        return (jnp.where(p == 2, s, 0), 0, 0)
+
+    total = 2 * (half + last)
     return pl.pallas_call(
         functools.partial(project_kernel, slots=slots, chunks=chunks),
         grid_spec=pltpu.PrefetchScalarGridSpec(
             num_scalar_prefetch=1,
-            grid=(2, tiles),
-            in_specs=[pl.BlockSpec((tokens, part), lambda s, j, side: (0, 0))] * (slots * chunks)
-            + [
-                pl.BlockSpec(block, lambda s, j, side: (0, 0, jnp.where(s == 0, j, tiles - 1))),
-                pl.BlockSpec(block, lambda s, j, side: (0, 0, jnp.where(s == 0, 0, j))),
-            ],
-            out_specs=pl.BlockSpec(
-                (tokens, tile), lambda s, j, side: (0, (s ^ side[0]) * tiles + j)
-            ),
-            scratch_shapes=[pltpu.VMEM((tokens, slots * width), BF16)],
+            grid=(3, slots),
+            in_specs=[pl.BlockSpec((tokens, part), lambda p, s, side: (0, 0))] * (slots * chunks)
+            + [pl.BlockSpec((1, width, half), mine_group)]
+            + [pl.BlockSpec((1, width, half), other_group)]
+            + [pl.BlockSpec((1, width, last), last_slot)] * 2,
+            out_specs=pl.BlockSpec((tokens, total), lambda p, s, side: (0, 0)),
+            scratch_shapes=[pltpu.VMEM((tokens, max(half, 2 * last)), F32)],
         ),
-        out_shape=jax.ShapeDtypeStruct((tokens, 2 * half), BF16),
+        out_shape=jax.ShapeDtypeStruct((tokens, total), BF16),
         compiler_params=params(24),
         cost_estimate=cost(
-            4 * slots * tokens * width * half, 2 * slots * width * (2 * half + tokens)
+            2 * slots * tokens * width * total, 2 * slots * width * (total + tokens)
         ),
         name="project",
-    )(side, *[slab for slabs in moved for slab in slabs], mine, other)
+    )(side, *[slab for slabs in moved for slab in slabs], mine, other, mine_last, other_last)
 
 
 def gather_ctx(rows):
@@ -471,27 +500,6 @@
     seat = lax.axis_index("head").astype(jnp.int32)
     sides = jnp.stack([side.astype(jnp.int32), seat])
 
-    rim, picked = edges(keys, values, ())
-    between, within, order = gather_ctx(picked)
-    summary = between + within
-    weight_half = half_of(sides, out_weight, (picked,))
-    mine = lax.all_gather(weight_half, "head", axis=0)
-    if ctx > STRIDE:
-        stride_out = stride_general(queries, keys, values)
-        sends = []
-    else:
-        sends = [prepare(queries, keys, values, ctx, 0, chunks, (weight_half,))]
-    rim = after(rim, (*between[1:], *sends))
-    sends = [after(send, (rim,)) for send in sends]
-    before = lax.ppermute(rim, "ctx", [(i, i + 1) for i in range(ctx - 1)])
-    for chunk in range(len(sends), chunks * len(sends)):
-        sends.append(prepare(queries, keys, values, ctx, chunk, chunks, within[-1:]))
-
-    def home(chunk, waits):
-        return home_sections(
-            place_word, queries, keys, values, before, summary, order, chunk, chunks, waits
-        )
-
     def exchange(slabs, axis):
         count = len(slabs)
         moved = [slabs[0]]
@@ -499,6 +507,32 @@
             pairs = [(i, partner(i, slot, count)) for i in range(count)]
             moved.append(lax.ppermute(slabs[slot], axis, pairs))
         return moved
+
+    rim, picked = edges(keys, values, ())
+    between, within, order = gather_ctx(picked)
+    summary = between + within
+    eighth = out_weight.shape[1] // 8
+    weight_half = cut(sides, out_weight, 3 * eighth, 0, (picked,))
+    mine = lax.all_gather(weight_half, "head", axis=0)
+    if ctx > STRIDE:
+        stride_out = stride_general(queries, keys, values)
+        sends = []
+    else:
+        sends = [prepare(queries, keys, values, ctx, 0, chunks, (weight_half,))]
+    weight_last = cut(sides, out_weight, eighth, 6, sends)
+    mine_last = jnp.stack(exchange([weight_last] * groups, "head"))
+    (rim,) = after([rim], (*between[1:], *sends))
+    if sends:
+        sends = list(after(sends, (rim,)))
+    before = lax.ppermute(rim, "ctx", [(i, i + 1) for i in range(ctx - 1)])
+    for chunk in range(len(sends), chunks * len(sends)):
+        sends.append(prepare(queries, keys, values, ctx, chunk, chunks, within[-1:]))
+
+    def home(chunk, waits):
+        return home_sections(
+            place_word, queries, keys, values, before, summary, order, chunk, chunks, waits
+        )
+
 
     moved, waits = [], ()
     if ctx > STRIDE:
@@ -513,25 +547,32 @@
     else:
         seats = jnp.stack([seat, place.astype(jnp.int32)])
         seats = jnp.stack([seat, place.astype(jnp.int32)])
-        sections, mark = home(0, ())
+        sections, mark = home(0, (mine_last,))
         homes, backs, waits = [sections], [], ()
-        sends[1:] = [after(send, (mark,)) for send in sends[1:]]
+        if chunks > 1:
+            sends[1:] = list(after(sends[1:], (mark,)))
         for chunk, send in enumerate(sends):
             received = lax.all_to_all(send, "ctx", split_axis=0, concat_axis=0, tiled=True)
-            *slabs, mark = stride_attend(place_word, received, waits)
-            backs.append(exchange(slabs, "ctx"))
+            beside = chunk < chunks - 1
+            *slabs, mark = stride_attend(place_word, received, beside, waits)
+            if beside:
+                backs.append(exchange(slabs, "ctx"))
+            else:
+                back = lax.all_to_all(slabs[0], "ctx", split_axis=0, concat_axis=0, tiled=True)
+                backs.append([back])
             waits = (mark,)
             for later in range(1, chunks) if chunk == 0 else ():
                 sections, mark = home(later, waits)
                 homes.append(sections)
-                waits = (mark,)
+                waits = (mark, *backs[0][1:-1])
         for chunk in range(chunks):
-            *slabs, mark = combine(seats, homes[chunk], backs[chunk], groups, waits)
+            *slabs, mark = combine(seats, homes[chunk], backs[chunk], groups, ctx, waits)
             moved.append(exchange(slabs, "head"))
             waits = (mark, *moved[-1][1:])
-    held = after(mine, (mark,))
+    held, held_last = after([mine, mine_last], (mark,))
     other = lax.ppermute(held, "ctx", sibling)
-    return project(sides, moved, held, other)
+    other_last = lax.ppermute(held_last, "ctx", sibling)
+    return project(sides, moved, held, other, held_last, other_last)
 
 
 def solution(mesh):

time: 139 us -> 202 us (1.45)
  waiting for transfers between devices: 41.1 us -> 90.8 us
  Pallas kernels: 38.6 us -> 42.8 us
  starting transfers between devices: 37 us -> 40.6 us
  local copies, waits for them, and re-layouts: 5.76 us -> 9.36 us
  other arithmetic: 0.72 us -> 2.74 us
    ppermute x20 -> x16, waiting for transfers between devices: 21.4 us -> 90.8 us  [exchange(): moved.append(lax.ppermute(slabs[slot], axis, pairs))]
    ppermute x1, waiting for transfers between devices: 9.44 us -> 0.01 us  [body(): before = lax.ppermute(rim, 'ctx', [(i, i + 1) for i in range(ctx - 1)])]
    all_to_all x2, waiting for transfers between devices: 8.86 us -> 0.01 us  [body(): lax.all_to_all(send, 'ctx', split_axis=0, concat_axis=0, tiled=True)]
    all_to_all x0 -> x1, starting transfers between devices: none -> 5.01 us  [body(): lax.all_to_all(slabs[0], 'ctx', split_axis=0, concat_axis=0, tiled=True)]
    unnamed x32 -> x39, local copies, waits for them, and re-layouts: 5.76 us -> 9.36 us
    pallas_call x9 -> x10, Pallas kernels: 8.82 us -> 11.2 us  [the longest x2 5.22 us: cut(): pl.pallas_call(cut_kernel, grid_spec=pltpu.PrefetchScalarGridSpec(num_sca...]
    another operation x0 -> x1, other arithmetic: none -> 2.06 us  [body(): mine_last = jnp.stack(exchange([weight_last] * groups, 'head'))]
    ppermute x20 -> x16, starting transfers between devices: 20.9 us -> 18.9 us  [exchange(): moved.append(lax.ppermute(slabs[slot], axis, pairs))]
  transfers between devices with their start and end apart: 32 -> 30, of which waited for: 13 -> 13; matrix products, arithmetic and copies ran while one was open for 0% -> 3% of each run, Pallas kernels for 21% -> 15%
where the time goes in v9:
time: 202 us; the launch traced here: 200 us
  waiting for transfers between devices  90.8 us (45%)
  Pallas kernels  42.8 us (21%)
  starting transfers between devices  40.6 us (20%)
  between operations  13.6 us (7%)
  local copies, waits for them, and re-layouts  9.36 us (5%)
  other arithmetic  2.74 us (1%)
    ppermute x16, waiting for transfers between devices, exchange(): moved.append(lax.ppermute(slabs[slot], axis, pairs))  90.8 us
    ppermute x16, starting transfers between devices, exchange(): moved.append(lax.ppermute(slabs[slot], axis, pairs))  18.9 us
    pallas_call x2, Pallas kernels, home_sections(): pl.pallas_call(functools.partial(home_kernel, order=order), grid=(heads,)...  14.2 us
    unnamed x39, local copies, waits for them, and re-layouts  9.36 us
    pallas_call x2, Pallas kernels, prepare(): pl.pallas_call(prep_kernel, grid=(tokens_dev // TILE,), in_specs=[pl.Bloc...  8.39 us
    all_to_all x2, starting transfers between devices, body(): lax.all_to_all(send, 'ctx', split_axis=0, concat_axis=0, tiled=True)  8.02 us
    pallas_call x1, Pallas kernels, project(): pl.pallas_call(functools.partial(project_kernel, slots=slots, chunks=chun...  6.89 us
    ppermute x7, starting transfers between devices, swapped(): return lax.ppermute(piece, 'ctx', [(i, i ^ distance) for i in range(count)])  5.99 us
  transfers between devices with their start and end apart: 30, of which 13 were waited for; matrix products, arithmetic and copies ran while one was open for 3% of the time, Pallas kernels for 15%

profile of v9, /device:TPU:10, one launch (start us, length us, event | category | flops | bytes accessed | tf_op | source)
XLA Modules:
  0.0 200.0 jit_solution(8077267040329646798)
XLA Ops:
  7.1 2.1 %edges.1 = (bf16[2,512,512]{2,1,0:T(8,128)(2,1)}, bf16[2,64,512]{2,1,0:T(8,128)(2,1)}) custom-call(bf16[1024,512]{1,0:T(8,128)(2,1)} %k_ref.9, bf16[1024,512]{1,0:T(8,128)(2,1)} %v_ref.9, bf16[8,128,512]{2,1,0:T(8,128)(2,1)} %bitcast.11, bf16[8,128,512]{2,1,0:T(8,128)(2,1)} %bitcast.12), custom_call_target="tpu_custom_call" | custom-call | bytes 2097152 | tf_op jit(solution)/shard_map/edges/pallas_call | solution.py:122
  9.3 2.9 %cut.2.refs_0_ = bf16[512,768]{1,0:T(8,128)(2,1)} custom-call(s32[2]{0:T(128)} %pad_add_fusion.side_ref, bf16[512,2048]{1,0:T(8,128)(2,1)} %weight_ref.3, bf16[2,64,512]{2,1,0:T(8,128)(2,1)} %get-tuple-element.35.refs_0_), custom_call_target="tpu_custom_call" | custom-call | bytes 1572864 | tf_op jit(solution)/shard_map/cut/pallas_call | solution.py:152
  12.2 1.6 collective-permute-start.2
  14.3 1.5 collective-permute-start
  15.8 4.2 %prepare.2.refs_4_.refs_0_ = bf16[8,3,2,64,256]{4,3,2,1,0:T(8,128)(2,1)} custom-call(bf16[1024,512]{1,0:T(8,128)(2,1)} %q_ref.7, bf16[1024,512]{1,0:T(8,128)(2,1)} %k_ref.9, bf16[1024,512]{1,0:T(8,128)(2,1)} %v_ref.9, bf16[512,768]{1,0:T(8,128)(2,1)} %cut.2.refs_0_), custom_call_target="tpu_custom_call" | custom-call | flops 402653184 | bytes 3145728 | tf_op jit(solution)/shard_map/prepare/pallas_call | solution.py:181
  20.0 2.9 %copy.11.refs_0_ = bf16[8,3,2,64,256]{4,3,2,1,0:T(8,128)(2,1)} copy(bf16[8,3,2,64,256]{4,3,2,1,0:T(8,128)(2,1)} %prepare.2.refs_4_.refs_0_) | data formatting | bytes 3145728
  23.6 4.3 %all-to-all-start = ((bf16[8,3,2,64,256]{4,3,2,1,0:T(8,128)(2,1)}), bf16[8,3,2,64,256]{4,3,2,1,0:T(8,128)(2,1)S(1)}, u32[]{:S(2)}, u32[]{:S(2)}) async-start(bf16[8,3,2,64,256]{4,3,2,1,0:T(8,128)(2,1)} %after.5), calls=%async_computation | async-start | bytes 3145728 | tf_op jit(solution)/shard_map/all_to_all | solution.py:555
  27.9 2.2 %collective-permute-start.3 = (bf16[2,512,512]{2,1,0:T(8,128)(2,1)}, bf16[2,512,512]{2,1,0:T(8,128)(2,1)}, u32[]{:S(2)}, u32[]{:S(2)}) collective-permute-start(bf16[2,512,512]{2,1,0:T(8,128)(2,1)} %after.4.refs_1_), channel_id=1, source_target_pairs={{0,4},{4,8},{8,12},{12,16},{16,20},{20,24},{24,28},{1,5},{5,9},{9,... | collective-permute-start | bytes 3145736 | tf_op jit(solution)/shard_map/ppermute | solution.py:527
  30.1 2.3 %cut.3 = bf16[512,256]{1,0:T(8,128)(2,1)} custom-call(s32[2]{0:T(128)} %pad_add_fusion.side_ref, bf16[512,2048]{1,0:T(8,128)(2,1)} %weight_ref.3, bf16[8,3,2,64,256]{4,3,2,1,0:T(8,128)(2,1)} %prepare.2.refs_4_.refs_0_), custom_call_target="tpu_custom_call" | custom-call | bytes 524288 | tf_op jit(solution)/shard_map/cut/pallas_call | solution.py:152
  32.4 1.6 collective-permute-start.10
  34.0 1.2 collective-permute-start.9
  35.2 1.2 collective-permute-start.8
  36.5 0.9 collective-permute-start.4
  37.3 28.7 %collective-permute-done.10 = bf16[512,256]{1,0:T(8,128)(2,1)S(1)} collective-permute-done((bf16[512,256]{1,0:T(8,128)(2,1)}, bf16[512,256]{1,0:T(8,128)(2,1)S(1)}, u32[]{:S(2)}, u32[]{:S(2)}) %collective-permute-start.10) | collective-permute-done | bytes 262176 | tf_op jit(solution)/shard_map/ppermute | solution.py:508
  66.0 1.1 collective-permute-start.7
  67.1 18.7 %collective-permute-done.9 = bf16[512,256]{1,0:T(8,128)(2,1)S(1)} collective-permute-done((bf16[512,256]{1,0:T(8,128)(2,1)}, bf16[512,256]{1,0:T(8,128)(2,1)S(1)}, u32[]{:S(2)}, u32[]{:S(2)}) %collective-permute-start.9) | collective-permute-done | bytes 262176 | tf_op jit(solution)/shard_map/ppermute | solution.py:508
  86.3 2.1 %pad_maximum_fusion.refs_8_.refs_1_ = bf16[4,512,256]{2,1,0:T(8,128)(2,1)} fusion(bf16[1,512,256]{2,1,0:T(8,128)(2,1)S(1)} %bitcast.14, bf16[1,512,256]{2,1,0:T(8,128)(2,1)S(1)} %bitcast.15, bf16[1,512,256]{2,1,0:T(8,128)(2,1)S(1)} %bitcast.16, bf16[1,512,256]{2,1,0:T(8,128)(2,1)} %bitcast.13), kind=kLoop, calls=%fused_computation | loop fusion | flops 1572864 | bytes 2097152 | tf_op jit(solution)/shard_map/stack | solution.py:523
  89.0 4.2 %prepare.3.refs_0_ = bf16[8,3,2,64,256]{4,3,2,1,0:T(8,128)(2,1)} custom-call(bf16[1024,512]{1,0:T(8,128)(2,1)} %q_ref.7, bf16[1024,512]{1,0:T(8,128)(2,1)} %k_ref.9, bf16[1024,512]{1,0:T(8,128)(2,1)} %v_ref.9, bf16[2,64,512]{2,1,0:T(8,128)(2,1)} %copy-done.15), custom_call_target="tpu_custom_call" | custom-call | flops 402653184 | bytes 3145728 | tf_op jit(solution)/shard_map/prepare/pallas_call | solution.py:181
  93.2 1.8 stride.2
  95.9 7.1 %home.2 = (f32[1024,256]{1,0:T(8,128)}, f32[8,128]{1,0:T(8,128)}) custom-call(s32[1]{0:T(128)} %bitcast.2.place_ref, bf16[1024,512]{1,0:T(8,128)(2,1)} %q_ref.7, bf16[1024,512]{1,0:T(8,128)(2,1)} %k_ref.9, bf16[1024,512]{1,0:T(8,128)(2,1)} %v_ref.9, bf16[2,512,512]{2,1,0:T(8,128)(2,1)} %collective-permute-done.3.rim_ref, ...), custom_call_target="tpu_custom_call" | custom-call | flops 2684354560 | bytes 7340032 | tf_op jit(solution)/shard_map/home/pallas_call | solution.py:249
  103.0 3.8 %all-to-all-start.1 = ((bf16[8,3,2,64,256]{4,3,2,1,0:T(8,128)(2,1)}), bf16[8,3,2,64,256]{4,3,2,1,0:T(8,128)(2,1)S(1)}, u32[]{:S(2)}, u32[]{:S(2)}) async-start(bf16[8,3,2,64,256]{4,3,2,1,0:T(8,128)(2,1)} %after.6), calls=%async_computation.1 | async-start | bytes 3145728 | tf_op jit(solution)/shard_map/all_to_all | solution.py:555
  106.9 1.4 collective-permute-start.13
  108.4 1.4 collective-permute-start.14
  110.3 1.5 collective-permute-start.16
  111.8 7.1 %home.3 = (f32[1024,256]{1,0:T(8,128)}, f32[8,128]{1,0:T(8,128)}) custom-call(s32[1]{0:T(128)} %bitcast.2.place_ref, bf16[1024,512]{1,0:T(8,128)(2,1)} %q_ref.7, bf16[1024,512]{1,0:T(8,128)(2,1)} %k_ref.9, bf16[1024,512]{1,0:T(8,128)(2,1)} %v_ref.9, bf16[2,512,512]{2,1,0:T(8,128)(2,1)} %collective-permute-done.3.rim_ref, ...), custom_call_target="tpu_custom_call" | custom-call | flops 21474836480 | bytes 7340032 | tf_op jit(solution)/shard_map/home/pallas_call | solution.py:249
  118.9 8.1 %collective-permute-done.12.refs_2_ = bf16[2,64,256]{2,1,0:T(8,128)(2,1)S(1)} collective-permute-done((bf16[2,64,256]{2,1,0:T(8,128)(2,1)S(1)}, bf16[2,64,256]{2,1,0:T(8,128)(2,1)S(1)}, u32[]{:S(2)}, u32[]{:S(2)}) %collective-permute-start.12) | collective-permute-done | bytes 65568 | tf_op jit(solution)/shard_map/ppermute | solution.py:508
  126.9 0.9 collective-permute-done.13.refs_3_
  127.9 1.6 collective-permute-done.15.refs_5_
  129.4 1.2 collective-permute-done.16.refs_6_
  131.3 2.5 %stride.3 = (bf16[8,2,64,256]{3,2,1,0:T(8,128)(2,1)}, f32[8,128]{1,0:T(8,128)S(1)}) custom-call(s32[1]{0:T(128)} %bitcast.2.place_ref, bf16[8,3,2,64,256]{4,3,2,1,0:T(8,128)(2,1)S(1)} %all-to-all-done.1.x_ref, f32[8,128]{1,0:T(8,128)S(1)} %copy-done.6, bf16[2,64,256]{2,1,0:T(8,128)(2,1)S(1)} %collective-permute-done.11.refs_1_, ...), custom_call_target="tpu_custom_call" | custom-call | flops 805306368 | bytes 2097152 | tf_op jit(solution)/shard_map/stride/pallas_call | solution.py:312
  133.8 5.0 %all-to-all-start.2 = ((bf16[8,2,64,256]{3,2,1,0:T(8,128)(2,1)}), bf16[8,2,64,256]{3,2,1,0:T(8,128)(2,1)S(1)}, u32[]{:S(2)}, u32[]{:S(2)}) async-start(bf16[8,2,64,256]{3,2,1,0:T(8,128)(2,1)} %get-tuple-element.54), calls=%async_computation.2 | async-start | bytes 1048576 | tf_op jit(solution)/shard_map/all_to_all | solution.py:561
  138.8 1.2 collective-permute-start.17
  140.1 7.9 %collective-permute-done.17.refs_7_ = bf16[2,64,256]{2,1,0:T(8,128)(2,1)S(1)} collective-permute-done((bf16[2,64,256]{2,1,0:T(8,128)(2,1)S(1)}, bf16[2,64,256]{2,1,0:T(8,128)(2,1)S(1)}, u32[]{:S(2)}, u32[]{:S(2)}) %collective-permute-start.17) | collective-permute-done | bytes 65568 | tf_op jit(solution)/shard_map/ppermute | solution.py:508
  148.1 0.9 combine.2
  148.9 3.4 %collective-permute-start.18 = (bf16[256,256]{1,0:T(8,128)(2,1)S(1)}, bf16[256,256]{1,0:T(8,128)(2,1)S(1)}, u32[]{:S(2)}, u32[]{:S(2)}) collective-permute-start(bf16[256,256]{1,0:T(8,128)(2,1)S(1)} %get-tuple-element.50), channel_id=1, source_target_pairs={{0,1},{1,0},{2,3},{3,2},{4,5},{5,4},{6,7},{7,6},{8,9},{9,8},{10,11... | collective-permute-start | bytes 393224 | tf_op jit(solution)/shard_map/ppermute | solution.py:508
  152.5 1.4 collective-permute-start.20
  153.9 3.3 %collective-permute-done.18.refs_2_.refs_1_ = bf16[256,256]{1,0:T(8,128)(2,1)S(1)} collective-permute-done((bf16[256,256]{1,0:T(8,128)(2,1)S(1)}, bf16[256,256]{1,0:T(8,128)(2,1)S(1)}, u32[]{:S(2)}, u32[]{:S(2)}) %collective-permute-start.18) | collective-permute-done | bytes 131104 | tf_op jit(solution)/shard_map/ppermute | solution.py:508
  157.2 4.8 %collective-permute-done.19.refs_3_.refs_2_ = bf16[256,256]{1,0:T(8,128)(2,1)S(1)} collective-permute-done((bf16[256,256]{1,0:T(8,128)(2,1)S(1)}, bf16[256,256]{1,0:T(8,128)(2,1)S(1)}, u32[]{:S(2)}, u32[]{:S(2)}) %collective-permute-start.19) | collective-permute-done | bytes 131104 | tf_op jit(solution)/shard_map/ppermute | solution.py:508
  162.0 4.1 %collective-permute-done.20.refs_4_.refs_3_ = bf16[256,256]{1,0:T(8,128)(2,1)S(1)} collective-permute-done((bf16[256,256]{1,0:T(8,128)(2,1)S(1)}, bf16[256,256]{1,0:T(8,128)(2,1)S(1)}, u32[]{:S(2)}, u32[]{:S(2)}) %collective-permute-start.20) | collective-permute-done | bytes 131104 | tf_op jit(solution)/shard_map/ppermute | solution.py:508
  166.1 0.9 combine.3
  168.0 2.0 %collective-permute-start.22 = (bf16[256,256]{1,0:T(8,128)(2,1)S(1)}, bf16[256,256]{1,0:T(8,128)(2,1)S(1)}, u32[]{:S(2)}, u32[]{:S(2)}) collective-permute-start(bf16[256,256]{1,0:T(8,128)(2,1)S(1)} %get-tuple-element.58), channel_id=1, source_target_pairs={{0,2},{1,3},{2,0},{3,1},{4,6},{5,7},{6,4},{7,5},{8,10},{9,11},{10,... | collective-permute-start | bytes 393224 | tf_op jit(solution)/shard_map/ppermute | solution.py:508
  170.1 1.5 collective-permute-start.23
  171.5 2.9 %collective-permute-done.21.refs_5_ = bf16[256,256]{1,0:T(8,128)(2,1)S(1)} collective-permute-done((bf16[256,256]{1,0:T(8,128)(2,1)S(1)}, bf16[256,256]{1,0:T(8,128)(2,1)S(1)}, u32[]{:S(2)}, u32[]{:S(2)}) %collective-permute-start.21) | collective-permute-done | bytes 131104 | tf_op jit(solution)/shard_map/ppermute | solution.py:508
  174.4 5.2 %collective-permute-done.22.refs_6_ = bf16[256,256]{1,0:T(8,128)(2,1)S(1)} collective-permute-done((bf16[256,256]{1,0:T(8,128)(2,1)S(1)}, bf16[256,256]{1,0:T(8,128)(2,1)S(1)}, u32[]{:S(2)}, u32[]{:S(2)}) %collective-permute-start.22) | collective-permute-done | bytes 131104 | tf_op jit(solution)/shard_map/ppermute | solution.py:508
  179.6 3.5 %collective-permute-done.23.refs_7_ = bf16[256,256]{1,0:T(8,128)(2,1)S(1)} collective-permute-done((bf16[256,256]{1,0:T(8,128)(2,1)S(1)}, bf16[256,256]{1,0:T(8,128)(2,1)S(1)}, u32[]{:S(2)}, u32[]{:S(2)}) %collective-permute-start.23) | collective-permute-done | bytes 131104 | tf_op jit(solution)/shard_map/ppermute | solution.py:508
  183.1 1.9 copy-done
  185.0 1.2 copy-done.1
  186.2 6.9 %project.1 = bf16[256,2048]{1,0:T(8,128)(2,1)} custom-call(s32[2]{0:T(128)S(1)} %copy-done.4, bf16[256,256]{1,0:T(8,128)(2,1)S(1)} %get-tuple-element.49.refs_0_, bf16[256,256]{1,0:T(8,128)(2,1)S(1)} %collective-permute-done.18.refs_2_.refs_1_, bf16[256,256]{1,0:T(8,128)(2,1)S(1)} %collective-permute-done.19.refs_3_.refs_2_, ...), custom_call_target="tpu_custom_call" | custom-call | flops 2147483648 | bytes 9437184 | tf_op jit(solution)/shard_map/project/pallas_call | solution.py:424
  (71 shorter events, 6.6 us)
Async XLA Ops:
  6.5 161.0 %all-gather.3.cloned.1.call-start = ((), (), s32[]{:S(2)}) async-start(), calls=%async_computation.3 | async-start | bytes 3932160 | tf_op jit(solution)/shard_map/all_gather | solution.py:516
  9.3 2.9 %copy-start.8 = (bf16[2,64,512]{2,1,0:T(8,128)(2,1)S(1)}, bf16[2,64,512]{2,1,0:T(8,128)(2,1)}, u32[]{:S(2)}) copy-start(bf16[2,64,512]{2,1,0:T(8,128)(2,1)} %get-tuple-element.35.refs_0_) | copy-start | bytes 393220
  12.2 10.6 %collective-permute-start.2 = (bf16[2,64,512]{2,1,0:T(8,128)(2,1)S(1)}, bf16[2,64,512]{2,1,0:T(8,128)(2,1)S(1)}, u32[]{:S(2)}, u32[]{:S(2)}) collective-permute-start(bf16[2,64,512]{2,1,0:T(8,128)(2,1)S(1)} %copy-done.8), channel_id=1, source_target_pairs={{0,24},{4,28},{8,16},{12,20},{16,8},{20,12},{24,0},{28,4},{1,25},{... | collective-permute-start | bytes 393224 | tf_op jit(solution)/shard_map/ppermute | solution.py:449
  13.8 9.1 %collective-permute-start.1 = (bf16[2,64,512]{2,1,0:T(8,128)(2,1)S(1)}, bf16[2,64,512]{2,1,0:T(8,128)(2,1)S(1)}, u32[]{:S(2)}, u32[]{:S(2)}) collective-permute-start(bf16[2,64,512]{2,1,0:T(8,128)(2,1)S(1)} %copy-done.8), channel_id=1, source_target_pairs={{0,16},{4,20},{8,24},{12,28},{16,0},{20,4},{24,8},{28,12},{1,17},{... | collective-permute-start | bytes 393224 | tf_op jit(solution)/shard_map/ppermute | solution.py:449
  14.3 8.6 %collective-permute-start = (bf16[2,64,512]{2,1,0:T(8,128)(2,1)S(1)}, bf16[2,64,512]{2,1,0:T(8,128)(2,1)S(1)}, u32[]{:S(2)}, u32[]{:S(2)}) collective-permute-start(bf16[2,64,512]{2,1,0:T(8,128)(2,1)S(1)} %copy-done.8), channel_id=1, source_target_pairs={{0,8},{4,12},{8,0},{12,4},{16,24},{20,28},{24,16},{28,20},{1,9},{5... | collective-permute-start | bytes 393224 | tf_op jit(solution)/shard_map/ppermute | solution.py:449
  22.8 0.7 copy-start.9
  22.9 0.7 copy-start.11
  22.9 0.7 copy-start.13
  23.6 69.6 %all-to-all-start = ((bf16[8,3,2,64,256]{4,3,2,1,0:T(8,128)(2,1)}), bf16[8,3,2,64,256]{4,3,2,1,0:T(8,128)(2,1)S(1)}, u32[]{:S(2)}, u32[]{:S(2)}) async-start(bf16[8,3,2,64,256]{4,3,2,1,0:T(8,128)(2,1)} %after.5), calls=%async_computation | async-start | bytes 3145728 | tf_op jit(solution)/shard_map/all_to_all | solution.py:555
  27.9 38.2 %copy-start.10 = (bf16[2,64,512]{2,1,0:T(8,128)(2,1)S(1)}, bf16[2,64,512]{2,1,0:T(8,128)(2,1)}, u32[]{:S(2)}) copy-start(bf16[2,64,512]{2,1,0:T(8,128)(2,1)} %copy-done.9) | copy-start | bytes 393220
  27.9 57.9 %copy-start.12 = (bf16[2,64,512]{2,1,0:T(8,128)(2,1)S(1)}, bf16[2,64,512]{2,1,0:T(8,128)(2,1)}, u32[]{:S(2)}) copy-start(bf16[2,64,512]{2,1,0:T(8,128)(2,1)} %copy-done.11) | copy-start | bytes 393220
  27.9 58.0 %copy-start.14 = (bf16[2,64,512]{2,1,0:T(8,128)(2,1)S(1)}, bf16[2,64,512]{2,1,0:T(8,128)(2,1)}, u32[]{:S(2)}) copy-start(bf16[2,64,512]{2,1,0:T(8,128)(2,1)} %copy-done.13) | copy-start | bytes 393220
  27.9 67.4 %collective-permute-start.3 = (bf16[2,512,512]{2,1,0:T(8,128)(2,1)}, bf16[2,512,512]{2,1,0:T(8,128)(2,1)}, u32[]{:S(2)}, u32[]{:S(2)}) collective-permute-start(bf16[2,512,512]{2,1,0:T(8,128)(2,1)} %after.4.refs_1_), channel_id=1, source_target_pairs={{0,4},{4,8},{8,12},{12,16},{16,20},{20,24},{24,28},{1,5},{5,9},{9,... | collective-permute-start | bytes 3145736 | tf_op jit(solution)/shard_map/ppermute | solution.py:527
  32.4 33.6 %collective-permute-start.10 = (bf16[512,256]{1,0:T(8,128)(2,1)}, bf16[512,256]{1,0:T(8,128)(2,1)S(1)}, u32[]{:S(2)}, u32[]{:S(2)}) collective-permute-start(bf16[512,256]{1,0:T(8,128)(2,1)} %cut.3), channel_id=1, source_target_pairs={{0,3},{1,2},{2,1},{3,0},{4,7},{5,6},{6,5},{7,4},{8,11},{9,10},{10,... | collective-permute-start | bytes 786440 | tf_op jit(solution)/shard_map/ppermute | solution.py:508
  34.0 51.8 %collective-permute-start.9 = (bf16[512,256]{1,0:T(8,128)(2,1)}, bf16[512,256]{1,0:T(8,128)(2,1)S(1)}, u32[]{:S(2)}, u32[]{:S(2)}) collective-permute-start(bf16[512,256]{1,0:T(8,128)(2,1)} %cut.3), channel_id=1, source_target_pairs={{0,2},{1,3},{2,0},{3,1},{4,6},{5,7},{6,4},{7,5},{8,10},{9,11},{10,... | collective-permute-start | bytes 786440 | tf_op jit(solution)/shard_map/ppermute | solution.py:508
  35.2 50.7 %collective-permute-start.8 = (bf16[512,256]{1,0:T(8,128)(2,1)}, bf16[512,256]{1,0:T(8,128)(2,1)S(1)}, u32[]{:S(2)}, u32[]{:S(2)}) collective-permute-start(bf16[512,256]{1,0:T(8,128)(2,1)} %cut.3), channel_id=1, source_target_pairs={{0,1},{1,0},{2,3},{3,2},{4,5},{5,4},{6,7},{7,6},{8,9},{9,8},{10,11... | collective-permute-start | bytes 786440 | tf_op jit(solution)/shard_map/ppermute | solution.py:508
  36.5 58.7 %collective-permute-start.4 = (bf16[2,64,512]{2,1,0:T(8,128)(2,1)S(1)}, bf16[2,64,512]{2,1,0:T(8,128)(2,1)S(1)}, u32[]{:S(2)}, u32[]{:S(2)}) collective-permute-start(bf16[2,64,512]{2,1,0:T(8,128)(2,1)S(1)} %copy-done.8), channel_id=1, source_target_pairs={{0,4},{4,0},{8,12},{12,8},{16,20},{20,16},{24,28},{28,24},{1,5},{5... | collective-permute-start | bytes 393224 | tf_op jit(solution)/shard_map/ppermute | solution.py:449
  66.0 22.3 %collective-permute-start.7 = (bf16[2,64,512]{2,1,0:T(8,128)(2,1)S(1)}, bf16[2,64,512]{2,1,0:T(8,128)(2,1)S(1)}, u32[]{:S(2)}, u32[]{:S(2)}) collective-permute-start(bf16[2,64,512]{2,1,0:T(8,128)(2,1)S(1)} %copy-done.10), channel_id=1, source_target_pairs={{0,4},{4,0},{8,12},{12,8},{16,20},{20,16},{24,28},{28,24},{1,5},{5... | collective-permute-start | bytes 393224 | tf_op jit(solution)/shard_map/ppermute | solution.py:449
  85.8 9.4 %collective-permute-start.6 = (bf16[2,64,512]{2,1,0:T(8,128)(2,1)S(1)}, bf16[2,64,512]{2,1,0:T(8,128)(2,1)S(1)}, u32[]{:S(2)}, u32[]{:S(2)}) collective-permute-start(bf16[2,64,512]{2,1,0:T(8,128)(2,1)S(1)} %copy-done.12), channel_id=1, source_target_pairs={{0,4},{4,0},{8,12},{12,8},{16,20},{20,16},{24,28},{28,24},{1,5},{5... | collective-permute-start | bytes 393224 | tf_op jit(solution)/shard_map/ppermute | solution.py:449
  85.9 9.3 %collective-permute-start.5 = (bf16[2,64,512]{2,1,0:T(8,128)(2,1)S(1)}, bf16[2,64,512]{2,1,0:T(8,128)(2,1)S(1)}, u32[]{:S(2)}, u32[]{:S(2)}) collective-permute-start(bf16[2,64,512]{2,1,0:T(8,128)(2,1)S(1)} %copy-done.14), channel_id=1, source_target_pairs={{0,4},{4,0},{8,12},{12,8},{16,20},{20,16},{24,28},{28,24},{1,5},{5... | collective-permute-start | bytes 393224 | tf_op jit(solution)/shard_map/ppermute | solution.py:449
  88.4 0.7 copy-start.15
  95.0 8.0 %copy-start.7 = (f32[8,128]{1,0:T(8,128)}, f32[8,128]{1,0:T(8,128)S(1)}, u32[]{:S(2)}) copy-start(f32[8,128]{1,0:T(8,128)S(1)} %get-tuple-element.46.refs_8_) | copy-start | bytes 12292
  95.0 15.3 %collective-permute-start.11 = (bf16[2,64,256]{2,1,0:T(8,128)(2,1)S(1)}, bf16[2,64,256]{2,1,0:T(8,128)(2,1)S(1)}, u32[]{:S(2)}, u32[]{:S(2)}) collective-permute-start(bf16[2,64,256]{2,1,0:T(8,128)(2,1)S(1)} %get-tuple-element.38), channel_id=1, source_target_pairs={{0,4},{4,0},{8,12},{12,8},{16,20},{20,16},{24,28},{28,24},{1,5},{5... | collective-permute-start | bytes 196616 | tf_op jit(solution)/shard_map/ppermute | solution.py:508
  95.2 0.7 copy-start.16
  95.2 0.7 copy-start.17
  95.2 0.7 copy-start.18
  103.0 27.6 %all-to-all-start.1 = ((bf16[8,3,2,64,256]{4,3,2,1,0:T(8,128)(2,1)}), bf16[8,3,2,64,256]{4,3,2,1,0:T(8,128)(2,1)S(1)}, u32[]{:S(2)}, u32[]{:S(2)}) async-start(bf16[8,3,2,64,256]{4,3,2,1,0:T(8,128)(2,1)} %after.6), calls=%async_computation.1 | async-start | bytes 3145728 | tf_op jit(solution)/shard_map/all_to_all | solution.py:555
  106.8 20.1 %collective-permute-start.12 = (bf16[2,64,256]{2,1,0:T(8,128)(2,1)S(1)}, bf16[2,64,256]{2,1,0:T(8,128)(2,1)S(1)}, u32[]{:S(2)}, u32[]{:S(2)}) collective-permute-start(bf16[2,64,256]{2,1,0:T(8,128)(2,1)S(1)} %get-tuple-element.39), channel_id=1, source_target_pairs={{0,8},{4,12},{8,0},{12,4},{16,24},{20,28},{24,16},{28,20},{1,9},{5... | collective-permute-start | bytes 196616 | tf_op jit(solution)/shard_map/ppermute | solution.py:508
  106.9 20.9 %collective-permute-start.13 = (bf16[2,64,256]{2,1,0:T(8,128)(2,1)S(1)}, bf16[2,64,256]{2,1,0:T(8,128)(2,1)S(1)}, u32[]{:S(2)}, u32[]{:S(2)}) collective-permute-start(bf16[2,64,256]{2,1,0:T(8,128)(2,1)S(1)} %get-tuple-element.40), channel_id=1, source_target_pairs={{0,12},{4,8},{8,4},{12,0},{16,28},{20,24},{24,20},{28,16},{1,13},{... | collective-permute-start | bytes 196616 | tf_op jit(solution)/shard_map/ppermute | solution.py:508
  108.4 19.5 %collective-permute-start.14 = (bf16[2,64,256]{2,1,0:T(8,128)(2,1)S(1)}, bf16[2,64,256]{2,1,0:T(8,128)(2,1)S(1)}, u32[]{:S(2)}, u32[]{:S(2)}) collective-permute-start(bf16[2,64,256]{2,1,0:T(8,128)(2,1)S(1)} %get-tuple-element.41), channel_id=1, source_target_pairs={{0,16},{4,20},{8,24},{12,28},{16,0},{20,4},{24,8},{28,12},{1,17},{... | collective-permute-start | bytes 196616 | tf_op jit(solution)/shard_map/ppermute | solution.py:508
  109.8 19.6 %collective-permute-start.15 = (bf16[2,64,256]{2,1,0:T(8,128)(2,1)S(1)}, bf16[2,64,256]{2,1,0:T(8,128)(2,1)S(1)}, u32[]{:S(2)}, u32[]{:S(2)}) collective-permute-start(bf16[2,64,256]{2,1,0:T(8,128)(2,1)S(1)} %get-tuple-element.42), channel_id=1, source_target_pairs={{0,20},{4,16},{8,28},{12,24},{16,4},{20,0},{24,12},{28,8},{1,21},{... | collective-permute-start | bytes 196616 | tf_op jit(solution)/shard_map/ppermute | solution.py:508
  110.3 20.3 %collective-permute-start.16 = (bf16[2,64,256]{2,1,0:T(8,128)(2,1)S(1)}, bf16[2,64,256]{2,1,0:T(8,128)(2,1)S(1)}, u32[]{:S(2)}, u32[]{:S(2)}) collective-permute-start(bf16[2,64,256]{2,1,0:T(8,128)(2,1)S(1)} %get-tuple-element.43), channel_id=1, source_target_pairs={{0,24},{4,28},{8,16},{12,20},{16,8},{20,12},{24,0},{28,4},{1,25},{... | collective-permute-start | bytes 196616 | tf_op jit(solution)/shard_map/ppermute | solution.py:508
  130.6 0.7 copy-start.6
  131.3 16.8 %copy-start.3 = (f32[1024,256]{1,0:T(8,128)S(1)}, f32[1024,256]{1,0:T(8,128)}, u32[]{:S(2)}) copy-start(f32[1024,256]{1,0:T(8,128)} %get-tuple-element.36.home_ref) | copy-start | bytes 3145732
  133.8 32.2 %copy-start.2 = (f32[1024,256]{1,0:T(8,128)S(1)}, f32[1024,256]{1,0:T(8,128)}, u32[]{:S(2)}) copy-start(f32[1024,256]{1,0:T(8,128)} %get-tuple-element.53.home_ref) | copy-start | bytes 3145732
  133.8 32.2 %all-to-all-start.2 = ((bf16[8,2,64,256]{3,2,1,0:T(8,128)(2,1)}), bf16[8,2,64,256]{3,2,1,0:T(8,128)(2,1)S(1)}, u32[]{:S(2)}, u32[]{:S(2)}) async-start(bf16[8,2,64,256]{3,2,1,0:T(8,128)(2,1)} %get-tuple-element.54), calls=%async_computation.2 | async-start | bytes 1048576 | tf_op jit(solution)/shard_map/all_to_all | solution.py:561
  138.8 9.2 %collective-permute-start.17 = (bf16[2,64,256]{2,1,0:T(8,128)(2,1)S(1)}, bf16[2,64,256]{2,1,0:T(8,128)(2,1)S(1)}, u32[]{:S(2)}, u32[]{:S(2)}) collective-permute-start(bf16[2,64,256]{2,1,0:T(8,128)(2,1)S(1)} %get-tuple-element.44), channel_id=1, source_target_pairs={{0,28},{4,24},{8,20},{12,16},{16,12},{20,8},{24,4},{28,0},{1,29},{... | collective-permute-start | bytes 196616 | tf_op jit(solution)/shard_map/ppermute | solution.py:508
  148.9 8.3 %collective-permute-start.18 = (bf16[256,256]{1,0:T(8,128)(2,1)S(1)}, bf16[256,256]{1,0:T(8,128)(2,1)S(1)}, u32[]{:S(2)}, u32[]{:S(2)}) collective-permute-start(bf16[256,256]{1,0:T(8,128)(2,1)S(1)} %get-tuple-element.50), channel_id=1, source_target_pairs={{0,1},{1,0},{2,3},{3,2},{4,5},{5,4},{6,7},{7,6},{8,9},{9,8},{10,11... | collective-permute-start | bytes 393224 | tf_op jit(solution)/shard_map/ppermute | solution.py:508
  152.4 9.6 %collective-permute-start.19 = (bf16[256,256]{1,0:T(8,128)(2,1)S(1)}, bf16[256,256]{1,0:T(8,128)(2,1)S(1)}, u32[]{:S(2)}, u32[]{:S(2)}) collective-permute-start(bf16[256,256]{1,0:T(8,128)(2,1)S(1)} %get-tuple-element.51), channel_id=1, source_target_pairs={{0,2},{1,3},{2,0},{3,1},{4,6},{5,7},{6,4},{7,5},{8,10},{9,11},{10,... | collective-permute-start | bytes 393224 | tf_op jit(solution)/shard_map/ppermute | solution.py:508
  152.5 13.6 %collective-permute-start.20 = (bf16[256,256]{1,0:T(8,128)(2,1)S(1)}, bf16[256,256]{1,0:T(8,128)(2,1)S(1)}, u32[]{:S(2)}, u32[]{:S(2)}) collective-permute-start(bf16[256,256]{1,0:T(8,128)(2,1)S(1)} %get-tuple-element.52), channel_id=1, source_target_pairs={{0,3},{1,2},{2,1},{3,0},{4,7},{5,6},{6,5},{7,4},{8,11},{9,10},{10,... | collective-permute-start | bytes 393224 | tf_op jit(solution)/shard_map/ppermute | solution.py:508
  167.5 15.6 %copy-start.4 = (s32[2]{0:T(128)S(1)}, s32[2]{0:T(128)}, u32[]{:S(2)}) copy-start(s32[2]{0:T(128)} %pad_add_fusion.side_ref) | copy-start | bytes 28
  167.5 15.6 %collective-permute-start.24 = (bf16[4,512,768]{2,1,0:T(8,128)(2,1)}, bf16[4,512,768]{2,1,0:T(8,128)(2,1)S(1)}, u32[]{:S(2)}, u32[]{:S(2)}) collective-permute-start(bf16[4,512,768]{2,1,0:T(8,128)(2,1)} %get-tuple-element.61.refs_8_), channel_id=1, source_target_pairs={{0,4},{4,0},{8,12},{12,8},{16,20},{20,16},{24,28},{28,24},{1,5},{5... | collective-permute-start | bytes 9437192 | tf_op jit(solution)/shard_map/ppermute | solution.py:573
  167.5 15.6 %collective-permute-start.25 = (bf16[4,512,256]{2,1,0:T(8,128)(2,1)}, bf16[4,512,256]{2,1,0:T(8,128)(2,1)S(1)}, u32[]{:S(2)}, u32[]{:S(2)}) collective-permute-start(bf16[4,512,256]{2,1,0:T(8,128)(2,1)} %get-tuple-element.62.refs_10_), channel_id=1, source_target_pairs={{0,4},{4,0},{8,12},{12,8},{16,20},{20,16},{24,28},{28,24},{1,5},{5... | collective-permute-start | bytes 3145736 | tf_op jit(solution)/shard_map/ppermute | solution.py:574
  168.0 6.4 %collective-permute-start.21 = (bf16[256,256]{1,0:T(8,128)(2,1)S(1)}, bf16[256,256]{1,0:T(8,128)(2,1)S(1)}, u32[]{:S(2)}, u32[]{:S(2)}) collective-permute-start(bf16[256,256]{1,0:T(8,128)(2,1)S(1)} %get-tuple-element.57), channel_id=1, source_target_pairs={{0,1},{1,0},{2,3},{3,2},{4,5},{5,4},{6,7},{7,6},{8,9},{9,8},{10,11... | collective-permute-start | bytes 393224 | tf_op jit(solution)/shard_map/ppermute | solution.py:508
  168.0 11.6 %collective-permute-start.22 = (bf16[256,256]{1,0:T(8,128)(2,1)S(1)}, bf16[256,256]{1,0:T(8,128)(2,1)S(1)}, u32[]{:S(2)}, u32[]{:S(2)}) collective-permute-start(bf16[256,256]{1,0:T(8,128)(2,1)S(1)} %get-tuple-element.58), channel_id=1, source_target_pairs={{0,2},{1,3},{2,0},{3,1},{4,6},{5,7},{6,4},{7,5},{8,10},{9,11},{10,... | collective-permute-start | bytes 393224 | tf_op jit(solution)/shard_map/ppermute | solution.py:508
  170.1 13.0 %collective-permute-start.23 = (bf16[256,256]{1,0:T(8,128)(2,1)S(1)}, bf16[256,256]{1,0:T(8,128)(2,1)S(1)}, u32[]{:S(2)}, u32[]{:S(2)}) collective-permute-start(bf16[256,256]{1,0:T(8,128)(2,1)S(1)} %get-tuple-element.59), channel_id=1, source_target_pairs={{0,3},{1,2},{2,1},{3,0},{4,7},{5,6},{6,5},{7,4},{8,11},{9,10},{10,... | collective-permute-start | bytes 393224 | tf_op jit(solution)/shard_map/ppermute | solution.py:508
  183.1 1.9 copy-start
  185.0 1.2 copy-start.1
  (1 other events, 0.6 us)
Sparse Core Ops, SparseCore 0:
  12.3 83.1 all-gather.2

commit v10 on v9

--- a/solution.py
+++ b/solution.py
@@ -245,7 +245,6 @@
     total = len(summary) * picks
     own = pl.BlockSpec((tokens_dev, HEAD_SIZE), lambda h: (0, first + h))
     pairs = tokens_dev * (WINDOW + TILE + total) * heads
-    weight = 8 if chunk == 0 else 64
     return pl.pallas_call(
         functools.partial(home_kernel, order=order),
         grid=(heads,),
@@ -261,7 +260,7 @@
         out_specs=[pl.BlockSpec((tokens_dev, HEAD_SIZE), lambda h: (0, h)), mark_spec()],
         out_shape=[jax.ShapeDtypeStruct((tokens_dev, heads * HEAD_SIZE), F32), MARK],
         compiler_params=params(60),
-        cost_estimate=cost(weight * pairs * HEAD_SIZE, 14 * tokens_dev * width, weight * pairs // 8),
+        cost_estimate=cost(64 * pairs * HEAD_SIZE, 14 * tokens_dev * width, 8 * pairs),
         name="home",
     )(place, queries, keys, values, rim, *summary, *waits)
 
@@ -362,84 +361,74 @@
         out_specs=[pl.BlockSpec(memory_space=pltpu.VMEM)] * (slots + 1),
         out_shape=[jax.ShapeDtypeStruct((size, width), BF16)] * slots + [MARK],
         compiler_params=params(24),
-        cost_estimate=cost(2 * tokens_dev * TILE * width, 8 * tokens_dev * width),
+        cost_estimate=cost(56 * tokens_dev * TILE * width, 8 * tokens_dev * width),
         name="combine",
     )(seat, home, *backs, *waits)
 
 
-def project_kernel(side_ref, *refs, slots, chunks):
-    moved_refs = refs[: slots * chunks]
-    mine_ref, other_ref, mine_last_ref, other_last_ref, o_ref, total_ref = refs[slots * chunks :]
-    part = moved_refs[0].shape[1]
-    half, last = mine_ref.shape[2], mine_last_ref.shape[2]
+def project_kernel(side_ref, *refs, slots, adds):
+    moved_refs, (mine_ref, other_ref), refs = refs[:slots], refs[slots : slots + 2], refs[slots + 2 :]
+    o_ref, mark_ref, total_ref = refs[-3:]
+    mark_ref[...] = jnp.zeros_like(mark_ref)
+    half = mine_ref.shape[2]
     phase, slot = pl.program_id(0), pl.program_id(1)
-
-    def add_up(weight_ref, begin, first):
-        size = weight_ref.shape[2]
-        here = slice(begin, begin + size)
+    here = pl.ds(pl.multiple_of((side_ref[0] ^ phase) * half, half), half)
+
+    def add_up(weight_ref):
         for one in range(slots):
 
             @pl.when(slot == one)
             def _():
-                total = None if one == 0 else total_ref[:, here]
-                for chunk in range(chunks):
-                    rows = weight_ref[0, chunk * part : (chunk + 1) * part]
-                    product = dot(moved_refs[chunk * slots + one][...], rows)
-                    total = product if total is None else total + product
+                total = dot(moved_refs[one][...], weight_ref[0])
+                if one > 0:
+                    total = total + total_ref[...]
+                elif adds:
+                    total = total + refs[0][:, here]
                 if one < slots - 1:
-                    total_ref[:, here] = total
+                    total_ref[...] = total
                 else:
-                    o_ref[:, pl.ds(pl.multiple_of(first, size), size)] = total.astype(BF16)
+                    o_ref[:, here] = total.astype(o_ref.dtype)
 
     @pl.when(phase == 0)
     def _():
-        add_up(mine_ref, 0, side_ref[0] * half)
+        add_up(mine_ref)
 
     @pl.when(phase == 1)
     def _():
-        add_up(other_ref, 0, (1 - side_ref[0]) * half)
-
-    @pl.when(phase == 2)
-    def _():
-        add_up(mine_last_ref, 0, 2 * half + side_ref[0] * last)
-        add_up(other_last_ref, last, 2 * half + (1 - side_ref[0]) * last)
-
-
-def project(side, moved, mine, other, mine_last, other_last):
-    chunks, slots = len(moved), len(moved[0])
-    tokens, part = moved[0][0].shape
-    width, half = mine.shape[1:]
-    last = mine_last.shape[2]
+        add_up(other_ref)
+
+
+def project(side, moved, mine, other, chunk, before, dtype):
+    slots = len(moved)
+    tokens, part = moved[0].shape
+    half = mine.shape[2]
 
     def mine_group(p, s, side):
-        return (side[1] ^ jnp.where(p == 0, s, slots - 1), 0, 0)
+        return (side[1] ^ jnp.where(p == 0, s, slots - 1), chunk, 0)
 
     def other_group(p, s, side):
-        return (side[1] ^ jnp.where(p == 0, 0, jnp.where(p == 1, s, slots - 1)), 0, 0)
-
-    def last_slot(p, s, side):
-        return (jnp.where(p == 2, s, 0), 0, 0)
-
-    total = 2 * (half + last)
-    return pl.pallas_call(
-        functools.partial(project_kernel, slots=slots, chunks=chunks),
+        return (side[1] ^ jnp.where(p == 0, 0, s), chunk, 0)
+
+    whole = pl.BlockSpec((tokens, 2 * half), lambda p, s, side: (0, 0))
+    return pl.pallas_call(
+        functools.partial(project_kernel, slots=slots, adds=len(before) > 0),
         grid_spec=pltpu.PrefetchScalarGridSpec(
             num_scalar_prefetch=1,
-            grid=(3, slots),
-            in_specs=[pl.BlockSpec((tokens, part), lambda p, s, side: (0, 0))] * (slots * chunks)
-            + [pl.BlockSpec((1, width, half), mine_group)]
-            + [pl.BlockSpec((1, width, half), other_group)]
-            + [pl.BlockSpec((1, width, last), last_slot)] * 2,
-            out_specs=pl.BlockSpec((tokens, total), lambda p, s, side: (0, 0)),
-            scratch_shapes=[pltpu.VMEM((tokens, max(half, 2 * last)), F32)],
+            grid=(2, slots),
+            in_specs=[pl.BlockSpec((tokens, part), lambda p, s, side: (0, 0))] * slots
+            + [pl.BlockSpec((1, part, half), mine_group)]
+            + [pl.BlockSpec((1, part, half), other_group)]
+            + [whole] * len(before),
+            out_specs=[whole, mark_spec()],
+            scratch_shapes=[pltpu.VMEM((tokens, half), F32)],
         ),
-        out_shape=jax.ShapeDtypeStruct((tokens, total), BF16),
+        out_shape=[jax.ShapeDtypeStruct((tokens, 2 * half), dtype), MARK],
         compiler_params=params(24),
         cost_estimate=cost(
-            2 * slots * tokens * width * total, 2 * slots * width * (total + tokens)
+            4 * slots * tokens * part * half, 2 * slots * part * (2 * half + tokens)
         ),
         name="project",
-    )(side, *[slab for slabs in moved for slab in slabs], mine, other, mine_last, other_last)
+    )(side, *moved, mine, other, *before)
 
 
 def gather_ctx(rows):
@@ -508,19 +497,16 @@
             moved.append(lax.ppermute(slabs[slot], axis, pairs))
         return moved
 
-    rim, picked = edges(keys, values, ())
+    weight_half = cut(sides, out_weight, out_weight.shape[1] // 2, 0, ())
+    mine = lax.all_gather(weight_half, "head", axis=0)
+    rim, picked = edges(keys, values, (weight_half,))
     between, within, order = gather_ctx(picked)
     summary = between + within
-    eighth = out_weight.shape[1] // 8
-    weight_half = cut(sides, out_weight, 3 * eighth, 0, (picked,))
-    mine = lax.all_gather(weight_half, "head", axis=0)
     if ctx > STRIDE:
         stride_out = stride_general(queries, keys, values)
         sends = []
     else:
         sends = [prepare(queries, keys, values, ctx, 0, chunks, (weight_half,))]
-    weight_last = cut(sides, out_weight, eighth, 6, sends)
-    mine_last = jnp.stack(exchange([weight_last] * groups, "head"))
     (rim,) = after([rim], (*between[1:], *sends))
     if sends:
         sends = list(after(sends, (rim,)))
@@ -547,7 +533,7 @@
     else:
         seats = jnp.stack([seat, place.astype(jnp.int32)])
         seats = jnp.stack([seat, place.astype(jnp.int32)])
-        sections, mark = home(0, (mine_last,))
+        sections, mark = home(0, ())
         homes, backs, waits = [sections], [], ()
         if chunks > 1:
             sends[1:] = list(after(sends[1:], (mark,)))
@@ -564,15 +550,18 @@
             for later in range(1, chunks) if chunk == 0 else ():
                 sections, mark = home(later, waits)
                 homes.append(sections)
-                waits = (mark, *backs[0][1:-1])
+                waits = (mark,)
         for chunk in range(chunks):
             *slabs, mark = combine(seats, homes[chunk], backs[chunk], groups, ctx, waits)
             moved.append(exchange(slabs, "head"))
-            waits = (mark, *moved[-1][1:])
-    held, held_last = after([mine, mine_last], (mark,))
+            waits = (mark, *moved[-1][1:3])
+    (held,) = after([mine], (mark,))
     other = lax.ppermute(held, "ctx", sibling)
-    other_last = lax.ppermute(held_last, "ctx", sibling)
-    return project(sides, moved, held, other, held_last, other_last)
+    total = ()
+    for chunk in range(chunks):
+        dtype = BF16 if chunk == chunks - 1 else F32
+        *total, _ = project(sides, moved[chunk], held, other, chunk, total, dtype)
+    return total[0]
 
 
 def solution(mesh):

time: 202 us -> 134 us (0.66)
  waiting for transfers between devices: 90.8 us -> 34.5 us
  starting transfers between devices: 40.6 us -> 36 us
  local copies, waits for them, and re-layouts: 9.36 us -> 6.95 us
  other arithmetic: 2.74 us -> 0.69 us
    ppermute x16 -> x13, waiting for transfers between devices: 90.8 us -> 21.1 us  [exchange(): moved.append(lax.ppermute(slabs[slot], axis, pairs))]
    ppermute x1, waiting for transfers between devices: 0.01 us -> 9.29 us  [body(): before = lax.ppermute(rim, 'ctx', [(i, i + 1) for i in range(ctx - 1)])]
    ppermute x16 -> x13, starting transfers between devices: 18.9 us -> 15.8 us  [exchange(): moved.append(lax.ppermute(slabs[slot], axis, pairs))]
    all_to_all x2, waiting for transfers between devices: 0.01 us -> 2.58 us  [body(): lax.all_to_all(send, 'ctx', split_axis=0, concat_axis=0, tiled=True)]
    unnamed x39 -> x32, local copies, waits for them, and re-layouts: 9.36 us -> 6.95 us
    pallas_call x2 -> x1, Pallas kernels: 5.22 us -> 2.93 us  [cut(): pl.pallas_call(cut_kernel, grid_spec=pltpu.PrefetchScalarGridSpec(num_sca...]
    another operation x1 -> x0, other arithmetic: 2.06 us -> none  [body(): mine_last = jnp.stack(exchange([weight_last] * groups, 'head'))]
    pallas_call x1 -> x2, Pallas kernels: 6.89 us -> 8.09 us  [project(): pl.pallas_call(functools.partial(project_kernel, slots=slots, adds=len(be...]
  transfers between devices with their start and end apart: 30 -> 26, of which waited for: 13 -> 9; matrix products, arithmetic and copies ran while one was open for 3% -> 0% of each run, Pallas kernels for 15% -> 26%
where the time goes in v10:
time: 134 us
  Pallas kernels  42 us (31%)
  starting transfers between devices  36 us (27%)
  waiting for transfers between devices  34.5 us (26%)
  between operations  13.6 us (10%)
  local copies, waits for them, and re-layouts  6.95 us (5%)
    ppermute x13, waiting for transfers between devices, exchange(): moved.append(lax.ppermute(slabs[slot], axis, pairs))  21.1 us
    ppermute x13, starting transfers between devices, exchange(): moved.append(lax.ppermute(slabs[slot], axis, pairs))  15.8 us
    pallas_call x2, Pallas kernels, home_sections(): pl.pallas_call(functools.partial(home_kernel, order=order), grid=(heads,)...  14.2 us
    ppermute x1, waiting for transfers between devices, body(): before = lax.ppermute(rim, 'ctx', [(i, i + 1) for i in range(ctx - 1)])  9.29 us
    pallas_call x2, Pallas kernels, prepare(): pl.pallas_call(prep_kernel, grid=(tokens_dev // TILE,), in_specs=[pl.Bloc...  8.53 us
    all_to_all x2, starting transfers between devices, body(): lax.all_to_all(send, 'ctx', split_axis=0, concat_axis=0, tiled=True)  8.32 us
    pallas_call x2, Pallas kernels, project(): pl.pallas_call(functools.partial(project_kernel, slots=slots, adds=len(be...  8.09 us
    unnamed x32, local copies, waits for them, and re-layouts  6.95 us
  transfers between devices with their start and end apart: 26, of which 9 were waited for; matrix products, arithmetic and copies ran while one was open for 0% of the time, Pallas kernels for 26%

profile of v10, /device:TPU:10, one launch (start us, length us, event | category | flops | bytes accessed | tf_op | source)
XLA Modules:
  0.0 133.8 jit_solution(7162430551414631)
XLA Ops:
  6.5 0.6 pad_add_fusion.side_ref
  7.2 2.9 %cut.1.refs_0_ = bf16[512,1024]{1,0:T(8,128)(2,1)} custom-call(s32[2]{0:T(128)} %pad_add_fusion.side_ref, bf16[512,2048]{1,0:T(8,128)(2,1)} %weight_ref.1), custom_call_target="tpu_custom_call" | custom-call | bytes 2097152 | tf_op jit(solution)/shard_map/cut/pallas_call | solution.py:152
  10.1 2.3 %edges.1 = (bf16[2,512,512]{2,1,0:T(8,128)(2,1)}, bf16[2,64,512]{2,1,0:T(8,128)(2,1)}) custom-call(bf16[1024,512]{1,0:T(8,128)(2,1)} %k_ref.9, bf16[1024,512]{1,0:T(8,128)(2,1)} %v_ref.9, bf16[8,128,512]{2,1,0:T(8,128)(2,1)} %bitcast.7, bf16[8,128,512]{2,1,0:T(8,128)(2,1)} %bitcast.8, bf16[512,1024]{1,0:T(8,128)(2,1)} %cut.1.refs_0_), custom_call_target="tpu_custom_call" | custom-call | bytes 2097152 | tf_op jit(solution)/shard_map/edges/pallas_call | solution.py:122
  12.4 1.5 %collective-permute-start.2 = (bf16[2,64,512]{2,1,0:T(8,128)(2,1)}, bf16[2,64,512]{2,1,0:T(8,128)(2,1)S(1)}, u32[]{:S(2)}, u32[]{:S(2)}) collective-permute-start(bf16[2,64,512]{2,1,0:T(8,128)(2,1)} %get-tuple-element.35.refs_0_), channel_id=1, source_target_pairs={{0,24},{4,28},{8,16},{12,20},{16,8},{20,12},{24,0},{28,4},{1,25},{... | collective-permute-start | bytes 393224 | tf_op jit(solution)/shard_map/ppermute | solution.py:438
  13.9 0.5 collective-permute-start.1
  14.4 1.5 %collective-permute-start = (bf16[2,64,512]{2,1,0:T(8,128)(2,1)}, bf16[2,64,512]{2,1,0:T(8,128)(2,1)S(1)}, u32[]{:S(2)}, u32[]{:S(2)}) collective-permute-start(bf16[2,64,512]{2,1,0:T(8,128)(2,1)} %get-tuple-element.35.refs_0_), channel_id=1, source_target_pairs={{0,8},{4,12},{8,0},{12,4},{16,24},{20,28},{24,16},{28,20},{1,9},{5... | collective-permute-start | bytes 393224 | tf_op jit(solution)/shard_map/ppermute | solution.py:438
  15.9 4.3 %prepare.2.refs_4_.refs_0_ = bf16[8,3,2,64,256]{4,3,2,1,0:T(8,128)(2,1)} custom-call(bf16[1024,512]{1,0:T(8,128)(2,1)} %q_ref.7, bf16[1024,512]{1,0:T(8,128)(2,1)} %k_ref.9, bf16[1024,512]{1,0:T(8,128)(2,1)} %v_ref.9, bf16[512,1024]{1,0:T(8,128)(2,1)} %cut.1.refs_0_), custom_call_target="tpu_custom_call" | custom-call | flops 402653184 | bytes 3145728 | tf_op jit(solution)/shard_map/prepare/pallas_call | solution.py:181
  20.2 1.4 %collective-permute-done.1.refs_2_ = bf16[2,64,512]{2,1,0:T(8,128)(2,1)S(1)} collective-permute-done((bf16[2,64,512]{2,1,0:T(8,128)(2,1)}, bf16[2,64,512]{2,1,0:T(8,128)(2,1)S(1)}, u32[]{:S(2)}, u32[]{:S(2)}) %collective-permute-start.1) | collective-permute-done | bytes 131104 | tf_op jit(solution)/shard_map/ppermute | solution.py:438
  21.6 0.5 copy-done.8
  22.3 2.0 %collective-permute-start.3 = (bf16[2,512,512]{2,1,0:T(8,128)(2,1)}, bf16[2,512,512]{2,1,0:T(8,128)(2,1)S(1)}, u32[]{:S(2)}, u32[]{:S(2)}) collective-permute-start(bf16[2,512,512]{2,1,0:T(8,128)(2,1)} %after.4.refs_1_), channel_id=1, source_target_pairs={{0,4},{4,8},{8,12},{12,16},{16,20},{20,24},{24,28},{1,5},{5,9},{9,... | collective-permute-start | bytes 3145736 | tf_op jit(solution)/shard_map/ppermute | solution.py:513
  24.3 1.6 %collective-permute-start.7 = (bf16[2,64,512]{2,1,0:T(8,128)(2,1)}, bf16[2,64,512]{2,1,0:T(8,128)(2,1)S(1)}, u32[]{:S(2)}, u32[]{:S(2)}) collective-permute-start(bf16[2,64,512]{2,1,0:T(8,128)(2,1)} %copy-done.7), channel_id=1, source_target_pairs={{0,4},{4,0},{8,12},{12,8},{16,20},{20,16},{24,28},{28,24},{1,5},{5... | collective-permute-start | bytes 393224 | tf_op jit(solution)/shard_map/ppermute | solution.py:438
  26.0 0.4 collective-permute-start.6
  26.6 4.1 %all-to-all-start = ((bf16[8,3,2,64,256]{4,3,2,1,0:T(8,128)(2,1)}), bf16[8,3,2,64,256]{4,3,2,1,0:T(8,128)(2,1)S(1)}, u32[]{:S(2)}, u32[]{:S(2)}) async-start(bf16[8,3,2,64,256]{4,3,2,1,0:T(8,128)(2,1)} %after.5), calls=%async_computation | async-start | bytes 3145728 | tf_op jit(solution)/shard_map/all_to_all | solution.py:541
  30.7 0.7 copy-done.10
  31.4 4.2 %prepare.3.refs_0_ = bf16[8,3,2,64,256]{4,3,2,1,0:T(8,128)(2,1)} custom-call(bf16[1024,512]{1,0:T(8,128)(2,1)} %q_ref.7, bf16[1024,512]{1,0:T(8,128)(2,1)} %k_ref.9, bf16[1024,512]{1,0:T(8,128)(2,1)} %v_ref.9, bf16[2,64,512]{2,1,0:T(8,128)(2,1)} %copy-done.10), custom_call_target="tpu_custom_call" | custom-call | flops 402653184 | bytes 3145728 | tf_op jit(solution)/shard_map/prepare/pallas_call | solution.py:181
  35.6 9.3 %collective-permute-done.3.rim_ref = bf16[2,512,512]{2,1,0:T(8,128)(2,1)S(1)} collective-permute-done((bf16[2,512,512]{2,1,0:T(8,128)(2,1)}, bf16[2,512,512]{2,1,0:T(8,128)(2,1)S(1)}, u32[]{:S(2)}, u32[]{:S(2)}) %collective-permute-start.3) | collective-permute-done | bytes 1048608 | tf_op jit(solution)/shard_map/ppermute | solution.py:513
  44.9 0.9 copy-done.11
  45.9 7.1 %home.3 = (f32[1024,256]{1,0:T(8,128)}, f32[8,128]{1,0:T(8,128)}) custom-call(s32[1]{0:T(128)} %bitcast.2.place_ref, bf16[1024,512]{1,0:T(8,128)(2,1)} %q_ref.7, bf16[1024,512]{1,0:T(8,128)(2,1)} %k_ref.9, bf16[1024,512]{1,0:T(8,128)(2,1)} %v_ref.9, bf16[2,512,512]{2,1,0:T(8,128)(2,1)} %copy-done.11, bf16[2,64,512]{2,1,0:T(8,128)(2,1)} %get-tuple-element.35.refs_0_, ...), custom_call_target="tpu_custom_call" | custom-call | flops 21474836480 | bytes 7340032 | tf_op jit(solution)/shard_map/home/pallas_call | solution.py:248
  53.0 2.6 %all-to-all-done.x_ref = bf16[8,3,2,64,256]{4,3,2,1,0:T(8,128)(2,1)S(1)} async-done(((bf16[8,3,2,64,256]{4,3,2,1,0:T(8,128)(2,1)}), bf16[8,3,2,64,256]{4,3,2,1,0:T(8,128)(2,1)S(1)}, u32[]{:S(2)}, u32[]{:S(2)}) %all-to-all-start) | async-done | bytes 1572896 | tf_op jit(solution)/shard_map/all_to_all | solution.py:541
  55.6 4.2 %all-to-all-start.1 = ((bf16[8,3,2,64,256]{4,3,2,1,0:T(8,128)(2,1)}), bf16[8,3,2,64,256]{4,3,2,1,0:T(8,128)(2,1)S(1)}, u32[]{:S(2)}, u32[]{:S(2)}) async-start(bf16[8,3,2,64,256]{4,3,2,1,0:T(8,128)(2,1)} %after.6), calls=%async_computation.1 | async-start | bytes 3145728 | tf_op jit(solution)/shard_map/all_to_all | solution.py:541
  59.8 1.8 %stride.2 = (bf16[2,64,256]{2,1,0:T(8,128)(2,1)S(1)}, bf16[2,64,256]{2,1,0:T(8,128)(2,1)S(1)}, bf16[2,64,256]{2,1,0:T(8,128)(2,1)S(1)}, bf16[2,64,256]{2,1,0:T(8...) custom-call(s32[1]{0:T(128)} %bitcast.2.place_ref, ...), custom_call_target="tpu_custom_call" | custom-call | flops 805306368 | bytes 2097152 | tf_op jit(solution)/shard_map/stride/pallas_call | solution.py:311
  61.8 0.4 collective-permute-start.9
  62.2 1.4 %collective-permute-start.10 = (bf16[2,64,256]{2,1,0:T(8,128)(2,1)S(1)}, bf16[2,64,256]{2,1,0:T(8,128)(2,1)S(1)}, u32[]{:S(2)}, u32[]{:S(2)}) collective-permute-start(bf16[2,64,256]{2,1,0:T(8,128)(2,1)S(1)} %get-tuple-element.45), channel_id=1, source_target_pairs={{0,12},{4,8},{8,4},{12,0},{16,28},{20,24},{24,20},{28,16},{1,13},{... | collective-permute-start | bytes 196616 | tf_op jit(solution)/shard_map/ppermute | solution.py:497
  63.6 1.5 %collective-permute-start.11 = (bf16[2,64,256]{2,1,0:T(8,128)(2,1)S(1)}, bf16[2,64,256]{2,1,0:T(8,128)(2,1)S(1)}, u32[]{:S(2)}, u32[]{:S(2)}) collective-permute-start(bf16[2,64,256]{2,1,0:T(8,128)(2,1)S(1)} %get-tuple-element.46), channel_id=1, source_target_pairs={{0,16},{4,20},{8,24},{12,28},{16,0},{20,4},{24,8},{28,12},{1,17},{... | collective-permute-start | bytes 196616 | tf_op jit(solution)/shard_map/ppermute | solution.py:497
  65.0 0.3 collective-permute-start.12
  65.4 7.1 %home.2 = (f32[1024,256]{1,0:T(8,128)}, f32[8,128]{1,0:T(8,128)}) custom-call(s32[1]{0:T(128)} %bitcast.2.place_ref, bf16[1024,512]{1,0:T(8,128)(2,1)} %q_ref.7, bf16[1024,512]{1,0:T(8,128)(2,1)} %k_ref.9, bf16[1024,512]{1,0:T(8,128)(2,1)} %v_ref.9, bf16[2,512,512]{2,1,0:T(8,128)(2,1)} %copy-done.11, bf16[2,64,512]{2,1,0:T(8,128)(2,1)} %get-tuple-element.35.refs_0_, ...), custom_call_target="tpu_custom_call" | custom-call | flops 21474836480 | bytes 7340032 | tf_op jit(solution)/shard_map/home/pallas_call | solution.py:248
  72.5 1.7 %collective-permute-start.13 = (bf16[2,64,256]{2,1,0:T(8,128)(2,1)S(1)}, bf16[2,64,256]{2,1,0:T(8,128)(2,1)S(1)}, u32[]{:S(2)}, u32[]{:S(2)}) collective-permute-start(bf16[2,64,256]{2,1,0:T(8,128)(2,1)S(1)} %get-tuple-element.48), channel_id=1, source_target_pairs={{0,24},{4,28},{8,16},{12,20},{16,8},{20,12},{24,0},{28,4},{1,25},{... | collective-permute-start | bytes 196616 | tf_op jit(solution)/shard_map/ppermute | solution.py:497
  74.2 5.8 %collective-permute-done.9.refs_2_ = bf16[2,64,256]{2,1,0:T(8,128)(2,1)S(1)} collective-permute-done((bf16[2,64,256]{2,1,0:T(8,128)(2,1)S(1)}, bf16[2,64,256]{2,1,0:T(8,128)(2,1)S(1)}, u32[]{:S(2)}, u32[]{:S(2)}) %collective-permute-start.9) | collective-permute-done | bytes 65568 | tf_op jit(solution)/shard_map/ppermute | solution.py:497
  79.9 1.7 %collective-permute-start.14 = (bf16[2,64,256]{2,1,0:T(8,128)(2,1)S(1)}, bf16[2,64,256]{2,1,0:T(8,128)(2,1)S(1)}, u32[]{:S(2)}, u32[]{:S(2)}) collective-permute-start(bf16[2,64,256]{2,1,0:T(8,128)(2,1)S(1)} %get-tuple-element.49), channel_id=1, source_target_pairs={{0,28},{4,24},{8,20},{12,16},{16,12},{20,8},{24,4},{28,0},{1,29},{... | collective-permute-start | bytes 196616 | tf_op jit(solution)/shard_map/ppermute | solution.py:497
  81.7 0.7 copy-done.5
  82.3 2.5 %stride.3 = (bf16[8,2,64,256]{3,2,1,0:T(8,128)(2,1)}, f32[8,128]{1,0:T(8,128)S(1)}) custom-call(s32[1]{0:T(128)} %bitcast.2.place_ref, bf16[8,3,2,64,256]{4,3,2,1,0:T(8,128)(2,1)S(1)} %all-to-all-done.1.x_ref, f32[8,128]{1,0:T(8,128)S(1)} %copy-done.5), custom_call_target="tpu_custom_call" | custom-call | flops 805306368 | bytes 2097152 | tf_op jit(solution)/shard_map/stride/pallas_call | solution.py:311
  84.9 4.1 %all-to-all-start.2 = ((bf16[8,2,64,256]{3,2,1,0:T(8,128)(2,1)}), bf16[8,2,64,256]{3,2,1,0:T(8,128)(2,1)S(1)}, u32[]{:S(2)}, u32[]{:S(2)}) async-start(bf16[8,2,64,256]{3,2,1,0:T(8,128)(2,1)} %get-tuple-element.40), calls=%async_computation.2 | async-start | bytes 1048576 | tf_op jit(solution)/shard_map/all_to_all | solution.py:547
  89.1 1.2 copy-done.4
  90.3 0.8 combine.2
  91.1 0.5 collective-permute-start.15
  91.7 2.6 %collective-permute-start.16 = (bf16[256,256]{1,0:T(8,128)(2,1)S(1)}, bf16[256,256]{1,0:T(8,128)(2,1)S(1)}, u32[]{:S(2)}, u32[]{:S(2)}) collective-permute-start(bf16[256,256]{1,0:T(8,128)(2,1)S(1)} %get-tuple-element.53), channel_id=1, source_target_pairs={{0,2},{1,3},{2,0},{3,1},{4,6},{5,7},{6,4},{7,5},{8,10},{9,11},{10,... | collective-permute-start | bytes 393224 | tf_op jit(solution)/shard_map/ppermute | solution.py:497
  94.2 3.8 %collective-permute-done.15.refs_2_.refs_1_ = bf16[256,256]{1,0:T(8,128)(2,1)S(1)} collective-permute-done((bf16[256,256]{1,0:T(8,128)(2,1)S(1)}, bf16[256,256]{1,0:T(8,128)(2,1)S(1)}, u32[]{:S(2)}, u32[]{:S(2)}) %collective-permute-start.15) | collective-permute-done | bytes 131104 | tf_op jit(solution)/shard_map/ppermute | solution.py:497
  98.0 3.2 %collective-permute-done.16.refs_3_.refs_2_ = bf16[256,256]{1,0:T(8,128)(2,1)S(1)} collective-permute-done((bf16[256,256]{1,0:T(8,128)(2,1)S(1)}, bf16[256,256]{1,0:T(8,128)(2,1)S(1)}, u32[]{:S(2)}, u32[]{:S(2)}) %collective-permute-start.16) | collective-permute-done | bytes 131104 | tf_op jit(solution)/shard_map/ppermute | solution.py:497
  101.3 0.9 combine.3
  102.1 0.6 copy-done.2
  102.7 0.5 collective-permute-start.21
  103.3 3.6 %collective-permute-start.17 = (bf16[256,256]{1,0:T(8,128)(2,1)S(1)}, bf16[256,256]{1,0:T(8,128)(2,1)S(1)}, u32[]{:S(2)}, u32[]{:S(2)}) collective-permute-start(bf16[256,256]{1,0:T(8,128)(2,1)S(1)} %get-tuple-element.55), channel_id=1, source_target_pairs={{0,1},{1,0},{2,3},{3,2},{4,5},{5,4},{6,7},{7,6},{8,9},{9,8},{10,11... | collective-permute-start | bytes 393224 | tf_op jit(solution)/shard_map/ppermute | solution.py:497
  106.9 1.5 %collective-permute-start.19 = (bf16[256,256]{1,0:T(8,128)(2,1)S(1)}, bf16[256,256]{1,0:T(8,128)(2,1)S(1)}, u32[]{:S(2)}, u32[]{:S(2)}) collective-permute-start(bf16[256,256]{1,0:T(8,128)(2,1)S(1)} %get-tuple-element.57), channel_id=1, source_target_pairs={{0,3},{1,2},{2,1},{3,0},{4,7},{5,6},{6,5},{7,4},{8,11},{9,10},{10,... | collective-permute-start | bytes 393224 | tf_op jit(solution)/shard_map/ppermute | solution.py:497
  108.3 3.6 %collective-permute-done.21.refs_3_ = bf16[256,256]{1,0:T(8,128)(2,1)S(1)} collective-permute-done((bf16[256,256]{1,0:T(8,128)(2,1)S(1)}, bf16[256,256]{1,0:T(8,128)(2,1)S(1)}, u32[]{:S(2)}, u32[]{:S(2)}) %collective-permute-start.21) | collective-permute-done | bytes 131104 | tf_op jit(solution)/shard_map/ppermute | solution.py:497
  111.9 2.2 %copy-done = bf16[4,512,1024]{2,1,0:T(8,128)(2,1)S(1)} copy-done((bf16[4,512,1024]{2,1,0:T(8,128)(2,1)S(1)}, bf16[4,512,1024]{2,1,0:T(8,128)(2,1)}, u32[]{:S(2)}) %copy-start) | copy-done | bytes 4194328
  114.1 3.8 %project.2 = (f32[256,2048]{1,0:T(8,128)S(1)}, f32[8,128]{1,0:T(8,128)}) custom-call(s32[2]{0:T(128)S(1)} %copy-done.1, bf16[256,256]{1,0:T(8,128)(2,1)S(1)} %get-tuple-element.59.refs_0_, bf16[256,256]{1,0:T(8,128)(2,1)S(1)} %collective-permute-done.15.refs_2_.refs_1_, bf16[256,256]{1,0:T(8,128)(2,1)S(1)} %collective-permute-done.16.refs_3_.refs_2_, ...), custom_call_target="tpu_custom_call" | custom-call | flops 1073741824 | bytes 4718592 | tf_op jit(solution)/shard_map/project/pallas_call | solution.py:413
  118.0 4.7 %collective-permute-done.19.refs_3_ = bf16[256,256]{1,0:T(8,128)(2,1)S(1)} collective-permute-done((bf16[256,256]{1,0:T(8,128)(2,1)S(1)}, bf16[256,256]{1,0:T(8,128)(2,1)S(1)}, u32[]{:S(2)}, u32[]{:S(2)}) %collective-permute-start.19) | collective-permute-done | bytes 131104 | tf_op jit(solution)/shard_map/ppermute | solution.py:497
  122.7 4.3 %project.3 = (bf16[256,2048]{1,0:T(8,128)(2,1)}, f32[8,128]{1,0:T(8,128)}) custom-call(s32[2]{0:T(128)S(1)} %copy-done.1, bf16[256,256]{1,0:T(8,128)(2,1)S(1)} %get-tuple-element.54.refs_0_, bf16[256,256]{1,0:T(8,128)(2,1)S(1)} %collective-permute-done.17.refs_1_, bf16[256,256]{1,0:T(8,128)(2,1)S(1)} %collective-permute-done.18.refs_2_, ...), custom_call_target="tpu_custom_call" | custom-call | flops 1073741824 | bytes 4718592 | tf_op jit(solution)/shard_map/project/pallas_call | solution.py:413
  (55 shorter events, 0.8 us)
Async XLA Ops:
  6.5 96.2 %all-gather.3.cloned.1.call-start = ((), (), s32[]{:S(2)}) async-start(), calls=%async_computation.3 | async-start | bytes 5242880 | tf_op jit(solution)/shard_map/all_gather | solution.py:501
  12.4 7.8 %collective-permute-start.2 = (bf16[2,64,512]{2,1,0:T(8,128)(2,1)}, bf16[2,64,512]{2,1,0:T(8,128)(2,1)S(1)}, u32[]{:S(2)}, u32[]{:S(2)}) collective-permute-start(bf16[2,64,512]{2,1,0:T(8,128)(2,1)} %get-tuple-element.35.refs_0_), channel_id=1, source_target_pairs={{0,24},{4,28},{8,16},{12,20},{16,8},{20,12},{24,0},{28,4},{1,25},{... | collective-permute-start | bytes 393224 | tf_op jit(solution)/shard_map/ppermute | solution.py:438
  13.9 7.7 %collective-permute-start.1 = (bf16[2,64,512]{2,1,0:T(8,128)(2,1)}, bf16[2,64,512]{2,1,0:T(8,128)(2,1)S(1)}, u32[]{:S(2)}, u32[]{:S(2)}) collective-permute-start(bf16[2,64,512]{2,1,0:T(8,128)(2,1)} %get-tuple-element.35.refs_0_), channel_id=1, source_target_pairs={{0,16},{4,20},{8,24},{12,28},{16,0},{20,4},{24,8},{28,12},{1,17},{... | collective-permute-start | bytes 393224 | tf_op jit(solution)/shard_map/ppermute | solution.py:438
  14.4 7.3 %collective-permute-start = (bf16[2,64,512]{2,1,0:T(8,128)(2,1)}, bf16[2,64,512]{2,1,0:T(8,128)(2,1)S(1)}, u32[]{:S(2)}, u32[]{:S(2)}) collective-permute-start(bf16[2,64,512]{2,1,0:T(8,128)(2,1)} %get-tuple-element.35.refs_0_), channel_id=1, source_target_pairs={{0,8},{4,12},{8,0},{12,4},{16,24},{20,28},{24,16},{28,20},{1,9},{5... | collective-permute-start | bytes 393224 | tf_op jit(solution)/shard_map/ppermute | solution.py:438
  20.2 1.5 %copy-start.7 = (bf16[2,64,512]{2,1,0:T(8,128)(2,1)}, bf16[2,64,512]{2,1,0:T(8,128)(2,1)S(1)}, u32[]{:S(2)}) copy-start(bf16[2,64,512]{2,1,0:T(8,128)(2,1)S(1)} %collective-permute-done.2.refs_3_) | copy-start | bytes 393220
  21.5 0.7 copy-start.8
  21.6 0.6 copy-start.9
  22.3 3.7 %copy-start.12 = (bf16[2,64,512]{2,1,0:T(8,128)(2,1)S(1)}, bf16[2,64,512]{2,1,0:T(8,128)(2,1)}, u32[]{:S(2)}) copy-start(bf16[2,64,512]{2,1,0:T(8,128)(2,1)} %get-tuple-element.35.refs_0_) | copy-start | bytes 393220
  22.3 22.6 %collective-permute-start.3 = (bf16[2,512,512]{2,1,0:T(8,128)(2,1)}, bf16[2,512,512]{2,1,0:T(8,128)(2,1)S(1)}, u32[]{:S(2)}, u32[]{:S(2)}) collective-permute-start(bf16[2,512,512]{2,1,0:T(8,128)(2,1)} %after.4.refs_1_), channel_id=1, source_target_pairs={{0,4},{4,8},{8,12},{12,16},{16,20},{20,24},{24,28},{1,5},{5,9},{9,... | collective-permute-start | bytes 3145736 | tf_op jit(solution)/shard_map/ppermute | solution.py:513
  24.3 6.4 %collective-permute-start.7 = (bf16[2,64,512]{2,1,0:T(8,128)(2,1)}, bf16[2,64,512]{2,1,0:T(8,128)(2,1)S(1)}, u32[]{:S(2)}, u32[]{:S(2)}) collective-permute-start(bf16[2,64,512]{2,1,0:T(8,128)(2,1)} %copy-done.7), channel_id=1, source_target_pairs={{0,4},{4,0},{8,12},{12,8},{16,20},{20,16},{24,28},{28,24},{1,5},{5... | collective-permute-start | bytes 393224 | tf_op jit(solution)/shard_map/ppermute | solution.py:438
  25.9 9.6 %collective-permute-start.4 = (bf16[2,64,512]{2,1,0:T(8,128)(2,1)S(1)}, bf16[2,64,512]{2,1,0:T(8,128)(2,1)S(1)}, u32[]{:S(2)}, u32[]{:S(2)}) collective-permute-start(bf16[2,64,512]{2,1,0:T(8,128)(2,1)S(1)} %copy-done.12), channel_id=1, source_target_pairs={{0,4},{4,0},{8,12},{12,8},{16,20},{20,16},{24,28},{28,24},{1,5},{5... | collective-permute-start | bytes 393224 | tf_op jit(solution)/shard_map/ppermute | solution.py:438
  26.0 9.6 %collective-permute-start.6 = (bf16[2,64,512]{2,1,0:T(8,128)(2,1)}, bf16[2,64,512]{2,1,0:T(8,128)(2,1)S(1)}, u32[]{:S(2)}, u32[]{:S(2)}) collective-permute-start(bf16[2,64,512]{2,1,0:T(8,128)(2,1)} %copy-done.8), channel_id=1, source_target_pairs={{0,4},{4,0},{8,12},{12,8},{16,20},{20,16},{24,28},{28,24},{1,5},{5... | collective-permute-start | bytes 393224 | tf_op jit(solution)/shard_map/ppermute | solution.py:438
  26.5 9.1 %collective-permute-start.5 = (bf16[2,64,512]{2,1,0:T(8,128)(2,1)}, bf16[2,64,512]{2,1,0:T(8,128)(2,1)S(1)}, u32[]{:S(2)}, u32[]{:S(2)}) collective-permute-start(bf16[2,64,512]{2,1,0:T(8,128)(2,1)} %copy-done.9), channel_id=1, source_target_pairs={{0,4},{4,0},{8,12},{12,8},{16,20},{20,16},{24,28},{28,24},{1,5},{5... | collective-permute-start | bytes 393224 | tf_op jit(solution)/shard_map/ppermute | solution.py:438
  26.6 29.0 %all-to-all-start = ((bf16[8,3,2,64,256]{4,3,2,1,0:T(8,128)(2,1)}), bf16[8,3,2,64,256]{4,3,2,1,0:T(8,128)(2,1)S(1)}, u32[]{:S(2)}, u32[]{:S(2)}) async-start(bf16[8,3,2,64,256]{4,3,2,1,0:T(8,128)(2,1)} %after.5), calls=%async_computation | async-start | bytes 3145728 | tf_op jit(solution)/shard_map/all_to_all | solution.py:541
  30.7 0.7 copy-start.10
  35.6 9.3 %copy-start.13 = (bf16[2,64,512]{2,1,0:T(8,128)(2,1)}, bf16[2,64,512]{2,1,0:T(8,128)(2,1)S(1)}, u32[]{:S(2)}) copy-start(bf16[2,64,512]{2,1,0:T(8,128)(2,1)S(1)} %collective-permute-done.4.refs_4_) | copy-start | bytes 393220
  35.6 9.3 %copy-start.14 = (bf16[2,64,512]{2,1,0:T(8,128)(2,1)}, bf16[2,64,512]{2,1,0:T(8,128)(2,1)S(1)}, u32[]{:S(2)}) copy-start(bf16[2,64,512]{2,1,0:T(8,128)(2,1)S(1)} %collective-permute-done.6.refs_6_) | copy-start | bytes 393220
  35.6 9.3 %copy-start.15 = (bf16[2,64,512]{2,1,0:T(8,128)(2,1)}, bf16[2,64,512]{2,1,0:T(8,128)(2,1)S(1)}, u32[]{:S(2)}) copy-start(bf16[2,64,512]{2,1,0:T(8,128)(2,1)S(1)} %collective-permute-done.5.refs_5_) | copy-start | bytes 393220
  44.9 1.0 copy-start.11
  55.6 26.1 %all-to-all-start.1 = ((bf16[8,3,2,64,256]{4,3,2,1,0:T(8,128)(2,1)}), bf16[8,3,2,64,256]{4,3,2,1,0:T(8,128)(2,1)S(1)}, u32[]{:S(2)}, u32[]{:S(2)}) async-start(bf16[8,3,2,64,256]{4,3,2,1,0:T(8,128)(2,1)} %after.6), calls=%async_computation.1 | async-start | bytes 3145728 | tf_op jit(solution)/shard_map/all_to_all | solution.py:541
  61.6 3.7 %copy-start.6 = (f32[8,128]{1,0:T(8,128)}, f32[8,128]{1,0:T(8,128)S(1)}, u32[]{:S(2)}) copy-start(f32[8,128]{1,0:T(8,128)S(1)} %get-tuple-element.36.refs_8_) | copy-start | bytes 12292
  61.6 10.8 %collective-permute-start.8 = (bf16[2,64,256]{2,1,0:T(8,128)(2,1)S(1)}, bf16[2,64,256]{2,1,0:T(8,128)(2,1)S(1)}, u32[]{:S(2)}, u32[]{:S(2)}) collective-permute-start(bf16[2,64,256]{2,1,0:T(8,128)(2,1)S(1)} %get-tuple-element.43), channel_id=1, source_target_pairs={{0,4},{4,0},{8,12},{12,8},{16,20},{20,16},{24,28},{28,24},{1,5},{5... | collective-permute-start | bytes 196616 | tf_op jit(solution)/shard_map/ppermute | solution.py:497
  61.8 18.1 %collective-permute-start.9 = (bf16[2,64,256]{2,1,0:T(8,128)(2,1)S(1)}, bf16[2,64,256]{2,1,0:T(8,128)(2,1)S(1)}, u32[]{:S(2)}, u32[]{:S(2)}) collective-permute-start(bf16[2,64,256]{2,1,0:T(8,128)(2,1)S(1)} %get-tuple-element.44), channel_id=1, source_target_pairs={{0,8},{4,12},{8,0},{12,4},{16,24},{20,28},{24,16},{28,20},{1,9},{5... | collective-permute-start | bytes 196616 | tf_op jit(solution)/shard_map/ppermute | solution.py:497
  62.2 26.8 %collective-permute-start.10 = (bf16[2,64,256]{2,1,0:T(8,128)(2,1)S(1)}, bf16[2,64,256]{2,1,0:T(8,128)(2,1)S(1)}, u32[]{:S(2)}, u32[]{:S(2)}) collective-permute-start(bf16[2,64,256]{2,1,0:T(8,128)(2,1)S(1)} %get-tuple-element.45), channel_id=1, source_target_pairs={{0,12},{4,8},{8,4},{12,0},{16,28},{20,24},{24,20},{28,16},{1,13},{... | collective-permute-start | bytes 196616 | tf_op jit(solution)/shard_map/ppermute | solution.py:497
  63.6 25.5 %collective-permute-start.11 = (bf16[2,64,256]{2,1,0:T(8,128)(2,1)S(1)}, bf16[2,64,256]{2,1,0:T(8,128)(2,1)S(1)}, u32[]{:S(2)}, u32[]{:S(2)}) collective-permute-start(bf16[2,64,256]{2,1,0:T(8,128)(2,1)S(1)} %get-tuple-element.46), channel_id=1, source_target_pairs={{0,16},{4,20},{8,24},{12,28},{16,0},{20,4},{24,8},{28,12},{1,17},{... | collective-permute-start | bytes 196616 | tf_op jit(solution)/shard_map/ppermute | solution.py:497
  65.0 24.0 %collective-permute-start.12 = (bf16[2,64,256]{2,1,0:T(8,128)(2,1)S(1)}, bf16[2,64,256]{2,1,0:T(8,128)(2,1)S(1)}, u32[]{:S(2)}, u32[]{:S(2)}) collective-permute-start(bf16[2,64,256]{2,1,0:T(8,128)(2,1)S(1)} %get-tuple-element.47), channel_id=1, source_target_pairs={{0,20},{4,16},{8,28},{12,24},{16,4},{20,0},{24,12},{28,8},{1,21},{... | collective-permute-start | bytes 196616 | tf_op jit(solution)/shard_map/ppermute | solution.py:497
  72.5 16.6 %collective-permute-start.13 = (bf16[2,64,256]{2,1,0:T(8,128)(2,1)S(1)}, bf16[2,64,256]{2,1,0:T(8,128)(2,1)S(1)}, u32[]{:S(2)}, u32[]{:S(2)}) collective-permute-start(bf16[2,64,256]{2,1,0:T(8,128)(2,1)S(1)} %get-tuple-element.48), channel_id=1, source_target_pairs={{0,24},{4,28},{8,16},{12,20},{16,8},{20,12},{24,0},{28,4},{1,25},{... | collective-permute-start | bytes 196616 | tf_op jit(solution)/shard_map/ppermute | solution.py:497
  79.9 9.1 %collective-permute-start.14 = (bf16[2,64,256]{2,1,0:T(8,128)(2,1)S(1)}, bf16[2,64,256]{2,1,0:T(8,128)(2,1)S(1)}, u32[]{:S(2)}, u32[]{:S(2)}) collective-permute-start(bf16[2,64,256]{2,1,0:T(8,128)(2,1)S(1)} %get-tuple-element.49), channel_id=1, source_target_pairs={{0,28},{4,24},{8,20},{12,16},{16,12},{20,8},{24,4},{28,0},{1,29},{... | collective-permute-start | bytes 196616 | tf_op jit(solution)/shard_map/ppermute | solution.py:497
  81.7 0.7 copy-start.5
  84.9 16.4 %all-to-all-start.2 = ((bf16[8,2,64,256]{3,2,1,0:T(8,128)(2,1)}), bf16[8,2,64,256]{3,2,1,0:T(8,128)(2,1)S(1)}, u32[]{:S(2)}, u32[]{:S(2)}) async-start(bf16[8,2,64,256]{3,2,1,0:T(8,128)(2,1)} %get-tuple-element.40), calls=%async_computation.2 | async-start | bytes 1048576 | tf_op jit(solution)/shard_map/all_to_all | solution.py:547
  89.1 1.2 copy-start.4
  90.3 11.0 %copy-start.3 = (f32[1024,256]{1,0:T(8,128)S(1)}, f32[1024,256]{1,0:T(8,128)}, u32[]{:S(2)}) copy-start(f32[1024,256]{1,0:T(8,128)} %get-tuple-element.37.home_ref) | copy-start | bytes 3145732
  91.1 6.9 %collective-permute-start.15 = (bf16[256,256]{1,0:T(8,128)(2,1)S(1)}, bf16[256,256]{1,0:T(8,128)(2,1)S(1)}, u32[]{:S(2)}, u32[]{:S(2)}) collective-permute-start(bf16[256,256]{1,0:T(8,128)(2,1)S(1)} %get-tuple-element.52), channel_id=1, source_target_pairs={{0,1},{1,0},{2,3},{3,2},{4,5},{5,4},{6,7},{7,6},{8,9},{9,8},{10,11... | collective-permute-start | bytes 393224 | tf_op jit(solution)/shard_map/ppermute | solution.py:497
  91.7 9.6 %collective-permute-start.16 = (bf16[256,256]{1,0:T(8,128)(2,1)S(1)}, bf16[256,256]{1,0:T(8,128)(2,1)S(1)}, u32[]{:S(2)}, u32[]{:S(2)}) collective-permute-start(bf16[256,256]{1,0:T(8,128)(2,1)S(1)} %get-tuple-element.53), channel_id=1, source_target_pairs={{0,2},{1,3},{2,0},{3,1},{4,6},{5,7},{6,4},{7,5},{8,10},{9,11},{10,... | collective-permute-start | bytes 393224 | tf_op jit(solution)/shard_map/ppermute | solution.py:497
  102.1 0.6 copy-start.2
  102.7 9.2 %copy-start.1 = (s32[2]{0:T(128)S(1)}, s32[2]{0:T(128)}, u32[]{:S(2)}) copy-start(s32[2]{0:T(128)} %pad_add_fusion.side_ref) | copy-start | bytes 28
  102.7 9.2 %collective-permute-start.20 = (bf16[4,512,1024]{2,1,0:T(8,128)(2,1)}, bf16[4,512,1024]{2,1,0:T(8,128)(2,1)S(1)}, u32[]{:S(2)}, u32[]{:S(2)}) collective-permute-start(bf16[4,512,1024]{2,1,0:T(8,128)(2,1)} %after.7.refs_4_), channel_id=1, source_target_pairs={{0,4},{4,0},{8,12},{12,8},{16,20},{20,16},{24,28},{28,24},{1,5},{5... | collective-permute-start | bytes 12582920 | tf_op jit(solution)/shard_map/ppermute | solution.py:559
  102.7 9.2 %collective-permute-start.21 = (bf16[256,256]{1,0:T(8,128)(2,1)S(1)}, bf16[256,256]{1,0:T(8,128)(2,1)S(1)}, u32[]{:S(2)}, u32[]{:S(2)}) collective-permute-start(bf16[256,256]{1,0:T(8,128)(2,1)S(1)} %get-tuple-element.60), channel_id=1, source_target_pairs={{0,3},{1,2},{2,1},{3,0},{4,7},{5,6},{6,5},{7,4},{8,11},{9,10},{10,... | collective-permute-start | bytes 393224 | tf_op jit(solution)/shard_map/ppermute | solution.py:497
  103.3 14.7 %collective-permute-start.17 = (bf16[256,256]{1,0:T(8,128)(2,1)S(1)}, bf16[256,256]{1,0:T(8,128)(2,1)S(1)}, u32[]{:S(2)}, u32[]{:S(2)}) collective-permute-start(bf16[256,256]{1,0:T(8,128)(2,1)S(1)} %get-tuple-element.55), channel_id=1, source_target_pairs={{0,1},{1,0},{2,3},{3,2},{4,5},{5,4},{6,7},{7,6},{8,9},{9,8},{10,11... | collective-permute-start | bytes 393224 | tf_op jit(solution)/shard_map/ppermute | solution.py:497
  106.9 11.1 %collective-permute-start.18 = (bf16[256,256]{1,0:T(8,128)(2,1)S(1)}, bf16[256,256]{1,0:T(8,128)(2,1)S(1)}, u32[]{:S(2)}, u32[]{:S(2)}) collective-permute-start(bf16[256,256]{1,0:T(8,128)(2,1)S(1)} %get-tuple-element.56), channel_id=1, source_target_pairs={{0,2},{1,3},{2,0},{3,1},{4,6},{5,7},{6,4},{7,5},{8,10},{9,11},{10,... | collective-permute-start | bytes 393224 | tf_op jit(solution)/shard_map/ppermute | solution.py:497
  106.9 15.8 %collective-permute-start.19 = (bf16[256,256]{1,0:T(8,128)(2,1)S(1)}, bf16[256,256]{1,0:T(8,128)(2,1)S(1)}, u32[]{:S(2)}, u32[]{:S(2)}) collective-permute-start(bf16[256,256]{1,0:T(8,128)(2,1)S(1)} %get-tuple-element.57), channel_id=1, source_target_pairs={{0,3},{1,2},{2,1},{3,0},{4,7},{5,6},{6,5},{7,4},{8,11},{9,10},{10,... | collective-permute-start | bytes 393224 | tf_op jit(solution)/shard_map/ppermute | solution.py:497
  111.9 2.2 %copy-start = (bf16[4,512,1024]{2,1,0:T(8,128)(2,1)S(1)}, bf16[4,512,1024]{2,1,0:T(8,128)(2,1)}, u32[]{:S(2)}) copy-start(bf16[4,512,1024]{2,1,0:T(8,128)(2,1)} %after.7.refs_4_) | copy-start | bytes 12582916
Sparse Core Ops, SparseCore 0:
  10.2 79.4 all-gather.2

commit v11 on v10

--- a/solution.py
+++ b/solution.py
@@ -153,10 +153,10 @@
         cut_kernel,
         grid_spec=pltpu.PrefetchScalarGridSpec(
             num_scalar_prefetch=1,
-            grid=(1,),
-            in_specs=[pl.BlockSpec((rows, size), lambda i, side: (0, first + side[0]))]
+            grid=(4,),
+            in_specs=[pl.BlockSpec((rows // 4, size), lambda i, side: (i, first + side[0]))]
             + moments(waits),
-            out_specs=pl.BlockSpec((rows, size), lambda i, side: (0, 0)),
+            out_specs=pl.BlockSpec((rows // 4, size), lambda i, side: (i, 0)),
         ),
         out_shape=jax.ShapeDtypeStruct((rows, size), BF16),
         compiler_params=params(60),
@@ -366,63 +366,38 @@
     )(seat, home, *backs, *waits)
 
 
-def project_kernel(side_ref, *refs, slots, adds):
-    moved_refs, (mine_ref, other_ref), refs = refs[:slots], refs[slots : slots + 2], refs[slots + 2 :]
-    o_ref, mark_ref, total_ref = refs[-3:]
-    mark_ref[...] = jnp.zeros_like(mark_ref)
-    half = mine_ref.shape[2]
-    phase, slot = pl.program_id(0), pl.program_id(1)
-    here = pl.ds(pl.multiple_of((side_ref[0] ^ phase) * half, half), half)
-
-    def add_up(weight_ref):
-        for one in range(slots):
-
-            @pl.when(slot == one)
-            def _():
-                total = dot(moved_refs[one][...], weight_ref[0])
-                if one > 0:
-                    total = total + total_ref[...]
-                elif adds:
-                    total = total + refs[0][:, here]
-                if one < slots - 1:
-                    total_ref[...] = total
-                else:
-                    o_ref[:, here] = total.astype(o_ref.dtype)
-
-    @pl.when(phase == 0)
-    def _():
-        add_up(mine_ref)
-
-    @pl.when(phase == 1)
-    def _():
-        add_up(other_ref)
+def project_kernel(side_ref, *refs, slots, chunk, adds):
+    moved_refs, weight_refs, refs = refs[:slots], refs[slots : slots + 2], refs[slots + 2 :]
+    o_ref = refs[-1]
+    part = moved_refs[0].shape[1]
+    half = weight_refs[0].shape[2]
+    tile = min(half, 512)
+    for phase, weight_ref in enumerate(weight_refs):
+        for j in range(half // tile):
+            first = pl.multiple_of((side_ref[0] ^ phase) * half + j * tile, tile)
+            here = pl.ds(first, tile)
+            total = refs[0][:, here] if adds else None
+            for slot in range(slots):
+                rows = weight_ref[
+                    partner(side_ref[1], slot, slots),
+                    chunk * part : (chunk + 1) * part,
+                    j * tile : (j + 1) * tile,
+                ]
+                product = dot(moved_refs[slot][...], rows)
+                total = product if total is None else total + product
+            o_ref[:, here] = total.astype(o_ref.dtype)
 
 
 def project(side, moved, mine, other, chunk, before, dtype):
     slots = len(moved)
     tokens, part = moved[0].shape
     half = mine.shape[2]
-
-    def mine_group(p, s, side):
-        return (side[1] ^ jnp.where(p == 0, s, slots - 1), chunk, 0)
-
-    def other_group(p, s, side):
-        return (side[1] ^ jnp.where(p == 0, 0, s), chunk, 0)
-
-    whole = pl.BlockSpec((tokens, 2 * half), lambda p, s, side: (0, 0))
-    return pl.pallas_call(
-        functools.partial(project_kernel, slots=slots, adds=len(before) > 0),
-        grid_spec=pltpu.PrefetchScalarGridSpec(
-            num_scalar_prefetch=1,
-            grid=(2, slots),
-            in_specs=[pl.BlockSpec((tokens, part), lambda p, s, side: (0, 0))] * slots
-            + [pl.BlockSpec((1, part, half), mine_group)]
-            + [pl.BlockSpec((1, part, half), other_group)]
-            + [whole] * len(before),
-            out_specs=[whole, mark_spec()],
-            scratch_shapes=[pltpu.VMEM((tokens, half), F32)],
-        ),
-        out_shape=[jax.ShapeDtypeStruct((tokens, 2 * half), dtype), MARK],
+    whole = pl.BlockSpec(memory_space=pltpu.VMEM)
+    return pl.pallas_call(
+        functools.partial(project_kernel, slots=slots, chunk=chunk, adds=len(before) > 0),
+        in_specs=[pl.BlockSpec(memory_space=pltpu.SMEM)] + [whole] * (slots + 2 + len(before)),
+        out_specs=whole,
+        out_shape=jax.ShapeDtypeStruct((tokens, 2 * half), dtype),
         compiler_params=params(24),
         cost_estimate=cost(
             4 * slots * tokens * part * half, 2 * slots * part * (2 * half + tokens)
@@ -560,7 +535,7 @@
     total = ()
     for chunk in range(chunks):
         dtype = BF16 if chunk == chunks - 1 else F32
-        *total, _ = project(sides, moved[chunk], held, other, chunk, total, dtype)
+        total = (project(sides, moved[chunk], held, other, chunk, total, dtype),)
     return total[0]
 
 

time: 134 us -> 134 us (level)
  Pallas kernels: 42 us -> 39.6 us
  waiting for transfers between devices: 34.5 us -> 36.5 us
    pallas_call x2, Pallas kernels: 8.09 us -> 4.6 us  [project(): pl.pallas_call(functools.partial(project_kernel, slots=slots, chunk=chunk...]
    ppermute x13, waiting for transfers between devices: 21.1 us -> 23.2 us  [exchange(): moved.append(lax.ppermute(slabs[slot], axis, pairs))]
  transfers between devices with their start and end apart: 26 -> 26, of which waited for: 9 -> 10; matrix products, arithmetic and copies ran while one was open for 0% -> 0% of each run, Pallas kernels for 26% -> 25%
where the time goes in v11:
time: 134 us; the launch traced here: 133 us
  Pallas kernels  39.6 us (30%)
  waiting for transfers between devices  36.5 us (27%)
  starting transfers between devices  36.1 us (27%)
  between operations  13.6 us (10%)
  local copies, waits for them, and re-layouts  6.93 us (5%)
    ppermute x13, waiting for transfers between devices, exchange(): moved.append(lax.ppermute(slabs[slot], axis, pairs))  23.2 us
    ppermute x13, starting transfers between devices, exchange(): moved.append(lax.ppermute(slabs[slot], axis, pairs))  15.8 us
    pallas_call x2, Pallas kernels, home_sections(): pl.pallas_call(functools.partial(home_kernel, order=order), grid=(heads,)...  14.2 us
    ppermute x1, waiting for transfers between devices, body(): before = lax.ppermute(rim, 'ctx', [(i, i + 1) for i in range(ctx - 1)])  9.29 us
    pallas_call x2, Pallas kernels, prepare(): pl.pallas_call(prep_kernel, grid=(tokens_dev // TILE,), in_specs=[pl.Bloc...  8.55 us
    all_to_all x2, starting transfers between devices, body(): lax.all_to_all(send, 'ctx', split_axis=0, concat_axis=0, tiled=True)  8.32 us
    unnamed x32, local copies, waits for them, and re-layouts  6.93 us
    ppermute x7, starting transfers between devices, swapped(): return lax.ppermute(piece, 'ctx', [(i, i ^ distance) for i in range(count)])  5.7 us
  transfers between devices with their start and end apart: 26, of which 10 were waited for; matrix products, arithmetic and copies ran while one was open for 0% of the time, Pallas kernels for 25%

profile of v11, /device:TPU:10, one launch (start us, length us, event | category | flops | bytes accessed | tf_op | source)
XLA Modules:
  0.0 133.4 jit_solution(16404547869073122631)
XLA Ops:
  6.5 0.6 pad_add_fusion.side_ref
  7.2 4.0 %cut.1.refs_0_ = bf16[512,1024]{1,0:T(8,128)(2,1)} custom-call(s32[2]{0:T(128)} %pad_add_fusion.side_ref, bf16[512,2048]{1,0:T(8,128)(2,1)} %weight_ref.1), custom_call_target="tpu_custom_call" | custom-call | bytes 2097152 | tf_op jit(solution)/shard_map/cut/pallas_call | solution.py:152
  11.2 2.3 %edges.1 = (bf16[2,512,512]{2,1,0:T(8,128)(2,1)}, bf16[2,64,512]{2,1,0:T(8,128)(2,1)}) custom-call(bf16[1024,512]{1,0:T(8,128)(2,1)} %k_ref.9, bf16[1024,512]{1,0:T(8,128)(2,1)} %v_ref.9, bf16[8,128,512]{2,1,0:T(8,128)(2,1)} %bitcast.7, bf16[8,128,512]{2,1,0:T(8,128)(2,1)} %bitcast.8, bf16[512,1024]{1,0:T(8,128)(2,1)} %cut.1.refs_0_), custom_call_target="tpu_custom_call" | custom-call | bytes 2097152 | tf_op jit(solution)/shard_map/edges/pallas_call | solution.py:122
  13.5 1.5 %collective-permute-start.2 = (bf16[2,64,512]{2,1,0:T(8,128)(2,1)}, bf16[2,64,512]{2,1,0:T(8,128)(2,1)S(1)}, u32[]{:S(2)}, u32[]{:S(2)}) collective-permute-start(bf16[2,64,512]{2,1,0:T(8,128)(2,1)} %get-tuple-element.33.refs_0_), channel_id=1, source_target_pairs={{0,24},{4,28},{8,16},{12,20},{16,8},{20,12},{24,0},{28,4},{1,25},{... | collective-permute-start | bytes 393224 | tf_op jit(solution)/shard_map/ppermute | solution.py:413
  15.0 0.5 collective-permute-start.1
  15.5 1.5 %collective-permute-start = (bf16[2,64,512]{2,1,0:T(8,128)(2,1)}, bf16[2,64,512]{2,1,0:T(8,128)(2,1)S(1)}, u32[]{:S(2)}, u32[]{:S(2)}) collective-permute-start(bf16[2,64,512]{2,1,0:T(8,128)(2,1)} %get-tuple-element.33.refs_0_), channel_id=1, source_target_pairs={{0,8},{4,12},{8,0},{12,4},{16,24},{20,28},{24,16},{28,20},{1,9},{5... | collective-permute-start | bytes 393224 | tf_op jit(solution)/shard_map/ppermute | solution.py:413
  17.0 4.3 %prepare.2.refs_4_.refs_0_ = bf16[8,3,2,64,256]{4,3,2,1,0:T(8,128)(2,1)} custom-call(bf16[1024,512]{1,0:T(8,128)(2,1)} %q_ref.7, bf16[1024,512]{1,0:T(8,128)(2,1)} %k_ref.9, bf16[1024,512]{1,0:T(8,128)(2,1)} %v_ref.9, bf16[512,1024]{1,0:T(8,128)(2,1)} %cut.1.refs_0_), custom_call_target="tpu_custom_call" | custom-call | flops 402653184 | bytes 3145728 | tf_op jit(solution)/shard_map/prepare/pallas_call | solution.py:181
  21.3 1.3 %collective-permute-done.1.refs_2_ = bf16[2,64,512]{2,1,0:T(8,128)(2,1)S(1)} collective-permute-done((bf16[2,64,512]{2,1,0:T(8,128)(2,1)}, bf16[2,64,512]{2,1,0:T(8,128)(2,1)S(1)}, u32[]{:S(2)}, u32[]{:S(2)}) %collective-permute-start.1) | collective-permute-done | bytes 131104 | tf_op jit(solution)/shard_map/ppermute | solution.py:413
  22.8 0.5 copy-done.8
  23.4 2.0 %collective-permute-start.3 = (bf16[2,512,512]{2,1,0:T(8,128)(2,1)}, bf16[2,512,512]{2,1,0:T(8,128)(2,1)S(1)}, u32[]{:S(2)}, u32[]{:S(2)}) collective-permute-start(bf16[2,512,512]{2,1,0:T(8,128)(2,1)} %after.4.refs_1_), channel_id=1, source_target_pairs={{0,4},{4,8},{8,12},{12,16},{16,20},{20,24},{24,28},{1,5},{5,9},{9,... | collective-permute-start | bytes 3145736 | tf_op jit(solution)/shard_map/ppermute | solution.py:488
  25.5 1.6 %collective-permute-start.7 = (bf16[2,64,512]{2,1,0:T(8,128)(2,1)}, bf16[2,64,512]{2,1,0:T(8,128)(2,1)S(1)}, u32[]{:S(2)}, u32[]{:S(2)}) collective-permute-start(bf16[2,64,512]{2,1,0:T(8,128)(2,1)} %copy-done.7), channel_id=1, source_target_pairs={{0,4},{4,0},{8,12},{12,8},{16,20},{20,16},{24,28},{28,24},{1,5},{5... | collective-permute-start | bytes 393224 | tf_op jit(solution)/shard_map/ppermute | solution.py:413
  27.2 0.4 collective-permute-start.6
  27.8 4.1 %all-to-all-start = ((bf16[8,3,2,64,256]{4,3,2,1,0:T(8,128)(2,1)}), bf16[8,3,2,64,256]{4,3,2,1,0:T(8,128)(2,1)S(1)}, u32[]{:S(2)}, u32[]{:S(2)}) async-start(bf16[8,3,2,64,256]{4,3,2,1,0:T(8,128)(2,1)} %after.5), calls=%async_computation | async-start | bytes 3145728 | tf_op jit(solution)/shard_map/all_to_all | solution.py:516
  31.8 0.6 copy-done.10
  32.5 4.2 %prepare.3.refs_0_ = bf16[8,3,2,64,256]{4,3,2,1,0:T(8,128)(2,1)} custom-call(bf16[1024,512]{1,0:T(8,128)(2,1)} %q_ref.7, bf16[1024,512]{1,0:T(8,128)(2,1)} %k_ref.9, bf16[1024,512]{1,0:T(8,128)(2,1)} %v_ref.9, bf16[2,64,512]{2,1,0:T(8,128)(2,1)} %copy-done.10), custom_call_target="tpu_custom_call" | custom-call | flops 402653184 | bytes 3145728 | tf_op jit(solution)/shard_map/prepare/pallas_call | solution.py:181
  36.7 9.3 %collective-permute-done.3.rim_ref = bf16[2,512,512]{2,1,0:T(8,128)(2,1)S(1)} collective-permute-done((bf16[2,512,512]{2,1,0:T(8,128)(2,1)}, bf16[2,512,512]{2,1,0:T(8,128)(2,1)S(1)}, u32[]{:S(2)}, u32[]{:S(2)}) %collective-permute-start.3) | collective-permute-done | bytes 1048608 | tf_op jit(solution)/shard_map/ppermute | solution.py:488
  46.1 1.0 copy-done.11
  47.0 7.1 %home.3 = (f32[1024,256]{1,0:T(8,128)}, f32[8,128]{1,0:T(8,128)}) custom-call(s32[1]{0:T(128)} %bitcast.2.place_ref, bf16[1024,512]{1,0:T(8,128)(2,1)} %q_ref.7, bf16[1024,512]{1,0:T(8,128)(2,1)} %k_ref.9, bf16[1024,512]{1,0:T(8,128)(2,1)} %v_ref.9, bf16[2,512,512]{2,1,0:T(8,128)(2,1)} %copy-done.11, bf16[2,64,512]{2,1,0:T(8,128)(2,1)} %get-tuple-element.33.refs_0_, ...), custom_call_target="tpu_custom_call" | custom-call | flops 21474836480 | bytes 7340032 | tf_op jit(solution)/shard_map/home/pallas_call | solution.py:248
  54.1 2.6 %all-to-all-done.x_ref = bf16[8,3,2,64,256]{4,3,2,1,0:T(8,128)(2,1)S(1)} async-done(((bf16[8,3,2,64,256]{4,3,2,1,0:T(8,128)(2,1)}), bf16[8,3,2,64,256]{4,3,2,1,0:T(8,128)(2,1)S(1)}, u32[]{:S(2)}, u32[]{:S(2)}) %all-to-all-start) | async-done | bytes 1572896 | tf_op jit(solution)/shard_map/all_to_all | solution.py:516
  56.7 4.3 %all-to-all-start.1 = ((bf16[8,3,2,64,256]{4,3,2,1,0:T(8,128)(2,1)}), bf16[8,3,2,64,256]{4,3,2,1,0:T(8,128)(2,1)S(1)}, u32[]{:S(2)}, u32[]{:S(2)}) async-start(bf16[8,3,2,64,256]{4,3,2,1,0:T(8,128)(2,1)} %after.6), calls=%async_computation.1 | async-start | bytes 3145728 | tf_op jit(solution)/shard_map/all_to_all | solution.py:516
  61.0 1.8 %stride.2 = (bf16[2,64,256]{2,1,0:T(8,128)(2,1)S(1)}, bf16[2,64,256]{2,1,0:T(8,128)(2,1)S(1)}, bf16[2,64,256]{2,1,0:T(8,128)(2,1)S(1)}, bf16[2,64,256]{2,1,0:T(8...) custom-call(s32[1]{0:T(128)} %bitcast.2.place_ref, ...), custom_call_target="tpu_custom_call" | custom-call | flops 805306368 | bytes 2097152 | tf_op jit(solution)/shard_map/stride/pallas_call | solution.py:311
  63.0 0.4 collective-permute-start.9
  63.3 1.4 %collective-permute-start.10 = (bf16[2,64,256]{2,1,0:T(8,128)(2,1)S(1)}, bf16[2,64,256]{2,1,0:T(8,128)(2,1)S(1)}, u32[]{:S(2)}, u32[]{:S(2)}) collective-permute-start(bf16[2,64,256]{2,1,0:T(8,128)(2,1)S(1)} %get-tuple-element.43), channel_id=1, source_target_pairs={{0,12},{4,8},{8,4},{12,0},{16,28},{20,24},{24,20},{28,16},{1,13},{... | collective-permute-start | bytes 196616 | tf_op jit(solution)/shard_map/ppermute | solution.py:472
  64.7 1.5 %collective-permute-start.11 = (bf16[2,64,256]{2,1,0:T(8,128)(2,1)S(1)}, bf16[2,64,256]{2,1,0:T(8,128)(2,1)S(1)}, u32[]{:S(2)}, u32[]{:S(2)}) collective-permute-start(bf16[2,64,256]{2,1,0:T(8,128)(2,1)S(1)} %get-tuple-element.44), channel_id=1, source_target_pairs={{0,16},{4,20},{8,24},{12,28},{16,0},{20,4},{24,8},{28,12},{1,17},{... | collective-permute-start | bytes 196616 | tf_op jit(solution)/shard_map/ppermute | solution.py:472
  66.5 7.1 %home.2 = (f32[1024,256]{1,0:T(8,128)}, f32[8,128]{1,0:T(8,128)}) custom-call(s32[1]{0:T(128)} %bitcast.2.place_ref, bf16[1024,512]{1,0:T(8,128)(2,1)} %q_ref.7, bf16[1024,512]{1,0:T(8,128)(2,1)} %k_ref.9, bf16[1024,512]{1,0:T(8,128)(2,1)} %v_ref.9, bf16[2,512,512]{2,1,0:T(8,128)(2,1)} %copy-done.11, bf16[2,64,512]{2,1,0:T(8,128)(2,1)} %get-tuple-element.33.refs_0_, ...), custom_call_target="tpu_custom_call" | custom-call | flops 21474836480 | bytes 7340032 | tf_op jit(solution)/shard_map/home/pallas_call | solution.py:248
  73.6 1.7 %collective-permute-start.13 = (bf16[2,64,256]{2,1,0:T(8,128)(2,1)S(1)}, bf16[2,64,256]{2,1,0:T(8,128)(2,1)S(1)}, u32[]{:S(2)}, u32[]{:S(2)}) collective-permute-start(bf16[2,64,256]{2,1,0:T(8,128)(2,1)S(1)} %get-tuple-element.46), channel_id=1, source_target_pairs={{0,24},{4,28},{8,16},{12,20},{16,8},{20,12},{24,0},{28,4},{1,25},{... | collective-permute-start | bytes 196616 | tf_op jit(solution)/shard_map/ppermute | solution.py:472
  75.3 5.8 %collective-permute-done.9.refs_2_ = bf16[2,64,256]{2,1,0:T(8,128)(2,1)S(1)} collective-permute-done((bf16[2,64,256]{2,1,0:T(8,128)(2,1)S(1)}, bf16[2,64,256]{2,1,0:T(8,128)(2,1)S(1)}, u32[]{:S(2)}, u32[]{:S(2)}) %collective-permute-start.9) | collective-permute-done | bytes 65568 | tf_op jit(solution)/shard_map/ppermute | solution.py:472
  81.1 1.7 %collective-permute-start.14 = (bf16[2,64,256]{2,1,0:T(8,128)(2,1)S(1)}, bf16[2,64,256]{2,1,0:T(8,128)(2,1)S(1)}, u32[]{:S(2)}, u32[]{:S(2)}) collective-permute-start(bf16[2,64,256]{2,1,0:T(8,128)(2,1)S(1)} %get-tuple-element.47), channel_id=1, source_target_pairs={{0,28},{4,24},{8,20},{12,16},{16,12},{20,8},{24,4},{28,0},{1,29},{... | collective-permute-start | bytes 196616 | tf_op jit(solution)/shard_map/ppermute | solution.py:472
  82.8 0.7 copy-done.5
  83.5 2.5 %stride.3 = (bf16[8,2,64,256]{3,2,1,0:T(8,128)(2,1)}, f32[8,128]{1,0:T(8,128)S(1)}) custom-call(s32[1]{0:T(128)} %bitcast.2.place_ref, bf16[8,3,2,64,256]{4,3,2,1,0:T(8,128)(2,1)S(1)} %all-to-all-done.1.x_ref, f32[8,128]{1,0:T(8,128)S(1)} %copy-done.5), custom_call_target="tpu_custom_call" | custom-call | flops 805306368 | bytes 2097152 | tf_op jit(solution)/shard_map/stride/pallas_call | solution.py:311
  86.0 4.1 %all-to-all-start.2 = ((bf16[8,2,64,256]{3,2,1,0:T(8,128)(2,1)}), bf16[8,2,64,256]{3,2,1,0:T(8,128)(2,1)S(1)}, u32[]{:S(2)}, u32[]{:S(2)}) async-start(bf16[8,2,64,256]{3,2,1,0:T(8,128)(2,1)} %get-tuple-element.38), calls=%async_computation.2 | async-start | bytes 1048576 | tf_op jit(solution)/shard_map/all_to_all | solution.py:522
  90.2 1.2 copy-done.4
  91.4 0.8 combine.2
  92.2 0.5 collective-permute-start.15
  92.8 2.6 %collective-permute-start.16 = (bf16[256,256]{1,0:T(8,128)(2,1)S(1)}, bf16[256,256]{1,0:T(8,128)(2,1)S(1)}, u32[]{:S(2)}, u32[]{:S(2)}) collective-permute-start(bf16[256,256]{1,0:T(8,128)(2,1)S(1)} %get-tuple-element.51), channel_id=1, source_target_pairs={{0,2},{1,3},{2,0},{3,1},{4,6},{5,7},{6,4},{7,5},{8,10},{9,11},{10,... | collective-permute-start | bytes 393224 | tf_op jit(solution)/shard_map/ppermute | solution.py:472
  95.4 3.8 %collective-permute-done.15.refs_2_.refs_1_ = bf16[256,256]{1,0:T(8,128)(2,1)S(1)} collective-permute-done((bf16[256,256]{1,0:T(8,128)(2,1)S(1)}, bf16[256,256]{1,0:T(8,128)(2,1)S(1)}, u32[]{:S(2)}, u32[]{:S(2)}) %collective-permute-start.15) | collective-permute-done | bytes 131104 | tf_op jit(solution)/shard_map/ppermute | solution.py:472
  99.1 3.2 %collective-permute-done.16.refs_3_.refs_2_ = bf16[256,256]{1,0:T(8,128)(2,1)S(1)} collective-permute-done((bf16[256,256]{1,0:T(8,128)(2,1)S(1)}, bf16[256,256]{1,0:T(8,128)(2,1)S(1)}, u32[]{:S(2)}, u32[]{:S(2)}) %collective-permute-start.16) | collective-permute-done | bytes 131104 | tf_op jit(solution)/shard_map/ppermute | solution.py:472
  102.4 0.8 combine.3
  103.2 0.6 copy-done.2
  103.8 0.5 collective-permute-start.21
  104.4 3.6 %collective-permute-start.17 = (bf16[256,256]{1,0:T(8,128)(2,1)S(1)}, bf16[256,256]{1,0:T(8,128)(2,1)S(1)}, u32[]{:S(2)}, u32[]{:S(2)}) collective-permute-start(bf16[256,256]{1,0:T(8,128)(2,1)S(1)} %get-tuple-element.53), channel_id=1, source_target_pairs={{0,1},{1,0},{2,3},{3,2},{4,5},{5,4},{6,7},{7,6},{8,9},{9,8},{10,11... | collective-permute-start | bytes 393224 | tf_op jit(solution)/shard_map/ppermute | solution.py:472
  108.0 1.5 %collective-permute-start.19 = (bf16[256,256]{1,0:T(8,128)(2,1)S(1)}, bf16[256,256]{1,0:T(8,128)(2,1)S(1)}, u32[]{:S(2)}, u32[]{:S(2)}) collective-permute-start(bf16[256,256]{1,0:T(8,128)(2,1)S(1)} %get-tuple-element.55), channel_id=1, source_target_pairs={{0,3},{1,2},{2,1},{3,0},{4,7},{5,6},{6,5},{7,4},{8,11},{9,10},{10,... | collective-permute-start | bytes 393224 | tf_op jit(solution)/shard_map/ppermute | solution.py:472
  109.4 3.6 %collective-permute-done.21.refs_3_ = bf16[256,256]{1,0:T(8,128)(2,1)S(1)} collective-permute-done((bf16[256,256]{1,0:T(8,128)(2,1)S(1)}, bf16[256,256]{1,0:T(8,128)(2,1)S(1)}, u32[]{:S(2)}, u32[]{:S(2)}) %collective-permute-start.21) | collective-permute-done | bytes 131104 | tf_op jit(solution)/shard_map/ppermute | solution.py:472
  113.0 2.2 %copy-done = bf16[4,512,1024]{2,1,0:T(8,128)(2,1)S(1)} copy-done((bf16[4,512,1024]{2,1,0:T(8,128)(2,1)S(1)}, bf16[4,512,1024]{2,1,0:T(8,128)(2,1)}, u32[]{:S(2)}) %copy-start) | copy-done | bytes 4194328
  115.2 1.8 %project.2.refs_6_ = f32[256,2048]{1,0:T(8,128)S(1)} custom-call(s32[2]{0:T(128)S(1)} %copy-done.1, bf16[256,256]{1,0:T(8,128)(2,1)S(1)} %get-tuple-element.57.refs_0_, bf16[256,256]{1,0:T(8,128)(2,1)S(1)} %collective-permute-done.15.refs_2_.refs_1_, bf16[256,256]{1,0:T(8,128)(2,1)S(1)} %collective-permute-done.16.refs_3_.refs_2_, ...), custom_call_target="tpu_custom_call" | custom-call | flops 1073741824 | bytes 4718592 | tf_op jit(solution)/shard_map/project/pallas_call | solution.py:396
  117.0 0.9 collective-permute-done.18.refs_2_
  117.9 5.9 %collective-permute-done.19.refs_3_ = bf16[256,256]{1,0:T(8,128)(2,1)S(1)} collective-permute-done((bf16[256,256]{1,0:T(8,128)(2,1)S(1)}, bf16[256,256]{1,0:T(8,128)(2,1)S(1)}, u32[]{:S(2)}, u32[]{:S(2)}) %collective-permute-start.19) | collective-permute-done | bytes 131104 | tf_op jit(solution)/shard_map/ppermute | solution.py:472
  123.8 2.8 %project.3 = bf16[256,2048]{1,0:T(8,128)(2,1)} custom-call(s32[2]{0:T(128)S(1)} %copy-done.1, bf16[256,256]{1,0:T(8,128)(2,1)S(1)} %get-tuple-element.52.refs_0_, bf16[256,256]{1,0:T(8,128)(2,1)S(1)} %collective-permute-done.17.refs_1_, bf16[256,256]{1,0:T(8,128)(2,1)S(1)} %collective-permute-done.18.refs_2_, ...), custom_call_target="tpu_custom_call" | custom-call | flops 1073741824 | bytes 4718592 | tf_op jit(solution)/shard_map/project/pallas_call | solution.py:396
  (55 shorter events, 1.1 us)
Async XLA Ops:
  6.5 97.3 %all-gather.3.cloned.1.call-start = ((), (), s32[]{:S(2)}) async-start(), calls=%async_computation.3 | async-start | bytes 5242880 | tf_op jit(solution)/shard_map/all_gather | solution.py:476
  13.5 7.8 %collective-permute-start.2 = (bf16[2,64,512]{2,1,0:T(8,128)(2,1)}, bf16[2,64,512]{2,1,0:T(8,128)(2,1)S(1)}, u32[]{:S(2)}, u32[]{:S(2)}) collective-permute-start(bf16[2,64,512]{2,1,0:T(8,128)(2,1)} %get-tuple-element.33.refs_0_), channel_id=1, source_target_pairs={{0,24},{4,28},{8,16},{12,20},{16,8},{20,12},{24,0},{28,4},{1,25},{... | collective-permute-start | bytes 393224 | tf_op jit(solution)/shard_map/ppermute | solution.py:413
  15.0 7.7 %collective-permute-start.1 = (bf16[2,64,512]{2,1,0:T(8,128)(2,1)}, bf16[2,64,512]{2,1,0:T(8,128)(2,1)S(1)}, u32[]{:S(2)}, u32[]{:S(2)}) collective-permute-start(bf16[2,64,512]{2,1,0:T(8,128)(2,1)} %get-tuple-element.33.refs_0_), channel_id=1, source_target_pairs={{0,16},{4,20},{8,24},{12,28},{16,0},{20,4},{24,8},{28,12},{1,17},{... | collective-permute-start | bytes 393224 | tf_op jit(solution)/shard_map/ppermute | solution.py:413
  15.5 7.3 %collective-permute-start = (bf16[2,64,512]{2,1,0:T(8,128)(2,1)}, bf16[2,64,512]{2,1,0:T(8,128)(2,1)S(1)}, u32[]{:S(2)}, u32[]{:S(2)}) collective-permute-start(bf16[2,64,512]{2,1,0:T(8,128)(2,1)} %get-tuple-element.33.refs_0_), channel_id=1, source_target_pairs={{0,8},{4,12},{8,0},{12,4},{16,24},{20,28},{24,16},{28,20},{1,9},{5... | collective-permute-start | bytes 393224 | tf_op jit(solution)/shard_map/ppermute | solution.py:413
  21.3 1.4 %copy-start.7 = (bf16[2,64,512]{2,1,0:T(8,128)(2,1)}, bf16[2,64,512]{2,1,0:T(8,128)(2,1)S(1)}, u32[]{:S(2)}) copy-start(bf16[2,64,512]{2,1,0:T(8,128)(2,1)S(1)} %collective-permute-done.2.refs_3_) | copy-start | bytes 393220
  22.7 0.7 copy-start.8
  22.8 0.6 copy-start.9
  23.4 3.7 %copy-start.12 = (bf16[2,64,512]{2,1,0:T(8,128)(2,1)S(1)}, bf16[2,64,512]{2,1,0:T(8,128)(2,1)}, u32[]{:S(2)}) copy-start(bf16[2,64,512]{2,1,0:T(8,128)(2,1)} %get-tuple-element.33.refs_0_) | copy-start | bytes 393220
  23.4 22.6 %collective-permute-start.3 = (bf16[2,512,512]{2,1,0:T(8,128)(2,1)}, bf16[2,512,512]{2,1,0:T(8,128)(2,1)S(1)}, u32[]{:S(2)}, u32[]{:S(2)}) collective-permute-start(bf16[2,512,512]{2,1,0:T(8,128)(2,1)} %after.4.refs_1_), channel_id=1, source_target_pairs={{0,4},{4,8},{8,12},{12,16},{16,20},{20,24},{24,28},{1,5},{5,9},{9,... | collective-permute-start | bytes 3145736 | tf_op jit(solution)/shard_map/ppermute | solution.py:488
  25.5 6.4 %collective-permute-start.7 = (bf16[2,64,512]{2,1,0:T(8,128)(2,1)}, bf16[2,64,512]{2,1,0:T(8,128)(2,1)S(1)}, u32[]{:S(2)}, u32[]{:S(2)}) collective-permute-start(bf16[2,64,512]{2,1,0:T(8,128)(2,1)} %copy-done.7), channel_id=1, source_target_pairs={{0,4},{4,0},{8,12},{12,8},{16,20},{20,16},{24,28},{28,24},{1,5},{5... | collective-permute-start | bytes 393224 | tf_op jit(solution)/shard_map/ppermute | solution.py:413
  27.1 9.6 %collective-permute-start.4 = (bf16[2,64,512]{2,1,0:T(8,128)(2,1)S(1)}, bf16[2,64,512]{2,1,0:T(8,128)(2,1)S(1)}, u32[]{:S(2)}, u32[]{:S(2)}) collective-permute-start(bf16[2,64,512]{2,1,0:T(8,128)(2,1)S(1)} %copy-done.12), channel_id=1, source_target_pairs={{0,4},{4,0},{8,12},{12,8},{16,20},{20,16},{24,28},{28,24},{1,5},{5... | collective-permute-start | bytes 393224 | tf_op jit(solution)/shard_map/ppermute | solution.py:413
  27.2 9.5 %collective-permute-start.6 = (bf16[2,64,512]{2,1,0:T(8,128)(2,1)}, bf16[2,64,512]{2,1,0:T(8,128)(2,1)S(1)}, u32[]{:S(2)}, u32[]{:S(2)}) collective-permute-start(bf16[2,64,512]{2,1,0:T(8,128)(2,1)} %copy-done.8), channel_id=1, source_target_pairs={{0,4},{4,0},{8,12},{12,8},{16,20},{20,16},{24,28},{28,24},{1,5},{5... | collective-permute-start | bytes 393224 | tf_op jit(solution)/shard_map/ppermute | solution.py:413
  27.6 9.1 %collective-permute-start.5 = (bf16[2,64,512]{2,1,0:T(8,128)(2,1)}, bf16[2,64,512]{2,1,0:T(8,128)(2,1)S(1)}, u32[]{:S(2)}, u32[]{:S(2)}) collective-permute-start(bf16[2,64,512]{2,1,0:T(8,128)(2,1)} %copy-done.9), channel_id=1, source_target_pairs={{0,4},{4,0},{8,12},{12,8},{16,20},{20,16},{24,28},{28,24},{1,5},{5... | collective-permute-start | bytes 393224 | tf_op jit(solution)/shard_map/ppermute | solution.py:413
  27.8 29.0 %all-to-all-start = ((bf16[8,3,2,64,256]{4,3,2,1,0:T(8,128)(2,1)}), bf16[8,3,2,64,256]{4,3,2,1,0:T(8,128)(2,1)S(1)}, u32[]{:S(2)}, u32[]{:S(2)}) async-start(bf16[8,3,2,64,256]{4,3,2,1,0:T(8,128)(2,1)} %after.5), calls=%async_computation | async-start | bytes 3145728 | tf_op jit(solution)/shard_map/all_to_all | solution.py:516
  31.8 0.7 copy-start.10
  36.7 9.3 %copy-start.13 = (bf16[2,64,512]{2,1,0:T(8,128)(2,1)}, bf16[2,64,512]{2,1,0:T(8,128)(2,1)S(1)}, u32[]{:S(2)}) copy-start(bf16[2,64,512]{2,1,0:T(8,128)(2,1)S(1)} %collective-permute-done.4.refs_4_) | copy-start | bytes 393220
  36.7 9.3 %copy-start.14 = (bf16[2,64,512]{2,1,0:T(8,128)(2,1)}, bf16[2,64,512]{2,1,0:T(8,128)(2,1)S(1)}, u32[]{:S(2)}) copy-start(bf16[2,64,512]{2,1,0:T(8,128)(2,1)S(1)} %collective-permute-done.6.refs_6_) | copy-start | bytes 393220
  36.7 9.3 %copy-start.15 = (bf16[2,64,512]{2,1,0:T(8,128)(2,1)}, bf16[2,64,512]{2,1,0:T(8,128)(2,1)S(1)}, u32[]{:S(2)}) copy-start(bf16[2,64,512]{2,1,0:T(8,128)(2,1)S(1)} %collective-permute-done.5.refs_5_) | copy-start | bytes 393220
  46.0 1.0 copy-start.11
  56.7 26.1 %all-to-all-start.1 = ((bf16[8,3,2,64,256]{4,3,2,1,0:T(8,128)(2,1)}), bf16[8,3,2,64,256]{4,3,2,1,0:T(8,128)(2,1)S(1)}, u32[]{:S(2)}, u32[]{:S(2)}) async-start(bf16[8,3,2,64,256]{4,3,2,1,0:T(8,128)(2,1)} %after.6), calls=%async_computation.1 | async-start | bytes 3145728 | tf_op jit(solution)/shard_map/all_to_all | solution.py:516
  62.7 3.7 %copy-start.6 = (f32[8,128]{1,0:T(8,128)}, f32[8,128]{1,0:T(8,128)S(1)}, u32[]{:S(2)}) copy-start(f32[8,128]{1,0:T(8,128)S(1)} %get-tuple-element.34.refs_8_) | copy-start | bytes 12292
  62.8 10.8 %collective-permute-start.8 = (bf16[2,64,256]{2,1,0:T(8,128)(2,1)S(1)}, bf16[2,64,256]{2,1,0:T(8,128)(2,1)S(1)}, u32[]{:S(2)}, u32[]{:S(2)}) collective-permute-start(bf16[2,64,256]{2,1,0:T(8,128)(2,1)S(1)} %get-tuple-element.41), channel_id=1, source_target_pairs={{0,4},{4,0},{8,12},{12,8},{16,20},{20,16},{24,28},{28,24},{1,5},{5... | collective-permute-start | bytes 196616 | tf_op jit(solution)/shard_map/ppermute | solution.py:472
  63.0 18.1 %collective-permute-start.9 = (bf16[2,64,256]{2,1,0:T(8,128)(2,1)S(1)}, bf16[2,64,256]{2,1,0:T(8,128)(2,1)S(1)}, u32[]{:S(2)}, u32[]{:S(2)}) collective-permute-start(bf16[2,64,256]{2,1,0:T(8,128)(2,1)S(1)} %get-tuple-element.42), channel_id=1, source_target_pairs={{0,8},{4,12},{8,0},{12,4},{16,24},{20,28},{24,16},{28,20},{1,9},{5... | collective-permute-start | bytes 196616 | tf_op jit(solution)/shard_map/ppermute | solution.py:472
  63.3 26.8 %collective-permute-start.10 = (bf16[2,64,256]{2,1,0:T(8,128)(2,1)S(1)}, bf16[2,64,256]{2,1,0:T(8,128)(2,1)S(1)}, u32[]{:S(2)}, u32[]{:S(2)}) collective-permute-start(bf16[2,64,256]{2,1,0:T(8,128)(2,1)S(1)} %get-tuple-element.43), channel_id=1, source_target_pairs={{0,12},{4,8},{8,4},{12,0},{16,28},{20,24},{24,20},{28,16},{1,13},{... | collective-permute-start | bytes 196616 | tf_op jit(solution)/shard_map/ppermute | solution.py:472
  64.7 25.5 %collective-permute-start.11 = (bf16[2,64,256]{2,1,0:T(8,128)(2,1)S(1)}, bf16[2,64,256]{2,1,0:T(8,128)(2,1)S(1)}, u32[]{:S(2)}, u32[]{:S(2)}) collective-permute-start(bf16[2,64,256]{2,1,0:T(8,128)(2,1)S(1)} %get-tuple-element.44), channel_id=1, source_target_pairs={{0,16},{4,20},{8,24},{12,28},{16,0},{20,4},{24,8},{28,12},{1,17},{... | collective-permute-start | bytes 196616 | tf_op jit(solution)/shard_map/ppermute | solution.py:472
  66.1 24.0 %collective-permute-start.12 = (bf16[2,64,256]{2,1,0:T(8,128)(2,1)S(1)}, bf16[2,64,256]{2,1,0:T(8,128)(2,1)S(1)}, u32[]{:S(2)}, u32[]{:S(2)}) collective-permute-start(bf16[2,64,256]{2,1,0:T(8,128)(2,1)S(1)} %get-tuple-element.45), channel_id=1, source_target_pairs={{0,20},{4,16},{8,28},{12,24},{16,4},{20,0},{24,12},{28,8},{1,21},{... | collective-permute-start | bytes 196616 | tf_op jit(solution)/shard_map/ppermute | solution.py:472
  73.6 16.6 %collective-permute-start.13 = (bf16[2,64,256]{2,1,0:T(8,128)(2,1)S(1)}, bf16[2,64,256]{2,1,0:T(8,128)(2,1)S(1)}, u32[]{:S(2)}, u32[]{:S(2)}) collective-permute-start(bf16[2,64,256]{2,1,0:T(8,128)(2,1)S(1)} %get-tuple-element.46), channel_id=1, source_target_pairs={{0,24},{4,28},{8,16},{12,20},{16,8},{20,12},{24,0},{28,4},{1,25},{... | collective-permute-start | bytes 196616 | tf_op jit(solution)/shard_map/ppermute | solution.py:472
  81.1 9.1 %collective-permute-start.14 = (bf16[2,64,256]{2,1,0:T(8,128)(2,1)S(1)}, bf16[2,64,256]{2,1,0:T(8,128)(2,1)S(1)}, u32[]{:S(2)}, u32[]{:S(2)}) collective-permute-start(bf16[2,64,256]{2,1,0:T(8,128)(2,1)S(1)} %get-tuple-element.47), channel_id=1, source_target_pairs={{0,28},{4,24},{8,20},{12,16},{16,12},{20,8},{24,4},{28,0},{1,29},{... | collective-permute-start | bytes 196616 | tf_op jit(solution)/shard_map/ppermute | solution.py:472
  82.8 0.7 copy-start.5
  86.0 16.4 %all-to-all-start.2 = ((bf16[8,2,64,256]{3,2,1,0:T(8,128)(2,1)}), bf16[8,2,64,256]{3,2,1,0:T(8,128)(2,1)S(1)}, u32[]{:S(2)}, u32[]{:S(2)}) async-start(bf16[8,2,64,256]{3,2,1,0:T(8,128)(2,1)} %get-tuple-element.38), calls=%async_computation.2 | async-start | bytes 1048576 | tf_op jit(solution)/shard_map/all_to_all | solution.py:522
  90.2 1.2 copy-start.4
  91.4 11.0 %copy-start.3 = (f32[1024,256]{1,0:T(8,128)S(1)}, f32[1024,256]{1,0:T(8,128)}, u32[]{:S(2)}) copy-start(f32[1024,256]{1,0:T(8,128)} %get-tuple-element.35.home_ref) | copy-start | bytes 3145732
  92.2 6.9 %collective-permute-start.15 = (bf16[256,256]{1,0:T(8,128)(2,1)S(1)}, bf16[256,256]{1,0:T(8,128)(2,1)S(1)}, u32[]{:S(2)}, u32[]{:S(2)}) collective-permute-start(bf16[256,256]{1,0:T(8,128)(2,1)S(1)} %get-tuple-element.50), channel_id=1, source_target_pairs={{0,1},{1,0},{2,3},{3,2},{4,5},{5,4},{6,7},{7,6},{8,9},{9,8},{10,11... | collective-permute-start | bytes 393224 | tf_op jit(solution)/shard_map/ppermute | solution.py:472
  92.8 9.6 %collective-permute-start.16 = (bf16[256,256]{1,0:T(8,128)(2,1)S(1)}, bf16[256,256]{1,0:T(8,128)(2,1)S(1)}, u32[]{:S(2)}, u32[]{:S(2)}) collective-permute-start(bf16[256,256]{1,0:T(8,128)(2,1)S(1)} %get-tuple-element.51), channel_id=1, source_target_pairs={{0,2},{1,3},{2,0},{3,1},{4,6},{5,7},{6,4},{7,5},{8,10},{9,11},{10,... | collective-permute-start | bytes 393224 | tf_op jit(solution)/shard_map/ppermute | solution.py:472
  103.2 0.6 copy-start.2
  103.8 9.2 %copy-start.1 = (s32[2]{0:T(128)S(1)}, s32[2]{0:T(128)}, u32[]{:S(2)}) copy-start(s32[2]{0:T(128)} %pad_add_fusion.side_ref) | copy-start | bytes 28
  103.8 9.2 %collective-permute-start.20 = (bf16[4,512,1024]{2,1,0:T(8,128)(2,1)}, bf16[4,512,1024]{2,1,0:T(8,128)(2,1)S(1)}, u32[]{:S(2)}, u32[]{:S(2)}) collective-permute-start(bf16[4,512,1024]{2,1,0:T(8,128)(2,1)} %after.7.refs_4_), channel_id=1, source_target_pairs={{0,4},{4,0},{8,12},{12,8},{16,20},{20,16},{24,28},{28,24},{1,5},{5... | collective-permute-start | bytes 12582920 | tf_op jit(solution)/shard_map/ppermute | solution.py:534
  103.8 9.2 %collective-permute-start.21 = (bf16[256,256]{1,0:T(8,128)(2,1)S(1)}, bf16[256,256]{1,0:T(8,128)(2,1)S(1)}, u32[]{:S(2)}, u32[]{:S(2)}) collective-permute-start(bf16[256,256]{1,0:T(8,128)(2,1)S(1)} %get-tuple-element.58), channel_id=1, source_target_pairs={{0,3},{1,2},{2,1},{3,0},{4,7},{5,6},{6,5},{7,4},{8,11},{9,10},{10,... | collective-permute-start | bytes 393224 | tf_op jit(solution)/shard_map/ppermute | solution.py:472
  104.4 12.7 %collective-permute-start.17 = (bf16[256,256]{1,0:T(8,128)(2,1)S(1)}, bf16[256,256]{1,0:T(8,128)(2,1)S(1)}, u32[]{:S(2)}, u32[]{:S(2)}) collective-permute-start(bf16[256,256]{1,0:T(8,128)(2,1)S(1)} %get-tuple-element.53), channel_id=1, source_target_pairs={{0,1},{1,0},{2,3},{3,2},{4,5},{5,4},{6,7},{7,6},{8,9},{9,8},{10,11... | collective-permute-start | bytes 393224 | tf_op jit(solution)/shard_map/ppermute | solution.py:472
  108.0 9.9 %collective-permute-start.18 = (bf16[256,256]{1,0:T(8,128)(2,1)S(1)}, bf16[256,256]{1,0:T(8,128)(2,1)S(1)}, u32[]{:S(2)}, u32[]{:S(2)}) collective-permute-start(bf16[256,256]{1,0:T(8,128)(2,1)S(1)} %get-tuple-element.54), channel_id=1, source_target_pairs={{0,2},{1,3},{2,0},{3,1},{4,6},{5,7},{6,4},{7,5},{8,10},{9,11},{10,... | collective-permute-start | bytes 393224 | tf_op jit(solution)/shard_map/ppermute | solution.py:472
  108.0 15.8 %collective-permute-start.19 = (bf16[256,256]{1,0:T(8,128)(2,1)S(1)}, bf16[256,256]{1,0:T(8,128)(2,1)S(1)}, u32[]{:S(2)}, u32[]{:S(2)}) collective-permute-start(bf16[256,256]{1,0:T(8,128)(2,1)S(1)} %get-tuple-element.55), channel_id=1, source_target_pairs={{0,3},{1,2},{2,1},{3,0},{4,7},{5,6},{6,5},{7,4},{8,11},{9,10},{10,... | collective-permute-start | bytes 393224 | tf_op jit(solution)/shard_map/ppermute | solution.py:472
  113.0 2.2 %copy-start = (bf16[4,512,1024]{2,1,0:T(8,128)(2,1)S(1)}, bf16[4,512,1024]{2,1,0:T(8,128)(2,1)}, u32[]{:S(2)}) copy-start(bf16[4,512,1024]{2,1,0:T(8,128)(2,1)} %after.7.refs_4_) | copy-start | bytes 12582916
Sparse Core Ops, SparseCore 0:
  11.4 79.4 all-gather.2

commit v12 on v11

--- a/solution.py
+++ b/solution.py
@@ -100,37 +100,52 @@
     return total[:, :HEAD_SIZE] / total[:, HEAD_SIZE:]
 
 
+def start_copies(source, target, sems, first, rows):
+    count = sems.shape[0]
+    each = rows // count
+    copies = []
+    for i in range(count):
+        copies.append(
+            pltpu.make_async_copy(
+                source(pl.ds(first + i * each, each)), target(pl.ds(i * each, each)), sems.at[i]
+            )
+        )
+        copies[-1].start()
+    return copies
+
+
 def edge_kernel(k_ref, v_ref, k_ends_ref, v_ends_ref, *refs):
-    rim_ref, sum_ref = refs[-2:]
-    rim_ref[0] = k_ref[...]
-    rim_ref[1] = v_ref[...]
-
-    @pl.when(pl.program_id(0) == 0)
-    def _():
-        for number, ref in enumerate((k_ends_ref, v_ends_ref)):
-            rows = ref[...].astype(F32)[:, 16 - SUMCOLS :]
-            sum_ref[number] = rows.reshape(sum_ref.shape[1:]).astype(BF16)
+    rim_ref, sum_ref, k_sems, v_sems = refs[-4:]
+    first = k_ref.shape[0] - WINDOW
+    copies = start_copies(
+        lambda rows: k_ref.at[rows], lambda rows: rim_ref.at[0, rows], k_sems, first, WINDOW
+    )
+    copies += start_copies(
+        lambda rows: v_ref.at[rows], lambda rows: rim_ref.at[1, rows], v_sems, first, WINDOW
+    )
+    for number, ref in enumerate((k_ends_ref, v_ends_ref)):
+        rows = ref[...].astype(F32)[:, 16 - SUMCOLS :]
+        sum_ref[number] = rows.reshape(sum_ref.shape[1:]).astype(BF16)
+    for copy in copies:
+        copy.wait()
 
 
 def edges(keys, values, waits):
     tokens_dev, width = keys.shape
     blocks = tokens_dev // BLOCK
-    first = (tokens_dev - WINDOW) // TILE
-    source = pl.BlockSpec((TILE, width), lambda i: (first + i, 0))
+    anywhere = pl.BlockSpec(memory_space=pl.ANY)
     ends = pl.BlockSpec((blocks, 16, width), lambda i: (0, BLOCK // 16 - 1, 0))
     shape = (2, blocks * SUMCOLS, width)
     return pl.pallas_call(
         edge_kernel,
-        grid=(WINDOW // TILE,),
-        in_specs=[source] * 2 + [ends] * 2 + moments(waits),
-        out_specs=[
-            pl.BlockSpec((2, TILE, width), lambda i: (0, i, 0)),
-            pl.BlockSpec(shape, lambda i: (0, 0, 0)),
-        ],
+        grid=(1,),
+        in_specs=[anywhere] * 2 + [ends] * 2 + moments(waits),
+        out_specs=[anywhere, pl.BlockSpec(shape, lambda i: (0, 0, 0))],
         out_shape=[
             jax.ShapeDtypeStruct((2, WINDOW, width), BF16),
             jax.ShapeDtypeStruct(shape, BF16),
         ],
+        scratch_shapes=[pltpu.SemaphoreType.DMA((2,))] * 2,
         compiler_params=params(60),
         cost_estimate=cost(0, 8 * WINDOW * width),
         name="edges",
@@ -143,46 +158,54 @@
     )
 
 
-def cut_kernel(side_ref, weight_ref, *refs):
-    refs[-1][...] = weight_ref[...]
-
-
-def cut(side, weight, size, first, waits):
-    rows = weight.shape[0]
+def cut_kernel(side_ref, weight_ref, o_ref, sems):
+    rows, half = o_ref.shape
+    columns = pl.ds(pl.multiple_of(side_ref[0] * half, half), half)
+    copies = start_copies(
+        lambda rows: weight_ref.at[rows, columns], lambda rows: o_ref.at[rows], sems, 0, rows
+    )
+    for copy in copies:
+        copy.wait()
+
+
+def cut(side, weight):
+    rows, width = weight.shape
+    anywhere = pl.BlockSpec(memory_space=pl.ANY)
     return pl.pallas_call(
         cut_kernel,
-        grid_spec=pltpu.PrefetchScalarGridSpec(
-            num_scalar_prefetch=1,
-            grid=(4,),
-            in_specs=[pl.BlockSpec((rows // 4, size), lambda i, side: (i, first + side[0]))]
-            + moments(waits),
-            out_specs=pl.BlockSpec((rows // 4, size), lambda i, side: (i, 0)),
-        ),
-        out_shape=jax.ShapeDtypeStruct((rows, size), BF16),
+        in_specs=[pl.BlockSpec(memory_space=pltpu.SMEM), anywhere],
+        out_specs=anywhere,
+        out_shape=jax.ShapeDtypeStruct((rows, width // 2), BF16),
+        scratch_shapes=[pltpu.SemaphoreType.DMA((4,))],
         compiler_params=params(60),
-        cost_estimate=cost(0, 4 * rows * size),
+        cost_estimate=cost(0, 2 * rows * width),
         name="cut",
-    )(side, weight, *waits)
+    )(side, weight)
 
 
 def prep_kernel(q_ref, k_ref, v_ref, *refs):
     send_ref = refs[-1]
     matrix = regroup_matrix()
-    ctx, _, per, rows, width = send_ref.shape
+    ctx, _, per, _, width = send_ref.shape
+    rows = TILE // STRIDE
     for number, ref in enumerate((q_ref, k_ref, v_ref)):
-        grouped = dot(matrix, ref[...]).astype(BF16)
-        send_ref[:, number] = grouped.reshape(ctx, per, rows, width)
+        for t in range(ref.shape[0] // TILE):
+            grouped = dot(matrix, ref[t * TILE : (t + 1) * TILE]).astype(BF16)
+            send_ref[:, number, :, t * rows : (t + 1) * rows] = grouped.reshape(
+                ctx, per, rows, width
+            )
 
 
 def prepare(queries, keys, values, ctx, chunk, chunks, waits):
     tokens_dev, width = queries.shape
     per = STRIDE // ctx
     part = width // chunks
+    size = tokens_dev // 2 if tokens_dev % (2 * TILE) == 0 else TILE
     return pl.pallas_call(
         prep_kernel,
-        grid=(tokens_dev // TILE,),
-        in_specs=[pl.BlockSpec((TILE, part), lambda b: (b, chunk))] * 3 + moments(waits),
-        out_specs=pl.BlockSpec((ctx, 3, per, TILE // STRIDE, part), lambda b: (0, 0, 0, b, 0)),
+        grid=(tokens_dev // size,),
+        in_specs=[pl.BlockSpec((size, part), lambda b: (b, chunk))] * 3 + moments(waits),
+        out_specs=pl.BlockSpec((ctx, 3, per, size // STRIDE, part), lambda b: (0, 0, 0, b, 0)),
         out_shape=jax.ShapeDtypeStruct((ctx, 3, per, tokens_dev // STRIDE, part), BF16),
         compiler_params=params(60),
         cost_estimate=cost(6 * tokens_dev * TILE * part, 12 * tokens_dev * part),
@@ -472,7 +495,7 @@
             moved.append(lax.ppermute(slabs[slot], axis, pairs))
         return moved
 
-    weight_half = cut(sides, out_weight, out_weight.shape[1] // 2, 0, ())
+    weight_half = cut(sides, out_weight)
     mine = lax.all_gather(weight_half, "head", axis=0)
     rim, picked = edges(keys, values, (weight_half,))
     between, within, order = gather_ctx(picked)

time: 134 us -> 196 us (1.46)
  Pallas kernels: 39.6 us -> 98.5 us
  waiting for transfers between devices: 36.5 us -> 39.4 us
    pallas_call x4, Pallas kernels: 14.8 us -> 73.7 us  [the longest x1 34.5 us: edges(): pl.pallas_call(edge_kernel, grid=(1,), in_specs=[anywhere] * 2 + [ends] *...]
  transfers between devices with their start and end apart: 26 -> 26, of which waited for: 10 -> 11; matrix products, arithmetic and copies ran while one was open for 0% -> 0% of each run, Pallas kernels for 25% -> 32%
where the time goes in v12:
time: 196 us; the launch traced here: 195 us
  Pallas kernels  98.5 us (50%)
  waiting for transfers between devices  39.4 us (20%)
  starting transfers between devices  36.1 us (18%)
  between operations  13.6 us (7%)
  local copies, waits for them, and re-layouts  6.93 us (4%)
    pallas_call x1, Pallas kernels, edges(): pl.pallas_call(edge_kernel, grid=(1,), in_specs=[anywhere] * 2 + [ends] *...  34.5 us
    pallas_call x1, Pallas kernels, cut(): pl.pallas_call(cut_kernel, in_specs=[pl.BlockSpec(memory_space=pltpu.SMEM...  33.6 us
    ppermute x13, waiting for transfers between devices, exchange(): moved.append(lax.ppermute(slabs[slot], axis, pairs))  23.2 us
    ppermute x13, starting transfers between devices, exchange(): moved.append(lax.ppermute(slabs[slot], axis, pairs))  15.7 us
    pallas_call x2, Pallas kernels, home_sections(): pl.pallas_call(functools.partial(home_kernel, order=order), grid=(heads,)...  14.2 us
    ppermute x1, waiting for transfers between devices, body(): before = lax.ppermute(rim, 'ctx', [(i, i + 1) for i in range(ctx - 1)])  10.7 us
    all_to_all x2, starting transfers between devices, body(): lax.all_to_all(send, 'ctx', split_axis=0, concat_axis=0, tiled=True)  8.32 us
    unnamed x32, local copies, waits for them, and re-layouts  6.93 us
  transfers between devices with their start and end apart: 26, of which 11 were waited for; matrix products, arithmetic and copies ran while one was open for 0% of the time, Pallas kernels for 32%

profile of v12, /device:TPU:10, one launch (start us, length us, event | category | flops | bytes accessed | tf_op | source)
XLA Modules:
  0.0 195.3 jit_solution(1155529300781419923)
XLA Ops:
  6.5 0.6 pad_add_fusion.side_ref
  7.2 33.6 %cut.1.refs_0_ = bf16[512,1024]{1,0:T(8,128)(2,1)} custom-call(s32[2]{0:T(128)} %pad_add_fusion.side_ref, bf16[512,2048]{1,0:T(8,128)(2,1)} %weight_ref.1), custom_call_target="tpu_custom_call" | custom-call | bytes 2097152 | tf_op jit(solution)/shard_map/cut/pallas_call | solution.py:174
  40.8 34.5 %edges.1 = (bf16[2,512,512]{2,1,0:T(8,128)(2,1)}, bf16[2,64,512]{2,1,0:T(8,128)(2,1)}) custom-call(bf16[1024,512]{1,0:T(8,128)(2,1)} %k_ref.9, bf16[1024,512]{1,0:T(8,128)(2,1)} %v_ref.9, bf16[8,128,512]{2,1,0:T(8,128)(2,1)} %bitcast.7, bf16[8,128,512]{2,1,0:T(8,128)(2,1)} %bitcast.8, bf16[512,1024]{1,0:T(8,128)(2,1)} %cut.1.refs_0_), custom_call_target="tpu_custom_call" | custom-call | bytes 2097152 | tf_op jit(solution)/shard_map/edges/pallas_call | solution.py:139
  75.3 1.6 collective-permute-start.2
  76.9 0.5 collective-permute-start.1
  77.4 1.5 collective-permute-start
  78.9 2.8 %prepare.2.refs_4_.refs_0_ = bf16[8,3,2,64,256]{4,3,2,1,0:T(8,128)(2,1)} custom-call(bf16[1024,512]{1,0:T(8,128)(2,1)} %q_ref.7, bf16[1024,512]{1,0:T(8,128)(2,1)} %k_ref.9, bf16[1024,512]{1,0:T(8,128)(2,1)} %v_ref.9, bf16[512,1024]{1,0:T(8,128)(2,1)} %cut.1.refs_0_), custom_call_target="tpu_custom_call" | custom-call | flops 402653184 | bytes 3145728 | tf_op jit(solution)/shard_map/prepare/pallas_call | solution.py:204
  81.7 1.2 collective-permute-done.2.refs_3_
  82.9 1.7 collective-permute-done.1.refs_2_
  84.6 0.5 copy-done.8
  85.3 2.1 %collective-permute-start.3 = (bf16[2,512,512]{2,1,0:T(8,128)(2,1)}, bf16[2,512,512]{2,1,0:T(8,128)(2,1)S(1)}, u32[]{:S(2)}, u32[]{:S(2)}) collective-permute-start(bf16[2,512,512]{2,1,0:T(8,128)(2,1)} %after.4.refs_1_), channel_id=1, source_target_pairs={{0,4},{4,8},{8,12},{12,16},{16,20},{20,24},{24,28},{1,5},{5,9},{9,... | collective-permute-start | bytes 3145736 | tf_op jit(solution)/shard_map/ppermute | solution.py:511
  87.4 1.6 collective-permute-start.7
  89.0 0.4 collective-permute-start.6
  89.6 4.1 %all-to-all-start = ((bf16[8,3,2,64,256]{4,3,2,1,0:T(8,128)(2,1)}), bf16[8,3,2,64,256]{4,3,2,1,0:T(8,128)(2,1)S(1)}, u32[]{:S(2)}, u32[]{:S(2)}) async-start(bf16[8,3,2,64,256]{4,3,2,1,0:T(8,128)(2,1)} %after.5), calls=%async_computation | async-start | bytes 3145728 | tf_op jit(solution)/shard_map/all_to_all | solution.py:539
  93.7 0.6 copy-done.10
  94.4 2.8 %prepare.3.refs_0_ = bf16[8,3,2,64,256]{4,3,2,1,0:T(8,128)(2,1)} custom-call(bf16[1024,512]{1,0:T(8,128)(2,1)} %q_ref.7, bf16[1024,512]{1,0:T(8,128)(2,1)} %k_ref.9, bf16[1024,512]{1,0:T(8,128)(2,1)} %v_ref.9, bf16[2,64,512]{2,1,0:T(8,128)(2,1)} %copy-done.10), custom_call_target="tpu_custom_call" | custom-call | flops 402653184 | bytes 3145728 | tf_op jit(solution)/shard_map/prepare/pallas_call | solution.py:204
  97.2 10.7 %collective-permute-done.3.rim_ref = bf16[2,512,512]{2,1,0:T(8,128)(2,1)S(1)} collective-permute-done((bf16[2,512,512]{2,1,0:T(8,128)(2,1)}, bf16[2,512,512]{2,1,0:T(8,128)(2,1)S(1)}, u32[]{:S(2)}, u32[]{:S(2)}) %collective-permute-start.3) | collective-permute-done | bytes 1048608 | tf_op jit(solution)/shard_map/ppermute | solution.py:511
  107.9 1.0 copy-done.11
  108.9 7.1 %home.3 = (f32[1024,256]{1,0:T(8,128)}, f32[8,128]{1,0:T(8,128)}) custom-call(s32[1]{0:T(128)} %bitcast.2.place_ref, bf16[1024,512]{1,0:T(8,128)(2,1)} %q_ref.7, bf16[1024,512]{1,0:T(8,128)(2,1)} %k_ref.9, bf16[1024,512]{1,0:T(8,128)(2,1)} %v_ref.9, bf16[2,512,512]{2,1,0:T(8,128)(2,1)} %copy-done.11, bf16[2,64,512]{2,1,0:T(8,128)(2,1)} %get-tuple-element.33.refs_0_, ...), custom_call_target="tpu_custom_call" | custom-call | flops 21474836480 | bytes 7340032 | tf_op jit(solution)/shard_map/home/pallas_call | solution.py:271
  116.0 2.6 %all-to-all-done.x_ref = bf16[8,3,2,64,256]{4,3,2,1,0:T(8,128)(2,1)S(1)} async-done(((bf16[8,3,2,64,256]{4,3,2,1,0:T(8,128)(2,1)}), bf16[8,3,2,64,256]{4,3,2,1,0:T(8,128)(2,1)S(1)}, u32[]{:S(2)}, u32[]{:S(2)}) %all-to-all-start) | async-done | bytes 1572896 | tf_op jit(solution)/shard_map/all_to_all | solution.py:539
  118.6 4.3 %all-to-all-start.1 = ((bf16[8,3,2,64,256]{4,3,2,1,0:T(8,128)(2,1)}), bf16[8,3,2,64,256]{4,3,2,1,0:T(8,128)(2,1)S(1)}, u32[]{:S(2)}, u32[]{:S(2)}) async-start(bf16[8,3,2,64,256]{4,3,2,1,0:T(8,128)(2,1)} %after.6), calls=%async_computation.1 | async-start | bytes 3145728 | tf_op jit(solution)/shard_map/all_to_all | solution.py:539
  122.8 1.8 stride.2
  125.2 1.4 collective-permute-start.10
  126.6 1.5 collective-permute-start.11
  128.4 7.1 %home.2 = (f32[1024,256]{1,0:T(8,128)}, f32[8,128]{1,0:T(8,128)}) custom-call(s32[1]{0:T(128)} %bitcast.2.place_ref, bf16[1024,512]{1,0:T(8,128)(2,1)} %q_ref.7, bf16[1024,512]{1,0:T(8,128)(2,1)} %k_ref.9, bf16[1024,512]{1,0:T(8,128)(2,1)} %v_ref.9, bf16[2,512,512]{2,1,0:T(8,128)(2,1)} %copy-done.11, bf16[2,64,512]{2,1,0:T(8,128)(2,1)} %get-tuple-element.33.refs_0_, ...), custom_call_target="tpu_custom_call" | custom-call | flops 21474836480 | bytes 7340032 | tf_op jit(solution)/shard_map/home/pallas_call | solution.py:271
  135.5 1.7 collective-permute-start.13
  137.2 5.8 %collective-permute-done.9.refs_2_ = bf16[2,64,256]{2,1,0:T(8,128)(2,1)S(1)} collective-permute-done((bf16[2,64,256]{2,1,0:T(8,128)(2,1)S(1)}, bf16[2,64,256]{2,1,0:T(8,128)(2,1)S(1)}, u32[]{:S(2)}, u32[]{:S(2)}) %collective-permute-start.9) | collective-permute-done | bytes 65568 | tf_op jit(solution)/shard_map/ppermute | solution.py:495
  142.9 1.6 collective-permute-start.14
  144.6 0.7 copy-done.5
  145.2 2.5 %stride.3 = (bf16[8,2,64,256]{3,2,1,0:T(8,128)(2,1)}, f32[8,128]{1,0:T(8,128)S(1)}) custom-call(s32[1]{0:T(128)} %bitcast.2.place_ref, bf16[8,3,2,64,256]{4,3,2,1,0:T(8,128)(2,1)S(1)} %all-to-all-done.1.x_ref, f32[8,128]{1,0:T(8,128)S(1)} %copy-done.5), custom_call_target="tpu_custom_call" | custom-call | flops 805306368 | bytes 2097152 | tf_op jit(solution)/shard_map/stride/pallas_call | solution.py:334
  147.8 4.2 %all-to-all-start.2 = ((bf16[8,2,64,256]{3,2,1,0:T(8,128)(2,1)}), bf16[8,2,64,256]{3,2,1,0:T(8,128)(2,1)S(1)}, u32[]{:S(2)}, u32[]{:S(2)}) async-start(bf16[8,2,64,256]{3,2,1,0:T(8,128)(2,1)} %get-tuple-element.38), calls=%async_computation.2 | async-start | bytes 1048576 | tf_op jit(solution)/shard_map/all_to_all | solution.py:545
  152.1 1.2 copy-done.4
  153.3 0.8 combine.2
  154.1 0.5 collective-permute-start.15
  154.6 2.6 %collective-permute-start.16 = (bf16[256,256]{1,0:T(8,128)(2,1)S(1)}, bf16[256,256]{1,0:T(8,128)(2,1)S(1)}, u32[]{:S(2)}, u32[]{:S(2)}) collective-permute-start(bf16[256,256]{1,0:T(8,128)(2,1)S(1)} %get-tuple-element.51), channel_id=1, source_target_pairs={{0,2},{1,3},{2,0},{3,1},{4,6},{5,7},{6,4},{7,5},{8,10},{9,11},{10,... | collective-permute-start | bytes 393224 | tf_op jit(solution)/shard_map/ppermute | solution.py:495
  157.2 3.8 %collective-permute-done.15.refs_2_.refs_1_ = bf16[256,256]{1,0:T(8,128)(2,1)S(1)} collective-permute-done((bf16[256,256]{1,0:T(8,128)(2,1)S(1)}, bf16[256,256]{1,0:T(8,128)(2,1)S(1)}, u32[]{:S(2)}, u32[]{:S(2)}) %collective-permute-start.15) | collective-permute-done | bytes 131104 | tf_op jit(solution)/shard_map/ppermute | solution.py:495
  161.0 3.2 %collective-permute-done.16.refs_3_.refs_2_ = bf16[256,256]{1,0:T(8,128)(2,1)S(1)} collective-permute-done((bf16[256,256]{1,0:T(8,128)(2,1)S(1)}, bf16[256,256]{1,0:T(8,128)(2,1)S(1)}, u32[]{:S(2)}, u32[]{:S(2)}) %collective-permute-start.16) | collective-permute-done | bytes 131104 | tf_op jit(solution)/shard_map/ppermute | solution.py:495
  164.3 0.9 combine.3
  165.1 0.6 copy-done.2
  165.7 0.5 collective-permute-start.21
  166.2 3.6 %collective-permute-start.17 = (bf16[256,256]{1,0:T(8,128)(2,1)S(1)}, bf16[256,256]{1,0:T(8,128)(2,1)S(1)}, u32[]{:S(2)}, u32[]{:S(2)}) collective-permute-start(bf16[256,256]{1,0:T(8,128)(2,1)S(1)} %get-tuple-element.53), channel_id=1, source_target_pairs={{0,1},{1,0},{2,3},{3,2},{4,5},{5,4},{6,7},{7,6},{8,9},{9,8},{10,11... | collective-permute-start | bytes 393224 | tf_op jit(solution)/shard_map/ppermute | solution.py:495
  169.8 1.5 collective-permute-start.19
  171.3 3.6 %collective-permute-done.21.refs_3_ = bf16[256,256]{1,0:T(8,128)(2,1)S(1)} collective-permute-done((bf16[256,256]{1,0:T(8,128)(2,1)S(1)}, bf16[256,256]{1,0:T(8,128)(2,1)S(1)}, u32[]{:S(2)}, u32[]{:S(2)}) %collective-permute-start.21) | collective-permute-done | bytes 131104 | tf_op jit(solution)/shard_map/ppermute | solution.py:495
  174.9 2.2 %copy-done = bf16[4,512,1024]{2,1,0:T(8,128)(2,1)S(1)} copy-done((bf16[4,512,1024]{2,1,0:T(8,128)(2,1)S(1)}, bf16[4,512,1024]{2,1,0:T(8,128)(2,1)}, u32[]{:S(2)}) %copy-start) | copy-done | bytes 4194328
  177.1 1.8 project.2.refs_6_
  178.9 0.8 collective-permute-done.18.refs_2_
  179.8 5.9 %collective-permute-done.19.refs_3_ = bf16[256,256]{1,0:T(8,128)(2,1)S(1)} collective-permute-done((bf16[256,256]{1,0:T(8,128)(2,1)S(1)}, bf16[256,256]{1,0:T(8,128)(2,1)S(1)}, u32[]{:S(2)}, u32[]{:S(2)}) %collective-permute-start.19) | collective-permute-done | bytes 131104 | tf_op jit(solution)/shard_map/ppermute | solution.py:495
  185.7 2.8 %project.3 = bf16[256,2048]{1,0:T(8,128)(2,1)} custom-call(s32[2]{0:T(128)S(1)} %copy-done.1, bf16[256,256]{1,0:T(8,128)(2,1)S(1)} %get-tuple-element.52.refs_0_, bf16[256,256]{1,0:T(8,128)(2,1)S(1)} %collective-permute-done.17.refs_1_, bf16[256,256]{1,0:T(8,128)(2,1)S(1)} %collective-permute-done.18.refs_2_, ...), custom_call_target="tpu_custom_call" | custom-call | flops 1073741824 | bytes 4718592 | tf_op jit(solution)/shard_map/project/pallas_call | solution.py:419
  (55 shorter events, 1.4 us)
Async XLA Ops:
  6.5 159.2 %all-gather.3.cloned.1.call-start = ((), (), s32[]{:S(2)}) async-start(), calls=%async_computation.3 | async-start | bytes 5242880 | tf_op jit(solution)/shard_map/all_gather | solution.py:499
  75.3 7.6 %collective-permute-start.2 = (bf16[2,64,512]{2,1,0:T(8,128)(2,1)}, bf16[2,64,512]{2,1,0:T(8,128)(2,1)S(1)}, u32[]{:S(2)}, u32[]{:S(2)}) collective-permute-start(bf16[2,64,512]{2,1,0:T(8,128)(2,1)} %get-tuple-element.33.refs_0_), channel_id=1, source_target_pairs={{0,24},{4,28},{8,16},{12,20},{16,8},{20,12},{24,0},{28,4},{1,25},{... | collective-permute-start | bytes 393224 | tf_op jit(solution)/shard_map/ppermute | solution.py:436
  76.9 7.7 %collective-permute-start.1 = (bf16[2,64,512]{2,1,0:T(8,128)(2,1)}, bf16[2,64,512]{2,1,0:T(8,128)(2,1)S(1)}, u32[]{:S(2)}, u32[]{:S(2)}) collective-permute-start(bf16[2,64,512]{2,1,0:T(8,128)(2,1)} %get-tuple-element.33.refs_0_), channel_id=1, source_target_pairs={{0,16},{4,20},{8,24},{12,28},{16,0},{20,4},{24,8},{28,12},{1,17},{... | collective-permute-start | bytes 393224 | tf_op jit(solution)/shard_map/ppermute | solution.py:436
  77.4 7.3 %collective-permute-start = (bf16[2,64,512]{2,1,0:T(8,128)(2,1)}, bf16[2,64,512]{2,1,0:T(8,128)(2,1)S(1)}, u32[]{:S(2)}, u32[]{:S(2)}) collective-permute-start(bf16[2,64,512]{2,1,0:T(8,128)(2,1)} %get-tuple-element.33.refs_0_), channel_id=1, source_target_pairs={{0,8},{4,12},{8,0},{12,4},{16,24},{20,28},{24,16},{28,20},{1,9},{5... | collective-permute-start | bytes 393224 | tf_op jit(solution)/shard_map/ppermute | solution.py:436
  82.9 1.8 copy-start.7
  84.5 0.7 copy-start.8
  84.6 0.6 copy-start.9
  85.3 3.7 %copy-start.12 = (bf16[2,64,512]{2,1,0:T(8,128)(2,1)S(1)}, bf16[2,64,512]{2,1,0:T(8,128)(2,1)}, u32[]{:S(2)}) copy-start(bf16[2,64,512]{2,1,0:T(8,128)(2,1)} %get-tuple-element.33.refs_0_) | copy-start | bytes 393220
  85.3 22.6 %collective-permute-start.3 = (bf16[2,512,512]{2,1,0:T(8,128)(2,1)}, bf16[2,512,512]{2,1,0:T(8,128)(2,1)S(1)}, u32[]{:S(2)}, u32[]{:S(2)}) collective-permute-start(bf16[2,512,512]{2,1,0:T(8,128)(2,1)} %after.4.refs_1_), channel_id=1, source_target_pairs={{0,4},{4,8},{8,12},{12,16},{16,20},{20,24},{24,28},{1,5},{5,9},{9,... | collective-permute-start | bytes 3145736 | tf_op jit(solution)/shard_map/ppermute | solution.py:511
  87.4 6.3 %collective-permute-start.7 = (bf16[2,64,512]{2,1,0:T(8,128)(2,1)}, bf16[2,64,512]{2,1,0:T(8,128)(2,1)S(1)}, u32[]{:S(2)}, u32[]{:S(2)}) collective-permute-start(bf16[2,64,512]{2,1,0:T(8,128)(2,1)} %copy-done.7), channel_id=1, source_target_pairs={{0,4},{4,0},{8,12},{12,8},{16,20},{20,16},{24,28},{28,24},{1,5},{5... | collective-permute-start | bytes 393224 | tf_op jit(solution)/shard_map/ppermute | solution.py:436
  89.0 8.2 %collective-permute-start.4 = (bf16[2,64,512]{2,1,0:T(8,128)(2,1)S(1)}, bf16[2,64,512]{2,1,0:T(8,128)(2,1)S(1)}, u32[]{:S(2)}, u32[]{:S(2)}) collective-permute-start(bf16[2,64,512]{2,1,0:T(8,128)(2,1)S(1)} %copy-done.12), channel_id=1, source_target_pairs={{0,4},{4,0},{8,12},{12,8},{16,20},{20,16},{24,28},{28,24},{1,5},{5... | collective-permute-start | bytes 393224 | tf_op jit(solution)/shard_map/ppermute | solution.py:436
  89.0 8.1 %collective-permute-start.6 = (bf16[2,64,512]{2,1,0:T(8,128)(2,1)}, bf16[2,64,512]{2,1,0:T(8,128)(2,1)S(1)}, u32[]{:S(2)}, u32[]{:S(2)}) collective-permute-start(bf16[2,64,512]{2,1,0:T(8,128)(2,1)} %copy-done.8), channel_id=1, source_target_pairs={{0,4},{4,0},{8,12},{12,8},{16,20},{20,16},{24,28},{28,24},{1,5},{5... | collective-permute-start | bytes 393224 | tf_op jit(solution)/shard_map/ppermute | solution.py:436
  89.5 7.7 %collective-permute-start.5 = (bf16[2,64,512]{2,1,0:T(8,128)(2,1)}, bf16[2,64,512]{2,1,0:T(8,128)(2,1)S(1)}, u32[]{:S(2)}, u32[]{:S(2)}) collective-permute-start(bf16[2,64,512]{2,1,0:T(8,128)(2,1)} %copy-done.9), channel_id=1, source_target_pairs={{0,4},{4,0},{8,12},{12,8},{16,20},{20,16},{24,28},{28,24},{1,5},{5... | collective-permute-start | bytes 393224 | tf_op jit(solution)/shard_map/ppermute | solution.py:436
  89.6 29.0 %all-to-all-start = ((bf16[8,3,2,64,256]{4,3,2,1,0:T(8,128)(2,1)}), bf16[8,3,2,64,256]{4,3,2,1,0:T(8,128)(2,1)S(1)}, u32[]{:S(2)}, u32[]{:S(2)}) async-start(bf16[8,3,2,64,256]{4,3,2,1,0:T(8,128)(2,1)} %after.5), calls=%async_computation | async-start | bytes 3145728 | tf_op jit(solution)/shard_map/all_to_all | solution.py:539
  93.7 0.7 copy-start.10
  97.2 10.8 %copy-start.13 = (bf16[2,64,512]{2,1,0:T(8,128)(2,1)}, bf16[2,64,512]{2,1,0:T(8,128)(2,1)S(1)}, u32[]{:S(2)}) copy-start(bf16[2,64,512]{2,1,0:T(8,128)(2,1)S(1)} %collective-permute-done.4.refs_4_) | copy-start | bytes 393220
  97.2 10.8 %copy-start.14 = (bf16[2,64,512]{2,1,0:T(8,128)(2,1)}, bf16[2,64,512]{2,1,0:T(8,128)(2,1)S(1)}, u32[]{:S(2)}) copy-start(bf16[2,64,512]{2,1,0:T(8,128)(2,1)S(1)} %collective-permute-done.6.refs_6_) | copy-start | bytes 393220
  97.2 10.7 %copy-start.15 = (bf16[2,64,512]{2,1,0:T(8,128)(2,1)}, bf16[2,64,512]{2,1,0:T(8,128)(2,1)S(1)}, u32[]{:S(2)}) copy-start(bf16[2,64,512]{2,1,0:T(8,128)(2,1)S(1)} %collective-permute-done.5.refs_5_) | copy-start | bytes 393220
  107.9 1.0 copy-start.11
  118.6 26.0 %all-to-all-start.1 = ((bf16[8,3,2,64,256]{4,3,2,1,0:T(8,128)(2,1)}), bf16[8,3,2,64,256]{4,3,2,1,0:T(8,128)(2,1)S(1)}, u32[]{:S(2)}, u32[]{:S(2)}) async-start(bf16[8,3,2,64,256]{4,3,2,1,0:T(8,128)(2,1)} %after.6), calls=%async_computation.1 | async-start | bytes 3145728 | tf_op jit(solution)/shard_map/all_to_all | solution.py:539
  124.6 3.7 %copy-start.6 = (f32[8,128]{1,0:T(8,128)}, f32[8,128]{1,0:T(8,128)S(1)}, u32[]{:S(2)}) copy-start(f32[8,128]{1,0:T(8,128)S(1)} %get-tuple-element.34.refs_8_) | copy-start | bytes 12292
  124.6 10.8 %collective-permute-start.8 = (bf16[2,64,256]{2,1,0:T(8,128)(2,1)S(1)}, bf16[2,64,256]{2,1,0:T(8,128)(2,1)S(1)}, u32[]{:S(2)}, u32[]{:S(2)}) collective-permute-start(bf16[2,64,256]{2,1,0:T(8,128)(2,1)S(1)} %get-tuple-element.41), channel_id=1, source_target_pairs={{0,4},{4,0},{8,12},{12,8},{16,20},{20,16},{24,28},{28,24},{1,5},{5... | collective-permute-start | bytes 196616 | tf_op jit(solution)/shard_map/ppermute | solution.py:495
  124.8 18.1 %collective-permute-start.9 = (bf16[2,64,256]{2,1,0:T(8,128)(2,1)S(1)}, bf16[2,64,256]{2,1,0:T(8,128)(2,1)S(1)}, u32[]{:S(2)}, u32[]{:S(2)}) collective-permute-start(bf16[2,64,256]{2,1,0:T(8,128)(2,1)S(1)} %get-tuple-element.42), channel_id=1, source_target_pairs={{0,8},{4,12},{8,0},{12,4},{16,24},{20,28},{24,16},{28,20},{1,9},{5... | collective-permute-start | bytes 196616 | tf_op jit(solution)/shard_map/ppermute | solution.py:495
  125.2 26.8 %collective-permute-start.10 = (bf16[2,64,256]{2,1,0:T(8,128)(2,1)S(1)}, bf16[2,64,256]{2,1,0:T(8,128)(2,1)S(1)}, u32[]{:S(2)}, u32[]{:S(2)}) collective-permute-start(bf16[2,64,256]{2,1,0:T(8,128)(2,1)S(1)} %get-tuple-element.43), channel_id=1, source_target_pairs={{0,12},{4,8},{8,4},{12,0},{16,28},{20,24},{24,20},{28,16},{1,13},{... | collective-permute-start | bytes 196616 | tf_op jit(solution)/shard_map/ppermute | solution.py:495
  126.6 25.5 %collective-permute-start.11 = (bf16[2,64,256]{2,1,0:T(8,128)(2,1)S(1)}, bf16[2,64,256]{2,1,0:T(8,128)(2,1)S(1)}, u32[]{:S(2)}, u32[]{:S(2)}) collective-permute-start(bf16[2,64,256]{2,1,0:T(8,128)(2,1)S(1)} %get-tuple-element.44), channel_id=1, source_target_pairs={{0,16},{4,20},{8,24},{12,28},{16,0},{20,4},{24,8},{28,12},{1,17},{... | collective-permute-start | bytes 196616 | tf_op jit(solution)/shard_map/ppermute | solution.py:495
  128.0 24.0 %collective-permute-start.12 = (bf16[2,64,256]{2,1,0:T(8,128)(2,1)S(1)}, bf16[2,64,256]{2,1,0:T(8,128)(2,1)S(1)}, u32[]{:S(2)}, u32[]{:S(2)}) collective-permute-start(bf16[2,64,256]{2,1,0:T(8,128)(2,1)S(1)} %get-tuple-element.45), channel_id=1, source_target_pairs={{0,20},{4,16},{8,28},{12,24},{16,4},{20,0},{24,12},{28,8},{1,21},{... | collective-permute-start | bytes 196616 | tf_op jit(solution)/shard_map/ppermute | solution.py:495
  135.5 16.6 %collective-permute-start.13 = (bf16[2,64,256]{2,1,0:T(8,128)(2,1)S(1)}, bf16[2,64,256]{2,1,0:T(8,128)(2,1)S(1)}, u32[]{:S(2)}, u32[]{:S(2)}) collective-permute-start(bf16[2,64,256]{2,1,0:T(8,128)(2,1)S(1)} %get-tuple-element.46), channel_id=1, source_target_pairs={{0,24},{4,28},{8,16},{12,20},{16,8},{20,12},{24,0},{28,4},{1,25},{... | collective-permute-start | bytes 196616 | tf_op jit(solution)/shard_map/ppermute | solution.py:495
  142.9 9.1 %collective-permute-start.14 = (bf16[2,64,256]{2,1,0:T(8,128)(2,1)S(1)}, bf16[2,64,256]{2,1,0:T(8,128)(2,1)S(1)}, u32[]{:S(2)}, u32[]{:S(2)}) collective-permute-start(bf16[2,64,256]{2,1,0:T(8,128)(2,1)S(1)} %get-tuple-element.47), channel_id=1, source_target_pairs={{0,28},{4,24},{8,20},{12,16},{16,12},{20,8},{24,4},{28,0},{1,29},{... | collective-permute-start | bytes 196616 | tf_op jit(solution)/shard_map/ppermute | solution.py:495
  144.6 0.7 copy-start.5
  147.8 16.5 %all-to-all-start.2 = ((bf16[8,2,64,256]{3,2,1,0:T(8,128)(2,1)}), bf16[8,2,64,256]{3,2,1,0:T(8,128)(2,1)S(1)}, u32[]{:S(2)}, u32[]{:S(2)}) async-start(bf16[8,2,64,256]{3,2,1,0:T(8,128)(2,1)} %get-tuple-element.38), calls=%async_computation.2 | async-start | bytes 1048576 | tf_op jit(solution)/shard_map/all_to_all | solution.py:545
  152.1 1.2 copy-start.4
  153.3 11.0 %copy-start.3 = (f32[1024,256]{1,0:T(8,128)S(1)}, f32[1024,256]{1,0:T(8,128)}, u32[]{:S(2)}) copy-start(f32[1024,256]{1,0:T(8,128)} %get-tuple-element.35.home_ref) | copy-start | bytes 3145732
  154.1 6.9 %collective-permute-start.15 = (bf16[256,256]{1,0:T(8,128)(2,1)S(1)}, bf16[256,256]{1,0:T(8,128)(2,1)S(1)}, u32[]{:S(2)}, u32[]{:S(2)}) collective-permute-start(bf16[256,256]{1,0:T(8,128)(2,1)S(1)} %get-tuple-element.50), channel_id=1, source_target_pairs={{0,1},{1,0},{2,3},{3,2},{4,5},{5,4},{6,7},{7,6},{8,9},{9,8},{10,11... | collective-permute-start | bytes 393224 | tf_op jit(solution)/shard_map/ppermute | solution.py:495
  154.6 9.6 %collective-permute-start.16 = (bf16[256,256]{1,0:T(8,128)(2,1)S(1)}, bf16[256,256]{1,0:T(8,128)(2,1)S(1)}, u32[]{:S(2)}, u32[]{:S(2)}) collective-permute-start(bf16[256,256]{1,0:T(8,128)(2,1)S(1)} %get-tuple-element.51), channel_id=1, source_target_pairs={{0,2},{1,3},{2,0},{3,1},{4,6},{5,7},{6,4},{7,5},{8,10},{9,11},{10,... | collective-permute-start | bytes 393224 | tf_op jit(solution)/shard_map/ppermute | solution.py:495
  165.1 0.6 copy-start.2
  165.7 9.2 %copy-start.1 = (s32[2]{0:T(128)S(1)}, s32[2]{0:T(128)}, u32[]{:S(2)}) copy-start(s32[2]{0:T(128)} %pad_add_fusion.side_ref) | copy-start | bytes 28
  165.7 9.2 %collective-permute-start.20 = (bf16[4,512,1024]{2,1,0:T(8,128)(2,1)}, bf16[4,512,1024]{2,1,0:T(8,128)(2,1)S(1)}, u32[]{:S(2)}, u32[]{:S(2)}) collective-permute-start(bf16[4,512,1024]{2,1,0:T(8,128)(2,1)} %after.7.refs_4_), channel_id=1, source_target_pairs={{0,4},{4,0},{8,12},{12,8},{16,20},{20,16},{24,28},{28,24},{1,5},{5... | collective-permute-start | bytes 12582920 | tf_op jit(solution)/shard_map/ppermute | solution.py:557
  165.7 9.2 %collective-permute-start.21 = (bf16[256,256]{1,0:T(8,128)(2,1)S(1)}, bf16[256,256]{1,0:T(8,128)(2,1)S(1)}, u32[]{:S(2)}, u32[]{:S(2)}) collective-permute-start(bf16[256,256]{1,0:T(8,128)(2,1)S(1)} %get-tuple-element.58), channel_id=1, source_target_pairs={{0,3},{1,2},{2,1},{3,0},{4,7},{5,6},{6,5},{7,4},{8,11},{9,10},{10,... | collective-permute-start | bytes 393224 | tf_op jit(solution)/shard_map/ppermute | solution.py:495
  166.2 12.7 %collective-permute-start.17 = (bf16[256,256]{1,0:T(8,128)(2,1)S(1)}, bf16[256,256]{1,0:T(8,128)(2,1)S(1)}, u32[]{:S(2)}, u32[]{:S(2)}) collective-permute-start(bf16[256,256]{1,0:T(8,128)(2,1)S(1)} %get-tuple-element.53), channel_id=1, source_target_pairs={{0,1},{1,0},{2,3},{3,2},{4,5},{5,4},{6,7},{7,6},{8,9},{9,8},{10,11... | collective-permute-start | bytes 393224 | tf_op jit(solution)/shard_map/ppermute | solution.py:495
  169.8 9.9 %collective-permute-start.18 = (bf16[256,256]{1,0:T(8,128)(2,1)S(1)}, bf16[256,256]{1,0:T(8,128)(2,1)S(1)}, u32[]{:S(2)}, u32[]{:S(2)}) collective-permute-start(bf16[256,256]{1,0:T(8,128)(2,1)S(1)} %get-tuple-element.54), channel_id=1, source_target_pairs={{0,2},{1,3},{2,0},{3,1},{4,6},{5,7},{6,4},{7,5},{8,10},{9,11},{10,... | collective-permute-start | bytes 393224 | tf_op jit(solution)/shard_map/ppermute | solution.py:495
  169.8 15.8 %collective-permute-start.19 = (bf16[256,256]{1,0:T(8,128)(2,1)S(1)}, bf16[256,256]{1,0:T(8,128)(2,1)S(1)}, u32[]{:S(2)}, u32[]{:S(2)}) collective-permute-start(bf16[256,256]{1,0:T(8,128)(2,1)S(1)} %get-tuple-element.55), channel_id=1, source_target_pairs={{0,3},{1,2},{2,1},{3,0},{4,7},{5,6},{6,5},{7,4},{8,11},{9,10},{10,... | collective-permute-start | bytes 393224 | tf_op jit(solution)/shard_map/ppermute | solution.py:495
  174.9 2.2 %copy-start = (bf16[4,512,1024]{2,1,0:T(8,128)(2,1)S(1)}, bf16[4,512,1024]{2,1,0:T(8,128)(2,1)}, u32[]{:S(2)}) copy-start(bf16[4,512,1024]{2,1,0:T(8,128)(2,1)} %after.7.refs_4_) | copy-start | bytes 12582916
Sparse Core Ops, SparseCore 0:
  40.9 79.4 all-gather.2

commit v13 on v12

--- a/solution.py
+++ b/solution.py
@@ -100,34 +100,38 @@
     return total[:, :HEAD_SIZE] / total[:, HEAD_SIZE:]
 
 
-def start_copies(source, target, sems, first, rows):
-    count = sems.shape[0]
-    each = rows // count
-    copies = []
-    for i in range(count):
-        copies.append(
-            pltpu.make_async_copy(
-                source(pl.ds(first + i * each, each)), target(pl.ds(i * each, each)), sems.at[i]
-            )
-        )
-        copies[-1].start()
+def start_copies(sources, held, sems):
+    copies = [
+        pltpu.make_async_copy(source, held.at[i], sems.at[0, i])
+        for i, source in enumerate(sources)
+    ]
+    for copy in copies:
+        copy.start()
     return copies
 
 
+def finish_copies(copies, held, targets, sems):
+    leaving = []
+    for i, (copy, target) in enumerate(zip(copies, targets)):
+        copy.wait()
+        leaving.append(pltpu.make_async_copy(held.at[i], target, sems.at[1, i]))
+        leaving[-1].start()
+    for copy in leaving:
+        copy.wait()
+
+
 def edge_kernel(k_ref, v_ref, k_ends_ref, v_ends_ref, *refs):
-    rim_ref, sum_ref, k_sems, v_sems = refs[-4:]
+    rim_ref, sum_ref, held, sems = refs[-4:]
     first = k_ref.shape[0] - WINDOW
-    copies = start_copies(
-        lambda rows: k_ref.at[rows], lambda rows: rim_ref.at[0, rows], k_sems, first, WINDOW
-    )
-    copies += start_copies(
-        lambda rows: v_ref.at[rows], lambda rows: rim_ref.at[1, rows], v_sems, first, WINDOW
-    )
+    size = held.shape[1]
+    pieces = range(WINDOW // size)
+    sources = [ref.at[pl.ds(first + i * size, size)] for ref in (k_ref, v_ref) for i in pieces]
+    targets = [rim_ref.at[n, pl.ds(i * size, size)] for n in range(2) for i in pieces]
+    copies = start_copies(sources, held, sems)
     for number, ref in enumerate((k_ends_ref, v_ends_ref)):
         rows = ref[...].astype(F32)[:, 16 - SUMCOLS :]
         sum_ref[number] = rows.reshape(sum_ref.shape[1:]).astype(BF16)
-    for copy in copies:
-        copy.wait()
+    finish_copies(copies, held, targets, sems)
 
 
 def edges(keys, values, waits):
@@ -145,7 +149,10 @@
             jax.ShapeDtypeStruct((2, WINDOW, width), BF16),
             jax.ShapeDtypeStruct(shape, BF16),
         ],
-        scratch_shapes=[pltpu.SemaphoreType.DMA((2,))] * 2,
+        scratch_shapes=[
+            pltpu.VMEM((4, WINDOW // 2, width), BF16),
+            pltpu.SemaphoreType.DMA((2, 4)),
+        ],
         compiler_params=params(60),
         cost_estimate=cost(0, 8 * WINDOW * width),
         name="edges",
@@ -158,29 +165,35 @@
     )
 
 
-def cut_kernel(side_ref, weight_ref, o_ref, sems):
-    rows, half = o_ref.shape
-    columns = pl.ds(pl.multiple_of(side_ref[0] * half, half), half)
+def cut_kernel(weight_ref, o_ref, held, sems):
+    half = o_ref.shape[1]
+    size = held.shape[1]
+    side = lax.axis_index("ctx") % 2
+    columns = pl.ds(pl.multiple_of(side * half, half), half)
+    pieces = range(held.shape[0])
     copies = start_copies(
-        lambda rows: weight_ref.at[rows, columns], lambda rows: o_ref.at[rows], sems, 0, rows
+        [weight_ref.at[pl.ds(i * size, size), columns] for i in pieces], held, sems
     )
-    for copy in copies:
-        copy.wait()
-
-
-def cut(side, weight):
+    finish_copies(copies, held, [o_ref.at[pl.ds(i * size, size)] for i in pieces], sems)
+
+
+def cut(weight):
     rows, width = weight.shape
+    pieces = 4
     anywhere = pl.BlockSpec(memory_space=pl.ANY)
     return pl.pallas_call(
         cut_kernel,
-        in_specs=[pl.BlockSpec(memory_space=pltpu.SMEM), anywhere],
+        in_specs=[anywhere],
         out_specs=anywhere,
         out_shape=jax.ShapeDtypeStruct((rows, width // 2), BF16),
-        scratch_shapes=[pltpu.SemaphoreType.DMA((4,))],
+        scratch_shapes=[
+            pltpu.VMEM((pieces, rows // pieces, width // 2), BF16),
+            pltpu.SemaphoreType.DMA((2, pieces)),
+        ],
         compiler_params=params(60),
         cost_estimate=cost(0, 2 * rows * width),
         name="cut",
-    )(side, weight)
+    )(weight)
 
 
 def prep_kernel(q_ref, k_ref, v_ref, *refs):
@@ -495,7 +508,7 @@
             moved.append(lax.ppermute(slabs[slot], axis, pairs))
         return moved
 
-    weight_half = cut(sides, out_weight)
+    weight_half = cut(out_weight)
     mine = lax.all_gather(weight_half, "head", axis=0)
     rim, picked = edges(keys, values, (weight_half,))
     between, within, order = gather_ctx(picked)

time: 196 us -> 135 us (0.69)
  Pallas kernels: 98.5 us -> 39.5 us
    pallas_call x1, Pallas kernels: 33.6 us -> 1.98 us  [cut(): pl.pallas_call(cut_kernel, in_specs=[anywhere], out_specs=anywhere, out_s...]
    pallas_call x1, Pallas kernels: 34.5 us -> 3.69 us  [edges(): pl.pallas_call(edge_kernel, grid=(1,), in_specs=[anywhere] * 2 + [ends] *...]
    pallas_call x2, Pallas kernels: 4.6 us -> 7.87 us  [project(): pl.pallas_call(functools.partial(project_kernel, slots=slots, chunk=chunk...]
    unnamed x32 -> x30, local copies, waits for them, and re-layouts: 6.93 us -> 6.95 us
  transfers between devices with their start and end apart: 26 -> 26, of which waited for: 11 -> 10; matrix products, arithmetic and copies ran while one was open for 0% -> 0% of each run, Pallas kernels for 32% -> 25%
where the time goes in v13:
time: 135 us; the launch traced here: 134 us
  Pallas kernels  39.5 us (29%)
  waiting for transfers between devices  37.7 us (28%)
  starting transfers between devices  36 us (27%)
  between operations  13.6 us (10%)
  local copies, waits for them, and re-layouts  6.95 us (5%)
    ppermute x13, waiting for transfers between devices, exchange(): moved.append(lax.ppermute(slabs[slot], axis, pairs))  21.5 us
    ppermute x13, starting transfers between devices, exchange(): moved.append(lax.ppermute(slabs[slot], axis, pairs))  15.8 us
    pallas_call x2, Pallas kernels, home_sections(): pl.pallas_call(functools.partial(home_kernel, order=order), grid=(heads,)...  14.2 us
    ppermute x1, waiting for transfers between devices, body(): before = lax.ppermute(rim, 'ctx', [(i, i + 1) for i in range(ctx - 1)])  10.7 us
    all_to_all x2, starting transfers between devices, body(): lax.all_to_all(send, 'ctx', split_axis=0, concat_axis=0, tiled=True)  8.31 us
    pallas_call x2, Pallas kernels, project(): pl.pallas_call(functools.partial(project_kernel, slots=slots, chunk=chunk...  7.87 us
    unnamed x30, local copies, waits for them, and re-layouts  6.95 us
    ppermute x7, starting transfers between devices, swapped(): return lax.ppermute(piece, 'ctx', [(i, i ^ distance) for i in range(count)])  5.78 us
  transfers between devices with their start and end apart: 26, of which 10 were waited for; matrix products, arithmetic and copies ran while one was open for 0% of the time, Pallas kernels for 25%

profile of v13, /device:TPU:10, one launch (start us, length us, event | category | flops | bytes accessed | tf_op | source)
XLA Modules:
  0.0 133.9 jit_solution(544717637448686570)
XLA Ops:
  6.5 2.0 %cut.1.refs_0_ = bf16[512,1024]{1,0:T(8,128)(2,1)} custom-call(bf16[512,2048]{1,0:T(8,128)(2,1)} %weight_ref.1), custom_call_target="tpu_custom_call" | custom-call | bytes 2097152 | tf_op jit(solution)/shard_map/cut/pallas_call | solution.py:184
  8.5 3.7 %edges.1 = (bf16[2,512,512]{2,1,0:T(8,128)(2,1)}, bf16[2,64,512]{2,1,0:T(8,128)(2,1)}) custom-call(bf16[1024,512]{1,0:T(8,128)(2,1)} %k_ref.9, bf16[1024,512]{1,0:T(8,128)(2,1)} %v_ref.9, bf16[8,128,512]{2,1,0:T(8,128)(2,1)} %bitcast.7, bf16[8,128,512]{2,1,0:T(8,128)(2,1)} %bitcast.8, bf16[512,1024]{1,0:T(8,128)(2,1)} %cut.1.refs_0_), custom_call_target="tpu_custom_call" | custom-call | bytes 2097152 | tf_op jit(solution)/shard_map/edges/pallas_call | solution.py:143
  12.2 1.6 %collective-permute-start.2 = (bf16[2,64,512]{2,1,0:T(8,128)(2,1)}, bf16[2,64,512]{2,1,0:T(8,128)(2,1)S(1)}, u32[]{:S(2)}, u32[]{:S(2)}) collective-permute-start(bf16[2,64,512]{2,1,0:T(8,128)(2,1)} %get-tuple-element.33.refs_0_), channel_id=1, source_target_pairs={{0,24},{4,28},{8,16},{12,20},{16,8},{20,12},{24,0},{28,4},{1,25},{... | collective-permute-start | bytes 393224 | tf_op jit(solution)/shard_map/ppermute | solution.py:449
  13.8 0.5 collective-permute-start.1
  14.3 1.5 %collective-permute-start = (bf16[2,64,512]{2,1,0:T(8,128)(2,1)}, bf16[2,64,512]{2,1,0:T(8,128)(2,1)S(1)}, u32[]{:S(2)}, u32[]{:S(2)}) collective-permute-start(bf16[2,64,512]{2,1,0:T(8,128)(2,1)} %get-tuple-element.33.refs_0_), channel_id=1, source_target_pairs={{0,8},{4,12},{8,0},{12,4},{16,24},{20,28},{24,16},{28,20},{1,9},{5... | collective-permute-start | bytes 393224 | tf_op jit(solution)/shard_map/ppermute | solution.py:449
  15.8 2.9 %prepare.2.refs_4_.refs_0_ = bf16[8,3,2,64,256]{4,3,2,1,0:T(8,128)(2,1)} custom-call(bf16[1024,512]{1,0:T(8,128)(2,1)} %q_ref.7, bf16[1024,512]{1,0:T(8,128)(2,1)} %k_ref.9, bf16[1024,512]{1,0:T(8,128)(2,1)} %v_ref.9, bf16[512,1024]{1,0:T(8,128)(2,1)} %cut.1.refs_0_), custom_call_target="tpu_custom_call" | custom-call | flops 402653184 | bytes 3145728 | tf_op jit(solution)/shard_map/prepare/pallas_call | solution.py:217
  18.7 1.1 collective-permute-done.2.refs_3_
  19.8 1.7 %collective-permute-done.1.refs_2_ = bf16[2,64,512]{2,1,0:T(8,128)(2,1)S(1)} collective-permute-done((bf16[2,64,512]{2,1,0:T(8,128)(2,1)}, bf16[2,64,512]{2,1,0:T(8,128)(2,1)S(1)}, u32[]{:S(2)}, u32[]{:S(2)}) %collective-permute-start.1) | collective-permute-done | bytes 131104 | tf_op jit(solution)/shard_map/ppermute | solution.py:449
  21.6 0.5 copy-done.7
  22.2 2.0 %collective-permute-start.3 = (bf16[2,512,512]{2,1,0:T(8,128)(2,1)}, bf16[2,512,512]{2,1,0:T(8,128)(2,1)S(1)}, u32[]{:S(2)}, u32[]{:S(2)}) collective-permute-start(bf16[2,512,512]{2,1,0:T(8,128)(2,1)} %after.4.refs_1_), channel_id=1, source_target_pairs={{0,4},{4,8},{8,12},{12,16},{16,20},{20,24},{24,28},{1,5},{5,9},{9,... | collective-permute-start | bytes 3145736 | tf_op jit(solution)/shard_map/ppermute | solution.py:524
  24.3 1.6 %collective-permute-start.7 = (bf16[2,64,512]{2,1,0:T(8,128)(2,1)}, bf16[2,64,512]{2,1,0:T(8,128)(2,1)S(1)}, u32[]{:S(2)}, u32[]{:S(2)}) collective-permute-start(bf16[2,64,512]{2,1,0:T(8,128)(2,1)} %copy-done.6), channel_id=1, source_target_pairs={{0,4},{4,0},{8,12},{12,8},{16,20},{20,16},{24,28},{28,24},{1,5},{5... | collective-permute-start | bytes 393224 | tf_op jit(solution)/shard_map/ppermute | solution.py:449
  26.0 0.4 collective-permute-start.6
  26.6 4.1 %all-to-all-start = ((bf16[8,3,2,64,256]{4,3,2,1,0:T(8,128)(2,1)}), bf16[8,3,2,64,256]{4,3,2,1,0:T(8,128)(2,1)S(1)}, u32[]{:S(2)}, u32[]{:S(2)}) async-start(bf16[8,3,2,64,256]{4,3,2,1,0:T(8,128)(2,1)} %after.5), calls=%async_computation | async-start | bytes 3145728 | tf_op jit(solution)/shard_map/all_to_all | solution.py:552
  30.6 0.7 copy-done.9
  31.3 2.8 %prepare.3.refs_0_ = bf16[8,3,2,64,256]{4,3,2,1,0:T(8,128)(2,1)} custom-call(bf16[1024,512]{1,0:T(8,128)(2,1)} %q_ref.7, bf16[1024,512]{1,0:T(8,128)(2,1)} %k_ref.9, bf16[1024,512]{1,0:T(8,128)(2,1)} %v_ref.9, bf16[2,64,512]{2,1,0:T(8,128)(2,1)} %copy-done.9), custom_call_target="tpu_custom_call" | custom-call | flops 402653184 | bytes 3145728 | tf_op jit(solution)/shard_map/prepare/pallas_call | solution.py:217
  34.2 10.7 %collective-permute-done.3.rim_ref = bf16[2,512,512]{2,1,0:T(8,128)(2,1)S(1)} collective-permute-done((bf16[2,512,512]{2,1,0:T(8,128)(2,1)}, bf16[2,512,512]{2,1,0:T(8,128)(2,1)S(1)}, u32[]{:S(2)}, u32[]{:S(2)}) %collective-permute-start.3) | collective-permute-done | bytes 1048608 | tf_op jit(solution)/shard_map/ppermute | solution.py:524
  44.9 0.9 copy-done.10
  45.8 7.1 %home.3 = (f32[1024,256]{1,0:T(8,128)}, f32[8,128]{1,0:T(8,128)}) custom-call(s32[1]{0:T(128)} %bitcast.2.place_ref, bf16[1024,512]{1,0:T(8,128)(2,1)} %q_ref.7, bf16[1024,512]{1,0:T(8,128)(2,1)} %k_ref.9, bf16[1024,512]{1,0:T(8,128)(2,1)} %v_ref.9, bf16[2,512,512]{2,1,0:T(8,128)(2,1)} %copy-done.10, bf16[2,64,512]{2,1,0:T(8,128)(2,1)} %get-tuple-element.33.refs_0_, ...), custom_call_target="tpu_custom_call" | custom-call | flops 21474836480 | bytes 7340032 | tf_op jit(solution)/shard_map/home/pallas_call | solution.py:284
  52.9 2.6 %all-to-all-done.x_ref = bf16[8,3,2,64,256]{4,3,2,1,0:T(8,128)(2,1)S(1)} async-done(((bf16[8,3,2,64,256]{4,3,2,1,0:T(8,128)(2,1)}), bf16[8,3,2,64,256]{4,3,2,1,0:T(8,128)(2,1)S(1)}, u32[]{:S(2)}, u32[]{:S(2)}) %all-to-all-start) | async-done | bytes 1572896 | tf_op jit(solution)/shard_map/all_to_all | solution.py:552
  55.5 4.3 %all-to-all-start.1 = ((bf16[8,3,2,64,256]{4,3,2,1,0:T(8,128)(2,1)}), bf16[8,3,2,64,256]{4,3,2,1,0:T(8,128)(2,1)S(1)}, u32[]{:S(2)}, u32[]{:S(2)}) async-start(bf16[8,3,2,64,256]{4,3,2,1,0:T(8,128)(2,1)} %after.6), calls=%async_computation.1 | async-start | bytes 3145728 | tf_op jit(solution)/shard_map/all_to_all | solution.py:552
  59.8 1.8 %stride.2 = (bf16[2,64,256]{2,1,0:T(8,128)(2,1)S(1)}, bf16[2,64,256]{2,1,0:T(8,128)(2,1)S(1)}, bf16[2,64,256]{2,1,0:T(8,128)(2,1)S(1)}, bf16[2,64,256]{2,1,0:T(8...) custom-call(s32[1]{0:T(128)} %bitcast.2.place_ref, ...), custom_call_target="tpu_custom_call" | custom-call | flops 805306368 | bytes 2097152 | tf_op jit(solution)/shard_map/stride/pallas_call | solution.py:347
  61.8 0.4 collective-permute-start.9
  62.2 1.3 %collective-permute-start.10 = (bf16[2,64,256]{2,1,0:T(8,128)(2,1)S(1)}, bf16[2,64,256]{2,1,0:T(8,128)(2,1)S(1)}, u32[]{:S(2)}, u32[]{:S(2)}) collective-permute-start(bf16[2,64,256]{2,1,0:T(8,128)(2,1)S(1)} %get-tuple-element.43), channel_id=1, source_target_pairs={{0,12},{4,8},{8,4},{12,0},{16,28},{20,24},{24,20},{28,16},{1,13},{... | collective-permute-start | bytes 196616 | tf_op jit(solution)/shard_map/ppermute | solution.py:508
  63.5 1.5 %collective-permute-start.11 = (bf16[2,64,256]{2,1,0:T(8,128)(2,1)S(1)}, bf16[2,64,256]{2,1,0:T(8,128)(2,1)S(1)}, u32[]{:S(2)}, u32[]{:S(2)}) collective-permute-start(bf16[2,64,256]{2,1,0:T(8,128)(2,1)S(1)} %get-tuple-element.44), channel_id=1, source_target_pairs={{0,16},{4,20},{8,24},{12,28},{16,0},{20,4},{24,8},{28,12},{1,17},{... | collective-permute-start | bytes 196616 | tf_op jit(solution)/shard_map/ppermute | solution.py:508
  65.0 0.3 collective-permute-start.12
  65.3 7.1 %home.2 = (f32[1024,256]{1,0:T(8,128)}, f32[8,128]{1,0:T(8,128)}) custom-call(s32[1]{0:T(128)} %bitcast.2.place_ref, bf16[1024,512]{1,0:T(8,128)(2,1)} %q_ref.7, bf16[1024,512]{1,0:T(8,128)(2,1)} %k_ref.9, bf16[1024,512]{1,0:T(8,128)(2,1)} %v_ref.9, bf16[2,512,512]{2,1,0:T(8,128)(2,1)} %copy-done.10, bf16[2,64,512]{2,1,0:T(8,128)(2,1)} %get-tuple-element.33.refs_0_, ...), custom_call_target="tpu_custom_call" | custom-call | flops 21474836480 | bytes 7340032 | tf_op jit(solution)/shard_map/home/pallas_call | solution.py:284
  72.4 1.7 %collective-permute-start.13 = (bf16[2,64,256]{2,1,0:T(8,128)(2,1)S(1)}, bf16[2,64,256]{2,1,0:T(8,128)(2,1)S(1)}, u32[]{:S(2)}, u32[]{:S(2)}) collective-permute-start(bf16[2,64,256]{2,1,0:T(8,128)(2,1)S(1)} %get-tuple-element.46), channel_id=1, source_target_pairs={{0,24},{4,28},{8,16},{12,20},{16,8},{20,12},{24,0},{28,4},{1,25},{... | collective-permute-start | bytes 196616 | tf_op jit(solution)/shard_map/ppermute | solution.py:508
  74.1 5.8 %collective-permute-done.9.refs_2_ = bf16[2,64,256]{2,1,0:T(8,128)(2,1)S(1)} collective-permute-done((bf16[2,64,256]{2,1,0:T(8,128)(2,1)S(1)}, bf16[2,64,256]{2,1,0:T(8,128)(2,1)S(1)}, u32[]{:S(2)}, u32[]{:S(2)}) %collective-permute-start.9) | collective-permute-done | bytes 65568 | tf_op jit(solution)/shard_map/ppermute | solution.py:508
  79.9 1.7 %collective-permute-start.14 = (bf16[2,64,256]{2,1,0:T(8,128)(2,1)S(1)}, bf16[2,64,256]{2,1,0:T(8,128)(2,1)S(1)}, u32[]{:S(2)}, u32[]{:S(2)}) collective-permute-start(bf16[2,64,256]{2,1,0:T(8,128)(2,1)S(1)} %get-tuple-element.47), channel_id=1, source_target_pairs={{0,28},{4,24},{8,20},{12,16},{16,12},{20,8},{24,4},{28,0},{1,29},{... | collective-permute-start | bytes 196616 | tf_op jit(solution)/shard_map/ppermute | solution.py:508
  81.6 0.7 copy-done.4
  82.3 2.5 %stride.3 = (bf16[8,2,64,256]{3,2,1,0:T(8,128)(2,1)}, f32[8,128]{1,0:T(8,128)S(1)}) custom-call(s32[1]{0:T(128)} %bitcast.2.place_ref, bf16[8,3,2,64,256]{4,3,2,1,0:T(8,128)(2,1)S(1)} %all-to-all-done.1.x_ref, f32[8,128]{1,0:T(8,128)S(1)} %copy-done.4), custom_call_target="tpu_custom_call" | custom-call | flops 805306368 | bytes 2097152 | tf_op jit(solution)/shard_map/stride/pallas_call | solution.py:347
  84.8 4.1 %all-to-all-start.2 = ((bf16[8,2,64,256]{3,2,1,0:T(8,128)(2,1)}), bf16[8,2,64,256]{3,2,1,0:T(8,128)(2,1)S(1)}, u32[]{:S(2)}, u32[]{:S(2)}) async-start(bf16[8,2,64,256]{3,2,1,0:T(8,128)(2,1)} %get-tuple-element.38), calls=%async_computation.2 | async-start | bytes 1048576 | tf_op jit(solution)/shard_map/all_to_all | solution.py:558
  89.0 1.2 copy-done.3
  90.2 0.8 combine.2
  91.1 0.5 collective-permute-start.15
  91.6 2.6 %collective-permute-start.16 = (bf16[256,256]{1,0:T(8,128)(2,1)S(1)}, bf16[256,256]{1,0:T(8,128)(2,1)S(1)}, u32[]{:S(2)}, u32[]{:S(2)}) collective-permute-start(bf16[256,256]{1,0:T(8,128)(2,1)S(1)} %get-tuple-element.51), channel_id=1, source_target_pairs={{0,2},{1,3},{2,0},{3,1},{4,6},{5,7},{6,4},{7,5},{8,10},{9,11},{10,... | collective-permute-start | bytes 393224 | tf_op jit(solution)/shard_map/ppermute | solution.py:508
  94.2 3.8 %collective-permute-done.15.refs_2_.refs_1_ = bf16[256,256]{1,0:T(8,128)(2,1)S(1)} collective-permute-done((bf16[256,256]{1,0:T(8,128)(2,1)S(1)}, bf16[256,256]{1,0:T(8,128)(2,1)S(1)}, u32[]{:S(2)}, u32[]{:S(2)}) %collective-permute-start.15) | collective-permute-done | bytes 131104 | tf_op jit(solution)/shard_map/ppermute | solution.py:508
  98.0 3.2 %collective-permute-done.16.refs_3_.refs_2_ = bf16[256,256]{1,0:T(8,128)(2,1)S(1)} collective-permute-done((bf16[256,256]{1,0:T(8,128)(2,1)S(1)}, bf16[256,256]{1,0:T(8,128)(2,1)S(1)}, u32[]{:S(2)}, u32[]{:S(2)}) %collective-permute-start.16) | collective-permute-done | bytes 131104 | tf_op jit(solution)/shard_map/ppermute | solution.py:508
  101.2 0.9 combine.3
  102.1 0.6 copy-done.1
  102.7 0.4 collective-permute-start.21
  103.1 3.6 %collective-permute-start.17 = (bf16[256,256]{1,0:T(8,128)(2,1)S(1)}, bf16[256,256]{1,0:T(8,128)(2,1)S(1)}, u32[]{:S(2)}, u32[]{:S(2)}) collective-permute-start(bf16[256,256]{1,0:T(8,128)(2,1)S(1)} %get-tuple-element.53), channel_id=1, source_target_pairs={{0,1},{1,0},{2,3},{3,2},{4,5},{5,4},{6,7},{7,6},{8,9},{9,8},{10,11... | collective-permute-start | bytes 393224 | tf_op jit(solution)/shard_map/ppermute | solution.py:508
  106.7 1.5 %collective-permute-start.19 = (bf16[256,256]{1,0:T(8,128)(2,1)S(1)}, bf16[256,256]{1,0:T(8,128)(2,1)S(1)}, u32[]{:S(2)}, u32[]{:S(2)}) collective-permute-start(bf16[256,256]{1,0:T(8,128)(2,1)S(1)} %get-tuple-element.55), channel_id=1, source_target_pairs={{0,3},{1,2},{2,1},{3,0},{4,7},{5,6},{6,5},{7,4},{8,11},{9,10},{10,... | collective-permute-start | bytes 393224 | tf_op jit(solution)/shard_map/ppermute | solution.py:508
  108.3 3.5 %collective-permute-done.21.refs_3_ = bf16[256,256]{1,0:T(8,128)(2,1)S(1)} collective-permute-done((bf16[256,256]{1,0:T(8,128)(2,1)S(1)}, bf16[256,256]{1,0:T(8,128)(2,1)S(1)}, u32[]{:S(2)}, u32[]{:S(2)}) %collective-permute-start.21) | collective-permute-done | bytes 131104 | tf_op jit(solution)/shard_map/ppermute | solution.py:508
  111.8 2.2 %copy-done = bf16[4,512,1024]{2,1,0:T(8,128)(2,1)S(1)} copy-done((bf16[4,512,1024]{2,1,0:T(8,128)(2,1)S(1)}, bf16[4,512,1024]{2,1,0:T(8,128)(2,1)}, u32[]{:S(2)}) %copy-start) | copy-done | bytes 4194328
  114.0 3.4 %project.2.refs_6_ = f32[256,2048]{1,0:T(8,128)S(1)} custom-call(s32[2]{0:T(128)S(1)} %pad_add_fusion.side_ref, bf16[256,256]{1,0:T(8,128)(2,1)S(1)} %get-tuple-element.57.refs_0_, bf16[256,256]{1,0:T(8,128)(2,1)S(1)} %collective-permute-done.15.refs_2_.refs_1_, bf16[256,256]{1,0:T(8,128)(2,1)S(1)} %collective-permute-done.16.refs_3_.refs_2_, ...), custom_call_target="tpu_custom_call" | custom-call | flops 1073741824 | bytes 4718592 | tf_op jit(solution)/shard_map/project/pallas_call | solution.py:432
  117.5 5.2 %collective-permute-done.19.refs_3_ = bf16[256,256]{1,0:T(8,128)(2,1)S(1)} collective-permute-done((bf16[256,256]{1,0:T(8,128)(2,1)S(1)}, bf16[256,256]{1,0:T(8,128)(2,1)S(1)}, u32[]{:S(2)}, u32[]{:S(2)}) %collective-permute-start.19) | collective-permute-done | bytes 131104 | tf_op jit(solution)/shard_map/ppermute | solution.py:508
  122.6 4.4 %project.3 = bf16[256,2048]{1,0:T(8,128)(2,1)} custom-call(s32[2]{0:T(128)S(1)} %pad_add_fusion.side_ref, bf16[256,256]{1,0:T(8,128)(2,1)S(1)} %get-tuple-element.52.refs_0_, bf16[256,256]{1,0:T(8,128)(2,1)S(1)} %collective-permute-done.17.refs_1_, bf16[256,256]{1,0:T(8,128)(2,1)S(1)} %collective-permute-done.18.refs_2_, ...), custom_call_target="tpu_custom_call" | custom-call | flops 1073741824 | bytes 4718592 | tf_op jit(solution)/shard_map/project/pallas_call | solution.py:432
  (53 shorter events, 0.8 us)
Async XLA Ops:
  6.5 96.1 %all-gather.3.cloned.1.call-start = ((), (), s32[]{:S(2)}) async-start(), calls=%async_computation.3 | async-start | bytes 5242880 | tf_op jit(solution)/shard_map/all_gather | solution.py:512
  12.2 7.6 %collective-permute-start.2 = (bf16[2,64,512]{2,1,0:T(8,128)(2,1)}, bf16[2,64,512]{2,1,0:T(8,128)(2,1)S(1)}, u32[]{:S(2)}, u32[]{:S(2)}) collective-permute-start(bf16[2,64,512]{2,1,0:T(8,128)(2,1)} %get-tuple-element.33.refs_0_), channel_id=1, source_target_pairs={{0,24},{4,28},{8,16},{12,20},{16,8},{20,12},{24,0},{28,4},{1,25},{... | collective-permute-start | bytes 393224 | tf_op jit(solution)/shard_map/ppermute | solution.py:449
  13.8 7.7 %collective-permute-start.1 = (bf16[2,64,512]{2,1,0:T(8,128)(2,1)}, bf16[2,64,512]{2,1,0:T(8,128)(2,1)S(1)}, u32[]{:S(2)}, u32[]{:S(2)}) collective-permute-start(bf16[2,64,512]{2,1,0:T(8,128)(2,1)} %get-tuple-element.33.refs_0_), channel_id=1, source_target_pairs={{0,16},{4,20},{8,24},{12,28},{16,0},{20,4},{24,8},{28,12},{1,17},{... | collective-permute-start | bytes 393224 | tf_op jit(solution)/shard_map/ppermute | solution.py:449
  14.3 7.3 %collective-permute-start = (bf16[2,64,512]{2,1,0:T(8,128)(2,1)}, bf16[2,64,512]{2,1,0:T(8,128)(2,1)S(1)}, u32[]{:S(2)}, u32[]{:S(2)}) collective-permute-start(bf16[2,64,512]{2,1,0:T(8,128)(2,1)} %get-tuple-element.33.refs_0_), channel_id=1, source_target_pairs={{0,8},{4,12},{8,0},{12,4},{16,24},{20,28},{24,16},{28,20},{1,9},{5... | collective-permute-start | bytes 393224 | tf_op jit(solution)/shard_map/ppermute | solution.py:449
  19.8 1.8 %copy-start.6 = (bf16[2,64,512]{2,1,0:T(8,128)(2,1)}, bf16[2,64,512]{2,1,0:T(8,128)(2,1)S(1)}, u32[]{:S(2)}) copy-start(bf16[2,64,512]{2,1,0:T(8,128)(2,1)S(1)} %collective-permute-done.2.refs_3_) | copy-start | bytes 393220
  21.5 0.6 copy-start.7
  21.6 0.7 copy-start.8
  22.2 3.7 %copy-start.11 = (bf16[2,64,512]{2,1,0:T(8,128)(2,1)S(1)}, bf16[2,64,512]{2,1,0:T(8,128)(2,1)}, u32[]{:S(2)}) copy-start(bf16[2,64,512]{2,1,0:T(8,128)(2,1)} %get-tuple-element.33.refs_0_) | copy-start | bytes 393220
  22.2 22.6 %collective-permute-start.3 = (bf16[2,512,512]{2,1,0:T(8,128)(2,1)}, bf16[2,512,512]{2,1,0:T(8,128)(2,1)S(1)}, u32[]{:S(2)}, u32[]{:S(2)}) collective-permute-start(bf16[2,512,512]{2,1,0:T(8,128)(2,1)} %after.4.refs_1_), channel_id=1, source_target_pairs={{0,4},{4,8},{8,12},{12,16},{16,20},{20,24},{24,28},{1,5},{5,9},{9,... | collective-permute-start | bytes 3145736 | tf_op jit(solution)/shard_map/ppermute | solution.py:524
  24.3 6.4 %collective-permute-start.7 = (bf16[2,64,512]{2,1,0:T(8,128)(2,1)}, bf16[2,64,512]{2,1,0:T(8,128)(2,1)S(1)}, u32[]{:S(2)}, u32[]{:S(2)}) collective-permute-start(bf16[2,64,512]{2,1,0:T(8,128)(2,1)} %copy-done.6), channel_id=1, source_target_pairs={{0,4},{4,0},{8,12},{12,8},{16,20},{20,16},{24,28},{28,24},{1,5},{5... | collective-permute-start | bytes 393224 | tf_op jit(solution)/shard_map/ppermute | solution.py:449
  25.9 8.2 %collective-permute-start.4 = (bf16[2,64,512]{2,1,0:T(8,128)(2,1)S(1)}, bf16[2,64,512]{2,1,0:T(8,128)(2,1)S(1)}, u32[]{:S(2)}, u32[]{:S(2)}) collective-permute-start(bf16[2,64,512]{2,1,0:T(8,128)(2,1)S(1)} %copy-done.11), channel_id=1, source_target_pairs={{0,4},{4,0},{8,12},{12,8},{16,20},{20,16},{24,28},{28,24},{1,5},{5... | collective-permute-start | bytes 393224 | tf_op jit(solution)/shard_map/ppermute | solution.py:449
  26.0 8.1 %collective-permute-start.6 = (bf16[2,64,512]{2,1,0:T(8,128)(2,1)}, bf16[2,64,512]{2,1,0:T(8,128)(2,1)S(1)}, u32[]{:S(2)}, u32[]{:S(2)}) collective-permute-start(bf16[2,64,512]{2,1,0:T(8,128)(2,1)} %copy-done.7), channel_id=1, source_target_pairs={{0,4},{4,0},{8,12},{12,8},{16,20},{20,16},{24,28},{28,24},{1,5},{5... | collective-permute-start | bytes 393224 | tf_op jit(solution)/shard_map/ppermute | solution.py:449
  26.4 7.7 %collective-permute-start.5 = (bf16[2,64,512]{2,1,0:T(8,128)(2,1)}, bf16[2,64,512]{2,1,0:T(8,128)(2,1)S(1)}, u32[]{:S(2)}, u32[]{:S(2)}) collective-permute-start(bf16[2,64,512]{2,1,0:T(8,128)(2,1)} %copy-done.8), channel_id=1, source_target_pairs={{0,4},{4,0},{8,12},{12,8},{16,20},{20,16},{24,28},{28,24},{1,5},{5... | collective-permute-start | bytes 393224 | tf_op jit(solution)/shard_map/ppermute | solution.py:449
  26.6 28.9 %all-to-all-start = ((bf16[8,3,2,64,256]{4,3,2,1,0:T(8,128)(2,1)}), bf16[8,3,2,64,256]{4,3,2,1,0:T(8,128)(2,1)S(1)}, u32[]{:S(2)}, u32[]{:S(2)}) async-start(bf16[8,3,2,64,256]{4,3,2,1,0:T(8,128)(2,1)} %after.5), calls=%async_computation | async-start | bytes 3145728 | tf_op jit(solution)/shard_map/all_to_all | solution.py:552
  30.6 0.7 copy-start.9
  34.1 10.7 %copy-start.12 = (bf16[2,64,512]{2,1,0:T(8,128)(2,1)}, bf16[2,64,512]{2,1,0:T(8,128)(2,1)S(1)}, u32[]{:S(2)}) copy-start(bf16[2,64,512]{2,1,0:T(8,128)(2,1)S(1)} %collective-permute-done.4.refs_4_) | copy-start | bytes 393220
  34.1 10.7 %copy-start.13 = (bf16[2,64,512]{2,1,0:T(8,128)(2,1)}, bf16[2,64,512]{2,1,0:T(8,128)(2,1)S(1)}, u32[]{:S(2)}) copy-start(bf16[2,64,512]{2,1,0:T(8,128)(2,1)S(1)} %collective-permute-done.6.refs_6_) | copy-start | bytes 393220
  34.1 10.7 %copy-start.14 = (bf16[2,64,512]{2,1,0:T(8,128)(2,1)}, bf16[2,64,512]{2,1,0:T(8,128)(2,1)S(1)}, u32[]{:S(2)}) copy-start(bf16[2,64,512]{2,1,0:T(8,128)(2,1)S(1)} %collective-permute-done.5.refs_5_) | copy-start | bytes 393220
  44.9 1.0 copy-start.10
  55.5 26.1 %all-to-all-start.1 = ((bf16[8,3,2,64,256]{4,3,2,1,0:T(8,128)(2,1)}), bf16[8,3,2,64,256]{4,3,2,1,0:T(8,128)(2,1)S(1)}, u32[]{:S(2)}, u32[]{:S(2)}) async-start(bf16[8,3,2,64,256]{4,3,2,1,0:T(8,128)(2,1)} %after.6), calls=%async_computation.1 | async-start | bytes 3145728 | tf_op jit(solution)/shard_map/all_to_all | solution.py:552
  61.6 3.7 %copy-start.5 = (f32[8,128]{1,0:T(8,128)}, f32[8,128]{1,0:T(8,128)S(1)}, u32[]{:S(2)}) copy-start(f32[8,128]{1,0:T(8,128)S(1)} %get-tuple-element.34.refs_8_) | copy-start | bytes 12292
  61.6 10.8 %collective-permute-start.8 = (bf16[2,64,256]{2,1,0:T(8,128)(2,1)S(1)}, bf16[2,64,256]{2,1,0:T(8,128)(2,1)S(1)}, u32[]{:S(2)}, u32[]{:S(2)}) collective-permute-start(bf16[2,64,256]{2,1,0:T(8,128)(2,1)S(1)} %get-tuple-element.41), channel_id=1, source_target_pairs={{0,4},{4,0},{8,12},{12,8},{16,20},{20,16},{24,28},{28,24},{1,5},{5... | collective-permute-start | bytes 196616 | tf_op jit(solution)/shard_map/ppermute | solution.py:508
  61.8 18.1 %collective-permute-start.9 = (bf16[2,64,256]{2,1,0:T(8,128)(2,1)S(1)}, bf16[2,64,256]{2,1,0:T(8,128)(2,1)S(1)}, u32[]{:S(2)}, u32[]{:S(2)}) collective-permute-start(bf16[2,64,256]{2,1,0:T(8,128)(2,1)S(1)} %get-tuple-element.42), channel_id=1, source_target_pairs={{0,8},{4,12},{8,0},{12,4},{16,24},{20,28},{24,16},{28,20},{1,9},{5... | collective-permute-start | bytes 196616 | tf_op jit(solution)/shard_map/ppermute | solution.py:508
  62.2 26.8 %collective-permute-start.10 = (bf16[2,64,256]{2,1,0:T(8,128)(2,1)S(1)}, bf16[2,64,256]{2,1,0:T(8,128)(2,1)S(1)}, u32[]{:S(2)}, u32[]{:S(2)}) collective-permute-start(bf16[2,64,256]{2,1,0:T(8,128)(2,1)S(1)} %get-tuple-element.43), channel_id=1, source_target_pairs={{0,12},{4,8},{8,4},{12,0},{16,28},{20,24},{24,20},{28,16},{1,13},{... | collective-permute-start | bytes 196616 | tf_op jit(solution)/shard_map/ppermute | solution.py:508
  63.5 25.5 %collective-permute-start.11 = (bf16[2,64,256]{2,1,0:T(8,128)(2,1)S(1)}, bf16[2,64,256]{2,1,0:T(8,128)(2,1)S(1)}, u32[]{:S(2)}, u32[]{:S(2)}) collective-permute-start(bf16[2,64,256]{2,1,0:T(8,128)(2,1)S(1)} %get-tuple-element.44), channel_id=1, source_target_pairs={{0,16},{4,20},{8,24},{12,28},{16,0},{20,4},{24,8},{28,12},{1,17},{... | collective-permute-start | bytes 196616 | tf_op jit(solution)/shard_map/ppermute | solution.py:508
  65.0 24.0 %collective-permute-start.12 = (bf16[2,64,256]{2,1,0:T(8,128)(2,1)S(1)}, bf16[2,64,256]{2,1,0:T(8,128)(2,1)S(1)}, u32[]{:S(2)}, u32[]{:S(2)}) collective-permute-start(bf16[2,64,256]{2,1,0:T(8,128)(2,1)S(1)} %get-tuple-element.45), channel_id=1, source_target_pairs={{0,20},{4,16},{8,28},{12,24},{16,4},{20,0},{24,12},{28,8},{1,21},{... | collective-permute-start | bytes 196616 | tf_op jit(solution)/shard_map/ppermute | solution.py:508
  72.4 16.6 %collective-permute-start.13 = (bf16[2,64,256]{2,1,0:T(8,128)(2,1)S(1)}, bf16[2,64,256]{2,1,0:T(8,128)(2,1)S(1)}, u32[]{:S(2)}, u32[]{:S(2)}) collective-permute-start(bf16[2,64,256]{2,1,0:T(8,128)(2,1)S(1)} %get-tuple-element.46), channel_id=1, source_target_pairs={{0,24},{4,28},{8,16},{12,20},{16,8},{20,12},{24,0},{28,4},{1,25},{... | collective-permute-start | bytes 196616 | tf_op jit(solution)/shard_map/ppermute | solution.py:508
  79.9 9.1 %collective-permute-start.14 = (bf16[2,64,256]{2,1,0:T(8,128)(2,1)S(1)}, bf16[2,64,256]{2,1,0:T(8,128)(2,1)S(1)}, u32[]{:S(2)}, u32[]{:S(2)}) collective-permute-start(bf16[2,64,256]{2,1,0:T(8,128)(2,1)S(1)} %get-tuple-element.47), channel_id=1, source_target_pairs={{0,28},{4,24},{8,20},{12,16},{16,12},{20,8},{24,4},{28,0},{1,29},{... | collective-permute-start | bytes 196616 | tf_op jit(solution)/shard_map/ppermute | solution.py:508
  81.6 0.7 copy-start.4
  84.8 16.4 %all-to-all-start.2 = ((bf16[8,2,64,256]{3,2,1,0:T(8,128)(2,1)}), bf16[8,2,64,256]{3,2,1,0:T(8,128)(2,1)S(1)}, u32[]{:S(2)}, u32[]{:S(2)}) async-start(bf16[8,2,64,256]{3,2,1,0:T(8,128)(2,1)} %get-tuple-element.38), calls=%async_computation.2 | async-start | bytes 1048576 | tf_op jit(solution)/shard_map/all_to_all | solution.py:558
  89.0 1.2 copy-start.3
  90.2 11.0 %copy-start.2 = (f32[1024,256]{1,0:T(8,128)S(1)}, f32[1024,256]{1,0:T(8,128)}, u32[]{:S(2)}) copy-start(f32[1024,256]{1,0:T(8,128)} %get-tuple-element.35.home_ref) | copy-start | bytes 3145732
  91.1 6.9 %collective-permute-start.15 = (bf16[256,256]{1,0:T(8,128)(2,1)S(1)}, bf16[256,256]{1,0:T(8,128)(2,1)S(1)}, u32[]{:S(2)}, u32[]{:S(2)}) collective-permute-start(bf16[256,256]{1,0:T(8,128)(2,1)S(1)} %get-tuple-element.50), channel_id=1, source_target_pairs={{0,1},{1,0},{2,3},{3,2},{4,5},{5,4},{6,7},{7,6},{8,9},{9,8},{10,11... | collective-permute-start | bytes 393224 | tf_op jit(solution)/shard_map/ppermute | solution.py:508
  91.6 9.6 %collective-permute-start.16 = (bf16[256,256]{1,0:T(8,128)(2,1)S(1)}, bf16[256,256]{1,0:T(8,128)(2,1)S(1)}, u32[]{:S(2)}, u32[]{:S(2)}) collective-permute-start(bf16[256,256]{1,0:T(8,128)(2,1)S(1)} %get-tuple-element.51), channel_id=1, source_target_pairs={{0,2},{1,3},{2,0},{3,1},{4,6},{5,7},{6,4},{7,5},{8,10},{9,11},{10,... | collective-permute-start | bytes 393224 | tf_op jit(solution)/shard_map/ppermute | solution.py:508
  102.1 0.6 copy-start.1
  102.7 9.1 %collective-permute-start.20 = (bf16[4,512,1024]{2,1,0:T(8,128)(2,1)}, bf16[4,512,1024]{2,1,0:T(8,128)(2,1)}, u32[]{:S(2)}, u32[]{:S(2)}) collective-permute-start(bf16[4,512,1024]{2,1,0:T(8,128)(2,1)} %after.7.refs_4_), channel_id=1, source_target_pairs={{0,4},{4,0},{8,12},{12,8},{16,20},{20,16},{24,28},{28,24},{1,5},{5... | collective-permute-start | bytes 12582920 | tf_op jit(solution)/shard_map/ppermute | solution.py:570
  102.7 9.1 %collective-permute-start.21 = (bf16[256,256]{1,0:T(8,128)(2,1)S(1)}, bf16[256,256]{1,0:T(8,128)(2,1)S(1)}, u32[]{:S(2)}, u32[]{:S(2)}) collective-permute-start(bf16[256,256]{1,0:T(8,128)(2,1)S(1)} %get-tuple-element.58), channel_id=1, source_target_pairs={{0,3},{1,2},{2,1},{3,0},{4,7},{5,6},{6,5},{7,4},{8,11},{9,10},{10,... | collective-permute-start | bytes 393224 | tf_op jit(solution)/shard_map/ppermute | solution.py:508
  103.1 14.3 %collective-permute-start.17 = (bf16[256,256]{1,0:T(8,128)(2,1)S(1)}, bf16[256,256]{1,0:T(8,128)(2,1)S(1)}, u32[]{:S(2)}, u32[]{:S(2)}) collective-permute-start(bf16[256,256]{1,0:T(8,128)(2,1)S(1)} %get-tuple-element.53), channel_id=1, source_target_pairs={{0,1},{1,0},{2,3},{3,2},{4,5},{5,4},{6,7},{7,6},{8,9},{9,8},{10,11... | collective-permute-start | bytes 393224 | tf_op jit(solution)/shard_map/ppermute | solution.py:508
  106.7 10.7 %collective-permute-start.18 = (bf16[256,256]{1,0:T(8,128)(2,1)S(1)}, bf16[256,256]{1,0:T(8,128)(2,1)S(1)}, u32[]{:S(2)}, u32[]{:S(2)}) collective-permute-start(bf16[256,256]{1,0:T(8,128)(2,1)S(1)} %get-tuple-element.54), channel_id=1, source_target_pairs={{0,2},{1,3},{2,0},{3,1},{4,6},{5,7},{6,4},{7,5},{8,10},{9,11},{10,... | collective-permute-start | bytes 393224 | tf_op jit(solution)/shard_map/ppermute | solution.py:508
  106.7 15.9 %collective-permute-start.19 = (bf16[256,256]{1,0:T(8,128)(2,1)S(1)}, bf16[256,256]{1,0:T(8,128)(2,1)S(1)}, u32[]{:S(2)}, u32[]{:S(2)}) collective-permute-start(bf16[256,256]{1,0:T(8,128)(2,1)S(1)} %get-tuple-element.55), channel_id=1, source_target_pairs={{0,3},{1,2},{2,1},{3,0},{4,7},{5,6},{6,5},{7,4},{8,11},{9,10},{10,... | collective-permute-start | bytes 393224 | tf_op jit(solution)/shard_map/ppermute | solution.py:508
  111.8 2.2 %copy-start = (bf16[4,512,1024]{2,1,0:T(8,128)(2,1)S(1)}, bf16[4,512,1024]{2,1,0:T(8,128)(2,1)}, u32[]{:S(2)}) copy-start(bf16[4,512,1024]{2,1,0:T(8,128)(2,1)} %after.7.refs_4_) | copy-start | bytes 12582916
Sparse Core Ops, SparseCore 0:
  8.9 79.4 all-gather.2

commit v14 on v13

--- a/solution.py
+++ b/solution.py
@@ -121,37 +121,35 @@
 
 
 def edge_kernel(k_ref, v_ref, k_ends_ref, v_ends_ref, *refs):
-    rim_ref, sum_ref, held, sems = refs[-4:]
-    first = k_ref.shape[0] - WINDOW
-    size = held.shape[1]
-    pieces = range(WINDOW // size)
-    sources = [ref.at[pl.ds(first + i * size, size)] for ref in (k_ref, v_ref) for i in pieces]
-    targets = [rim_ref.at[n, pl.ds(i * size, size)] for n in range(2) for i in pieces]
-    copies = start_copies(sources, held, sems)
-    for number, ref in enumerate((k_ends_ref, v_ends_ref)):
-        rows = ref[...].astype(F32)[:, 16 - SUMCOLS :]
-        sum_ref[number] = rows.reshape(sum_ref.shape[1:]).astype(BF16)
-    finish_copies(copies, held, targets, sems)
+    rim_ref, sum_ref = refs[-2:]
+    rim_ref[0] = k_ref[...]
+    rim_ref[1] = v_ref[...]
+
+    @pl.when(pl.program_id(0) == 0)
+    def _():
+        for number, ref in enumerate((k_ends_ref, v_ends_ref)):
+            rows = ref[...].astype(F32)[:, 16 - SUMCOLS :]
+            sum_ref[number] = rows.reshape(sum_ref.shape[1:]).astype(BF16)
 
 
 def edges(keys, values, waits):
     tokens_dev, width = keys.shape
     blocks = tokens_dev // BLOCK
-    anywhere = pl.BlockSpec(memory_space=pl.ANY)
+    first = (tokens_dev - WINDOW) // TILE
+    source = pl.BlockSpec((TILE, width), lambda i: (first + i, 0))
     ends = pl.BlockSpec((blocks, 16, width), lambda i: (0, BLOCK // 16 - 1, 0))
     shape = (2, blocks * SUMCOLS, width)
     return pl.pallas_call(
         edge_kernel,
-        grid=(1,),
-        in_specs=[anywhere] * 2 + [ends] * 2 + moments(waits),
-        out_specs=[anywhere, pl.BlockSpec(shape, lambda i: (0, 0, 0))],
+        grid=(WINDOW // TILE,),
+        in_specs=[source] * 2 + [ends] * 2 + moments(waits),
+        out_specs=[
+            pl.BlockSpec((2, TILE, width), lambda i: (0, i, 0)),
+            pl.BlockSpec(shape, lambda i: (0, 0, 0)),
+        ],
         out_shape=[
             jax.ShapeDtypeStruct((2, WINDOW, width), BF16),
             jax.ShapeDtypeStruct(shape, BF16),
-        ],
-        scratch_shapes=[
-            pltpu.VMEM((4, WINDOW // 2, width), BF16),
-            pltpu.SemaphoreType.DMA((2, 4)),
         ],
         compiler_params=params(60),
         cost_estimate=cost(0, 8 * WINDOW * width),
@@ -361,7 +359,8 @@
     )(place, moved, *waits)
 
 
-def combine_kernel(seat_ref, home_ref, *refs, slots, arrays, ctx):
+def combine_kernel(home_ref, *refs, slots, arrays, ctx):
+    seat, place = lax.axis_index("head"), lax.axis_index("ctx")
     back_refs, o_refs, mark_ref = refs[:arrays], refs[-slots - 1 : -1], refs[-1]
     mark_ref[...] = jnp.zeros_like(mark_ref)
     tokens_dev, width = home_ref.shape
@@ -370,10 +369,10 @@
     token = iota2((TILE, TILE), 0)
     col = iota2((TILE, TILE), 1)
     group = col >> 4
-    owner = group // per if arrays == 1 else partner(seat_ref[1], group // per, ctx)
+    owner = group // per if arrays == 1 else partner(place, group // per, ctx)
     matrix = (token == (col & 15) * 16 + owner * per + group % per).astype(BF16)
     for slot in range(slots):
-        owner = partner(seat_ref[0], slot, slots)
+        owner = partner(seat, slot, slots)
         for b in range(size // TILE):
             first = owner * (size // TILE) + b
             here = pl.ds(pl.multiple_of(first * STRIDE, STRIDE), STRIDE)
@@ -386,23 +385,23 @@
             o_refs[slot][b * TILE : (b + 1) * TILE] = (home + back).astype(BF16)
 
 
-def combine(seat, home, backs, slots, ctx, waits):
+def combine(home, backs, slots, ctx, waits):
     tokens_dev, width = home.shape
     size = tokens_dev // slots
     return pl.pallas_call(
         functools.partial(combine_kernel, slots=slots, arrays=len(backs), ctx=ctx),
-        in_specs=[pl.BlockSpec(memory_space=pltpu.SMEM)]
-        + [pl.BlockSpec(memory_space=pltpu.VMEM)] * (1 + len(backs))
+        in_specs=[pl.BlockSpec(memory_space=pltpu.VMEM)] * (1 + len(backs))
         + moments(waits),
         out_specs=[pl.BlockSpec(memory_space=pltpu.VMEM)] * (slots + 1),
         out_shape=[jax.ShapeDtypeStruct((size, width), BF16)] * slots + [MARK],
         compiler_params=params(24),
         cost_estimate=cost(56 * tokens_dev * TILE * width, 8 * tokens_dev * width),
         name="combine",
-    )(seat, home, *backs, *waits)
-
-
-def project_kernel(side_ref, *refs, slots, chunk, adds):
+    )(home, *backs, *waits)
+
+
+def project_kernel(*refs, slots, chunk, adds):
+    side, seat = lax.axis_index("ctx") % 2, lax.axis_index("head")
     moved_refs, weight_refs, refs = refs[:slots], refs[slots : slots + 2], refs[slots + 2 :]
     o_ref = refs[-1]
     part = moved_refs[0].shape[1]
@@ -410,12 +409,12 @@
     tile = min(half, 512)
     for phase, weight_ref in enumerate(weight_refs):
         for j in range(half // tile):
-            first = pl.multiple_of((side_ref[0] ^ phase) * half + j * tile, tile)
+            first = pl.multiple_of((side ^ phase) * half + j * tile, tile)
             here = pl.ds(first, tile)
             total = refs[0][:, here] if adds else None
             for slot in range(slots):
                 rows = weight_ref[
-                    partner(side_ref[1], slot, slots),
+                    partner(seat, slot, slots),
                     chunk * part : (chunk + 1) * part,
                     j * tile : (j + 1) * tile,
                 ]
@@ -424,14 +423,14 @@
             o_ref[:, here] = total.astype(o_ref.dtype)
 
 
-def project(side, moved, mine, other, chunk, before, dtype):
+def project(moved, mine, other, chunk, before, dtype):
     slots = len(moved)
     tokens, part = moved[0].shape
     half = mine.shape[2]
     whole = pl.BlockSpec(memory_space=pltpu.VMEM)
     return pl.pallas_call(
         functools.partial(project_kernel, slots=slots, chunk=chunk, adds=len(before) > 0),
-        in_specs=[pl.BlockSpec(memory_space=pltpu.SMEM)] + [whole] * (slots + 2 + len(before)),
+        in_specs=[whole] * (slots + 2 + len(before)),
         out_specs=whole,
         out_shape=jax.ShapeDtypeStruct((tokens, 2 * half), dtype),
         compiler_params=params(24),
@@ -439,7 +438,7 @@
             4 * slots * tokens * part * half, 2 * slots * part * (2 * half + tokens)
         ),
         name="project",
-    )(side, *moved, mine, other, *before)
+    )(*moved, mine, other, *before)
 
 
 def gather_ctx(rows):
@@ -493,12 +492,10 @@
     groups = lax.axis_size("head")
     place = lax.axis_index("ctx")
     place_word = place.astype(jnp.int32).reshape(1)
-    side = place % 2
     sibling = [(i, i ^ 1) for i in range(ctx)]
 
     part = width // chunks
     seat = lax.axis_index("head").astype(jnp.int32)
-    sides = jnp.stack([side.astype(jnp.int32), seat])
 
     def exchange(slabs, axis):
         count = len(slabs)
@@ -542,8 +539,6 @@
             moved.append(exchange([attended[owner] for owner in owners], "head"))
             waits = (mark,)
     else:
-        seats = jnp.stack([seat, place.astype(jnp.int32)])
-        seats = jnp.stack([seat, place.astype(jnp.int32)])
         sections, mark = home(0, ())
         homes, backs, waits = [sections], [], ()
         if chunks > 1:
@@ -563,7 +558,7 @@
                 homes.append(sections)
                 waits = (mark,)
         for chunk in range(chunks):
-            *slabs, mark = combine(seats, homes[chunk], backs[chunk], groups, ctx, waits)
+            *slabs, mark = combine(homes[chunk], backs[chunk], groups, ctx, waits)
             moved.append(exchange(slabs, "head"))
             waits = (mark, *moved[-1][1:3])
     (held,) = after([mine], (mark,))
@@ -571,7 +566,7 @@
     total = ()
     for chunk in range(chunks):
         dtype = BF16 if chunk == chunks - 1 else F32
-        total = (project(sides, moved[chunk], held, other, chunk, total, dtype),)
+        total = (project(moved[chunk], held, other, chunk, total, dtype),)
     return total[0]
 
 

time: 135 us -> 130 us (0.963)
  Pallas kernels: 39.5 us -> 32.5 us
  waiting for transfers between devices: 37.7 us -> 40.1 us
    pallas_call x2, Pallas kernels: 7.87 us -> 3.47 us  [project(): pl.pallas_call(functools.partial(project_kernel, slots=slots, chunk=chunk...]
    ppermute x13, waiting for transfers between devices: 21.5 us -> 23.8 us  [exchange(): moved.append(lax.ppermute(slabs[slot], axis, pairs))]
    pallas_call x1, Pallas kernels: 3.69 us -> 2.27 us  [edges(): pl.pallas_call(edge_kernel, grid=(WINDOW // TILE,), in_specs=[source] * 2...]
  transfers between devices with their start and end apart: 26 -> 26, of which waited for: 10 -> 11; matrix products, arithmetic and copies ran while one was open for 0% -> 0% of each run, Pallas kernels for 25% -> 22%
where the time goes in v14:
time: 130 us; the launch traced here: 129 us
  waiting for transfers between devices  40.1 us (31%)
  starting transfers between devices  36 us (28%)
  Pallas kernels  32.5 us (25%)
  between operations  13.6 us (10%)
  local copies, waits for them, and re-layouts  6.95 us (5%)
    ppermute x13, waiting for transfers between devices, exchange(): moved.append(lax.ppermute(slabs[slot], axis, pairs))  23.8 us
    ppermute x13, starting transfers between devices, exchange(): moved.append(lax.ppermute(slabs[slot], axis, pairs))  15.7 us
    pallas_call x2, Pallas kernels, home_sections(): pl.pallas_call(functools.partial(home_kernel, order=order), grid=(heads,)...  14.2 us
    ppermute x1, waiting for transfers between devices, body(): before = lax.ppermute(rim, 'ctx', [(i, i + 1) for i in range(ctx - 1)])  10.9 us
    all_to_all x2, starting transfers between devices, body(): lax.all_to_all(send, 'ctx', split_axis=0, concat_axis=0, tiled=True)  8.32 us
    unnamed x30, local copies, waits for them, and re-layouts  6.95 us
    ppermute x7, starting transfers between devices, swapped(): return lax.ppermute(piece, 'ctx', [(i, i ^ distance) for i in range(count)])  5.72 us
    pallas_call x2, Pallas kernels, prepare(): pl.pallas_call(prep_kernel, grid=(tokens_dev // size,), in_specs=[pl.Bloc...  5.61 us
  transfers between devices with their start and end apart: 26, of which 11 were waited for; matrix products, arithmetic and copies ran while one was open for 0% of the time, Pallas kernels for 22%

profile of v14, /device:TPU:10, one launch (start us, length us, event | category | flops | bytes accessed | tf_op | source)
XLA Modules:
  0.0 129.1 jit_solution(4132226259061513465)
XLA Ops:
  6.5 2.0 %cut.1.refs_0_ = bf16[512,1024]{1,0:T(8,128)(2,1)} custom-call(bf16[512,2048]{1,0:T(8,128)(2,1)} %weight_ref.1), custom_call_target="tpu_custom_call" | custom-call | bytes 2097152 | tf_op jit(solution)/shard_map/cut/pallas_call | solution.py:182
  8.5 2.3 %edges.1 = (bf16[2,512,512]{2,1,0:T(8,128)(2,1)}, bf16[2,64,512]{2,1,0:T(8,128)(2,1)}) custom-call(bf16[1024,512]{1,0:T(8,128)(2,1)} %k_ref.9, bf16[1024,512]{1,0:T(8,128)(2,1)} %v_ref.9, bf16[8,128,512]{2,1,0:T(8,128)(2,1)} %bitcast.5, bf16[8,128,512]{2,1,0:T(8,128)(2,1)} %bitcast.6, bf16[512,1024]{1,0:T(8,128)(2,1)} %cut.1.refs_0_), custom_call_target="tpu_custom_call" | custom-call | bytes 2097152 | tf_op jit(solution)/shard_map/edges/pallas_call | solution.py:142
  10.8 1.5 %collective-permute-start.2 = (bf16[2,64,512]{2,1,0:T(8,128)(2,1)}, bf16[2,64,512]{2,1,0:T(8,128)(2,1)S(1)}, u32[]{:S(2)}, u32[]{:S(2)}) collective-permute-start(bf16[2,64,512]{2,1,0:T(8,128)(2,1)} %get-tuple-element.33.refs_0_), channel_id=1, source_target_pairs={{0,24},{4,28},{8,16},{12,20},{16,8},{20,12},{24,0},{28,4},{1,25},{... | collective-permute-start | bytes 393224 | tf_op jit(solution)/shard_map/ppermute | solution.py:448
  12.3 0.5 collective-permute-start.1
  12.8 1.5 %collective-permute-start = (bf16[2,64,512]{2,1,0:T(8,128)(2,1)}, bf16[2,64,512]{2,1,0:T(8,128)(2,1)S(1)}, u32[]{:S(2)}, u32[]{:S(2)}) collective-permute-start(bf16[2,64,512]{2,1,0:T(8,128)(2,1)} %get-tuple-element.33.refs_0_), channel_id=1, source_target_pairs={{0,8},{4,12},{8,0},{12,4},{16,24},{20,28},{24,16},{28,20},{1,9},{5... | collective-permute-start | bytes 393224 | tf_op jit(solution)/shard_map/ppermute | solution.py:448
  14.3 2.8 %prepare.2.refs_4_.refs_0_ = bf16[8,3,2,64,256]{4,3,2,1,0:T(8,128)(2,1)} custom-call(bf16[1024,512]{1,0:T(8,128)(2,1)} %q_ref.7, bf16[1024,512]{1,0:T(8,128)(2,1)} %k_ref.9, bf16[1024,512]{1,0:T(8,128)(2,1)} %v_ref.9, bf16[512,1024]{1,0:T(8,128)(2,1)} %cut.1.refs_0_), custom_call_target="tpu_custom_call" | custom-call | flops 402653184 | bytes 3145728 | tf_op jit(solution)/shard_map/prepare/pallas_call | solution.py:215
  17.1 1.2 collective-permute-done.2.refs_3_
  18.3 1.7 %collective-permute-done.1.refs_2_ = bf16[2,64,512]{2,1,0:T(8,128)(2,1)S(1)} collective-permute-done((bf16[2,64,512]{2,1,0:T(8,128)(2,1)}, bf16[2,64,512]{2,1,0:T(8,128)(2,1)S(1)}, u32[]{:S(2)}, u32[]{:S(2)}) %collective-permute-start.1) | collective-permute-done | bytes 131104 | tf_op jit(solution)/shard_map/ppermute | solution.py:448
  20.1 0.5 copy-done.7
  20.7 2.0 %collective-permute-start.3 = (bf16[2,512,512]{2,1,0:T(8,128)(2,1)}, bf16[2,512,512]{2,1,0:T(8,128)(2,1)S(1)}, u32[]{:S(2)}, u32[]{:S(2)}) collective-permute-start(bf16[2,512,512]{2,1,0:T(8,128)(2,1)} %after.4.refs_1_), channel_id=1, source_target_pairs={{0,4},{4,8},{8,12},{12,16},{16,20},{20,24},{24,28},{1,5},{5,9},{9,... | collective-permute-start | bytes 3145736 | tf_op jit(solution)/shard_map/ppermute | solution.py:521
  22.8 1.6 %collective-permute-start.7 = (bf16[2,64,512]{2,1,0:T(8,128)(2,1)}, bf16[2,64,512]{2,1,0:T(8,128)(2,1)S(1)}, u32[]{:S(2)}, u32[]{:S(2)}) collective-permute-start(bf16[2,64,512]{2,1,0:T(8,128)(2,1)} %copy-done.6), channel_id=1, source_target_pairs={{0,4},{4,0},{8,12},{12,8},{16,20},{20,16},{24,28},{28,24},{1,5},{5... | collective-permute-start | bytes 393224 | tf_op jit(solution)/shard_map/ppermute | solution.py:448
  24.5 0.4 collective-permute-start.6
  25.0 4.1 %all-to-all-start = ((bf16[8,3,2,64,256]{4,3,2,1,0:T(8,128)(2,1)}), bf16[8,3,2,64,256]{4,3,2,1,0:T(8,128)(2,1)S(1)}, u32[]{:S(2)}, u32[]{:S(2)}) async-start(bf16[8,3,2,64,256]{4,3,2,1,0:T(8,128)(2,1)} %after.5), calls=%async_computation | async-start | bytes 3145728 | tf_op jit(solution)/shard_map/all_to_all | solution.py:547
  29.1 0.7 copy-done.9
  29.7 2.8 %prepare.3.refs_0_ = bf16[8,3,2,64,256]{4,3,2,1,0:T(8,128)(2,1)} custom-call(bf16[1024,512]{1,0:T(8,128)(2,1)} %q_ref.7, bf16[1024,512]{1,0:T(8,128)(2,1)} %k_ref.9, bf16[1024,512]{1,0:T(8,128)(2,1)} %v_ref.9, bf16[2,64,512]{2,1,0:T(8,128)(2,1)} %copy-done.9), custom_call_target="tpu_custom_call" | custom-call | flops 402653184 | bytes 3145728 | tf_op jit(solution)/shard_map/prepare/pallas_call | solution.py:215
  32.6 10.9 %collective-permute-done.3.rim_ref = bf16[2,512,512]{2,1,0:T(8,128)(2,1)S(1)} collective-permute-done((bf16[2,512,512]{2,1,0:T(8,128)(2,1)}, bf16[2,512,512]{2,1,0:T(8,128)(2,1)S(1)}, u32[]{:S(2)}, u32[]{:S(2)}) %collective-permute-start.3) | collective-permute-done | bytes 1048608 | tf_op jit(solution)/shard_map/ppermute | solution.py:521
  43.4 0.9 copy-done.10
  44.4 7.1 %home.3 = (f32[1024,256]{1,0:T(8,128)}, f32[8,128]{1,0:T(8,128)}) custom-call(s32[1]{0:T(128)} %bitcast.place_ref, bf16[1024,512]{1,0:T(8,128)(2,1)} %q_ref.7, bf16[1024,512]{1,0:T(8,128)(2,1)} %k_ref.9, bf16[1024,512]{1,0:T(8,128)(2,1)} %v_ref.9, bf16[2,512,512]{2,1,0:T(8,128)(2,1)} %copy-done.10, bf16[2,64,512]{2,1,0:T(8,128)(2,1)} %get-tuple-element.33.refs_0_, ...), custom_call_target="tpu_custom_call" | custom-call | flops 21474836480 | bytes 7340032 | tf_op jit(solution)/shard_map/home/pallas_call | solution.py:282
  51.5 2.5 %all-to-all-done.x_ref = bf16[8,3,2,64,256]{4,3,2,1,0:T(8,128)(2,1)S(1)} async-done(((bf16[8,3,2,64,256]{4,3,2,1,0:T(8,128)(2,1)}), bf16[8,3,2,64,256]{4,3,2,1,0:T(8,128)(2,1)S(1)}, u32[]{:S(2)}, u32[]{:S(2)}) %all-to-all-start) | async-done | bytes 1572896 | tf_op jit(solution)/shard_map/all_to_all | solution.py:547
  54.0 4.3 %all-to-all-start.1 = ((bf16[8,3,2,64,256]{4,3,2,1,0:T(8,128)(2,1)}), bf16[8,3,2,64,256]{4,3,2,1,0:T(8,128)(2,1)S(1)}, u32[]{:S(2)}, u32[]{:S(2)}) async-start(bf16[8,3,2,64,256]{4,3,2,1,0:T(8,128)(2,1)} %after.6), calls=%async_computation.1 | async-start | bytes 3145728 | tf_op jit(solution)/shard_map/all_to_all | solution.py:547
  58.3 1.8 %stride.2 = (bf16[2,64,256]{2,1,0:T(8,128)(2,1)S(1)}, bf16[2,64,256]{2,1,0:T(8,128)(2,1)S(1)}, bf16[2,64,256]{2,1,0:T(8,128)(2,1)S(1)}, bf16[2,64,256]{2,1,0:T(8...) custom-call(s32[1]{0:T(128)} %bitcast.place_ref, ...), custom_call_target="tpu_custom_call" | custom-call | flops 805306368 | bytes 2097152 | tf_op jit(solution)/shard_map/stride/pallas_call | solution.py:345
  60.3 0.4 collective-permute-start.9
  60.7 1.3 %collective-permute-start.10 = (bf16[2,64,256]{2,1,0:T(8,128)(2,1)S(1)}, bf16[2,64,256]{2,1,0:T(8,128)(2,1)S(1)}, u32[]{:S(2)}, u32[]{:S(2)}) collective-permute-start(bf16[2,64,256]{2,1,0:T(8,128)(2,1)S(1)} %get-tuple-element.43), channel_id=1, source_target_pairs={{0,12},{4,8},{8,4},{12,0},{16,28},{20,24},{24,20},{28,16},{1,13},{... | collective-permute-start | bytes 196616 | tf_op jit(solution)/shard_map/ppermute | solution.py:505
  62.0 1.5 %collective-permute-start.11 = (bf16[2,64,256]{2,1,0:T(8,128)(2,1)S(1)}, bf16[2,64,256]{2,1,0:T(8,128)(2,1)S(1)}, u32[]{:S(2)}, u32[]{:S(2)}) collective-permute-start(bf16[2,64,256]{2,1,0:T(8,128)(2,1)S(1)} %get-tuple-element.44), channel_id=1, source_target_pairs={{0,16},{4,20},{8,24},{12,28},{16,0},{20,4},{24,8},{28,12},{1,17},{... | collective-permute-start | bytes 196616 | tf_op jit(solution)/shard_map/ppermute | solution.py:505
  63.5 0.3 collective-permute-start.12
  63.8 7.1 %home.2 = (f32[1024,256]{1,0:T(8,128)}, f32[8,128]{1,0:T(8,128)}) custom-call(s32[1]{0:T(128)} %bitcast.place_ref, bf16[1024,512]{1,0:T(8,128)(2,1)} %q_ref.7, bf16[1024,512]{1,0:T(8,128)(2,1)} %k_ref.9, bf16[1024,512]{1,0:T(8,128)(2,1)} %v_ref.9, bf16[2,512,512]{2,1,0:T(8,128)(2,1)} %copy-done.10, bf16[2,64,512]{2,1,0:T(8,128)(2,1)} %get-tuple-element.33.refs_0_, ...), custom_call_target="tpu_custom_call" | custom-call | flops 21474836480 | bytes 7340032 | tf_op jit(solution)/shard_map/home/pallas_call | solution.py:282
  70.9 1.7 %collective-permute-start.13 = (bf16[2,64,256]{2,1,0:T(8,128)(2,1)S(1)}, bf16[2,64,256]{2,1,0:T(8,128)(2,1)S(1)}, u32[]{:S(2)}, u32[]{:S(2)}) collective-permute-start(bf16[2,64,256]{2,1,0:T(8,128)(2,1)S(1)} %get-tuple-element.46), channel_id=1, source_target_pairs={{0,24},{4,28},{8,16},{12,20},{16,8},{20,12},{24,0},{28,4},{1,25},{... | collective-permute-start | bytes 196616 | tf_op jit(solution)/shard_map/ppermute | solution.py:505
  72.6 5.8 %collective-permute-done.9.refs_2_ = bf16[2,64,256]{2,1,0:T(8,128)(2,1)S(1)} collective-permute-done((bf16[2,64,256]{2,1,0:T(8,128)(2,1)S(1)}, bf16[2,64,256]{2,1,0:T(8,128)(2,1)S(1)}, u32[]{:S(2)}, u32[]{:S(2)}) %collective-permute-start.9) | collective-permute-done | bytes 65568 | tf_op jit(solution)/shard_map/ppermute | solution.py:505
  78.4 1.6 %collective-permute-start.14 = (bf16[2,64,256]{2,1,0:T(8,128)(2,1)S(1)}, bf16[2,64,256]{2,1,0:T(8,128)(2,1)S(1)}, u32[]{:S(2)}, u32[]{:S(2)}) collective-permute-start(bf16[2,64,256]{2,1,0:T(8,128)(2,1)S(1)} %get-tuple-element.47), channel_id=1, source_target_pairs={{0,28},{4,24},{8,20},{12,16},{16,12},{20,8},{24,4},{28,0},{1,29},{... | collective-permute-start | bytes 196616 | tf_op jit(solution)/shard_map/ppermute | solution.py:505
  80.0 0.7 copy-done.4
  80.7 2.5 %stride.3 = (bf16[8,2,64,256]{3,2,1,0:T(8,128)(2,1)}, f32[8,128]{1,0:T(8,128)S(1)}) custom-call(s32[1]{0:T(128)} %bitcast.place_ref, bf16[8,3,2,64,256]{4,3,2,1,0:T(8,128)(2,1)S(1)} %all-to-all-done.1.x_ref, f32[8,128]{1,0:T(8,128)S(1)} %copy-done.4), custom_call_target="tpu_custom_call" | custom-call | flops 805306368 | bytes 2097152 | tf_op jit(solution)/shard_map/stride/pallas_call | solution.py:345
  83.2 4.2 %all-to-all-start.2 = ((bf16[8,2,64,256]{3,2,1,0:T(8,128)(2,1)}), bf16[8,2,64,256]{3,2,1,0:T(8,128)(2,1)S(1)}, u32[]{:S(2)}, u32[]{:S(2)}) async-start(bf16[8,2,64,256]{3,2,1,0:T(8,128)(2,1)} %get-tuple-element.38), calls=%async_computation.2 | async-start | bytes 1048576 | tf_op jit(solution)/shard_map/all_to_all | solution.py:553
  87.5 1.2 copy-done.3
  89.1 0.5 collective-permute-start.15
  89.6 2.6 %collective-permute-start.16 = (bf16[256,256]{1,0:T(8,128)(2,1)S(1)}, bf16[256,256]{1,0:T(8,128)(2,1)S(1)}, u32[]{:S(2)}, u32[]{:S(2)}) collective-permute-start(bf16[256,256]{1,0:T(8,128)(2,1)S(1)} %get-tuple-element.51), channel_id=1, source_target_pairs={{0,2},{1,3},{2,0},{3,1},{4,6},{5,7},{6,4},{7,5},{8,10},{9,11},{10,... | collective-permute-start | bytes 393224 | tf_op jit(solution)/shard_map/ppermute | solution.py:505
  92.2 3.8 %collective-permute-done.15.refs_2_.refs_1_ = bf16[256,256]{1,0:T(8,128)(2,1)S(1)} collective-permute-done((bf16[256,256]{1,0:T(8,128)(2,1)S(1)}, bf16[256,256]{1,0:T(8,128)(2,1)S(1)}, u32[]{:S(2)}, u32[]{:S(2)}) %collective-permute-start.15) | collective-permute-done | bytes 131104 | tf_op jit(solution)/shard_map/ppermute | solution.py:505
  96.0 3.2 %collective-permute-done.16.refs_3_.refs_2_ = bf16[256,256]{1,0:T(8,128)(2,1)S(1)} collective-permute-done((bf16[256,256]{1,0:T(8,128)(2,1)S(1)}, bf16[256,256]{1,0:T(8,128)(2,1)S(1)}, u32[]{:S(2)}, u32[]{:S(2)}) %collective-permute-start.16) | collective-permute-done | bytes 131104 | tf_op jit(solution)/shard_map/ppermute | solution.py:505
  99.2 0.3 combine.3
  99.5 0.6 copy-done.1
  100.1 0.4 collective-permute-start.21
  100.6 3.6 %collective-permute-start.17 = (bf16[256,256]{1,0:T(8,128)(2,1)S(1)}, bf16[256,256]{1,0:T(8,128)(2,1)S(1)}, u32[]{:S(2)}, u32[]{:S(2)}) collective-permute-start(bf16[256,256]{1,0:T(8,128)(2,1)S(1)} %get-tuple-element.53), channel_id=1, source_target_pairs={{0,1},{1,0},{2,3},{3,2},{4,5},{5,4},{6,7},{7,6},{8,9},{9,8},{10,11... | collective-permute-start | bytes 393224 | tf_op jit(solution)/shard_map/ppermute | solution.py:505
  104.2 1.5 %collective-permute-start.19 = (bf16[256,256]{1,0:T(8,128)(2,1)S(1)}, bf16[256,256]{1,0:T(8,128)(2,1)S(1)}, u32[]{:S(2)}, u32[]{:S(2)}) collective-permute-start(bf16[256,256]{1,0:T(8,128)(2,1)S(1)} %get-tuple-element.55), channel_id=1, source_target_pairs={{0,3},{1,2},{2,1},{3,0},{4,7},{5,6},{6,5},{7,4},{8,11},{9,10},{10,... | collective-permute-start | bytes 393224 | tf_op jit(solution)/shard_map/ppermute | solution.py:505
  105.6 3.6 %collective-permute-done.21.refs_3_ = bf16[256,256]{1,0:T(8,128)(2,1)S(1)} collective-permute-done((bf16[256,256]{1,0:T(8,128)(2,1)S(1)}, bf16[256,256]{1,0:T(8,128)(2,1)S(1)}, u32[]{:S(2)}, u32[]{:S(2)}) %collective-permute-start.21) | collective-permute-done | bytes 131104 | tf_op jit(solution)/shard_map/ppermute | solution.py:505
  109.2 2.2 %copy-done = bf16[4,512,1024]{2,1,0:T(8,128)(2,1)S(1)} copy-done((bf16[4,512,1024]{2,1,0:T(8,128)(2,1)S(1)}, bf16[4,512,1024]{2,1,0:T(8,128)(2,1)}, u32[]{:S(2)}) %copy-start) | copy-done | bytes 4194328
  111.4 1.2 project.2.refs_6_
  112.7 1.4 %collective-permute-done.18.refs_2_ = bf16[256,256]{1,0:T(8,128)(2,1)S(1)} collective-permute-done((bf16[256,256]{1,0:T(8,128)(2,1)S(1)}, bf16[256,256]{1,0:T(8,128)(2,1)S(1)}, u32[]{:S(2)}, u32[]{:S(2)}) %collective-permute-start.18) | collective-permute-done | bytes 131104 | tf_op jit(solution)/shard_map/ppermute | solution.py:505
  114.1 6.0 %collective-permute-done.19.refs_3_ = bf16[256,256]{1,0:T(8,128)(2,1)S(1)} collective-permute-done((bf16[256,256]{1,0:T(8,128)(2,1)S(1)}, bf16[256,256]{1,0:T(8,128)(2,1)S(1)}, u32[]{:S(2)}, u32[]{:S(2)}) %collective-permute-start.19) | collective-permute-done | bytes 131104 | tf_op jit(solution)/shard_map/ppermute | solution.py:505
  120.1 2.2 %project.3 = bf16[256,2048]{1,0:T(8,128)(2,1)} custom-call(bf16[256,256]{1,0:T(8,128)(2,1)S(1)} %get-tuple-element.52.refs_0_, bf16[256,256]{1,0:T(8,128)(2,1)S(1)} %collective-permute-done.17.refs_1_, bf16[256,256]{1,0:T(8,128)(2,1)S(1)} %collective-permute-done.18.refs_2_, bf16[256,256]{1,0:T(8,128)(2,1)S(1)} %collective-permute-done.19.refs_3_, ...), custom_call_target="tpu_custom_call" | custom-call | flops 1073741824 | bytes 4718592 | tf_op jit(solution)/shard_map/project/pallas_call | solution.py:431
  (51 shorter events, 1.0 us)
Async XLA Ops:
  6.5 93.6 %all-gather.3.cloned.1.call-start = ((), (), s32[]{:S(2)}) async-start(), calls=%async_computation.3 | async-start | bytes 5242880 | tf_op jit(solution)/shard_map/all_gather | solution.py:509
  10.8 7.5 %collective-permute-start.2 = (bf16[2,64,512]{2,1,0:T(8,128)(2,1)}, bf16[2,64,512]{2,1,0:T(8,128)(2,1)S(1)}, u32[]{:S(2)}, u32[]{:S(2)}) collective-permute-start(bf16[2,64,512]{2,1,0:T(8,128)(2,1)} %get-tuple-element.33.refs_0_), channel_id=1, source_target_pairs={{0,24},{4,28},{8,16},{12,20},{16,8},{20,12},{24,0},{28,4},{1,25},{... | collective-permute-start | bytes 393224 | tf_op jit(solution)/shard_map/ppermute | solution.py:448
  12.3 7.7 %collective-permute-start.1 = (bf16[2,64,512]{2,1,0:T(8,128)(2,1)}, bf16[2,64,512]{2,1,0:T(8,128)(2,1)S(1)}, u32[]{:S(2)}, u32[]{:S(2)}) collective-permute-start(bf16[2,64,512]{2,1,0:T(8,128)(2,1)} %get-tuple-element.33.refs_0_), channel_id=1, source_target_pairs={{0,16},{4,20},{8,24},{12,28},{16,0},{20,4},{24,8},{28,12},{1,17},{... | collective-permute-start | bytes 393224 | tf_op jit(solution)/shard_map/ppermute | solution.py:448
  12.8 7.3 %collective-permute-start = (bf16[2,64,512]{2,1,0:T(8,128)(2,1)}, bf16[2,64,512]{2,1,0:T(8,128)(2,1)S(1)}, u32[]{:S(2)}, u32[]{:S(2)}) collective-permute-start(bf16[2,64,512]{2,1,0:T(8,128)(2,1)} %get-tuple-element.33.refs_0_), channel_id=1, source_target_pairs={{0,8},{4,12},{8,0},{12,4},{16,24},{20,28},{24,16},{28,20},{1,9},{5... | collective-permute-start | bytes 393224 | tf_op jit(solution)/shard_map/ppermute | solution.py:448
  18.3 1.8 %copy-start.6 = (bf16[2,64,512]{2,1,0:T(8,128)(2,1)}, bf16[2,64,512]{2,1,0:T(8,128)(2,1)S(1)}, u32[]{:S(2)}) copy-start(bf16[2,64,512]{2,1,0:T(8,128)(2,1)S(1)} %collective-permute-done.2.refs_3_) | copy-start | bytes 393220
  20.0 0.6 copy-start.7
  20.1 0.7 copy-start.8
  20.7 3.7 %copy-start.11 = (bf16[2,64,512]{2,1,0:T(8,128)(2,1)S(1)}, bf16[2,64,512]{2,1,0:T(8,128)(2,1)}, u32[]{:S(2)}) copy-start(bf16[2,64,512]{2,1,0:T(8,128)(2,1)} %get-tuple-element.33.refs_0_) | copy-start | bytes 393220
  20.7 22.7 %collective-permute-start.3 = (bf16[2,512,512]{2,1,0:T(8,128)(2,1)}, bf16[2,512,512]{2,1,0:T(8,128)(2,1)S(1)}, u32[]{:S(2)}, u32[]{:S(2)}) collective-permute-start(bf16[2,512,512]{2,1,0:T(8,128)(2,1)} %after.4.refs_1_), channel_id=1, source_target_pairs={{0,4},{4,8},{8,12},{12,16},{16,20},{20,24},{24,28},{1,5},{5,9},{9,... | collective-permute-start | bytes 3145736 | tf_op jit(solution)/shard_map/ppermute | solution.py:521
  22.8 6.3 %collective-permute-start.7 = (bf16[2,64,512]{2,1,0:T(8,128)(2,1)}, bf16[2,64,512]{2,1,0:T(8,128)(2,1)S(1)}, u32[]{:S(2)}, u32[]{:S(2)}) collective-permute-start(bf16[2,64,512]{2,1,0:T(8,128)(2,1)} %copy-done.6), channel_id=1, source_target_pairs={{0,4},{4,0},{8,12},{12,8},{16,20},{20,16},{24,28},{28,24},{1,5},{5... | collective-permute-start | bytes 393224 | tf_op jit(solution)/shard_map/ppermute | solution.py:448
  24.4 8.1 %collective-permute-start.4 = (bf16[2,64,512]{2,1,0:T(8,128)(2,1)S(1)}, bf16[2,64,512]{2,1,0:T(8,128)(2,1)S(1)}, u32[]{:S(2)}, u32[]{:S(2)}) collective-permute-start(bf16[2,64,512]{2,1,0:T(8,128)(2,1)S(1)} %copy-done.11), channel_id=1, source_target_pairs={{0,4},{4,0},{8,12},{12,8},{16,20},{20,16},{24,28},{28,24},{1,5},{5... | collective-permute-start | bytes 393224 | tf_op jit(solution)/shard_map/ppermute | solution.py:448
  24.5 8.0 %collective-permute-start.6 = (bf16[2,64,512]{2,1,0:T(8,128)(2,1)}, bf16[2,64,512]{2,1,0:T(8,128)(2,1)S(1)}, u32[]{:S(2)}, u32[]{:S(2)}) collective-permute-start(bf16[2,64,512]{2,1,0:T(8,128)(2,1)} %copy-done.7), channel_id=1, source_target_pairs={{0,4},{4,0},{8,12},{12,8},{16,20},{20,16},{24,28},{28,24},{1,5},{5... | collective-permute-start | bytes 393224 | tf_op jit(solution)/shard_map/ppermute | solution.py:448
  24.9 7.6 %collective-permute-start.5 = (bf16[2,64,512]{2,1,0:T(8,128)(2,1)}, bf16[2,64,512]{2,1,0:T(8,128)(2,1)S(1)}, u32[]{:S(2)}, u32[]{:S(2)}) collective-permute-start(bf16[2,64,512]{2,1,0:T(8,128)(2,1)} %copy-done.8), channel_id=1, source_target_pairs={{0,4},{4,0},{8,12},{12,8},{16,20},{20,16},{24,28},{28,24},{1,5},{5... | collective-permute-start | bytes 393224 | tf_op jit(solution)/shard_map/ppermute | solution.py:448
  25.0 29.0 %all-to-all-start = ((bf16[8,3,2,64,256]{4,3,2,1,0:T(8,128)(2,1)}), bf16[8,3,2,64,256]{4,3,2,1,0:T(8,128)(2,1)S(1)}, u32[]{:S(2)}, u32[]{:S(2)}) async-start(bf16[8,3,2,64,256]{4,3,2,1,0:T(8,128)(2,1)} %after.5), calls=%async_computation | async-start | bytes 3145728 | tf_op jit(solution)/shard_map/all_to_all | solution.py:547
  29.1 0.7 copy-start.9
  32.5 10.9 %copy-start.12 = (bf16[2,64,512]{2,1,0:T(8,128)(2,1)}, bf16[2,64,512]{2,1,0:T(8,128)(2,1)S(1)}, u32[]{:S(2)}) copy-start(bf16[2,64,512]{2,1,0:T(8,128)(2,1)S(1)} %collective-permute-done.4.refs_4_) | copy-start | bytes 393220
  32.5 10.9 %copy-start.13 = (bf16[2,64,512]{2,1,0:T(8,128)(2,1)}, bf16[2,64,512]{2,1,0:T(8,128)(2,1)S(1)}, u32[]{:S(2)}) copy-start(bf16[2,64,512]{2,1,0:T(8,128)(2,1)S(1)} %collective-permute-done.6.refs_6_) | copy-start | bytes 393220
  32.6 10.9 %copy-start.14 = (bf16[2,64,512]{2,1,0:T(8,128)(2,1)}, bf16[2,64,512]{2,1,0:T(8,128)(2,1)S(1)}, u32[]{:S(2)}) copy-start(bf16[2,64,512]{2,1,0:T(8,128)(2,1)S(1)} %collective-permute-done.5.refs_5_) | copy-start | bytes 393220
  43.4 1.0 copy-start.10
  54.0 26.0 %all-to-all-start.1 = ((bf16[8,3,2,64,256]{4,3,2,1,0:T(8,128)(2,1)}), bf16[8,3,2,64,256]{4,3,2,1,0:T(8,128)(2,1)S(1)}, u32[]{:S(2)}, u32[]{:S(2)}) async-start(bf16[8,3,2,64,256]{4,3,2,1,0:T(8,128)(2,1)} %after.6), calls=%async_computation.1 | async-start | bytes 3145728 | tf_op jit(solution)/shard_map/all_to_all | solution.py:547
  60.1 3.7 %copy-start.5 = (f32[8,128]{1,0:T(8,128)}, f32[8,128]{1,0:T(8,128)S(1)}, u32[]{:S(2)}) copy-start(f32[8,128]{1,0:T(8,128)S(1)} %get-tuple-element.34.refs_8_) | copy-start | bytes 12292
  60.1 10.8 %collective-permute-start.8 = (bf16[2,64,256]{2,1,0:T(8,128)(2,1)S(1)}, bf16[2,64,256]{2,1,0:T(8,128)(2,1)S(1)}, u32[]{:S(2)}, u32[]{:S(2)}) collective-permute-start(bf16[2,64,256]{2,1,0:T(8,128)(2,1)S(1)} %get-tuple-element.41), channel_id=1, source_target_pairs={{0,4},{4,0},{8,12},{12,8},{16,20},{20,16},{24,28},{28,24},{1,5},{5... | collective-permute-start | bytes 196616 | tf_op jit(solution)/shard_map/ppermute | solution.py:505
  60.3 18.1 %collective-permute-start.9 = (bf16[2,64,256]{2,1,0:T(8,128)(2,1)S(1)}, bf16[2,64,256]{2,1,0:T(8,128)(2,1)S(1)}, u32[]{:S(2)}, u32[]{:S(2)}) collective-permute-start(bf16[2,64,256]{2,1,0:T(8,128)(2,1)S(1)} %get-tuple-element.42), channel_id=1, source_target_pairs={{0,8},{4,12},{8,0},{12,4},{16,24},{20,28},{24,16},{28,20},{1,9},{5... | collective-permute-start | bytes 196616 | tf_op jit(solution)/shard_map/ppermute | solution.py:505
  60.7 26.8 %collective-permute-start.10 = (bf16[2,64,256]{2,1,0:T(8,128)(2,1)S(1)}, bf16[2,64,256]{2,1,0:T(8,128)(2,1)S(1)}, u32[]{:S(2)}, u32[]{:S(2)}) collective-permute-start(bf16[2,64,256]{2,1,0:T(8,128)(2,1)S(1)} %get-tuple-element.43), channel_id=1, source_target_pairs={{0,12},{4,8},{8,4},{12,0},{16,28},{20,24},{24,20},{28,16},{1,13},{... | collective-permute-start | bytes 196616 | tf_op jit(solution)/shard_map/ppermute | solution.py:505
  62.0 25.5 %collective-permute-start.11 = (bf16[2,64,256]{2,1,0:T(8,128)(2,1)S(1)}, bf16[2,64,256]{2,1,0:T(8,128)(2,1)S(1)}, u32[]{:S(2)}, u32[]{:S(2)}) collective-permute-start(bf16[2,64,256]{2,1,0:T(8,128)(2,1)S(1)} %get-tuple-element.44), channel_id=1, source_target_pairs={{0,16},{4,20},{8,24},{12,28},{16,0},{20,4},{24,8},{28,12},{1,17},{... | collective-permute-start | bytes 196616 | tf_op jit(solution)/shard_map/ppermute | solution.py:505
  63.5 24.0 %collective-permute-start.12 = (bf16[2,64,256]{2,1,0:T(8,128)(2,1)S(1)}, bf16[2,64,256]{2,1,0:T(8,128)(2,1)S(1)}, u32[]{:S(2)}, u32[]{:S(2)}) collective-permute-start(bf16[2,64,256]{2,1,0:T(8,128)(2,1)S(1)} %get-tuple-element.45), channel_id=1, source_target_pairs={{0,20},{4,16},{8,28},{12,24},{16,4},{20,0},{24,12},{28,8},{1,21},{... | collective-permute-start | bytes 196616 | tf_op jit(solution)/shard_map/ppermute | solution.py:505
  70.9 16.6 %collective-permute-start.13 = (bf16[2,64,256]{2,1,0:T(8,128)(2,1)S(1)}, bf16[2,64,256]{2,1,0:T(8,128)(2,1)S(1)}, u32[]{:S(2)}, u32[]{:S(2)}) collective-permute-start(bf16[2,64,256]{2,1,0:T(8,128)(2,1)S(1)} %get-tuple-element.46), channel_id=1, source_target_pairs={{0,24},{4,28},{8,16},{12,20},{16,8},{20,12},{24,0},{28,4},{1,25},{... | collective-permute-start | bytes 196616 | tf_op jit(solution)/shard_map/ppermute | solution.py:505
  78.4 9.1 %collective-permute-start.14 = (bf16[2,64,256]{2,1,0:T(8,128)(2,1)S(1)}, bf16[2,64,256]{2,1,0:T(8,128)(2,1)S(1)}, u32[]{:S(2)}, u32[]{:S(2)}) collective-permute-start(bf16[2,64,256]{2,1,0:T(8,128)(2,1)S(1)} %get-tuple-element.47), channel_id=1, source_target_pairs={{0,28},{4,24},{8,20},{12,16},{16,12},{20,8},{24,4},{28,0},{1,29},{... | collective-permute-start | bytes 196616 | tf_op jit(solution)/shard_map/ppermute | solution.py:505
  80.0 0.7 copy-start.4
  83.2 16.0 %all-to-all-start.2 = ((bf16[8,2,64,256]{3,2,1,0:T(8,128)(2,1)}), bf16[8,2,64,256]{3,2,1,0:T(8,128)(2,1)S(1)}, u32[]{:S(2)}, u32[]{:S(2)}) async-start(bf16[8,2,64,256]{3,2,1,0:T(8,128)(2,1)} %get-tuple-element.38), calls=%async_computation.2 | async-start | bytes 1048576 | tf_op jit(solution)/shard_map/all_to_all | solution.py:553
  87.5 1.2 copy-start.3
  88.7 10.5 %copy-start.2 = (f32[1024,256]{1,0:T(8,128)S(1)}, f32[1024,256]{1,0:T(8,128)}, u32[]{:S(2)}) copy-start(f32[1024,256]{1,0:T(8,128)} %get-tuple-element.35.home_ref) | copy-start | bytes 3145732
  89.1 6.9 %collective-permute-start.15 = (bf16[256,256]{1,0:T(8,128)(2,1)S(1)}, bf16[256,256]{1,0:T(8,128)(2,1)S(1)}, u32[]{:S(2)}, u32[]{:S(2)}) collective-permute-start(bf16[256,256]{1,0:T(8,128)(2,1)S(1)} %get-tuple-element.50), channel_id=1, source_target_pairs={{0,1},{1,0},{2,3},{3,2},{4,5},{5,4},{6,7},{7,6},{8,9},{9,8},{10,11... | collective-permute-start | bytes 393224 | tf_op jit(solution)/shard_map/ppermute | solution.py:505
  89.6 9.6 %collective-permute-start.16 = (bf16[256,256]{1,0:T(8,128)(2,1)S(1)}, bf16[256,256]{1,0:T(8,128)(2,1)S(1)}, u32[]{:S(2)}, u32[]{:S(2)}) collective-permute-start(bf16[256,256]{1,0:T(8,128)(2,1)S(1)} %get-tuple-element.51), channel_id=1, source_target_pairs={{0,2},{1,3},{2,0},{3,1},{4,6},{5,7},{6,4},{7,5},{8,10},{9,11},{10,... | collective-permute-start | bytes 393224 | tf_op jit(solution)/shard_map/ppermute | solution.py:505
  99.5 0.6 copy-start.1
  100.1 9.1 %collective-permute-start.20 = (bf16[4,512,1024]{2,1,0:T(8,128)(2,1)}, bf16[4,512,1024]{2,1,0:T(8,128)(2,1)S(1)}, u32[]{:S(2)}, u32[]{:S(2)}) collective-permute-start(bf16[4,512,1024]{2,1,0:T(8,128)(2,1)} %after.7.refs_4_), channel_id=1, source_target_pairs={{0,4},{4,0},{8,12},{12,8},{16,20},{20,16},{24,28},{28,24},{1,5},{5... | collective-permute-start | bytes 12582920 | tf_op jit(solution)/shard_map/ppermute | solution.py:565
  100.1 9.1 %collective-permute-start.21 = (bf16[256,256]{1,0:T(8,128)(2,1)S(1)}, bf16[256,256]{1,0:T(8,128)(2,1)S(1)}, u32[]{:S(2)}, u32[]{:S(2)}) collective-permute-start(bf16[256,256]{1,0:T(8,128)(2,1)S(1)} %get-tuple-element.58), channel_id=1, source_target_pairs={{0,3},{1,2},{2,1},{3,0},{4,7},{5,6},{6,5},{7,4},{8,11},{9,10},{10,... | collective-permute-start | bytes 393224 | tf_op jit(solution)/shard_map/ppermute | solution.py:505
  100.6 12.1 %collective-permute-start.17 = (bf16[256,256]{1,0:T(8,128)(2,1)S(1)}, bf16[256,256]{1,0:T(8,128)(2,1)S(1)}, u32[]{:S(2)}, u32[]{:S(2)}) collective-permute-start(bf16[256,256]{1,0:T(8,128)(2,1)S(1)} %get-tuple-element.53), channel_id=1, source_target_pairs={{0,1},{1,0},{2,3},{3,2},{4,5},{5,4},{6,7},{7,6},{8,9},{9,8},{10,11... | collective-permute-start | bytes 393224 | tf_op jit(solution)/shard_map/ppermute | solution.py:505
  104.2 9.9 %collective-permute-start.18 = (bf16[256,256]{1,0:T(8,128)(2,1)S(1)}, bf16[256,256]{1,0:T(8,128)(2,1)S(1)}, u32[]{:S(2)}, u32[]{:S(2)}) collective-permute-start(bf16[256,256]{1,0:T(8,128)(2,1)S(1)} %get-tuple-element.54), channel_id=1, source_target_pairs={{0,2},{1,3},{2,0},{3,1},{4,6},{5,7},{6,4},{7,5},{8,10},{9,11},{10,... | collective-permute-start | bytes 393224 | tf_op jit(solution)/shard_map/ppermute | solution.py:505
  104.2 15.9 %collective-permute-start.19 = (bf16[256,256]{1,0:T(8,128)(2,1)S(1)}, bf16[256,256]{1,0:T(8,128)(2,1)S(1)}, u32[]{:S(2)}, u32[]{:S(2)}) collective-permute-start(bf16[256,256]{1,0:T(8,128)(2,1)S(1)} %get-tuple-element.55), channel_id=1, source_target_pairs={{0,3},{1,2},{2,1},{3,0},{4,7},{5,6},{6,5},{7,4},{8,11},{9,10},{10,... | collective-permute-start | bytes 393224 | tf_op jit(solution)/shard_map/ppermute | solution.py:505
  109.2 2.2 %copy-start = (bf16[4,512,1024]{2,1,0:T(8,128)(2,1)S(1)}, bf16[4,512,1024]{2,1,0:T(8,128)(2,1)}, u32[]{:S(2)}) copy-start(bf16[4,512,1024]{2,1,0:T(8,128)(2,1)} %after.7.refs_4_) | copy-start | bytes 12582916
Sparse Core Ops, SparseCore 0:
  8.9 79.4 all-gather.2

commit v15 on v14

--- a/solution.py
+++ b/solution.py
@@ -30,11 +30,23 @@
 
 
 def mark_spec():
-    return pl.BlockSpec(MARK.shape, lambda *place: (0, 0))
+    return pl.BlockSpec(memory_space=pltpu.HBM)
 
 
 def moments(arrays):
     return [pl.BlockSpec(memory_space=pl.ANY)] * len(arrays)
+
+
+def gate(arrays):
+    return pl.pallas_call(
+        lambda *refs: None,
+        in_specs=moments(arrays),
+        out_specs=mark_spec(),
+        out_shape=MARK,
+        compiler_params=params(24),
+        cost_estimate=cost(0, 0),
+        name="gate",
+    )(*arrays)
 
 
 def after(arrays, others):
@@ -45,7 +57,7 @@
         out_specs=[anywhere] * len(arrays),
         out_shape=[jax.ShapeDtypeStruct(array.shape, array.dtype) for array in arrays],
         input_output_aliases={i: i for i in range(len(arrays))},
-        compiler_params=params(60),
+        compiler_params=params(52),
         cost_estimate=cost(0, 0),
         name="after",
     )(*arrays, *others)
@@ -226,7 +238,6 @@
 
 def home_kernel(place_ref, q_ref, k_ref, v_ref, rim_ref, *refs, order):
     sum_refs, (o_ref, mark_ref) = refs[: len(order)], refs[-2:]
-    mark_ref[...] = jnp.zeros_like(mark_ref)
     place = place_ref[0]
     tokens_dev = q_ref.shape[0]
     back = WINDOW // TILE
@@ -302,7 +313,6 @@
 def stride_kernel(place_ref, x_ref, *refs, slabs):
     ctx, _, _, rows, width = x_ref.shape
     o_refs, mark_ref, held_ref = refs[-2 - (ctx if slabs else 1) : -2], refs[-2], refs[-1]
-    mark_ref[...] = jnp.zeros_like(mark_ref)
     count = ctx * rows
     row = iota2((TILE, TILE), 0)
     col = iota2((TILE, TILE), 1)
@@ -362,7 +372,6 @@
 def combine_kernel(home_ref, *refs, slots, arrays, ctx):
     seat, place = lax.axis_index("head"), lax.axis_index("ctx")
     back_refs, o_refs, mark_ref = refs[:arrays], refs[-slots - 1 : -1], refs[-1]
-    mark_ref[...] = jnp.zeros_like(mark_ref)
     tokens_dev, width = home_ref.shape
     size = tokens_dev // slots
     per = STRIDE // ctx
@@ -392,7 +401,7 @@
         functools.partial(combine_kernel, slots=slots, arrays=len(backs), ctx=ctx),
         in_specs=[pl.BlockSpec(memory_space=pltpu.VMEM)] * (1 + len(backs))
         + moments(waits),
-        out_specs=[pl.BlockSpec(memory_space=pltpu.VMEM)] * (slots + 1),
+        out_specs=[pl.BlockSpec(memory_space=pltpu.VMEM)] * slots + [mark_spec()],
         out_shape=[jax.ShapeDtypeStruct((size, width), BF16)] * slots + [MARK],
         compiler_params=params(24),
         cost_estimate=cost(56 * tokens_dev * TILE * width, 8 * tokens_dev * width),
@@ -560,8 +569,8 @@
         for chunk in range(chunks):
             *slabs, mark = combine(homes[chunk], backs[chunk], groups, ctx, waits)
             moved.append(exchange(slabs, "head"))
-            waits = (mark, *moved[-1][1:3])
-    (held,) = after([mine], (mark,))
+            waits = (mark, *moved[-1][1:2])
+    (held,) = after([mine], (gate((mark, *moved[0][2:])),))
     other = lax.ppermute(held, "ctx", sibling)
     total = ()
     for chunk in range(chunks):

time: 130 us -> 130 us (level)
  waiting for transfers between devices: 40.1 us -> 42.7 us
  local copies, waits for them, and re-layouts: 6.95 us -> 5.43 us
  starting transfers between devices: 36 us -> 34.5 us
    ppermute x1, waiting for transfers between devices: 0.01 us -> 3.82 us  [body(): other = lax.ppermute(held, 'ctx', sibling)]
    ppermute x13, starting transfers between devices: 15.7 us -> 14.2 us  [exchange(): moved.append(lax.ppermute(slabs[slot], axis, pairs))]
    unnamed x30 -> x28, local copies, waits for them, and re-layouts: 6.95 us -> 5.43 us
  transfers between devices with their start and end apart: 26 -> 26, of which waited for: 11 -> 12; matrix products, arithmetic and copies ran while one was open for 0% -> 0% of each run, Pallas kernels for 22% -> 22%
where the time goes in v15:
time: 130 us; the launch traced here: 129 us
  waiting for transfers between devices  42.7 us (33%)
  starting transfers between devices  34.5 us (27%)
  Pallas kernels  32.4 us (25%)
  between operations  13.6 us (10%)
  local copies, waits for them, and re-layouts  5.43 us (4%)
    ppermute x13, waiting for transfers between devices, exchange(): moved.append(lax.ppermute(slabs[slot], axis, pairs))  22.5 us
    pallas_call x2, Pallas kernels, home_sections(): pl.pallas_call(functools.partial(home_kernel, order=order), grid=(heads,)...  14.2 us
    ppermute x13, starting transfers between devices, exchange(): moved.append(lax.ppermute(slabs[slot], axis, pairs))  14.2 us
    ppermute x1, waiting for transfers between devices, body(): before = lax.ppermute(rim, 'ctx', [(i, i + 1) for i in range(ctx - 1)])  10.5 us
    all_to_all x2, starting transfers between devices, body(): lax.all_to_all(send, 'ctx', split_axis=0, concat_axis=0, tiled=True)  8.32 us
    ppermute x7, starting transfers between devices, swapped(): return lax.ppermute(piece, 'ctx', [(i, i ^ distance) for i in range(count)])  5.73 us
    pallas_call x2, Pallas kernels, prepare(): pl.pallas_call(prep_kernel, grid=(tokens_dev // size,), in_specs=[pl.Bloc...  5.63 us
    unnamed x28, local copies, waits for them, and re-layouts  5.43 us
  transfers between devices with their start and end apart: 26, of which 12 were waited for; matrix products, arithmetic and copies ran while one was open for 0% of the time, Pallas kernels for 22%

profile of v15, /device:TPU:10, one launch (start us, length us, event | category | flops | bytes accessed | tf_op | source)
XLA Modules:
  0.0 128.7 jit_solution(7279360108565459354)
XLA Ops:
  6.5 2.0 %cut.1.refs_0_ = bf16[512,1024]{1,0:T(8,128)(2,1)} custom-call(bf16[512,2048]{1,0:T(8,128)(2,1)} %weight_ref.1), custom_call_target="tpu_custom_call" | custom-call | bytes 2097152 | tf_op jit(solution)/shard_map/cut/pallas_call | solution.py:194
  8.5 2.2 %edges.1 = (bf16[2,512,512]{2,1,0:T(8,128)(2,1)}, bf16[2,64,512]{2,1,0:T(8,128)(2,1)}) custom-call(bf16[1024,512]{1,0:T(8,128)(2,1)} %k_ref.9, bf16[1024,512]{1,0:T(8,128)(2,1)} %v_ref.9, bf16[8,128,512]{2,1,0:T(8,128)(2,1)} %bitcast.5, bf16[8,128,512]{2,1,0:T(8,128)(2,1)} %bitcast.6, bf16[512,1024]{1,0:T(8,128)(2,1)} %cut.1.refs_0_), custom_call_target="tpu_custom_call" | custom-call | bytes 2097152 | tf_op jit(solution)/shard_map/edges/pallas_call | solution.py:154
  10.8 1.6 %collective-permute-start.2 = (bf16[2,64,512]{2,1,0:T(8,128)(2,1)}, bf16[2,64,512]{2,1,0:T(8,128)(2,1)S(1)}, u32[]{:S(2)}, u32[]{:S(2)}) collective-permute-start(bf16[2,64,512]{2,1,0:T(8,128)(2,1)} %get-tuple-element.33.refs_0_), channel_id=1, source_target_pairs={{0,24},{4,28},{8,16},{12,20},{16,8},{20,12},{24,0},{28,4},{1,25},{... | collective-permute-start | bytes 393224 | tf_op jit(solution)/shard_map/ppermute | solution.py:457
  12.3 0.5 collective-permute-start.1
  12.8 1.5 %collective-permute-start = (bf16[2,64,512]{2,1,0:T(8,128)(2,1)}, bf16[2,64,512]{2,1,0:T(8,128)(2,1)S(1)}, u32[]{:S(2)}, u32[]{:S(2)}) collective-permute-start(bf16[2,64,512]{2,1,0:T(8,128)(2,1)} %get-tuple-element.33.refs_0_), channel_id=1, source_target_pairs={{0,8},{4,12},{8,0},{12,4},{16,24},{20,28},{24,16},{28,20},{1,9},{5... | collective-permute-start | bytes 393224 | tf_op jit(solution)/shard_map/ppermute | solution.py:457
  14.3 2.8 %prepare.2.refs_4_.refs_0_ = bf16[8,3,2,64,256]{4,3,2,1,0:T(8,128)(2,1)} custom-call(bf16[1024,512]{1,0:T(8,128)(2,1)} %q_ref.7, bf16[1024,512]{1,0:T(8,128)(2,1)} %k_ref.9, bf16[1024,512]{1,0:T(8,128)(2,1)} %v_ref.9, bf16[512,1024]{1,0:T(8,128)(2,1)} %cut.1.refs_0_), custom_call_target="tpu_custom_call" | custom-call | flops 402653184 | bytes 3145728 | tf_op jit(solution)/shard_map/prepare/pallas_call | solution.py:227
  17.1 1.2 collective-permute-done.2.refs_3_
  18.3 1.7 %collective-permute-done.1.refs_2_ = bf16[2,64,512]{2,1,0:T(8,128)(2,1)S(1)} collective-permute-done((bf16[2,64,512]{2,1,0:T(8,128)(2,1)}, bf16[2,64,512]{2,1,0:T(8,128)(2,1)S(1)}, u32[]{:S(2)}, u32[]{:S(2)}) %collective-permute-start.1) | collective-permute-done | bytes 131104 | tf_op jit(solution)/shard_map/ppermute | solution.py:457
  20.1 2.1 %collective-permute-start.3 = (bf16[2,512,512]{2,1,0:T(8,128)(2,1)S(1)}, bf16[2,512,512]{2,1,0:T(8,128)(2,1)}, u32[]{:S(2)}, u32[]{:S(2)}) collective-permute-start(bf16[2,512,512]{2,1,0:T(8,128)(2,1)S(1)} %after.4.refs_1_), channel_id=1, source_target_pairs={{0,4},{4,8},{8,12},{12,16},{16,20},{20,24},{24,28},{1,5},{5,9},{9,... | collective-permute-start | bytes 3145736 | tf_op jit(solution)/shard_map/ppermute | solution.py:530
  22.2 1.6 %collective-permute-start.7 = (bf16[2,64,512]{2,1,0:T(8,128)(2,1)S(1)}, bf16[2,64,512]{2,1,0:T(8,128)(2,1)S(1)}, u32[]{:S(2)}, u32[]{:S(2)}) collective-permute-start(bf16[2,64,512]{2,1,0:T(8,128)(2,1)S(1)} %collective-permute-done.2.refs_3_), channel_id=1, source_target_pairs={{0,4},{4,0},{8,12},{12,8},{16,20},{20,16},{24,28},{28,24},{1,5},{5... | collective-permute-start | bytes 393224 | tf_op jit(solution)/shard_map/ppermute | solution.py:457
  23.9 0.4 collective-permute-start.6
  24.4 4.1 %all-to-all-start = ((bf16[8,3,2,64,256]{4,3,2,1,0:T(8,128)(2,1)}), bf16[8,3,2,64,256]{4,3,2,1,0:T(8,128)(2,1)S(1)}, u32[]{:S(2)}, u32[]{:S(2)}) async-start(bf16[8,3,2,64,256]{4,3,2,1,0:T(8,128)(2,1)} %after.5), calls=%async_computation | async-start | bytes 3145728 | tf_op jit(solution)/shard_map/all_to_all | solution.py:556
  28.5 0.6 copy-done.10
  29.1 2.8 %prepare.3.refs_0_ = bf16[8,3,2,64,256]{4,3,2,1,0:T(8,128)(2,1)} custom-call(bf16[1024,512]{1,0:T(8,128)(2,1)} %q_ref.7, bf16[1024,512]{1,0:T(8,128)(2,1)} %k_ref.9, bf16[1024,512]{1,0:T(8,128)(2,1)} %v_ref.9, bf16[2,64,512]{2,1,0:T(8,128)(2,1)} %copy-done.10), custom_call_target="tpu_custom_call" | custom-call | flops 402653184 | bytes 3145728 | tf_op jit(solution)/shard_map/prepare/pallas_call | solution.py:227
  32.0 10.5 %collective-permute-done.3.rim_ref = bf16[2,512,512]{2,1,0:T(8,128)(2,1)} collective-permute-done((bf16[2,512,512]{2,1,0:T(8,128)(2,1)S(1)}, bf16[2,512,512]{2,1,0:T(8,128)(2,1)}, u32[]{:S(2)}, u32[]{:S(2)}) %collective-permute-start.3) | collective-permute-done | bytes 1048608 | tf_op jit(solution)/shard_map/ppermute | solution.py:530
  42.5 7.1 %home.3 = (f32[1024,256]{1,0:T(8,128)}, f32[8,128]{1,0:T(8,128)}) custom-call(s32[1]{0:T(128)} %bitcast.place_ref, bf16[1024,512]{1,0:T(8,128)(2,1)} %q_ref.7, bf16[1024,512]{1,0:T(8,128)(2,1)} %k_ref.9, bf16[1024,512]{1,0:T(8,128)(2,1)} %v_ref.9, bf16[2,512,512]{2,1,0:T(8,128)(2,1)} %collective-permute-done.3.rim_ref, ...), custom_call_target="tpu_custom_call" | custom-call | flops 21474836480 | bytes 7340032 | tf_op jit(solution)/shard_map/home/pallas_call | solution.py:293
  49.6 0.7 copy-done.5
  50.3 2.9 %all-to-all-done.x_ref = bf16[8,3,2,64,256]{4,3,2,1,0:T(8,128)(2,1)S(1)} async-done(((bf16[8,3,2,64,256]{4,3,2,1,0:T(8,128)(2,1)}), bf16[8,3,2,64,256]{4,3,2,1,0:T(8,128)(2,1)S(1)}, u32[]{:S(2)}, u32[]{:S(2)}) %all-to-all-start) | async-done | bytes 1572896 | tf_op jit(solution)/shard_map/all_to_all | solution.py:556
  53.2 4.2 %all-to-all-start.1 = ((bf16[8,3,2,64,256]{4,3,2,1,0:T(8,128)(2,1)}), bf16[8,3,2,64,256]{4,3,2,1,0:T(8,128)(2,1)S(1)}, u32[]{:S(2)}, u32[]{:S(2)}) async-start(bf16[8,3,2,64,256]{4,3,2,1,0:T(8,128)(2,1)} %after.6), calls=%async_computation.1 | async-start | bytes 3145728 | tf_op jit(solution)/shard_map/all_to_all | solution.py:556
  57.4 1.8 %stride.2 = (bf16[2,64,256]{2,1,0:T(8,128)(2,1)S(1)}, bf16[2,64,256]{2,1,0:T(8,128)(2,1)S(1)}, bf16[2,64,256]{2,1,0:T(8,128)(2,1)S(1)}, bf16[2,64,256]{2,1,0:T(8...) custom-call(s32[1]{0:T(128)} %bitcast.place_ref, ...), custom_call_target="tpu_custom_call" | custom-call | flops 805306368 | bytes 2097152 | tf_op jit(solution)/shard_map/stride/pallas_call | solution.py:355
  59.4 0.4 collective-permute-start.9
  59.8 1.4 %collective-permute-start.10 = (bf16[2,64,256]{2,1,0:T(8,128)(2,1)S(1)}, bf16[2,64,256]{2,1,0:T(8,128)(2,1)S(1)}, u32[]{:S(2)}, u32[]{:S(2)}) collective-permute-start(bf16[2,64,256]{2,1,0:T(8,128)(2,1)S(1)} %get-tuple-element.43), channel_id=1, source_target_pairs={{0,12},{4,8},{8,4},{12,0},{16,28},{20,24},{24,20},{28,16},{1,13},{... | collective-permute-start | bytes 196616 | tf_op jit(solution)/shard_map/ppermute | solution.py:514
  61.1 1.5 %collective-permute-start.11 = (bf16[2,64,256]{2,1,0:T(8,128)(2,1)S(1)}, bf16[2,64,256]{2,1,0:T(8,128)(2,1)S(1)}, u32[]{:S(2)}, u32[]{:S(2)}) collective-permute-start(bf16[2,64,256]{2,1,0:T(8,128)(2,1)S(1)} %get-tuple-element.44), channel_id=1, source_target_pairs={{0,16},{4,20},{8,24},{12,28},{16,0},{20,4},{24,8},{28,12},{1,17},{... | collective-permute-start | bytes 196616 | tf_op jit(solution)/shard_map/ppermute | solution.py:514
  62.6 0.3 collective-permute-start.12
  62.9 7.1 %home.2 = (f32[1024,256]{1,0:T(8,128)}, f32[8,128]{1,0:T(8,128)}) custom-call(s32[1]{0:T(128)} %bitcast.place_ref, bf16[1024,512]{1,0:T(8,128)(2,1)} %q_ref.7, bf16[1024,512]{1,0:T(8,128)(2,1)} %k_ref.9, bf16[1024,512]{1,0:T(8,128)(2,1)} %v_ref.9, bf16[2,512,512]{2,1,0:T(8,128)(2,1)} %collective-permute-done.3.rim_ref, ...), custom_call_target="tpu_custom_call" | custom-call | flops 21474836480 | bytes 7340032 | tf_op jit(solution)/shard_map/home/pallas_call | solution.py:293
  70.0 1.7 %collective-permute-start.13 = (bf16[2,64,256]{2,1,0:T(8,128)(2,1)S(1)}, bf16[2,64,256]{2,1,0:T(8,128)(2,1)S(1)}, u32[]{:S(2)}, u32[]{:S(2)}) collective-permute-start(bf16[2,64,256]{2,1,0:T(8,128)(2,1)S(1)} %get-tuple-element.46), channel_id=1, source_target_pairs={{0,24},{4,28},{8,16},{12,20},{16,8},{20,12},{24,0},{28,4},{1,25},{... | collective-permute-start | bytes 196616 | tf_op jit(solution)/shard_map/ppermute | solution.py:514
  71.7 5.8 %collective-permute-done.9.refs_2_ = bf16[2,64,256]{2,1,0:T(8,128)(2,1)S(1)} collective-permute-done((bf16[2,64,256]{2,1,0:T(8,128)(2,1)S(1)}, bf16[2,64,256]{2,1,0:T(8,128)(2,1)S(1)}, u32[]{:S(2)}, u32[]{:S(2)}) %collective-permute-start.9) | collective-permute-done | bytes 65568 | tf_op jit(solution)/shard_map/ppermute | solution.py:514
  77.5 1.6 %collective-permute-start.14 = (bf16[2,64,256]{2,1,0:T(8,128)(2,1)S(1)}, bf16[2,64,256]{2,1,0:T(8,128)(2,1)S(1)}, u32[]{:S(2)}, u32[]{:S(2)}) collective-permute-start(bf16[2,64,256]{2,1,0:T(8,128)(2,1)S(1)} %get-tuple-element.47), channel_id=1, source_target_pairs={{0,28},{4,24},{8,20},{12,16},{16,12},{20,8},{24,4},{28,0},{1,29},{... | collective-permute-start | bytes 196616 | tf_op jit(solution)/shard_map/ppermute | solution.py:514
  79.2 0.7 copy-done.8
  79.8 2.5 %stride.3 = (bf16[8,2,64,256]{3,2,1,0:T(8,128)(2,1)}, f32[8,128]{1,0:T(8,128)S(1)}) custom-call(s32[1]{0:T(128)} %bitcast.place_ref, bf16[8,3,2,64,256]{4,3,2,1,0:T(8,128)(2,1)S(1)} %all-to-all-done.1.x_ref, f32[8,128]{1,0:T(8,128)S(1)} %copy-done.8), custom_call_target="tpu_custom_call" | custom-call | flops 805306368 | bytes 2097152 | tf_op jit(solution)/shard_map/stride/pallas_call | solution.py:355
  82.3 4.2 %all-to-all-start.2 = ((bf16[8,2,64,256]{3,2,1,0:T(8,128)(2,1)}), bf16[8,2,64,256]{3,2,1,0:T(8,128)(2,1)S(1)}, u32[]{:S(2)}, u32[]{:S(2)}) async-start(bf16[8,2,64,256]{3,2,1,0:T(8,128)(2,1)} %get-tuple-element.38), calls=%async_computation.2 | async-start | bytes 1048576 | tf_op jit(solution)/shard_map/all_to_all | solution.py:562
  86.6 1.2 copy-done.7
  87.8 0.3 combine.2
  88.2 0.5 collective-permute-start.15
  88.7 2.6 %collective-permute-start.19 = (bf16[256,256]{1,0:T(8,128)(2,1)S(1)}, bf16[256,256]{1,0:T(8,128)(2,1)S(1)}, u32[]{:S(2)}, u32[]{:S(2)}) collective-permute-start(bf16[256,256]{1,0:T(8,128)(2,1)S(1)} %get-tuple-element.56), channel_id=1, source_target_pairs={{0,2},{1,3},{2,0},{3,1},{4,6},{5,7},{6,4},{7,5},{8,10},{9,11},{10,... | collective-permute-start | bytes 393224 | tf_op jit(solution)/shard_map/ppermute | solution.py:514
  91.3 0.4 collective-permute-start.20
  91.7 3.2 %collective-permute-done.15.refs_2_.refs_1_ = bf16[256,256]{1,0:T(8,128)(2,1)S(1)} collective-permute-done((bf16[256,256]{1,0:T(8,128)(2,1)S(1)}, bf16[256,256]{1,0:T(8,128)(2,1)S(1)}, u32[]{:S(2)}, u32[]{:S(2)}) %collective-permute-start.15) | collective-permute-done | bytes 131104 | tf_op jit(solution)/shard_map/ppermute | solution.py:514
  94.9 0.3 combine.3
  95.2 5.5 %collective-permute-done.19.refs_1_.refs_2_ = bf16[256,256]{1,0:T(8,128)(2,1)S(1)} collective-permute-done((bf16[256,256]{1,0:T(8,128)(2,1)S(1)}, bf16[256,256]{1,0:T(8,128)(2,1)S(1)}, u32[]{:S(2)}, u32[]{:S(2)}) %collective-permute-start.19) | collective-permute-done | bytes 131104 | tf_op jit(solution)/shard_map/ppermute | solution.py:514
  100.7 3.3 %collective-permute-done.20.refs_2_.refs_3_ = bf16[256,256]{1,0:T(8,128)(2,1)S(1)} collective-permute-done((bf16[256,256]{1,0:T(8,128)(2,1)S(1)}, bf16[256,256]{1,0:T(8,128)(2,1)S(1)}, u32[]{:S(2)}, u32[]{:S(2)}) %collective-permute-start.20) | collective-permute-done | bytes 131104 | tf_op jit(solution)/shard_map/ppermute | solution.py:514
  104.1 3.0 %collective-permute-start.17 = (bf16[256,256]{1,0:T(8,128)(2,1)S(1)}, bf16[256,256]{1,0:T(8,128)(2,1)S(1)}, u32[]{:S(2)}, u32[]{:S(2)}) collective-permute-start(bf16[256,256]{1,0:T(8,128)(2,1)S(1)} %get-tuple-element.53), channel_id=1, source_target_pairs={{0,2},{1,3},{2,0},{3,1},{4,6},{5,7},{6,4},{7,5},{8,10},{9,11},{10,... | collective-permute-start | bytes 393224 | tf_op jit(solution)/shard_map/ppermute | solution.py:514
  107.1 0.5 collective-permute-start.18
  107.6 3.8 %collective-permute-done.21.refs_5_ = bf16[4,512,1024]{2,1,0:T(8,128)(2,1)S(1)} collective-permute-done((bf16[4,512,1024]{2,1,0:T(8,128)(2,1)}, bf16[4,512,1024]{2,1,0:T(8,128)(2,1)S(1)}, u32[]{:S(2)}, u32[]{:S(2)}) %collective-permute-start.21) | collective-permute-done | bytes 4194336 | tf_op jit(solution)/shard_map/ppermute | solution.py:574
  111.4 2.2 %copy-done = bf16[4,512,1024]{2,1,0:T(8,128)(2,1)S(1)} copy-done((bf16[4,512,1024]{2,1,0:T(8,128)(2,1)S(1)}, bf16[4,512,1024]{2,1,0:T(8,128)(2,1)}, u32[]{:S(2)}) %copy-start) | copy-done | bytes 4194328
  113.6 1.2 project.2.refs_6_
  114.8 1.8 %collective-permute-done.17.refs_2_ = bf16[256,256]{1,0:T(8,128)(2,1)S(1)} collective-permute-done((bf16[256,256]{1,0:T(8,128)(2,1)S(1)}, bf16[256,256]{1,0:T(8,128)(2,1)S(1)}, u32[]{:S(2)}, u32[]{:S(2)}) %collective-permute-start.17) | collective-permute-done | bytes 131104 | tf_op jit(solution)/shard_map/ppermute | solution.py:514
  116.7 2.9 %collective-permute-done.18.refs_3_ = bf16[256,256]{1,0:T(8,128)(2,1)S(1)} collective-permute-done((bf16[256,256]{1,0:T(8,128)(2,1)S(1)}, bf16[256,256]{1,0:T(8,128)(2,1)S(1)}, u32[]{:S(2)}, u32[]{:S(2)}) %collective-permute-start.18) | collective-permute-done | bytes 131104 | tf_op jit(solution)/shard_map/ppermute | solution.py:514
  119.6 2.2 %project.3 = bf16[256,2048]{1,0:T(8,128)(2,1)} custom-call(bf16[256,256]{1,0:T(8,128)(2,1)S(1)} %get-tuple-element.51.refs_0_, bf16[256,256]{1,0:T(8,128)(2,1)S(1)} %collective-permute-done.16.refs_1_, bf16[256,256]{1,0:T(8,128)(2,1)S(1)} %collective-permute-done.17.refs_2_, bf16[256,256]{1,0:T(8,128)(2,1)S(1)} %collective-permute-done.18.refs_3_, ...), custom_call_target="tpu_custom_call" | custom-call | flops 1073741824 | bytes 4718592 | tf_op jit(solution)/shard_map/project/pallas_call | solution.py:440
  (50 shorter events, 0.7 us)
Async XLA Ops:
  6.5 97.5 %all-gather.3.cloned.1.call-start = ((), (), s32[]{:S(2)}) async-start(), calls=%async_computation.3 | async-start | bytes 5242880 | tf_op jit(solution)/shard_map/all_gather | solution.py:518
  10.8 9.3 %copy-start.1 = (bf16[2,512,512]{2,1,0:T(8,128)(2,1)S(1)}, bf16[2,512,512]{2,1,0:T(8,128)(2,1)}, u32[]{:S(2)}) copy-start(bf16[2,512,512]{2,1,0:T(8,128)(2,1)} %get-tuple-element.32.refs_0_) | copy-start | bytes 3145732
  10.8 7.6 %collective-permute-start.2 = (bf16[2,64,512]{2,1,0:T(8,128)(2,1)}, bf16[2,64,512]{2,1,0:T(8,128)(2,1)S(1)}, u32[]{:S(2)}, u32[]{:S(2)}) collective-permute-start(bf16[2,64,512]{2,1,0:T(8,128)(2,1)} %get-tuple-element.33.refs_0_), channel_id=1, source_target_pairs={{0,24},{4,28},{8,16},{12,20},{16,8},{20,12},{24,0},{28,4},{1,25},{... | collective-permute-start | bytes 393224 | tf_op jit(solution)/shard_map/ppermute | solution.py:457
  12.3 7.7 %collective-permute-start.1 = (bf16[2,64,512]{2,1,0:T(8,128)(2,1)}, bf16[2,64,512]{2,1,0:T(8,128)(2,1)S(1)}, u32[]{:S(2)}, u32[]{:S(2)}) collective-permute-start(bf16[2,64,512]{2,1,0:T(8,128)(2,1)} %get-tuple-element.33.refs_0_), channel_id=1, source_target_pairs={{0,16},{4,20},{8,24},{12,28},{16,0},{20,4},{24,8},{28,12},{1,17},{... | collective-permute-start | bytes 393224 | tf_op jit(solution)/shard_map/ppermute | solution.py:457
  12.8 7.3 %collective-permute-start = (bf16[2,64,512]{2,1,0:T(8,128)(2,1)}, bf16[2,64,512]{2,1,0:T(8,128)(2,1)S(1)}, u32[]{:S(2)}, u32[]{:S(2)}) collective-permute-start(bf16[2,64,512]{2,1,0:T(8,128)(2,1)} %get-tuple-element.33.refs_0_), channel_id=1, source_target_pairs={{0,8},{4,12},{8,0},{12,4},{16,24},{20,28},{24,16},{28,20},{1,9},{5... | collective-permute-start | bytes 393224 | tf_op jit(solution)/shard_map/ppermute | solution.py:457
  18.3 3.8 %copy-start.2 = (bf16[2,64,512]{2,1,0:T(8,128)(2,1)}, bf16[2,64,512]{2,1,0:T(8,128)(2,1)S(1)}, u32[]{:S(2)}) copy-start(bf16[2,64,512]{2,1,0:T(8,128)(2,1)S(1)} %collective-permute-done.2.refs_3_) | copy-start | bytes 393220
  20.0 3.9 %copy-start.3 = (bf16[2,64,512]{2,1,0:T(8,128)(2,1)}, bf16[2,64,512]{2,1,0:T(8,128)(2,1)S(1)}, u32[]{:S(2)}) copy-start(bf16[2,64,512]{2,1,0:T(8,128)(2,1)S(1)} %collective-permute-done.1.refs_2_) | copy-start | bytes 393220
  20.1 4.2 %copy-start.4 = (bf16[2,64,512]{2,1,0:T(8,128)(2,1)}, bf16[2,64,512]{2,1,0:T(8,128)(2,1)S(1)}, u32[]{:S(2)}) copy-start(bf16[2,64,512]{2,1,0:T(8,128)(2,1)S(1)} %collective-permute-done.refs_1_) | copy-start | bytes 393220
  20.1 3.7 %copy-start.11 = (bf16[2,64,512]{2,1,0:T(8,128)(2,1)S(1)}, bf16[2,64,512]{2,1,0:T(8,128)(2,1)}, u32[]{:S(2)}) copy-start(bf16[2,64,512]{2,1,0:T(8,128)(2,1)} %get-tuple-element.33.refs_0_) | copy-start | bytes 393220
  20.1 22.4 %collective-permute-start.3 = (bf16[2,512,512]{2,1,0:T(8,128)(2,1)S(1)}, bf16[2,512,512]{2,1,0:T(8,128)(2,1)}, u32[]{:S(2)}, u32[]{:S(2)}) collective-permute-start(bf16[2,512,512]{2,1,0:T(8,128)(2,1)S(1)} %after.4.refs_1_), channel_id=1, source_target_pairs={{0,4},{4,8},{8,12},{12,16},{16,20},{20,24},{24,28},{1,5},{5,9},{9,... | collective-permute-start | bytes 3145736 | tf_op jit(solution)/shard_map/ppermute | solution.py:530
  22.2 6.3 %collective-permute-start.7 = (bf16[2,64,512]{2,1,0:T(8,128)(2,1)S(1)}, bf16[2,64,512]{2,1,0:T(8,128)(2,1)S(1)}, u32[]{:S(2)}, u32[]{:S(2)}) collective-permute-start(bf16[2,64,512]{2,1,0:T(8,128)(2,1)S(1)} %collective-permute-done.2.refs_3_), channel_id=1, source_target_pairs={{0,4},{4,0},{8,12},{12,8},{16,20},{20,16},{24,28},{28,24},{1,5},{5... | collective-permute-start | bytes 393224 | tf_op jit(solution)/shard_map/ppermute | solution.py:457
  23.8 8.2 %collective-permute-start.4 = (bf16[2,64,512]{2,1,0:T(8,128)(2,1)S(1)}, bf16[2,64,512]{2,1,0:T(8,128)(2,1)S(1)}, u32[]{:S(2)}, u32[]{:S(2)}) collective-permute-start(bf16[2,64,512]{2,1,0:T(8,128)(2,1)S(1)} %copy-done.11), channel_id=1, source_target_pairs={{0,4},{4,0},{8,12},{12,8},{16,20},{20,16},{24,28},{28,24},{1,5},{5... | collective-permute-start | bytes 393224 | tf_op jit(solution)/shard_map/ppermute | solution.py:457
  23.9 8.1 %collective-permute-start.6 = (bf16[2,64,512]{2,1,0:T(8,128)(2,1)S(1)}, bf16[2,64,512]{2,1,0:T(8,128)(2,1)S(1)}, u32[]{:S(2)}, u32[]{:S(2)}) collective-permute-start(bf16[2,64,512]{2,1,0:T(8,128)(2,1)S(1)} %collective-permute-done.1.refs_2_), channel_id=1, source_target_pairs={{0,4},{4,0},{8,12},{12,8},{16,20},{20,16},{24,28},{28,24},{1,5},{5... | collective-permute-start | bytes 393224 | tf_op jit(solution)/shard_map/ppermute | solution.py:457
  24.3 7.7 %collective-permute-start.5 = (bf16[2,64,512]{2,1,0:T(8,128)(2,1)S(1)}, bf16[2,64,512]{2,1,0:T(8,128)(2,1)}, u32[]{:S(2)}, u32[]{:S(2)}) collective-permute-start(bf16[2,64,512]{2,1,0:T(8,128)(2,1)S(1)} %collective-permute-done.refs_1_), channel_id=1, source_target_pairs={{0,4},{4,0},{8,12},{12,8},{16,20},{20,16},{24,28},{28,24},{1,5},{5... | collective-permute-start | bytes 393224 | tf_op jit(solution)/shard_map/ppermute | solution.py:457
  24.4 28.8 %all-to-all-start = ((bf16[8,3,2,64,256]{4,3,2,1,0:T(8,128)(2,1)}), bf16[8,3,2,64,256]{4,3,2,1,0:T(8,128)(2,1)S(1)}, u32[]{:S(2)}, u32[]{:S(2)}) async-start(bf16[8,3,2,64,256]{4,3,2,1,0:T(8,128)(2,1)} %after.5), calls=%async_computation | async-start | bytes 3145728 | tf_op jit(solution)/shard_map/all_to_all | solution.py:556
  28.5 0.6 copy-start.10
  32.0 10.5 %copy-start.12 = (bf16[2,64,512]{2,1,0:T(8,128)(2,1)}, bf16[2,64,512]{2,1,0:T(8,128)(2,1)S(1)}, u32[]{:S(2)}) copy-start(bf16[2,64,512]{2,1,0:T(8,128)(2,1)S(1)} %collective-permute-done.4.refs_4_) | copy-start | bytes 393220
  32.0 10.5 %copy-start.13 = (bf16[2,64,512]{2,1,0:T(8,128)(2,1)}, bf16[2,64,512]{2,1,0:T(8,128)(2,1)S(1)}, u32[]{:S(2)}) copy-start(bf16[2,64,512]{2,1,0:T(8,128)(2,1)S(1)} %collective-permute-done.6.refs_6_) | copy-start | bytes 393220
  49.6 0.7 copy-start.5
  53.2 25.9 %all-to-all-start.1 = ((bf16[8,3,2,64,256]{4,3,2,1,0:T(8,128)(2,1)}), bf16[8,3,2,64,256]{4,3,2,1,0:T(8,128)(2,1)S(1)}, u32[]{:S(2)}, u32[]{:S(2)}) async-start(bf16[8,3,2,64,256]{4,3,2,1,0:T(8,128)(2,1)} %after.6), calls=%async_computation.1 | async-start | bytes 3145728 | tf_op jit(solution)/shard_map/all_to_all | solution.py:556
  59.2 3.7 %copy-start.9 = (f32[8,128]{1,0:T(8,128)}, f32[8,128]{1,0:T(8,128)S(1)}, u32[]{:S(2)}) copy-start(f32[8,128]{1,0:T(8,128)S(1)} %get-tuple-element.34.refs_8_) | copy-start | bytes 12292
  59.2 10.8 %collective-permute-start.8 = (bf16[2,64,256]{2,1,0:T(8,128)(2,1)S(1)}, bf16[2,64,256]{2,1,0:T(8,128)(2,1)S(1)}, u32[]{:S(2)}, u32[]{:S(2)}) collective-permute-start(bf16[2,64,256]{2,1,0:T(8,128)(2,1)S(1)} %get-tuple-element.41), channel_id=1, source_target_pairs={{0,4},{4,0},{8,12},{12,8},{16,20},{20,16},{24,28},{28,24},{1,5},{5... | collective-permute-start | bytes 196616 | tf_op jit(solution)/shard_map/ppermute | solution.py:514
  59.4 18.1 %collective-permute-start.9 = (bf16[2,64,256]{2,1,0:T(8,128)(2,1)S(1)}, bf16[2,64,256]{2,1,0:T(8,128)(2,1)S(1)}, u32[]{:S(2)}, u32[]{:S(2)}) collective-permute-start(bf16[2,64,256]{2,1,0:T(8,128)(2,1)S(1)} %get-tuple-element.42), channel_id=1, source_target_pairs={{0,8},{4,12},{8,0},{12,4},{16,24},{20,28},{24,16},{28,20},{1,9},{5... | collective-permute-start | bytes 196616 | tf_op jit(solution)/shard_map/ppermute | solution.py:514
  59.8 26.8 %collective-permute-start.10 = (bf16[2,64,256]{2,1,0:T(8,128)(2,1)S(1)}, bf16[2,64,256]{2,1,0:T(8,128)(2,1)S(1)}, u32[]{:S(2)}, u32[]{:S(2)}) collective-permute-start(bf16[2,64,256]{2,1,0:T(8,128)(2,1)S(1)} %get-tuple-element.43), channel_id=1, source_target_pairs={{0,12},{4,8},{8,4},{12,0},{16,28},{20,24},{24,20},{28,16},{1,13},{... | collective-permute-start | bytes 196616 | tf_op jit(solution)/shard_map/ppermute | solution.py:514
  61.1 25.4 %collective-permute-start.11 = (bf16[2,64,256]{2,1,0:T(8,128)(2,1)S(1)}, bf16[2,64,256]{2,1,0:T(8,128)(2,1)S(1)}, u32[]{:S(2)}, u32[]{:S(2)}) collective-permute-start(bf16[2,64,256]{2,1,0:T(8,128)(2,1)S(1)} %get-tuple-element.44), channel_id=1, source_target_pairs={{0,16},{4,20},{8,24},{12,28},{16,0},{20,4},{24,8},{28,12},{1,17},{... | collective-permute-start | bytes 196616 | tf_op jit(solution)/shard_map/ppermute | solution.py:514
  62.6 24.0 %collective-permute-start.12 = (bf16[2,64,256]{2,1,0:T(8,128)(2,1)S(1)}, bf16[2,64,256]{2,1,0:T(8,128)(2,1)S(1)}, u32[]{:S(2)}, u32[]{:S(2)}) collective-permute-start(bf16[2,64,256]{2,1,0:T(8,128)(2,1)S(1)} %get-tuple-element.45), channel_id=1, source_target_pairs={{0,20},{4,16},{8,28},{12,24},{16,4},{20,0},{24,12},{28,8},{1,21},{... | collective-permute-start | bytes 196616 | tf_op jit(solution)/shard_map/ppermute | solution.py:514
  70.0 16.6 %collective-permute-start.13 = (bf16[2,64,256]{2,1,0:T(8,128)(2,1)S(1)}, bf16[2,64,256]{2,1,0:T(8,128)(2,1)S(1)}, u32[]{:S(2)}, u32[]{:S(2)}) collective-permute-start(bf16[2,64,256]{2,1,0:T(8,128)(2,1)S(1)} %get-tuple-element.46), channel_id=1, source_target_pairs={{0,24},{4,28},{8,16},{12,20},{16,8},{20,12},{24,0},{28,4},{1,25},{... | collective-permute-start | bytes 196616 | tf_op jit(solution)/shard_map/ppermute | solution.py:514
  77.5 9.1 %collective-permute-start.14 = (bf16[2,64,256]{2,1,0:T(8,128)(2,1)S(1)}, bf16[2,64,256]{2,1,0:T(8,128)(2,1)S(1)}, u32[]{:S(2)}, u32[]{:S(2)}) collective-permute-start(bf16[2,64,256]{2,1,0:T(8,128)(2,1)S(1)} %get-tuple-element.47), channel_id=1, source_target_pairs={{0,28},{4,24},{8,20},{12,16},{16,12},{20,8},{24,4},{28,0},{1,29},{... | collective-permute-start | bytes 196616 | tf_op jit(solution)/shard_map/ppermute | solution.py:514
  79.2 0.7 copy-start.8
  82.3 12.6 %all-to-all-start.2 = ((bf16[8,2,64,256]{3,2,1,0:T(8,128)(2,1)}), bf16[8,2,64,256]{3,2,1,0:T(8,128)(2,1)S(1)}, u32[]{:S(2)}, u32[]{:S(2)}) async-start(bf16[8,2,64,256]{3,2,1,0:T(8,128)(2,1)} %get-tuple-element.38), calls=%async_computation.2 | async-start | bytes 1048576 | tf_op jit(solution)/shard_map/all_to_all | solution.py:562
  86.6 1.2 copy-start.7
  87.8 7.0 %copy-start.6 = (f32[1024,256]{1,0:T(8,128)S(1)}, f32[1024,256]{1,0:T(8,128)}, u32[]{:S(2)}) copy-start(f32[1024,256]{1,0:T(8,128)} %get-tuple-element.35.home_ref) | copy-start | bytes 3145732
  88.2 6.7 %collective-permute-start.15 = (bf16[256,256]{1,0:T(8,128)(2,1)S(1)}, bf16[256,256]{1,0:T(8,128)(2,1)S(1)}, u32[]{:S(2)}, u32[]{:S(2)}) collective-permute-start(bf16[256,256]{1,0:T(8,128)(2,1)S(1)} %get-tuple-element.50), channel_id=1, source_target_pairs={{0,1},{1,0},{2,3},{3,2},{4,5},{5,4},{6,7},{7,6},{8,9},{9,8},{10,11... | collective-permute-start | bytes 393224 | tf_op jit(solution)/shard_map/ppermute | solution.py:514
  88.7 12.1 %collective-permute-start.19 = (bf16[256,256]{1,0:T(8,128)(2,1)S(1)}, bf16[256,256]{1,0:T(8,128)(2,1)S(1)}, u32[]{:S(2)}, u32[]{:S(2)}) collective-permute-start(bf16[256,256]{1,0:T(8,128)(2,1)S(1)} %get-tuple-element.56), channel_id=1, source_target_pairs={{0,2},{1,3},{2,0},{3,1},{4,6},{5,7},{6,4},{7,5},{8,10},{9,11},{10,... | collective-permute-start | bytes 393224 | tf_op jit(solution)/shard_map/ppermute | solution.py:514
  91.3 12.8 %collective-permute-start.20 = (bf16[256,256]{1,0:T(8,128)(2,1)S(1)}, bf16[256,256]{1,0:T(8,128)(2,1)S(1)}, u32[]{:S(2)}, u32[]{:S(2)}) collective-permute-start(bf16[256,256]{1,0:T(8,128)(2,1)S(1)} %get-tuple-element.57), channel_id=1, source_target_pairs={{0,3},{1,2},{2,1},{3,0},{4,7},{5,6},{6,5},{7,4},{8,11},{9,10},{10,... | collective-permute-start | bytes 393224 | tf_op jit(solution)/shard_map/ppermute | solution.py:514
  104.0 7.4 %collective-permute-start.21 = (bf16[4,512,1024]{2,1,0:T(8,128)(2,1)}, bf16[4,512,1024]{2,1,0:T(8,128)(2,1)S(1)}, u32[]{:S(2)}, u32[]{:S(2)}) collective-permute-start(bf16[4,512,1024]{2,1,0:T(8,128)(2,1)} %after.7.refs_4_), channel_id=1, source_target_pairs={{0,4},{4,0},{8,12},{12,8},{16,20},{20,16},{24,28},{28,24},{1,5},{5... | collective-permute-start | bytes 12582920 | tf_op jit(solution)/shard_map/ppermute | solution.py:574
  104.0 10.8 %collective-permute-start.16 = (bf16[256,256]{1,0:T(8,128)(2,1)S(1)}, bf16[256,256]{1,0:T(8,128)(2,1)S(1)}, u32[]{:S(2)}, u32[]{:S(2)}) collective-permute-start(bf16[256,256]{1,0:T(8,128)(2,1)S(1)} %get-tuple-element.52), channel_id=1, source_target_pairs={{0,1},{1,0},{2,3},{3,2},{4,5},{5,4},{6,7},{7,6},{8,9},{9,8},{10,11... | collective-permute-start | bytes 393224 | tf_op jit(solution)/shard_map/ppermute | solution.py:514
  104.1 12.5 %collective-permute-start.17 = (bf16[256,256]{1,0:T(8,128)(2,1)S(1)}, bf16[256,256]{1,0:T(8,128)(2,1)S(1)}, u32[]{:S(2)}, u32[]{:S(2)}) collective-permute-start(bf16[256,256]{1,0:T(8,128)(2,1)S(1)} %get-tuple-element.53), channel_id=1, source_target_pairs={{0,2},{1,3},{2,0},{3,1},{4,6},{5,7},{6,4},{7,5},{8,10},{9,11},{10,... | collective-permute-start | bytes 393224 | tf_op jit(solution)/shard_map/ppermute | solution.py:514
  107.1 12.5 %collective-permute-start.18 = (bf16[256,256]{1,0:T(8,128)(2,1)S(1)}, bf16[256,256]{1,0:T(8,128)(2,1)S(1)}, u32[]{:S(2)}, u32[]{:S(2)}) collective-permute-start(bf16[256,256]{1,0:T(8,128)(2,1)S(1)} %get-tuple-element.54), channel_id=1, source_target_pairs={{0,3},{1,2},{2,1},{3,0},{4,7},{5,6},{6,5},{7,4},{8,11},{9,10},{10,... | collective-permute-start | bytes 393224 | tf_op jit(solution)/shard_map/ppermute | solution.py:514
  111.4 2.2 %copy-start = (bf16[4,512,1024]{2,1,0:T(8,128)(2,1)S(1)}, bf16[4,512,1024]{2,1,0:T(8,128)(2,1)}, u32[]{:S(2)}) copy-start(bf16[4,512,1024]{2,1,0:T(8,128)(2,1)} %after.7.refs_4_) | copy-start | bytes 12582916
Sparse Core Ops, SparseCore 0:
  8.9 79.4 all-gather.2

commit v16 on v14

--- a/solution.py
+++ b/solution.py
@@ -30,7 +30,7 @@
 
 
 def mark_spec():
-    return pl.BlockSpec(MARK.shape, lambda *place: (0, 0))
+    return pl.BlockSpec(memory_space=pltpu.HBM)
 
 
 def moments(arrays):
@@ -41,11 +41,11 @@
     anywhere = pl.BlockSpec(memory_space=pl.ANY)
     return pl.pallas_call(
         lambda *refs: None,
-        in_specs=[anywhere] * (len(arrays) + len(others)),
+        in_specs=[anywhere] * len(arrays) + moments(others),
         out_specs=[anywhere] * len(arrays),
         out_shape=[jax.ShapeDtypeStruct(array.shape, array.dtype) for array in arrays],
         input_output_aliases={i: i for i in range(len(arrays))},
-        compiler_params=params(60),
+        compiler_params=params(52),
         cost_estimate=cost(0, 0),
         name="after",
     )(*arrays, *others)
@@ -225,8 +225,7 @@
 
 
 def home_kernel(place_ref, q_ref, k_ref, v_ref, rim_ref, *refs, order):
-    sum_refs, (o_ref, mark_ref) = refs[: len(order)], refs[-2:]
-    mark_ref[...] = jnp.zeros_like(mark_ref)
+    sum_refs, o_ref = refs[: len(order)], refs[-2]
     place = place_ref[0]
     tokens_dev = q_ref.shape[0]
     back = WINDOW // TILE
@@ -301,8 +300,7 @@
 
 def stride_kernel(place_ref, x_ref, *refs, slabs):
     ctx, _, _, rows, width = x_ref.shape
-    o_refs, mark_ref, held_ref = refs[-2 - (ctx if slabs else 1) : -2], refs[-2], refs[-1]
-    mark_ref[...] = jnp.zeros_like(mark_ref)
+    o_refs, held_ref = refs[-2 - (ctx if slabs else 1) : -2], refs[-1]
     count = ctx * rows
     row = iota2((TILE, TILE), 0)
     col = iota2((TILE, TILE), 1)
@@ -361,8 +359,7 @@
 
 def combine_kernel(home_ref, *refs, slots, arrays, ctx):
     seat, place = lax.axis_index("head"), lax.axis_index("ctx")
-    back_refs, o_refs, mark_ref = refs[:arrays], refs[-slots - 1 : -1], refs[-1]
-    mark_ref[...] = jnp.zeros_like(mark_ref)
+    back_refs, o_refs = refs[:arrays], refs[-slots - 1 : -1]
     tokens_dev, width = home_ref.shape
     size = tokens_dev // slots
     per = STRIDE // ctx
@@ -392,7 +389,7 @@
         functools.partial(combine_kernel, slots=slots, arrays=len(backs), ctx=ctx),
         in_specs=[pl.BlockSpec(memory_space=pltpu.VMEM)] * (1 + len(backs))
         + moments(waits),
-        out_specs=[pl.BlockSpec(memory_space=pltpu.VMEM)] * (slots + 1),
+        out_specs=[pl.BlockSpec(memory_space=pltpu.VMEM)] * slots + [mark_spec()],
         out_shape=[jax.ShapeDtypeStruct((size, width), BF16)] * slots + [MARK],
         compiler_params=params(24),
         cost_estimate=cost(56 * tokens_dev * TILE * width, 8 * tokens_dev * width),

time: 130 us -> 128 us (0.985)
  local copies, waits for them, and re-layouts: 6.95 us -> 5.43 us
    unnamed x30 -> x28, local copies, waits for them, and re-layouts: 6.95 us -> 5.43 us
where the time goes in v16:
time: 128 us
  waiting for transfers between devices  40.2 us (31%)
  starting transfers between devices  36.2 us (28%)
  Pallas kernels  32.4 us (25%)
  between operations  13.6 us (11%)
  local copies, waits for them, and re-layouts  5.43 us (4%)
    ppermute x13, waiting for transfers between devices, exchange(): moved.append(lax.ppermute(slabs[slot], axis, pairs))  23.7 us
    ppermute x13, starting transfers between devices, exchange(): moved.append(lax.ppermute(slabs[slot], axis, pairs))  15.7 us
    pallas_call x2, Pallas kernels, home_sections(): pl.pallas_call(functools.partial(home_kernel, order=order), grid=(heads,)...  14.2 us
    ppermute x1, waiting for transfers between devices, body(): before = lax.ppermute(rim, 'ctx', [(i, i + 1) for i in range(ctx - 1)])  10.5 us
    all_to_all x2, starting transfers between devices, body(): lax.all_to_all(send, 'ctx', split_axis=0, concat_axis=0, tiled=True)  8.32 us
    ppermute x7, starting transfers between devices, swapped(): return lax.ppermute(piece, 'ctx', [(i, i ^ distance) for i in range(count)])  5.73 us
    pallas_call x2, Pallas kernels, prepare(): pl.pallas_call(prep_kernel, grid=(tokens_dev // size,), in_specs=[pl.Bloc...  5.63 us
    unnamed x28, local copies, waits for them, and re-layouts  5.43 us
  transfers between devices with their start and end apart: 26, of which 11 were waited for; matrix products, arithmetic and copies ran while one was open for 0% of the time, Pallas kernels for 22%

profile of v16, /device:TPU:10, one launch (start us, length us, event | category | flops | bytes accessed | tf_op | source)
XLA Modules:
  0.0 127.8 jit_solution(18163937060134922005)
XLA Ops:
  6.5 2.0 %cut.1.refs_0_ = bf16[512,1024]{1,0:T(8,128)(2,1)} custom-call(bf16[512,2048]{1,0:T(8,128)(2,1)} %weight_ref.1), custom_call_target="tpu_custom_call" | custom-call | bytes 2097152 | tf_op jit(solution)/shard_map/cut/pallas_call | solution.py:182
  8.5 2.2 %edges.1 = (bf16[2,512,512]{2,1,0:T(8,128)(2,1)}, bf16[2,64,512]{2,1,0:T(8,128)(2,1)}) custom-call(bf16[1024,512]{1,0:T(8,128)(2,1)} %k_ref.9, bf16[1024,512]{1,0:T(8,128)(2,1)} %v_ref.9, bf16[8,128,512]{2,1,0:T(8,128)(2,1)} %bitcast.5, bf16[8,128,512]{2,1,0:T(8,128)(2,1)} %bitcast.6, bf16[512,1024]{1,0:T(8,128)(2,1)} %cut.1.refs_0_), custom_call_target="tpu_custom_call" | custom-call | bytes 2097152 | tf_op jit(solution)/shard_map/edges/pallas_call | solution.py:142
  10.8 1.6 %collective-permute-start.2 = (bf16[2,64,512]{2,1,0:T(8,128)(2,1)}, bf16[2,64,512]{2,1,0:T(8,128)(2,1)S(1)}, u32[]{:S(2)}, u32[]{:S(2)}) collective-permute-start(bf16[2,64,512]{2,1,0:T(8,128)(2,1)} %get-tuple-element.33.refs_0_), channel_id=1, source_target_pairs={{0,24},{4,28},{8,16},{12,20},{16,8},{20,12},{24,0},{28,4},{1,25},{... | collective-permute-start | bytes 393224 | tf_op jit(solution)/shard_map/ppermute | solution.py:445
  12.3 0.5 collective-permute-start.1
  12.8 1.5 %collective-permute-start = (bf16[2,64,512]{2,1,0:T(8,128)(2,1)}, bf16[2,64,512]{2,1,0:T(8,128)(2,1)S(1)}, u32[]{:S(2)}, u32[]{:S(2)}) collective-permute-start(bf16[2,64,512]{2,1,0:T(8,128)(2,1)} %get-tuple-element.33.refs_0_), channel_id=1, source_target_pairs={{0,8},{4,12},{8,0},{12,4},{16,24},{20,28},{24,16},{28,20},{1,9},{5... | collective-permute-start | bytes 393224 | tf_op jit(solution)/shard_map/ppermute | solution.py:445
  14.3 2.8 %prepare.2.refs_4_.refs_0_ = bf16[8,3,2,64,256]{4,3,2,1,0:T(8,128)(2,1)} custom-call(bf16[1024,512]{1,0:T(8,128)(2,1)} %q_ref.7, bf16[1024,512]{1,0:T(8,128)(2,1)} %k_ref.9, bf16[1024,512]{1,0:T(8,128)(2,1)} %v_ref.9, bf16[512,1024]{1,0:T(8,128)(2,1)} %cut.1.refs_0_), custom_call_target="tpu_custom_call" | custom-call | flops 402653184 | bytes 3145728 | tf_op jit(solution)/shard_map/prepare/pallas_call | solution.py:215
  17.1 1.2 collective-permute-done.2.refs_3_
  18.3 1.7 %collective-permute-done.1.refs_2_ = bf16[2,64,512]{2,1,0:T(8,128)(2,1)S(1)} collective-permute-done((bf16[2,64,512]{2,1,0:T(8,128)(2,1)}, bf16[2,64,512]{2,1,0:T(8,128)(2,1)S(1)}, u32[]{:S(2)}, u32[]{:S(2)}) %collective-permute-start.1) | collective-permute-done | bytes 131104 | tf_op jit(solution)/shard_map/ppermute | solution.py:445
  20.1 2.1 %collective-permute-start.3 = (bf16[2,512,512]{2,1,0:T(8,128)(2,1)S(1)}, bf16[2,512,512]{2,1,0:T(8,128)(2,1)}, u32[]{:S(2)}, u32[]{:S(2)}) collective-permute-start(bf16[2,512,512]{2,1,0:T(8,128)(2,1)S(1)} %after.4.refs_1_), channel_id=1, source_target_pairs={{0,4},{4,8},{8,12},{12,16},{16,20},{20,24},{24,28},{1,5},{5,9},{9,... | collective-permute-start | bytes 3145736 | tf_op jit(solution)/shard_map/ppermute | solution.py:518
  22.2 1.6 %collective-permute-start.7 = (bf16[2,64,512]{2,1,0:T(8,128)(2,1)S(1)}, bf16[2,64,512]{2,1,0:T(8,128)(2,1)S(1)}, u32[]{:S(2)}, u32[]{:S(2)}) collective-permute-start(bf16[2,64,512]{2,1,0:T(8,128)(2,1)S(1)} %collective-permute-done.2.refs_3_), channel_id=1, source_target_pairs={{0,4},{4,0},{8,12},{12,8},{16,20},{20,16},{24,28},{28,24},{1,5},{5... | collective-permute-start | bytes 393224 | tf_op jit(solution)/shard_map/ppermute | solution.py:445
  23.9 0.4 collective-permute-start.6
  24.4 4.1 %all-to-all-start = ((bf16[8,3,2,64,256]{4,3,2,1,0:T(8,128)(2,1)}), bf16[8,3,2,64,256]{4,3,2,1,0:T(8,128)(2,1)S(1)}, u32[]{:S(2)}, u32[]{:S(2)}) async-start(bf16[8,3,2,64,256]{4,3,2,1,0:T(8,128)(2,1)} %after.5), calls=%async_computation | async-start | bytes 3145728 | tf_op jit(solution)/shard_map/all_to_all | solution.py:544
  28.5 0.6 copy-done.10
  29.1 2.8 %prepare.3.refs_0_ = bf16[8,3,2,64,256]{4,3,2,1,0:T(8,128)(2,1)} custom-call(bf16[1024,512]{1,0:T(8,128)(2,1)} %q_ref.7, bf16[1024,512]{1,0:T(8,128)(2,1)} %k_ref.9, bf16[1024,512]{1,0:T(8,128)(2,1)} %v_ref.9, bf16[2,64,512]{2,1,0:T(8,128)(2,1)} %copy-done.10), custom_call_target="tpu_custom_call" | custom-call | flops 402653184 | bytes 3145728 | tf_op jit(solution)/shard_map/prepare/pallas_call | solution.py:215
  32.0 10.5 %collective-permute-done.3.rim_ref = bf16[2,512,512]{2,1,0:T(8,128)(2,1)} collective-permute-done((bf16[2,512,512]{2,1,0:T(8,128)(2,1)S(1)}, bf16[2,512,512]{2,1,0:T(8,128)(2,1)}, u32[]{:S(2)}, u32[]{:S(2)}) %collective-permute-start.3) | collective-permute-done | bytes 1048608 | tf_op jit(solution)/shard_map/ppermute | solution.py:518
  42.5 7.1 %home.3 = (f32[1024,256]{1,0:T(8,128)}, f32[8,128]{1,0:T(8,128)}) custom-call(s32[1]{0:T(128)} %bitcast.place_ref, bf16[1024,512]{1,0:T(8,128)(2,1)} %q_ref.7, bf16[1024,512]{1,0:T(8,128)(2,1)} %k_ref.9, bf16[1024,512]{1,0:T(8,128)(2,1)} %v_ref.9, bf16[2,512,512]{2,1,0:T(8,128)(2,1)} %collective-permute-done.3.rim_ref, ...), custom_call_target="tpu_custom_call" | custom-call | flops 21474836480 | bytes 7340032 | tf_op jit(solution)/shard_map/home/pallas_call | solution.py:281
  49.6 0.7 copy-done.5
  50.3 2.9 %all-to-all-done.x_ref = bf16[8,3,2,64,256]{4,3,2,1,0:T(8,128)(2,1)S(1)} async-done(((bf16[8,3,2,64,256]{4,3,2,1,0:T(8,128)(2,1)}), bf16[8,3,2,64,256]{4,3,2,1,0:T(8,128)(2,1)S(1)}, u32[]{:S(2)}, u32[]{:S(2)}) %all-to-all-start) | async-done | bytes 1572896 | tf_op jit(solution)/shard_map/all_to_all | solution.py:544
  53.2 4.2 %all-to-all-start.1 = ((bf16[8,3,2,64,256]{4,3,2,1,0:T(8,128)(2,1)}), bf16[8,3,2,64,256]{4,3,2,1,0:T(8,128)(2,1)S(1)}, u32[]{:S(2)}, u32[]{:S(2)}) async-start(bf16[8,3,2,64,256]{4,3,2,1,0:T(8,128)(2,1)} %after.6), calls=%async_computation.1 | async-start | bytes 3145728 | tf_op jit(solution)/shard_map/all_to_all | solution.py:544
  57.4 1.8 %stride.2 = (bf16[2,64,256]{2,1,0:T(8,128)(2,1)S(1)}, bf16[2,64,256]{2,1,0:T(8,128)(2,1)S(1)}, bf16[2,64,256]{2,1,0:T(8,128)(2,1)S(1)}, bf16[2,64,256]{2,1,0:T(8...) custom-call(s32[1]{0:T(128)} %bitcast.place_ref, ...), custom_call_target="tpu_custom_call" | custom-call | flops 805306368 | bytes 2097152 | tf_op jit(solution)/shard_map/stride/pallas_call | solution.py:343
  59.2 0.2 collective-permute-start.8
  59.4 0.4 collective-permute-start.9
  59.8 1.4 %collective-permute-start.10 = (bf16[2,64,256]{2,1,0:T(8,128)(2,1)S(1)}, bf16[2,64,256]{2,1,0:T(8,128)(2,1)S(1)}, u32[]{:S(2)}, u32[]{:S(2)}) collective-permute-start(bf16[2,64,256]{2,1,0:T(8,128)(2,1)S(1)} %get-tuple-element.43), channel_id=1, source_target_pairs={{0,12},{4,8},{8,4},{12,0},{16,28},{20,24},{24,20},{28,16},{1,13},{... | collective-permute-start | bytes 196616 | tf_op jit(solution)/shard_map/ppermute | solution.py:502
  61.1 1.5 %collective-permute-start.11 = (bf16[2,64,256]{2,1,0:T(8,128)(2,1)S(1)}, bf16[2,64,256]{2,1,0:T(8,128)(2,1)S(1)}, u32[]{:S(2)}, u32[]{:S(2)}) collective-permute-start(bf16[2,64,256]{2,1,0:T(8,128)(2,1)S(1)} %get-tuple-element.44), channel_id=1, source_target_pairs={{0,16},{4,20},{8,24},{12,28},{16,0},{20,4},{24,8},{28,12},{1,17},{... | collective-permute-start | bytes 196616 | tf_op jit(solution)/shard_map/ppermute | solution.py:502
  62.6 0.3 collective-permute-start.12
  62.9 7.1 %home.2 = (f32[1024,256]{1,0:T(8,128)}, f32[8,128]{1,0:T(8,128)}) custom-call(s32[1]{0:T(128)} %bitcast.place_ref, bf16[1024,512]{1,0:T(8,128)(2,1)} %q_ref.7, bf16[1024,512]{1,0:T(8,128)(2,1)} %k_ref.9, bf16[1024,512]{1,0:T(8,128)(2,1)} %v_ref.9, bf16[2,512,512]{2,1,0:T(8,128)(2,1)} %collective-permute-done.3.rim_ref, ...), custom_call_target="tpu_custom_call" | custom-call | flops 21474836480 | bytes 7340032 | tf_op jit(solution)/shard_map/home/pallas_call | solution.py:281
  70.0 1.7 %collective-permute-start.13 = (bf16[2,64,256]{2,1,0:T(8,128)(2,1)S(1)}, bf16[2,64,256]{2,1,0:T(8,128)(2,1)S(1)}, u32[]{:S(2)}, u32[]{:S(2)}) collective-permute-start(bf16[2,64,256]{2,1,0:T(8,128)(2,1)S(1)} %get-tuple-element.46), channel_id=1, source_target_pairs={{0,24},{4,28},{8,16},{12,20},{16,8},{20,12},{24,0},{28,4},{1,25},{... | collective-permute-start | bytes 196616 | tf_op jit(solution)/shard_map/ppermute | solution.py:502
  71.7 5.8 %collective-permute-done.9.refs_2_ = bf16[2,64,256]{2,1,0:T(8,128)(2,1)S(1)} collective-permute-done((bf16[2,64,256]{2,1,0:T(8,128)(2,1)S(1)}, bf16[2,64,256]{2,1,0:T(8,128)(2,1)S(1)}, u32[]{:S(2)}, u32[]{:S(2)}) %collective-permute-start.9) | collective-permute-done | bytes 65568 | tf_op jit(solution)/shard_map/ppermute | solution.py:502
  77.5 1.6 %collective-permute-start.14 = (bf16[2,64,256]{2,1,0:T(8,128)(2,1)S(1)}, bf16[2,64,256]{2,1,0:T(8,128)(2,1)S(1)}, u32[]{:S(2)}, u32[]{:S(2)}) collective-permute-start(bf16[2,64,256]{2,1,0:T(8,128)(2,1)S(1)} %get-tuple-element.47), channel_id=1, source_target_pairs={{0,28},{4,24},{8,20},{12,16},{16,12},{20,8},{24,4},{28,0},{1,29},{... | collective-permute-start | bytes 196616 | tf_op jit(solution)/shard_map/ppermute | solution.py:502
  79.2 0.7 copy-done.8
  79.8 2.5 %stride.3 = (bf16[8,2,64,256]{3,2,1,0:T(8,128)(2,1)}, f32[8,128]{1,0:T(8,128)S(1)}) custom-call(s32[1]{0:T(128)} %bitcast.place_ref, bf16[8,3,2,64,256]{4,3,2,1,0:T(8,128)(2,1)S(1)} %all-to-all-done.1.x_ref, f32[8,128]{1,0:T(8,128)S(1)} %copy-done.8), custom_call_target="tpu_custom_call" | custom-call | flops 805306368 | bytes 2097152 | tf_op jit(solution)/shard_map/stride/pallas_call | solution.py:343
  82.3 4.2 %all-to-all-start.2 = ((bf16[8,2,64,256]{3,2,1,0:T(8,128)(2,1)}), bf16[8,2,64,256]{3,2,1,0:T(8,128)(2,1)S(1)}, u32[]{:S(2)}, u32[]{:S(2)}) async-start(bf16[8,2,64,256]{3,2,1,0:T(8,128)(2,1)} %get-tuple-element.38), calls=%async_computation.2 | async-start | bytes 1048576 | tf_op jit(solution)/shard_map/all_to_all | solution.py:550
  86.6 1.2 copy-done.7
  87.8 0.3 combine.2
  88.2 0.5 collective-permute-start.15
  88.7 2.6 %collective-permute-start.16 = (bf16[256,256]{1,0:T(8,128)(2,1)S(1)}, bf16[256,256]{1,0:T(8,128)(2,1)S(1)}, u32[]{:S(2)}, u32[]{:S(2)}) collective-permute-start(bf16[256,256]{1,0:T(8,128)(2,1)S(1)} %get-tuple-element.51), channel_id=1, source_target_pairs={{0,2},{1,3},{2,0},{3,1},{4,6},{5,7},{6,4},{7,5},{8,10},{9,11},{10,... | collective-permute-start | bytes 393224 | tf_op jit(solution)/shard_map/ppermute | solution.py:502
  91.3 3.8 %collective-permute-done.15.refs_2_.refs_1_ = bf16[256,256]{1,0:T(8,128)(2,1)S(1)} collective-permute-done((bf16[256,256]{1,0:T(8,128)(2,1)S(1)}, bf16[256,256]{1,0:T(8,128)(2,1)S(1)}, u32[]{:S(2)}, u32[]{:S(2)}) %collective-permute-start.15) | collective-permute-done | bytes 131104 | tf_op jit(solution)/shard_map/ppermute | solution.py:502
  95.1 3.2 %collective-permute-done.16.refs_3_.refs_2_ = bf16[256,256]{1,0:T(8,128)(2,1)S(1)} collective-permute-done((bf16[256,256]{1,0:T(8,128)(2,1)S(1)}, bf16[256,256]{1,0:T(8,128)(2,1)S(1)}, u32[]{:S(2)}, u32[]{:S(2)}) %collective-permute-start.16) | collective-permute-done | bytes 131104 | tf_op jit(solution)/shard_map/ppermute | solution.py:502
  98.3 0.3 combine.3
  98.7 0.5 collective-permute-start.21
  99.3 3.6 %collective-permute-start.17 = (bf16[256,256]{1,0:T(8,128)(2,1)S(1)}, bf16[256,256]{1,0:T(8,128)(2,1)S(1)}, u32[]{:S(2)}, u32[]{:S(2)}) collective-permute-start(bf16[256,256]{1,0:T(8,128)(2,1)S(1)} %get-tuple-element.53), channel_id=1, source_target_pairs={{0,1},{1,0},{2,3},{3,2},{4,5},{5,4},{6,7},{7,6},{8,9},{9,8},{10,11... | collective-permute-start | bytes 393224 | tf_op jit(solution)/shard_map/ppermute | solution.py:502
  102.9 1.5 %collective-permute-start.19 = (bf16[256,256]{1,0:T(8,128)(2,1)S(1)}, bf16[256,256]{1,0:T(8,128)(2,1)S(1)}, u32[]{:S(2)}, u32[]{:S(2)}) collective-permute-start(bf16[256,256]{1,0:T(8,128)(2,1)S(1)} %get-tuple-element.55), channel_id=1, source_target_pairs={{0,3},{1,2},{2,1},{3,0},{4,7},{5,6},{6,5},{7,4},{8,11},{9,10},{10,... | collective-permute-start | bytes 393224 | tf_op jit(solution)/shard_map/ppermute | solution.py:502
  104.3 3.6 %collective-permute-done.21.refs_3_ = bf16[256,256]{1,0:T(8,128)(2,1)S(1)} collective-permute-done((bf16[256,256]{1,0:T(8,128)(2,1)S(1)}, bf16[256,256]{1,0:T(8,128)(2,1)S(1)}, u32[]{:S(2)}, u32[]{:S(2)}) %collective-permute-start.21) | collective-permute-done | bytes 131104 | tf_op jit(solution)/shard_map/ppermute | solution.py:502
  107.9 2.2 %copy-done = bf16[4,512,1024]{2,1,0:T(8,128)(2,1)S(1)} copy-done((bf16[4,512,1024]{2,1,0:T(8,128)(2,1)S(1)}, bf16[4,512,1024]{2,1,0:T(8,128)(2,1)}, u32[]{:S(2)}) %copy-start) | copy-done | bytes 4194328
  110.1 1.2 project.2.refs_6_
  111.4 1.4 %collective-permute-done.18.refs_2_ = bf16[256,256]{1,0:T(8,128)(2,1)S(1)} collective-permute-done((bf16[256,256]{1,0:T(8,128)(2,1)S(1)}, bf16[256,256]{1,0:T(8,128)(2,1)S(1)}, u32[]{:S(2)}, u32[]{:S(2)}) %collective-permute-start.18) | collective-permute-done | bytes 131104 | tf_op jit(solution)/shard_map/ppermute | solution.py:502
  112.8 5.9 %collective-permute-done.19.refs_3_ = bf16[256,256]{1,0:T(8,128)(2,1)S(1)} collective-permute-done((bf16[256,256]{1,0:T(8,128)(2,1)S(1)}, bf16[256,256]{1,0:T(8,128)(2,1)S(1)}, u32[]{:S(2)}, u32[]{:S(2)}) %collective-permute-start.19) | collective-permute-done | bytes 131104 | tf_op jit(solution)/shard_map/ppermute | solution.py:502
  118.7 2.2 %project.3 = bf16[256,2048]{1,0:T(8,128)(2,1)} custom-call(bf16[256,256]{1,0:T(8,128)(2,1)S(1)} %get-tuple-element.52.refs_0_, bf16[256,256]{1,0:T(8,128)(2,1)S(1)} %collective-permute-done.17.refs_1_, bf16[256,256]{1,0:T(8,128)(2,1)S(1)} %collective-permute-done.18.refs_2_, bf16[256,256]{1,0:T(8,128)(2,1)S(1)} %collective-permute-done.19.refs_3_, ...), custom_call_target="tpu_custom_call" | custom-call | flops 1073741824 | bytes 4718592 | tf_op jit(solution)/shard_map/project/pallas_call | solution.py:428
  (49 shorter events, 0.5 us)
Async XLA Ops:
  6.5 92.1 %all-gather.3.cloned.1.call-start = ((), (), s32[]{:S(2)}) async-start(), calls=%async_computation.3 | async-start | bytes 5242880 | tf_op jit(solution)/shard_map/all_gather | solution.py:506
  10.8 9.3 %copy-start.1 = (bf16[2,512,512]{2,1,0:T(8,128)(2,1)S(1)}, bf16[2,512,512]{2,1,0:T(8,128)(2,1)}, u32[]{:S(2)}) copy-start(bf16[2,512,512]{2,1,0:T(8,128)(2,1)} %get-tuple-element.32.refs_0_) | copy-start | bytes 3145732
  10.8 7.6 %collective-permute-start.2 = (bf16[2,64,512]{2,1,0:T(8,128)(2,1)}, bf16[2,64,512]{2,1,0:T(8,128)(2,1)S(1)}, u32[]{:S(2)}, u32[]{:S(2)}) collective-permute-start(bf16[2,64,512]{2,1,0:T(8,128)(2,1)} %get-tuple-element.33.refs_0_), channel_id=1, source_target_pairs={{0,24},{4,28},{8,16},{12,20},{16,8},{20,12},{24,0},{28,4},{1,25},{... | collective-permute-start | bytes 393224 | tf_op jit(solution)/shard_map/ppermute | solution.py:445
  12.3 7.7 %collective-permute-start.1 = (bf16[2,64,512]{2,1,0:T(8,128)(2,1)}, bf16[2,64,512]{2,1,0:T(8,128)(2,1)S(1)}, u32[]{:S(2)}, u32[]{:S(2)}) collective-permute-start(bf16[2,64,512]{2,1,0:T(8,128)(2,1)} %get-tuple-element.33.refs_0_), channel_id=1, source_target_pairs={{0,16},{4,20},{8,24},{12,28},{16,0},{20,4},{24,8},{28,12},{1,17},{... | collective-permute-start | bytes 393224 | tf_op jit(solution)/shard_map/ppermute | solution.py:445
  12.8 7.3 %collective-permute-start = (bf16[2,64,512]{2,1,0:T(8,128)(2,1)}, bf16[2,64,512]{2,1,0:T(8,128)(2,1)S(1)}, u32[]{:S(2)}, u32[]{:S(2)}) collective-permute-start(bf16[2,64,512]{2,1,0:T(8,128)(2,1)} %get-tuple-element.33.refs_0_), channel_id=1, source_target_pairs={{0,8},{4,12},{8,0},{12,4},{16,24},{20,28},{24,16},{28,20},{1,9},{5... | collective-permute-start | bytes 393224 | tf_op jit(solution)/shard_map/ppermute | solution.py:445
  18.3 3.8 %copy-start.2 = (bf16[2,64,512]{2,1,0:T(8,128)(2,1)}, bf16[2,64,512]{2,1,0:T(8,128)(2,1)S(1)}, u32[]{:S(2)}) copy-start(bf16[2,64,512]{2,1,0:T(8,128)(2,1)S(1)} %collective-permute-done.2.refs_3_) | copy-start | bytes 393220
  20.0 3.9 %copy-start.3 = (bf16[2,64,512]{2,1,0:T(8,128)(2,1)}, bf16[2,64,512]{2,1,0:T(8,128)(2,1)S(1)}, u32[]{:S(2)}) copy-start(bf16[2,64,512]{2,1,0:T(8,128)(2,1)S(1)} %collective-permute-done.1.refs_2_) | copy-start | bytes 393220
  20.1 4.2 %copy-start.4 = (bf16[2,64,512]{2,1,0:T(8,128)(2,1)}, bf16[2,64,512]{2,1,0:T(8,128)(2,1)S(1)}, u32[]{:S(2)}) copy-start(bf16[2,64,512]{2,1,0:T(8,128)(2,1)S(1)} %collective-permute-done.refs_1_) | copy-start | bytes 393220
  20.1 3.7 %copy-start.11 = (bf16[2,64,512]{2,1,0:T(8,128)(2,1)S(1)}, bf16[2,64,512]{2,1,0:T(8,128)(2,1)}, u32[]{:S(2)}) copy-start(bf16[2,64,512]{2,1,0:T(8,128)(2,1)} %get-tuple-element.33.refs_0_) | copy-start | bytes 393220
  20.1 22.4 %collective-permute-start.3 = (bf16[2,512,512]{2,1,0:T(8,128)(2,1)S(1)}, bf16[2,512,512]{2,1,0:T(8,128)(2,1)}, u32[]{:S(2)}, u32[]{:S(2)}) collective-permute-start(bf16[2,512,512]{2,1,0:T(8,128)(2,1)S(1)} %after.4.refs_1_), channel_id=1, source_target_pairs={{0,4},{4,8},{8,12},{12,16},{16,20},{20,24},{24,28},{1,5},{5,9},{9,... | collective-permute-start | bytes 3145736 | tf_op jit(solution)/shard_map/ppermute | solution.py:518
  22.2 6.3 %collective-permute-start.7 = (bf16[2,64,512]{2,1,0:T(8,128)(2,1)S(1)}, bf16[2,64,512]{2,1,0:T(8,128)(2,1)S(1)}, u32[]{:S(2)}, u32[]{:S(2)}) collective-permute-start(bf16[2,64,512]{2,1,0:T(8,128)(2,1)S(1)} %collective-permute-done.2.refs_3_), channel_id=1, source_target_pairs={{0,4},{4,0},{8,12},{12,8},{16,20},{20,16},{24,28},{28,24},{1,5},{5... | collective-permute-start | bytes 393224 | tf_op jit(solution)/shard_map/ppermute | solution.py:445
  23.8 8.2 %collective-permute-start.4 = (bf16[2,64,512]{2,1,0:T(8,128)(2,1)S(1)}, bf16[2,64,512]{2,1,0:T(8,128)(2,1)S(1)}, u32[]{:S(2)}, u32[]{:S(2)}) collective-permute-start(bf16[2,64,512]{2,1,0:T(8,128)(2,1)S(1)} %copy-done.11), channel_id=1, source_target_pairs={{0,4},{4,0},{8,12},{12,8},{16,20},{20,16},{24,28},{28,24},{1,5},{5... | collective-permute-start | bytes 393224 | tf_op jit(solution)/shard_map/ppermute | solution.py:445
  23.9 8.1 %collective-permute-start.6 = (bf16[2,64,512]{2,1,0:T(8,128)(2,1)S(1)}, bf16[2,64,512]{2,1,0:T(8,128)(2,1)S(1)}, u32[]{:S(2)}, u32[]{:S(2)}) collective-permute-start(bf16[2,64,512]{2,1,0:T(8,128)(2,1)S(1)} %collective-permute-done.1.refs_2_), channel_id=1, source_target_pairs={{0,4},{4,0},{8,12},{12,8},{16,20},{20,16},{24,28},{28,24},{1,5},{5... | collective-permute-start | bytes 393224 | tf_op jit(solution)/shard_map/ppermute | solution.py:445
  24.3 7.7 %collective-permute-start.5 = (bf16[2,64,512]{2,1,0:T(8,128)(2,1)S(1)}, bf16[2,64,512]{2,1,0:T(8,128)(2,1)}, u32[]{:S(2)}, u32[]{:S(2)}) collective-permute-start(bf16[2,64,512]{2,1,0:T(8,128)(2,1)S(1)} %collective-permute-done.refs_1_), channel_id=1, source_target_pairs={{0,4},{4,0},{8,12},{12,8},{16,20},{20,16},{24,28},{28,24},{1,5},{5... | collective-permute-start | bytes 393224 | tf_op jit(solution)/shard_map/ppermute | solution.py:445
  24.4 28.8 %all-to-all-start = ((bf16[8,3,2,64,256]{4,3,2,1,0:T(8,128)(2,1)}), bf16[8,3,2,64,256]{4,3,2,1,0:T(8,128)(2,1)S(1)}, u32[]{:S(2)}, u32[]{:S(2)}) async-start(bf16[8,3,2,64,256]{4,3,2,1,0:T(8,128)(2,1)} %after.5), calls=%async_computation | async-start | bytes 3145728 | tf_op jit(solution)/shard_map/all_to_all | solution.py:544
  28.5 0.6 copy-start.10
  32.0 10.5 %copy-start.12 = (bf16[2,64,512]{2,1,0:T(8,128)(2,1)}, bf16[2,64,512]{2,1,0:T(8,128)(2,1)S(1)}, u32[]{:S(2)}) copy-start(bf16[2,64,512]{2,1,0:T(8,128)(2,1)S(1)} %collective-permute-done.4.refs_4_) | copy-start | bytes 393220
  32.0 10.5 %copy-start.13 = (bf16[2,64,512]{2,1,0:T(8,128)(2,1)}, bf16[2,64,512]{2,1,0:T(8,128)(2,1)S(1)}, u32[]{:S(2)}) copy-start(bf16[2,64,512]{2,1,0:T(8,128)(2,1)S(1)} %collective-permute-done.6.refs_6_) | copy-start | bytes 393220
  49.6 0.7 copy-start.5
  53.2 25.9 %all-to-all-start.1 = ((bf16[8,3,2,64,256]{4,3,2,1,0:T(8,128)(2,1)}), bf16[8,3,2,64,256]{4,3,2,1,0:T(8,128)(2,1)S(1)}, u32[]{:S(2)}, u32[]{:S(2)}) async-start(bf16[8,3,2,64,256]{4,3,2,1,0:T(8,128)(2,1)} %after.6), calls=%async_computation.1 | async-start | bytes 3145728 | tf_op jit(solution)/shard_map/all_to_all | solution.py:544
  59.2 3.7 %copy-start.9 = (f32[8,128]{1,0:T(8,128)}, f32[8,128]{1,0:T(8,128)S(1)}, u32[]{:S(2)}) copy-start(f32[8,128]{1,0:T(8,128)S(1)} %get-tuple-element.34.refs_8_) | copy-start | bytes 12292
  59.2 10.8 %collective-permute-start.8 = (bf16[2,64,256]{2,1,0:T(8,128)(2,1)S(1)}, bf16[2,64,256]{2,1,0:T(8,128)(2,1)S(1)}, u32[]{:S(2)}, u32[]{:S(2)}) collective-permute-start(bf16[2,64,256]{2,1,0:T(8,128)(2,1)S(1)} %get-tuple-element.41), channel_id=1, source_target_pairs={{0,4},{4,0},{8,12},{12,8},{16,20},{20,16},{24,28},{28,24},{1,5},{5... | collective-permute-start | bytes 196616 | tf_op jit(solution)/shard_map/ppermute | solution.py:502
  59.4 18.1 %collective-permute-start.9 = (bf16[2,64,256]{2,1,0:T(8,128)(2,1)S(1)}, bf16[2,64,256]{2,1,0:T(8,128)(2,1)S(1)}, u32[]{:S(2)}, u32[]{:S(2)}) collective-permute-start(bf16[2,64,256]{2,1,0:T(8,128)(2,1)S(1)} %get-tuple-element.42), channel_id=1, source_target_pairs={{0,8},{4,12},{8,0},{12,4},{16,24},{20,28},{24,16},{28,20},{1,9},{5... | collective-permute-start | bytes 196616 | tf_op jit(solution)/shard_map/ppermute | solution.py:502
  59.8 26.8 %collective-permute-start.10 = (bf16[2,64,256]{2,1,0:T(8,128)(2,1)S(1)}, bf16[2,64,256]{2,1,0:T(8,128)(2,1)S(1)}, u32[]{:S(2)}, u32[]{:S(2)}) collective-permute-start(bf16[2,64,256]{2,1,0:T(8,128)(2,1)S(1)} %get-tuple-element.43), channel_id=1, source_target_pairs={{0,12},{4,8},{8,4},{12,0},{16,28},{20,24},{24,20},{28,16},{1,13},{... | collective-permute-start | bytes 196616 | tf_op jit(solution)/shard_map/ppermute | solution.py:502
  61.1 25.4 %collective-permute-start.11 = (bf16[2,64,256]{2,1,0:T(8,128)(2,1)S(1)}, bf16[2,64,256]{2,1,0:T(8,128)(2,1)S(1)}, u32[]{:S(2)}, u32[]{:S(2)}) collective-permute-start(bf16[2,64,256]{2,1,0:T(8,128)(2,1)S(1)} %get-tuple-element.44), channel_id=1, source_target_pairs={{0,16},{4,20},{8,24},{12,28},{16,0},{20,4},{24,8},{28,12},{1,17},{... | collective-permute-start | bytes 196616 | tf_op jit(solution)/shard_map/ppermute | solution.py:502
  62.6 24.0 %collective-permute-start.12 = (bf16[2,64,256]{2,1,0:T(8,128)(2,1)S(1)}, bf16[2,64,256]{2,1,0:T(8,128)(2,1)S(1)}, u32[]{:S(2)}, u32[]{:S(2)}) collective-permute-start(bf16[2,64,256]{2,1,0:T(8,128)(2,1)S(1)} %get-tuple-element.45), channel_id=1, source_target_pairs={{0,20},{4,16},{8,28},{12,24},{16,4},{20,0},{24,12},{28,8},{1,21},{... | collective-permute-start | bytes 196616 | tf_op jit(solution)/shard_map/ppermute | solution.py:502
  70.0 16.6 %collective-permute-start.13 = (bf16[2,64,256]{2,1,0:T(8,128)(2,1)S(1)}, bf16[2,64,256]{2,1,0:T(8,128)(2,1)S(1)}, u32[]{:S(2)}, u32[]{:S(2)}) collective-permute-start(bf16[2,64,256]{2,1,0:T(8,128)(2,1)S(1)} %get-tuple-element.46), channel_id=1, source_target_pairs={{0,24},{4,28},{8,16},{12,20},{16,8},{20,12},{24,0},{28,4},{1,25},{... | collective-permute-start | bytes 196616 | tf_op jit(solution)/shard_map/ppermute | solution.py:502
  77.5 9.1 %collective-permute-start.14 = (bf16[2,64,256]{2,1,0:T(8,128)(2,1)S(1)}, bf16[2,64,256]{2,1,0:T(8,128)(2,1)S(1)}, u32[]{:S(2)}, u32[]{:S(2)}) collective-permute-start(bf16[2,64,256]{2,1,0:T(8,128)(2,1)S(1)} %get-tuple-element.47), channel_id=1, source_target_pairs={{0,28},{4,24},{8,20},{12,16},{16,12},{20,8},{24,4},{28,0},{1,29},{... | collective-permute-start | bytes 196616 | tf_op jit(solution)/shard_map/ppermute | solution.py:502
  79.2 0.7 copy-start.8
  82.3 16.0 %all-to-all-start.2 = ((bf16[8,2,64,256]{3,2,1,0:T(8,128)(2,1)}), bf16[8,2,64,256]{3,2,1,0:T(8,128)(2,1)S(1)}, u32[]{:S(2)}, u32[]{:S(2)}) async-start(bf16[8,2,64,256]{3,2,1,0:T(8,128)(2,1)} %get-tuple-element.38), calls=%async_computation.2 | async-start | bytes 1048576 | tf_op jit(solution)/shard_map/all_to_all | solution.py:550
  86.6 1.2 copy-start.7
  87.8 10.4 %copy-start.6 = (f32[1024,256]{1,0:T(8,128)S(1)}, f32[1024,256]{1,0:T(8,128)}, u32[]{:S(2)}) copy-start(f32[1024,256]{1,0:T(8,128)} %get-tuple-element.35.home_ref) | copy-start | bytes 3145732
  88.2 6.9 %collective-permute-start.15 = (bf16[256,256]{1,0:T(8,128)(2,1)S(1)}, bf16[256,256]{1,0:T(8,128)(2,1)S(1)}, u32[]{:S(2)}, u32[]{:S(2)}) collective-permute-start(bf16[256,256]{1,0:T(8,128)(2,1)S(1)} %get-tuple-element.50), channel_id=1, source_target_pairs={{0,1},{1,0},{2,3},{3,2},{4,5},{5,4},{6,7},{7,6},{8,9},{9,8},{10,11... | collective-permute-start | bytes 393224 | tf_op jit(solution)/shard_map/ppermute | solution.py:502
  88.7 9.6 %collective-permute-start.16 = (bf16[256,256]{1,0:T(8,128)(2,1)S(1)}, bf16[256,256]{1,0:T(8,128)(2,1)S(1)}, u32[]{:S(2)}, u32[]{:S(2)}) collective-permute-start(bf16[256,256]{1,0:T(8,128)(2,1)S(1)} %get-tuple-element.51), channel_id=1, source_target_pairs={{0,2},{1,3},{2,0},{3,1},{4,6},{5,7},{6,4},{7,5},{8,10},{9,11},{10,... | collective-permute-start | bytes 393224 | tf_op jit(solution)/shard_map/ppermute | solution.py:502
  98.7 9.3 %collective-permute-start.20 = (bf16[4,512,1024]{2,1,0:T(8,128)(2,1)}, bf16[4,512,1024]{2,1,0:T(8,128)(2,1)S(1)}, u32[]{:S(2)}, u32[]{:S(2)}) collective-permute-start(bf16[4,512,1024]{2,1,0:T(8,128)(2,1)} %after.7.refs_4_), channel_id=1, source_target_pairs={{0,4},{4,0},{8,12},{12,8},{16,20},{20,16},{24,28},{28,24},{1,5},{5... | collective-permute-start | bytes 12582920 | tf_op jit(solution)/shard_map/ppermute | solution.py:562
  98.7 9.2 %collective-permute-start.21 = (bf16[256,256]{1,0:T(8,128)(2,1)S(1)}, bf16[256,256]{1,0:T(8,128)(2,1)S(1)}, u32[]{:S(2)}, u32[]{:S(2)}) collective-permute-start(bf16[256,256]{1,0:T(8,128)(2,1)S(1)} %get-tuple-element.58), channel_id=1, source_target_pairs={{0,3},{1,2},{2,1},{3,0},{4,7},{5,6},{6,5},{7,4},{8,11},{9,10},{10,... | collective-permute-start | bytes 393224 | tf_op jit(solution)/shard_map/ppermute | solution.py:502
  99.3 12.1 %collective-permute-start.17 = (bf16[256,256]{1,0:T(8,128)(2,1)S(1)}, bf16[256,256]{1,0:T(8,128)(2,1)S(1)}, u32[]{:S(2)}, u32[]{:S(2)}) collective-permute-start(bf16[256,256]{1,0:T(8,128)(2,1)S(1)} %get-tuple-element.53), channel_id=1, source_target_pairs={{0,1},{1,0},{2,3},{3,2},{4,5},{5,4},{6,7},{7,6},{8,9},{9,8},{10,11... | collective-permute-start | bytes 393224 | tf_op jit(solution)/shard_map/ppermute | solution.py:502
  102.9 9.9 %collective-permute-start.18 = (bf16[256,256]{1,0:T(8,128)(2,1)S(1)}, bf16[256,256]{1,0:T(8,128)(2,1)S(1)}, u32[]{:S(2)}, u32[]{:S(2)}) collective-permute-start(bf16[256,256]{1,0:T(8,128)(2,1)S(1)} %get-tuple-element.54), channel_id=1, source_target_pairs={{0,2},{1,3},{2,0},{3,1},{4,6},{5,7},{6,4},{7,5},{8,10},{9,11},{10,... | collective-permute-start | bytes 393224 | tf_op jit(solution)/shard_map/ppermute | solution.py:502
  102.9 15.8 %collective-permute-start.19 = (bf16[256,256]{1,0:T(8,128)(2,1)S(1)}, bf16[256,256]{1,0:T(8,128)(2,1)S(1)}, u32[]{:S(2)}, u32[]{:S(2)}) collective-permute-start(bf16[256,256]{1,0:T(8,128)(2,1)S(1)} %get-tuple-element.55), channel_id=1, source_target_pairs={{0,3},{1,2},{2,1},{3,0},{4,7},{5,6},{6,5},{7,4},{8,11},{9,10},{10,... | collective-permute-start | bytes 393224 | tf_op jit(solution)/shard_map/ppermute | solution.py:502
  107.9 2.2 %copy-start = (bf16[4,512,1024]{2,1,0:T(8,128)(2,1)S(1)}, bf16[4,512,1024]{2,1,0:T(8,128)(2,1)}, u32[]{:S(2)}) copy-start(bf16[4,512,1024]{2,1,0:T(8,128)(2,1)} %after.7.refs_4_) | copy-start | bytes 12582916
Sparse Core Ops, SparseCore 0:
  8.9 79.4 all-gather.2

commit v17 on v16

--- a/solution.py
+++ b/solution.py
@@ -357,9 +357,9 @@
     )(place, moved, *waits)
 
 
-def combine_kernel(home_ref, *refs, slots, arrays, ctx):
+def combine_kernel(home_ref, *refs, slots, arrays, ctx, slabs):
     seat, place = lax.axis_index("head"), lax.axis_index("ctx")
-    back_refs, o_refs = refs[:arrays], refs[-slots - 1 : -1]
+    back_refs, o_refs = refs[:arrays], refs[-1 - (slots if slabs else 1) : -1]
     tokens_dev, width = home_ref.shape
     size = tokens_dev // slots
     per = STRIDE // ctx
@@ -369,7 +369,7 @@
     owner = group // per if arrays == 1 else partner(place, group // per, ctx)
     matrix = (token == (col & 15) * 16 + owner * per + group % per).astype(BF16)
     for slot in range(slots):
-        owner = partner(seat, slot, slots)
+        owner = partner(seat, slot, slots) if slabs else slot
         for b in range(size // TILE):
             first = owner * (size // TILE) + b
             here = pl.ds(pl.multiple_of(first * STRIDE, STRIDE), STRIDE)
@@ -379,29 +379,36 @@
                 rows = jnp.concatenate([ref[r, here] for ref in back_refs for r in range(per)])
             back = dot(matrix, rows)
             home = home_ref[pl.ds(pl.multiple_of(first * TILE, TILE), TILE)]
-            o_refs[slot][b * TILE : (b + 1) * TILE] = (home + back).astype(BF16)
-
-
-def combine(home, backs, slots, ctx, waits):
+            o_ref = o_refs[slot] if slabs else o_refs[0].at[slot]
+            o_ref[b * TILE : (b + 1) * TILE] = (home + back).astype(BF16)
+
+
+def combine(home, backs, slots, ctx, slabs, waits):
     tokens_dev, width = home.shape
     size = tokens_dev // slots
-    return pl.pallas_call(
-        functools.partial(combine_kernel, slots=slots, arrays=len(backs), ctx=ctx),
+    if slabs:
+        out_shape = [jax.ShapeDtypeStruct((size, width), BF16)] * slots
+    else:
+        out_shape = [jax.ShapeDtypeStruct((slots, size, width), BF16)]
+    return pl.pallas_call(
+        functools.partial(
+            combine_kernel, slots=slots, arrays=len(backs), ctx=ctx, slabs=slabs
+        ),
         in_specs=[pl.BlockSpec(memory_space=pltpu.VMEM)] * (1 + len(backs))
         + moments(waits),
-        out_specs=[pl.BlockSpec(memory_space=pltpu.VMEM)] * slots + [mark_spec()],
-        out_shape=[jax.ShapeDtypeStruct((size, width), BF16)] * slots + [MARK],
+        out_specs=[pl.BlockSpec(memory_space=pltpu.VMEM)] * len(out_shape) + [mark_spec()],
+        out_shape=out_shape + [MARK],
         compiler_params=params(24),
         cost_estimate=cost(56 * tokens_dev * TILE * width, 8 * tokens_dev * width),
         name="combine",
     )(home, *backs, *waits)
 
 
-def project_kernel(*refs, slots, chunk, adds):
+def project_kernel(*refs, slots, arrays, chunk, adds):
     side, seat = lax.axis_index("ctx") % 2, lax.axis_index("head")
-    moved_refs, weight_refs, refs = refs[:slots], refs[slots : slots + 2], refs[slots + 2 :]
+    moved_refs, weight_refs, refs = refs[:arrays], refs[arrays : arrays + 2], refs[arrays + 2 :]
     o_ref = refs[-1]
-    part = moved_refs[0].shape[1]
+    part = moved_refs[0].shape[-1]
     half = weight_refs[0].shape[2]
     tile = min(half, 512)
     for phase, weight_ref in enumerate(weight_refs):
@@ -411,23 +418,25 @@
             total = refs[0][:, here] if adds else None
             for slot in range(slots):
                 rows = weight_ref[
-                    partner(seat, slot, slots),
+                    slot if arrays == 1 else partner(seat, slot, slots),
                     chunk * part : (chunk + 1) * part,
                     j * tile : (j + 1) * tile,
                 ]
-                product = dot(moved_refs[slot][...], rows)
+                moved = moved_refs[0][slot] if arrays == 1 else moved_refs[slot][...]
+                product = dot(moved, rows)
                 total = product if total is None else total + product
             o_ref[:, here] = total.astype(o_ref.dtype)
 
 
 def project(moved, mine, other, chunk, before, dtype):
-    slots = len(moved)
-    tokens, part = moved[0].shape
-    half = mine.shape[2]
+    slots, _, half = mine.shape
+    tokens, part = moved[0].shape[-2:]
     whole = pl.BlockSpec(memory_space=pltpu.VMEM)
     return pl.pallas_call(
-        functools.partial(project_kernel, slots=slots, chunk=chunk, adds=len(before) > 0),
-        in_specs=[whole] * (slots + 2 + len(before)),
+        functools.partial(
+            project_kernel, slots=slots, arrays=len(moved), chunk=chunk, adds=len(before) > 0
+        ),
+        in_specs=[whole] * (len(moved) + 2 + len(before)),
         out_specs=whole,
         out_shape=jax.ShapeDtypeStruct((tokens, 2 * half), dtype),
         compiler_params=params(24),
@@ -555,8 +564,13 @@
                 homes.append(sections)
                 waits = (mark,)
         for chunk in range(chunks):
-            *slabs, mark = combine(homes[chunk], backs[chunk], groups, ctx, waits)
-            moved.append(exchange(slabs, "head"))
+            beside = chunk < chunks - 1
+            *slabs, mark = combine(homes[chunk], backs[chunk], groups, ctx, beside, waits)
+            if beside:
+                moved.append(exchange(slabs, "head"))
+            else:
+                rows = lax.all_to_all(slabs[0], "head", split_axis=0, concat_axis=0, tiled=True)
+                moved.append([rows])
             waits = (mark, *moved[-1][1:3])
     (held,) = after([mine], (mark,))
     other = lax.ppermute(held, "ctx", sibling)

time: 128 us -> 145 us (1.13)
  waiting for transfers between devices: 40.2 us -> 46.9 us
  Pallas kernels: 32.4 us -> 37.6 us
  local copies, waits for them, and re-layouts: 5.43 us -> 8.83 us
    ppermute x13 -> x10, waiting for transfers between devices: 23.7 us -> 30.5 us  [exchange(): moved.append(lax.ppermute(slabs[slot], axis, pairs))]
    all_to_all x0 -> x1, starting transfers between devices: none -> 5.32 us  [body(): lax.all_to_all(slabs[0], 'head', split_axis=0, concat_axis=0, tiled=True)]
    pallas_call x2, Pallas kernels: 3.47 us -> 7.84 us  [project(): pl.pallas_call(functools.partial(project_kernel, slots=slots, arrays=len(...]
    ppermute x13 -> x10, starting transfers between devices: 15.7 us -> 11.6 us  [exchange(): moved.append(lax.ppermute(slabs[slot], axis, pairs))]
    unnamed x28 -> x30, local copies, waits for them, and re-layouts: 5.43 us -> 8.83 us
  transfers between devices with their start and end apart: 26 -> 24, of which waited for: 11 -> 9; matrix products, arithmetic and copies ran while one was open for 0% -> 0% of each run, Pallas kernels for 22% -> 22%
where the time goes in v17:
time: 145 us; the launch traced here: 144 us
  waiting for transfers between devices  46.9 us (32%)
  Pallas kernels  37.6 us (26%)
  starting transfers between devices  37.3 us (26%)
  between operations  13.6 us (9%)
  local copies, waits for them, and re-layouts  8.83 us (6%)
    ppermute x10, waiting for transfers between devices, exchange(): moved.append(lax.ppermute(slabs[slot], axis, pairs))  30.5 us
    pallas_call x2, Pallas kernels, home_sections(): pl.pallas_call(functools.partial(home_kernel, order=order), grid=(heads,)...  14.2 us
    ppermute x10, starting transfers between devices, exchange(): moved.append(lax.ppermute(slabs[slot], axis, pairs))  11.6 us
    ppermute x1, waiting for transfers between devices, body(): before = lax.ppermute(rim, 'ctx', [(i, i + 1) for i in range(ctx - 1)])  10.5 us
    unnamed x30, local copies, waits for them, and re-layouts  8.83 us
    all_to_all x2, starting transfers between devices, body(): lax.all_to_all(send, 'ctx', split_axis=0, concat_axis=0, tiled=True)  8.32 us
    pallas_call x2, Pallas kernels, project(): pl.pallas_call(functools.partial(project_kernel, slots=slots, arrays=len(...  7.84 us
    ppermute x7, starting transfers between devices, swapped(): return lax.ppermute(piece, 'ctx', [(i, i ^ distance) for i in range(count)])  5.73 us
  transfers between devices with their start and end apart: 24, of which 9 were waited for; matrix products, arithmetic and copies ran while one was open for 0% of the time, Pallas kernels for 22%

profile of v17, /device:TPU:10, one launch (start us, length us, event | category | flops | bytes accessed | tf_op | source)
XLA Modules:
  0.0 144.2 jit_solution(4834407101232257901)
XLA Ops:
  6.5 2.0 %cut.1.refs_0_ = bf16[512,1024]{1,0:T(8,128)(2,1)} custom-call(bf16[512,2048]{1,0:T(8,128)(2,1)} %weight_ref.1), custom_call_target="tpu_custom_call" | custom-call | bytes 2097152 | tf_op jit(solution)/shard_map/cut/pallas_call | solution.py:182
  8.5 2.2 %edges.1 = (bf16[2,512,512]{2,1,0:T(8,128)(2,1)}, bf16[2,64,512]{2,1,0:T(8,128)(2,1)}) custom-call(bf16[1024,512]{1,0:T(8,128)(2,1)} %k_ref.9, bf16[1024,512]{1,0:T(8,128)(2,1)} %v_ref.9, bf16[8,128,512]{2,1,0:T(8,128)(2,1)} %bitcast.5, bf16[8,128,512]{2,1,0:T(8,128)(2,1)} %bitcast.6, bf16[512,1024]{1,0:T(8,128)(2,1)} %cut.1.refs_0_), custom_call_target="tpu_custom_call" | custom-call | bytes 2097152 | tf_op jit(solution)/shard_map/edges/pallas_call | solution.py:142
  10.8 1.6 %collective-permute-start.2 = (bf16[2,64,512]{2,1,0:T(8,128)(2,1)}, bf16[2,64,512]{2,1,0:T(8,128)(2,1)S(1)}, u32[]{:S(2)}, u32[]{:S(2)}) collective-permute-start(bf16[2,64,512]{2,1,0:T(8,128)(2,1)} %get-tuple-element.30.refs_0_), channel_id=1, source_target_pairs={{0,24},{4,28},{8,16},{12,20},{16,8},{20,12},{24,0},{28,4},{1,25},{... | collective-permute-start | bytes 393224 | tf_op jit(solution)/shard_map/ppermute | solution.py:454
  12.3 0.5 collective-permute-start.1
  12.8 1.5 %collective-permute-start = (bf16[2,64,512]{2,1,0:T(8,128)(2,1)}, bf16[2,64,512]{2,1,0:T(8,128)(2,1)S(1)}, u32[]{:S(2)}, u32[]{:S(2)}) collective-permute-start(bf16[2,64,512]{2,1,0:T(8,128)(2,1)} %get-tuple-element.30.refs_0_), channel_id=1, source_target_pairs={{0,8},{4,12},{8,0},{12,4},{16,24},{20,28},{24,16},{28,20},{1,9},{5... | collective-permute-start | bytes 393224 | tf_op jit(solution)/shard_map/ppermute | solution.py:454
  14.3 2.8 %prepare.2.refs_4_.refs_0_ = bf16[8,3,2,64,256]{4,3,2,1,0:T(8,128)(2,1)} custom-call(bf16[1024,512]{1,0:T(8,128)(2,1)} %q_ref.7, bf16[1024,512]{1,0:T(8,128)(2,1)} %k_ref.9, bf16[1024,512]{1,0:T(8,128)(2,1)} %v_ref.9, bf16[512,1024]{1,0:T(8,128)(2,1)} %cut.1.refs_0_), custom_call_target="tpu_custom_call" | custom-call | flops 402653184 | bytes 3145728 | tf_op jit(solution)/shard_map/prepare/pallas_call | solution.py:215
  17.1 1.2 collective-permute-done.2.refs_3_
  18.3 1.7 %collective-permute-done.1.refs_2_ = bf16[2,64,512]{2,1,0:T(8,128)(2,1)S(1)} collective-permute-done((bf16[2,64,512]{2,1,0:T(8,128)(2,1)}, bf16[2,64,512]{2,1,0:T(8,128)(2,1)S(1)}, u32[]{:S(2)}, u32[]{:S(2)}) %collective-permute-start.1) | collective-permute-done | bytes 131104 | tf_op jit(solution)/shard_map/ppermute | solution.py:454
  20.0 0.1 collective-permute-done.refs_1_
  20.1 2.1 %collective-permute-start.3 = (bf16[2,512,512]{2,1,0:T(8,128)(2,1)S(1)}, bf16[2,512,512]{2,1,0:T(8,128)(2,1)}, u32[]{:S(2)}, u32[]{:S(2)}) collective-permute-start(bf16[2,512,512]{2,1,0:T(8,128)(2,1)S(1)} %after.4.refs_1_), channel_id=1, source_target_pairs={{0,4},{4,8},{8,12},{12,16},{16,20},{20,24},{24,28},{1,5},{5,9},{9,... | collective-permute-start | bytes 3145736 | tf_op jit(solution)/shard_map/ppermute | solution.py:527
  22.2 1.6 %collective-permute-start.7 = (bf16[2,64,512]{2,1,0:T(8,128)(2,1)S(1)}, bf16[2,64,512]{2,1,0:T(8,128)(2,1)S(1)}, u32[]{:S(2)}, u32[]{:S(2)}) collective-permute-start(bf16[2,64,512]{2,1,0:T(8,128)(2,1)S(1)} %collective-permute-done.2.refs_3_), channel_id=1, source_target_pairs={{0,4},{4,0},{8,12},{12,8},{16,20},{20,16},{24,28},{28,24},{1,5},{5... | collective-permute-start | bytes 393224 | tf_op jit(solution)/shard_map/ppermute | solution.py:454
  23.9 0.4 collective-permute-start.6
  24.4 4.1 %all-to-all-start = ((bf16[8,3,2,64,256]{4,3,2,1,0:T(8,128)(2,1)}), bf16[8,3,2,64,256]{4,3,2,1,0:T(8,128)(2,1)S(1)}, u32[]{:S(2)}, u32[]{:S(2)}) async-start(bf16[8,3,2,64,256]{4,3,2,1,0:T(8,128)(2,1)} %after.5), calls=%async_computation | async-start | bytes 3145728 | tf_op jit(solution)/shard_map/all_to_all | solution.py:553
  28.5 0.6 copy-done.11
  29.1 2.8 %prepare.3.refs_0_ = bf16[8,3,2,64,256]{4,3,2,1,0:T(8,128)(2,1)} custom-call(bf16[1024,512]{1,0:T(8,128)(2,1)} %q_ref.7, bf16[1024,512]{1,0:T(8,128)(2,1)} %k_ref.9, bf16[1024,512]{1,0:T(8,128)(2,1)} %v_ref.9, bf16[2,64,512]{2,1,0:T(8,128)(2,1)} %copy-done.11), custom_call_target="tpu_custom_call" | custom-call | flops 402653184 | bytes 3145728 | tf_op jit(solution)/shard_map/prepare/pallas_call | solution.py:215
  32.0 10.5 %collective-permute-done.3.rim_ref = bf16[2,512,512]{2,1,0:T(8,128)(2,1)} collective-permute-done((bf16[2,512,512]{2,1,0:T(8,128)(2,1)S(1)}, bf16[2,512,512]{2,1,0:T(8,128)(2,1)}, u32[]{:S(2)}, u32[]{:S(2)}) %collective-permute-start.3) | collective-permute-done | bytes 1048608 | tf_op jit(solution)/shard_map/ppermute | solution.py:527
  42.5 7.1 %home.3 = (f32[1024,256]{1,0:T(8,128)}, f32[8,128]{1,0:T(8,128)}) custom-call(s32[1]{0:T(128)} %bitcast.place_ref, bf16[1024,512]{1,0:T(8,128)(2,1)} %q_ref.7, bf16[1024,512]{1,0:T(8,128)(2,1)} %k_ref.9, bf16[1024,512]{1,0:T(8,128)(2,1)} %v_ref.9, bf16[2,512,512]{2,1,0:T(8,128)(2,1)} %collective-permute-done.3.rim_ref, ...), custom_call_target="tpu_custom_call" | custom-call | flops 21474836480 | bytes 7340032 | tf_op jit(solution)/shard_map/home/pallas_call | solution.py:281
  49.6 0.7 copy-done.6
  50.3 2.9 %all-to-all-done.x_ref = bf16[8,3,2,64,256]{4,3,2,1,0:T(8,128)(2,1)S(1)} async-done(((bf16[8,3,2,64,256]{4,3,2,1,0:T(8,128)(2,1)}), bf16[8,3,2,64,256]{4,3,2,1,0:T(8,128)(2,1)S(1)}, u32[]{:S(2)}, u32[]{:S(2)}) %all-to-all-start) | async-done | bytes 1572896 | tf_op jit(solution)/shard_map/all_to_all | solution.py:553
  53.2 4.2 %all-to-all-start.1 = ((bf16[8,3,2,64,256]{4,3,2,1,0:T(8,128)(2,1)}), bf16[8,3,2,64,256]{4,3,2,1,0:T(8,128)(2,1)S(1)}, u32[]{:S(2)}, u32[]{:S(2)}) async-start(bf16[8,3,2,64,256]{4,3,2,1,0:T(8,128)(2,1)} %after.6), calls=%async_computation.1 | async-start | bytes 3145728 | tf_op jit(solution)/shard_map/all_to_all | solution.py:553
  57.4 1.8 %stride.2 = (bf16[2,64,256]{2,1,0:T(8,128)(2,1)S(1)}, bf16[2,64,256]{2,1,0:T(8,128)(2,1)S(1)}, bf16[2,64,256]{2,1,0:T(8,128)(2,1)S(1)}, bf16[2,64,256]{2,1,0:T(8...) custom-call(s32[1]{0:T(128)} %bitcast.place_ref, ...), custom_call_target="tpu_custom_call" | custom-call | flops 805306368 | bytes 2097152 | tf_op jit(solution)/shard_map/stride/pallas_call | solution.py:343
  59.2 0.2 collective-permute-start.8
  59.4 0.4 collective-permute-start.9
  59.8 1.4 collective-permute-start.10
  61.1 1.5 %collective-permute-start.11 = (bf16[2,64,256]{2,1,0:T(8,128)(2,1)S(1)}, bf16[2,64,256]{2,1,0:T(8,128)(2,1)S(1)}, u32[]{:S(2)}, u32[]{:S(2)}) collective-permute-start(bf16[2,64,256]{2,1,0:T(8,128)(2,1)S(1)} %get-tuple-element.41), channel_id=1, source_target_pairs={{0,16},{4,20},{8,24},{12,28},{16,0},{20,4},{24,8},{28,12},{1,17},{... | collective-permute-start | bytes 196616 | tf_op jit(solution)/shard_map/ppermute | solution.py:511
  62.6 0.3 collective-permute-start.12
  62.9 7.1 %home.2 = (f32[1024,256]{1,0:T(8,128)}, f32[8,128]{1,0:T(8,128)}) custom-call(s32[1]{0:T(128)} %bitcast.place_ref, bf16[1024,512]{1,0:T(8,128)(2,1)} %q_ref.7, bf16[1024,512]{1,0:T(8,128)(2,1)} %k_ref.9, bf16[1024,512]{1,0:T(8,128)(2,1)} %v_ref.9, bf16[2,512,512]{2,1,0:T(8,128)(2,1)} %collective-permute-done.3.rim_ref, ...), custom_call_target="tpu_custom_call" | custom-call | flops 21474836480 | bytes 7340032 | tf_op jit(solution)/shard_map/home/pallas_call | solution.py:281
  70.0 1.7 %collective-permute-start.13 = (bf16[2,64,256]{2,1,0:T(8,128)(2,1)S(1)}, bf16[2,64,256]{2,1,0:T(8,128)(2,1)S(1)}, u32[]{:S(2)}, u32[]{:S(2)}) collective-permute-start(bf16[2,64,256]{2,1,0:T(8,128)(2,1)S(1)} %get-tuple-element.43), channel_id=1, source_target_pairs={{0,24},{4,28},{8,16},{12,20},{16,8},{20,12},{24,0},{28,4},{1,25},{... | collective-permute-start | bytes 196616 | tf_op jit(solution)/shard_map/ppermute | solution.py:511
  71.7 5.8 %collective-permute-done.9.refs_2_ = bf16[2,64,256]{2,1,0:T(8,128)(2,1)S(1)} collective-permute-done((bf16[2,64,256]{2,1,0:T(8,128)(2,1)S(1)}, bf16[2,64,256]{2,1,0:T(8,128)(2,1)S(1)}, u32[]{:S(2)}, u32[]{:S(2)}) %collective-permute-start.9) | collective-permute-done | bytes 65568 | tf_op jit(solution)/shard_map/ppermute | solution.py:511
  77.5 1.6 %collective-permute-start.14 = (bf16[2,64,256]{2,1,0:T(8,128)(2,1)S(1)}, bf16[2,64,256]{2,1,0:T(8,128)(2,1)S(1)}, u32[]{:S(2)}, u32[]{:S(2)}) collective-permute-start(bf16[2,64,256]{2,1,0:T(8,128)(2,1)S(1)} %get-tuple-element.44), channel_id=1, source_target_pairs={{0,28},{4,24},{8,20},{12,16},{16,12},{20,8},{24,4},{28,0},{1,29},{... | collective-permute-start | bytes 196616 | tf_op jit(solution)/shard_map/ppermute | solution.py:511
  79.2 0.7 copy-done.9
  79.8 2.5 %stride.3 = (bf16[8,2,64,256]{3,2,1,0:T(8,128)(2,1)}, f32[8,128]{1,0:T(8,128)S(1)}) custom-call(s32[1]{0:T(128)} %bitcast.place_ref, bf16[8,3,2,64,256]{4,3,2,1,0:T(8,128)(2,1)S(1)} %all-to-all-done.1.x_ref, f32[8,128]{1,0:T(8,128)S(1)} %copy-done.9), custom_call_target="tpu_custom_call" | custom-call | flops 805306368 | bytes 2097152 | tf_op jit(solution)/shard_map/stride/pallas_call | solution.py:343
  82.3 4.2 %all-to-all-start.2 = ((bf16[8,2,64,256]{3,2,1,0:T(8,128)(2,1)}), bf16[8,2,64,256]{3,2,1,0:T(8,128)(2,1)S(1)}, u32[]{:S(2)}, u32[]{:S(2)}) async-start(bf16[8,2,64,256]{3,2,1,0:T(8,128)(2,1)} %get-tuple-element.35), calls=%async_computation.2 | async-start | bytes 1048576 | tf_op jit(solution)/shard_map/all_to_all | solution.py:559
  86.6 1.2 copy-done.8
  87.8 0.3 combine.2
  88.2 0.5 collective-permute-start.15
  88.7 2.6 %collective-permute-start.16 = (bf16[256,256]{1,0:T(8,128)(2,1)S(1)}, bf16[256,256]{1,0:T(8,128)(2,1)S(1)}, u32[]{:S(2)}, u32[]{:S(2)}) collective-permute-start(bf16[256,256]{1,0:T(8,128)(2,1)S(1)} %get-tuple-element.48), channel_id=1, source_target_pairs={{0,2},{1,3},{2,0},{3,1},{4,6},{5,7},{6,4},{7,5},{8,10},{9,11},{10,... | collective-permute-start | bytes 393224 | tf_op jit(solution)/shard_map/ppermute | solution.py:511
  91.3 3.6 %collective-permute-done.15.refs_2_.refs_1_ = bf16[256,256]{1,0:T(8,128)(2,1)S(1)} collective-permute-done((bf16[256,256]{1,0:T(8,128)(2,1)S(1)}, bf16[256,256]{1,0:T(8,128)(2,1)S(1)}, u32[]{:S(2)}, u32[]{:S(2)}) %collective-permute-start.15) | collective-permute-done | bytes 131104 | tf_op jit(solution)/shard_map/ppermute | solution.py:511
  94.9 3.2 %collective-permute-done.16.refs_3_.refs_2_ = bf16[256,256]{1,0:T(8,128)(2,1)S(1)} collective-permute-done((bf16[256,256]{1,0:T(8,128)(2,1)S(1)}, bf16[256,256]{1,0:T(8,128)(2,1)S(1)}, u32[]{:S(2)}, u32[]{:S(2)}) %collective-permute-start.16) | collective-permute-done | bytes 131104 | tf_op jit(solution)/shard_map/ppermute | solution.py:511
  98.1 1.2 copy-done.7
  99.3 1.1 combine.3
  100.5 5.3 %all-to-all-start.3 = ((bf16[4,256,256]{2,1,0:T(8,128)(2,1)}), bf16[4,256,256]{2,1,0:T(8,128)(2,1)S(1)}, u32[]{:S(2)}, u32[]{:S(2)}) async-start(bf16[4,256,256]{2,1,0:T(8,128)(2,1)} %get-tuple-element.49), calls=%async_computation.3 | async-start | bytes 1048576 | tf_op jit(solution)/shard_map/all_to_all | solution.py:572
  105.8 1.5 %collective-permute-start.18 = (bf16[256,256]{1,0:T(8,128)(2,1)S(1)}, bf16[256,256]{1,0:T(8,128)(2,1)S(1)}, u32[]{:S(2)}, u32[]{:S(2)}) collective-permute-start(bf16[256,256]{1,0:T(8,128)(2,1)S(1)} %get-tuple-element.52), channel_id=1, source_target_pairs={{0,3},{1,2},{2,1},{3,0},{4,7},{5,6},{6,5},{7,4},{8,11},{9,10},{10,... | collective-permute-start | bytes 393224 | tf_op jit(solution)/shard_map/ppermute | solution.py:511
  107.3 17.9 %collective-permute-done.18.refs_3_ = bf16[256,256]{1,0:T(8,128)(2,1)S(1)} collective-permute-done((bf16[256,256]{1,0:T(8,128)(2,1)S(1)}, bf16[256,256]{1,0:T(8,128)(2,1)S(1)}, u32[]{:S(2)}, u32[]{:S(2)}) %collective-permute-start.18) | collective-permute-done | bytes 131104 | tf_op jit(solution)/shard_map/ppermute | solution.py:511
  125.1 2.2 %copy-done = bf16[4,512,1024]{2,1,0:T(8,128)(2,1)S(1)} copy-done((bf16[4,512,1024]{2,1,0:T(8,128)(2,1)S(1)}, bf16[4,512,1024]{2,1,0:T(8,128)(2,1)}, u32[]{:S(2)}) %copy-start) | copy-done | bytes 4194328
  127.3 3.4 %project.2.refs_3_ = f32[256,2048]{1,0:T(8,128)S(1)} custom-call(bf16[256,256]{1,0:T(8,128)(2,1)S(1)} %get-tuple-element.51.refs_0_, bf16[256,256]{1,0:T(8,128)(2,1)S(1)} %collective-permute-done.15.refs_2_.refs_1_, bf16[256,256]{1,0:T(8,128)(2,1)S(1)} %collective-permute-done.16.refs_3_.refs_2_, bf16[256,256]{1,0:T(8,128)(2,1)S(1)} %collective-permute-done.18.refs_3_, ...), custom_call_target="tpu_custom_call" | custom-call | flops 1073741824 | bytes 4718592 | tf_op jit(solution)/shard_map/project/pallas_call | solution.py:435
  130.8 2.2 %copy-done.1 = bf16[4,512,1024]{2,1,0:T(8,128)(2,1)S(1)} copy-done((bf16[4,512,1024]{2,1,0:T(8,128)(2,1)S(1)}, bf16[4,512,1024]{2,1,0:T(8,128)(2,1)}, u32[]{:S(2)}) %copy-start.1) | copy-done | bytes 4194328
  132.9 4.4 %project.3 = bf16[256,2048]{1,0:T(8,128)(2,1)} custom-call(bf16[4,256,256]{2,1,0:T(8,128)(2,1)S(1)} %all-to-all-done.3.refs_0_, bf16[4,512,1024]{2,1,0:T(8,128)(2,1)S(1)} %copy-done.1, bf16[4,512,1024]{2,1,0:T(8,128)(2,1)} %collective-permute-done.17.refs_5_.refs_2_, f32[256,2048]{1,0:T(8,128)S(1)} %project.2.refs_3_), custom_call_target="tpu_custom_call" | custom-call | flops 1073741824 | bytes 4718592 | tf_op jit(solution)/shard_map/project/pallas_call | solution.py:435
  (47 shorter events, 0.3 us)
Async XLA Ops:
  6.5 93.9 %all-gather.3.cloned.1.call-start = ((), (), s32[]{:S(2)}) async-start(), calls=%async_computation.4 | async-start | bytes 5242880 | tf_op jit(solution)/shard_map/all_gather | solution.py:515
  10.8 9.3 %copy-start.2 = (bf16[2,512,512]{2,1,0:T(8,128)(2,1)S(1)}, bf16[2,512,512]{2,1,0:T(8,128)(2,1)}, u32[]{:S(2)}) copy-start(bf16[2,512,512]{2,1,0:T(8,128)(2,1)} %get-tuple-element.29.refs_0_) | copy-start | bytes 3145732
  10.8 7.6 %collective-permute-start.2 = (bf16[2,64,512]{2,1,0:T(8,128)(2,1)}, bf16[2,64,512]{2,1,0:T(8,128)(2,1)S(1)}, u32[]{:S(2)}, u32[]{:S(2)}) collective-permute-start(bf16[2,64,512]{2,1,0:T(8,128)(2,1)} %get-tuple-element.30.refs_0_), channel_id=1, source_target_pairs={{0,24},{4,28},{8,16},{12,20},{16,8},{20,12},{24,0},{28,4},{1,25},{... | collective-permute-start | bytes 393224 | tf_op jit(solution)/shard_map/ppermute | solution.py:454
  12.3 7.7 %collective-permute-start.1 = (bf16[2,64,512]{2,1,0:T(8,128)(2,1)}, bf16[2,64,512]{2,1,0:T(8,128)(2,1)S(1)}, u32[]{:S(2)}, u32[]{:S(2)}) collective-permute-start(bf16[2,64,512]{2,1,0:T(8,128)(2,1)} %get-tuple-element.30.refs_0_), channel_id=1, source_target_pairs={{0,16},{4,20},{8,24},{12,28},{16,0},{20,4},{24,8},{28,12},{1,17},{... | collective-permute-start | bytes 393224 | tf_op jit(solution)/shard_map/ppermute | solution.py:454
  12.8 7.3 %collective-permute-start = (bf16[2,64,512]{2,1,0:T(8,128)(2,1)}, bf16[2,64,512]{2,1,0:T(8,128)(2,1)S(1)}, u32[]{:S(2)}, u32[]{:S(2)}) collective-permute-start(bf16[2,64,512]{2,1,0:T(8,128)(2,1)} %get-tuple-element.30.refs_0_), channel_id=1, source_target_pairs={{0,8},{4,12},{8,0},{12,4},{16,24},{20,28},{24,16},{28,20},{1,9},{5... | collective-permute-start | bytes 393224 | tf_op jit(solution)/shard_map/ppermute | solution.py:454
  18.3 3.8 %copy-start.3 = (bf16[2,64,512]{2,1,0:T(8,128)(2,1)}, bf16[2,64,512]{2,1,0:T(8,128)(2,1)S(1)}, u32[]{:S(2)}) copy-start(bf16[2,64,512]{2,1,0:T(8,128)(2,1)S(1)} %collective-permute-done.2.refs_3_) | copy-start | bytes 393220
  20.0 3.9 %copy-start.4 = (bf16[2,64,512]{2,1,0:T(8,128)(2,1)}, bf16[2,64,512]{2,1,0:T(8,128)(2,1)S(1)}, u32[]{:S(2)}) copy-start(bf16[2,64,512]{2,1,0:T(8,128)(2,1)S(1)} %collective-permute-done.1.refs_2_) | copy-start | bytes 393220
  20.1 4.2 %copy-start.5 = (bf16[2,64,512]{2,1,0:T(8,128)(2,1)}, bf16[2,64,512]{2,1,0:T(8,128)(2,1)S(1)}, u32[]{:S(2)}) copy-start(bf16[2,64,512]{2,1,0:T(8,128)(2,1)S(1)} %collective-permute-done.refs_1_) | copy-start | bytes 393220
  20.1 3.7 %copy-start.12 = (bf16[2,64,512]{2,1,0:T(8,128)(2,1)S(1)}, bf16[2,64,512]{2,1,0:T(8,128)(2,1)}, u32[]{:S(2)}) copy-start(bf16[2,64,512]{2,1,0:T(8,128)(2,1)} %get-tuple-element.30.refs_0_) | copy-start | bytes 393220
  20.1 22.4 %collective-permute-start.3 = (bf16[2,512,512]{2,1,0:T(8,128)(2,1)S(1)}, bf16[2,512,512]{2,1,0:T(8,128)(2,1)}, u32[]{:S(2)}, u32[]{:S(2)}) collective-permute-start(bf16[2,512,512]{2,1,0:T(8,128)(2,1)S(1)} %after.4.refs_1_), channel_id=1, source_target_pairs={{0,4},{4,8},{8,12},{12,16},{16,20},{20,24},{24,28},{1,5},{5,9},{9,... | collective-permute-start | bytes 3145736 | tf_op jit(solution)/shard_map/ppermute | solution.py:527
  22.2 6.3 %collective-permute-start.7 = (bf16[2,64,512]{2,1,0:T(8,128)(2,1)S(1)}, bf16[2,64,512]{2,1,0:T(8,128)(2,1)S(1)}, u32[]{:S(2)}, u32[]{:S(2)}) collective-permute-start(bf16[2,64,512]{2,1,0:T(8,128)(2,1)S(1)} %collective-permute-done.2.refs_3_), channel_id=1, source_target_pairs={{0,4},{4,0},{8,12},{12,8},{16,20},{20,16},{24,28},{28,24},{1,5},{5... | collective-permute-start | bytes 393224 | tf_op jit(solution)/shard_map/ppermute | solution.py:454
  23.8 8.2 %collective-permute-start.4 = (bf16[2,64,512]{2,1,0:T(8,128)(2,1)S(1)}, bf16[2,64,512]{2,1,0:T(8,128)(2,1)S(1)}, u32[]{:S(2)}, u32[]{:S(2)}) collective-permute-start(bf16[2,64,512]{2,1,0:T(8,128)(2,1)S(1)} %copy-done.12), channel_id=1, source_target_pairs={{0,4},{4,0},{8,12},{12,8},{16,20},{20,16},{24,28},{28,24},{1,5},{5... | collective-permute-start | bytes 393224 | tf_op jit(solution)/shard_map/ppermute | solution.py:454
  23.9 8.1 %collective-permute-start.6 = (bf16[2,64,512]{2,1,0:T(8,128)(2,1)S(1)}, bf16[2,64,512]{2,1,0:T(8,128)(2,1)S(1)}, u32[]{:S(2)}, u32[]{:S(2)}) collective-permute-start(bf16[2,64,512]{2,1,0:T(8,128)(2,1)S(1)} %collective-permute-done.1.refs_2_), channel_id=1, source_target_pairs={{0,4},{4,0},{8,12},{12,8},{16,20},{20,16},{24,28},{28,24},{1,5},{5... | collective-permute-start | bytes 393224 | tf_op jit(solution)/shard_map/ppermute | solution.py:454
  24.3 7.7 %collective-permute-start.5 = (bf16[2,64,512]{2,1,0:T(8,128)(2,1)S(1)}, bf16[2,64,512]{2,1,0:T(8,128)(2,1)}, u32[]{:S(2)}, u32[]{:S(2)}) collective-permute-start(bf16[2,64,512]{2,1,0:T(8,128)(2,1)S(1)} %collective-permute-done.refs_1_), channel_id=1, source_target_pairs={{0,4},{4,0},{8,12},{12,8},{16,20},{20,16},{24,28},{28,24},{1,5},{5... | collective-permute-start | bytes 393224 | tf_op jit(solution)/shard_map/ppermute | solution.py:454
  24.4 28.8 %all-to-all-start = ((bf16[8,3,2,64,256]{4,3,2,1,0:T(8,128)(2,1)}), bf16[8,3,2,64,256]{4,3,2,1,0:T(8,128)(2,1)S(1)}, u32[]{:S(2)}, u32[]{:S(2)}) async-start(bf16[8,3,2,64,256]{4,3,2,1,0:T(8,128)(2,1)} %after.5), calls=%async_computation | async-start | bytes 3145728 | tf_op jit(solution)/shard_map/all_to_all | solution.py:553
  28.5 0.6 copy-start.11
  32.0 10.5 %copy-start.13 = (bf16[2,64,512]{2,1,0:T(8,128)(2,1)}, bf16[2,64,512]{2,1,0:T(8,128)(2,1)S(1)}, u32[]{:S(2)}) copy-start(bf16[2,64,512]{2,1,0:T(8,128)(2,1)S(1)} %collective-permute-done.4.refs_4_) | copy-start | bytes 393220
  32.0 10.5 %copy-start.14 = (bf16[2,64,512]{2,1,0:T(8,128)(2,1)}, bf16[2,64,512]{2,1,0:T(8,128)(2,1)S(1)}, u32[]{:S(2)}) copy-start(bf16[2,64,512]{2,1,0:T(8,128)(2,1)S(1)} %collective-permute-done.6.refs_6_) | copy-start | bytes 393220
  49.6 0.7 copy-start.6
  53.2 25.9 %all-to-all-start.1 = ((bf16[8,3,2,64,256]{4,3,2,1,0:T(8,128)(2,1)}), bf16[8,3,2,64,256]{4,3,2,1,0:T(8,128)(2,1)S(1)}, u32[]{:S(2)}, u32[]{:S(2)}) async-start(bf16[8,3,2,64,256]{4,3,2,1,0:T(8,128)(2,1)} %after.6), calls=%async_computation.1 | async-start | bytes 3145728 | tf_op jit(solution)/shard_map/all_to_all | solution.py:553
  59.2 3.7 %copy-start.10 = (f32[8,128]{1,0:T(8,128)}, f32[8,128]{1,0:T(8,128)S(1)}, u32[]{:S(2)}) copy-start(f32[8,128]{1,0:T(8,128)S(1)} %get-tuple-element.31.refs_8_) | copy-start | bytes 12292
  59.2 10.8 %collective-permute-start.8 = (bf16[2,64,256]{2,1,0:T(8,128)(2,1)S(1)}, bf16[2,64,256]{2,1,0:T(8,128)(2,1)S(1)}, u32[]{:S(2)}, u32[]{:S(2)}) collective-permute-start(bf16[2,64,256]{2,1,0:T(8,128)(2,1)S(1)} %get-tuple-element.38), channel_id=1, source_target_pairs={{0,4},{4,0},{8,12},{12,8},{16,20},{20,16},{24,28},{28,24},{1,5},{5... | collective-permute-start | bytes 196616 | tf_op jit(solution)/shard_map/ppermute | solution.py:511
  59.4 18.1 %collective-permute-start.9 = (bf16[2,64,256]{2,1,0:T(8,128)(2,1)S(1)}, bf16[2,64,256]{2,1,0:T(8,128)(2,1)S(1)}, u32[]{:S(2)}, u32[]{:S(2)}) collective-permute-start(bf16[2,64,256]{2,1,0:T(8,128)(2,1)S(1)} %get-tuple-element.39), channel_id=1, source_target_pairs={{0,8},{4,12},{8,0},{12,4},{16,24},{20,28},{24,16},{28,20},{1,9},{5... | collective-permute-start | bytes 196616 | tf_op jit(solution)/shard_map/ppermute | solution.py:511
  59.8 26.8 %collective-permute-start.10 = (bf16[2,64,256]{2,1,0:T(8,128)(2,1)S(1)}, bf16[2,64,256]{2,1,0:T(8,128)(2,1)S(1)}, u32[]{:S(2)}, u32[]{:S(2)}) collective-permute-start(bf16[2,64,256]{2,1,0:T(8,128)(2,1)S(1)} %get-tuple-element.40), channel_id=1, source_target_pairs={{0,12},{4,8},{8,4},{12,0},{16,28},{20,24},{24,20},{28,16},{1,13},{... | collective-permute-start | bytes 196616 | tf_op jit(solution)/shard_map/ppermute | solution.py:511
  61.1 25.4 %collective-permute-start.11 = (bf16[2,64,256]{2,1,0:T(8,128)(2,1)S(1)}, bf16[2,64,256]{2,1,0:T(8,128)(2,1)S(1)}, u32[]{:S(2)}, u32[]{:S(2)}) collective-permute-start(bf16[2,64,256]{2,1,0:T(8,128)(2,1)S(1)} %get-tuple-element.41), channel_id=1, source_target_pairs={{0,16},{4,20},{8,24},{12,28},{16,0},{20,4},{24,8},{28,12},{1,17},{... | collective-permute-start | bytes 196616 | tf_op jit(solution)/shard_map/ppermute | solution.py:511
  62.6 24.0 %collective-permute-start.12 = (bf16[2,64,256]{2,1,0:T(8,128)(2,1)S(1)}, bf16[2,64,256]{2,1,0:T(8,128)(2,1)S(1)}, u32[]{:S(2)}, u32[]{:S(2)}) collective-permute-start(bf16[2,64,256]{2,1,0:T(8,128)(2,1)S(1)} %get-tuple-element.42), channel_id=1, source_target_pairs={{0,20},{4,16},{8,28},{12,24},{16,4},{20,0},{24,12},{28,8},{1,21},{... | collective-permute-start | bytes 196616 | tf_op jit(solution)/shard_map/ppermute | solution.py:511
  70.0 16.6 %collective-permute-start.13 = (bf16[2,64,256]{2,1,0:T(8,128)(2,1)S(1)}, bf16[2,64,256]{2,1,0:T(8,128)(2,1)S(1)}, u32[]{:S(2)}, u32[]{:S(2)}) collective-permute-start(bf16[2,64,256]{2,1,0:T(8,128)(2,1)S(1)} %get-tuple-element.43), channel_id=1, source_target_pairs={{0,24},{4,28},{8,16},{12,20},{16,8},{20,12},{24,0},{28,4},{1,25},{... | collective-permute-start | bytes 196616 | tf_op jit(solution)/shard_map/ppermute | solution.py:511
  77.5 9.1 %collective-permute-start.14 = (bf16[2,64,256]{2,1,0:T(8,128)(2,1)S(1)}, bf16[2,64,256]{2,1,0:T(8,128)(2,1)S(1)}, u32[]{:S(2)}, u32[]{:S(2)}) collective-permute-start(bf16[2,64,256]{2,1,0:T(8,128)(2,1)S(1)} %get-tuple-element.44), channel_id=1, source_target_pairs={{0,28},{4,24},{8,20},{12,16},{16,12},{20,8},{24,4},{28,0},{1,29},{... | collective-permute-start | bytes 196616 | tf_op jit(solution)/shard_map/ppermute | solution.py:511
  79.2 0.7 copy-start.9
  82.3 15.8 %all-to-all-start.2 = ((bf16[8,2,64,256]{3,2,1,0:T(8,128)(2,1)}), bf16[8,2,64,256]{3,2,1,0:T(8,128)(2,1)S(1)}, u32[]{:S(2)}, u32[]{:S(2)}) async-start(bf16[8,2,64,256]{3,2,1,0:T(8,128)(2,1)} %get-tuple-element.35), calls=%async_computation.2 | async-start | bytes 1048576 | tf_op jit(solution)/shard_map/all_to_all | solution.py:559
  86.6 1.2 copy-start.8
  88.2 6.7 %collective-permute-start.15 = (bf16[256,256]{1,0:T(8,128)(2,1)S(1)}, bf16[256,256]{1,0:T(8,128)(2,1)S(1)}, u32[]{:S(2)}, u32[]{:S(2)}) collective-permute-start(bf16[256,256]{1,0:T(8,128)(2,1)S(1)} %get-tuple-element.47), channel_id=1, source_target_pairs={{0,1},{1,0},{2,3},{3,2},{4,5},{5,4},{6,7},{7,6},{8,9},{9,8},{10,11... | collective-permute-start | bytes 393224 | tf_op jit(solution)/shard_map/ppermute | solution.py:511
  88.7 9.4 %collective-permute-start.16 = (bf16[256,256]{1,0:T(8,128)(2,1)S(1)}, bf16[256,256]{1,0:T(8,128)(2,1)S(1)}, u32[]{:S(2)}, u32[]{:S(2)}) collective-permute-start(bf16[256,256]{1,0:T(8,128)(2,1)S(1)} %get-tuple-element.48), channel_id=1, source_target_pairs={{0,2},{1,3},{2,0},{3,1},{4,6},{5,7},{6,4},{7,5},{8,10},{9,11},{10,... | collective-permute-start | bytes 393224 | tf_op jit(solution)/shard_map/ppermute | solution.py:511
  98.1 1.2 copy-start.7
  100.5 24.6 %collective-permute-start.17 = (bf16[4,512,1024]{2,1,0:T(8,128)(2,1)}, bf16[4,512,1024]{2,1,0:T(8,128)(2,1)}, u32[]{:S(2)}, u32[]{:S(2)}) collective-permute-start(bf16[4,512,1024]{2,1,0:T(8,128)(2,1)} %after.7.refs_4_.refs_1_), channel_id=1, source_target_pairs={{0,4},{4,0},{8,12},{12,8},{16,20},{20,16},{24,28},{28,24},{1,5},{5... | collective-permute-start | bytes 12582920 | tf_op jit(solution)/shard_map/ppermute | solution.py:576
  100.5 30.3 %all-to-all-start.3 = ((bf16[4,256,256]{2,1,0:T(8,128)(2,1)}), bf16[4,256,256]{2,1,0:T(8,128)(2,1)S(1)}, u32[]{:S(2)}, u32[]{:S(2)}) async-start(bf16[4,256,256]{2,1,0:T(8,128)(2,1)} %get-tuple-element.49), calls=%async_computation.3 | async-start | bytes 1048576 | tf_op jit(solution)/shard_map/all_to_all | solution.py:572
  105.8 19.3 %collective-permute-start.18 = (bf16[256,256]{1,0:T(8,128)(2,1)S(1)}, bf16[256,256]{1,0:T(8,128)(2,1)S(1)}, u32[]{:S(2)}, u32[]{:S(2)}) collective-permute-start(bf16[256,256]{1,0:T(8,128)(2,1)S(1)} %get-tuple-element.52), channel_id=1, source_target_pairs={{0,3},{1,2},{2,1},{3,0},{4,7},{5,6},{6,5},{7,4},{8,11},{9,10},{10,... | collective-permute-start | bytes 393224 | tf_op jit(solution)/shard_map/ppermute | solution.py:511
  125.1 2.2 %copy-start = (bf16[4,512,1024]{2,1,0:T(8,128)(2,1)S(1)}, bf16[4,512,1024]{2,1,0:T(8,128)(2,1)}, u32[]{:S(2)}) copy-start(bf16[4,512,1024]{2,1,0:T(8,128)(2,1)} %after.7.refs_4_.refs_1_) | copy-start | bytes 12582916
  130.8 2.2 %copy-start.1 = (bf16[4,512,1024]{2,1,0:T(8,128)(2,1)S(1)}, bf16[4,512,1024]{2,1,0:T(8,128)(2,1)}, u32[]{:S(2)}) copy-start(bf16[4,512,1024]{2,1,0:T(8,128)(2,1)} %after.7.refs_4_.refs_1_) | copy-start | bytes 12582916
Sparse Core Ops, SparseCore 0:
  8.9 79.4 all-gather.2

commit v18 on v16

--- a/solution.py
+++ b/solution.py
@@ -135,16 +135,16 @@
 def edges(keys, values, waits):
     tokens_dev, width = keys.shape
     blocks = tokens_dev // BLOCK
-    first = (tokens_dev - WINDOW) // TILE
-    source = pl.BlockSpec((TILE, width), lambda i: (first + i, 0))
+    first = tokens_dev // WINDOW - 1
+    source = pl.BlockSpec((WINDOW, width), lambda i: (first, 0))
     ends = pl.BlockSpec((blocks, 16, width), lambda i: (0, BLOCK // 16 - 1, 0))
     shape = (2, blocks * SUMCOLS, width)
     return pl.pallas_call(
         edge_kernel,
-        grid=(WINDOW // TILE,),
+        grid=(1,),
         in_specs=[source] * 2 + [ends] * 2 + moments(waits),
         out_specs=[
-            pl.BlockSpec((2, TILE, width), lambda i: (0, i, 0)),
+            pl.BlockSpec((2, WINDOW, width), lambda i: (0, 0, 0)),
             pl.BlockSpec(shape, lambda i: (0, 0, 0)),
         ],
         out_shape=[

time: 128 us -> 128 us (level)
  no operation moved by 1% of the time
where the time goes in v18:
time: 128 us
  waiting for transfers between devices  40.2 us (31%)
  starting transfers between devices  36.1 us (28%)
  Pallas kernels  32.6 us (25%)
  between operations  13.6 us (11%)
  local copies, waits for them, and re-layouts  5.43 us (4%)
    ppermute x13, waiting for transfers between devices, exchange(): moved.append(lax.ppermute(slabs[slot], axis, pairs))  23.7 us
    ppermute x13, starting transfers between devices, exchange(): moved.append(lax.ppermute(slabs[slot], axis, pairs))  15.7 us
    pallas_call x2, Pallas kernels, home_sections(): pl.pallas_call(functools.partial(home_kernel, order=order), grid=(heads,)...  14.2 us
    ppermute x1, waiting for transfers between devices, body(): before = lax.ppermute(rim, 'ctx', [(i, i + 1) for i in range(ctx - 1)])  10.5 us
    all_to_all x2, starting transfers between devices, body(): lax.all_to_all(send, 'ctx', split_axis=0, concat_axis=0, tiled=True)  8.32 us
    ppermute x7, starting transfers between devices, swapped(): return lax.ppermute(piece, 'ctx', [(i, i ^ distance) for i in range(count)])  5.66 us
    pallas_call x2, Pallas kernels, prepare(): pl.pallas_call(prep_kernel, grid=(tokens_dev // size,), in_specs=[pl.Bloc...  5.63 us
    unnamed x28, local copies, waits for them, and re-layouts  5.43 us
  transfers between devices with their start and end apart: 26, of which 11 were waited for; matrix products, arithmetic and copies ran while one was open for 0% of the time, Pallas kernels for 22%

profile of v18, /device:TPU:10, one launch (start us, length us, event | category | flops | bytes accessed | tf_op | source)
XLA Modules:
  0.0 127.8 jit_solution(5441688680688216310)
XLA Ops:
  6.5 2.0 %cut.1.refs_0_ = bf16[512,1024]{1,0:T(8,128)(2,1)} custom-call(bf16[512,2048]{1,0:T(8,128)(2,1)} %weight_ref.1), custom_call_target="tpu_custom_call" | custom-call | bytes 2097152 | tf_op jit(solution)/shard_map/cut/pallas_call | solution.py:182
  8.5 2.4 %edges.1 = (bf16[2,512,512]{2,1,0:T(8,128)(2,1)}, bf16[2,64,512]{2,1,0:T(8,128)(2,1)}) custom-call(bf16[1024,512]{1,0:T(8,128)(2,1)} %k_ref.9, bf16[1024,512]{1,0:T(8,128)(2,1)} %v_ref.9, bf16[8,128,512]{2,1,0:T(8,128)(2,1)} %bitcast.5, bf16[8,128,512]{2,1,0:T(8,128)(2,1)} %bitcast.6, bf16[512,1024]{1,0:T(8,128)(2,1)} %cut.1.refs_0_), custom_call_target="tpu_custom_call" | custom-call | bytes 2097152 | tf_op jit(solution)/shard_map/edges/pallas_call | solution.py:142
  10.9 1.5 %collective-permute-start.2 = (bf16[2,64,512]{2,1,0:T(8,128)(2,1)}, bf16[2,64,512]{2,1,0:T(8,128)(2,1)S(1)}, u32[]{:S(2)}, u32[]{:S(2)}) collective-permute-start(bf16[2,64,512]{2,1,0:T(8,128)(2,1)} %get-tuple-element.33.refs_0_), channel_id=1, source_target_pairs={{0,24},{4,28},{8,16},{12,20},{16,8},{20,12},{24,0},{28,4},{1,25},{... | collective-permute-start | bytes 393224 | tf_op jit(solution)/shard_map/ppermute | solution.py:445
  12.4 0.5 collective-permute-start.1
  12.9 1.5 %collective-permute-start = (bf16[2,64,512]{2,1,0:T(8,128)(2,1)}, bf16[2,64,512]{2,1,0:T(8,128)(2,1)S(1)}, u32[]{:S(2)}, u32[]{:S(2)}) collective-permute-start(bf16[2,64,512]{2,1,0:T(8,128)(2,1)} %get-tuple-element.33.refs_0_), channel_id=1, source_target_pairs={{0,8},{4,12},{8,0},{12,4},{16,24},{20,28},{24,16},{28,20},{1,9},{5... | collective-permute-start | bytes 393224 | tf_op jit(solution)/shard_map/ppermute | solution.py:445
  14.4 2.8 %prepare.2.refs_4_.refs_0_ = bf16[8,3,2,64,256]{4,3,2,1,0:T(8,128)(2,1)} custom-call(bf16[1024,512]{1,0:T(8,128)(2,1)} %q_ref.7, bf16[1024,512]{1,0:T(8,128)(2,1)} %k_ref.9, bf16[1024,512]{1,0:T(8,128)(2,1)} %v_ref.9, bf16[512,1024]{1,0:T(8,128)(2,1)} %cut.1.refs_0_), custom_call_target="tpu_custom_call" | custom-call | flops 402653184 | bytes 3145728 | tf_op jit(solution)/shard_map/prepare/pallas_call | solution.py:215
  17.2 1.2 collective-permute-done.2.refs_3_
  18.4 1.7 %collective-permute-done.1.refs_2_ = bf16[2,64,512]{2,1,0:T(8,128)(2,1)S(1)} collective-permute-done((bf16[2,64,512]{2,1,0:T(8,128)(2,1)}, bf16[2,64,512]{2,1,0:T(8,128)(2,1)S(1)}, u32[]{:S(2)}, u32[]{:S(2)}) %collective-permute-start.1) | collective-permute-done | bytes 131104 | tf_op jit(solution)/shard_map/ppermute | solution.py:445
  20.2 2.1 %collective-permute-start.3 = (bf16[2,512,512]{2,1,0:T(8,128)(2,1)S(1)}, bf16[2,512,512]{2,1,0:T(8,128)(2,1)}, u32[]{:S(2)}, u32[]{:S(2)}) collective-permute-start(bf16[2,512,512]{2,1,0:T(8,128)(2,1)S(1)} %after.4.refs_1_), channel_id=1, source_target_pairs={{0,4},{4,8},{8,12},{12,16},{16,20},{20,24},{24,28},{1,5},{5,9},{9,... | collective-permute-start | bytes 3145736 | tf_op jit(solution)/shard_map/ppermute | solution.py:518
  22.3 1.6 %collective-permute-start.7 = (bf16[2,64,512]{2,1,0:T(8,128)(2,1)S(1)}, bf16[2,64,512]{2,1,0:T(8,128)(2,1)S(1)}, u32[]{:S(2)}, u32[]{:S(2)}) collective-permute-start(bf16[2,64,512]{2,1,0:T(8,128)(2,1)S(1)} %collective-permute-done.2.refs_3_), channel_id=1, source_target_pairs={{0,4},{4,0},{8,12},{12,8},{16,20},{20,16},{24,28},{28,24},{1,5},{5... | collective-permute-start | bytes 393224 | tf_op jit(solution)/shard_map/ppermute | solution.py:445
  23.9 0.4 collective-permute-start.6
  24.5 4.1 %all-to-all-start = ((bf16[8,3,2,64,256]{4,3,2,1,0:T(8,128)(2,1)}), bf16[8,3,2,64,256]{4,3,2,1,0:T(8,128)(2,1)S(1)}, u32[]{:S(2)}, u32[]{:S(2)}) async-start(bf16[8,3,2,64,256]{4,3,2,1,0:T(8,128)(2,1)} %after.5), calls=%async_computation | async-start | bytes 3145728 | tf_op jit(solution)/shard_map/all_to_all | solution.py:544
  28.6 0.6 copy-done.10
  29.2 2.8 %prepare.3.refs_0_ = bf16[8,3,2,64,256]{4,3,2,1,0:T(8,128)(2,1)} custom-call(bf16[1024,512]{1,0:T(8,128)(2,1)} %q_ref.7, bf16[1024,512]{1,0:T(8,128)(2,1)} %k_ref.9, bf16[1024,512]{1,0:T(8,128)(2,1)} %v_ref.9, bf16[2,64,512]{2,1,0:T(8,128)(2,1)} %copy-done.10), custom_call_target="tpu_custom_call" | custom-call | flops 402653184 | bytes 3145728 | tf_op jit(solution)/shard_map/prepare/pallas_call | solution.py:215
  32.1 10.5 %collective-permute-done.3.rim_ref = bf16[2,512,512]{2,1,0:T(8,128)(2,1)} collective-permute-done((bf16[2,512,512]{2,1,0:T(8,128)(2,1)S(1)}, bf16[2,512,512]{2,1,0:T(8,128)(2,1)}, u32[]{:S(2)}, u32[]{:S(2)}) %collective-permute-start.3) | collective-permute-done | bytes 1048608 | tf_op jit(solution)/shard_map/ppermute | solution.py:518
  42.6 7.1 %home.3 = (f32[1024,256]{1,0:T(8,128)}, f32[8,128]{1,0:T(8,128)}) custom-call(s32[1]{0:T(128)} %bitcast.place_ref, bf16[1024,512]{1,0:T(8,128)(2,1)} %q_ref.7, bf16[1024,512]{1,0:T(8,128)(2,1)} %k_ref.9, bf16[1024,512]{1,0:T(8,128)(2,1)} %v_ref.9, bf16[2,512,512]{2,1,0:T(8,128)(2,1)} %collective-permute-done.3.rim_ref, ...), custom_call_target="tpu_custom_call" | custom-call | flops 21474836480 | bytes 7340032 | tf_op jit(solution)/shard_map/home/pallas_call | solution.py:281
  49.7 0.7 copy-done.5
  50.4 2.9 %all-to-all-done.x_ref = bf16[8,3,2,64,256]{4,3,2,1,0:T(8,128)(2,1)S(1)} async-done(((bf16[8,3,2,64,256]{4,3,2,1,0:T(8,128)(2,1)}), bf16[8,3,2,64,256]{4,3,2,1,0:T(8,128)(2,1)S(1)}, u32[]{:S(2)}, u32[]{:S(2)}) %all-to-all-start) | async-done | bytes 1572896 | tf_op jit(solution)/shard_map/all_to_all | solution.py:544
  53.3 4.2 %all-to-all-start.1 = ((bf16[8,3,2,64,256]{4,3,2,1,0:T(8,128)(2,1)}), bf16[8,3,2,64,256]{4,3,2,1,0:T(8,128)(2,1)S(1)}, u32[]{:S(2)}, u32[]{:S(2)}) async-start(bf16[8,3,2,64,256]{4,3,2,1,0:T(8,128)(2,1)} %after.6), calls=%async_computation.1 | async-start | bytes 3145728 | tf_op jit(solution)/shard_map/all_to_all | solution.py:544
  57.5 1.8 %stride.2 = (bf16[2,64,256]{2,1,0:T(8,128)(2,1)S(1)}, bf16[2,64,256]{2,1,0:T(8,128)(2,1)S(1)}, bf16[2,64,256]{2,1,0:T(8,128)(2,1)S(1)}, bf16[2,64,256]{2,1,0:T(8...) custom-call(s32[1]{0:T(128)} %bitcast.place_ref, ...), custom_call_target="tpu_custom_call" | custom-call | flops 805306368 | bytes 2097152 | tf_op jit(solution)/shard_map/stride/pallas_call | solution.py:343
  59.3 0.2 collective-permute-start.8
  59.5 0.4 collective-permute-start.9
  59.9 1.4 %collective-permute-start.10 = (bf16[2,64,256]{2,1,0:T(8,128)(2,1)S(1)}, bf16[2,64,256]{2,1,0:T(8,128)(2,1)S(1)}, u32[]{:S(2)}, u32[]{:S(2)}) collective-permute-start(bf16[2,64,256]{2,1,0:T(8,128)(2,1)S(1)} %get-tuple-element.43), channel_id=1, source_target_pairs={{0,12},{4,8},{8,4},{12,0},{16,28},{20,24},{24,20},{28,16},{1,13},{... | collective-permute-start | bytes 196616 | tf_op jit(solution)/shard_map/ppermute | solution.py:502
  61.2 1.5 %collective-permute-start.11 = (bf16[2,64,256]{2,1,0:T(8,128)(2,1)S(1)}, bf16[2,64,256]{2,1,0:T(8,128)(2,1)S(1)}, u32[]{:S(2)}, u32[]{:S(2)}) collective-permute-start(bf16[2,64,256]{2,1,0:T(8,128)(2,1)S(1)} %get-tuple-element.44), channel_id=1, source_target_pairs={{0,16},{4,20},{8,24},{12,28},{16,0},{20,4},{24,8},{28,12},{1,17},{... | collective-permute-start | bytes 196616 | tf_op jit(solution)/shard_map/ppermute | solution.py:502
  62.7 0.3 collective-permute-start.12
  63.0 7.1 %home.2 = (f32[1024,256]{1,0:T(8,128)}, f32[8,128]{1,0:T(8,128)}) custom-call(s32[1]{0:T(128)} %bitcast.place_ref, bf16[1024,512]{1,0:T(8,128)(2,1)} %q_ref.7, bf16[1024,512]{1,0:T(8,128)(2,1)} %k_ref.9, bf16[1024,512]{1,0:T(8,128)(2,1)} %v_ref.9, bf16[2,512,512]{2,1,0:T(8,128)(2,1)} %collective-permute-done.3.rim_ref, ...), custom_call_target="tpu_custom_call" | custom-call | flops 21474836480 | bytes 7340032 | tf_op jit(solution)/shard_map/home/pallas_call | solution.py:281
  70.1 1.7 %collective-permute-start.13 = (bf16[2,64,256]{2,1,0:T(8,128)(2,1)S(1)}, bf16[2,64,256]{2,1,0:T(8,128)(2,1)S(1)}, u32[]{:S(2)}, u32[]{:S(2)}) collective-permute-start(bf16[2,64,256]{2,1,0:T(8,128)(2,1)S(1)} %get-tuple-element.46), channel_id=1, source_target_pairs={{0,24},{4,28},{8,16},{12,20},{16,8},{20,12},{24,0},{28,4},{1,25},{... | collective-permute-start | bytes 196616 | tf_op jit(solution)/shard_map/ppermute | solution.py:502
  71.8 5.8 %collective-permute-done.9.refs_2_ = bf16[2,64,256]{2,1,0:T(8,128)(2,1)S(1)} collective-permute-done((bf16[2,64,256]{2,1,0:T(8,128)(2,1)S(1)}, bf16[2,64,256]{2,1,0:T(8,128)(2,1)S(1)}, u32[]{:S(2)}, u32[]{:S(2)}) %collective-permute-start.9) | collective-permute-done | bytes 65568 | tf_op jit(solution)/shard_map/ppermute | solution.py:502
  77.6 1.6 %collective-permute-start.14 = (bf16[2,64,256]{2,1,0:T(8,128)(2,1)S(1)}, bf16[2,64,256]{2,1,0:T(8,128)(2,1)S(1)}, u32[]{:S(2)}, u32[]{:S(2)}) collective-permute-start(bf16[2,64,256]{2,1,0:T(8,128)(2,1)S(1)} %get-tuple-element.47), channel_id=1, source_target_pairs={{0,28},{4,24},{8,20},{12,16},{16,12},{20,8},{24,4},{28,0},{1,29},{... | collective-permute-start | bytes 196616 | tf_op jit(solution)/shard_map/ppermute | solution.py:502
  79.2 0.7 copy-done.8
  79.9 2.5 %stride.3 = (bf16[8,2,64,256]{3,2,1,0:T(8,128)(2,1)}, f32[8,128]{1,0:T(8,128)S(1)}) custom-call(s32[1]{0:T(128)} %bitcast.place_ref, bf16[8,3,2,64,256]{4,3,2,1,0:T(8,128)(2,1)S(1)} %all-to-all-done.1.x_ref, f32[8,128]{1,0:T(8,128)S(1)} %copy-done.8), custom_call_target="tpu_custom_call" | custom-call | flops 805306368 | bytes 2097152 | tf_op jit(solution)/shard_map/stride/pallas_call | solution.py:343
  82.4 4.2 %all-to-all-start.2 = ((bf16[8,2,64,256]{3,2,1,0:T(8,128)(2,1)}), bf16[8,2,64,256]{3,2,1,0:T(8,128)(2,1)S(1)}, u32[]{:S(2)}, u32[]{:S(2)}) async-start(bf16[8,2,64,256]{3,2,1,0:T(8,128)(2,1)} %get-tuple-element.38), calls=%async_computation.2 | async-start | bytes 1048576 | tf_op jit(solution)/shard_map/all_to_all | solution.py:550
  86.7 1.2 copy-done.7
  87.9 0.3 combine.2
  88.2 0.5 collective-permute-start.15
  88.8 2.6 %collective-permute-start.16 = (bf16[256,256]{1,0:T(8,128)(2,1)S(1)}, bf16[256,256]{1,0:T(8,128)(2,1)S(1)}, u32[]{:S(2)}, u32[]{:S(2)}) collective-permute-start(bf16[256,256]{1,0:T(8,128)(2,1)S(1)} %get-tuple-element.51), channel_id=1, source_target_pairs={{0,2},{1,3},{2,0},{3,1},{4,6},{5,7},{6,4},{7,5},{8,10},{9,11},{10,... | collective-permute-start | bytes 393224 | tf_op jit(solution)/shard_map/ppermute | solution.py:502
  91.3 3.8 %collective-permute-done.15.refs_2_.refs_1_ = bf16[256,256]{1,0:T(8,128)(2,1)S(1)} collective-permute-done((bf16[256,256]{1,0:T(8,128)(2,1)S(1)}, bf16[256,256]{1,0:T(8,128)(2,1)S(1)}, u32[]{:S(2)}, u32[]{:S(2)}) %collective-permute-start.15) | collective-permute-done | bytes 131104 | tf_op jit(solution)/shard_map/ppermute | solution.py:502
  95.1 3.2 %collective-permute-done.16.refs_3_.refs_2_ = bf16[256,256]{1,0:T(8,128)(2,1)S(1)} collective-permute-done((bf16[256,256]{1,0:T(8,128)(2,1)S(1)}, bf16[256,256]{1,0:T(8,128)(2,1)S(1)}, u32[]{:S(2)}, u32[]{:S(2)}) %collective-permute-start.16) | collective-permute-done | bytes 131104 | tf_op jit(solution)/shard_map/ppermute | solution.py:502
  98.4 0.3 combine.3
  98.8 0.5 collective-permute-start.21
  99.3 3.6 %collective-permute-start.17 = (bf16[256,256]{1,0:T(8,128)(2,1)S(1)}, bf16[256,256]{1,0:T(8,128)(2,1)S(1)}, u32[]{:S(2)}, u32[]{:S(2)}) collective-permute-start(bf16[256,256]{1,0:T(8,128)(2,1)S(1)} %get-tuple-element.53), channel_id=1, source_target_pairs={{0,1},{1,0},{2,3},{3,2},{4,5},{5,4},{6,7},{7,6},{8,9},{9,8},{10,11... | collective-permute-start | bytes 393224 | tf_op jit(solution)/shard_map/ppermute | solution.py:502
  102.9 1.5 %collective-permute-start.19 = (bf16[256,256]{1,0:T(8,128)(2,1)S(1)}, bf16[256,256]{1,0:T(8,128)(2,1)S(1)}, u32[]{:S(2)}, u32[]{:S(2)}) collective-permute-start(bf16[256,256]{1,0:T(8,128)(2,1)S(1)} %get-tuple-element.55), channel_id=1, source_target_pairs={{0,3},{1,2},{2,1},{3,0},{4,7},{5,6},{6,5},{7,4},{8,11},{9,10},{10,... | collective-permute-start | bytes 393224 | tf_op jit(solution)/shard_map/ppermute | solution.py:502
  104.4 3.6 %collective-permute-done.21.refs_3_ = bf16[256,256]{1,0:T(8,128)(2,1)S(1)} collective-permute-done((bf16[256,256]{1,0:T(8,128)(2,1)S(1)}, bf16[256,256]{1,0:T(8,128)(2,1)S(1)}, u32[]{:S(2)}, u32[]{:S(2)}) %collective-permute-start.21) | collective-permute-done | bytes 131104 | tf_op jit(solution)/shard_map/ppermute | solution.py:502
  108.0 2.2 %copy-done = bf16[4,512,1024]{2,1,0:T(8,128)(2,1)S(1)} copy-done((bf16[4,512,1024]{2,1,0:T(8,128)(2,1)S(1)}, bf16[4,512,1024]{2,1,0:T(8,128)(2,1)}, u32[]{:S(2)}) %copy-start) | copy-done | bytes 4194328
  110.2 1.2 project.2.refs_6_
  111.4 1.4 %collective-permute-done.18.refs_2_ = bf16[256,256]{1,0:T(8,128)(2,1)S(1)} collective-permute-done((bf16[256,256]{1,0:T(8,128)(2,1)S(1)}, bf16[256,256]{1,0:T(8,128)(2,1)S(1)}, u32[]{:S(2)}, u32[]{:S(2)}) %collective-permute-start.18) | collective-permute-done | bytes 131104 | tf_op jit(solution)/shard_map/ppermute | solution.py:502
  112.9 5.9 %collective-permute-done.19.refs_3_ = bf16[256,256]{1,0:T(8,128)(2,1)S(1)} collective-permute-done((bf16[256,256]{1,0:T(8,128)(2,1)S(1)}, bf16[256,256]{1,0:T(8,128)(2,1)S(1)}, u32[]{:S(2)}, u32[]{:S(2)}) %collective-permute-start.19) | collective-permute-done | bytes 131104 | tf_op jit(solution)/shard_map/ppermute | solution.py:502
  118.8 2.2 %project.3 = bf16[256,2048]{1,0:T(8,128)(2,1)} custom-call(bf16[256,256]{1,0:T(8,128)(2,1)S(1)} %get-tuple-element.52.refs_0_, bf16[256,256]{1,0:T(8,128)(2,1)S(1)} %collective-permute-done.17.refs_1_, bf16[256,256]{1,0:T(8,128)(2,1)S(1)} %collective-permute-done.18.refs_2_, bf16[256,256]{1,0:T(8,128)(2,1)S(1)} %collective-permute-done.19.refs_3_, ...), custom_call_target="tpu_custom_call" | custom-call | flops 1073741824 | bytes 4718592 | tf_op jit(solution)/shard_map/project/pallas_call | solution.py:428
  (49 shorter events, 0.5 us)
Async XLA Ops:
  6.5 92.2 %all-gather.3.cloned.1.call-start = ((), (), s32[]{:S(2)}) async-start(), calls=%async_computation.3 | async-start | bytes 5242880 | tf_op jit(solution)/shard_map/all_gather | solution.py:506
  10.9 9.3 %copy-start.1 = (bf16[2,512,512]{2,1,0:T(8,128)(2,1)S(1)}, bf16[2,512,512]{2,1,0:T(8,128)(2,1)}, u32[]{:S(2)}) copy-start(bf16[2,512,512]{2,1,0:T(8,128)(2,1)} %get-tuple-element.32.refs_0_) | copy-start | bytes 3145732
  10.9 7.5 %collective-permute-start.2 = (bf16[2,64,512]{2,1,0:T(8,128)(2,1)}, bf16[2,64,512]{2,1,0:T(8,128)(2,1)S(1)}, u32[]{:S(2)}, u32[]{:S(2)}) collective-permute-start(bf16[2,64,512]{2,1,0:T(8,128)(2,1)} %get-tuple-element.33.refs_0_), channel_id=1, source_target_pairs={{0,24},{4,28},{8,16},{12,20},{16,8},{20,12},{24,0},{28,4},{1,25},{... | collective-permute-start | bytes 393224 | tf_op jit(solution)/shard_map/ppermute | solution.py:445
  12.4 7.7 %collective-permute-start.1 = (bf16[2,64,512]{2,1,0:T(8,128)(2,1)}, bf16[2,64,512]{2,1,0:T(8,128)(2,1)S(1)}, u32[]{:S(2)}, u32[]{:S(2)}) collective-permute-start(bf16[2,64,512]{2,1,0:T(8,128)(2,1)} %get-tuple-element.33.refs_0_), channel_id=1, source_target_pairs={{0,16},{4,20},{8,24},{12,28},{16,0},{20,4},{24,8},{28,12},{1,17},{... | collective-permute-start | bytes 393224 | tf_op jit(solution)/shard_map/ppermute | solution.py:445
  12.9 7.3 %collective-permute-start = (bf16[2,64,512]{2,1,0:T(8,128)(2,1)}, bf16[2,64,512]{2,1,0:T(8,128)(2,1)S(1)}, u32[]{:S(2)}, u32[]{:S(2)}) collective-permute-start(bf16[2,64,512]{2,1,0:T(8,128)(2,1)} %get-tuple-element.33.refs_0_), channel_id=1, source_target_pairs={{0,8},{4,12},{8,0},{12,4},{16,24},{20,28},{24,16},{28,20},{1,9},{5... | collective-permute-start | bytes 393224 | tf_op jit(solution)/shard_map/ppermute | solution.py:445
  18.4 3.8 %copy-start.2 = (bf16[2,64,512]{2,1,0:T(8,128)(2,1)}, bf16[2,64,512]{2,1,0:T(8,128)(2,1)S(1)}, u32[]{:S(2)}) copy-start(bf16[2,64,512]{2,1,0:T(8,128)(2,1)S(1)} %collective-permute-done.2.refs_3_) | copy-start | bytes 393220
  20.1 3.9 %copy-start.3 = (bf16[2,64,512]{2,1,0:T(8,128)(2,1)}, bf16[2,64,512]{2,1,0:T(8,128)(2,1)S(1)}, u32[]{:S(2)}) copy-start(bf16[2,64,512]{2,1,0:T(8,128)(2,1)S(1)} %collective-permute-done.1.refs_2_) | copy-start | bytes 393220
  20.2 4.2 %copy-start.4 = (bf16[2,64,512]{2,1,0:T(8,128)(2,1)}, bf16[2,64,512]{2,1,0:T(8,128)(2,1)S(1)}, u32[]{:S(2)}) copy-start(bf16[2,64,512]{2,1,0:T(8,128)(2,1)S(1)} %collective-permute-done.refs_1_) | copy-start | bytes 393220
  20.2 3.7 %copy-start.11 = (bf16[2,64,512]{2,1,0:T(8,128)(2,1)S(1)}, bf16[2,64,512]{2,1,0:T(8,128)(2,1)}, u32[]{:S(2)}) copy-start(bf16[2,64,512]{2,1,0:T(8,128)(2,1)} %get-tuple-element.33.refs_0_) | copy-start | bytes 393220
  20.2 22.4 %collective-permute-start.3 = (bf16[2,512,512]{2,1,0:T(8,128)(2,1)S(1)}, bf16[2,512,512]{2,1,0:T(8,128)(2,1)}, u32[]{:S(2)}, u32[]{:S(2)}) collective-permute-start(bf16[2,512,512]{2,1,0:T(8,128)(2,1)S(1)} %after.4.refs_1_), channel_id=1, source_target_pairs={{0,4},{4,8},{8,12},{12,16},{16,20},{20,24},{24,28},{1,5},{5,9},{9,... | collective-permute-start | bytes 3145736 | tf_op jit(solution)/shard_map/ppermute | solution.py:518
  22.3 6.3 %collective-permute-start.7 = (bf16[2,64,512]{2,1,0:T(8,128)(2,1)S(1)}, bf16[2,64,512]{2,1,0:T(8,128)(2,1)S(1)}, u32[]{:S(2)}, u32[]{:S(2)}) collective-permute-start(bf16[2,64,512]{2,1,0:T(8,128)(2,1)S(1)} %collective-permute-done.2.refs_3_), channel_id=1, source_target_pairs={{0,4},{4,0},{8,12},{12,8},{16,20},{20,16},{24,28},{28,24},{1,5},{5... | collective-permute-start | bytes 393224 | tf_op jit(solution)/shard_map/ppermute | solution.py:445
  23.8 8.2 %collective-permute-start.4 = (bf16[2,64,512]{2,1,0:T(8,128)(2,1)S(1)}, bf16[2,64,512]{2,1,0:T(8,128)(2,1)S(1)}, u32[]{:S(2)}, u32[]{:S(2)}) collective-permute-start(bf16[2,64,512]{2,1,0:T(8,128)(2,1)S(1)} %copy-done.11), channel_id=1, source_target_pairs={{0,4},{4,0},{8,12},{12,8},{16,20},{20,16},{24,28},{28,24},{1,5},{5... | collective-permute-start | bytes 393224 | tf_op jit(solution)/shard_map/ppermute | solution.py:445
  23.9 8.1 %collective-permute-start.6 = (bf16[2,64,512]{2,1,0:T(8,128)(2,1)S(1)}, bf16[2,64,512]{2,1,0:T(8,128)(2,1)S(1)}, u32[]{:S(2)}, u32[]{:S(2)}) collective-permute-start(bf16[2,64,512]{2,1,0:T(8,128)(2,1)S(1)} %collective-permute-done.1.refs_2_), channel_id=1, source_target_pairs={{0,4},{4,0},{8,12},{12,8},{16,20},{20,16},{24,28},{28,24},{1,5},{5... | collective-permute-start | bytes 393224 | tf_op jit(solution)/shard_map/ppermute | solution.py:445
  24.4 7.7 %collective-permute-start.5 = (bf16[2,64,512]{2,1,0:T(8,128)(2,1)S(1)}, bf16[2,64,512]{2,1,0:T(8,128)(2,1)}, u32[]{:S(2)}, u32[]{:S(2)}) collective-permute-start(bf16[2,64,512]{2,1,0:T(8,128)(2,1)S(1)} %collective-permute-done.refs_1_), channel_id=1, source_target_pairs={{0,4},{4,0},{8,12},{12,8},{16,20},{20,16},{24,28},{28,24},{1,5},{5... | collective-permute-start | bytes 393224 | tf_op jit(solution)/shard_map/ppermute | solution.py:445
  24.5 28.8 %all-to-all-start = ((bf16[8,3,2,64,256]{4,3,2,1,0:T(8,128)(2,1)}), bf16[8,3,2,64,256]{4,3,2,1,0:T(8,128)(2,1)S(1)}, u32[]{:S(2)}, u32[]{:S(2)}) async-start(bf16[8,3,2,64,256]{4,3,2,1,0:T(8,128)(2,1)} %after.5), calls=%async_computation | async-start | bytes 3145728 | tf_op jit(solution)/shard_map/all_to_all | solution.py:544
  28.6 0.6 copy-start.10
  32.0 10.5 %copy-start.12 = (bf16[2,64,512]{2,1,0:T(8,128)(2,1)}, bf16[2,64,512]{2,1,0:T(8,128)(2,1)S(1)}, u32[]{:S(2)}) copy-start(bf16[2,64,512]{2,1,0:T(8,128)(2,1)S(1)} %collective-permute-done.4.refs_4_) | copy-start | bytes 393220
  32.1 10.5 %copy-start.13 = (bf16[2,64,512]{2,1,0:T(8,128)(2,1)}, bf16[2,64,512]{2,1,0:T(8,128)(2,1)S(1)}, u32[]{:S(2)}) copy-start(bf16[2,64,512]{2,1,0:T(8,128)(2,1)S(1)} %collective-permute-done.6.refs_6_) | copy-start | bytes 393220
  49.7 0.7 copy-start.5
  53.3 25.9 %all-to-all-start.1 = ((bf16[8,3,2,64,256]{4,3,2,1,0:T(8,128)(2,1)}), bf16[8,3,2,64,256]{4,3,2,1,0:T(8,128)(2,1)S(1)}, u32[]{:S(2)}, u32[]{:S(2)}) async-start(bf16[8,3,2,64,256]{4,3,2,1,0:T(8,128)(2,1)} %after.6), calls=%async_computation.1 | async-start | bytes 3145728 | tf_op jit(solution)/shard_map/all_to_all | solution.py:544
  59.3 3.7 %copy-start.9 = (f32[8,128]{1,0:T(8,128)}, f32[8,128]{1,0:T(8,128)S(1)}, u32[]{:S(2)}) copy-start(f32[8,128]{1,0:T(8,128)S(1)} %get-tuple-element.34.refs_8_) | copy-start | bytes 12292
  59.3 10.8 %collective-permute-start.8 = (bf16[2,64,256]{2,1,0:T(8,128)(2,1)S(1)}, bf16[2,64,256]{2,1,0:T(8,128)(2,1)S(1)}, u32[]{:S(2)}, u32[]{:S(2)}) collective-permute-start(bf16[2,64,256]{2,1,0:T(8,128)(2,1)S(1)} %get-tuple-element.41), channel_id=1, source_target_pairs={{0,4},{4,0},{8,12},{12,8},{16,20},{20,16},{24,28},{28,24},{1,5},{5... | collective-permute-start | bytes 196616 | tf_op jit(solution)/shard_map/ppermute | solution.py:502
  59.5 18.1 %collective-permute-start.9 = (bf16[2,64,256]{2,1,0:T(8,128)(2,1)S(1)}, bf16[2,64,256]{2,1,0:T(8,128)(2,1)S(1)}, u32[]{:S(2)}, u32[]{:S(2)}) collective-permute-start(bf16[2,64,256]{2,1,0:T(8,128)(2,1)S(1)} %get-tuple-element.42), channel_id=1, source_target_pairs={{0,8},{4,12},{8,0},{12,4},{16,24},{20,28},{24,16},{28,20},{1,9},{5... | collective-permute-start | bytes 196616 | tf_op jit(solution)/shard_map/ppermute | solution.py:502
  59.9 26.8 %collective-permute-start.10 = (bf16[2,64,256]{2,1,0:T(8,128)(2,1)S(1)}, bf16[2,64,256]{2,1,0:T(8,128)(2,1)S(1)}, u32[]{:S(2)}, u32[]{:S(2)}) collective-permute-start(bf16[2,64,256]{2,1,0:T(8,128)(2,1)S(1)} %get-tuple-element.43), channel_id=1, source_target_pairs={{0,12},{4,8},{8,4},{12,0},{16,28},{20,24},{24,20},{28,16},{1,13},{... | collective-permute-start | bytes 196616 | tf_op jit(solution)/shard_map/ppermute | solution.py:502
  61.2 25.4 %collective-permute-start.11 = (bf16[2,64,256]{2,1,0:T(8,128)(2,1)S(1)}, bf16[2,64,256]{2,1,0:T(8,128)(2,1)S(1)}, u32[]{:S(2)}, u32[]{:S(2)}) collective-permute-start(bf16[2,64,256]{2,1,0:T(8,128)(2,1)S(1)} %get-tuple-element.44), channel_id=1, source_target_pairs={{0,16},{4,20},{8,24},{12,28},{16,0},{20,4},{24,8},{28,12},{1,17},{... | collective-permute-start | bytes 196616 | tf_op jit(solution)/shard_map/ppermute | solution.py:502
  62.7 24.0 %collective-permute-start.12 = (bf16[2,64,256]{2,1,0:T(8,128)(2,1)S(1)}, bf16[2,64,256]{2,1,0:T(8,128)(2,1)S(1)}, u32[]{:S(2)}, u32[]{:S(2)}) collective-permute-start(bf16[2,64,256]{2,1,0:T(8,128)(2,1)S(1)} %get-tuple-element.45), channel_id=1, source_target_pairs={{0,20},{4,16},{8,28},{12,24},{16,4},{20,0},{24,12},{28,8},{1,21},{... | collective-permute-start | bytes 196616 | tf_op jit(solution)/shard_map/ppermute | solution.py:502
  70.1 16.6 %collective-permute-start.13 = (bf16[2,64,256]{2,1,0:T(8,128)(2,1)S(1)}, bf16[2,64,256]{2,1,0:T(8,128)(2,1)S(1)}, u32[]{:S(2)}, u32[]{:S(2)}) collective-permute-start(bf16[2,64,256]{2,1,0:T(8,128)(2,1)S(1)} %get-tuple-element.46), channel_id=1, source_target_pairs={{0,24},{4,28},{8,16},{12,20},{16,8},{20,12},{24,0},{28,4},{1,25},{... | collective-permute-start | bytes 196616 | tf_op jit(solution)/shard_map/ppermute | solution.py:502
  77.6 9.1 %collective-permute-start.14 = (bf16[2,64,256]{2,1,0:T(8,128)(2,1)S(1)}, bf16[2,64,256]{2,1,0:T(8,128)(2,1)S(1)}, u32[]{:S(2)}, u32[]{:S(2)}) collective-permute-start(bf16[2,64,256]{2,1,0:T(8,128)(2,1)S(1)} %get-tuple-element.47), channel_id=1, source_target_pairs={{0,28},{4,24},{8,20},{12,16},{16,12},{20,8},{24,4},{28,0},{1,29},{... | collective-permute-start | bytes 196616 | tf_op jit(solution)/shard_map/ppermute | solution.py:502
  79.2 0.7 copy-start.8
  82.4 16.0 %all-to-all-start.2 = ((bf16[8,2,64,256]{3,2,1,0:T(8,128)(2,1)}), bf16[8,2,64,256]{3,2,1,0:T(8,128)(2,1)S(1)}, u32[]{:S(2)}, u32[]{:S(2)}) async-start(bf16[8,2,64,256]{3,2,1,0:T(8,128)(2,1)} %get-tuple-element.38), calls=%async_computation.2 | async-start | bytes 1048576 | tf_op jit(solution)/shard_map/all_to_all | solution.py:550
  86.7 1.2 copy-start.7
  87.9 10.5 %copy-start.6 = (f32[1024,256]{1,0:T(8,128)S(1)}, f32[1024,256]{1,0:T(8,128)}, u32[]{:S(2)}) copy-start(f32[1024,256]{1,0:T(8,128)} %get-tuple-element.35.home_ref) | copy-start | bytes 3145732
  88.2 6.9 %collective-permute-start.15 = (bf16[256,256]{1,0:T(8,128)(2,1)S(1)}, bf16[256,256]{1,0:T(8,128)(2,1)S(1)}, u32[]{:S(2)}, u32[]{:S(2)}) collective-permute-start(bf16[256,256]{1,0:T(8,128)(2,1)S(1)} %get-tuple-element.50), channel_id=1, source_target_pairs={{0,1},{1,0},{2,3},{3,2},{4,5},{5,4},{6,7},{7,6},{8,9},{9,8},{10,11... | collective-permute-start | bytes 393224 | tf_op jit(solution)/shard_map/ppermute | solution.py:502
  88.8 9.6 %collective-permute-start.16 = (bf16[256,256]{1,0:T(8,128)(2,1)S(1)}, bf16[256,256]{1,0:T(8,128)(2,1)S(1)}, u32[]{:S(2)}, u32[]{:S(2)}) collective-permute-start(bf16[256,256]{1,0:T(8,128)(2,1)S(1)} %get-tuple-element.51), channel_id=1, source_target_pairs={{0,2},{1,3},{2,0},{3,1},{4,6},{5,7},{6,4},{7,5},{8,10},{9,11},{10,... | collective-permute-start | bytes 393224 | tf_op jit(solution)/shard_map/ppermute | solution.py:502
  98.7 9.3 %collective-permute-start.20 = (bf16[4,512,1024]{2,1,0:T(8,128)(2,1)}, bf16[4,512,1024]{2,1,0:T(8,128)(2,1)S(1)}, u32[]{:S(2)}, u32[]{:S(2)}) collective-permute-start(bf16[4,512,1024]{2,1,0:T(8,128)(2,1)} %after.7.refs_4_), channel_id=1, source_target_pairs={{0,4},{4,0},{8,12},{12,8},{16,20},{20,16},{24,28},{28,24},{1,5},{5... | collective-permute-start | bytes 12582920 | tf_op jit(solution)/shard_map/ppermute | solution.py:562
  98.8 9.2 %collective-permute-start.21 = (bf16[256,256]{1,0:T(8,128)(2,1)S(1)}, bf16[256,256]{1,0:T(8,128)(2,1)S(1)}, u32[]{:S(2)}, u32[]{:S(2)}) collective-permute-start(bf16[256,256]{1,0:T(8,128)(2,1)S(1)} %get-tuple-element.58), channel_id=1, source_target_pairs={{0,3},{1,2},{2,1},{3,0},{4,7},{5,6},{6,5},{7,4},{8,11},{9,10},{10,... | collective-permute-start | bytes 393224 | tf_op jit(solution)/shard_map/ppermute | solution.py:502
  99.3 12.1 %collective-permute-start.17 = (bf16[256,256]{1,0:T(8,128)(2,1)S(1)}, bf16[256,256]{1,0:T(8,128)(2,1)S(1)}, u32[]{:S(2)}, u32[]{:S(2)}) collective-permute-start(bf16[256,256]{1,0:T(8,128)(2,1)S(1)} %get-tuple-element.53), channel_id=1, source_target_pairs={{0,1},{1,0},{2,3},{3,2},{4,5},{5,4},{6,7},{7,6},{8,9},{9,8},{10,11... | collective-permute-start | bytes 393224 | tf_op jit(solution)/shard_map/ppermute | solution.py:502
  102.9 9.9 %collective-permute-start.18 = (bf16[256,256]{1,0:T(8,128)(2,1)S(1)}, bf16[256,256]{1,0:T(8,128)(2,1)S(1)}, u32[]{:S(2)}, u32[]{:S(2)}) collective-permute-start(bf16[256,256]{1,0:T(8,128)(2,1)S(1)} %get-tuple-element.54), channel_id=1, source_target_pairs={{0,2},{1,3},{2,0},{3,1},{4,6},{5,7},{6,4},{7,5},{8,10},{9,11},{10,... | collective-permute-start | bytes 393224 | tf_op jit(solution)/shard_map/ppermute | solution.py:502
  102.9 15.8 %collective-permute-start.19 = (bf16[256,256]{1,0:T(8,128)(2,1)S(1)}, bf16[256,256]{1,0:T(8,128)(2,1)S(1)}, u32[]{:S(2)}, u32[]{:S(2)}) collective-permute-start(bf16[256,256]{1,0:T(8,128)(2,1)S(1)} %get-tuple-element.55), channel_id=1, source_target_pairs={{0,3},{1,2},{2,1},{3,0},{4,7},{5,6},{6,5},{7,4},{8,11},{9,10},{10,... | collective-permute-start | bytes 393224 | tf_op jit(solution)/shard_map/ppermute | solution.py:502
  108.0 2.2 %copy-start = (bf16[4,512,1024]{2,1,0:T(8,128)(2,1)S(1)}, bf16[4,512,1024]{2,1,0:T(8,128)(2,1)}, u32[]{:S(2)}) copy-start(bf16[4,512,1024]{2,1,0:T(8,128)(2,1)} %after.7.refs_4_) | copy-start | bytes 12582916
Sparse Core Ops, SparseCore 0:
  8.9 79.4 all-gather.2
